TPU v7x, 32 devices: a whole 2x2x4 slice. The times are simulated.
32 devices in a mesh: rows: 4 (over x, core), cols: 8 (over z, y).
Axes of the slice: x: 2, y: 2, z: 4, core: 2. Of those that a mesh axis runs over, the one named last changes fastest.
Arguments:
- tokens: bfloat16 [1280, 8192], P(('rows', 'cols')), may hold values from -6 to 6
- norm_gain: float32 [8192], replicated, may hold values from 0.1 to 1.9
- gate_weight: bfloat16 [8192, 14336], P('rows', 'cols'), may hold values from -0.09375 to 0.09375
- up_weight: bfloat16 [8192, 14336], P('rows', 'cols'), may hold values from -0.09375 to 0.09375
- down_weight: bfloat16 [14336, 8192], P('cols'), may hold values from -0.125 to 0.125
- gate_mask: int32 [128, 224], P('rows', 'cols'), may hold values 0 or 1
- up_mask: int32 [128, 224], P('rows', 'cols'), may hold values 0 or 1
- down_mask: int32 [224, 128], P('cols'), may hold values 0 or 1
Outputs:
- branch_out: bfloat16 [1280, 8192], P(('rows', 'cols'))
All inputs are finite; a program needn't handle non-finite values. No bound on the sum of `gate_mask` or of `up_mask` or of `down_mask` on one device may be relied on, other than what follows from the above.
Results may differ from a plain program's by a relative error of at most 0.025.
Values may be sent and summed in bfloat16 or wider, within the bound.
No kernel may reach another device: no remote copies, remote signals or barrier semaphores. Data moves between devices by JAX's collectives and lax.ppermute only.
A program may use at most 256 MiB of HBM per device.

v0:
```python
import jax
import jax.numpy as jnp
from jax import lax
from jax.sharding import PartitionSpec as P

BLOCK = 64


def expand(mask):
    return jnp.repeat(jnp.repeat(mask, BLOCK, 0), BLOCK, 1).astype(jnp.bfloat16)


def rms_normed(rows_in, norm_gain):
    values = rows_in.astype(jnp.float32)
    meansq = jnp.mean(values * values, axis=-1, keepdims=True)
    return (values * lax.rsqrt(meansq + 1e-05) * norm_gain).astype(jnp.bfloat16)


def rounded_dot(left, right):
    part = jnp.dot(left, right, preferred_element_type=jnp.float32).astype(jnp.bfloat16)
    part = lax.optimization_barrier(part)
    return part.astype(jnp.float32)


def body(tokens, norm_gain, gate_weight, up_weight, down_weight, gate_mask, up_mask, down_mask):
    whole_rows = lax.all_gather(tokens, "cols", axis=0, tiled=True)
    normed = rms_normed(whole_rows, norm_gain)
    gate_kept = gate_weight * expand(gate_mask)
    up_kept = up_weight * expand(up_mask)
    down_kept = down_weight * expand(down_mask)
    row_count = normed.shape[0]
    width_local = gate_kept.shape[1]
    feature_rows = gate_kept.shape[0]
    empty = jnp.zeros((row_count, width_local), jnp.float32)
    pieces = (
        lax.all_gather(gate_kept, "rows", axis=0, tiled=True),
        lax.all_gather(up_kept, "rows", axis=0, tiled=True),
    )
    gate_total = empty
    up_total = empty
    shard_count = pieces[0].shape[0] // feature_rows
    for shard in range(shard_count):
        offset = shard * feature_rows
        features = lax.dynamic_slice_in_dim(normed, offset, feature_rows, 1)
        gate_total = gate_total + rounded_dot(features, pieces[0][offset : offset + feature_rows])
        up_total = up_total + rounded_dot(features, pieces[1][offset : offset + feature_rows])
    hidden = (jax.nn.silu(gate_total) * up_total).astype(jnp.bfloat16)
    return lax.psum_scatter(
        rounded_dot(hidden, down_kept).astype(jnp.bfloat16), "cols", scatter_dimension=0, tiled=True
    )


def solution(mesh):
    return jax.shard_map(
        body,
        mesh=mesh,
        in_specs=(
            P(("rows", "cols"), None),
            P(),
            P("rows", "cols"),
            P("rows", "cols"),
            P("cols", None),
            P("rows", "cols"),
            P("rows", "cols"),
            P("cols", None),
        ),
        out_specs=P(("rows", "cols"), None),
        check_vma=False,
    )
```

profile of v0, /device:TPU:0, one launch (start us, length us, event | category | flops | bytes accessed | tf_op | source)
XLA Modules:
  0.0 613.9 jit_solution(12342203849844668395)
XLA Ops:
  6.5 0.0 all-gather.4.cloned.1.call-start
  6.5 0.7 all-gather.4.cloned.1.call-update
  7.3 0.0 copy-start.3
  7.3 0.0 all-gather.6.cloned.1.call-start
  7.3 10.5 %copy.16 = bf16[2048,1792]{0,1:T(8,128)(2,1)} copy(bf16[2048,1792]{1,0:T(8,128)(2,1)} %param.10) | data formatting | bytes 14680064 | tf_op args[2]
  17.8 0.0 copy-done.3
  17.8 0.1 copy.15
  17.9 0.2 broadcast_in_dim.20
  18.1 0.2 convert_element_type.98
  18.3 7.0 %bitcast_multiply_fusion.2 = bf16[2048,1792]{0,1:T(8,128)(2,1)} fusion(bf16[2048,1792]{0,1:T(8,128)(2,1)} %copy.16, bf16[2048,28]{0,1:T(8,128)(2,1)S(1)} %convert_element_type.98), kind=kLoop, calls=%fused_computation.24 | loop fusion | flops 3670016 | bytes 14794752 | tf_op jit(solution)/shard_map/mul | solution.py:28
  25.3 0.0 all-gather.6.cloned.1.call-update
  25.4 0.0 copy-start.4
  25.4 0.0 all-gather.8.cloned.1.call-start
  25.4 10.5 %copy.18 = bf16[2048,1792]{0,1:T(8,128)(2,1)} copy(bf16[2048,1792]{1,0:T(8,128)(2,1)} %param.11) | data formatting | bytes 14680064 | tf_op args[3]
  36.0 0.0 copy-done.4
  36.0 0.1 copy.17
  36.1 0.2 broadcast_in_dim.22
  36.3 0.2 convert_element_type.109
  36.5 6.5 %bitcast_multiply_fusion.1 = bf16[2048,1792]{0,1:T(8,128)(2,1)} fusion(bf16[2048,1792]{0,1:T(8,128)(2,1)} %copy.18, bf16[2048,28]{0,1:T(8,128)(2,1)S(1)} %convert_element_type.109), kind=kLoop, calls=%fused_computation.23 | loop fusion | flops 3670016 | bytes 14794752 | tf_op jit(solution)/shard_map/mul | solution.py:29
  43.0 0.0 all-gather.8.cloned.1.call-update
  43.1 0.0 copy-start.5
  43.1 0.0 reduce-scatter.2.cloned.1.call-start
  43.1 36.1 %copy.20 = bf16[1792,8192]{0,1:T(8,128)(2,1)} copy(bf16[1792,8192]{1,0:T(8,128)(2,1)} %param.12) | data formatting | bytes 58720256 | tf_op args[4]
  79.2 0.0 copy-done.5
  79.2 0.1 broadcast_in_dim.24
  79.3 0.2 copy.19
  79.5 0.0 copy-start.2
  79.5 20.3 %bitcast_multiply_fusion = bf16[1792,8192]{0,1:T(8,128)(2,1)} fusion(bf16[1792,8192]{0,1:T(8,128)(2,1)} %copy.20, bf16[1792,128]{0,1:T(8,128)(2,1)S(1)} %copy.19), kind=kLoop, calls=%fused_computation | loop fusion | flops 14680064 | bytes 59179008 | tf_op jit(solution)/shard_map/mul | solution.py:30
  99.8 0.0 copy-start
  99.8 3.8 fusion
  103.6 0.0 copy-done.2
  103.6 0.2 copy-done
  103.9 5.4 fusion.2
  109.3 167.0 %all-gather.6.cloned.1.call-done = bf16[8192,1792]{0,1:T(8,128)(2,1)} async-done(((bf16[2048,1792]{0,1:T(8,128)(2,1)}), bf16[8192,1792]{0,1:T(8,128)(2,1)}) %all-gather.6.cloned.1.call-update) | async-done | bytes 29360144 | tf_op jit(solution)/shard_map/all_gather | solution.py:36
  276.3 6.2 %fusion.19 = bf16[320,1792]{1,0:T(8,128)(2,1)S(1)} fusion(bf16[8192,1792]{0,1:T(8,128)(2,1)} %all-gather.6.cloned.1.call-done, bf16[320,8192]{1,0:T(8,128)(2,1)} %fusion.2), kind=kOutput, calls=%fused_computation.25 | convolution fusion | flops 2349383680 | bytes 9797632 | tf_op jit(solution)/shard_map/dot_general | solution.py:20
  282.5 0.0 copy-done.1
  282.6 7.2 %fusion.22 = bf16[320,1792]{1,0:T(8,128)(2,1)S(1)} fusion(bf16[8192,1792]{0,1:T(8,128)(2,1)} %all-gather.6.cloned.1.call-done, bf16[320,8192]{1,0:T(8,128)(2,1)S(1)} %copy-done.1), kind=kOutput, calls=%fused_computation.26 | convolution fusion | flops 2349383680 | bytes 9797632 | tf_op jit(solution)/shard_map/dot_general | solution.py:20
  289.7 7.2 %fusion.25 = bf16[320,1792]{1,0:T(8,128)(2,1)S(1)} fusion(bf16[8192,1792]{0,1:T(8,128)(2,1)} %all-gather.6.cloned.1.call-done, bf16[320,8192]{1,0:T(8,128)(2,1)S(1)} %copy-done.1), kind=kOutput, calls=%fused_computation.27 | convolution fusion | flops 2349383680 | bytes 9797632 | tf_op jit(solution)/shard_map/dot_general | solution.py:20
  296.9 8.3 %fusion.28 = bf16[320,1792]{1,0:T(8,128)(2,1)} fusion(bf16[8192,1792]{0,1:T(8,128)(2,1)} %all-gather.6.cloned.1.call-done, bf16[320,8192]{1,0:T(8,128)(2,1)S(1)} %copy-done.1), kind=kOutput, calls=%fused_computation.28 | convolution fusion | flops 2349383680 | bytes 9797632 | tf_op jit(solution)/shard_map/dot_general | solution.py:20
  305.2 150.7 %all-gather.8.cloned.1.call-done = bf16[8192,1792]{0,1:T(8,128)(2,1)} async-done(((bf16[2048,1792]{0,1:T(8,128)(2,1)}), bf16[8192,1792]{0,1:T(8,128)(2,1)}) %all-gather.8.cloned.1.call-update) | async-done | bytes 29360144 | tf_op jit(solution)/shard_map/all_gather | solution.py:37
  456.0 7.2 %fusion.31 = bf16[320,1792]{1,0:T(8,128)(2,1)} fusion(bf16[8192,1792]{0,1:T(8,128)(2,1)} %all-gather.8.cloned.1.call-done, bf16[320,8192]{1,0:T(8,128)(2,1)} %fusion.2), kind=kOutput, calls=%fused_computation.29 | convolution fusion | flops 2349383680 | bytes 9797632 | tf_op jit(solution)/shard_map/dot_general | solution.py:20
  463.2 7.2 %fusion.34 = bf16[320,1792]{1,0:T(8,128)(2,1)} fusion(bf16[8192,1792]{0,1:T(8,128)(2,1)} %all-gather.8.cloned.1.call-done, bf16[320,8192]{1,0:T(8,128)(2,1)} %fusion.2), kind=kOutput, calls=%fused_computation.30 | convolution fusion | flops 2349383680 | bytes 9797632 | tf_op jit(solution)/shard_map/dot_general | solution.py:20
  470.4 0.0 slice-done
  470.4 6.8 %fusion.37 = bf16[320,1792]{1,0:T(8,128)(2,1)} fusion(bf16[8192,1792]{0,1:T(8,128)(2,1)} %all-gather.8.cloned.1.call-done, bf16[320,8192]{1,0:T(8,128)(2,1)S(1)} %bitcast.13), kind=kOutput, calls=%fused_computation.31 | convolution fusion | flops 2349383680 | bytes 9797632 | tf_op jit(solution)/shard_map/dot_general | solution.py:20
  477.2 6.8 %fusion.40 = bf16[320,1792]{1,0:T(8,128)(2,1)} fusion(bf16[8192,1792]{0,1:T(8,128)(2,1)} %all-gather.8.cloned.1.call-done, bf16[320,8192]{1,0:T(8,128)(2,1)S(1)} %bitcast.13), kind=kOutput, calls=%fused_computation.32 | convolution fusion | flops 2349383680 | bytes 9797632 | tf_op jit(solution)/shard_map/dot_general | solution.py:20
  484.0 20.6 %convolution_convert_fusion = bf16[320,8192]{1,0:T(8,128)(2,1)} fusion(bf16[1792,8192]{0,1:T(8,128)(2,1)} %bitcast_multiply_fusion, bf16[320,1792]{1,0:T(8,128)(2,1)} %fusion.40, bf16[320,1792]{1,0:T(8,128)(2,1)} %fusion.37, bf16[320,1792]{1,0:T(8,128)(2,1)} %fusion.34, bf16[320,1792]{1,0:T(8,128)(2,1)} %fusion.31, bf16[320,1792]{1,0:T(8,128)(2,1)} %fusion.28, ...), kind=kOutput, calls=%fused_computation.3 | convolution fusion | flops 9409331200 | bytes 43778048 | tf_op jit(solution)/shard_map/dot_general | solution.py:20
  504.6 0.0 reduce-scatter.2.cloned.1.call-update
  504.6 102.8 %reduce-scatter.2.cloned.1.call-done = bf16[40,8192]{1,0:T(8,128)(2,1)} async-done(((bf16[320,8192]{1,0:T(8,128)(2,1)}), bf16[40,8192]{1,0:T(8,128)(2,1)}) %reduce-scatter.2.cloned.1.call-update) | async-done | bytes 655376 | tf_op jit(solution)/shard_map/reduce_scatter | solution.py:48
  (10 shorter events, 0.0 us)
Async XLA Ops:
  6.5 93.3 %all-gather.4.cloned.1.call-start = ((), (), s32[]{:S(2)}) async-start(), calls=%async_computation.1 | async-start | bytes 5898240 | tf_op jit(solution)/shard_map/all_gather | solution.py:26
  7.3 10.5 %copy-start.3 = (s32[32,28]{1,0:T(8,128)S(1)}, s32[32,28]{1,0:T(8,128)}, u32[]{:S(2)}) copy-start(s32[32,28]{1,0:T(8,128)} %param.13) | copy-start | bytes 10756
  7.3 269.1 %all-gather.6.cloned.1.call-start = ((), (), s32[]{:S(2)}) async-start(), calls=%async_computation.2 | async-start | bytes 36700160 | tf_op jit(solution)/shard_map/all_gather | solution.py:36
  25.4 10.6 %copy-start.4 = (s32[32,28]{1,0:T(8,128)S(1)}, s32[32,28]{1,0:T(8,128)}, u32[]{:S(2)}) copy-start(s32[32,28]{1,0:T(8,128)} %param.14) | copy-start | bytes 10756
  25.4 430.6 %all-gather.8.cloned.1.call-start = ((), (), s32[]{:S(2)}) async-start(), calls=%async_computation.3 | async-start | bytes 36700160 | tf_op jit(solution)/shard_map/all_gather | solution.py:37
  43.1 36.1 %copy-start.5 = (s32[28,128]{1,0:T(8,128)S(1)}, s32[28,128]{1,0:T(8,128)}, u32[]{:S(2)}) copy-start(s32[28,128]{1,0:T(8,128)} %param.15) | copy-start | bytes 43012
  43.1 564.3 %reduce-scatter.2.cloned.1.call-start = ((), (), s32[]{:S(2)}) async-start(), calls=%async_computation.4 | async-start | bytes 5898240 | tf_op jit(solution)/shard_map/reduce_scatter | solution.py:48
  79.5 24.1 %copy-start.2 = (f32[8192]{0:T(1024)S(1)}, f32[8192]{0:T(1024)}, u32[]{:S(2)}) copy-start(f32[8192]{0:T(1024)} %param.9) | copy-start | bytes 98308
  99.8 4.0 copy-start
  276.3 6.2 %copy-start.1 = (bf16[320,8192]{1,0:T(8,128)(2,1)S(1)}, bf16[320,8192]{1,0:T(8,128)(2,1)}, u32[]{:S(2)}) copy-start(bf16[320,8192]{1,0:T(8,128)(2,1)} %fusion.2) | copy-start | bytes 15728644
  456.0 14.5 %slice-start = ((s8[5242880]{0:T(1024)(128)(4,1)}), s8[4194304]{0:T(1024)(128)(4,1)S(1)}, s32[]{:S(2)}) async-start(s8[5242880]{0:T(1024)(128)(4,1)} %bitcast.12), calls=%async_computation.5 | async-start | bytes 8388608
  463.2 7.2 %slice-start.1 = ((s8[5242880]{0:T(1024)(128)(4,1)}), s8[1048576]{0:T(1024)(128)(4,1)S(1)}, s32[]{:S(2)}) async-start(s8[5242880]{0:T(1024)(128)(4,1)} %bitcast.12), calls=%async_computation.6 | async-start | bytes 2097152
Sparse Core Ops, SparseCore 0:
  9.5 88.9 all-gather.3
  100.1 176.1 all-gather.5
  277.9 177.9 all-gather.7
  504.8 102.5 reduce-scatter.1
where the time goes:
time: 616 us; the launch traced here: 614 us
  waiting for transfers between devices  421 us (68%)
  matrix products  77.5 us (13%)
  local copies, waits for them, and re-layouts  58.6 us (10%)
  other arithmetic  43.1 us (7%)
  between operations  13.3 us (2%)
    all_gather x1, waiting for transfers between devices, body(): lax.all_gather(gate_kept, 'rows', axis=0, tiled=True)  167 us
    all_gather x1, waiting for transfers between devices, body(): lax.all_gather(up_kept, 'rows', axis=0, tiled=True)  151 us
    reduce_scatter x1, waiting for transfers between devices, body(): lax.psum_scatter(rounded_dot(hidden, down_kept).astype(jnp.bfloat16), 'co...  103 us
    dot_general x9, matrix products, rounded_dot(): jnp.dot(left, right, preferred_element_type=jnp.float32)  77.5 us
    unnamed x19, local copies, waits for them, and re-layouts  57.4 us
    mul x1, other arithmetic, body(): down_kept = down_weight * expand(down_mask)  20.3 us
  transfers between devices with their start and end apart: 4, of which 3 were waited for; matrix products, arithmetic and copies ran while one was open for 21% of the time, Pallas kernels for 0%

commit v1 on v0

v1 whole, which is shorter than its diff:
```python
import functools

import jax
import jax.numpy as jnp
from jax import lax
from jax.experimental import pallas as pl
from jax.experimental.pallas import tpu as pltpu
from jax.sharding import PartitionSpec as P

BLOCK = 64
CORES = 2
PLANES = 4
VMEM = 48 * 1024 * 1024
F32 = jnp.float32
BF16 = jnp.bfloat16


def tile_of(size, most):
    tile = most
    while size % tile:
        tile //= 2
    return tile


def spread(mask):
    return jnp.repeat(mask, BLOCK, 1).astype(F32)


def rms_normed(rows_in, norm_gain):
    values = rows_in.astype(F32)
    meansq = jnp.mean(values * values, axis=-1, keepdims=True)
    return (values * lax.rsqrt(meansq + 1e-05) * norm_gain).astype(BF16)


def params(*semantics):
    return pltpu.CompilerParams(dimension_semantics=semantics, vmem_limit_bytes=VMEM)


def cost(flops, moved):
    return pl.CostEstimate(flops=flops, bytes_accessed=moved, transcendentals=0)


def mask_kernel(weight_ref, mask_ref, kept_ref):
    for block in range(weight_ref.shape[0] // BLOCK):
        rows = pl.ds(block * BLOCK, BLOCK)
        keep = jnp.broadcast_to(mask_ref[block : block + 1, :], (BLOCK, weight_ref.shape[1]))
        kept_ref[rows, :] = weight_ref[rows, :] * keep.astype(BF16)


def masked(weight, mask, rows, columns):
    depth, width = weight.shape
    return pl.pallas_call(
        mask_kernel,
        grid=(depth // rows, width // columns),
        in_specs=[
            pl.BlockSpec((rows, columns), lambda i, j: (i, j)),
            pl.BlockSpec((rows // BLOCK, columns), lambda i, j: (i, j)),
        ],
        out_specs=pl.BlockSpec((rows, columns), lambda i, j: (i, j)),
        out_shape=jax.ShapeDtypeStruct(weight.shape, weight.dtype),
        compiler_params=params("arbitrary", "arbitrary"),
        cost_estimate=cost(weight.size, 4 * weight.size),
        name="masked",
    )(weight, spread(mask))


def gate_up_kernel(*refs):
    (*parts, gate_ref, up_ref, keep_ref, send_ref, all_rows) = refs
    half = parts[0].shape[0] // 2
    kept = half * len(parts)

    @pl.when(pl.program_id(0) == 0)
    def _():
        for place, part in enumerate(parts):
            all_rows[pl.ds(place * half, half), :] = part[:half, :]
            all_rows[pl.ds(kept + place * half, half), :] = part[half:, :]

    for which, weight_ref in enumerate((gate_ref, up_ref)):
        total = jnp.dot(all_rows[...], weight_ref[...], preferred_element_type=F32).astype(BF16)
        keep_ref[which] = total[:kept]
        send_ref[which] = total[kept:]


def gate_up(parts, gate_kept, up_kept):
    rows = sum(part.shape[0] for part in parts)
    depth, width = gate_kept.shape
    tile = tile_of(width, 256)
    half = jax.ShapeDtypeStruct((2, rows // 2, width), BF16)
    whole = pl.BlockSpec(parts[0].shape, lambda i: (0, 0))
    columns = pl.BlockSpec((depth, tile), lambda i: (0, i))
    result = pl.BlockSpec((2, rows // 2, tile), lambda i: (0, 0, i))
    return pl.pallas_call(
        gate_up_kernel,
        grid=(width // tile,),
        in_specs=[whole] * len(parts) + [columns] * 2,
        out_specs=[result] * 2,
        out_shape=[half] * 2,
        scratch_shapes=[pltpu.VMEM((rows, depth), BF16)],
        compiler_params=params("arbitrary"),
        cost_estimate=cost(4 * rows * depth * width, 4 * depth * width + 4 * rows * width),
        name="gate_up",
    )(*parts, gate_kept, up_kept)


def down_kernel(hidden_ref, weight_ref, partial_ref):
    total = jnp.dot(hidden_ref[...], weight_ref[...], preferred_element_type=F32)
    partial_ref[...] = total.reshape(partial_ref.shape).astype(BF16)


def down(hidden, down_kept, groups):
    rows, depth = hidden.shape
    width = down_kept.shape[1]
    tile = tile_of(width, 1024)
    return pl.pallas_call(
        down_kernel,
        grid=(width // tile,),
        in_specs=[
            pl.BlockSpec((rows, depth), lambda i: (0, 0)),
            pl.BlockSpec((depth, tile), lambda i: (0, i)),
        ],
        out_specs=pl.BlockSpec((groups, rows // groups, tile), lambda i: (0, 0, i)),
        out_shape=jax.ShapeDtypeStruct((groups, rows // groups, width), BF16),
        compiler_params=params("arbitrary"),
        cost_estimate=cost(2 * rows * depth * width, 2 * depth * width + 2 * rows * width),
        name="down",
    )(hidden, down_kept)


def swap(values, axis, size, step):
    return lax.ppermute(values, axis, [(place, place ^ step) for place in range(size)])


def body(row_count, col_count, tokens, norm_gain, gate_weight, up_weight, down_weight, gate_mask, up_mask, down_mask):
    chips = row_count // CORES
    per_plane = col_count // PLANES
    own, _ = tokens.shape
    features, width = gate_weight.shape
    row = lax.axis_index("rows")

    normed = rms_normed(tokens, norm_gain)
    order = [chip * CORES + core for core in range(CORES) for chip in range(chips)]
    blocks = []
    for step in order:
        block = lax.dynamic_slice_in_dim(normed, (row ^ step) * features, features, 1)
        blocks.append(swap(block, "rows", row_count, step) if step else block)
    mine = jnp.concatenate(blocks, 0)

    gate_kept = masked(gate_weight, gate_mask, tile_of(features, 512), width)
    up_kept = masked(up_weight, up_mask, tile_of(features, 512), width)
    down_kept = masked(down_weight, down_mask, down_weight.shape[0], tile_of(down_weight.shape[1], 1024))

    planes = [mine]
    for plane in range(1, PLANES):
        planes.append(swap(mine, "cols", col_count, plane * per_plane))

    total = None
    for plane in range(PLANES):
        parts = [planes[plane]]
        for step in range(1, per_plane):
            parts.append(swap(planes[plane], "cols", col_count, step))
        keep, send = gate_up(parts, gate_kept, up_kept)
        came = swap(send, "rows", row_count, 1)
        sums = (keep.astype(F32) + came.astype(F32)).reshape(2, per_plane, chips, own, width)
        both = sums[:, :, 0]
        for chip in range(1, chips):
            both = both + swap(sums[:, :, chip].astype(BF16), "rows", row_count, chip * CORES).astype(F32)
        hidden = (jax.nn.silu(both[0]) * both[1]).astype(BF16)
        partial = down(hidden.reshape(per_plane * own, width), down_kept, per_plane)
        summed = partial[0].astype(F32)
        for step in range(1, per_plane):
            summed = summed + swap(partial[step], "cols", col_count, step).astype(F32)
        if plane:
            summed = swap(summed.astype(BF16), "cols", col_count, plane * per_plane).astype(F32)
        total = summed if total is None else total + summed
    return total.astype(BF16)


def solution(mesh):
    return jax.shard_map(
        functools.partial(body, mesh.shape["rows"], mesh.shape["cols"]),
        mesh=mesh,
        in_specs=(
            P(("rows", "cols"), None),
            P(),
            P("rows", "cols"),
            P("rows", "cols"),
            P("cols", None),
            P("rows", "cols"),
            P("rows", "cols"),
            P("cols", None),
        ),
        out_specs=P(("rows", "cols"), None),
        check_vma=False,
    )
```

time: 616 us -> 296 us (0.48)
  waiting for transfers between devices: 421 us -> 127 us
  Pallas kernels: 0 us -> 127 us
  matrix products: 77.5 us -> 0 us
  local copies, waits for them, and re-layouts: 58.6 us -> 5.42 us
  other arithmetic: 43.1 us -> 7.66 us
  starting transfers between devices: 0.13 us -> 27.3 us
  between operations: 13.3 us -> 0.39 us
    all_gather x3 -> x0, waiting for transfers between devices: 318 us -> none  [the longest x1 167 us: body(): lax.all_gather(gate_kept, 'rows', axis=0, tiled=True)]
    ppermute x0 -> x25, waiting for transfers between devices: none -> 127 us  [swap(): lax.ppermute(values, axis, [(place, place ^ step) for place in range(size)])]
    pallas_call x0 -> x11, Pallas kernels: none -> 127 us  [the longest x4 52.2 us: down(): pl.pallas_call(down_kernel, grid=(width // tile,), in_specs=[pl.BlockSpec...]
    reduce_scatter x1 -> x0, waiting for transfers between devices: 103 us -> none  [body(): lax.psum_scatter(rounded_dot(hidden, down_kept).astype(jnp.bfloat16), 'co...]
    dot_general x9 -> x0, matrix products: 77.5 us -> none  [rounded_dot(): jnp.dot(left, right, preferred_element_type=jnp.float32)]
    unnamed x19 -> x6, local copies, waits for them, and re-layouts: 57.4 us -> 0.02 us
    mul x3 -> x0, other arithmetic: 33.9 us -> none  [the longest x1 20.3 us: body(): down_kept = down_weight * expand(down_mask)]
    ppermute x0 -> x25, starting transfers between devices: none -> 27.3 us  [swap(): lax.ppermute(values, axis, [(place, place ^ step) for place in range(size)])]
  transfers between devices with their start and end apart: 4 -> 25, of which waited for: 3 -> 10; matrix products, arithmetic and copies ran while one was open for 21% -> 3% of each run, Pallas kernels for 0% -> 43%
where the time goes in v1:
time: 296 us; the launch traced here: 295 us
  waiting for transfers between devices  127 us (43%)
  Pallas kernels  127 us (43%)
  starting transfers between devices  27.3 us (9%)
  other arithmetic  7.66 us (3%)
  local copies, waits for them, and re-layouts  5.42 us (2%)
    ppermute x25, waiting for transfers between devices, swap(): lax.ppermute(values, axis, [(place, place ^ step) for place in range(size)])  127 us
    pallas_call x4, Pallas kernels, down(): pl.pallas_call(down_kernel, grid=(width // tile,), in_specs=[pl.BlockSpec...  52.2 us
    pallas_call x4, Pallas kernels, gate_up(): pl.pallas_call(gate_up_kernel, grid=(width // tile,), in_specs=[whole] *...  41.1 us
    pallas_call x3, Pallas kernels, masked(): pl.pallas_call(mask_kernel, grid=(depth // rows, width // columns), in_sp...  33.7 us
    ppermute x25, starting transfers between devices, swap(): lax.ppermute(values, axis, [(place, place ^ step) for place in range(size)])  27.3 us
  transfers between devices with their start and end apart: 25, of which 10 were waited for; matrix products, arithmetic and copies ran while one was open for 3% of the time, Pallas kernels for 43%

profile of v1, /device:TPU:0, one launch (start us, length us, event | category | flops | bytes accessed | tf_op | source)
XLA Modules:
  0.0 295.0 jit_solution(14476325474233866901)
XLA Ops:
  0.0 1.3 fusion
  1.3 1.3 fusion.2
  2.8 2.4 collective-permute-start.2
  5.2 0.7 collective-permute-start.1
  5.9 3.9 %collective-permute-done.2 = bf16[40,2048]{1,0:T(8,128)(2,1)S(1)} collective-permute-done((bf16[40,2048]{1,0:T(8,128)(2,1)S(1)}, bf16[40,2048]{1,0:T(8,128)(2,1)S(1)}, u32[]{:S(2)}, u32[]{:S(2)}) %collective-permute-start.2) | collective-permute-done | bytes 163872 | tf_op jit(solution)/shard_map/ppermute | solution.py:130
  9.8 3.7 %collective-permute-done = bf16[40,2048]{1,0:T(8,128)(2,1)S(1)} collective-permute-done((bf16[40,2048]{1,0:T(8,128)(2,1)S(1)}, bf16[40,2048]{1,0:T(8,128)(2,1)S(1)}, u32[]{:S(2)}, u32[]{:S(2)}) %collective-permute-start) | collective-permute-done | bytes 163872 | tf_op jit(solution)/shard_map/ppermute | solution.py:130
  13.5 2.4 collective-permute-start.3
  15.9 1.6 collective-permute-start.7
  18.2 6.5 %masked.3.refs_2_ = bf16[2048,1792]{1,0:T(8,128)(2,1)} custom-call(bf16[2048,1792]{1,0:T(8,128)(2,1)} %weight_ref.3, f32[32,1792]{1,0:T(8,128)S(1)} %convert_element_type.149.mask_ref), custom_call_target="tpu_custom_call" | custom-call | flops 3670016 | bytes 14680064 | tf_op jit(solution)/shard_map/masked/pallas_call | solution.py:52
  24.8 6.5 %masked.4.refs_3_ = bf16[2048,1792]{1,0:T(8,128)(2,1)} custom-call(bf16[2048,1792]{1,0:T(8,128)(2,1)} %weight_ref.4, f32[32,1792]{1,0:T(8,128)S(1)} %convert_element_type.151.mask_ref), custom_call_target="tpu_custom_call" | custom-call | flops 3670016 | bytes 14680064 | tf_op jit(solution)/shard_map/masked/pallas_call | solution.py:52
  31.3 10.7 %gate_up.4 = (bf16[2,160,1792]{2,1,0:T(8,128)(2,1)S(1)}, bf16[2,160,1792]{2,1,0:T(8,128)(2,1)}) custom-call(bf16[160,2048]{1,0:T(8,128)(2,1)S(1)} %pad_maximum_fusion.refs_0_, bf16[160,2048]{1,0:T(8,128)(2,1)S(1)} %collective-permute-done.3.refs_1_, bf16[2048,1792]{1,0:T(8,128)(2,1)} %masked.3.refs_2_, bf16[2048,1792]{1,0:T(8,128)(2,1)} %masked.4.refs_3_), custom_call_target="tpu_custom_call" | custom-call | flops 4697620480 | bytes 16973824 | tf_op jit(solution)/shard_map/gate_up/pallas_call | solution.py:92
  42.1 3.4 %collective-permute-start.19 = (bf16[160,2048]{1,0:T(8,128)(2,1)S(1)}, bf16[160,2048]{1,0:T(8,128)(2,1)S(1)}, u32[]{:S(2)}, u32[]{:S(2)}) collective-permute-start(bf16[160,2048]{1,0:T(8,128)(2,1)S(1)} %pad_maximum_fusion.refs_0_), channel_id=1, source_target_pairs={{0,6},{1,7},{2,4},{3,5},{4,2},{5,3},{6,0},{7,1},{8,14},{9,15},{10,... | collective-permute-start | bytes 1966088 | tf_op jit(solution)/shard_map/ppermute | solution.py:130
  45.4 1.5 collective-permute-start.8
  47.0 1.8 broadcast_in_dim.13
  48.8 2.1 convert_element_type.158.mask_ref
  50.9 20.6 %masked.5.weight_ref = bf16[1792,8192]{1,0:T(8,128)(2,1)} custom-call(bf16[1792,8192]{1,0:T(8,128)(2,1)} %weight_ref.5, f32[28,8192]{1,0:T(8,128)S(1)} %convert_element_type.158.mask_ref), custom_call_target="tpu_custom_call" | custom-call | flops 14680064 | bytes 58720256 | tf_op jit(solution)/shard_map/masked/pallas_call | solution.py:52
  71.5 0.5 collective-permute-start.20
  72.0 30.3 %collective-permute-done.13.refs_0_ = bf16[160,2048]{1,0:T(8,128)(2,1)} collective-permute-done((bf16[160,2048]{1,0:T(8,128)(2,1)S(1)}, bf16[160,2048]{1,0:T(8,128)(2,1)}, u32[]{:S(2)}, u32[]{:S(2)}) %collective-permute-start.13) | collective-permute-done | bytes 655392 | tf_op jit(solution)/shard_map/ppermute | solution.py:130
  102.3 1.4 collective-permute-start.14
  103.7 10.3 %gate_up.5 = (bf16[2,160,1792]{2,1,0:T(8,128)(2,1)S(1)}, bf16[2,160,1792]{2,1,0:T(8,128)(2,1)S(1)}) custom-call(bf16[160,2048]{1,0:T(8,128)(2,1)} %collective-permute-done.7.refs_0_, bf16[160,2048]{1,0:T(8,128)(2,1)} %collective-permute-done.8.refs_1_, bf16[2048,1792]{1,0:T(8,128)(2,1)} %masked.3.refs_2_, bf16[2048,1792]{1,0:T(8,128)(2,1)} %masked.4.refs_3_), custom_call_target="tpu_custom_call" | custom-call | flops 4697620480 | bytes 16973824 | tf_op jit(solution)/shard_map/gate_up/pallas_call | solution.py:92
  114.2 1.5 convert_add_fusion.3
  115.7 1.6 collective-permute-start.5
  117.3 1.6 collective-permute-done.14.refs_1_
  119.0 10.1 %gate_up.6 = (bf16[2,160,1792]{2,1,0:T(8,128)(2,1)S(1)}, bf16[2,160,1792]{2,1,0:T(8,128)(2,1)S(1)}) custom-call(bf16[160,2048]{1,0:T(8,128)(2,1)} %collective-permute-done.13.refs_0_, bf16[160,2048]{1,0:T(8,128)(2,1)S(1)} %collective-permute-done.14.refs_1_, bf16[2048,1792]{1,0:T(8,128)(2,1)} %masked.3.refs_2_, bf16[2048,1792]{1,0:T(8,128)(2,1)} %masked.4.refs_3_), custom_call_target="tpu_custom_call" | custom-call | flops 4697620480 | bytes 16973824 | tf_op jit(solution)/shard_map/gate_up/pallas_call | solution.py:92
  129.2 9.9 %gate_up.7 = (bf16[2,160,1792]{2,1,0:T(8,128)(2,1)S(1)}, bf16[2,160,1792]{2,1,0:T(8,128)(2,1)S(1)}) custom-call(bf16[160,2048]{1,0:T(8,128)(2,1)S(1)} %collective-permute-done.19.refs_0_, bf16[160,2048]{1,0:T(8,128)(2,1)S(1)} %collective-permute-done.20.refs_1_, bf16[2048,1792]{1,0:T(8,128)(2,1)} %masked.3.refs_2_, bf16[2048,1792]{1,0:T(8,128)(2,1)} %masked.4.refs_3_), custom_call_target="tpu_custom_call" | custom-call | flops 4697620480 | bytes 16973824 | tf_op jit(solution)/shard_map/gate_up/pallas_call | solution.py:92
  139.1 0.5 collective-permute-start.21
  140.0 13.1 %down.4 = bf16[2,40,8192]{2,1,0:T(8,128)(2,1)S(1)} custom-call(bf16[80,1792]{1,0:T(8,128)(2,1)S(1)} %fusion.30.hidden_ref, bf16[1792,8192]{1,0:T(8,128)(2,1)} %masked.5.weight_ref), custom_call_target="tpu_custom_call" | custom-call | flops 2348810240 | bytes 30670848 | tf_op jit(solution)/shard_map/down/pallas_call | solution.py:114
  153.1 1.4 collective-permute-start.6
  154.5 0.2 convert_add_fusion.2
  154.8 1.6 collective-permute-start.10
  156.4 0.2 convert_add_fusion.1
  156.7 0.6 collective-permute-start.16
  157.6 1.6 collective-permute-start.22
  159.2 11.6 %collective-permute-done.10 = bf16[2,2,40,1792]{3,2,1,0:T(8,128)(2,1)S(1)} collective-permute-done((bf16[2,2,40,1792]{3,2,1,0:T(8,128)(2,1)S(1)}, bf16[2,2,40,1792]{3,2,1,0:T(8,128)(2,1)S(1)}, u32[]{:S(2)}, u32[]{:S(2)}) %collective-permute-start.10) | collective-permute-done | bytes 573472 | tf_op jit(solution)/shard_map/ppermute | solution.py:130
  170.9 12.2 %collective-permute-done.16 = bf16[2,2,40,1792]{3,2,1,0:T(8,128)(2,1)S(1)} collective-permute-done((bf16[2,2,40,1792]{3,2,1,0:T(8,128)(2,1)S(1)}, bf16[2,2,40,1792]{3,2,1,0:T(8,128)(2,1)S(1)}, u32[]{:S(2)}, u32[]{:S(2)}) %collective-permute-start.16) | collective-permute-done | bytes 573472 | tf_op jit(solution)/shard_map/ppermute | solution.py:130
  183.4 10.7 %collective-permute-done.22 = bf16[2,2,40,1792]{3,2,1,0:T(8,128)(2,1)S(1)} collective-permute-done((bf16[2,2,40,1792]{3,2,1,0:T(8,128)(2,1)S(1)}, bf16[2,2,40,1792]{3,2,1,0:T(8,128)(2,1)S(1)}, u32[]{:S(2)}, u32[]{:S(2)}) %collective-permute-start.22) | collective-permute-done | bytes 573472 | tf_op jit(solution)/shard_map/ppermute | solution.py:130
  194.5 13.1 %down.7 = bf16[2,40,8192]{2,1,0:T(8,128)(2,1)S(1)} custom-call(bf16[80,1792]{1,0:T(8,128)(2,1)S(1)} %fusion.18.hidden_ref, bf16[1792,8192]{1,0:T(8,128)(2,1)} %masked.5.weight_ref), custom_call_target="tpu_custom_call" | custom-call | flops 2348810240 | bytes 30670848 | tf_op jit(solution)/shard_map/down/pallas_call | solution.py:114
  207.6 0.7 collective-permute-start.23
  208.5 13.1 %down.6 = bf16[2,40,8192]{2,1,0:T(8,128)(2,1)S(1)} custom-call(bf16[80,1792]{1,0:T(8,128)(2,1)S(1)} %fusion.22.hidden_ref, bf16[1792,8192]{1,0:T(8,128)(2,1)} %masked.5.weight_ref), custom_call_target="tpu_custom_call" | custom-call | flops 2348810240 | bytes 30670848 | tf_op jit(solution)/shard_map/down/pallas_call | solution.py:114
  221.6 1.4 collective-permute-start.17
  223.2 13.1 %down.5 = bf16[2,40,8192]{2,1,0:T(8,128)(2,1)S(1)} custom-call(bf16[80,1792]{1,0:T(8,128)(2,1)S(1)} %fusion.26.hidden_ref, bf16[1792,8192]{1,0:T(8,128)(2,1)} %masked.5.weight_ref), custom_call_target="tpu_custom_call" | custom-call | flops 2348810240 | bytes 30670848 | tf_op jit(solution)/shard_map/down/pallas_call | solution.py:114
  236.3 0.7 collective-permute-start.11
  237.2 2.6 collective-permute-start.24
  240.1 11.3 %collective-permute-done.11 = bf16[40,8192]{1,0:T(8,128)(2,1)S(1)} collective-permute-done((bf16[40,8192]{1,0:T(8,128)(2,1)S(1)}, bf16[40,8192]{1,0:T(8,128)(2,1)S(1)}, u32[]{:S(2)}, u32[]{:S(2)}) %collective-permute-start.11) | collective-permute-done | bytes 655392 | tf_op jit(solution)/shard_map/ppermute | solution.py:130
  251.5 0.3 collective-permute-start.12
  251.8 5.0 %collective-permute-done.24 = bf16[40,8192]{1,0:T(8,128)(2,1)S(1)} collective-permute-done((bf16[40,8192]{1,0:T(8,128)(2,1)S(1)}, bf16[40,8192]{1,0:T(8,128)(2,1)S(1)}, u32[]{:S(2)}, u32[]{:S(2)}) %collective-permute-start.24) | collective-permute-done | bytes 655392 | tf_op jit(solution)/shard_map/ppermute | solution.py:130
  256.8 37.0 %collective-permute-done.18 = bf16[40,8192]{1,0:T(8,128)(2,1)S(1)} collective-permute-done((bf16[40,8192]{1,0:T(8,128)(2,1)S(1)}, bf16[40,8192]{1,0:T(8,128)(2,1)S(1)}, u32[]{:S(2)}, u32[]{:S(2)}) %collective-permute-start.18) | collective-permute-done | bytes 655392 | tf_op jit(solution)/shard_map/ppermute | solution.py:130
  293.8 1.2 fusion.9
  (61 shorter events, 3.7 us)
Async XLA Ops:
  2.7 14.8 %copy-start = (s32[32,28]{1,0:T(8,128)S(1)}, s32[32,28]{1,0:T(8,128)}, u32[]{:S(2)}) copy-start(s32[32,28]{1,0:T(8,128)} %param.13) | copy-start | bytes 10756
  2.7 14.8 %copy-start.1 = (s32[32,28]{1,0:T(8,128)S(1)}, s32[32,28]{1,0:T(8,128)}, u32[]{:S(2)}) copy-start(s32[32,28]{1,0:T(8,128)} %param.14) | copy-start | bytes 10756
  2.8 7.0 %collective-permute-start.2 = (bf16[40,2048]{1,0:T(8,128)(2,1)S(1)}, bf16[40,2048]{1,0:T(8,128)(2,1)S(1)}, u32[]{:S(2)}, u32[]{:S(2)}) collective-permute-start(bf16[40,2048]{1,0:T(8,128)(2,1)S(1)} %get-tuple-element.30), channel_id=1, source_target_pairs={{0,24},{8,16},{16,8},{24,0},{1,25},{9,17},{17,9},{25,1},{2,26},{10... | collective-permute-start | bytes 491528 | tf_op jit(solution)/shard_map/ppermute | solution.py:130
  5.2 4.6 %collective-permute-start.1 = (bf16[40,2048]{1,0:T(8,128)(2,1)S(1)}, bf16[40,2048]{1,0:T(8,128)(2,1)S(1)}, u32[]{:S(2)}, u32[]{:S(2)}) collective-permute-start(bf16[40,2048]{1,0:T(8,128)(2,1)S(1)} %get-tuple-element.31), channel_id=1, source_target_pairs={{0,8},{8,0},{16,24},{24,16},{1,9},{9,1},{17,25},{25,17},{2,10},{10... | collective-permute-start | bytes 491528 | tf_op jit(solution)/shard_map/ppermute | solution.py:130
  5.9 7.6 %collective-permute-start = (bf16[40,2048]{1,0:T(8,128)(2,1)S(1)}, bf16[40,2048]{1,0:T(8,128)(2,1)S(1)}, u32[]{:S(2)}, u32[]{:S(2)}) collective-permute-start(bf16[40,2048]{1,0:T(8,128)(2,1)S(1)} %get-tuple-element.32), channel_id=1, source_target_pairs={{0,16},{8,24},{16,0},{24,8},{1,17},{9,25},{17,1},{25,9},{2,18},{10... | collective-permute-start | bytes 491528 | tf_op jit(solution)/shard_map/ppermute | solution.py:130
  13.5 17.8 %collective-permute-start.3 = (bf16[160,2048]{1,0:T(8,128)(2,1)S(1)}, bf16[160,2048]{1,0:T(8,128)(2,1)S(1)}, u32[]{:S(2)}, u32[]{:S(2)}) collective-permute-start(bf16[160,2048]{1,0:T(8,128)(2,1)S(1)} %pad_maximum_fusion.refs_0_), channel_id=1, source_target_pairs={{0,1},{1,0},{2,3},{3,2},{4,5},{5,4},{6,7},{7,6},{8,9},{9,8},{10,11... | collective-permute-start | bytes 1966088 | tf_op jit(solution)/shard_map/ppermute | solution.py:130
  15.9 29.5 %collective-permute-start.7 = (bf16[160,2048]{1,0:T(8,128)(2,1)S(1)}, bf16[160,2048]{1,0:T(8,128)(2,1)}, u32[]{:S(2)}, u32[]{:S(2)}) collective-permute-start(bf16[160,2048]{1,0:T(8,128)(2,1)S(1)} %pad_maximum_fusion.refs_0_), channel_id=1, source_target_pairs={{0,2},{1,3},{2,0},{3,1},{4,6},{5,7},{6,4},{7,5},{8,10},{9,11},{10,... | collective-permute-start | bytes 1966088 | tf_op jit(solution)/shard_map/ppermute | solution.py:130
  31.3 15.6 %copy-start.2 = (s32[28,128]{1,0:T(8,128)S(1)}, s32[28,128]{1,0:T(8,128)}, u32[]{:S(2)}) copy-start(s32[28,128]{1,0:T(8,128)} %param.15) | copy-start | bytes 43012
  42.1 72.1 %collective-permute-start.4 = (bf16[2,160,1792]{2,1,0:T(8,128)(2,1)}, bf16[2,160,1792]{2,1,0:T(8,128)(2,1)}, u32[]{:S(2)}, u32[]{:S(2)}) collective-permute-start(bf16[2,160,1792]{2,1,0:T(8,128)(2,1)} %get-tuple-element.14), channel_id=1, source_target_pairs={{0,8},{8,0},{16,24},{24,16},{1,9},{9,1},{17,25},{25,17},{2,10},{10... | collective-permute-start | bytes 3440648 | tf_op jit(solution)/shard_map/ppermute | solution.py:130
  42.1 29.5 %collective-permute-start.19 = (bf16[160,2048]{1,0:T(8,128)(2,1)S(1)}, bf16[160,2048]{1,0:T(8,128)(2,1)S(1)}, u32[]{:S(2)}, u32[]{:S(2)}) collective-permute-start(bf16[160,2048]{1,0:T(8,128)(2,1)S(1)} %pad_maximum_fusion.refs_0_), channel_id=1, source_target_pairs={{0,6},{1,7},{2,4},{3,5},{4,2},{5,3},{6,0},{7,1},{8,14},{9,15},{10,... | collective-permute-start | bytes 1966088 | tf_op jit(solution)/shard_map/ppermute | solution.py:130
  45.4 56.9 %collective-permute-start.13 = (bf16[160,2048]{1,0:T(8,128)(2,1)S(1)}, bf16[160,2048]{1,0:T(8,128)(2,1)}, u32[]{:S(2)}, u32[]{:S(2)}) collective-permute-start(bf16[160,2048]{1,0:T(8,128)(2,1)S(1)} %pad_maximum_fusion.refs_0_), channel_id=1, source_target_pairs={{0,4},{1,5},{2,6},{3,7},{4,0},{5,1},{6,2},{7,3},{8,12},{9,13},{10,... | collective-permute-start | bytes 1966088 | tf_op jit(solution)/shard_map/ppermute | solution.py:130
  45.4 58.3 %collective-permute-start.8 = (bf16[160,2048]{1,0:T(8,128)(2,1)}, bf16[160,2048]{1,0:T(8,128)(2,1)}, u32[]{:S(2)}, u32[]{:S(2)}) collective-permute-start(bf16[160,2048]{1,0:T(8,128)(2,1)} %collective-permute-done.7.refs_0_), channel_id=1, source_target_pairs={{0,1},{1,0},{2,3},{3,2},{4,5},{5,4},{6,7},{7,6},{8,9},{9,8},{10,11... | collective-permute-start | bytes 1966088 | tf_op jit(solution)/shard_map/ppermute | solution.py:130
  71.5 57.6 %collective-permute-start.20 = (bf16[160,2048]{1,0:T(8,128)(2,1)S(1)}, bf16[160,2048]{1,0:T(8,128)(2,1)S(1)}, u32[]{:S(2)}, u32[]{:S(2)}) collective-permute-start(bf16[160,2048]{1,0:T(8,128)(2,1)S(1)} %collective-permute-done.19.refs_0_), channel_id=1, source_target_pairs={{0,1},{1,0},{2,3},{3,2},{4,5},{5,4},{6,7},{7,6},{8,9},{9,8},{10,11... | collective-permute-start | bytes 1966088 | tf_op jit(solution)/shard_map/ppermute | solution.py:130
  102.3 16.7 %collective-permute-start.14 = (bf16[160,2048]{1,0:T(8,128)(2,1)}, bf16[160,2048]{1,0:T(8,128)(2,1)S(1)}, u32[]{:S(2)}, u32[]{:S(2)}) collective-permute-start(bf16[160,2048]{1,0:T(8,128)(2,1)} %collective-permute-done.13.refs_0_), channel_id=1, source_target_pairs={{0,1},{1,0},{2,3},{3,2},{4,5},{5,4},{6,7},{7,6},{8,9},{9,8},{10,11... | collective-permute-start | bytes 1966088 | tf_op jit(solution)/shard_map/ppermute | solution.py:130
  114.1 40.5 %collective-permute-start.9 = (bf16[2,160,1792]{2,1,0:T(8,128)(2,1)S(1)}, bf16[2,160,1792]{2,1,0:T(8,128)(2,1)S(1)}, u32[]{:S(2)}, u32[]{:S(2)}) collective-permute-start(bf16[2,160,1792]{2,1,0:T(8,128)(2,1)S(1)} %get-tuple-element.16), channel_id=1, source_target_pairs={{0,8},{8,0},{16,24},{24,16},{1,9},{9,1},{17,25},{25,17},{2,10},{10... | collective-permute-start | bytes 3440648 | tf_op jit(solution)/shard_map/ppermute | solution.py:130
  115.7 23.9 %collective-permute-start.5 = (bf16[2,2,40,1792]{3,2,1,0:T(8,128)(2,1)S(1)}, bf16[2,2,40,1792]{3,2,1,0:T(8,128)(2,1)S(1)}, u32[]{:S(2)}, u32[]{:S(2)}) collective-permute-start(bf16[2,2,40,1792]{3,2,1,0:T(8,128)(2,1)S(1)} %fusion.14), channel_id=1, source_target_pairs={{0,16},{8,24},{16,0},{24,8},{1,17},{9,25},{17,1},{25,9},{2,18},{10... | collective-permute-start | bytes 1720328 | tf_op jit(solution)/shard_map/ppermute | solution.py:130
  129.1 27.3 %collective-permute-start.15 = (bf16[2,160,1792]{2,1,0:T(8,128)(2,1)S(1)}, bf16[2,160,1792]{2,1,0:T(8,128)(2,1)S(1)}, u32[]{:S(2)}, u32[]{:S(2)}) collective-permute-start(bf16[2,160,1792]{2,1,0:T(8,128)(2,1)S(1)} %get-tuple-element.18), channel_id=1, source_target_pairs={{0,8},{8,0},{16,24},{24,16},{1,9},{9,1},{17,25},{25,17},{2,10},{10... | collective-permute-start | bytes 3440648 | tf_op jit(solution)/shard_map/ppermute | solution.py:130
  139.1 18.2 %collective-permute-start.21 = (bf16[2,160,1792]{2,1,0:T(8,128)(2,1)S(1)}, bf16[2,160,1792]{2,1,0:T(8,128)(2,1)S(1)}, u32[]{:S(2)}, u32[]{:S(2)}) collective-permute-start(bf16[2,160,1792]{2,1,0:T(8,128)(2,1)S(1)} %get-tuple-element.20), channel_id=1, source_target_pairs={{0,8},{8,0},{16,24},{24,16},{1,9},{9,1},{17,25},{25,17},{2,10},{10... | collective-permute-start | bytes 3440648 | tf_op jit(solution)/shard_map/ppermute | solution.py:130
  153.1 98.7 %collective-permute-start.6 = (bf16[40,8192]{1,0:T(8,128)(2,1)S(1)}, bf16[40,8192]{1,0:T(8,128)(2,1)S(1)}, u32[]{:S(2)}, u32[]{:S(2)}) collective-permute-start(bf16[40,8192]{1,0:T(8,128)(2,1)S(1)} %slice_bitcast_fusion.6), channel_id=1, source_target_pairs={{0,1},{1,0},{2,3},{3,2},{4,5},{5,4},{6,7},{7,6},{8,9},{9,8},{10,11... | collective-permute-start | bytes 1966088 | tf_op jit(solution)/shard_map/ppermute | solution.py:130
  154.8 15.9 %collective-permute-start.10 = (bf16[2,2,40,1792]{3,2,1,0:T(8,128)(2,1)S(1)}, bf16[2,2,40,1792]{3,2,1,0:T(8,128)(2,1)S(1)}, u32[]{:S(2)}, u32[]{:S(2)}) collective-permute-start(bf16[2,2,40,1792]{3,2,1,0:T(8,128)(2,1)S(1)} %fusion.15), channel_id=1, source_target_pairs={{0,16},{8,24},{16,0},{24,8},{1,17},{9,25},{17,1},{25,9},{2,18},{10... | collective-permute-start | bytes 1720328 | tf_op jit(solution)/shard_map/ppermute | solution.py:130
  156.7 26.3 %collective-permute-start.16 = (bf16[2,2,40,1792]{3,2,1,0:T(8,128)(2,1)S(1)}, bf16[2,2,40,1792]{3,2,1,0:T(8,128)(2,1)S(1)}, u32[]{:S(2)}, u32[]{:S(2)}) collective-permute-start(bf16[2,2,40,1792]{3,2,1,0:T(8,128)(2,1)S(1)} %fusion.16), channel_id=1, source_target_pairs={{0,16},{8,24},{16,0},{24,8},{1,17},{9,25},{17,1},{25,9},{2,18},{10... | collective-permute-start | bytes 1720328 | tf_op jit(solution)/shard_map/ppermute | solution.py:130
  157.6 36.5 %collective-permute-start.22 = (bf16[2,2,40,1792]{3,2,1,0:T(8,128)(2,1)S(1)}, bf16[2,2,40,1792]{3,2,1,0:T(8,128)(2,1)S(1)}, u32[]{:S(2)}, u32[]{:S(2)}) collective-permute-start(bf16[2,2,40,1792]{3,2,1,0:T(8,128)(2,1)S(1)} %fusion.17), channel_id=1, source_target_pairs={{0,16},{8,24},{16,0},{24,8},{1,17},{9,25},{17,1},{25,9},{2,18},{10... | collective-permute-start | bytes 1720328 | tf_op jit(solution)/shard_map/ppermute | solution.py:130
  207.6 29.5 %collective-permute-start.23 = (bf16[40,8192]{1,0:T(8,128)(2,1)S(1)}, bf16[40,8192]{1,0:T(8,128)(2,1)S(1)}, u32[]{:S(2)}, u32[]{:S(2)}) collective-permute-start(bf16[40,8192]{1,0:T(8,128)(2,1)S(1)} %slice_bitcast_fusion), channel_id=1, source_target_pairs={{0,1},{1,0},{2,3},{3,2},{4,5},{5,4},{6,7},{7,6},{8,9},{9,8},{10,11... | collective-permute-start | bytes 1966088 | tf_op jit(solution)/shard_map/ppermute | solution.py:130
  221.6 18.2 %collective-permute-start.17 = (bf16[40,8192]{1,0:T(8,128)(2,1)S(1)}, bf16[40,8192]{1,0:T(8,128)(2,1)S(1)}, u32[]{:S(2)}, u32[]{:S(2)}) collective-permute-start(bf16[40,8192]{1,0:T(8,128)(2,1)S(1)} %slice_bitcast_fusion.2), channel_id=1, source_target_pairs={{0,1},{1,0},{2,3},{3,2},{4,5},{5,4},{6,7},{7,6},{8,9},{9,8},{10,11... | collective-permute-start | bytes 1966088 | tf_op jit(solution)/shard_map/ppermute | solution.py:130
  236.3 15.0 %collective-permute-start.11 = (bf16[40,8192]{1,0:T(8,128)(2,1)S(1)}, bf16[40,8192]{1,0:T(8,128)(2,1)S(1)}, u32[]{:S(2)}, u32[]{:S(2)}) collective-permute-start(bf16[40,8192]{1,0:T(8,128)(2,1)S(1)} %slice_bitcast_fusion.4), channel_id=1, source_target_pairs={{0,1},{1,0},{2,3},{3,2},{4,5},{5,4},{6,7},{7,6},{8,9},{9,8},{10,11... | collective-permute-start | bytes 1966088 | tf_op jit(solution)/shard_map/ppermute | solution.py:130
  237.2 19.6 %collective-permute-start.24 = (bf16[40,8192]{1,0:T(8,128)(2,1)S(1)}, bf16[40,8192]{1,0:T(8,128)(2,1)S(1)}, u32[]{:S(2)}, u32[]{:S(2)}) collective-permute-start(bf16[40,8192]{1,0:T(8,128)(2,1)S(1)} %fusion.3), channel_id=1, source_target_pairs={{0,6},{1,7},{2,4},{3,5},{4,2},{5,3},{6,0},{7,1},{8,14},{9,15},{10,... | collective-permute-start | bytes 1966088 | tf_op jit(solution)/shard_map/ppermute | solution.py:130
  240.0 53.8 %collective-permute-start.18 = (bf16[40,8192]{1,0:T(8,128)(2,1)S(1)}, bf16[40,8192]{1,0:T(8,128)(2,1)S(1)}, u32[]{:S(2)}, u32[]{:S(2)}) collective-permute-start(bf16[40,8192]{1,0:T(8,128)(2,1)S(1)} %fusion.4), channel_id=1, source_target_pairs={{0,4},{1,5},{2,6},{3,7},{4,0},{5,1},{6,2},{7,3},{8,12},{9,13},{10,... | collective-permute-start | bytes 1966088 | tf_op jit(solution)/shard_map/ppermute | solution.py:130
  251.5 42.3 %collective-permute-start.12 = (bf16[40,8192]{1,0:T(8,128)(2,1)S(1)}, bf16[40,8192]{1,0:T(8,128)(2,1)S(1)}, u32[]{:S(2)}, u32[]{:S(2)}) collective-permute-start(bf16[40,8192]{1,0:T(8,128)(2,1)S(1)} %fusion.5), channel_id=1, source_target_pairs={{0,2},{1,3},{2,0},{3,1},{4,6},{5,7},{6,4},{7,5},{8,10},{9,11},{10,... | collective-permute-start | bytes 1966088 | tf_op jit(solution)/shard_map/ppermute | solution.py:130

commit v2 on v0

v2 whole, which is shorter than its diff:
```python
import functools

import jax
import jax.numpy as jnp
from jax import lax
from jax.experimental import pallas as pl
from jax.experimental.pallas import tpu as pltpu
from jax.sharding import PartitionSpec as P

BLOCK = 64
CORES = 2
PLANES = 4
VMEM = 14 * 1024 * 1024
F32 = jnp.float32
BF16 = jnp.bfloat16


def tile_of(size, most):
    tile = most
    while size % tile:
        tile //= 2
    return tile


def spread(mask):
    return jnp.repeat(mask, BLOCK, 1).astype(F32)[:, None, :]


def rms_normed(rows_in, norm_gain):
    values = rows_in.astype(F32)
    meansq = jnp.mean(values * values, axis=-1, keepdims=True)
    return (values * lax.rsqrt(meansq + 1e-05) * norm_gain).astype(BF16)


def params(*semantics):
    return pltpu.CompilerParams(dimension_semantics=semantics, vmem_limit_bytes=VMEM)


HURRY = 4


def cost(flops, moved):
    return pl.CostEstimate(flops=flops // HURRY, bytes_accessed=moved // HURRY, transcendentals=0)


ANYWHERE = pl.BlockSpec(memory_space=pl.ANY)
INSIDE = pl.BlockSpec(memory_space=pltpu.VMEM)


def mask_kernel(core_ref, weight_ref, mask_ref, *refs):
    del core_ref
    kept_ref = refs[-1]
    for block in range(weight_ref.shape[0] // BLOCK):
        rows = pl.ds(block * BLOCK, BLOCK)
        keep = jnp.broadcast_to(mask_ref[block], (BLOCK, weight_ref.shape[1]))
        kept_ref[rows, :] = weight_ref[rows, :] * keep.astype(BF16)


def masked(weight, mask, rows, core, shares, after):
    depth, width = weight.shape
    width = width // shares
    mask = spread(mask)
    return pl.pallas_call(
        mask_kernel,
        grid_spec=pltpu.PrefetchScalarGridSpec(
            num_scalar_prefetch=1,
            grid=(depth // rows,),
            in_specs=[
                pl.BlockSpec((rows, width), lambda i, core: (i, core[0])),
                pl.BlockSpec((rows // BLOCK, 1, width), lambda i, core: (i, 0, core[0])),
            ]
            + [ANYWHERE] * len(after),
            out_specs=pl.BlockSpec((rows, width), lambda i, core: (i, 0)),
        ),
        out_shape=jax.ShapeDtypeStruct((depth, width), weight.dtype),
        compiler_params=params("arbitrary"),
        cost_estimate=cost(0, 4 * depth * width),
        name="masked",
    )(core, pltpu.with_memory_space_constraint(weight, pltpu.HBM), mask, *after)


def resident(values):
    return pltpu.with_memory_space_constraint(values, pltpu.VMEM)


def gate_up_kernel(part_count, after_count, *refs):
    parts, (gate_ref, up_ref) = refs[:part_count], refs[part_count : part_count + 2]
    keep_ref, *send_refs, all_rows = refs[part_count + 2 + after_count :]
    half = parts[0].shape[0] // 2
    kept = half * len(parts)
    for place, part in enumerate(parts):
        all_rows[pl.ds(place * half, half), :] = part[:half, :]
        all_rows[pl.ds(kept + place * half, half), :] = part[half:, :]
    tile = tile_of(gate_ref.shape[1], 256)

    @pl.loop(0, gate_ref.shape[1] // tile)
    def _(number):
        columns = pl.ds(pl.multiple_of(number * tile, tile), tile)
        for which, weight_ref in enumerate((gate_ref, up_ref)):
            total = jnp.dot(all_rows[...], weight_ref[:, columns], preferred_element_type=F32)
            total = total.reshape(2, *keep_ref.shape[1:4], tile).astype(BF16)
            keep_ref[which, :, :, :, columns] = total[0]
            send_refs[which][:, :, :, columns] = total[1]


def gate_up(parts, gate_kept, up_kept, chips, after):
    rows = sum(part.shape[0] for part in parts)
    depth, width = gate_kept.shape
    half = jax.ShapeDtypeStruct((2, len(parts), chips, rows // (2 * len(parts) * chips), width), BF16)
    return pl.pallas_call(
        functools.partial(gate_up_kernel, len(parts), len(after)),
        in_specs=[INSIDE] * (len(parts) + 2) + [ANYWHERE] * len(after),
        out_specs=[INSIDE] * 3,
        out_shape=[half] + [jax.ShapeDtypeStruct(half.shape[1:], BF16)] * 2,
        scratch_shapes=[pltpu.VMEM((rows, depth), BF16)],
        compiler_params=pltpu.CompilerParams(vmem_limit_bytes=VMEM),
        cost_estimate=cost(4 * rows * depth * width, 0),
        name="gate_up",
    )(*parts, resident(gate_kept), resident(up_kept), *after)


def down_kernel(after_count, own_ref, other_ref, weight_ref, *refs):
    *partial_refs, both = refs[after_count:]
    groups, own, depth = own_ref.shape
    rows = groups * own
    both[:rows, :] = own_ref[...].astype(F32).reshape(rows, depth).astype(BF16)
    both[rows:, :] = other_ref[...].astype(F32).reshape(rows, depth).astype(BF16)
    tile = tile_of(weight_ref.shape[1], 512)

    @pl.loop(0, weight_ref.shape[1] // tile)
    def _(number):
        columns = pl.ds(pl.multiple_of(number * tile, tile), tile)
        total = jnp.dot(both[...], weight_ref[:, columns], preferred_element_type=F32)
        total = total.reshape(CORES, groups, own, tile)
        for place, partial_ref in enumerate(partial_refs):
            partial_ref[:, :, columns] = total[:, place].astype(BF16)


def down(own, other, down_kept, after):
    groups, rows, depth = own.shape
    width = down_kept.shape[1]
    shape = (CORES, rows, width)
    return pl.pallas_call(
        functools.partial(down_kernel, len(after)),
        in_specs=[INSIDE] * 3 + [ANYWHERE] * len(after),
        out_specs=[INSIDE] * groups,
        out_shape=[jax.ShapeDtypeStruct(shape, BF16)] * groups,
        scratch_shapes=[pltpu.VMEM((CORES * groups * rows, depth), BF16)],
        compiler_params=pltpu.CompilerParams(vmem_limit_bytes=VMEM),
        cost_estimate=cost(2 * CORES * groups * rows * depth * width, 0),
        name="down",
    )(own, other, resident(down_kept), *after)


def sums_kernel(sizes, after_count, *refs):
    to_chips, to_hidden, to_rows = sizes
    refs = list(refs)
    ins = [[refs.pop(0) for _ in range(size)] for size in sizes]
    del refs[:after_count]

    if to_chips:
        keep_ref, *came_refs = ins[0]
        for chip in range(1, keep_ref.shape[2]):
            sent_ref = refs.pop(0)
            for which in range(2):
                for group in range(keep_ref.shape[1]):
                    came = came_refs[which][group, chip].astype(F32)
                    sent_ref[which, group] = (keep_ref[which, group, chip].astype(F32) + came).astype(BF16)
    if to_hidden:
        keep_ref, *came_refs = ins[1][:3]
        chip_refs = ins[1][3:]
        hidden_ref = refs.pop(0)
        for group in range(keep_ref.shape[1]):
            both = []
            for which in range(2):
                total = keep_ref[which, group, 0].astype(F32) + came_refs[which][group, 0].astype(F32)
                for chip_ref in chip_refs:
                    total = total + chip_ref[which, group].astype(F32)
                both.append(total)
            hidden_ref[group] = (jax.nn.silu(both[0]) * both[1]).astype(BF16)
    if to_rows:
        summed_ref = refs.pop(0)
        for core in range(CORES):
            total = ins[2][0][core].astype(F32)
            for ref in ins[2][1:]:
                total = total + ref[core].astype(F32)
            summed_ref[core] = total.astype(BF16)


def sums(to_chips, to_hidden, to_rows, after):
    shapes = []
    if to_chips:
        two, groups, chips, own, width = to_chips[0].shape
        shapes += [(two, groups, own, width)] * (chips - 1)
    if to_hidden:
        shapes.append((to_hidden[0].shape[1], *to_hidden[0].shape[3:]))
    if to_rows:
        shapes.append(to_rows[0].shape)
    given = [*to_chips, *to_hidden, *to_rows]
    results = list(pl.pallas_call(
        functools.partial(sums_kernel, (len(to_chips), len(to_hidden), len(to_rows)), len(after)),
        in_specs=[INSIDE] * len(given) + [ANYWHERE] * len(after),
        out_specs=[INSIDE] * len(shapes),
        out_shape=[jax.ShapeDtypeStruct(shape, BF16) for shape in shapes],
        compiler_params=pltpu.CompilerParams(vmem_limit_bytes=VMEM),
        cost_estimate=cost(0, 4000000),
        name="sums",
    )(*given, *after))
    sent = [results.pop(0) for _ in range(chips - 1)] if to_chips else []
    hidden = results.pop(0) if to_hidden else None
    summed = results.pop(0) if to_rows else None
    return sent, hidden, summed


def swap(values, axis, size, step):
    return lax.ppermute(values, axis, [(place, place ^ step) for place in range(size)])


def body(row_count, col_count, tokens, norm_gain, gate_weight, up_weight, down_weight, gate_mask, up_mask, down_mask):
    chips = row_count // CORES
    per_plane = col_count // PLANES
    features, width = gate_weight.shape
    row = lax.axis_index("rows")
    core = row % CORES
    place = jnp.reshape(core, (1,)).astype(jnp.int32)
    nowhere = jnp.zeros((1,), jnp.int32)

    normed = rms_normed(tokens, norm_gain)
    blocks = []
    for step in [chip * CORES + other for other in range(CORES) for chip in range(chips)]:
        block = lax.dynamic_slice_in_dim(normed, (row ^ step) * features, features, 1)
        blocks.append(swap(block, "rows", row_count, step) if step else block)
    mine = jnp.concatenate(blocks, 0)

    order = [0, *range(1, PLANES, 2), *range(2, PLANES, 2)]
    planes = {0: mine}
    for plane in order[1:]:
        planes[plane] = swap(mine, "cols", col_count, plane * per_plane)
    parts = {}
    for plane in order:
        parts[plane] = [planes[plane]]
        for step in range(1, per_plane):
            parts[plane].append(swap(planes[plane], "cols", col_count, step))

    gate_kept = masked(gate_weight, gate_mask, tile_of(features, 256), nowhere, 1, [])
    up_kept = masked(up_weight, up_mask, tile_of(features, 256), nowhere, 1, [gate_kept])

    halves, came, chip_sums, hiddens, others, partials, rows_in = {}, {}, {}, {}, {}, {}, {}
    last = [up_kept]
    down_kept = None
    arrived = []
    steps = len(order)
    for number in range(steps + 3):
        now, before, earlier, first = (
            order[at] if 0 <= at < steps else None for at in range(number, number - 4, -1)
        )
        if now is not None:
            halves[now] = gate_up(parts[now], gate_kept, up_kept, chips, last)
            came[now] = [swap(part, "rows", row_count, 1) for part in halves[now][1:]]
            last = [halves[now][0]]
        if number == 0:
            down_kept = masked(down_weight, down_mask, 2 * BLOCK, place, CORES, last + [planes[1], planes[order[2]]])
            last = [down_kept]
        if earlier is not None:
            partials[earlier] = down(hiddens[earlier], others[earlier], down_kept, last)
            last = [partials[earlier][0]]
            rows_in[earlier] = [partials[earlier][0]]
            for step in range(1, per_plane):
                rows_in[earlier].append(swap(partials[earlier][step], "cols", col_count, step))
        to_chips = [halves[now][0], *came[now]] if now is not None else []
        to_hidden = [halves[before][0], *came[before], *chip_sums[before]] if before is not None else []
        to_rows = rows_in[first] if first is not None else []
        sent, hidden, summed = sums(to_chips, to_hidden, to_rows, last)
        last = (sent + [hidden, summed])[:1]
        if sent:
            chip_sums[now] = [
                swap(part, "rows", row_count, (chip + 1) * CORES) for chip, part in enumerate(sent)
            ]
        if hidden is not None:
            hiddens[before] = hidden
            others[before] = swap(hidden, "rows", row_count, 1)
            last = [hidden]
        if summed is not None:
            last = [summed]
            arrived.append(swap(summed, "cols", col_count, first * per_plane) if first else summed)

    total = arrived[0].astype(F32)
    for part in arrived[1:]:
        total = total + part.astype(F32)
    mine_now = total[0].astype(BF16)
    other = swap(total[1].astype(BF16), "rows", row_count, 1)
    left = jnp.where(core == 0, mine_now, other)
    right = jnp.where(core == 0, other, mine_now)
    return jnp.concatenate([left, right], 1)


def solution(mesh):
    return jax.shard_map(
        functools.partial(body, mesh.shape["rows"], mesh.shape["cols"]),
        mesh=mesh,
        in_specs=(
            P(("rows", "cols"), None),
            P(),
            P("rows", "cols"),
            P("rows", "cols"),
            P("cols", None),
            P("rows", "cols"),
            P("rows", "cols"),
            P("cols", None),
        ),
        out_specs=P(("rows", "cols"), None),
        check_vma=False,
    )
```

time: 616 us -> 248 us (0.40)
  waiting for transfers between devices: 421 us -> 93.6 us
  matrix products: 77.5 us -> 0 us
  Pallas kernels: 0 us -> 72.2 us
  starting transfers between devices: 0.13 us -> 63.7 us
  local copies, waits for them, and re-layouts: 58.6 us -> 12.7 us
  other arithmetic: 43.1 us -> 4.78 us
  between operations: 13.3 us -> 0.36 us
    all_gather x3 -> x0, waiting for transfers between devices: 318 us -> none  [the longest x1 167 us: body(): lax.all_gather(gate_kept, 'rows', axis=0, tiled=True)]
    reduce_scatter x1 -> x0, waiting for transfers between devices: 103 us -> none  [body(): lax.psum_scatter(rounded_dot(hidden, down_kept).astype(jnp.bfloat16), 'co...]
    ppermute x0 -> x34, waiting for transfers between devices: none -> 93.6 us  [swap(): lax.ppermute(values, axis, [(place, place ^ step) for place in range(size)])]
    dot_general x9 -> x0, matrix products: 77.5 us -> none  [rounded_dot(): jnp.dot(left, right, preferred_element_type=jnp.float32)]
    pallas_call x0 -> x18, Pallas kernels: none -> 72.2 us  [the longest x4 28.9 us: gate_up(): pl.pallas_call(functools.partial(gate_up_kernel, len(parts), len(after)),...]
    ppermute x0 -> x34, starting transfers between devices: none -> 63.7 us  [swap(): lax.ppermute(values, axis, [(place, place ^ step) for place in range(size)])]
    unnamed x19 -> x22, local copies, waits for them, and re-layouts: 57.4 us -> 6.58 us
    mul x3 -> x0, other arithmetic: 33.9 us -> none  [the longest x1 20.3 us: body(): down_kept = down_weight * expand(down_mask)]
  transfers between devices with their start and end apart: 4 -> 34, of which waited for: 3 -> 14; matrix products, arithmetic and copies ran while one was open for 21% -> 2% of each run, Pallas kernels for 0% -> 29%
where the time goes in v2:
time: 248 us; the launch traced here: 247 us
  waiting for transfers between devices  93.6 us (38%)
  Pallas kernels  72.2 us (29%)
  starting transfers between devices  63.7 us (26%)
  local copies, waits for them, and re-layouts  12.7 us (5%)
  other arithmetic  4.78 us (2%)
    ppermute x34, waiting for transfers between devices, swap(): lax.ppermute(values, axis, [(place, place ^ step) for place in range(size)])  93.6 us
    ppermute x34, starting transfers between devices, swap(): lax.ppermute(values, axis, [(place, place ^ step) for place in range(size)])  63.7 us
    pallas_call x4, Pallas kernels, gate_up(): pl.pallas_call(functools.partial(gate_up_kernel, len(parts), len(after)),...  28.9 us
    pallas_call x3, Pallas kernels, masked(): pl.pallas_call(mask_kernel, grid_spec=pltpu.PrefetchScalarGridSpec(num_sc...  23.2 us
    pallas_call x4, Pallas kernels, down(): pl.pallas_call(functools.partial(down_kernel, len(after)), in_specs=[INSI...  15.5 us
    unnamed x22, local copies, waits for them, and re-layouts  6.58 us
  transfers between devices with their start and end apart: 34, of which 14 were waited for; matrix products, arithmetic and copies ran while one was open for 2% of the time, Pallas kernels for 29%

profile of v2, /device:TPU:0, one launch (start us, length us, event | category | flops | bytes accessed | tf_op | source)
XLA Modules:
  0.0 247.4 jit_solution(11919427586586857555)
XLA Ops:
  0.0 1.3 fusion
  1.3 1.3 fusion.2
  2.7 3.0 %collective-permute-start = (bf16[40,2048]{1,0:T(8,128)(2,1)S(1)}, bf16[40,2048]{1,0:T(8,128)(2,1)S(1)}, u32[]{:S(2)}, u32[]{:S(2)}) collective-permute-start(bf16[40,2048]{1,0:T(8,128)(2,1)S(1)} %get-tuple-element.68), channel_id=1, source_target_pairs={{0,16},{8,24},{16,0},{24,8},{1,17},{9,25},{17,1},{25,9},{2,18},{10... | collective-permute-start | bytes 491528 | tf_op jit(solution)/shard_map/ppermute | solution.py:216
  6.0 4.8 %collective-permute-done = bf16[40,2048]{1,0:T(8,128)(2,1)S(1)} collective-permute-done((bf16[40,2048]{1,0:T(8,128)(2,1)S(1)}, bf16[40,2048]{1,0:T(8,128)(2,1)S(1)}, u32[]{:S(2)}, u32[]{:S(2)}) %collective-permute-start) | collective-permute-done | bytes 163872 | tf_op jit(solution)/shard_map/ppermute | solution.py:216
  10.8 1.9 collective-permute-done.2
  13.6 1.6 collective-permute-start.7
  15.2 1.5 collective-permute-start.9
  17.7 5.5 %masked.3.refs_0_.refs_2_ = bf16[2048,1792]{1,0:T(8,128)(2,1)S(1)} custom-call(s32[1]{0:T(128)} %constant.34.clone.1.core_ref, bf16[2048,1792]{1,0:T(8,128)(2,1)} %weight_ref.3, f32[32,1,1792]{2,1,0:T(1,128)S(1)} %convert_element_type.82.mask_ref), custom_call_target="tpu_custom_call" | custom-call | bytes 3670016 | tf_op jit(solution)/shard_map/masked/pallas_call | solution.py:63
  23.2 7.5 %masked.4.refs_3_.refs_4_ = bf16[2048,1792]{1,0:T(8,128)(2,1)S(1)} custom-call(s32[1]{0:T(128)} %constant.34.clone.1.core_ref, bf16[2048,1792]{1,0:T(8,128)(2,1)} %weight_ref.4, f32[32,1,1792]{2,1,0:T(1,128)S(1)} %convert_element_type.83.mask_ref, bf16[2048,1792]{1,0:T(8,128)(2,1)S(1)} %masked.3.refs_0_.refs_2_), custom_call_target="tpu_custom_call" | custom-call | bytes 3670016 | tf_op jit(solution)/shard_map/masked/pallas_call | solution.py:63
  30.7 2.5 %collective-permute-start.5 = (bf16[160,2048]{1,0:T(8,128)(2,1)}, bf16[160,2048]{1,0:T(8,128)(2,1)}, u32[]{:S(2)}, u32[]{:S(2)}) collective-permute-start(bf16[160,2048]{1,0:T(8,128)(2,1)} %pad_maximum_fusion.refs_0_), channel_id=1, source_target_pairs={{0,6},{1,7},{2,4},{3,5},{4,2},{5,3},{6,0},{7,1},{8,14},{9,15},{10,... | collective-permute-start | bytes 1966088 | tf_op jit(solution)/shard_map/ppermute | solution.py:216
  33.8 8.2 %gate_up.4 = (bf16[2,2,2,40,1792]{4,3,2,1,0:T(8,128)(2,1)S(1)}, bf16[2,2,40,1792]{3,2,1,0:T(8,128)(2,1)}, bf16[2,2,40,1792]{3,2,1,0:T(8,128)(2,1)}) custom-call(bf16[160,2048]{1,0:T(8,128)(2,1)} %pad_maximum_fusion.refs_0_, bf16[160,2048]{1,0:T(8,128)(2,1)S(1)} %collective-permute-done.9.refs_1_, bf16[2048,1792]{1,0:T(8,128)(2,1)S(1)} %masked.3.refs_0_.refs_2_, ...), custom_call_target="tpu_custom_call" | custom-call | flops 1174405120 | tf_op jit(solution)/shard_map/gate_up/pallas_call | solution.py:110
  43.5 1.8 broadcast_in_dim.16
  45.3 3.4 %convert_element_type.84.mask_ref = f32[28,1,8192]{2,1,0:T(1,128)} reshape(f32[28,128,64]{2,1,0:T(8,128)} %broadcast_in_dim.16) | data formatting | bytes 1835008 | tf_op jit(solution)/shard_map/convert_element_type | solution.py:26
  48.7 2.0 collective-permute-start.3
  51.6 1.3 copy-done.4
  54.0 10.3 %masked.5.refs_3_.weight_ref = bf16[1792,4096]{1,0:T(8,128)(2,1)S(1)} custom-call(s32[1]{0:T(128)} %bitcast.core_ref, bf16[1792,8192]{1,0:T(8,128)(2,1)} %weight_ref.5, f32[28,1,8192]{2,1,0:T(1,128)S(1)} %copy-done.5, bf16[2,2,2,40,1792]{4,3,2,1,0:T(8,128)(2,1)S(1)} %copy-done.4, bf16[160,2048]{1,0:T(8,128)(2,1)} %collective-permute-done.7.refs_1_.refs_0_, ...), custom_call_target="tpu_custom_call" | custom-call | bytes 7340032 | tf_op jit(solution)/shard_map/masked/pallas_call | solution.py:63
  64.3 1.4 sums.7.refs_4_
  65.7 1.6 collective-permute-start.14
  67.2 3.1 %copy-done.2 = bf16[2048,1792]{1,0:T(8,128)(2,1)S(1)} copy-done((bf16[2048,1792]{1,0:T(8,128)(2,1)S(1)}, bf16[2048,1792]{1,0:T(8,128)(2,1)}, u32[]{:S(2)}) %copy-start.2) | copy-done | bytes 7340056
  70.3 7.4 %gate_up.5 = (bf16[2,2,2,40,1792]{4,3,2,1,0:T(8,128)(2,1)S(1)}, bf16[2,2,40,1792]{3,2,1,0:T(8,128)(2,1)S(1)}, bf16[2,2,40,1792]{3,2,1,0:T(8,128)(2,1)S(1)}) custom-call(bf16[160,2048]{1,0:T(8,128)(2,1)} %collective-permute-done.7.refs_1_.refs_0_, bf16[160,2048]{1,0:T(8,128)(2,1)} %collective-permute-done.8.refs_1_, bf16[2048,1792]{1,0:T(8,128)(2,1)S(1)} %bitcast.10, ...), custom_call_target="tpu_custom_call" | custom-call | flops 1174405120 | tf_op jit(solution)/shard_map/gate_up/pallas_call | solution.py:110
  78.3 12.6 %collective-permute-done.3.refs_0_ = bf16[160,2048]{1,0:T(8,128)(2,1)S(1)} collective-permute-done((bf16[160,2048]{1,0:T(8,128)(2,1)}, bf16[160,2048]{1,0:T(8,128)(2,1)S(1)}, u32[]{:S(2)}, u32[]{:S(2)}) %collective-permute-start.3) | collective-permute-done | bytes 655392 | tf_op jit(solution)/shard_map/ppermute | solution.py:216
  91.4 1.6 sums.8
  93.0 7.2 %gate_up.6 = (bf16[2,2,2,40,1792]{4,3,2,1,0:T(8,128)(2,1)S(1)}, bf16[2,2,40,1792]{3,2,1,0:T(8,128)(2,1)S(1)}, bf16[2,2,40,1792]{3,2,1,0:T(8,128)(2,1)S(1)}) custom-call(bf16[160,2048]{1,0:T(8,128)(2,1)} %collective-permute-done.5.refs_2_.refs_0_, bf16[160,2048]{1,0:T(8,128)(2,1)S(1)} %collective-permute-done.6.refs_1_, bf16[2048,1792]{1,0:T(8,128)(2,1)S(1)} %bitcast.10, ...), custom_call_target="tpu_custom_call" | custom-call | flops 1174405120 | tf_op jit(solution)/shard_map/gate_up/pallas_call | solution.py:110
  100.8 1.5 collective-permute-start.17
  102.3 1.6 collective-permute-done.18.other_ref
  103.9 3.9 %down.4 = (bf16[2,40,4096]{2,1,0:T(8,128)(2,1)S(1)}, bf16[2,40,4096]{2,1,0:T(8,128)(2,1)S(1)}) custom-call(bf16[2,40,1792]{2,1,0:T(8,128)(2,1)S(1)} %get-tuple-element.40.refs_4_.own_ref, bf16[2,40,1792]{2,1,0:T(8,128)(2,1)S(1)} %collective-permute-done.18.other_ref, bf16[1792,4096]{1,0:T(8,128)(2,1)S(1)} %masked.5.refs_3_.weight_ref, ...), custom_call_target="tpu_custom_call" | custom-call | flops 587202560 | tf_op jit(solution)/shard_map/down/pallas_call | solution.py:143
  107.7 1.6 collective-permute-start.22
  109.3 6.4 %collective-permute-done.17.refs_6_ = bf16[2,2,40,1792]{3,2,1,0:T(8,128)(2,1)S(1)} collective-permute-done((bf16[2,2,40,1792]{3,2,1,0:T(8,128)(2,1)S(1)}, bf16[2,2,40,1792]{3,2,1,0:T(8,128)(2,1)S(1)}, u32[]{:S(2)}, u32[]{:S(2)}) %collective-permute-start.17) | collective-permute-done | bytes 573472 | tf_op jit(solution)/shard_map/ppermute | solution.py:216
  116.2 6.1 %gate_up.7 = (bf16[2,2,2,40,1792]{4,3,2,1,0:T(8,128)(2,1)S(1)}, bf16[2,2,40,1792]{3,2,1,0:T(8,128)(2,1)S(1)}, bf16[2,2,40,1792]{3,2,1,0:T(8,128)(2,1)S(1)}) custom-call(bf16[160,2048]{1,0:T(8,128)(2,1)S(1)} %collective-permute-done.3.refs_0_, bf16[160,2048]{1,0:T(8,128)(2,1)S(1)} %collective-permute-done.4.refs_1_, bf16[2048,1792]{1,0:T(8,128)(2,1)S(1)} %bitcast.10, ...), custom_call_target="tpu_custom_call" | custom-call | flops 1174405120 | tf_op jit(solution)/shard_map/gate_up/pallas_call | solution.py:110
  122.9 1.5 collective-permute-start.21
  124.3 1.6 collective-permute-done.23.other_ref
  125.9 3.9 %down.5 = (bf16[2,40,4096]{2,1,0:T(8,128)(2,1)S(1)}, bf16[2,40,4096]{2,1,0:T(8,128)(2,1)S(1)}) custom-call(bf16[2,40,1792]{2,1,0:T(8,128)(2,1)S(1)} %get-tuple-element.46.refs_4_.own_ref, bf16[2,40,1792]{2,1,0:T(8,128)(2,1)S(1)} %collective-permute-done.23.other_ref, bf16[1792,4096]{1,0:T(8,128)(2,1)S(1)} %masked.5.refs_3_.weight_ref, ...), custom_call_target="tpu_custom_call" | custom-call | flops 587202560 | tf_op jit(solution)/shard_map/down/pallas_call | solution.py:143
  129.8 1.6 collective-permute-start.25
  131.4 6.4 %collective-permute-done.21.refs_6_ = bf16[2,2,40,1792]{3,2,1,0:T(8,128)(2,1)S(1)} collective-permute-done((bf16[2,2,40,1792]{3,2,1,0:T(8,128)(2,1)S(1)}, bf16[2,2,40,1792]{3,2,1,0:T(8,128)(2,1)S(1)}, u32[]{:S(2)}, u32[]{:S(2)}) %collective-permute-start.21) | collective-permute-done | bytes 573472 | tf_op jit(solution)/shard_map/ppermute | solution.py:216
  138.4 1.5 collective-permute-start.24
  139.9 1.6 collective-permute-done.26.other_ref
  141.5 3.9 %down.6 = (bf16[2,40,4096]{2,1,0:T(8,128)(2,1)S(1)}, bf16[2,40,4096]{2,1,0:T(8,128)(2,1)S(1)}) custom-call(bf16[2,40,1792]{2,1,0:T(8,128)(2,1)S(1)} %get-tuple-element.56.own_ref, bf16[2,40,1792]{2,1,0:T(8,128)(2,1)S(1)} %collective-permute-done.26.other_ref, bf16[1792,4096]{1,0:T(8,128)(2,1)S(1)} %masked.5.refs_3_.weight_ref, ...), custom_call_target="tpu_custom_call" | custom-call | flops 587202560 | tf_op jit(solution)/shard_map/down/pallas_call | solution.py:143
  146.6 5.9 %collective-permute-done.24.refs_3_ = bf16[2,2,40,1792]{3,2,1,0:T(8,128)(2,1)S(1)} collective-permute-done((bf16[2,2,40,1792]{3,2,1,0:T(8,128)(2,1)S(1)}, bf16[2,2,40,1792]{3,2,1,0:T(8,128)(2,1)S(1)}, u32[]{:S(2)}, u32[]{:S(2)}) %collective-permute-start.24) | collective-permute-done | bytes 573472 | tf_op jit(solution)/shard_map/ppermute | solution.py:216
  153.1 1.6 collective-permute-start.28
  154.6 3.9 %down.7 = (bf16[2,40,4096]{2,1,0:T(8,128)(2,1)S(1)}, bf16[2,40,4096]{2,1,0:T(8,128)(2,1)S(1)}) custom-call(bf16[2,40,1792]{2,1,0:T(8,128)(2,1)S(1)} %get-tuple-element.60.own_ref, bf16[2,40,1792]{2,1,0:T(8,128)(2,1)S(1)} %collective-permute-done.29.other_ref, bf16[1792,4096]{1,0:T(8,128)(2,1)S(1)} %masked.5.refs_3_.weight_ref, ...), custom_call_target="tpu_custom_call" | custom-call | flops 587202560 | tf_op jit(solution)/shard_map/down/pallas_call | solution.py:143
  158.5 1.6 collective-permute-start.31
  160.1 15.9 %collective-permute-start.27 = (bf16[2,40,4096]{2,1,0:T(8,128)(2,1)S(1)}, bf16[2,40,4096]{2,1,0:T(8,128)(2,1)S(1)}, u32[]{:S(2)}, u32[]{:S(2)}) collective-permute-start(bf16[2,40,4096]{2,1,0:T(8,128)(2,1)S(1)} %get-tuple-element.58.refs_0_), channel_id=1, source_target_pairs={{0,2},{1,3},{2,0},{3,1},{4,6},{5,7},{6,4},{7,5},{8,10},{9,11},{10,... | collective-permute-start | bytes 1966088 | tf_op jit(solution)/shard_map/ppermute | solution.py:216
  176.2 2.9 %collective-permute-start.30 = (bf16[2,40,4096]{2,1,0:T(8,128)(2,1)S(1)}, bf16[2,40,4096]{2,1,0:T(8,128)(2,1)S(1)}, u32[]{:S(2)}, u32[]{:S(2)}) collective-permute-start(bf16[2,40,4096]{2,1,0:T(8,128)(2,1)S(1)} %sums.12.refs_2_), channel_id=1, source_target_pairs={{0,6},{1,7},{2,4},{3,5},{4,2},{5,3},{6,0},{7,1},{8,14},{9,15},{10,... | collective-permute-start | bytes 1966088 | tf_op jit(solution)/shard_map/ppermute | solution.py:216
  179.1 5.2 %collective-permute-done.31.refs_1_ = bf16[2,40,4096]{2,1,0:T(8,128)(2,1)S(1)} collective-permute-done((bf16[2,40,4096]{2,1,0:T(8,128)(2,1)S(1)}, bf16[2,40,4096]{2,1,0:T(8,128)(2,1)S(1)}, u32[]{:S(2)}, u32[]{:S(2)}) %collective-permute-start.31) | collective-permute-done | bytes 655392 | tf_op jit(solution)/shard_map/ppermute | solution.py:216
  184.4 17.4 %collective-permute-start.32 = (bf16[2,40,4096]{2,1,0:T(8,128)(2,1)S(1)}, bf16[2,40,4096]{2,1,0:T(8,128)(2,1)S(1)}, u32[]{:S(2)}, u32[]{:S(2)}) collective-permute-start(bf16[2,40,4096]{2,1,0:T(8,128)(2,1)S(1)} %sums.13), channel_id=1, source_target_pairs={{0,4},{1,5},{2,6},{3,7},{4,0},{5,1},{6,2},{7,3},{8,12},{9,13},{10,... | collective-permute-start | bytes 1966088 | tf_op jit(solution)/shard_map/ppermute | solution.py:216
  201.8 6.8 %collective-permute-done.30 = bf16[2,40,4096]{2,1,0:T(8,128)(2,1)S(1)} collective-permute-done((bf16[2,40,4096]{2,1,0:T(8,128)(2,1)S(1)}, bf16[2,40,4096]{2,1,0:T(8,128)(2,1)S(1)}, u32[]{:S(2)}, u32[]{:S(2)}) %collective-permute-start.30) | collective-permute-done | bytes 655392 | tf_op jit(solution)/shard_map/ppermute | solution.py:216
  208.6 35.8 %collective-permute-done.32 = bf16[2,40,4096]{2,1,0:T(8,128)(2,1)S(1)} collective-permute-done((bf16[2,40,4096]{2,1,0:T(8,128)(2,1)S(1)}, bf16[2,40,4096]{2,1,0:T(8,128)(2,1)S(1)}, u32[]{:S(2)}, u32[]{:S(2)}) %collective-permute-start.32) | collective-permute-done | bytes 655392 | tf_op jit(solution)/shard_map/ppermute | solution.py:216
  244.9 1.6 collective-permute-done.33
  (79 shorter events, 12.9 us)
Async XLA Ops:
  2.7 14.0 %copy-start.6 = (s32[32,28]{1,0:T(8,128)S(1)}, s32[32,28]{1,0:T(8,128)}, u32[]{:S(2)}) copy-start(s32[32,28]{1,0:T(8,128)} %param.13) | copy-start | bytes 10756
  2.7 8.0 %collective-permute-start = (bf16[40,2048]{1,0:T(8,128)(2,1)S(1)}, bf16[40,2048]{1,0:T(8,128)(2,1)S(1)}, u32[]{:S(2)}, u32[]{:S(2)}) collective-permute-start(bf16[40,2048]{1,0:T(8,128)(2,1)S(1)} %get-tuple-element.68), channel_id=1, source_target_pairs={{0,16},{8,24},{16,0},{24,8},{1,17},{9,25},{17,1},{25,9},{2,18},{10... | collective-permute-start | bytes 491528 | tf_op jit(solution)/shard_map/ppermute | solution.py:216
  5.7 5.0 %collective-permute-start.1 = (bf16[40,2048]{1,0:T(8,128)(2,1)S(1)}, bf16[40,2048]{1,0:T(8,128)(2,1)S(1)}, u32[]{:S(2)}, u32[]{:S(2)}) collective-permute-start(bf16[40,2048]{1,0:T(8,128)(2,1)S(1)} %get-tuple-element.67), channel_id=1, source_target_pairs={{0,8},{8,0},{16,24},{24,16},{1,9},{9,1},{17,25},{25,17},{2,10},{10... | collective-permute-start | bytes 491528 | tf_op jit(solution)/shard_map/ppermute | solution.py:216
  5.8 7.0 %collective-permute-start.2 = (bf16[40,2048]{1,0:T(8,128)(2,1)S(1)}, bf16[40,2048]{1,0:T(8,128)(2,1)S(1)}, u32[]{:S(2)}, u32[]{:S(2)}) collective-permute-start(bf16[40,2048]{1,0:T(8,128)(2,1)S(1)} %get-tuple-element.66), channel_id=1, source_target_pairs={{0,24},{8,16},{16,8},{24,0},{1,25},{9,17},{17,9},{25,1},{2,26},{10... | collective-permute-start | bytes 491528 | tf_op jit(solution)/shard_map/ppermute | solution.py:216
  12.7 4.5 %copy-start.7 = (s32[32,28]{1,0:T(8,128)S(1)}, s32[32,28]{1,0:T(8,128)}, u32[]{:S(2)}) copy-start(s32[32,28]{1,0:T(8,128)} %param.14) | copy-start | bytes 10756
  13.6 19.7 %collective-permute-start.7 = (bf16[160,2048]{1,0:T(8,128)(2,1)}, bf16[160,2048]{1,0:T(8,128)(2,1)}, u32[]{:S(2)}, u32[]{:S(2)}) collective-permute-start(bf16[160,2048]{1,0:T(8,128)(2,1)} %pad_maximum_fusion.refs_0_), channel_id=1, source_target_pairs={{0,2},{1,3},{2,0},{3,1},{4,6},{5,7},{6,4},{7,5},{8,10},{9,11},{10,... | collective-permute-start | bytes 1966088 | tf_op jit(solution)/shard_map/ppermute | solution.py:216
  15.2 18.6 %collective-permute-start.9 = (bf16[160,2048]{1,0:T(8,128)(2,1)}, bf16[160,2048]{1,0:T(8,128)(2,1)S(1)}, u32[]{:S(2)}, u32[]{:S(2)}) collective-permute-start(bf16[160,2048]{1,0:T(8,128)(2,1)} %pad_maximum_fusion.refs_0_), channel_id=1, source_target_pairs={{0,1},{1,0},{2,3},{3,2},{4,5},{5,4},{6,7},{7,6},{8,9},{9,8},{10,11... | collective-permute-start | bytes 1966088 | tf_op jit(solution)/shard_map/ppermute | solution.py:216
  23.2 10.6 %copy-start = (bf16[2048,1792]{1,0:T(8,128)(2,1)}, bf16[2048,1792]{1,0:T(8,128)(2,1)S(1)}, u32[]{:S(2)}) copy-start(bf16[2048,1792]{1,0:T(8,128)(2,1)S(1)} %masked.3.refs_0_.refs_2_) | copy-start | bytes 22020100
  30.7 11.3 %copy-start.1 = (bf16[2048,1792]{1,0:T(8,128)(2,1)}, bf16[2048,1792]{1,0:T(8,128)(2,1)S(1)}, u32[]{:S(2)}) copy-start(bf16[2048,1792]{1,0:T(8,128)(2,1)S(1)} %masked.4.refs_3_.refs_4_) | copy-start | bytes 22020100
  30.7 12.8 %copy-start.8 = (s32[28,128]{1,0:T(8,128)S(1)}, s32[28,128]{1,0:T(8,128)}, u32[]{:S(2)}) copy-start(s32[28,128]{1,0:T(8,128)} %param.15) | copy-start | bytes 43012
  30.7 19.9 %collective-permute-start.5 = (bf16[160,2048]{1,0:T(8,128)(2,1)}, bf16[160,2048]{1,0:T(8,128)(2,1)}, u32[]{:S(2)}, u32[]{:S(2)}) collective-permute-start(bf16[160,2048]{1,0:T(8,128)(2,1)} %pad_maximum_fusion.refs_0_), channel_id=1, source_target_pairs={{0,6},{1,7},{2,4},{3,5},{4,2},{5,3},{6,0},{7,1},{8,14},{9,15},{10,... | collective-permute-start | bytes 1966088 | tf_op jit(solution)/shard_map/ppermute | solution.py:216
  33.3 34.0 %collective-permute-start.8 = (bf16[160,2048]{1,0:T(8,128)(2,1)}, bf16[160,2048]{1,0:T(8,128)(2,1)}, u32[]{:S(2)}, u32[]{:S(2)}) collective-permute-start(bf16[160,2048]{1,0:T(8,128)(2,1)} %collective-permute-done.7.refs_1_.refs_0_), channel_id=1, source_target_pairs={{0,1},{1,0},{2,3},{3,2},{4,5},{5,4},{6,7},{7,6},{8,9},{9,8},{10,11... | collective-permute-start | bytes 1966088 | tf_op jit(solution)/shard_map/ppermute | solution.py:216
  42.0 1.0 copy-start.3
  43.0 21.3 %collective-permute-start.10 = (bf16[2,2,40,1792]{3,2,1,0:T(8,128)(2,1)}, bf16[2,2,40,1792]{3,2,1,0:T(8,128)(2,1)}, u32[]{:S(2)}, u32[]{:S(2)}) collective-permute-start(bf16[2,2,40,1792]{3,2,1,0:T(8,128)(2,1)} %get-tuple-element.35), channel_id=1, source_target_pairs={{0,8},{8,0},{16,24},{24,16},{1,9},{9,1},{17,25},{25,17},{2,10},{10... | collective-permute-start | bytes 1720328 | tf_op jit(solution)/shard_map/ppermute | solution.py:216
  43.0 21.3 %collective-permute-start.11 = (bf16[2,2,40,1792]{3,2,1,0:T(8,128)(2,1)}, bf16[2,2,40,1792]{3,2,1,0:T(8,128)(2,1)}, u32[]{:S(2)}, u32[]{:S(2)}) collective-permute-start(bf16[2,2,40,1792]{3,2,1,0:T(8,128)(2,1)} %get-tuple-element.36), channel_id=1, source_target_pairs={{0,8},{8,0},{16,24},{24,16},{1,9},{9,1},{17,25},{25,17},{2,10},{10... | collective-permute-start | bytes 1720328 | tf_op jit(solution)/shard_map/ppermute | solution.py:216
  45.3 21.9 %slice-start = ((s8[7340032]{0:T(1024)(128)(4,1)}), s8[3145728]{0:T(1024)(128)(4,1)S(1)}, s32[]{:S(2)}) async-start(s8[7340032]{0:T(1024)(128)(4,1)} %bitcast.9), calls=%async_computation | async-start | bytes 6291456
  48.7 42.2 %collective-permute-start.3 = (bf16[160,2048]{1,0:T(8,128)(2,1)}, bf16[160,2048]{1,0:T(8,128)(2,1)S(1)}, u32[]{:S(2)}, u32[]{:S(2)}) collective-permute-start(bf16[160,2048]{1,0:T(8,128)(2,1)} %pad_maximum_fusion.refs_0_), channel_id=1, source_target_pairs={{0,4},{1,5},{2,6},{3,7},{4,0},{5,1},{6,2},{7,3},{8,12},{9,13},{10,... | collective-permute-start | bytes 1966088 | tf_op jit(solution)/shard_map/ppermute | solution.py:216
  50.7 42.4 %collective-permute-start.6 = (bf16[160,2048]{1,0:T(8,128)(2,1)}, bf16[160,2048]{1,0:T(8,128)(2,1)S(1)}, u32[]{:S(2)}, u32[]{:S(2)}) collective-permute-start(bf16[160,2048]{1,0:T(8,128)(2,1)} %collective-permute-done.5.refs_2_.refs_0_), channel_id=1, source_target_pairs={{0,1},{1,0},{2,3},{3,2},{4,5},{5,4},{6,7},{7,6},{8,9},{9,8},{10,11... | collective-permute-start | bytes 1966088 | tf_op jit(solution)/shard_map/ppermute | solution.py:216
  51.6 1.3 copy-start.4
  52.8 1.2 copy-start.5
  54.0 13.2 %slice-start.1 = ((s8[7340032]{0:T(1024)(128)(4,1)}), s8[4194304]{0:T(1024)(128)(4,1)S(1)}, s32[]{:S(2)}) async-start(s8[7340032]{0:T(1024)(128)(4,1)} %bitcast.9), calls=%async_computation.1 | async-start | bytes 8388608
  65.7 25.7 %collective-permute-start.14 = (bf16[2,2,40,1792]{3,2,1,0:T(8,128)(2,1)S(1)}, bf16[2,2,40,1792]{3,2,1,0:T(8,128)(2,1)S(1)}, u32[]{:S(2)}, u32[]{:S(2)}) collective-permute-start(bf16[2,2,40,1792]{3,2,1,0:T(8,128)(2,1)S(1)} %sums.7.refs_4_), channel_id=1, source_target_pairs={{0,16},{8,24},{16,0},{24,8},{1,17},{9,25},{17,1},{25,9},{2,18},{10... | collective-permute-start | bytes 1720328 | tf_op jit(solution)/shard_map/ppermute | solution.py:216
  67.2 3.1 %copy-start.2 = (bf16[2048,1792]{1,0:T(8,128)(2,1)S(1)}, bf16[2048,1792]{1,0:T(8,128)(2,1)}, u32[]{:S(2)}) copy-start(bf16[2048,1792]{1,0:T(8,128)(2,1)} %copy-done.1) | copy-start | bytes 22020100
  77.7 13.7 %collective-permute-start.12 = (bf16[2,2,40,1792]{3,2,1,0:T(8,128)(2,1)S(1)}, bf16[2,2,40,1792]{3,2,1,0:T(8,128)(2,1)S(1)}, u32[]{:S(2)}, u32[]{:S(2)}) collective-permute-start(bf16[2,2,40,1792]{3,2,1,0:T(8,128)(2,1)S(1)} %get-tuple-element.38), channel_id=1, source_target_pairs={{0,8},{8,0},{16,24},{24,16},{1,9},{9,1},{17,25},{25,17},{2,10},{10... | collective-permute-start | bytes 1720328 | tf_op jit(solution)/shard_map/ppermute | solution.py:216
  77.8 13.6 %collective-permute-start.13 = (bf16[2,2,40,1792]{3,2,1,0:T(8,128)(2,1)S(1)}, bf16[2,2,40,1792]{3,2,1,0:T(8,128)(2,1)S(1)}, u32[]{:S(2)}, u32[]{:S(2)}) collective-permute-start(bf16[2,2,40,1792]{3,2,1,0:T(8,128)(2,1)S(1)} %get-tuple-element.39), channel_id=1, source_target_pairs={{0,8},{8,0},{16,24},{24,16},{1,9},{9,1},{17,25},{25,17},{2,10},{10... | collective-permute-start | bytes 1720328 | tf_op jit(solution)/shard_map/ppermute | solution.py:216
  90.9 25.3 %collective-permute-start.4 = (bf16[160,2048]{1,0:T(8,128)(2,1)S(1)}, bf16[160,2048]{1,0:T(8,128)(2,1)S(1)}, u32[]{:S(2)}, u32[]{:S(2)}) collective-permute-start(bf16[160,2048]{1,0:T(8,128)(2,1)S(1)} %collective-permute-done.3.refs_0_), channel_id=1, source_target_pairs={{0,1},{1,0},{2,3},{3,2},{4,5},{5,4},{6,7},{7,6},{8,9},{9,8},{10,11... | collective-permute-start | bytes 1966088 | tf_op jit(solution)/shard_map/ppermute | solution.py:216
  100.2 9.1 %collective-permute-start.15 = (bf16[2,2,40,1792]{3,2,1,0:T(8,128)(2,1)S(1)}, bf16[2,2,40,1792]{3,2,1,0:T(8,128)(2,1)S(1)}, u32[]{:S(2)}, u32[]{:S(2)}) collective-permute-start(bf16[2,2,40,1792]{3,2,1,0:T(8,128)(2,1)S(1)} %get-tuple-element.42), channel_id=1, source_target_pairs={{0,8},{8,0},{16,24},{24,16},{1,9},{9,1},{17,25},{25,17},{2,10},{10... | collective-permute-start | bytes 1720328 | tf_op jit(solution)/shard_map/ppermute | solution.py:216
  100.3 9.0 %collective-permute-start.16 = (bf16[2,2,40,1792]{3,2,1,0:T(8,128)(2,1)S(1)}, bf16[2,2,40,1792]{3,2,1,0:T(8,128)(2,1)S(1)}, u32[]{:S(2)}, u32[]{:S(2)}) collective-permute-start(bf16[2,2,40,1792]{3,2,1,0:T(8,128)(2,1)S(1)} %get-tuple-element.43), channel_id=1, source_target_pairs={{0,8},{8,0},{16,24},{24,16},{1,9},{9,1},{17,25},{25,17},{2,10},{10... | collective-permute-start | bytes 1720328 | tf_op jit(solution)/shard_map/ppermute | solution.py:216
  100.8 15.0 %collective-permute-start.17 = (bf16[2,2,40,1792]{3,2,1,0:T(8,128)(2,1)S(1)}, bf16[2,2,40,1792]{3,2,1,0:T(8,128)(2,1)S(1)}, u32[]{:S(2)}, u32[]{:S(2)}) collective-permute-start(bf16[2,2,40,1792]{3,2,1,0:T(8,128)(2,1)S(1)} %get-tuple-element.44), channel_id=1, source_target_pairs={{0,16},{8,24},{16,0},{24,8},{1,17},{9,25},{17,1},{25,9},{2,18},{10... | collective-permute-start | bytes 1720328 | tf_op jit(solution)/shard_map/ppermute | solution.py:216
  102.3 1.6 collective-permute-start.18
  107.7 23.7 %collective-permute-start.22 = (bf16[2,40,4096]{2,1,0:T(8,128)(2,1)S(1)}, bf16[2,40,4096]{2,1,0:T(8,128)(2,1)S(1)}, u32[]{:S(2)}, u32[]{:S(2)}) collective-permute-start(bf16[2,40,4096]{2,1,0:T(8,128)(2,1)S(1)} %get-tuple-element.51), channel_id=1, source_target_pairs={{0,1},{1,0},{2,3},{3,2},{4,5},{5,4},{6,7},{7,6},{8,9},{9,8},{10,11... | collective-permute-start | bytes 1966088 | tf_op jit(solution)/shard_map/ppermute | solution.py:216
  122.3 9.1 %collective-permute-start.19 = (bf16[2,2,40,1792]{3,2,1,0:T(8,128)(2,1)S(1)}, bf16[2,2,40,1792]{3,2,1,0:T(8,128)(2,1)S(1)}, u32[]{:S(2)}, u32[]{:S(2)}) collective-permute-start(bf16[2,2,40,1792]{3,2,1,0:T(8,128)(2,1)S(1)} %get-tuple-element.48), channel_id=1, source_target_pairs={{0,8},{8,0},{16,24},{24,16},{1,9},{9,1},{17,25},{25,17},{2,10},{10... | collective-permute-start | bytes 1720328 | tf_op jit(solution)/shard_map/ppermute | solution.py:216
  122.4 9.0 %collective-permute-start.20 = (bf16[2,2,40,1792]{3,2,1,0:T(8,128)(2,1)S(1)}, bf16[2,2,40,1792]{3,2,1,0:T(8,128)(2,1)S(1)}, u32[]{:S(2)}, u32[]{:S(2)}) collective-permute-start(bf16[2,2,40,1792]{3,2,1,0:T(8,128)(2,1)S(1)} %get-tuple-element.49), channel_id=1, source_target_pairs={{0,8},{8,0},{16,24},{24,16},{1,9},{9,1},{17,25},{25,17},{2,10},{10... | collective-permute-start | bytes 1720328 | tf_op jit(solution)/shard_map/ppermute | solution.py:216
  122.9 15.0 %collective-permute-start.21 = (bf16[2,2,40,1792]{3,2,1,0:T(8,128)(2,1)S(1)}, bf16[2,2,40,1792]{3,2,1,0:T(8,128)(2,1)S(1)}, u32[]{:S(2)}, u32[]{:S(2)}) collective-permute-start(bf16[2,2,40,1792]{3,2,1,0:T(8,128)(2,1)S(1)} %get-tuple-element.50), channel_id=1, source_target_pairs={{0,16},{8,24},{16,0},{24,8},{1,17},{9,25},{17,1},{25,9},{2,18},{10... | collective-permute-start | bytes 1720328 | tf_op jit(solution)/shard_map/ppermute | solution.py:216
  124.3 1.6 collective-permute-start.23
  129.8 16.8 %collective-permute-start.25 = (bf16[2,40,4096]{2,1,0:T(8,128)(2,1)S(1)}, bf16[2,40,4096]{2,1,0:T(8,128)(2,1)S(1)}, u32[]{:S(2)}, u32[]{:S(2)}) collective-permute-start(bf16[2,40,4096]{2,1,0:T(8,128)(2,1)S(1)} %get-tuple-element.55), channel_id=1, source_target_pairs={{0,1},{1,0},{2,3},{3,2},{4,5},{5,4},{6,7},{7,6},{8,9},{9,8},{10,11... | collective-permute-start | bytes 1966088 | tf_op jit(solution)/shard_map/ppermute | solution.py:216
  138.4 14.2 %collective-permute-start.24 = (bf16[2,2,40,1792]{3,2,1,0:T(8,128)(2,1)S(1)}, bf16[2,2,40,1792]{3,2,1,0:T(8,128)(2,1)S(1)}, u32[]{:S(2)}, u32[]{:S(2)}) collective-permute-start(bf16[2,2,40,1792]{3,2,1,0:T(8,128)(2,1)S(1)} %get-tuple-element.54), channel_id=1, source_target_pairs={{0,16},{8,24},{16,0},{24,8},{1,17},{9,25},{17,1},{25,9},{2,18},{10... | collective-permute-start | bytes 1720328 | tf_op jit(solution)/shard_map/ppermute | solution.py:216
  139.9 1.6 collective-permute-start.26
  153.0 1.7 collective-permute-start.29
  153.1 23.0 %collective-permute-start.28 = (bf16[2,40,4096]{2,1,0:T(8,128)(2,1)S(1)}, bf16[2,40,4096]{2,1,0:T(8,128)(2,1)S(1)}, u32[]{:S(2)}, u32[]{:S(2)}) collective-permute-start(bf16[2,40,4096]{2,1,0:T(8,128)(2,1)S(1)} %get-tuple-element.59), channel_id=1, source_target_pairs={{0,1},{1,0},{2,3},{3,2},{4,5},{5,4},{6,7},{7,6},{8,9},{9,8},{10,11... | collective-permute-start | bytes 1966088 | tf_op jit(solution)/shard_map/ppermute | solution.py:216
  158.5 25.7 %collective-permute-start.31 = (bf16[2,40,4096]{2,1,0:T(8,128)(2,1)S(1)}, bf16[2,40,4096]{2,1,0:T(8,128)(2,1)S(1)}, u32[]{:S(2)}, u32[]{:S(2)}) collective-permute-start(bf16[2,40,4096]{2,1,0:T(8,128)(2,1)S(1)} %get-tuple-element.62), channel_id=1, source_target_pairs={{0,1},{1,0},{2,3},{3,2},{4,5},{5,4},{6,7},{7,6},{8,9},{9,8},{10,11... | collective-permute-start | bytes 1966088 | tf_op jit(solution)/shard_map/ppermute | solution.py:216
  160.1 41.7 %collective-permute-start.27 = (bf16[2,40,4096]{2,1,0:T(8,128)(2,1)S(1)}, bf16[2,40,4096]{2,1,0:T(8,128)(2,1)S(1)}, u32[]{:S(2)}, u32[]{:S(2)}) collective-permute-start(bf16[2,40,4096]{2,1,0:T(8,128)(2,1)S(1)} %get-tuple-element.58.refs_0_), channel_id=1, source_target_pairs={{0,2},{1,3},{2,0},{3,1},{4,6},{5,7},{6,4},{7,5},{8,10},{9,11},{10,... | collective-permute-start | bytes 1966088 | tf_op jit(solution)/shard_map/ppermute | solution.py:216
  176.2 32.4 %collective-permute-start.30 = (bf16[2,40,4096]{2,1,0:T(8,128)(2,1)S(1)}, bf16[2,40,4096]{2,1,0:T(8,128)(2,1)S(1)}, u32[]{:S(2)}, u32[]{:S(2)}) collective-permute-start(bf16[2,40,4096]{2,1,0:T(8,128)(2,1)S(1)} %sums.12.refs_2_), channel_id=1, source_target_pairs={{0,6},{1,7},{2,4},{3,5},{4,2},{5,3},{6,0},{7,1},{8,14},{9,15},{10,... | collective-permute-start | bytes 1966088 | tf_op jit(solution)/shard_map/ppermute | solution.py:216
  184.4 60.0 %collective-permute-start.32 = (bf16[2,40,4096]{2,1,0:T(8,128)(2,1)S(1)}, bf16[2,40,4096]{2,1,0:T(8,128)(2,1)S(1)}, u32[]{:S(2)}, u32[]{:S(2)}) collective-permute-start(bf16[2,40,4096]{2,1,0:T(8,128)(2,1)S(1)} %sums.13), channel_id=1, source_target_pairs={{0,4},{1,5},{2,6},{3,7},{4,0},{5,1},{6,2},{7,3},{8,12},{9,13},{10,... | collective-permute-start | bytes 1966088 | tf_op jit(solution)/shard_map/ppermute | solution.py:216
  244.8 1.7 collective-permute-start.33

commit v3 on v2

--- a/solution.py
+++ b/solution.py
@@ -10,7 +10,7 @@
 BLOCK = 64
 CORES = 2
 PLANES = 4
-VMEM = 14 * 1024 * 1024
+VMEM = 12 * 1024 * 1024
 F32 = jnp.float32
 BF16 = jnp.bfloat16
 
@@ -22,10 +22,6 @@
     return tile
 
 
-def spread(mask):
-    return jnp.repeat(mask, BLOCK, 1).astype(F32)[:, None, :]
-
-
 def rms_normed(rows_in, norm_gain):
     values = rows_in.astype(F32)
     meansq = jnp.mean(values * values, axis=-1, keepdims=True)
@@ -36,7 +32,7 @@
     return pltpu.CompilerParams(dimension_semantics=semantics, vmem_limit_bytes=VMEM)
 
 
-HURRY = 4
+HURRY = 1000
 
 
 def cost(flops, moved):
@@ -47,30 +43,41 @@
 INSIDE = pl.BlockSpec(memory_space=pltpu.VMEM)
 
 
-def mask_kernel(core_ref, weight_ref, mask_ref, *refs):
-    del core_ref
-    kept_ref = refs[-1]
-    for block in range(weight_ref.shape[0] // BLOCK):
+def mask_kernel(after_count, core_ref, weight_ref, mask_ref, *refs):
+    kept_ref, spread = refs[after_count:]
+    depth, width = weight_ref.shape
+    blocks = depth // BLOCK
+    step = pl.program_id(0)
+
+    @pl.when(step == 0)
+    def _():
+        marks = mask_ref.shape[1]
+        first = core_ref[0] * (width // BLOCK)
+        owner = lax.broadcasted_iota(jnp.int32, (marks, width), 1) // BLOCK + first
+        chosen = (owner == lax.broadcasted_iota(jnp.int32, (marks, width), 0)).astype(F32)
+        spread[...] = jnp.dot(mask_ref[...].astype(F32), chosen, preferred_element_type=F32)
+
+    for block in range(blocks):
         rows = pl.ds(block * BLOCK, BLOCK)
-        keep = jnp.broadcast_to(mask_ref[block], (BLOCK, weight_ref.shape[1]))
+        keep = jnp.broadcast_to(spread[pl.ds(step * blocks + block, 1), :], (BLOCK, width))
         kept_ref[rows, :] = weight_ref[rows, :] * keep.astype(BF16)
 
 
 def masked(weight, mask, rows, core, shares, after):
     depth, width = weight.shape
     width = width // shares
-    mask = spread(mask)
     return pl.pallas_call(
-        mask_kernel,
+        functools.partial(mask_kernel, len(after)),
         grid_spec=pltpu.PrefetchScalarGridSpec(
             num_scalar_prefetch=1,
             grid=(depth // rows,),
             in_specs=[
                 pl.BlockSpec((rows, width), lambda i, core: (i, core[0])),
-                pl.BlockSpec((rows // BLOCK, 1, width), lambda i, core: (i, 0, core[0])),
+                pl.BlockSpec(mask.shape, lambda i, core: (0, 0)),
             ]
             + [ANYWHERE] * len(after),
             out_specs=pl.BlockSpec((rows, width), lambda i, core: (i, 0)),
+            scratch_shapes=[pltpu.VMEM((mask.shape[0], width), F32)],
         ),
         out_shape=jax.ShapeDtypeStruct((depth, width), weight.dtype),
         compiler_params=params("arbitrary"),
@@ -79,13 +86,32 @@
     )(core, pltpu.with_memory_space_constraint(weight, pltpu.HBM), mask, *after)
 
 
+def assemble_kernel(after_count, *refs):
+    block_refs, mine_ref = refs[: -1 - after_count], refs[-1]
+    rows = jnp.concatenate([block_ref[...].astype(F32) for block_ref in block_refs], 0)
+    mine_ref[...] = rows.astype(BF16)
+
+
+def assemble(blocks, after):
+    shape = (sum(block.shape[0] for block in blocks), blocks[0].shape[1])
+    return pl.pallas_call(
+        functools.partial(assemble_kernel, len(after)),
+        in_specs=[INSIDE] * len(blocks) + [ANYWHERE] * len(after),
+        out_specs=INSIDE,
+        out_shape=jax.ShapeDtypeStruct(shape, BF16),
+        compiler_params=pltpu.CompilerParams(vmem_limit_bytes=VMEM // 2),
+        cost_estimate=cost(0, 1000000),
+        name="assemble",
+    )(*blocks, *after)
+
+
 def resident(values):
     return pltpu.with_memory_space_constraint(values, pltpu.VMEM)
 
 
 def gate_up_kernel(part_count, after_count, *refs):
     parts, (gate_ref, up_ref) = refs[:part_count], refs[part_count : part_count + 2]
-    keep_ref, *send_refs, all_rows = refs[part_count + 2 + after_count :]
+    keep_ref, near_ref, *far_refs, all_rows = refs[part_count + 2 + after_count :]
     half = parts[0].shape[0] // 2
     kept = half * len(parts)
     for place, part in enumerate(parts):
@@ -100,20 +126,22 @@
             total = jnp.dot(all_rows[...], weight_ref[:, columns], preferred_element_type=F32)
             total = total.reshape(2, *keep_ref.shape[1:4], tile).astype(BF16)
             keep_ref[which, :, :, :, columns] = total[0]
-            send_refs[which][:, :, :, columns] = total[1]
+            near_ref[which, :, :, columns] = total[1, :, 0]
+            far_refs[which][:, :, :, columns] = total[1, :, 1:]
 
 
 def gate_up(parts, gate_kept, up_kept, chips, after):
     rows = sum(part.shape[0] for part in parts)
     depth, width = gate_kept.shape
-    half = jax.ShapeDtypeStruct((2, len(parts), chips, rows // (2 * len(parts) * chips), width), BF16)
+    groups, own = len(parts), rows // (2 * len(parts) * chips)
+    shapes = [(2, groups, chips, own, width), (2, groups, own, width)] + [(groups, chips - 1, own, width)] * 2
     return pl.pallas_call(
         functools.partial(gate_up_kernel, len(parts), len(after)),
         in_specs=[INSIDE] * (len(parts) + 2) + [ANYWHERE] * len(after),
-        out_specs=[INSIDE] * 3,
-        out_shape=[half] + [jax.ShapeDtypeStruct(half.shape[1:], BF16)] * 2,
+        out_specs=[INSIDE] * len(shapes),
+        out_shape=[jax.ShapeDtypeStruct(shape, BF16) for shape in shapes],
         scratch_shapes=[pltpu.VMEM((rows, depth), BF16)],
-        compiler_params=pltpu.CompilerParams(vmem_limit_bytes=VMEM),
+        compiler_params=pltpu.CompilerParams(vmem_limit_bytes=VMEM // 2),
         cost_estimate=cost(4 * rows * depth * width, 0),
         name="gate_up",
     )(*parts, resident(gate_kept), resident(up_kept), *after)
@@ -146,7 +174,7 @@
         out_specs=[INSIDE] * groups,
         out_shape=[jax.ShapeDtypeStruct(shape, BF16)] * groups,
         scratch_shapes=[pltpu.VMEM((CORES * groups * rows, depth), BF16)],
-        compiler_params=pltpu.CompilerParams(vmem_limit_bytes=VMEM),
+        compiler_params=pltpu.CompilerParams(vmem_limit_bytes=VMEM // 2),
         cost_estimate=cost(2 * CORES * groups * rows * depth * width, 0),
         name="down",
     )(own, other, resident(down_kept), *after)
@@ -164,16 +192,15 @@
             sent_ref = refs.pop(0)
             for which in range(2):
                 for group in range(keep_ref.shape[1]):
-                    came = came_refs[which][group, chip].astype(F32)
+                    came = came_refs[which][group, chip - 1].astype(F32)
                     sent_ref[which, group] = (keep_ref[which, group, chip].astype(F32) + came).astype(BF16)
     if to_hidden:
-        keep_ref, *came_refs = ins[1][:3]
-        chip_refs = ins[1][3:]
+        keep_ref, came_ref, *chip_refs = ins[1]
         hidden_ref = refs.pop(0)
         for group in range(keep_ref.shape[1]):
             both = []
             for which in range(2):
-                total = keep_ref[which, group, 0].astype(F32) + came_refs[which][group, 0].astype(F32)
+                total = keep_ref[which, group, 0].astype(F32) + came_ref[which, group].astype(F32)
                 for chip_ref in chip_refs:
                     total = total + chip_ref[which, group].astype(F32)
                 both.append(total)
@@ -202,7 +229,7 @@
         in_specs=[INSIDE] * len(given) + [ANYWHERE] * len(after),
         out_specs=[INSIDE] * len(shapes),
         out_shape=[jax.ShapeDtypeStruct(shape, BF16) for shape in shapes],
-        compiler_params=pltpu.CompilerParams(vmem_limit_bytes=VMEM),
+        compiler_params=pltpu.CompilerParams(vmem_limit_bytes=VMEM // 2),
         cost_estimate=cost(0, 4000000),
         name="sums",
     )(*given, *after))
@@ -230,65 +257,102 @@
     for step in [chip * CORES + other for other in range(CORES) for chip in range(chips)]:
         block = lax.dynamic_slice_in_dim(normed, (row ^ step) * features, features, 1)
         blocks.append(swap(block, "rows", row_count, step) if step else block)
-    mine = jnp.concatenate(blocks, 0)
-
-    order = [0, *range(1, PLANES, 2), *range(2, PLANES, 2)]
-    planes = {0: mine}
-    for plane in order[1:]:
-        planes[plane] = swap(mine, "cols", col_count, plane * per_plane)
-    parts = {}
-    for plane in order:
+    gate_kept = masked(gate_weight, gate_mask, tile_of(features, 256), nowhere, 1, [normed])
+    mine = assemble(blocks, [gate_kept])
+
+    def behind(values, after):
+        return lax.optimization_barrier((values, *after))[0] if after else values
+
+    def by_plane(values, plane, after=()):
+        return swap(behind(values, after), "cols", col_count, plane * per_plane)
+
+    def by_row_of_plane(values, step, after=()):
+        return swap(behind(values, after), "cols", col_count, step)
+
+    def by_chip(values, chip, after=()):
+        return swap(behind(values, after), "rows", row_count, chip * CORES)
+
+    def by_core(values):
+        return swap(values, "rows", row_count, 1)
+
+    up_kept = masked(up_weight, up_mask, tile_of(features, 256), nowhere, 1, [mine])
+    down_kept = masked(down_weight, down_mask, 2 * BLOCK, place, CORES, [up_kept])
+
+    parts, halves, came, chip_sums, hiddens, others, rows_in, arrived, partials, near = ({} for _ in range(10))
+    last = [down_kept]
+
+    def forward(plane, after=()):
         parts[plane] = [planes[plane]]
         for step in range(1, per_plane):
-            parts[plane].append(swap(planes[plane], "cols", col_count, step))
-
-    gate_kept = masked(gate_weight, gate_mask, tile_of(features, 256), nowhere, 1, [])
-    up_kept = masked(up_weight, up_mask, tile_of(features, 256), nowhere, 1, [gate_kept])
-
-    halves, came, chip_sums, hiddens, others, partials, rows_in = {}, {}, {}, {}, {}, {}, {}
-    last = [up_kept]
-    down_kept = None
-    arrived = []
-    steps = len(order)
-    for number in range(steps + 3):
-        now, before, earlier, first = (
-            order[at] if 0 <= at < steps else None for at in range(number, number - 4, -1)
-        )
-        if now is not None:
-            halves[now] = gate_up(parts[now], gate_kept, up_kept, chips, last)
-            came[now] = [swap(part, "rows", row_count, 1) for part in halves[now][1:]]
-            last = [halves[now][0]]
-        if number == 0:
-            down_kept = masked(down_weight, down_mask, 2 * BLOCK, place, CORES, last + [planes[1], planes[order[2]]])
-            last = [down_kept]
-        if earlier is not None:
-            partials[earlier] = down(hiddens[earlier], others[earlier], down_kept, last)
-            last = [partials[earlier][0]]
-            rows_in[earlier] = [partials[earlier][0]]
-            for step in range(1, per_plane):
-                rows_in[earlier].append(swap(partials[earlier][step], "cols", col_count, step))
-        to_chips = [halves[now][0], *came[now]] if now is not None else []
-        to_hidden = [halves[before][0], *came[before], *chip_sums[before]] if before is not None else []
-        to_rows = rows_in[first] if first is not None else []
-        sent, hidden, summed = sums(to_chips, to_hidden, to_rows, last)
-        last = (sent + [hidden, summed])[:1]
-        if sent:
-            chip_sums[now] = [
-                swap(part, "rows", row_count, (chip + 1) * CORES) for chip, part in enumerate(sent)
-            ]
-        if hidden is not None:
-            hiddens[before] = hidden
-            others[before] = swap(hidden, "rows", row_count, 1)
-            last = [hidden]
-        if summed is not None:
-            last = [summed]
-            arrived.append(swap(summed, "cols", col_count, first * per_plane) if first else summed)
-
+            parts[plane].append(by_row_of_plane(planes[plane], step, after))
+
+    def multiply_in(plane, after=()):
+        halves[plane] = gate_up(parts[plane], gate_kept, up_kept, chips, last + list(after))
+        came[plane] = [by_core(part) for part in halves[plane][2:]]
+        last[:] = [halves[plane][0]]
+
+    def multiply_out(plane, after=()):
+        partials[plane] = down(hiddens[plane], others[plane], down_kept, last + list(after))
+        last[:] = [partials[plane][0]]
+
+    def send_rows(plane, after=()):
+        rows_in[plane] = [partials[plane][0]]
+        for step in range(1, per_plane):
+            rows_in[plane].append(by_row_of_plane(partials[plane][step], step, after))
+
+    def add(chip=None, hide=None, rows=None, after=(), chip_after=()):
+        to_chips = [halves[chip][0], *came[chip]] if chip is not None else []
+        to_hidden = [halves[hide][0], near[hide], *chip_sums[hide]] if hide is not None else []
+        to_rows = rows_in[rows] if rows is not None else []
+        sent, hidden, summed = sums(to_chips, to_hidden, to_rows, last + list(after))
+        if chip is not None:
+            chip_sums[chip] = [by_chip(part, number + 1, chip_after) for number, part in enumerate(sent)]
+            near[chip] = by_core(behind(halves[chip][1], sent[:1]))
+            last[:] = sent[:1]
+        if hide is not None:
+            hiddens[hide], others[hide] = hidden, by_core(hidden)
+            last[:] = [hidden]
+        if rows is not None:
+            arrived[rows] = by_plane(summed, rows) if rows else summed
+            last[:] = [summed]
+
+    planes = {0: mine, 3: by_plane(mine, 3), 1: by_plane(mine, 1)}
+    forward(0)
+    multiply_in(0)
+    planes[2] = by_plane(mine, 2, [planes[3], planes[1]])
+    forward(3, last)
+    add(chip=0, after=[planes[3], planes[1]])
+    add(hide=0)
+    forward(1, parts[3][1:])
+    multiply_in(3)
+    add(chip=3)
+    forward(2, parts[1][1:] + last)
+    multiply_in(1, [planes[2]])
+    add(hide=3)
+    add(chip=1)
+    multiply_out(3)
+    send_rows(3, parts[2][1:])
+    multiply_in(2)
+    add(hide=1)
+    add(chip=2)
+    multiply_out(0)
+    send_rows(0, rows_in[3][1:])
+    add(rows=3)
+    multiply_out(1)
+    add(hide=2)
+    multiply_out(2)
+    send_rows(2, rows_in[0][1:])
+    add(rows=0, after=[arrived[3]])
+    add(rows=2)
+    send_rows(1, rows_in[2][1:] + last)
+    add(rows=1)
+
+    arrived = [arrived[plane] for plane in (0, 3, 1, 2)]
     total = arrived[0].astype(F32)
     for part in arrived[1:]:
         total = total + part.astype(F32)
     mine_now = total[0].astype(BF16)
-    other = swap(total[1].astype(BF16), "rows", row_count, 1)
+    other = by_core(total[1].astype(BF16))
     left = jnp.where(core == 0, mine_now, other)
     right = jnp.where(core == 0, other, mine_now)
     return jnp.concatenate([left, right], 1)

time: 248 us -> 200 us (0.81)
  starting transfers between devices: 63.7 us -> 42.4 us
  local copies, waits for them, and re-layouts: 12.7 us -> 1.83 us
  Pallas kernels: 72.2 us -> 64.2 us
  waiting for transfers between devices: 93.6 us -> 86.9 us
    ppermute x34 -> x38, starting transfers between devices: 63.7 us -> 42.4 us  [swap(): lax.ppermute(values, axis, [(place, place ^ step) for place in range(size)])]
    ppermute x34 -> x38, waiting for transfers between devices: 93.6 us -> 86.9 us  [swap(): lax.ppermute(values, axis, [(place, place ^ step) for place in range(size)])]
    unnamed x22 -> x12, local copies, waits for them, and re-layouts: 6.58 us -> 1.75 us
    pallas_call x4, Pallas kernels: 28.9 us -> 24.4 us  [gate_up(): pl.pallas_call(functools.partial(gate_up_kernel, len(parts), len(after)),...]
    convert_element_type x4 -> x1, local copies, waits for them, and re-layouts: 3.96 us -> 0.02 us  [body(): other = by_core(total[1].astype(BF16))]
    pallas_call x3 -> x4, Pallas kernels: 23.2 us -> 22.1 us  [the longest x3 22 us: masked(): pl.pallas_call(functools.partial(mask_kernel, len(after)), grid_spec=pltp...]
  transfers between devices with their start and end apart: 34 -> 38, of which waited for: 14 -> 21; matrix products, arithmetic and copies ran while one was open for 2% -> 0% of each run, Pallas kernels for 29% -> 32%
where the time goes in v3:
time: 200 us
  waiting for transfers between devices  86.9 us (43%)
  Pallas kernels  64.2 us (32%)
  starting transfers between devices  42.4 us (21%)
  other arithmetic  3.89 us (2%)
    ppermute x38, waiting for transfers between devices, swap(): lax.ppermute(values, axis, [(place, place ^ step) for place in range(size)])  86.9 us
    ppermute x38, starting transfers between devices, swap(): lax.ppermute(values, axis, [(place, place ^ step) for place in range(size)])  42.4 us
    pallas_call x4, Pallas kernels, gate_up(): pl.pallas_call(functools.partial(gate_up_kernel, len(parts), len(after)),...  24.4 us
    pallas_call x3, Pallas kernels, masked(): pl.pallas_call(functools.partial(mask_kernel, len(after)), grid_spec=pltp...  22 us
    pallas_call x4, Pallas kernels, down(): pl.pallas_call(functools.partial(down_kernel, len(after)), in_specs=[INSI...  15.4 us
  transfers between devices with their start and end apart: 38, of which 21 were waited for; matrix products, arithmetic and copies ran while one was open for 0% of the time, Pallas kernels for 32%

profile of v3, /device:TPU:0, one launch (start us, length us, event | category | flops | bytes accessed | tf_op | source)
XLA Modules:
  0.0 199.6 jit_solution(6333057756185517840)
XLA Ops:
  0.0 1.3 fusion
  1.4 1.3 fusion.2.refs_0_
  2.7 3.0 %collective-permute-start = (bf16[40,2048]{1,0:T(8,128)(2,1)S(1)}, bf16[40,2048]{1,0:T(8,128)(2,1)S(1)}, u32[]{:S(2)}, u32[]{:S(2)}) collective-permute-start(bf16[40,2048]{1,0:T(8,128)(2,1)S(1)} %get-tuple-element.81), channel_id=1, source_target_pairs={{0,16},{8,24},{16,0},{24,8},{1,17},{9,25},{17,1},{25,9},{2,18},{10... | collective-permute-start | bytes 491528 | tf_op jit(solution)/shard_map/ppermute | solution.py:243
  6.0 5.6 %masked.3.refs_4_.refs_2_ = bf16[2048,1792]{1,0:T(8,128)(2,1)S(1)} custom-call(s32[1]{0:T(128)} %constant.34.clone.1.core_ref, bf16[2048,1792]{1,0:T(8,128)(2,1)} %weight_ref.3, s32[32,28]{1,0:T(8,128)S(1)} %copy-done.2, bf16[40,8192]{1,0:T(8,128)(2,1)S(1)} %fusion.2.refs_0_), custom_call_target="tpu_custom_call" | custom-call | bytes 14680 | tf_op jit(solution)/shard_map/masked/pallas_call | solution.py:69
  11.6 1.1 collective-permute-done.2.refs_3_
  12.8 1.7 copy-done
  14.5 2.0 collective-permute-start.3
  16.5 3.6 %collective-permute-start.6 = (bf16[160,2048]{1,0:T(8,128)(2,1)S(1)}, bf16[160,2048]{1,0:T(8,128)(2,1)S(1)}, u32[]{:S(2)}, u32[]{:S(2)}) collective-permute-start(bf16[160,2048]{1,0:T(8,128)(2,1)S(1)} %assemble.1.refs_0_), channel_id=1, source_target_pairs={{0,6},{1,7},{2,4},{3,5},{4,2},{5,3},{6,0},{7,1},{8,14},{9,15},{10,... | collective-permute-start | bytes 1966088 | tf_op jit(solution)/shard_map/ppermute | solution.py:243
  20.1 6.0 %masked.4.refs_0_.refs_3_ = bf16[2048,1792]{1,0:T(8,128)(2,1)S(1)} custom-call(s32[1]{0:T(128)} %constant.34.clone.1.core_ref, bf16[2048,1792]{1,0:T(8,128)(2,1)} %weight_ref.4, s32[32,28]{1,0:T(8,128)S(1)} %copy-done.3, bf16[160,2048]{1,0:T(8,128)(2,1)S(1)} %assemble.1.refs_0_), custom_call_target="tpu_custom_call" | custom-call | bytes 14680 | tf_op jit(solution)/shard_map/masked/pallas_call | solution.py:69
  26.1 10.4 %masked.5.refs_4_.weight_ref = bf16[1792,4096]{1,0:T(8,128)(2,1)S(1)} custom-call(s32[1]{0:T(128)} %bitcast.core_ref, bf16[1792,8192]{1,0:T(8,128)(2,1)} %weight_ref.5, s32[28,128]{1,0:T(8,128)S(1)} %copy-done.1, bf16[2048,1792]{1,0:T(8,128)(2,1)S(1)} %masked.4.refs_0_.refs_3_), custom_call_target="tpu_custom_call" | custom-call | bytes 29360 | tf_op jit(solution)/shard_map/masked/pallas_call | solution.py:69
  36.5 6.1 %gate_up.4 = (bf16[2,2,2,40,1792]{4,3,2,1,0:T(8,128)(2,1)S(1)}, bf16[2,2,40,1792]{3,2,1,0:T(8,128)(2,1)S(1)}, bf16[2,1,40,1792]{3,2,1,0:T(8,128)(2,1)S(1)}, bf16[2,1,40,1792]{3,2,1,0:T(8,128)(2,1)S(1)}) custom-call(bf16[160,2048]{1,0:T(8,128)(2,1)S(1)} %assemble.1.refs_0_, bf16[160,2048]{1,0:T(8,128)(2,1)S(1)} %collective-permute-done.3.refs_1_, ...), custom_call_target="tpu_custom_call" | custom-call | flops 4697620 | tf_op jit(solution)/shard_map/gate_up/pallas_call | solution.py:138
  43.7 5.1 %collective-permute-done.7.refs_5_.refs_0_ = bf16[160,2048]{1,0:T(8,128)(2,1)S(1)} collective-permute-done((bf16[160,2048]{1,0:T(8,128)(2,1)S(1)}, bf16[160,2048]{1,0:T(8,128)(2,1)S(1)}, u32[]{:S(2)}, u32[]{:S(2)}) %collective-permute-start.7) | collective-permute-done | bytes 655392 | tf_op jit(solution)/shard_map/ppermute | solution.py:243
  49.1 1.6 collective-permute-start.9
  50.6 1.1 collective-permute-start.11
  51.8 8.2 %collective-permute-done.12.refs_1_ = bf16[160,2048]{1,0:T(8,128)(2,1)S(1)} collective-permute-done((bf16[160,2048]{1,0:T(8,128)(2,1)S(1)}, bf16[160,2048]{1,0:T(8,128)(2,1)S(1)}, u32[]{:S(2)}, u32[]{:S(2)}) %collective-permute-start.12) | collective-permute-done | bytes 655392 | tf_op jit(solution)/shard_map/ppermute | solution.py:243
  60.4 4.0 %collective-permute-done.9.refs_2_ = bf16[2,2,40,1792]{3,2,1,0:T(8,128)(2,1)S(1)} collective-permute-done((bf16[2,2,40,1792]{3,2,1,0:T(8,128)(2,1)S(1)}, bf16[2,2,40,1792]{3,2,1,0:T(8,128)(2,1)S(1)}, u32[]{:S(2)}, u32[]{:S(2)}) %collective-permute-start.9) | collective-permute-done | bytes 573472 | tf_op jit(solution)/shard_map/ppermute | solution.py:243
  64.7 6.1 %gate_up.5 = (bf16[2,2,2,40,1792]{4,3,2,1,0:T(8,128)(2,1)S(1)}, bf16[2,2,40,1792]{3,2,1,0:T(8,128)(2,1)S(1)}, bf16[2,1,40,1792]{3,2,1,0:T(8,128)(2,1)S(1)}, bf16[2,1,40,1792]{3,2,1,0:T(8,128)(2,1)S(1)}) custom-call(bf16[160,2048]{1,0:T(8,128)(2,1)S(1)} %collective-permute-done.6.refs_4_.refs_0_, bf16[160,2048]{1,0:T(8,128)(2,1)S(1)} %collective-permute-done.12.refs_1_, ...), custom_call_target="tpu_custom_call" | custom-call | flops 4697620 | tf_op jit(solution)/shard_map/gate_up/pallas_call | solution.py:138
  71.4 1.1 collective-permute-done.14.refs_1_
  73.2 1.5 collective-permute-start.18
  74.7 7.6 %collective-permute-done.11.refs_5_.refs_0_ = bf16[160,2048]{1,0:T(8,128)(2,1)S(1)} collective-permute-done((bf16[160,2048]{1,0:T(8,128)(2,1)S(1)}, bf16[160,2048]{1,0:T(8,128)(2,1)S(1)}, u32[]{:S(2)}, u32[]{:S(2)}) %collective-permute-start.11) | collective-permute-done | bytes 655392 | tf_op jit(solution)/shard_map/ppermute | solution.py:243
  82.4 0.5 collective-permute-start.16
  82.9 6.1 %gate_up.6 = (bf16[2,2,2,40,1792]{4,3,2,1,0:T(8,128)(2,1)S(1)}, bf16[2,2,40,1792]{3,2,1,0:T(8,128)(2,1)S(1)}, bf16[2,1,40,1792]{3,2,1,0:T(8,128)(2,1)S(1)}, bf16[2,1,40,1792]{3,2,1,0:T(8,128)(2,1)S(1)}) custom-call(bf16[160,2048]{1,0:T(8,128)(2,1)S(1)} %collective-permute-done.7.refs_5_.refs_0_, bf16[160,2048]{1,0:T(8,128)(2,1)S(1)} %collective-permute-done.13.refs_1_, ...), custom_call_target="tpu_custom_call" | custom-call | flops 4697620 | tf_op jit(solution)/shard_map/gate_up/pallas_call | solution.py:138
  90.0 0.6 collective-permute-done.20.refs_1_
  91.4 0.6 collective-permute-start.25
  91.9 3.9 %down.4 = (bf16[2,40,4096]{2,1,0:T(8,128)(2,1)S(1)}, bf16[2,40,4096]{2,1,0:T(8,128)(2,1)S(1)}) custom-call(bf16[2,40,1792]{2,1,0:T(8,128)(2,1)S(1)} %sums.15.refs_3_.own_ref, bf16[2,40,1792]{2,1,0:T(8,128)(2,1)S(1)} %collective-permute-done.19.other_ref, bf16[1792,4096]{1,0:T(8,128)(2,1)S(1)} %masked.5.refs_4_.weight_ref, ...), custom_call_target="tpu_custom_call" | custom-call | flops 2348810 | tf_op jit(solution)/shard_map/down/pallas_call | solution.py:171
  95.8 2.5 %collective-permute-done.16.refs_1_ = bf16[160,2048]{1,0:T(8,128)(2,1)S(1)} collective-permute-done((bf16[160,2048]{1,0:T(8,128)(2,1)S(1)}, bf16[160,2048]{1,0:T(8,128)(2,1)S(1)}, u32[]{:S(2)}, u32[]{:S(2)}) %collective-permute-start.16) | collective-permute-done | bytes 655392 | tf_op jit(solution)/shard_map/ppermute | solution.py:243
  98.8 6.1 %gate_up.7 = (bf16[2,2,2,40,1792]{4,3,2,1,0:T(8,128)(2,1)S(1)}, bf16[2,2,40,1792]{3,2,1,0:T(8,128)(2,1)S(1)}, bf16[2,1,40,1792]{3,2,1,0:T(8,128)(2,1)S(1)}, bf16[2,1,40,1792]{3,2,1,0:T(8,128)(2,1)S(1)}) custom-call(bf16[160,2048]{1,0:T(8,128)(2,1)S(1)} %collective-permute-done.11.refs_5_.refs_0_, bf16[160,2048]{1,0:T(8,128)(2,1)S(1)} %collective-permute-done.16.refs_1_, ...), custom_call_target="tpu_custom_call" | custom-call | flops 4697620 | tf_op jit(solution)/shard_map/gate_up/pallas_call | solution.py:138
  105.6 1.0 collective-permute-done.25.refs_2_
  107.3 0.6 collective-permute-start.29
  107.9 3.9 %down.5 = (bf16[2,40,4096]{2,1,0:T(8,128)(2,1)S(1)}, bf16[2,40,4096]{2,1,0:T(8,128)(2,1)S(1)}) custom-call(bf16[2,40,1792]{2,1,0:T(8,128)(2,1)S(1)} %sums.13.refs_4_.own_ref, bf16[2,40,1792]{2,1,0:T(8,128)(2,1)S(1)} %collective-permute-done.10.other_ref, bf16[1792,4096]{1,0:T(8,128)(2,1)S(1)} %masked.5.refs_4_.weight_ref, ...), custom_call_target="tpu_custom_call" | custom-call | flops 2348810 | tf_op jit(solution)/shard_map/down/pallas_call | solution.py:171
  111.8 1.6 collective-permute-done.26.refs_1_
  113.4 0.7 collective-permute-start.27
  114.3 1.4 collective-permute-done.30.other_ref
  115.7 3.9 %down.6 = (bf16[2,40,4096]{2,1,0:T(8,128)(2,1)S(1)}, bf16[2,40,4096]{2,1,0:T(8,128)(2,1)S(1)}) custom-call(bf16[2,40,1792]{2,1,0:T(8,128)(2,1)S(1)} %sums.17.refs_3_.own_ref, bf16[2,40,1792]{2,1,0:T(8,128)(2,1)S(1)} %collective-permute-done.30.other_ref, bf16[1792,4096]{1,0:T(8,128)(2,1)S(1)} %masked.5.refs_4_.weight_ref, bf16[2,40,4096]{2,1,0:T(8,128)(2,1)S(1)} %sums.19.refs_0_), custom_call_target="tpu_custom_call" | custom-call | flops 2348810 | tf_op jit(solution)/shard_map/down/pallas_call | solution.py:171
  119.6 3.0 %collective-permute-done.29.refs_2_ = bf16[2,2,40,1792]{3,2,1,0:T(8,128)(2,1)S(1)} collective-permute-done((bf16[2,2,40,1792]{3,2,1,0:T(8,128)(2,1)S(1)}, bf16[2,2,40,1792]{3,2,1,0:T(8,128)(2,1)S(1)}, u32[]{:S(2)}, u32[]{:S(2)}) %collective-permute-start.29) | collective-permute-done | bytes 573472 | tf_op jit(solution)/shard_map/ppermute | solution.py:243
  123.0 1.8 collective-permute-start.32
  124.8 3.9 %down.7 = (bf16[2,40,4096]{2,1,0:T(8,128)(2,1)S(1)}, bf16[2,40,4096]{2,1,0:T(8,128)(2,1)S(1)}) custom-call(bf16[2,40,1792]{2,1,0:T(8,128)(2,1)S(1)} %sums.20.own_ref.refs_0_, bf16[2,40,1792]{2,1,0:T(8,128)(2,1)S(1)} %collective-permute-done.31.other_ref, bf16[1792,4096]{1,0:T(8,128)(2,1)S(1)} %masked.5.refs_4_.weight_ref, ...), custom_call_target="tpu_custom_call" | custom-call | flops 2348810 | tf_op jit(solution)/shard_map/down/pallas_call | solution.py:171
  128.6 1.8 collective-permute-start.33
  130.5 11.6 %collective-permute-done.32.refs_3_ = bf16[2,40,4096]{2,1,0:T(8,128)(2,1)S(1)} collective-permute-done((bf16[2,40,4096]{2,1,0:T(8,128)(2,1)S(1)}, bf16[2,40,4096]{2,1,0:T(8,128)(2,1)S(1)}, u32[]{:S(2)}, u32[]{:S(2)}) %collective-permute-start.32) | collective-permute-done | bytes 655392 | tf_op jit(solution)/shard_map/ppermute | solution.py:243
  142.2 3.4 %collective-permute-done.33.refs_1_ = bf16[2,40,4096]{2,1,0:T(8,128)(2,1)S(1)} collective-permute-done((bf16[2,40,4096]{2,1,0:T(8,128)(2,1)S(1)}, bf16[2,40,4096]{2,1,0:T(8,128)(2,1)S(1)}, u32[]{:S(2)}, u32[]{:S(2)}) %collective-permute-start.33) | collective-permute-done | bytes 655392 | tf_op jit(solution)/shard_map/ppermute | solution.py:243
  145.7 1.8 collective-permute-start.34
  147.5 8.1 %collective-permute-start.36 = (bf16[2,40,4096]{2,1,0:T(8,128)(2,1)S(1)}, bf16[2,40,4096]{2,1,0:T(8,128)(2,1)S(1)}, u32[]{:S(2)}, u32[]{:S(2)}) collective-permute-start(bf16[2,40,4096]{2,1,0:T(8,128)(2,1)S(1)} %sums.22.refs_2_), channel_id=1, source_target_pairs={{0,4},{1,5},{2,6},{3,7},{4,0},{5,1},{6,2},{7,3},{8,12},{9,13},{10,... | collective-permute-start | bytes 1966088 | tf_op jit(solution)/shard_map/ppermute | solution.py:243
  155.6 6.1 %collective-permute-done.34.refs_1_ = bf16[2,40,4096]{2,1,0:T(8,128)(2,1)S(1)} collective-permute-done((bf16[2,40,4096]{2,1,0:T(8,128)(2,1)S(1)}, bf16[2,40,4096]{2,1,0:T(8,128)(2,1)S(1)}, u32[]{:S(2)}, u32[]{:S(2)}) %collective-permute-start.34) | collective-permute-done | bytes 655392 | tf_op jit(solution)/shard_map/ppermute | solution.py:243
  161.9 8.7 %collective-permute-start.35 = (bf16[2,40,4096]{2,1,0:T(8,128)(2,1)S(1)}, bf16[2,40,4096]{2,1,0:T(8,128)(2,1)S(1)}, u32[]{:S(2)}, u32[]{:S(2)}) collective-permute-start(bf16[2,40,4096]{2,1,0:T(8,128)(2,1)S(1)} %sums.23), channel_id=1, source_target_pairs={{0,2},{1,3},{2,0},{3,1},{4,6},{5,7},{6,4},{7,5},{8,10},{9,11},{10,... | collective-permute-start | bytes 1966088 | tf_op jit(solution)/shard_map/ppermute | solution.py:243
  170.6 13.4 %collective-permute-done.36 = bf16[2,40,4096]{2,1,0:T(8,128)(2,1)S(1)} collective-permute-done((bf16[2,40,4096]{2,1,0:T(8,128)(2,1)S(1)}, bf16[2,40,4096]{2,1,0:T(8,128)(2,1)S(1)}, u32[]{:S(2)}, u32[]{:S(2)}) %collective-permute-start.36) | collective-permute-done | bytes 655392 | tf_op jit(solution)/shard_map/ppermute | solution.py:243
  184.1 12.5 %collective-permute-done.35 = bf16[2,40,4096]{2,1,0:T(8,128)(2,1)S(1)} collective-permute-done((bf16[2,40,4096]{2,1,0:T(8,128)(2,1)S(1)}, bf16[2,40,4096]{2,1,0:T(8,128)(2,1)S(1)}, u32[]{:S(2)}, u32[]{:S(2)}) %collective-permute-start.35) | collective-permute-done | bytes 655392 | tf_op jit(solution)/shard_map/ppermute | solution.py:243
  197.0 1.6 collective-permute-done.37
  198.7 0.9 pad_maximum_fusion
  (73 shorter events, 8.8 us)
Async XLA Ops:
  1.3 4.6 %copy-start.2 = (s32[32,28]{1,0:T(8,128)S(1)}, s32[32,28]{1,0:T(8,128)}, u32[]{:S(2)}) copy-start(s32[32,28]{1,0:T(8,128)} %mask_ref.3) | copy-start | bytes 10756
  2.7 8.9 %collective-permute-start = (bf16[40,2048]{1,0:T(8,128)(2,1)S(1)}, bf16[40,2048]{1,0:T(8,128)(2,1)S(1)}, u32[]{:S(2)}, u32[]{:S(2)}) collective-permute-start(bf16[40,2048]{1,0:T(8,128)(2,1)S(1)} %get-tuple-element.81), channel_id=1, source_target_pairs={{0,16},{8,24},{16,0},{24,8},{1,17},{9,25},{17,1},{25,9},{2,18},{10... | collective-permute-start | bytes 491528 | tf_op jit(solution)/shard_map/ppermute | solution.py:243
  5.7 5.9 %collective-permute-start.1 = (bf16[40,2048]{1,0:T(8,128)(2,1)S(1)}, bf16[40,2048]{1,0:T(8,128)(2,1)S(1)}, u32[]{:S(2)}, u32[]{:S(2)}) collective-permute-start(bf16[40,2048]{1,0:T(8,128)(2,1)S(1)} %get-tuple-element.80), channel_id=1, source_target_pairs={{0,8},{8,0},{16,24},{24,16},{1,9},{9,1},{17,25},{25,17},{2,10},{10... | collective-permute-start | bytes 491528 | tf_op jit(solution)/shard_map/ppermute | solution.py:243
  5.7 7.0 %collective-permute-start.2 = (bf16[40,2048]{1,0:T(8,128)(2,1)S(1)}, bf16[40,2048]{1,0:T(8,128)(2,1)S(1)}, u32[]{:S(2)}, u32[]{:S(2)}) collective-permute-start(bf16[40,2048]{1,0:T(8,128)(2,1)S(1)} %get-tuple-element.79), channel_id=1, source_target_pairs={{0,24},{8,16},{16,8},{24,0},{1,25},{9,17},{17,9},{25,1},{2,26},{10... | collective-permute-start | bytes 491528 | tf_op jit(solution)/shard_map/ppermute | solution.py:243
  11.6 2.9 %copy-start = (bf16[2048,1792]{1,0:T(8,128)(2,1)}, bf16[2048,1792]{1,0:T(8,128)(2,1)S(1)}, u32[]{:S(2)}) copy-start(bf16[2048,1792]{1,0:T(8,128)(2,1)S(1)} %masked.3.refs_4_.refs_2_) | copy-start | bytes 22020100
  12.7 7.3 %copy-start.3 = (s32[32,28]{1,0:T(8,128)S(1)}, s32[32,28]{1,0:T(8,128)}, u32[]{:S(2)}) copy-start(s32[32,28]{1,0:T(8,128)} %mask_ref.4) | copy-start | bytes 10756
  14.5 22.0 %collective-permute-start.3 = (bf16[160,2048]{1,0:T(8,128)(2,1)S(1)}, bf16[160,2048]{1,0:T(8,128)(2,1)S(1)}, u32[]{:S(2)}, u32[]{:S(2)}) collective-permute-start(bf16[160,2048]{1,0:T(8,128)(2,1)S(1)} %assemble.1.refs_0_), channel_id=1, source_target_pairs={{0,1},{1,0},{2,3},{3,2},{4,5},{5,4},{6,7},{7,6},{8,9},{9,8},{10,11... | collective-permute-start | bytes 1966088 | tf_op jit(solution)/shard_map/ppermute | solution.py:243
  16.5 26.8 %collective-permute-start.6 = (bf16[160,2048]{1,0:T(8,128)(2,1)S(1)}, bf16[160,2048]{1,0:T(8,128)(2,1)S(1)}, u32[]{:S(2)}, u32[]{:S(2)}) collective-permute-start(bf16[160,2048]{1,0:T(8,128)(2,1)S(1)} %assemble.1.refs_0_), channel_id=1, source_target_pairs={{0,6},{1,7},{2,4},{3,5},{4,2},{5,3},{6,0},{7,1},{8,14},{9,15},{10,... | collective-permute-start | bytes 1966088 | tf_op jit(solution)/shard_map/ppermute | solution.py:243
  20.1 28.8 %collective-permute-start.7 = (bf16[160,2048]{1,0:T(8,128)(2,1)S(1)}, bf16[160,2048]{1,0:T(8,128)(2,1)S(1)}, u32[]{:S(2)}, u32[]{:S(2)}) collective-permute-start(bf16[160,2048]{1,0:T(8,128)(2,1)S(1)} %assemble.1.refs_0_), channel_id=1, source_target_pairs={{0,2},{1,3},{2,0},{3,1},{4,6},{5,7},{6,4},{7,5},{8,10},{9,11},{10,... | collective-permute-start | bytes 1966088 | tf_op jit(solution)/shard_map/ppermute | solution.py:243
  20.1 6.0 %copy-start.1 = (s32[28,128]{1,0:T(8,128)S(1)}, s32[28,128]{1,0:T(8,128)}, u32[]{:S(2)}) copy-start(s32[28,128]{1,0:T(8,128)} %mask_ref.5) | copy-start | bytes 43012
  20.1 16.4 %slice-start = ((s8[7340032]{0:T(1024)(128)(4,1)}), s8[4194304]{0:T(1024)(128)(4,1)S(1)}, s32[]{:S(2)}) async-start(s8[7340032]{0:T(1024)(128)(4,1)} %bitcast.9), calls=%async_computation | async-start | bytes 8388608
  26.1 10.4 %slice-start.1 = ((s8[7340032]{0:T(1024)(128)(4,1)}), s8[3145728]{0:T(1024)(128)(4,1)S(1)}, s32[]{:S(2)}) async-start(s8[7340032]{0:T(1024)(128)(4,1)} %bitcast.9), calls=%async_computation.1 | async-start | bytes 6291456
  42.6 6.2 %collective-permute-start.4 = (bf16[2,1,40,1792]{3,2,1,0:T(8,128)(2,1)S(1)}, bf16[2,1,40,1792]{3,2,1,0:T(8,128)(2,1)S(1)}, u32[]{:S(2)}, u32[]{:S(2)}) collective-permute-start(bf16[2,1,40,1792]{3,2,1,0:T(8,128)(2,1)S(1)} %get-tuple-element.43), channel_id=1, source_target_pairs={{0,8},{8,0},{16,24},{24,16},{1,9},{9,1},{17,25},{25,17},{2,10},{10... | collective-permute-start | bytes 860168 | tf_op jit(solution)/shard_map/ppermute | solution.py:243
  42.7 6.1 %collective-permute-start.5 = (bf16[2,1,40,1792]{3,2,1,0:T(8,128)(2,1)S(1)}, bf16[2,1,40,1792]{3,2,1,0:T(8,128)(2,1)S(1)}, u32[]{:S(2)}, u32[]{:S(2)}) collective-permute-start(bf16[2,1,40,1792]{3,2,1,0:T(8,128)(2,1)S(1)} %get-tuple-element.44), channel_id=1, source_target_pairs={{0,8},{8,0},{16,24},{24,16},{1,9},{9,1},{17,25},{25,17},{2,10},{10... | collective-permute-start | bytes 860168 | tf_op jit(solution)/shard_map/ppermute | solution.py:243
  43.2 16.7 %collective-permute-start.12 = (bf16[160,2048]{1,0:T(8,128)(2,1)S(1)}, bf16[160,2048]{1,0:T(8,128)(2,1)S(1)}, u32[]{:S(2)}, u32[]{:S(2)}) collective-permute-start(bf16[160,2048]{1,0:T(8,128)(2,1)S(1)} %collective-permute-done.6.refs_4_.refs_0_), channel_id=1, source_target_pairs={{0,1},{1,0},{2,3},{3,2},{4,5},{5,4},{6,7},{7,6},{8,9},{9,8},{10,11... | collective-permute-start | bytes 1966088 | tf_op jit(solution)/shard_map/ppermute | solution.py:243
  49.0 11.5 %collective-permute-start.8 = (bf16[2,2,40,1792]{3,2,1,0:T(8,128)(2,1)S(1)}, bf16[2,2,40,1792]{3,2,1,0:T(8,128)(2,1)S(1)}, u32[]{:S(2)}, u32[]{:S(2)}) collective-permute-start(bf16[2,2,40,1792]{3,2,1,0:T(8,128)(2,1)S(1)} %get-tuple-element.45), channel_id=1, source_target_pairs={{0,8},{8,0},{16,24},{24,16},{1,9},{9,1},{17,25},{25,17},{2,10},{10... | collective-permute-start | bytes 1720328 | tf_op jit(solution)/shard_map/ppermute | solution.py:243
  49.1 15.4 %collective-permute-start.9 = (bf16[2,2,40,1792]{3,2,1,0:T(8,128)(2,1)S(1)}, bf16[2,2,40,1792]{3,2,1,0:T(8,128)(2,1)S(1)}, u32[]{:S(2)}, u32[]{:S(2)}) collective-permute-start(bf16[2,2,40,1792]{3,2,1,0:T(8,128)(2,1)S(1)} %sums.12.refs_3_), channel_id=1, source_target_pairs={{0,16},{8,24},{16,0},{24,8},{1,17},{9,25},{17,1},{25,9},{2,18},{10... | collective-permute-start | bytes 1720328 | tf_op jit(solution)/shard_map/ppermute | solution.py:243
  50.6 31.7 %collective-permute-start.11 = (bf16[160,2048]{1,0:T(8,128)(2,1)S(1)}, bf16[160,2048]{1,0:T(8,128)(2,1)S(1)}, u32[]{:S(2)}, u32[]{:S(2)}) collective-permute-start(bf16[160,2048]{1,0:T(8,128)(2,1)S(1)} %assemble.1.refs_0_), channel_id=1, source_target_pairs={{0,4},{1,5},{2,6},{3,7},{4,0},{5,1},{6,2},{7,3},{8,12},{9,13},{10,... | collective-permute-start | bytes 1966088 | tf_op jit(solution)/shard_map/ppermute | solution.py:243
  59.9 22.4 %collective-permute-start.13 = (bf16[160,2048]{1,0:T(8,128)(2,1)S(1)}, bf16[160,2048]{1,0:T(8,128)(2,1)S(1)}, u32[]{:S(2)}, u32[]{:S(2)}) collective-permute-start(bf16[160,2048]{1,0:T(8,128)(2,1)S(1)} %collective-permute-done.7.refs_5_.refs_0_), channel_id=1, source_target_pairs={{0,1},{1,0},{2,3},{3,2},{4,5},{5,4},{6,7},{7,6},{8,9},{9,8},{10,11... | collective-permute-start | bytes 1966088 | tf_op jit(solution)/shard_map/ppermute | solution.py:243
  70.8 1.6 collective-permute-start.14
  70.9 2.0 collective-permute-start.15
  73.0 16.5 %collective-permute-start.17 = (bf16[2,2,40,1792]{3,2,1,0:T(8,128)(2,1)S(1)}, bf16[2,2,40,1792]{3,2,1,0:T(8,128)(2,1)S(1)}, u32[]{:S(2)}, u32[]{:S(2)}) collective-permute-start(bf16[2,2,40,1792]{3,2,1,0:T(8,128)(2,1)S(1)} %get-tuple-element.54), channel_id=1, source_target_pairs={{0,8},{8,0},{16,24},{24,16},{1,9},{9,1},{17,25},{25,17},{2,10},{10... | collective-permute-start | bytes 1720328 | tf_op jit(solution)/shard_map/ppermute | solution.py:243
  73.2 16.3 %collective-permute-start.18 = (bf16[2,2,40,1792]{3,2,1,0:T(8,128)(2,1)S(1)}, bf16[2,2,40,1792]{3,2,1,0:T(8,128)(2,1)S(1)}, u32[]{:S(2)}, u32[]{:S(2)}) collective-permute-start(bf16[2,2,40,1792]{3,2,1,0:T(8,128)(2,1)S(1)} %sums.14.refs_4_), channel_id=1, source_target_pairs={{0,16},{8,24},{16,0},{24,8},{1,17},{9,25},{17,1},{25,9},{2,18},{10... | collective-permute-start | bytes 1720328 | tf_op jit(solution)/shard_map/ppermute | solution.py:243
  82.4 16.0 %collective-permute-start.16 = (bf16[160,2048]{1,0:T(8,128)(2,1)S(1)}, bf16[160,2048]{1,0:T(8,128)(2,1)S(1)}, u32[]{:S(2)}, u32[]{:S(2)}) collective-permute-start(bf16[160,2048]{1,0:T(8,128)(2,1)S(1)} %collective-permute-done.11.refs_5_.refs_0_), channel_id=1, source_target_pairs={{0,1},{1,0},{2,3},{3,2},{4,5},{5,4},{6,7},{7,6},{8,9},{9,8},{10,11... | collective-permute-start | bytes 1966088 | tf_op jit(solution)/shard_map/ppermute | solution.py:243
  89.0 1.6 collective-permute-start.20
  89.0 2.0 collective-permute-start.21
  89.8 2.1 %collective-permute-start.19 = (bf16[2,40,1792]{2,1,0:T(8,128)(2,1)S(1)}, bf16[2,40,1792]{2,1,0:T(8,128)(2,1)S(1)}, u32[]{:S(2)}, u32[]{:S(2)}) collective-permute-start(bf16[2,40,1792]{2,1,0:T(8,128)(2,1)S(1)} %sums.15.refs_3_.own_ref), channel_id=1, source_target_pairs={{0,8},{8,0},{16,24},{24,16},{1,9},{9,1},{17,25},{25,17},{2,10},{10... | collective-permute-start | bytes 860168 | tf_op jit(solution)/shard_map/ppermute | solution.py:243
  91.2 14.4 %collective-permute-start.24 = (bf16[2,2,40,1792]{3,2,1,0:T(8,128)(2,1)S(1)}, bf16[2,2,40,1792]{3,2,1,0:T(8,128)(2,1)S(1)}, u32[]{:S(2)}, u32[]{:S(2)}) collective-permute-start(bf16[2,2,40,1792]{3,2,1,0:T(8,128)(2,1)S(1)} %get-tuple-element.63), channel_id=1, source_target_pairs={{0,8},{8,0},{16,24},{24,16},{1,9},{9,1},{17,25},{25,17},{2,10},{10... | collective-permute-start | bytes 1720328 | tf_op jit(solution)/shard_map/ppermute | solution.py:243
  91.4 15.3 %collective-permute-start.25 = (bf16[2,2,40,1792]{3,2,1,0:T(8,128)(2,1)S(1)}, bf16[2,2,40,1792]{3,2,1,0:T(8,128)(2,1)S(1)}, u32[]{:S(2)}, u32[]{:S(2)}) collective-permute-start(bf16[2,2,40,1792]{3,2,1,0:T(8,128)(2,1)S(1)} %sums.16.refs_0_), channel_id=1, source_target_pairs={{0,16},{8,24},{16,0},{24,8},{1,17},{9,25},{17,1},{25,9},{2,18},{10... | collective-permute-start | bytes 1720328 | tf_op jit(solution)/shard_map/ppermute | solution.py:243
  98.3 15.1 %collective-permute-start.26 = (bf16[2,40,4096]{2,1,0:T(8,128)(2,1)S(1)}, bf16[2,40,4096]{2,1,0:T(8,128)(2,1)S(1)}, u32[]{:S(2)}, u32[]{:S(2)}) collective-permute-start(bf16[2,40,4096]{2,1,0:T(8,128)(2,1)S(1)} %get-tuple-element.67), channel_id=1, source_target_pairs={{0,1},{1,0},{2,3},{3,2},{4,5},{5,4},{6,7},{7,6},{8,9},{9,8},{10,11... | collective-permute-start | bytes 1966088 | tf_op jit(solution)/shard_map/ppermute | solution.py:243
  104.9 2.0 collective-permute-start.22
  105.0 2.0 collective-permute-start.23
  105.5 2.4 %collective-permute-start.10 = (bf16[2,40,1792]{2,1,0:T(8,128)(2,1)S(1)}, bf16[2,40,1792]{2,1,0:T(8,128)(2,1)S(1)}, u32[]{:S(2)}, u32[]{:S(2)}) collective-permute-start(bf16[2,40,1792]{2,1,0:T(8,128)(2,1)S(1)} %sums.13.refs_4_.own_ref), channel_id=1, source_target_pairs={{0,8},{8,0},{16,24},{24,16},{1,9},{9,1},{17,25},{25,17},{2,10},{10... | collective-permute-start | bytes 860168 | tf_op jit(solution)/shard_map/ppermute | solution.py:243
  107.1 12.4 %collective-permute-start.28 = (bf16[2,2,40,1792]{3,2,1,0:T(8,128)(2,1)S(1)}, bf16[2,2,40,1792]{3,2,1,0:T(8,128)(2,1)S(1)}, u32[]{:S(2)}, u32[]{:S(2)}) collective-permute-start(bf16[2,2,40,1792]{3,2,1,0:T(8,128)(2,1)S(1)} %get-tuple-element.70), channel_id=1, source_target_pairs={{0,8},{8,0},{16,24},{24,16},{1,9},{9,1},{17,25},{25,17},{2,10},{10... | collective-permute-start | bytes 1720328 | tf_op jit(solution)/shard_map/ppermute | solution.py:243
  107.3 15.3 %collective-permute-start.29 = (bf16[2,2,40,1792]{3,2,1,0:T(8,128)(2,1)S(1)}, bf16[2,2,40,1792]{3,2,1,0:T(8,128)(2,1)S(1)}, u32[]{:S(2)}, u32[]{:S(2)}) collective-permute-start(bf16[2,2,40,1792]{3,2,1,0:T(8,128)(2,1)S(1)} %sums.18.refs_0_), channel_id=1, source_target_pairs={{0,16},{8,24},{16,0},{24,8},{1,17},{9,25},{17,1},{25,9},{2,18},{10... | collective-permute-start | bytes 1720328 | tf_op jit(solution)/shard_map/ppermute | solution.py:243
  113.4 15.2 %collective-permute-start.27 = (bf16[2,40,4096]{2,1,0:T(8,128)(2,1)S(1)}, bf16[2,40,4096]{2,1,0:T(8,128)(2,1)S(1)}, u32[]{:S(2)}, u32[]{:S(2)}) collective-permute-start(bf16[2,40,4096]{2,1,0:T(8,128)(2,1)S(1)} %get-tuple-element.68), channel_id=1, source_target_pairs={{0,1},{1,0},{2,3},{3,2},{4,5},{5,4},{6,7},{7,6},{8,9},{9,8},{10,11... | collective-permute-start | bytes 1966088 | tf_op jit(solution)/shard_map/ppermute | solution.py:243
  114.1 1.6 collective-permute-start.30
  122.9 1.9 collective-permute-start.31
  123.0 19.1 %collective-permute-start.32 = (bf16[2,40,4096]{2,1,0:T(8,128)(2,1)S(1)}, bf16[2,40,4096]{2,1,0:T(8,128)(2,1)S(1)}, u32[]{:S(2)}, u32[]{:S(2)}) collective-permute-start(bf16[2,40,4096]{2,1,0:T(8,128)(2,1)S(1)} %sums.19.refs_0_), channel_id=1, source_target_pairs={{0,6},{1,7},{2,4},{3,5},{4,2},{5,3},{6,0},{7,1},{8,14},{9,15},{10,... | collective-permute-start | bytes 1966088 | tf_op jit(solution)/shard_map/ppermute | solution.py:243
  128.6 16.9 %collective-permute-start.33 = (bf16[2,40,4096]{2,1,0:T(8,128)(2,1)S(1)}, bf16[2,40,4096]{2,1,0:T(8,128)(2,1)S(1)}, u32[]{:S(2)}, u32[]{:S(2)}) collective-permute-start(bf16[2,40,4096]{2,1,0:T(8,128)(2,1)S(1)} %get-tuple-element.75), channel_id=1, source_target_pairs={{0,1},{1,0},{2,3},{3,2},{4,5},{5,4},{6,7},{7,6},{8,9},{9,8},{10,11... | collective-permute-start | bytes 1966088 | tf_op jit(solution)/shard_map/ppermute | solution.py:243
  145.7 16.1 %collective-permute-start.34 = (bf16[2,40,4096]{2,1,0:T(8,128)(2,1)S(1)}, bf16[2,40,4096]{2,1,0:T(8,128)(2,1)S(1)}, u32[]{:S(2)}, u32[]{:S(2)}) collective-permute-start(bf16[2,40,4096]{2,1,0:T(8,128)(2,1)S(1)} %get-tuple-element.76), channel_id=1, source_target_pairs={{0,1},{1,0},{2,3},{3,2},{4,5},{5,4},{6,7},{7,6},{8,9},{9,8},{10,11... | collective-permute-start | bytes 1966088 | tf_op jit(solution)/shard_map/ppermute | solution.py:243
  147.5 36.6 %collective-permute-start.36 = (bf16[2,40,4096]{2,1,0:T(8,128)(2,1)S(1)}, bf16[2,40,4096]{2,1,0:T(8,128)(2,1)S(1)}, u32[]{:S(2)}, u32[]{:S(2)}) collective-permute-start(bf16[2,40,4096]{2,1,0:T(8,128)(2,1)S(1)} %sums.22.refs_2_), channel_id=1, source_target_pairs={{0,4},{1,5},{2,6},{3,7},{4,0},{5,1},{6,2},{7,3},{8,12},{9,13},{10,... | collective-permute-start | bytes 1966088 | tf_op jit(solution)/shard_map/ppermute | solution.py:243
  161.9 34.7 %collective-permute-start.35 = (bf16[2,40,4096]{2,1,0:T(8,128)(2,1)S(1)}, bf16[2,40,4096]{2,1,0:T(8,128)(2,1)S(1)}, u32[]{:S(2)}, u32[]{:S(2)}) collective-permute-start(bf16[2,40,4096]{2,1,0:T(8,128)(2,1)S(1)} %sums.23), channel_id=1, source_target_pairs={{0,2},{1,3},{2,0},{3,1},{4,6},{5,7},{6,4},{7,5},{8,10},{9,11},{10,... | collective-permute-start | bytes 1966088 | tf_op jit(solution)/shard_map/ppermute | solution.py:243
  196.9 1.7 collective-permute-start.37

commit v4 on v3

--- a/solution.py
+++ b/solution.py
@@ -10,6 +10,11 @@
 BLOCK = 64
 CORES = 2
 PLANES = 4
+NEXT = ((0, 1), (1, 0), (2, 3), (3, 2))
+ACROSS = ((1, 2), (2, 1))
+BEYOND = ((1, 3), (2, 0))
+OUTWARD = ((1, 0), (2, 3))
+INWARD = ((0, 1), (3, 2))
 VMEM = 12 * 1024 * 1024
 F32 = jnp.float32
 BF16 = jnp.bfloat16
@@ -40,11 +45,13 @@
 
 
 ANYWHERE = pl.BlockSpec(memory_space=pl.ANY)
+TOKEN = jax.ShapeDtypeStruct((8, 128), F32)
 INSIDE = pl.BlockSpec(memory_space=pltpu.VMEM)
 
 
 def mask_kernel(after_count, core_ref, weight_ref, mask_ref, *refs):
-    kept_ref, spread = refs[after_count:]
+    kept_ref, token_ref, spread = refs[after_count:]
+    token_ref[...] = jnp.zeros_like(token_ref)
     depth, width = weight_ref.shape
     blocks = depth // BLOCK
     step = pl.program_id(0)
@@ -76,10 +83,13 @@
                 pl.BlockSpec(mask.shape, lambda i, core: (0, 0)),
             ]
             + [ANYWHERE] * len(after),
-            out_specs=pl.BlockSpec((rows, width), lambda i, core: (i, 0)),
+            out_specs=[
+                pl.BlockSpec((rows, width), lambda i, core: (i, 0)),
+                pl.BlockSpec(TOKEN.shape, lambda i, core: (0, 0)),
+            ],
             scratch_shapes=[pltpu.VMEM((mask.shape[0], width), F32)],
         ),
-        out_shape=jax.ShapeDtypeStruct((depth, width), weight.dtype),
+        out_shape=[jax.ShapeDtypeStruct((depth, width), weight.dtype), TOKEN],
         compiler_params=params("arbitrary"),
         cost_estimate=cost(0, 4 * depth * width),
         name="masked",
@@ -87,7 +97,8 @@
 
 
 def assemble_kernel(after_count, *refs):
-    block_refs, mine_ref = refs[: -1 - after_count], refs[-1]
+    block_refs, (mine_ref, token_ref) = refs[: -2 - after_count], refs[-2:]
+    token_ref[...] = jnp.zeros_like(token_ref)
     rows = jnp.concatenate([block_ref[...].astype(F32) for block_ref in block_refs], 0)
     mine_ref[...] = rows.astype(BF16)
 
@@ -97,8 +108,8 @@
     return pl.pallas_call(
         functools.partial(assemble_kernel, len(after)),
         in_specs=[INSIDE] * len(blocks) + [ANYWHERE] * len(after),
-        out_specs=INSIDE,
-        out_shape=jax.ShapeDtypeStruct(shape, BF16),
+        out_specs=[INSIDE] * 2,
+        out_shape=[jax.ShapeDtypeStruct(shape, BF16), TOKEN],
         compiler_params=pltpu.CompilerParams(vmem_limit_bytes=VMEM // 2),
         cost_estimate=cost(0, 1000000),
         name="assemble",
@@ -111,7 +122,8 @@
 
 def gate_up_kernel(part_count, after_count, *refs):
     parts, (gate_ref, up_ref) = refs[:part_count], refs[part_count : part_count + 2]
-    keep_ref, near_ref, *far_refs, all_rows = refs[part_count + 2 + after_count :]
+    keep_ref, near_ref, *far_refs, token_ref, all_rows = refs[part_count + 2 + after_count :]
+    token_ref[...] = jnp.zeros_like(token_ref)
     half = parts[0].shape[0] // 2
     kept = half * len(parts)
     for place, part in enumerate(parts):
@@ -138,8 +150,8 @@
     return pl.pallas_call(
         functools.partial(gate_up_kernel, len(parts), len(after)),
         in_specs=[INSIDE] * (len(parts) + 2) + [ANYWHERE] * len(after),
-        out_specs=[INSIDE] * len(shapes),
-        out_shape=[jax.ShapeDtypeStruct(shape, BF16) for shape in shapes],
+        out_specs=[INSIDE] * (len(shapes) + 1),
+        out_shape=[jax.ShapeDtypeStruct(shape, BF16) for shape in shapes] + [TOKEN],
         scratch_shapes=[pltpu.VMEM((rows, depth), BF16)],
         compiler_params=pltpu.CompilerParams(vmem_limit_bytes=VMEM // 2),
         cost_estimate=cost(4 * rows * depth * width, 0),
@@ -148,7 +160,8 @@
 
 
 def down_kernel(after_count, own_ref, other_ref, weight_ref, *refs):
-    *partial_refs, both = refs[after_count:]
+    *partial_refs, token_ref, both = refs[after_count:]
+    token_ref[...] = jnp.zeros_like(token_ref)
     groups, own, depth = own_ref.shape
     rows = groups * own
     both[:rows, :] = own_ref[...].astype(F32).reshape(rows, depth).astype(BF16)
@@ -171,8 +184,8 @@
     return pl.pallas_call(
         functools.partial(down_kernel, len(after)),
         in_specs=[INSIDE] * 3 + [ANYWHERE] * len(after),
-        out_specs=[INSIDE] * groups,
-        out_shape=[jax.ShapeDtypeStruct(shape, BF16)] * groups,
+        out_specs=[INSIDE] * (groups + 1),
+        out_shape=[jax.ShapeDtypeStruct(shape, BF16)] * groups + [TOKEN],
         scratch_shapes=[pltpu.VMEM((CORES * groups * rows, depth), BF16)],
         compiler_params=pltpu.CompilerParams(vmem_limit_bytes=VMEM // 2),
         cost_estimate=cost(2 * CORES * groups * rows * depth * width, 0),
@@ -181,8 +194,9 @@
 
 
 def sums_kernel(sizes, after_count, *refs):
-    to_chips, to_hidden, to_rows = sizes
+    to_chips, to_hidden, *to_rows = sizes
     refs = list(refs)
+    refs.pop()[...] = jnp.zeros(TOKEN.shape, F32)
     ins = [[refs.pop(0) for _ in range(size)] for size in sizes]
     del refs[:after_count]
 
@@ -205,12 +219,12 @@
                     total = total + chip_ref[which, group].astype(F32)
                 both.append(total)
             hidden_ref[group] = (jax.nn.silu(both[0]) * both[1]).astype(BF16)
-    if to_rows:
+    for part_refs in ins[2:]:
         summed_ref = refs.pop(0)
         for core in range(CORES):
-            total = ins[2][0][core].astype(F32)
-            for ref in ins[2][1:]:
-                total = total + ref[core].astype(F32)
+            total = part_refs[0][core].astype(F32)
+            for part_ref in part_refs[1:]:
+                total = total + part_ref[core].astype(F32)
             summed_ref[core] = total.astype(BF16)
 
 
@@ -221,22 +235,23 @@
         shapes += [(two, groups, own, width)] * (chips - 1)
     if to_hidden:
         shapes.append((to_hidden[0].shape[1], *to_hidden[0].shape[3:]))
-    if to_rows:
-        shapes.append(to_rows[0].shape)
-    given = [*to_chips, *to_hidden, *to_rows]
+    shapes += [parts[0].shape for parts in to_rows]
+    given = [to_chips, to_hidden, *to_rows]
+    sizes = tuple(len(parts) for parts in given)
+    given = [part for parts in given for part in parts]
     results = list(pl.pallas_call(
-        functools.partial(sums_kernel, (len(to_chips), len(to_hidden), len(to_rows)), len(after)),
+        functools.partial(sums_kernel, sizes, len(after)),
         in_specs=[INSIDE] * len(given) + [ANYWHERE] * len(after),
-        out_specs=[INSIDE] * len(shapes),
-        out_shape=[jax.ShapeDtypeStruct(shape, BF16) for shape in shapes],
+        out_specs=[INSIDE] * (len(shapes) + 1),
+        out_shape=[jax.ShapeDtypeStruct(shape, BF16) for shape in shapes] + [TOKEN],
         compiler_params=pltpu.CompilerParams(vmem_limit_bytes=VMEM // 2),
         cost_estimate=cost(0, 4000000),
         name="sums",
     )(*given, *after))
+    token = results.pop()
     sent = [results.pop(0) for _ in range(chips - 1)] if to_chips else []
     hidden = results.pop(0) if to_hidden else None
-    summed = results.pop(0) if to_rows else None
-    return sent, hidden, summed
+    return sent, hidden, results, token
 
 
 def swap(values, axis, size, step):
@@ -257,14 +272,15 @@
     for step in [chip * CORES + other for other in range(CORES) for chip in range(chips)]:
         block = lax.dynamic_slice_in_dim(normed, (row ^ step) * features, features, 1)
         blocks.append(swap(block, "rows", row_count, step) if step else block)
-    gate_kept = masked(gate_weight, gate_mask, tile_of(features, 256), nowhere, 1, [normed])
-    mine = assemble(blocks, [gate_kept])
+    gate_kept, token = masked(gate_weight, gate_mask, tile_of(features, 256), nowhere, 1, [normed])
+    mine, token = assemble(blocks, [token])
 
     def behind(values, after):
         return lax.optimization_barrier((values, *after))[0] if after else values
 
-    def by_plane(values, plane, after=()):
-        return swap(behind(values, after), "cols", col_count, plane * per_plane)
+    def by_plane(values, planes, after=()):
+        pairs = [(a * per_plane + b, c * per_plane + b) for a, c in planes for b in range(per_plane)]
+        return lax.ppermute(behind(values, after), "cols", pairs)
 
     def by_row_of_plane(values, step, after=()):
         return swap(behind(values, after), "cols", col_count, step)
@@ -272,82 +288,83 @@
     def by_chip(values, chip, after=()):
         return swap(behind(values, after), "rows", row_count, chip * CORES)
 
-    def by_core(values):
-        return swap(values, "rows", row_count, 1)
-
-    up_kept = masked(up_weight, up_mask, tile_of(features, 256), nowhere, 1, [mine])
-    down_kept = masked(down_weight, down_mask, 2 * BLOCK, place, CORES, [up_kept])
-
-    parts, halves, came, chip_sums, hiddens, others, rows_in, arrived, partials, near = ({} for _ in range(10))
-    last = [down_kept]
-
-    def forward(plane, after=()):
-        parts[plane] = [planes[plane]]
+    def by_core(values, after=()):
+        return swap(behind(values, after), "rows", row_count, 1)
+
+    inner = (lax.axis_index("cols") // per_plane) % 3 != 0
+    parts, halves, near, came, chip_sums, hiddens, others, rows_in, partials = ({} for _ in range(9))
+    last = [token]
+
+    def forward(plane, values, after=()):
+        parts[plane] = [values]
         for step in range(1, per_plane):
-            parts[plane].append(by_row_of_plane(planes[plane], step, after))
-
-    def multiply_in(plane, after=()):
-        halves[plane] = gate_up(parts[plane], gate_kept, up_kept, chips, last + list(after))
-        came[plane] = [by_core(part) for part in halves[plane][2:]]
-        last[:] = [halves[plane][0]]
-
-    def multiply_out(plane, after=()):
-        partials[plane] = down(hiddens[plane], others[plane], down_kept, last + list(after))
-        last[:] = [partials[plane][0]]
-
-    def send_rows(plane, after=()):
+            parts[plane].append(by_row_of_plane(values, step, after))
+
+    def multiply_in(plane, after=(), send_after=()):
+        *halves[plane], last[0] = gate_up(parts[plane], gate_kept, up_kept, chips, last + list(after))
+        came[plane] = [by_core(part, send_after) for part in halves[plane][2:]]
+
+    def multiply_out(plane, after=(), send_after=()):
+        *partials[plane], last[0] = down(hiddens[plane], others[plane], down_kept, last + list(after))
         rows_in[plane] = [partials[plane][0]]
         for step in range(1, per_plane):
-            rows_in[plane].append(by_row_of_plane(partials[plane][step], step, after))
-
-    def add(chip=None, hide=None, rows=None, after=(), chip_after=()):
-        to_chips = [halves[chip][0], *came[chip]] if chip is not None else []
-        to_hidden = [halves[hide][0], near[hide], *chip_sums[hide]] if hide is not None else []
-        to_rows = rows_in[rows] if rows is not None else []
-        sent, hidden, summed = sums(to_chips, to_hidden, to_rows, last + list(after))
-        if chip is not None:
-            chip_sums[chip] = [by_chip(part, number + 1, chip_after) for number, part in enumerate(sent)]
-            near[chip] = by_core(behind(halves[chip][1], sent[:1]))
-            last[:] = sent[:1]
-        if hide is not None:
-            hiddens[hide], others[hide] = hidden, by_core(hidden)
-            last[:] = [hidden]
-        if rows is not None:
-            arrived[rows] = by_plane(summed, rows) if rows else summed
-            last[:] = [summed]
-
-    planes = {0: mine, 3: by_plane(mine, 3), 1: by_plane(mine, 1)}
-    forward(0)
-    multiply_in(0)
-    planes[2] = by_plane(mine, 2, [planes[3], planes[1]])
-    forward(3, last)
-    add(chip=0, after=[planes[3], planes[1]])
-    add(hide=0)
-    forward(1, parts[3][1:])
-    multiply_in(3)
-    add(chip=3)
-    forward(2, parts[1][1:] + last)
-    multiply_in(1, [planes[2]])
-    add(hide=3)
-    add(chip=1)
-    multiply_out(3)
-    send_rows(3, parts[2][1:])
-    multiply_in(2)
-    add(hide=1)
-    add(chip=2)
-    multiply_out(0)
-    send_rows(0, rows_in[3][1:])
-    add(rows=3)
-    multiply_out(1)
-    add(hide=2)
-    multiply_out(2)
-    send_rows(2, rows_in[0][1:])
-    add(rows=0, after=[arrived[3]])
-    add(rows=2)
-    send_rows(1, rows_in[2][1:] + last)
-    add(rows=1)
-
-    arrived = [arrived[plane] for plane in (0, 3, 1, 2)]
+            rows_in[plane].append(by_row_of_plane(partials[plane][step], step, send_after))
+
+    def to_chips(plane, send_after=()):
+        sent, _, _, last[0] = sums([halves[plane][0], *came[plane]], [], [], last)
+        chip_sums[plane] = [by_chip(part, number + 1, send_after) for number, part in enumerate(sent)]
+        near[plane] = by_core(halves[plane][1], last)
+
+    def to_hidden(plane):
+        _, hiddens[plane], _, last[0] = sums([], [halves[plane][0], near[plane], *chip_sums[plane]], [], last)
+        others[plane] = by_core(hiddens[plane])
+
+    def to_rows(*lists, after=()):
+        _, _, summed, last[0] = sums([], [], lists, last + list(after))
+        return summed
+
+    next_mine = by_plane(mine, NEXT)
+    across_mine = by_plane(mine, ACROSS)
+    forward(0, mine)
+    up_kept, last[0] = masked(up_weight, up_mask, tile_of(features, 256), nowhere, 1, last)
+    across_next = by_plane(next_mine, ACROSS, last)
+    outward_mine = by_plane(across_mine, OUTWARD, last)
+    forward(1, next_mine, [*parts[0][1:], *last])
+    down_kept, last[0] = masked(
+        down_weight, down_mask, 2 * BLOCK, place, CORES, last + [next_mine, across_mine, *parts[0][1:]]
+    )
+    two_away = jnp.where(inner, across_next, outward_mine)
+    outward_next = by_plane(across_next, OUTWARD, last)
+    forward(2, two_away, parts[1][1:])
+    multiply_in(1, [across_next, outward_mine])
+    to_chips(1)
+    three_away = jnp.where(inner, across_mine, outward_next)
+    forward(3, three_away, [*parts[2][1:], *last])
+    multiply_in(2, [near[1]])
+    to_hidden(1)
+    to_chips(2)
+    multiply_out(1, send_after=parts[3][1:])
+    multiply_in(3, [near[2]])
+    to_hidden(2)
+    to_chips(3)
+    multiply_out(2, send_after=rows_in[1][1:])
+    (one,) = to_rows(rows_in[1])
+    next_one = by_plane(one, NEXT)
+    multiply_in(0, [near[3]], chip_sums[3])
+    to_hidden(3)
+    multiply_out(3, send_after=rows_in[2][1:])
+    (two,) = to_rows(rows_in[2], after=[next_one])
+    inward_two = by_plane(two, INWARD)
+    to_chips(0)
+    three, three_and_two = to_rows(rows_in[3], [*rows_in[3], inward_two])
+    inward_three = by_plane(three, INWARD)
+    across_three = by_plane(three_and_two, ACROSS)
+    to_hidden(0)
+    multiply_out(0, send_after=rows_in[3][1:])
+    (two_and_three,) = to_rows([two, inward_three])
+    beyond_two = by_plane(two_and_three, BEYOND)
+    arrived = [*rows_in[0], next_one, across_three, beyond_two]
+
     total = arrived[0].astype(F32)
     for part in arrived[1:]:
         total = total + part.astype(F32)

time: 200 us -> 192 us (0.960)
  waiting for transfers between devices: 86.9 us -> 76.4 us
  starting transfers between devices: 42.4 us -> 36.8 us
  local copies, waits for them, and re-layouts: 1.83 us -> 6.03 us
  Pallas kernels: 64.2 us -> 67.2 us
    ppermute x38 -> x32, waiting for transfers between devices: 86.9 us -> 52.4 us  [swap(): lax.ppermute(values, axis, [(place, place ^ step) for place in range(size)])]
    ppermute x0 -> x10, waiting for transfers between devices: none -> 24 us  [by_plane(): return lax.ppermute(behind(values, after), 'cols', pairs)]
    ppermute x38 -> x32, starting transfers between devices: 42.4 us -> 19.3 us  [swap(): lax.ppermute(values, axis, [(place, place ^ step) for place in range(size)])]
    ppermute x0 -> x10, starting transfers between devices: none -> 17.5 us  [by_plane(): return lax.ppermute(behind(values, after), 'cols', pairs)]
    unnamed x12 -> x22, local copies, waits for them, and re-layouts: 1.75 us -> 5.94 us
  transfers between devices with their start and end apart: 38 -> 42, of which waited for: 21 -> 23; matrix products, arithmetic and copies ran while one was open for 0% -> 0% of each run, Pallas kernels for 32% -> 31%
where the time goes in v4:
time: 192 us; the launch traced here: 191 us
  waiting for transfers between devices  76.4 us (40%)
  Pallas kernels  67.2 us (35%)
  starting transfers between devices  36.8 us (19%)
  local copies, waits for them, and re-layouts  6.03 us (3%)
  other arithmetic  4.2 us (2%)
    ppermute x32, waiting for transfers between devices, swap(): lax.ppermute(values, axis, [(place, place ^ step) for place in range(size)])  52.4 us
    pallas_call x4, Pallas kernels, gate_up(): pl.pallas_call(functools.partial(gate_up_kernel, len(parts), len(after)),...  25.4 us
    ppermute x10, waiting for transfers between devices, by_plane(): return lax.ppermute(behind(values, after), 'cols', pairs)  24 us
    pallas_call x3, Pallas kernels, masked(): pl.pallas_call(functools.partial(mask_kernel, len(after)), grid_spec=pltp...  23.2 us
    ppermute x32, starting transfers between devices, swap(): lax.ppermute(values, axis, [(place, place ^ step) for place in range(size)])  19.3 us
    ppermute x10, starting transfers between devices, by_plane(): return lax.ppermute(behind(values, after), 'cols', pairs)  17.5 us
    pallas_call x4, Pallas kernels, down(): pl.pallas_call(functools.partial(down_kernel, len(after)), in_specs=[INSI...  15.4 us
    unnamed x22, local copies, waits for them, and re-layouts  5.94 us
  transfers between devices with their start and end apart: 42, of which 23 were waited for; matrix products, arithmetic and copies ran while one was open for 0% of the time, Pallas kernels for 31%

profile of v4, /device:TPU:0, one launch (start us, length us, event | category | flops | bytes accessed | tf_op | source)
XLA Modules:
  0.0 191.3 jit_solution(12534288558490588765)
XLA Ops:
  0.0 1.3 fusion
  1.4 1.3 fusion.2.refs_0_
  2.7 2.4 %collective-permute-start.2 = (bf16[40,2048]{1,0:T(8,128)(2,1)S(1)}, bf16[40,2048]{1,0:T(8,128)(2,1)S(1)}, u32[]{:S(2)}, u32[]{:S(2)}) collective-permute-start(bf16[40,2048]{1,0:T(8,128)(2,1)S(1)} %get-tuple-element.167), channel_id=1, source_target_pairs={{0,24},{8,16},{16,8},{24,0},{1,25},{9,17},{17,9},{25,1},{2,26},{10... | collective-permute-start | bytes 491528 | tf_op jit(solution)/shard_map/ppermute | solution.py:258
  5.9 5.6 %masked.3 = (bf16[2048,1792]{1,0:T(8,128)(2,1)S(1)}, f32[8,128]{1,0:T(8,128)S(1)}) custom-call(s32[1]{0:T(128)} %constant.51.clone.1.core_ref, bf16[2048,1792]{1,0:T(8,128)(2,1)} %weight_ref.3, s32[32,28]{1,0:T(8,128)S(1)} %copy-done.4, bf16[40,8192]{1,0:T(8,128)(2,1)S(1)} %fusion.2.refs_0_), custom_call_target="tpu_custom_call" | custom-call | bytes 14680 | tf_op jit(solution)/shard_map/masked/pallas_call | solution.py:76
  11.6 2.9 %copy-done = bf16[2048,1792]{1,0:T(8,128)(2,1)} copy-done((bf16[2048,1792]{1,0:T(8,128)(2,1)}, bf16[2048,1792]{1,0:T(8,128)(2,1)S(1)}, u32[]{:S(2)}) %copy-start) | copy-done | bytes 7340056
  14.6 0.7 collective-permute-start.6
  15.3 4.9 %collective-permute-start.4 = (bf16[160,2048]{1,0:T(8,128)(2,1)S(1)}, bf16[160,2048]{1,0:T(8,128)(2,1)S(1)}, u32[]{:S(2)}, u32[]{:S(2)}) collective-permute-start(bf16[160,2048]{1,0:T(8,128)(2,1)S(1)} %get-tuple-element.86.refs_0_), channel_id=1, source_target_pairs={{0,2},{1,3},{2,0},{3,1},{4,6},{5,7},{6,4},{7,5},{8,10},{9,11},{10,... | collective-permute-start | bytes 1966088 | tf_op jit(solution)/shard_map/ppermute | solution.py:283
  20.2 1.5 collective-permute-start.3
  21.7 5.7 %masked.4 = (bf16[2048,1792]{1,0:T(8,128)(2,1)S(1)}, f32[8,128]{1,0:T(8,128)S(1)}) custom-call(s32[1]{0:T(128)} %constant.51.clone.1.core_ref, bf16[2048,1792]{1,0:T(8,128)(2,1)} %weight_ref.4, s32[32,28]{1,0:T(8,128)S(1)} %copy-done.5, f32[8,128]{1,0:T(8,128)S(1)} %get-tuple-element.88.refs_0_), custom_call_target="tpu_custom_call" | custom-call | bytes 14680 | tf_op jit(solution)/shard_map/masked/pallas_call | solution.py:76
  27.4 3.0 %copy-done.1 = bf16[2048,1792]{1,0:T(8,128)(2,1)} copy-done((bf16[2048,1792]{1,0:T(8,128)(2,1)}, bf16[2048,1792]{1,0:T(8,128)(2,1)S(1)}, u32[]{:S(2)}) %copy-start.1) | copy-done | bytes 7340056
  30.4 4.1 %collective-permute-done.4.refs_1_.refs_0_ = bf16[160,2048]{1,0:T(8,128)(2,1)S(1)} collective-permute-done((bf16[160,2048]{1,0:T(8,128)(2,1)S(1)}, bf16[160,2048]{1,0:T(8,128)(2,1)S(1)}, u32[]{:S(2)}, u32[]{:S(2)}) %collective-permute-start.4) | collective-permute-done | bytes 655392 | tf_op jit(solution)/shard_map/ppermute | solution.py:283
  34.5 1.5 collective-permute-done.3.refs_3_.refs_1_
  36.0 1.5 collective-permute-start.5
  38.2 1.3 collective-permute-start.8
  39.6 11.9 %masked.5 = (bf16[1792,4096]{1,0:T(8,128)(2,1)S(1)}, f32[8,128]{1,0:T(8,128)S(1)}) custom-call(s32[1]{0:T(128)} %bitcast.core_ref, bf16[1792,8192]{1,0:T(8,128)(2,1)} %weight_ref.5, s32[28,128]{1,0:T(8,128)S(1)} %copy-done.6, f32[8,128]{1,0:T(8,128)S(1)} %get-tuple-element.90.refs_0_, bf16[160,2048]{1,0:T(8,128)(2,1)S(1)} %collective-permute-done.4.refs_1_.refs_0_, ...), custom_call_target="tpu_custom_call" | custom-call | bytes 29360 | tf_op jit(solution)/shard_map/masked/pallas_call | solution.py:76
  51.5 3.1 %collective-permute-done.8.refs_6_ = bf16[160,2048]{1,0:T(8,128)(2,1)S(1)} collective-permute-done((bf16[160,2048]{1,0:T(8,128)(2,1)S(1)}, bf16[160,2048]{1,0:T(8,128)(2,1)S(1)}, u32[]{:S(2)}, u32[]{:S(2)}) %collective-permute-start.8) | collective-permute-done | bytes 655392 | tf_op jit(solution)/shard_map/ppermute | solution.py:283
  54.7 7.2 %gate_up.4 = (bf16[2,2,2,40,1792]{4,3,2,1,0:T(8,128)(2,1)S(1)}, bf16[2,2,40,1792]{3,2,1,0:T(8,128)(2,1)S(1)}, bf16[2,1,40,1792]{3,2,1,0:T(8,128)(2,1)S(1)}, bf16...) custom-call(bf16[160,2048]{1,0:T(8,128)(2,1)S(1)} %collective-permute-done.4.refs_1_.refs_0_, ...), custom_call_target="tpu_custom_call" | custom-call | flops 4697620 | tf_op jit(solution)/shard_map/gate_up/pallas_call | solution.py:150
  63.1 1.3 collective-permute-start.17
  64.7 1.6 collective-permute-start.12
  66.2 13.1 %collective-permute-done.13.refs_1_ = bf16[160,2048]{1,0:T(8,128)(2,1)S(1)} collective-permute-done((bf16[160,2048]{1,0:T(8,128)(2,1)S(1)}, bf16[160,2048]{1,0:T(8,128)(2,1)S(1)}, u32[]{:S(2)}, u32[]{:S(2)}) %collective-permute-start.13) | collective-permute-done | bytes 655392 | tf_op jit(solution)/shard_map/ppermute | solution.py:258
  79.3 6.1 %gate_up.5 = (bf16[2,2,2,40,1792]{4,3,2,1,0:T(8,128)(2,1)S(1)}, bf16[2,2,40,1792]{3,2,1,0:T(8,128)(2,1)S(1)}, bf16[2,1,40,1792]{3,2,1,0:T(8,128)(2,1)S(1)}, bf16...) custom-call(bf16[160,2048]{1,0:T(8,128)(2,1)S(1)} %broadcast_select_fusion.1.refs_0_, ...), custom_call_target="tpu_custom_call" | custom-call | flops 4697620 | tf_op jit(solution)/shard_map/gate_up/pallas_call | solution.py:150
  88.2 1.5 collective-permute-start.21
  90.1 3.9 %down.4 = (bf16[2,40,4096]{2,1,0:T(8,128)(2,1)S(1)}, bf16[2,40,4096]{2,1,0:T(8,128)(2,1)S(1)}, f32[8,128]{1,0:T(8,128)S(1)}) custom-call(bf16[2,40,1792]{2,1,0:T(8,128)(2,1)S(1)} %get-tuple-element.105.own_ref, bf16[2,40,1792]{2,1,0:T(8,128)(2,1)S(1)} %collective-permute-done.14.other_ref, bf16[1792,4096]{1,0:T(8,128)(2,1)S(1)} %get-tuple-element.106.weight_ref, ...), custom_call_target="tpu_custom_call" | custom-call | flops 2348810 | tf_op jit(solution)/shard_map/down/pallas_call | solution.py:184
  93.9 8.9 %collective-permute-done.18.refs_1_ = bf16[160,2048]{1,0:T(8,128)(2,1)S(1)} collective-permute-done((bf16[160,2048]{1,0:T(8,128)(2,1)S(1)}, bf16[160,2048]{1,0:T(8,128)(2,1)S(1)}, u32[]{:S(2)}, u32[]{:S(2)}) %collective-permute-start.18) | collective-permute-done | bytes 655392 | tf_op jit(solution)/shard_map/ppermute | solution.py:258
  103.4 6.1 %gate_up.6 = (bf16[2,2,2,40,1792]{4,3,2,1,0:T(8,128)(2,1)S(1)}, bf16[2,2,40,1792]{3,2,1,0:T(8,128)(2,1)S(1)}, bf16[2,1,40,1792]{3,2,1,0:T(8,128)(2,1)S(1)}, bf16...) custom-call(bf16[160,2048]{1,0:T(8,128)(2,1)S(1)} %broadcast_select_fusion.refs_0_, ...), custom_call_target="tpu_custom_call" | custom-call | flops 4697620 | tf_op jit(solution)/shard_map/gate_up/pallas_call | solution.py:150
  111.9 1.5 collective-permute-start.26
  113.4 3.8 %down.5 = (bf16[2,40,4096]{2,1,0:T(8,128)(2,1)S(1)}, bf16[2,40,4096]{2,1,0:T(8,128)(2,1)S(1)}, f32[8,128]{1,0:T(8,128)S(1)}) custom-call(bf16[2,40,1792]{2,1,0:T(8,128)(2,1)S(1)} %get-tuple-element.122.own_ref, bf16[2,40,1792]{2,1,0:T(8,128)(2,1)S(1)} %collective-permute-done.22.other_ref, bf16[1792,4096]{1,0:T(8,128)(2,1)S(1)} %get-tuple-element.106.weight_ref, ...), custom_call_target="tpu_custom_call" | custom-call | flops 2348810 | tf_op jit(solution)/shard_map/down/pallas_call | solution.py:184
  117.2 1.5 collective-permute-done.19.refs_1_
  119.5 6.1 %gate_up.7 = (bf16[2,2,2,40,1792]{4,3,2,1,0:T(8,128)(2,1)S(1)}, bf16[2,2,40,1792]{3,2,1,0:T(8,128)(2,1)S(1)}, bf16[2,1,40,1792]{3,2,1,0:T(8,128)(2,1)S(1)}, bf16...) custom-call(bf16[160,2048]{1,0:T(8,128)(2,1)S(1)} %copy-done.3, ...), custom_call_target="tpu_custom_call" | custom-call | flops 4697620 | tf_op jit(solution)/shard_map/gate_up/pallas_call | solution.py:150
  125.6 1.5 collective-permute-done.26.refs_2_
  127.5 1.6 collective-permute-done.30.other_ref
  129.1 3.9 %down.6 = (bf16[2,40,4096]{2,1,0:T(8,128)(2,1)S(1)}, bf16[2,40,4096]{2,1,0:T(8,128)(2,1)S(1)}, f32[8,128]{1,0:T(8,128)S(1)}) custom-call(bf16[2,40,1792]{2,1,0:T(8,128)(2,1)S(1)} %get-tuple-element.143.own_ref, bf16[2,40,1792]{2,1,0:T(8,128)(2,1)S(1)} %collective-permute-done.30.other_ref, bf16[1792,4096]{1,0:T(8,128)(2,1)S(1)} %get-tuple-element.106.weight_ref, ...), custom_call_target="tpu_custom_call" | custom-call | flops 2348810 | tf_op jit(solution)/shard_map/down/pallas_call | solution.py:184
  132.9 1.1 collective-permute-done.29.refs_1_
  134.1 1.5 collective-permute-start.34
  135.7 2.2 %collective-permute-start.35 = (bf16[2,40,4096]{2,1,0:T(8,128)(2,1)S(1)}, bf16[2,40,4096]{2,1,0:T(8,128)(2,1)S(1)}, u32[]{:S(2)}, u32[]{:S(2)}) collective-permute-start(bf16[2,40,4096]{2,1,0:T(8,128)(2,1)S(1)} %get-tuple-element.154.refs_0_), channel_id=1, source_target_pairs={{0,2},{1,3},{6,4},{7,5},{8,10},{9,11},{14,12},{15,13},{16,18},{17,... | collective-permute-start | bytes 1966088 | tf_op jit(solution)/shard_map/ppermute | solution.py:283
  138.5 1.1 collective-permute-done.28.refs_2_
  140.3 0.7 collective-permute-start.33
  141.0 8.8 %collective-permute-done.34.refs_1_.refs_3_ = bf16[2,40,4096]{2,1,0:T(8,128)(2,1)S(1)} collective-permute-done((bf16[2,40,4096]{2,1,0:T(8,128)(2,1)S(1)}, bf16[2,40,4096]{2,1,0:T(8,128)(2,1)S(1)}, u32[]{:S(2)}, u32[]{:S(2)}) %collective-permute-start.34) | collective-permute-done | bytes 655392 | tf_op jit(solution)/shard_map/ppermute | solution.py:258
  149.8 1.3 collective-permute-done.35.refs_4_
  151.4 4.4 %collective-permute-start.39 = (bf16[2,40,4096]{2,1,0:T(8,128)(2,1)S(1)}, bf16[2,40,4096]{2,1,0:T(8,128)(2,1)S(1)}, u32[]{:S(2)}, u32[]{:S(2)}) collective-permute-start(bf16[2,40,4096]{2,1,0:T(8,128)(2,1)S(1)} %get-tuple-element.162), channel_id=1, source_target_pairs={{0,2},{1,3},{6,4},{7,5},{8,10},{9,11},{14,12},{15,13},{16,18},{17,... | collective-permute-start | bytes 1966088 | tf_op jit(solution)/shard_map/ppermute | solution.py:283
  157.0 0.8 collective-permute-done.36.other_ref
  157.8 3.9 %down.7 = (bf16[2,40,4096]{2,1,0:T(8,128)(2,1)S(1)}, bf16[2,40,4096]{2,1,0:T(8,128)(2,1)S(1)}, f32[8,128]{1,0:T(8,128)S(1)}) custom-call(bf16[2,40,1792]{2,1,0:T(8,128)(2,1)S(1)} %get-tuple-element.156.own_ref, bf16[2,40,1792]{2,1,0:T(8,128)(2,1)S(1)} %collective-permute-done.36.other_ref, bf16[1792,4096]{1,0:T(8,128)(2,1)S(1)} %get-tuple-element.106.weight_ref, ...), custom_call_target="tpu_custom_call" | custom-call | flops 2348810 | tf_op jit(solution)/shard_map/down/pallas_call | solution.py:184
  162.3 5.8 %collective-permute-done.39.refs_1_ = bf16[2,40,4096]{2,1,0:T(8,128)(2,1)S(1)} collective-permute-done((bf16[2,40,4096]{2,1,0:T(8,128)(2,1)S(1)}, bf16[2,40,4096]{2,1,0:T(8,128)(2,1)S(1)}, u32[]{:S(2)}, u32[]{:S(2)}) %collective-permute-start.39) | collective-permute-done | bytes 655392 | tf_op jit(solution)/shard_map/ppermute | solution.py:283
  168.7 1.3 collective-permute-start.40
  170.0 8.5 %collective-permute-done.37 = bf16[2,40,4096]{2,1,0:T(8,128)(2,1)S(1)} collective-permute-done((bf16[2,40,4096]{2,1,0:T(8,128)(2,1)S(1)}, bf16[2,40,4096]{2,1,0:T(8,128)(2,1)S(1)}, u32[]{:S(2)}, u32[]{:S(2)}) %collective-permute-start.37) | collective-permute-done | bytes 655392 | tf_op jit(solution)/shard_map/ppermute | solution.py:258
  178.5 9.6 %collective-permute-done.40 = bf16[2,40,4096]{2,1,0:T(8,128)(2,1)S(1)} collective-permute-done((bf16[2,40,4096]{2,1,0:T(8,128)(2,1)S(1)}, bf16[2,40,4096]{2,1,0:T(8,128)(2,1)S(1)}, u32[]{:S(2)}, u32[]{:S(2)}) %collective-permute-start.40) | collective-permute-done | bytes 655392 | tf_op jit(solution)/shard_map/ppermute | solution.py:283
  188.7 1.6 collective-permute-done.41
  190.4 0.9 pad_maximum_fusion
  (94 shorter events, 14.9 us)
Async XLA Ops:
  2.7 11.8 %collective-permute-start.2 = (bf16[40,2048]{1,0:T(8,128)(2,1)S(1)}, bf16[40,2048]{1,0:T(8,128)(2,1)S(1)}, u32[]{:S(2)}, u32[]{:S(2)}) collective-permute-start(bf16[40,2048]{1,0:T(8,128)(2,1)S(1)} %get-tuple-element.167), channel_id=1, source_target_pairs={{0,24},{8,16},{16,8},{24,0},{1,25},{9,17},{17,9},{25,1},{2,26},{10... | collective-permute-start | bytes 491528 | tf_op jit(solution)/shard_map/ppermute | solution.py:258
  5.2 9.3 %collective-permute-start.1 = (bf16[40,2048]{1,0:T(8,128)(2,1)S(1)}, bf16[40,2048]{1,0:T(8,128)(2,1)S(1)}, u32[]{:S(2)}, u32[]{:S(2)}) collective-permute-start(bf16[40,2048]{1,0:T(8,128)(2,1)S(1)} %get-tuple-element.168), channel_id=1, source_target_pairs={{0,8},{8,0},{16,24},{24,16},{1,9},{9,1},{17,25},{25,17},{2,10},{10... | collective-permute-start | bytes 491528 | tf_op jit(solution)/shard_map/ppermute | solution.py:258
  5.9 15.8 %copy-start.5 = (s32[32,28]{1,0:T(8,128)S(1)}, s32[32,28]{1,0:T(8,128)}, u32[]{:S(2)}) copy-start(s32[32,28]{1,0:T(8,128)} %mask_ref.4) | copy-start | bytes 10756
  5.9 8.6 %collective-permute-start = (bf16[40,2048]{1,0:T(8,128)(2,1)S(1)}, bf16[40,2048]{1,0:T(8,128)(2,1)S(1)}, u32[]{:S(2)}, u32[]{:S(2)}) collective-permute-start(bf16[40,2048]{1,0:T(8,128)(2,1)S(1)} %get-tuple-element.169), channel_id=1, source_target_pairs={{0,16},{8,24},{16,0},{24,8},{1,17},{9,25},{17,1},{25,9},{2,18},{10... | collective-permute-start | bytes 491528 | tf_op jit(solution)/shard_map/ppermute | solution.py:258
  14.6 15.8 %collective-permute-start.6 = (bf16[160,2048]{1,0:T(8,128)(2,1)S(1)}, bf16[160,2048]{1,0:T(8,128)(2,1)S(1)}, u32[]{:S(2)}, u32[]{:S(2)}) collective-permute-start(bf16[160,2048]{1,0:T(8,128)(2,1)S(1)} %get-tuple-element.86.refs_0_), channel_id=1, source_target_pairs={{2,4},{3,5},{4,2},{5,3},{10,12},{11,13},{12,10},{13,11},{18,20},{1... | collective-permute-start | bytes 1966088 | tf_op jit(solution)/shard_map/ppermute | solution.py:283
  15.3 19.2 %collective-permute-start.4 = (bf16[160,2048]{1,0:T(8,128)(2,1)S(1)}, bf16[160,2048]{1,0:T(8,128)(2,1)S(1)}, u32[]{:S(2)}, u32[]{:S(2)}) collective-permute-start(bf16[160,2048]{1,0:T(8,128)(2,1)S(1)} %get-tuple-element.86.refs_0_), channel_id=1, source_target_pairs={{0,2},{1,3},{2,0},{3,1},{4,6},{5,7},{6,4},{7,5},{8,10},{9,11},{10,... | collective-permute-start | bytes 1966088 | tf_op jit(solution)/shard_map/ppermute | solution.py:283
  20.2 15.8 %collective-permute-start.3 = (bf16[160,2048]{1,0:T(8,128)(2,1)S(1)}, bf16[160,2048]{1,0:T(8,128)(2,1)S(1)}, u32[]{:S(2)}, u32[]{:S(2)}) collective-permute-start(bf16[160,2048]{1,0:T(8,128)(2,1)S(1)} %get-tuple-element.86.refs_0_), channel_id=1, source_target_pairs={{0,1},{1,0},{2,3},{3,2},{4,5},{5,4},{6,7},{7,6},{8,9},{9,8},{10,11... | collective-permute-start | bytes 1966088 | tf_op jit(solution)/shard_map/ppermute | solution.py:258
  21.7 17.9 %copy-start.6 = (s32[28,128]{1,0:T(8,128)S(1)}, s32[28,128]{1,0:T(8,128)}, u32[]{:S(2)}) copy-start(s32[28,128]{1,0:T(8,128)} %mask_ref.5) | copy-start | bytes 43012
  36.0 15.5 %collective-permute-start.5 = (bf16[160,2048]{1,0:T(8,128)(2,1)S(1)}, bf16[160,2048]{1,0:T(8,128)(2,1)}, u32[]{:S(2)}, u32[]{:S(2)}) collective-permute-start(bf16[160,2048]{1,0:T(8,128)(2,1)S(1)} %collective-permute-done.4.refs_1_.refs_0_), channel_id=1, source_target_pairs={{0,1},{1,0},{2,3},{3,2},{4,5},{5,4},{6,7},{7,6},{8,9},{9,8},{10,11... | collective-permute-start | bytes 1966088 | tf_op jit(solution)/shard_map/ppermute | solution.py:258
  37.5 14.0 %collective-permute-start.7 = (bf16[160,2048]{1,0:T(8,128)(2,1)S(1)}, bf16[160,2048]{1,0:T(8,128)(2,1)S(1)}, u32[]{:S(2)}, u32[]{:S(2)}) collective-permute-start(bf16[160,2048]{1,0:T(8,128)(2,1)S(1)} %collective-permute-done.4.refs_1_.refs_0_), channel_id=1, source_target_pairs={{2,4},{3,5},{4,2},{5,3},{10,12},{11,13},{12,10},{13,11},{18,20},{1... | collective-permute-start | bytes 1966088 | tf_op jit(solution)/shard_map/ppermute | solution.py:283
  38.2 16.5 %collective-permute-start.8 = (bf16[160,2048]{1,0:T(8,128)(2,1)S(1)}, bf16[160,2048]{1,0:T(8,128)(2,1)S(1)}, u32[]{:S(2)}, u32[]{:S(2)}) collective-permute-start(bf16[160,2048]{1,0:T(8,128)(2,1)S(1)} %collective-permute-done.6.refs_2_), channel_id=1, source_target_pairs={{2,0},{3,1},{4,6},{5,7},{10,8},{11,9},{12,14},{13,15},{18,16},{19,... | collective-permute-start | bytes 1966088 | tf_op jit(solution)/shard_map/ppermute | solution.py:283
  39.5 15.2 %slice-start = ((s8[7340032]{0:T(1024)(128)(4,1)}), s8[4194304]{0:T(1024)(128)(4,1)S(1)}, s32[]{:S(2)}) async-start(s8[7340032]{0:T(1024)(128)(4,1)} %bitcast.9), calls=%async_computation | async-start | bytes 8388608
  39.6 15.1 %slice-start.2 = ((s8[7340032]{0:T(1024)(128)(4,1)}), s8[4194304]{0:T(1024)(128)(4,1)S(1)}, s32[]{:S(2)}) async-start(s8[7340032]{0:T(1024)(128)(4,1)} %bitcast.11), calls=%async_computation.2 | async-start | bytes 8388608
  39.6 15.1 %slice-start.1 = ((s8[7340032]{0:T(1024)(128)(4,1)}), s8[3145728]{0:T(1024)(128)(4,1)S(1)}, s32[]{:S(2)}) async-start(s8[7340032]{0:T(1024)(128)(4,1)} %bitcast.9), calls=%async_computation.1 | async-start | bytes 6291456
  39.6 15.1 %slice-start.3 = ((s8[7340032]{0:T(1024)(128)(4,1)}), s8[3145728]{0:T(1024)(128)(4,1)S(1)}, s32[]{:S(2)}) async-start(s8[7340032]{0:T(1024)(128)(4,1)} %bitcast.11), calls=%async_computation.3 | async-start | bytes 6291456
  61.9 2.5 %collective-permute-start.9 = (bf16[2,1,40,1792]{3,2,1,0:T(8,128)(2,1)S(1)}, bf16[2,1,40,1792]{3,2,1,0:T(8,128)(2,1)S(1)}, u32[]{:S(2)}, u32[]{:S(2)}) collective-permute-start(bf16[2,1,40,1792]{3,2,1,0:T(8,128)(2,1)S(1)} %get-tuple-element.97), channel_id=1, source_target_pairs={{0,8},{8,0},{16,24},{24,16},{1,9},{9,1},{17,25},{25,17},{2,10},{10... | collective-permute-start | bytes 860168 | tf_op jit(solution)/shard_map/ppermute | solution.py:258
  62.0 2.4 %collective-permute-start.10 = (bf16[2,1,40,1792]{3,2,1,0:T(8,128)(2,1)S(1)}, bf16[2,1,40,1792]{3,2,1,0:T(8,128)(2,1)S(1)}, u32[]{:S(2)}, u32[]{:S(2)}) collective-permute-start(bf16[2,1,40,1792]{3,2,1,0:T(8,128)(2,1)S(1)} %get-tuple-element.98), channel_id=1, source_target_pairs={{0,8},{8,0},{16,24},{24,16},{1,9},{9,1},{17,25},{25,17},{2,10},{10... | collective-permute-start | bytes 860168 | tf_op jit(solution)/shard_map/ppermute | solution.py:258
  62.6 16.8 %collective-permute-start.13 = (bf16[160,2048]{1,0:T(8,128)(2,1)S(1)}, bf16[160,2048]{1,0:T(8,128)(2,1)S(1)}, u32[]{:S(2)}, u32[]{:S(2)}) collective-permute-start(bf16[160,2048]{1,0:T(8,128)(2,1)S(1)} %broadcast_select_fusion.1.refs_0_), channel_id=1, source_target_pairs={{0,1},{1,0},{2,3},{3,2},{4,5},{5,4},{6,7},{7,6},{8,9},{9,8},{10,11... | collective-permute-start | bytes 1966088 | tf_op jit(solution)/shard_map/ppermute | solution.py:258
  63.1 22.9 %collective-permute-start.17 = (bf16[160,2048]{1,0:T(8,128)(2,1)S(1)}, bf16[160,2048]{1,0:T(8,128)(2,1)S(1)}, u32[]{:S(2)}, u32[]{:S(2)}) collective-permute-start(bf16[160,2048]{1,0:T(8,128)(2,1)S(1)} %collective-permute-done.7.refs_5_), channel_id=1, source_target_pairs={{2,0},{3,1},{4,6},{5,7},{10,8},{11,9},{12,14},{13,15},{18,16},{19,... | collective-permute-start | bytes 1966088 | tf_op jit(solution)/shard_map/ppermute | solution.py:283
  64.6 14.8 %collective-permute-start.11 = (bf16[2,2,40,1792]{3,2,1,0:T(8,128)(2,1)S(1)}, bf16[2,2,40,1792]{3,2,1,0:T(8,128)(2,1)S(1)}, u32[]{:S(2)}, u32[]{:S(2)}) collective-permute-start(bf16[2,2,40,1792]{3,2,1,0:T(8,128)(2,1)S(1)} %get-tuple-element.101), channel_id=1, source_target_pairs={{0,8},{8,0},{16,24},{24,16},{1,9},{9,1},{17,25},{25,17},{2,10},{10... | collective-permute-start | bytes 1720328 | tf_op jit(solution)/shard_map/ppermute | solution.py:258
  64.7 22.0 %collective-permute-start.12 = (bf16[2,2,40,1792]{3,2,1,0:T(8,128)(2,1)S(1)}, bf16[2,2,40,1792]{3,2,1,0:T(8,128)(2,1)S(1)}, u32[]{:S(2)}, u32[]{:S(2)}) collective-permute-start(bf16[2,2,40,1792]{3,2,1,0:T(8,128)(2,1)S(1)} %get-tuple-element.102), channel_id=1, source_target_pairs={{0,16},{8,24},{16,0},{24,8},{1,17},{9,25},{17,1},{25,9},{2,18},{10... | collective-permute-start | bytes 1720328 | tf_op jit(solution)/shard_map/ppermute | solution.py:258
  85.4 1.6 collective-permute-start.15
  85.5 2.0 %collective-permute-start.16 = (bf16[2,1,40,1792]{3,2,1,0:T(8,128)(2,1)S(1)}, bf16[2,1,40,1792]{3,2,1,0:T(8,128)(2,1)S(1)}, u32[]{:S(2)}, u32[]{:S(2)}) collective-permute-start(bf16[2,1,40,1792]{3,2,1,0:T(8,128)(2,1)S(1)} %get-tuple-element.109), channel_id=1, source_target_pairs={{0,8},{8,0},{16,24},{24,16},{1,9},{9,1},{17,25},{25,17},{2,10},{10... | collective-permute-start | bytes 860168 | tf_op jit(solution)/shard_map/ppermute | solution.py:258
  86.1 16.8 %collective-permute-start.18 = (bf16[160,2048]{1,0:T(8,128)(2,1)S(1)}, bf16[160,2048]{1,0:T(8,128)(2,1)S(1)}, u32[]{:S(2)}, u32[]{:S(2)}) collective-permute-start(bf16[160,2048]{1,0:T(8,128)(2,1)S(1)} %broadcast_select_fusion.refs_0_), channel_id=1, source_target_pairs={{0,1},{1,0},{2,3},{3,2},{4,5},{5,4},{6,7},{7,6},{8,9},{9,8},{10,11... | collective-permute-start | bytes 1966088 | tf_op jit(solution)/shard_map/ppermute | solution.py:258
  87.6 15.7 %collective-permute-start.20 = (bf16[2,2,40,1792]{3,2,1,0:T(8,128)(2,1)S(1)}, bf16[2,2,40,1792]{3,2,1,0:T(8,128)(2,1)S(1)}, u32[]{:S(2)}, u32[]{:S(2)}) collective-permute-start(bf16[2,2,40,1792]{3,2,1,0:T(8,128)(2,1)S(1)} %get-tuple-element.118), channel_id=1, source_target_pairs={{0,8},{8,0},{16,24},{24,16},{1,9},{9,1},{17,25},{25,17},{2,10},{10... | collective-permute-start | bytes 1720328 | tf_op jit(solution)/shard_map/ppermute | solution.py:258
  87.8 2.3 %collective-permute-start.14 = (bf16[2,40,1792]{2,1,0:T(8,128)(2,1)S(1)}, bf16[2,40,1792]{2,1,0:T(8,128)(2,1)S(1)}, u32[]{:S(2)}, u32[]{:S(2)}) collective-permute-start(bf16[2,40,1792]{2,1,0:T(8,128)(2,1)S(1)} %get-tuple-element.105.own_ref), channel_id=1, source_target_pairs={{0,8},{8,0},{16,24},{24,16},{1,9},{9,1},{17,25},{25,17},{2,10},{10... | collective-permute-start | bytes 860168 | tf_op jit(solution)/shard_map/ppermute | solution.py:258
  88.2 21.8 %collective-permute-start.21 = (bf16[2,2,40,1792]{3,2,1,0:T(8,128)(2,1)S(1)}, bf16[2,2,40,1792]{3,2,1,0:T(8,128)(2,1)S(1)}, u32[]{:S(2)}, u32[]{:S(2)}) collective-permute-start(bf16[2,2,40,1792]{3,2,1,0:T(8,128)(2,1)S(1)} %get-tuple-element.119), channel_id=1, source_target_pairs={{0,16},{8,24},{16,0},{24,8},{1,17},{9,25},{17,1},{25,9},{2,18},{10... | collective-permute-start | bytes 1720328 | tf_op jit(solution)/shard_map/ppermute | solution.py:258
  102.9 15.9 %collective-permute-start.19 = (bf16[2,40,4096]{2,1,0:T(8,128)(2,1)S(1)}, bf16[2,40,4096]{2,1,0:T(8,128)(2,1)S(1)}, u32[]{:S(2)}, u32[]{:S(2)}) collective-permute-start(bf16[2,40,4096]{2,1,0:T(8,128)(2,1)S(1)} %get-tuple-element.116), channel_id=1, source_target_pairs={{0,1},{1,0},{2,3},{3,2},{4,5},{5,4},{6,7},{7,6},{8,9},{9,8},{10,11... | collective-permute-start | bytes 1966088 | tf_op jit(solution)/shard_map/ppermute | solution.py:258
  109.5 1.6 collective-permute-start.23
  109.5 2.0 %collective-permute-start.24 = (bf16[2,1,40,1792]{3,2,1,0:T(8,128)(2,1)S(1)}, bf16[2,1,40,1792]{3,2,1,0:T(8,128)(2,1)S(1)}, u32[]{:S(2)}, u32[]{:S(2)}) collective-permute-start(bf16[2,1,40,1792]{3,2,1,0:T(8,128)(2,1)S(1)} %get-tuple-element.125), channel_id=1, source_target_pairs={{0,8},{8,0},{16,24},{24,16},{1,9},{9,1},{17,25},{25,17},{2,10},{10... | collective-permute-start | bytes 860168 | tf_op jit(solution)/shard_map/ppermute | solution.py:258
  110.3 3.0 %collective-permute-start.22 = (bf16[2,40,1792]{2,1,0:T(8,128)(2,1)S(1)}, bf16[2,40,1792]{2,1,0:T(8,128)(2,1)S(1)}, u32[]{:S(2)}, u32[]{:S(2)}) collective-permute-start(bf16[2,40,1792]{2,1,0:T(8,128)(2,1)S(1)} %get-tuple-element.122.own_ref), channel_id=1, source_target_pairs={{0,8},{8,0},{16,24},{24,16},{1,9},{9,1},{17,25},{25,17},{2,10},{10... | collective-permute-start | bytes 860168 | tf_op jit(solution)/shard_map/ppermute | solution.py:258
  111.7 7.8 %collective-permute-start.25 = (bf16[2,2,40,1792]{3,2,1,0:T(8,128)(2,1)S(1)}, bf16[2,2,40,1792]{3,2,1,0:T(8,128)(2,1)S(1)}, u32[]{:S(2)}, u32[]{:S(2)}) collective-permute-start(bf16[2,2,40,1792]{3,2,1,0:T(8,128)(2,1)S(1)} %get-tuple-element.131), channel_id=1, source_target_pairs={{0,8},{8,0},{16,24},{24,16},{1,9},{9,1},{17,25},{25,17},{2,10},{10... | collective-permute-start | bytes 1720328 | tf_op jit(solution)/shard_map/ppermute | solution.py:258
  111.9 15.3 %collective-permute-start.26 = (bf16[2,2,40,1792]{3,2,1,0:T(8,128)(2,1)S(1)}, bf16[2,2,40,1792]{3,2,1,0:T(8,128)(2,1)S(1)}, u32[]{:S(2)}, u32[]{:S(2)}) collective-permute-start(bf16[2,2,40,1792]{3,2,1,0:T(8,128)(2,1)S(1)} %get-tuple-element.135), channel_id=1, source_target_pairs={{0,16},{8,24},{16,0},{24,8},{1,17},{9,25},{17,1},{25,9},{2,18},{10... | collective-permute-start | bytes 1720328 | tf_op jit(solution)/shard_map/ppermute | solution.py:258
  118.8 15.3 %collective-permute-start.29 = (bf16[2,40,4096]{2,1,0:T(8,128)(2,1)S(1)}, bf16[2,40,4096]{2,1,0:T(8,128)(2,1)S(1)}, u32[]{:S(2)}, u32[]{:S(2)}) collective-permute-start(bf16[2,40,4096]{2,1,0:T(8,128)(2,1)S(1)} %get-tuple-element.141), channel_id=1, source_target_pairs={{0,1},{1,0},{2,3},{3,2},{4,5},{5,4},{6,7},{7,6},{8,9},{9,8},{10,11... | collective-permute-start | bytes 1966088 | tf_op jit(solution)/shard_map/ppermute | solution.py:258
  119.4 16.2 %collective-permute-start.31 = (bf16[2,40,4096]{2,1,0:T(8,128)(2,1)S(1)}, bf16[2,40,4096]{2,1,0:T(8,128)(2,1)S(1)}, u32[]{:S(2)}, u32[]{:S(2)}) collective-permute-start(bf16[2,40,4096]{2,1,0:T(8,128)(2,1)S(1)} %get-tuple-element.146), channel_id=1, source_target_pairs={{0,2},{1,3},{2,0},{3,1},{4,6},{5,7},{6,4},{7,5},{8,10},{9,11},{10,... | collective-permute-start | bytes 1966088 | tf_op jit(solution)/shard_map/ppermute | solution.py:283
  127.4 1.6 collective-permute-start.30
  134.1 15.7 %collective-permute-start.34 = (bf16[2,40,4096]{2,1,0:T(8,128)(2,1)S(1)}, bf16[2,40,4096]{2,1,0:T(8,128)(2,1)S(1)}, u32[]{:S(2)}, u32[]{:S(2)}) collective-permute-start(bf16[2,40,4096]{2,1,0:T(8,128)(2,1)S(1)} %get-tuple-element.153), channel_id=1, source_target_pairs={{0,1},{1,0},{2,3},{3,2},{4,5},{5,4},{6,7},{7,6},{8,9},{9,8},{10,11... | collective-permute-start | bytes 1966088 | tf_op jit(solution)/shard_map/ppermute | solution.py:258
  135.7 15.3 %collective-permute-start.35 = (bf16[2,40,4096]{2,1,0:T(8,128)(2,1)S(1)}, bf16[2,40,4096]{2,1,0:T(8,128)(2,1)S(1)}, u32[]{:S(2)}, u32[]{:S(2)}) collective-permute-start(bf16[2,40,4096]{2,1,0:T(8,128)(2,1)S(1)} %get-tuple-element.154.refs_0_), channel_id=1, source_target_pairs={{0,2},{1,3},{6,4},{7,5},{8,10},{9,11},{14,12},{15,13},{16,18},{17,... | collective-permute-start | bytes 1966088 | tf_op jit(solution)/shard_map/ppermute | solution.py:283
  137.9 1.6 collective-permute-start.28
  138.0 2.0 %collective-permute-start.27 = (bf16[2,1,40,1792]{3,2,1,0:T(8,128)(2,1)S(1)}, bf16[2,1,40,1792]{3,2,1,0:T(8,128)(2,1)S(1)}, u32[]{:S(2)}, u32[]{:S(2)}) collective-permute-start(bf16[2,1,40,1792]{3,2,1,0:T(8,128)(2,1)S(1)} %get-tuple-element.136), channel_id=1, source_target_pairs={{0,8},{8,0},{16,24},{24,16},{1,9},{9,1},{17,25},{25,17},{2,10},{10... | collective-permute-start | bytes 860168 | tf_op jit(solution)/shard_map/ppermute | solution.py:258
  140.1 15.8 %collective-permute-start.32 = (bf16[2,2,40,1792]{3,2,1,0:T(8,128)(2,1)S(1)}, bf16[2,2,40,1792]{3,2,1,0:T(8,128)(2,1)S(1)}, u32[]{:S(2)}, u32[]{:S(2)}) collective-permute-start(bf16[2,2,40,1792]{3,2,1,0:T(8,128)(2,1)S(1)} %get-tuple-element.149), channel_id=1, source_target_pairs={{0,8},{8,0},{16,24},{24,16},{1,9},{9,1},{17,25},{25,17},{2,10},{10... | collective-permute-start | bytes 1720328 | tf_op jit(solution)/shard_map/ppermute | solution.py:258
  140.3 15.6 %collective-permute-start.33 = (bf16[2,2,40,1792]{3,2,1,0:T(8,128)(2,1)S(1)}, bf16[2,2,40,1792]{3,2,1,0:T(8,128)(2,1)S(1)}, u32[]{:S(2)}, u32[]{:S(2)}) collective-permute-start(bf16[2,2,40,1792]{3,2,1,0:T(8,128)(2,1)S(1)} %get-tuple-element.150), channel_id=1, source_target_pairs={{0,16},{8,24},{16,0},{24,8},{1,17},{9,25},{17,1},{25,9},{2,18},{10... | collective-permute-start | bytes 1720328 | tf_op jit(solution)/shard_map/ppermute | solution.py:258
  151.4 16.7 %collective-permute-start.39 = (bf16[2,40,4096]{2,1,0:T(8,128)(2,1)S(1)}, bf16[2,40,4096]{2,1,0:T(8,128)(2,1)S(1)}, u32[]{:S(2)}, u32[]{:S(2)}) collective-permute-start(bf16[2,40,4096]{2,1,0:T(8,128)(2,1)S(1)} %get-tuple-element.162), channel_id=1, source_target_pairs={{0,2},{1,3},{6,4},{7,5},{8,10},{9,11},{14,12},{15,13},{16,18},{17,... | collective-permute-start | bytes 1966088 | tf_op jit(solution)/shard_map/ppermute | solution.py:283
  156.2 1.6 collective-permute-start.36
  156.3 13.8 %collective-permute-start.38 = (bf16[2,40,4096]{2,1,0:T(8,128)(2,1)S(1)}, bf16[2,40,4096]{2,1,0:T(8,128)(2,1)S(1)}, u32[]{:S(2)}, u32[]{:S(2)}) collective-permute-start(bf16[2,40,4096]{2,1,0:T(8,128)(2,1)S(1)} %get-tuple-element.161), channel_id=1, source_target_pairs={{2,4},{3,5},{4,2},{5,3},{10,12},{11,13},{12,10},{13,11},{18,20},{1... | collective-permute-start | bytes 1966088 | tf_op jit(solution)/shard_map/ppermute | solution.py:283
  161.7 16.8 %collective-permute-start.37 = (bf16[2,40,4096]{2,1,0:T(8,128)(2,1)S(1)}, bf16[2,40,4096]{2,1,0:T(8,128)(2,1)S(1)}, u32[]{:S(2)}, u32[]{:S(2)}) collective-permute-start(bf16[2,40,4096]{2,1,0:T(8,128)(2,1)S(1)} %get-tuple-element.160), channel_id=1, source_target_pairs={{0,1},{1,0},{2,3},{3,2},{4,5},{5,4},{6,7},{7,6},{8,9},{9,8},{10,11... | collective-permute-start | bytes 1966088 | tf_op jit(solution)/shard_map/ppermute | solution.py:258
  168.7 19.4 %collective-permute-start.40 = (bf16[2,40,4096]{2,1,0:T(8,128)(2,1)S(1)}, bf16[2,40,4096]{2,1,0:T(8,128)(2,1)S(1)}, u32[]{:S(2)}, u32[]{:S(2)}) collective-permute-start(bf16[2,40,4096]{2,1,0:T(8,128)(2,1)S(1)} %get-tuple-element.164), channel_id=1, source_target_pairs={{2,6},{3,7},{4,0},{5,1},{10,14},{11,15},{12,8},{13,9},{18,22},{19,... | collective-permute-start | bytes 1966088 | tf_op jit(solution)/shard_map/ppermute | solution.py:283
  188.6 1.7 collective-permute-start.41
  (5 other events, 25.6 us)

commit v5 on v4

--- a/solution.py
+++ b/solution.py
@@ -10,11 +10,6 @@
 BLOCK = 64
 CORES = 2
 PLANES = 4
-NEXT = ((0, 1), (1, 0), (2, 3), (3, 2))
-ACROSS = ((1, 2), (2, 1))
-BEYOND = ((1, 3), (2, 0))
-OUTWARD = ((1, 0), (2, 3))
-INWARD = ((0, 1), (3, 2))
 VMEM = 12 * 1024 * 1024
 F32 = jnp.float32
 BF16 = jnp.bfloat16
@@ -122,7 +117,7 @@
 
 def gate_up_kernel(part_count, after_count, *refs):
     parts, (gate_ref, up_ref) = refs[:part_count], refs[part_count : part_count + 2]
-    keep_ref, near_ref, *far_refs, token_ref, all_rows = refs[part_count + 2 + after_count :]
+    keep_ref, near_ref, far_ref, token_ref, all_rows = refs[part_count + 2 + after_count :]
     token_ref[...] = jnp.zeros_like(token_ref)
     half = parts[0].shape[0] // 2
     kept = half * len(parts)
@@ -139,14 +134,14 @@
             total = total.reshape(2, *keep_ref.shape[1:4], tile).astype(BF16)
             keep_ref[which, :, :, :, columns] = total[0]
             near_ref[which, :, :, columns] = total[1, :, 0]
-            far_refs[which][:, :, :, columns] = total[1, :, 1:]
+            far_ref[which, :, :, :, columns] = total[1, :, 1:]
 
 
 def gate_up(parts, gate_kept, up_kept, chips, after):
     rows = sum(part.shape[0] for part in parts)
     depth, width = gate_kept.shape
     groups, own = len(parts), rows // (2 * len(parts) * chips)
-    shapes = [(2, groups, chips, own, width), (2, groups, own, width)] + [(groups, chips - 1, own, width)] * 2
+    shapes = [(2, groups, chips, own, width), (2, groups, own, width), (2, groups, chips - 1, own, width)]
     return pl.pallas_call(
         functools.partial(gate_up_kernel, len(parts), len(after)),
         in_specs=[INSIDE] * (len(parts) + 2) + [ANYWHERE] * len(after),
@@ -201,12 +196,12 @@
     del refs[:after_count]
 
     if to_chips:
-        keep_ref, *came_refs = ins[0]
+        keep_ref, came_ref = ins[0]
         for chip in range(1, keep_ref.shape[2]):
             sent_ref = refs.pop(0)
             for which in range(2):
                 for group in range(keep_ref.shape[1]):
-                    came = came_refs[which][group, chip - 1].astype(F32)
+                    came = came_ref[which, group, chip - 1].astype(F32)
                     sent_ref[which, group] = (keep_ref[which, group, chip].astype(F32) + came).astype(BF16)
     if to_hidden:
         keep_ref, came_ref, *chip_refs = ins[1]
@@ -273,14 +268,13 @@
         block = lax.dynamic_slice_in_dim(normed, (row ^ step) * features, features, 1)
         blocks.append(swap(block, "rows", row_count, step) if step else block)
     gate_kept, token = masked(gate_weight, gate_mask, tile_of(features, 256), nowhere, 1, [normed])
-    mine, token = assemble(blocks, [token])
+    mine, token = assemble(blocks, [token, resident(gate_kept)])
 
     def behind(values, after):
         return lax.optimization_barrier((values, *after))[0] if after else values
 
-    def by_plane(values, planes, after=()):
-        pairs = [(a * per_plane + b, c * per_plane + b) for a, c in planes for b in range(per_plane)]
-        return lax.ppermute(behind(values, after), "cols", pairs)
+    def by_plane(values, plane, after=()):
+        return swap(behind(values, after), "cols", col_count, plane * per_plane)
 
     def by_row_of_plane(values, step, after=()):
         return swap(behind(values, after), "cols", col_count, step)
@@ -291,8 +285,7 @@
     def by_core(values, after=()):
         return swap(behind(values, after), "rows", row_count, 1)
 
-    inner = (lax.axis_index("cols") // per_plane) % 3 != 0
-    parts, halves, near, came, chip_sums, hiddens, others, rows_in, partials = ({} for _ in range(9))
+    parts, halves, near, far, chip_sums, hiddens, others, rows_in, partials, sent = ({} for _ in range(10))
     last = [token]
 
     def forward(plane, values, after=()):
@@ -300,70 +293,81 @@
         for step in range(1, per_plane):
             parts[plane].append(by_row_of_plane(values, step, after))
 
-    def multiply_in(plane, after=(), send_after=()):
+    def multiply_in(plane, after=()):
         *halves[plane], last[0] = gate_up(parts[plane], gate_kept, up_kept, chips, last + list(after))
-        came[plane] = [by_core(part, send_after) for part in halves[plane][2:]]
-
-    def multiply_out(plane, after=(), send_after=()):
-        *partials[plane], last[0] = down(hiddens[plane], others[plane], down_kept, last + list(after))
+
+    def exchange(plane, after=()):
+        far[plane] = by_core(halves[plane][2], after)
+        near[plane] = by_core(halves[plane][1], after)
+
+    def multiply_out(plane):
+        *partials[plane], last[0] = down(hiddens[plane], others[plane], down_kept, last)
+
+    def send_rows(plane, after=()):
         rows_in[plane] = [partials[plane][0]]
         for step in range(1, per_plane):
-            rows_in[plane].append(by_row_of_plane(partials[plane][step], step, send_after))
-
-    def to_chips(plane, send_after=()):
-        sent, _, _, last[0] = sums([halves[plane][0], *came[plane]], [], [], last)
-        chip_sums[plane] = [by_chip(part, number + 1, send_after) for number, part in enumerate(sent)]
-        near[plane] = by_core(halves[plane][1], last)
+            rows_in[plane].append(by_row_of_plane(partials[plane][step], step, after))
+
+    def to_chips(plane):
+        sent[plane], _, _, last[0] = sums([halves[plane][0], far[plane]], [], [], last + [near[plane]])
+
+    def send_chips(plane, after=()):
+        chip_sums[plane] = [by_chip(part, number + 1, after) for number, part in enumerate(sent[plane])]
 
     def to_hidden(plane):
         _, hiddens[plane], _, last[0] = sums([], [halves[plane][0], near[plane], *chip_sums[plane]], [], last)
         others[plane] = by_core(hiddens[plane])
 
-    def to_rows(*lists, after=()):
-        _, _, summed, last[0] = sums([], [], lists, last + list(after))
+    def to_rows(*parts, after=()):
+        _, _, (summed,), last[0] = sums([], [], [parts], last + list(after))
         return summed
 
-    next_mine = by_plane(mine, NEXT)
-    across_mine = by_plane(mine, ACROSS)
+    one_away = by_plane(mine, 1)
+    two_away = by_plane(mine, 2)
     forward(0, mine)
-    up_kept, last[0] = masked(up_weight, up_mask, tile_of(features, 256), nowhere, 1, last)
-    across_next = by_plane(next_mine, ACROSS, last)
-    outward_mine = by_plane(across_mine, OUTWARD, last)
-    forward(1, next_mine, [*parts[0][1:], *last])
+    up_kept, last[0] = masked(up_weight, up_mask, tile_of(features, 256), nowhere, 1, last + [resident(gate_kept)])
     down_kept, last[0] = masked(
-        down_weight, down_mask, 2 * BLOCK, place, CORES, last + [next_mine, across_mine, *parts[0][1:]]
+        down_weight, down_mask, 2 * BLOCK, place, CORES, last + [resident(gate_kept), resident(up_kept)]
     )
-    two_away = jnp.where(inner, across_next, outward_mine)
-    outward_next = by_plane(across_next, OUTWARD, last)
-    forward(2, two_away, parts[1][1:])
-    multiply_in(1, [across_next, outward_mine])
+    forward(1, one_away, [*parts[0][1:], *last])
+    multiply_in(0, [one_away])
+    exchange(0)
+    to_chips(0)
+    three_away = by_plane(two_away, 1, last)
+    forward(2, two_away, [*parts[1][1:], *last])
+    multiply_in(1, [two_away])
+    exchange(1)
     to_chips(1)
-    three_away = jnp.where(inner, across_mine, outward_next)
-    forward(3, three_away, [*parts[2][1:], *last])
-    multiply_in(2, [near[1]])
+    send_chips(1)
+    forward(3, three_away, parts[2][1:])
+    multiply_in(2, [three_away])
+    exchange(2)
     to_hidden(1)
     to_chips(2)
-    multiply_out(1, send_after=parts[3][1:])
-    multiply_in(3, [near[2]])
+    send_chips(2)
+    multiply_in(3)
+    exchange(3)
+    multiply_out(1)
     to_hidden(2)
     to_chips(3)
-    multiply_out(2, send_after=rows_in[1][1:])
-    (one,) = to_rows(rows_in[1])
-    next_one = by_plane(one, NEXT)
-    multiply_in(0, [near[3]], chip_sums[3])
+    send_chips(3)
+    multiply_out(2)
+    send_rows(2)
     to_hidden(3)
-    multiply_out(3, send_after=rows_in[2][1:])
-    (two,) = to_rows(rows_in[2], after=[next_one])
-    inward_two = by_plane(two, INWARD)
-    to_chips(0)
-    three, three_and_two = to_rows(rows_in[3], [*rows_in[3], inward_two])
-    inward_three = by_plane(three, INWARD)
-    across_three = by_plane(three_and_two, ACROSS)
+    send_chips(0, [last[0], *chip_sums[3]])
+    multiply_out(3)
+    send_rows(3, rows_in[2][1:])
+    two = to_rows(*rows_in[2])
+    two_out = by_plane(two, 1)
     to_hidden(0)
-    multiply_out(0, send_after=rows_in[3][1:])
-    (two_and_three,) = to_rows([two, inward_three])
-    beyond_two = by_plane(two_and_three, BEYOND)
-    arrived = [*rows_in[0], next_one, across_three, beyond_two]
+    multiply_out(0)
+    send_rows(1, [*rows_in[3][1:], *last])
+    three = to_rows(*rows_in[3], two_out)
+    three_out = by_plane(three, 3)
+    send_rows(0, rows_in[1][1:])
+    one = to_rows(*rows_in[1])
+    one_out = by_plane(one, 1)
+    arrived = [*rows_in[0], one_out, three_out]
 
     total = arrived[0].astype(F32)
     for part in arrived[1:]:

time: 192 us -> 189 us (0.984)
  waiting for transfers between devices: 76.4 us -> 88 us
  starting transfers between devices: 36.8 us -> 26.8 us
  Pallas kernels: 67.2 us -> 64.9 us
    ppermute x32 -> x34, waiting for transfers between devices: 52.4 us -> 88 us  [swap(): lax.ppermute(values, axis, [(place, place ^ step) for place in range(size)])]
    ppermute x10 -> x0, waiting for transfers between devices: 24 us -> none  [by_plane(): return lax.ppermute(behind(values, after), 'cols', pairs)]
    ppermute x10 -> x0, starting transfers between devices: 17.5 us -> none  [by_plane(): return lax.ppermute(behind(values, after), 'cols', pairs)]
    ppermute x32 -> x34, starting transfers between devices: 19.3 us -> 26.8 us  [swap(): lax.ppermute(values, axis, [(place, place ^ step) for place in range(size)])]
    unnamed x22 -> x12, local copies, waits for them, and re-layouts: 5.94 us -> 4.86 us
  transfers between devices with their start and end apart: 42 -> 34, of which waited for: 23 -> 22; matrix products, arithmetic and copies ran while one was open for 0% -> 0% of each run, Pallas kernels for 31% -> 34%
where the time goes in v5:
time: 189 us
  waiting for transfers between devices  88 us (47%)
  Pallas kernels  64.9 us (34%)
  starting transfers between devices  26.8 us (14%)
  local copies, waits for them, and re-layouts  4.94 us (3%)
  other arithmetic  3.89 us (2%)
    ppermute x34, waiting for transfers between devices, swap(): lax.ppermute(values, axis, [(place, place ^ step) for place in range(size)])  88 us
    ppermute x34, starting transfers between devices, swap(): lax.ppermute(values, axis, [(place, place ^ step) for place in range(size)])  26.8 us
    pallas_call x4, Pallas kernels, gate_up(): pl.pallas_call(functools.partial(gate_up_kernel, len(parts), len(after)),...  24.3 us
    pallas_call x3, Pallas kernels, masked(): pl.pallas_call(functools.partial(mask_kernel, len(after)), grid_spec=pltp...  22.3 us
    pallas_call x4, Pallas kernels, down(): pl.pallas_call(functools.partial(down_kernel, len(after)), in_specs=[INSI...  15.5 us
    unnamed x12, local copies, waits for them, and re-layouts  4.86 us
  transfers between devices with their start and end apart: 34, of which 22 were waited for; matrix products, arithmetic and copies ran while one was open for 0% of the time, Pallas kernels for 34%

profile of v5, /device:TPU:0, one launch (start us, length us, event | category | flops | bytes accessed | tf_op | source)
XLA Modules:
  0.0 188.9 jit_solution(4201082174022841699)
XLA Ops:
  0.0 1.3 fusion
  1.4 1.3 fusion.2.refs_0_
  2.7 3.0 %collective-permute-start = (bf16[40,2048]{1,0:T(8,128)(2,1)S(1)}, bf16[40,2048]{1,0:T(8,128)(2,1)S(1)}, u32[]{:S(2)}, u32[]{:S(2)}) collective-permute-start(bf16[40,2048]{1,0:T(8,128)(2,1)S(1)} %get-tuple-element.139), channel_id=1, source_target_pairs={{0,16},{8,24},{16,0},{24,8},{1,17},{9,25},{17,1},{25,9},{2,18},{10... | collective-permute-start | bytes 491528 | tf_op jit(solution)/shard_map/ppermute | solution.py:253
  6.0 5.6 %masked.3 = (bf16[2048,1792]{1,0:T(8,128)(2,1)S(1)}, f32[8,128]{1,0:T(8,128)S(1)}) custom-call(s32[1]{0:T(128)} %constant.34.clone.1.core_ref, bf16[2048,1792]{1,0:T(8,128)(2,1)} %weight_ref.3, s32[32,28]{1,0:T(8,128)S(1)} %copy-done.3, bf16[40,8192]{1,0:T(8,128)(2,1)S(1)} %fusion.2.refs_0_), custom_call_target="tpu_custom_call" | custom-call | bytes 14680 | tf_op jit(solution)/shard_map/masked/pallas_call | solution.py:71
  11.6 1.1 collective-permute-done.2.refs_3_
  12.8 1.8 copy-done
  14.5 2.0 %collective-permute-start.3 = (bf16[160,2048]{1,0:T(8,128)(2,1)S(1)}, bf16[160,2048]{1,0:T(8,128)(2,1)S(1)}, u32[]{:S(2)}, u32[]{:S(2)}) collective-permute-start(bf16[160,2048]{1,0:T(8,128)(2,1)S(1)} %get-tuple-element.72.refs_0_), channel_id=1, source_target_pairs={{0,1},{1,0},{2,3},{3,2},{4,5},{5,4},{6,7},{7,6},{8,9},{9,8},{10,11... | collective-permute-start | bytes 1966088 | tf_op jit(solution)/shard_map/ppermute | solution.py:253
  16.5 1.6 collective-permute-start.4
  18.1 2.6 %collective-permute-start.7 = (bf16[160,2048]{1,0:T(8,128)(2,1)S(1)}, bf16[160,2048]{1,0:T(8,128)(2,1)S(1)}, u32[]{:S(2)}, u32[]{:S(2)}) collective-permute-start(bf16[160,2048]{1,0:T(8,128)(2,1)S(1)} %get-tuple-element.72.refs_0_), channel_id=1, source_target_pairs={{0,4},{1,5},{2,6},{3,7},{4,0},{5,1},{6,2},{7,3},{8,12},{9,13},{10,... | collective-permute-start | bytes 1966088 | tf_op jit(solution)/shard_map/ppermute | solution.py:253
  20.7 3.1 %copy-done.1 = bf16[2048,1792]{1,0:T(8,128)(2,1)S(1)} copy-done((bf16[2048,1792]{1,0:T(8,128)(2,1)S(1)}, bf16[2048,1792]{1,0:T(8,128)(2,1)}, u32[]{:S(2)}) %copy-start.1) | copy-done | bytes 7340056
  23.7 6.4 %masked.4 = (bf16[2048,1792]{1,0:T(8,128)(2,1)S(1)}, f32[8,128]{1,0:T(8,128)S(1)}) custom-call(s32[1]{0:T(128)} %constant.34.clone.1.core_ref, bf16[2048,1792]{1,0:T(8,128)(2,1)} %weight_ref.4, s32[32,28]{1,0:T(8,128)S(1)} %copy-done.5, f32[8,128]{1,0:T(8,128)S(1)} %get-tuple-element.73.refs_0_, bf16[2048,1792]{1,0:T(8,128)(2,1)S(1)} %copy-done.1), custom_call_target="tpu_custom_call" | custom-call | bytes 14680 | tf_op jit(solution)/shard_map/masked/pallas_call | solution.py:71
  30.2 10.2 %masked.5 = (bf16[1792,4096]{1,0:T(8,128)(2,1)S(1)}, f32[8,128]{1,0:T(8,128)S(1)}) custom-call(s32[1]{0:T(128)} %bitcast.core_ref, bf16[1792,8192]{1,0:T(8,128)(2,1)} %weight_ref.5, s32[28,128]{1,0:T(8,128)S(1)} %copy-done.4, f32[8,128]{1,0:T(8,128)S(1)} %get-tuple-element.75.refs_0_, bf16[2048,1792]{1,0:T(8,128)(2,1)S(1)} %copy-done.2, ...), custom_call_target="tpu_custom_call" | custom-call | bytes 29360 | tf_op jit(solution)/shard_map/masked/pallas_call | solution.py:71
  40.4 6.3 %collective-permute-done.4.refs_5_.refs_0_ = bf16[160,2048]{1,0:T(8,128)(2,1)S(1)} collective-permute-done((bf16[160,2048]{1,0:T(8,128)(2,1)S(1)}, bf16[160,2048]{1,0:T(8,128)(2,1)S(1)}, u32[]{:S(2)}, u32[]{:S(2)}) %collective-permute-start.4) | collective-permute-done | bytes 655392 | tf_op jit(solution)/shard_map/ppermute | solution.py:253
  47.1 6.1 %gate_up.4 = (bf16[2,2,2,40,1792]{4,3,2,1,0:T(8,128)(2,1)S(1)}, bf16[2,2,40,1792]{3,2,1,0:T(8,128)(2,1)S(1)}, bf16[2,2,1,40,1792]{4,3,2,1,0:T(8,128)(2,1)S(1)}, f32[8,128]{1,0:T(8,128)S(1)}) custom-call(bf16[160,2048]{1,0:T(8,128)(2,1)S(1)} %get-tuple-element.72.refs_0_, bf16[160,2048]{1,0:T(8,128)(2,1)S(1)} %collective-permute-done.3.refs_1_, ...), custom_call_target="tpu_custom_call" | custom-call | flops 4697620 | tf_op jit(solution)/shard_map/gate_up/pallas_call | solution.py:145
  53.8 1.5 collective-permute-done.5.refs_3_.refs_1_
  55.3 0.8 collective-permute-done.6.refs_1_
  56.3 5.9 %collective-permute-done.9.refs_1_ = bf16[160,2048]{1,0:T(8,128)(2,1)S(1)} collective-permute-done((bf16[160,2048]{1,0:T(8,128)(2,1)S(1)}, bf16[160,2048]{1,0:T(8,128)(2,1)S(1)}, u32[]{:S(2)}, u32[]{:S(2)}) %collective-permute-start.9) | collective-permute-done | bytes 655392 | tf_op jit(solution)/shard_map/ppermute | solution.py:253
  63.0 6.1 %gate_up.5 = (bf16[2,2,2,40,1792]{4,3,2,1,0:T(8,128)(2,1)S(1)}, bf16[2,2,40,1792]{3,2,1,0:T(8,128)(2,1)S(1)}, bf16[2,2,1,40,1792]{4,3,2,1,0:T(8,128)(2,1)S(1)}, f32[8,128]{1,0:T(8,128)S(1)}) custom-call(bf16[160,2048]{1,0:T(8,128)(2,1)S(1)} %collective-permute-done.4.refs_5_.refs_0_, bf16[160,2048]{1,0:T(8,128)(2,1)S(1)} %collective-permute-done.9.refs_1_, ...), custom_call_target="tpu_custom_call" | custom-call | flops 4697620 | tf_op jit(solution)/shard_map/gate_up/pallas_call | solution.py:145
  69.6 1.5 collective-permute-done.12.refs_1_
  71.1 0.8 collective-permute-done.13.refs_3_.refs_1_
  72.0 1.4 collective-permute-start.15
  73.4 3.7 %collective-permute-done.10.refs_1_ = bf16[160,2048]{1,0:T(8,128)(2,1)S(1)} collective-permute-done((bf16[160,2048]{1,0:T(8,128)(2,1)S(1)}, bf16[160,2048]{1,0:T(8,128)(2,1)S(1)}, u32[]{:S(2)}, u32[]{:S(2)}) %collective-permute-start.10) | collective-permute-done | bytes 655392 | tf_op jit(solution)/shard_map/ppermute | solution.py:253
  77.9 6.1 %gate_up.6 = (bf16[2,2,2,40,1792]{4,3,2,1,0:T(8,128)(2,1)S(1)}, bf16[2,2,40,1792]{3,2,1,0:T(8,128)(2,1)S(1)}, bf16[2,2,1,40,1792]{4,3,2,1,0:T(8,128)(2,1)S(1)}, f32[8,128]{1,0:T(8,128)S(1)}) custom-call(bf16[160,2048]{1,0:T(8,128)(2,1)S(1)} %collective-permute-done.7.refs_5_.refs_0_, bf16[160,2048]{1,0:T(8,128)(2,1)S(1)} %collective-permute-done.10.refs_1_, ...), custom_call_target="tpu_custom_call" | custom-call | flops 4697620 | tf_op jit(solution)/shard_map/gate_up/pallas_call | solution.py:145
  84.5 2.6 %collective-permute-done.15.refs_2_ = bf16[2,2,40,1792]{3,2,1,0:T(8,128)(2,1)S(1)} collective-permute-done((bf16[2,2,40,1792]{3,2,1,0:T(8,128)(2,1)S(1)}, bf16[2,2,40,1792]{3,2,1,0:T(8,128)(2,1)S(1)}, u32[]{:S(2)}, u32[]{:S(2)}) %collective-permute-start.15) | collective-permute-done | bytes 573472 | tf_op jit(solution)/shard_map/ppermute | solution.py:253
  87.6 1.4 collective-permute-start.19
  88.9 1.9 %collective-permute-done.11.refs_1_ = bf16[160,2048]{1,0:T(8,128)(2,1)S(1)} collective-permute-done((bf16[160,2048]{1,0:T(8,128)(2,1)S(1)}, bf16[160,2048]{1,0:T(8,128)(2,1)S(1)}, u32[]{:S(2)}, u32[]{:S(2)}) %collective-permute-start.11) | collective-permute-done | bytes 655392 | tf_op jit(solution)/shard_map/ppermute | solution.py:253
  90.8 6.1 %gate_up.7 = (bf16[2,2,2,40,1792]{4,3,2,1,0:T(8,128)(2,1)S(1)}, bf16[2,2,40,1792]{3,2,1,0:T(8,128)(2,1)S(1)}, bf16[2,2,1,40,1792]{4,3,2,1,0:T(8,128)(2,1)S(1)}, f32[8,128]{1,0:T(8,128)S(1)}) custom-call(bf16[160,2048]{1,0:T(8,128)(2,1)S(1)} %collective-permute-done.8.refs_5_.refs_0_, bf16[160,2048]{1,0:T(8,128)(2,1)S(1)} %collective-permute-done.11.refs_1_, ...), custom_call_target="tpu_custom_call" | custom-call | flops 4697620 | tf_op jit(solution)/shard_map/gate_up/pallas_call | solution.py:145
  97.6 2.6 %collective-permute-done.20.other_ref = bf16[2,40,1792]{2,1,0:T(8,128)(2,1)S(1)} collective-permute-done((bf16[2,40,1792]{2,1,0:T(8,128)(2,1)S(1)}, bf16[2,40,1792]{2,1,0:T(8,128)(2,1)S(1)}, u32[]{:S(2)}, u32[]{:S(2)}) %collective-permute-start.20) | collective-permute-done | bytes 286752 | tf_op jit(solution)/shard_map/ppermute | solution.py:253
  100.2 3.9 %down.4 = (bf16[2,40,4096]{2,1,0:T(8,128)(2,1)S(1)}, bf16[2,40,4096]{2,1,0:T(8,128)(2,1)S(1)}, f32[8,128]{1,0:T(8,128)S(1)}) custom-call(bf16[2,40,1792]{2,1,0:T(8,128)(2,1)S(1)} %get-tuple-element.103.own_ref, bf16[2,40,1792]{2,1,0:T(8,128)(2,1)S(1)} %collective-permute-done.20.other_ref, bf16[1792,4096]{1,0:T(8,128)(2,1)S(1)} %get-tuple-element.104.weight_ref, ...), custom_call_target="tpu_custom_call" | custom-call | flops 2348810 | tf_op jit(solution)/shard_map/down/pallas_call | solution.py:179
  104.7 1.6 collective-permute-start.21
  106.3 3.9 %down.5 = (bf16[2,40,4096]{2,1,0:T(8,128)(2,1)S(1)}, bf16[2,40,4096]{2,1,0:T(8,128)(2,1)S(1)}, f32[8,128]{1,0:T(8,128)S(1)}) custom-call(bf16[2,40,1792]{2,1,0:T(8,128)(2,1)S(1)} %get-tuple-element.109.own_ref, bf16[2,40,1792]{2,1,0:T(8,128)(2,1)S(1)} %collective-permute-done.22.other_ref, bf16[1792,4096]{1,0:T(8,128)(2,1)S(1)} %get-tuple-element.104.weight_ref, ...), custom_call_target="tpu_custom_call" | custom-call | flops 2348810 | tf_op jit(solution)/shard_map/down/pallas_call | solution.py:179
  111.0 9.1 %collective-permute-done.21.refs_2_ = bf16[2,2,40,1792]{3,2,1,0:T(8,128)(2,1)S(1)} collective-permute-done((bf16[2,2,40,1792]{3,2,1,0:T(8,128)(2,1)S(1)}, bf16[2,2,40,1792]{3,2,1,0:T(8,128)(2,1)S(1)}, u32[]{:S(2)}, u32[]{:S(2)}) %collective-permute-start.21) | collective-permute-done | bytes 573472 | tf_op jit(solution)/shard_map/ppermute | solution.py:253
  120.4 1.6 collective-permute-start.23
  122.0 3.9 %down.6 = (bf16[2,40,4096]{2,1,0:T(8,128)(2,1)S(1)}, bf16[2,40,4096]{2,1,0:T(8,128)(2,1)S(1)}, f32[8,128]{1,0:T(8,128)S(1)}) custom-call(bf16[2,40,1792]{2,1,0:T(8,128)(2,1)S(1)} %get-tuple-element.116.own_ref, bf16[2,40,1792]{2,1,0:T(8,128)(2,1)S(1)} %collective-permute-done.25.other_ref, bf16[1792,4096]{1,0:T(8,128)(2,1)S(1)} %get-tuple-element.104.weight_ref, ...), custom_call_target="tpu_custom_call" | custom-call | flops 2348810 | tf_op jit(solution)/shard_map/down/pallas_call | solution.py:179
  125.9 1.1 collective-permute-done.24.refs_1_
  127.9 7.9 %collective-permute-done.23.refs_2_ = bf16[2,2,40,1792]{3,2,1,0:T(8,128)(2,1)S(1)} collective-permute-done((bf16[2,2,40,1792]{3,2,1,0:T(8,128)(2,1)S(1)}, bf16[2,2,40,1792]{3,2,1,0:T(8,128)(2,1)S(1)}, u32[]{:S(2)}, u32[]{:S(2)}) %collective-permute-start.23) | collective-permute-done | bytes 573472 | tf_op jit(solution)/shard_map/ppermute | solution.py:253
  136.3 1.5 collective-permute-done.26.other_ref
  137.8 3.9 %down.7 = (bf16[2,40,4096]{2,1,0:T(8,128)(2,1)S(1)}, bf16[2,40,4096]{2,1,0:T(8,128)(2,1)S(1)}, f32[8,128]{1,0:T(8,128)S(1)}) custom-call(bf16[2,40,1792]{2,1,0:T(8,128)(2,1)S(1)} %get-tuple-element.119.own_ref, bf16[2,40,1792]{2,1,0:T(8,128)(2,1)S(1)} %collective-permute-done.26.other_ref, bf16[1792,4096]{1,0:T(8,128)(2,1)S(1)} %get-tuple-element.104.weight_ref, ...), custom_call_target="tpu_custom_call" | custom-call | flops 2348810 | tf_op jit(solution)/shard_map/down/pallas_call | solution.py:179
  141.6 1.2 collective-permute-done.27.refs_1_
  142.8 1.0 collective-permute-start.28
  143.8 9.6 %collective-permute-done.30.refs_2_ = bf16[2,40,4096]{2,1,0:T(8,128)(2,1)S(1)} collective-permute-done((bf16[2,40,4096]{2,1,0:T(8,128)(2,1)S(1)}, bf16[2,40,4096]{2,1,0:T(8,128)(2,1)S(1)}, u32[]{:S(2)}, u32[]{:S(2)}) %collective-permute-start.30) | collective-permute-done | bytes 655392 | tf_op jit(solution)/shard_map/ppermute | solution.py:253
  153.6 2.7 %collective-permute-start.32 = (bf16[2,40,4096]{2,1,0:T(8,128)(2,1)S(1)}, bf16[2,40,4096]{2,1,0:T(8,128)(2,1)S(1)}, u32[]{:S(2)}, u32[]{:S(2)}) collective-permute-start(bf16[2,40,4096]{2,1,0:T(8,128)(2,1)S(1)} %get-tuple-element.134), channel_id=1, source_target_pairs={{0,6},{1,7},{2,4},{3,5},{4,2},{5,3},{6,0},{7,1},{8,14},{9,15},{10,... | collective-permute-start | bytes 1966088 | tf_op jit(solution)/shard_map/ppermute | solution.py:253
  156.3 2.2 %collective-permute-done.28.refs_1_ = bf16[2,40,4096]{2,1,0:T(8,128)(2,1)S(1)} collective-permute-done((bf16[2,40,4096]{2,1,0:T(8,128)(2,1)S(1)}, bf16[2,40,4096]{2,1,0:T(8,128)(2,1)S(1)}, u32[]{:S(2)}, u32[]{:S(2)}) %collective-permute-start.28) | collective-permute-done | bytes 655392 | tf_op jit(solution)/shard_map/ppermute | solution.py:253
  158.5 1.1 collective-permute-start.29
  160.8 12.4 %collective-permute-done.32 = bf16[2,40,4096]{2,1,0:T(8,128)(2,1)S(1)} collective-permute-done((bf16[2,40,4096]{2,1,0:T(8,128)(2,1)S(1)}, bf16[2,40,4096]{2,1,0:T(8,128)(2,1)S(1)}, u32[]{:S(2)}, u32[]{:S(2)}) %collective-permute-start.32) | collective-permute-done | bytes 655392 | tf_op jit(solution)/shard_map/ppermute | solution.py:253
  173.2 12.7 %collective-permute-done.31 = bf16[2,40,4096]{2,1,0:T(8,128)(2,1)S(1)} collective-permute-done((bf16[2,40,4096]{2,1,0:T(8,128)(2,1)S(1)}, bf16[2,40,4096]{2,1,0:T(8,128)(2,1)S(1)}, u32[]{:S(2)}, u32[]{:S(2)}) %collective-permute-start.31) | collective-permute-done | bytes 655392 | tf_op jit(solution)/shard_map/ppermute | solution.py:253
  186.3 1.6 collective-permute-done.33
  188.0 0.9 pad_maximum_fusion
  (63 shorter events, 10.5 us)
Async XLA Ops:
  1.3 4.6 %copy-start.3 = (s32[32,28]{1,0:T(8,128)S(1)}, s32[32,28]{1,0:T(8,128)}, u32[]{:S(2)}) copy-start(s32[32,28]{1,0:T(8,128)} %mask_ref.3) | copy-start | bytes 10756
  2.7 8.9 %collective-permute-start = (bf16[40,2048]{1,0:T(8,128)(2,1)S(1)}, bf16[40,2048]{1,0:T(8,128)(2,1)S(1)}, u32[]{:S(2)}, u32[]{:S(2)}) collective-permute-start(bf16[40,2048]{1,0:T(8,128)(2,1)S(1)} %get-tuple-element.139), channel_id=1, source_target_pairs={{0,16},{8,24},{16,0},{24,8},{1,17},{9,25},{17,1},{25,9},{2,18},{10... | collective-permute-start | bytes 491528 | tf_op jit(solution)/shard_map/ppermute | solution.py:253
  5.7 5.9 %collective-permute-start.1 = (bf16[40,2048]{1,0:T(8,128)(2,1)S(1)}, bf16[40,2048]{1,0:T(8,128)(2,1)S(1)}, u32[]{:S(2)}, u32[]{:S(2)}) collective-permute-start(bf16[40,2048]{1,0:T(8,128)(2,1)S(1)} %get-tuple-element.138), channel_id=1, source_target_pairs={{0,8},{8,0},{16,24},{24,16},{1,9},{9,1},{17,25},{25,17},{2,10},{10... | collective-permute-start | bytes 491528 | tf_op jit(solution)/shard_map/ppermute | solution.py:253
  5.7 7.0 %collective-permute-start.2 = (bf16[40,2048]{1,0:T(8,128)(2,1)S(1)}, bf16[40,2048]{1,0:T(8,128)(2,1)S(1)}, u32[]{:S(2)}, u32[]{:S(2)}) collective-permute-start(bf16[40,2048]{1,0:T(8,128)(2,1)S(1)} %get-tuple-element.137), channel_id=1, source_target_pairs={{0,24},{8,16},{16,8},{24,0},{1,25},{9,17},{17,9},{25,1},{2,26},{10... | collective-permute-start | bytes 491528 | tf_op jit(solution)/shard_map/ppermute | solution.py:253
  11.6 2.9 %copy-start = (bf16[2048,1792]{1,0:T(8,128)(2,1)}, bf16[2048,1792]{1,0:T(8,128)(2,1)S(1)}, u32[]{:S(2)}) copy-start(bf16[2048,1792]{1,0:T(8,128)(2,1)S(1)} %get-tuple-element.71.refs_5_.refs_1_.refs_2_) | copy-start | bytes 22020100
  12.7 7.9 %copy-start.5 = (s32[32,28]{1,0:T(8,128)S(1)}, s32[32,28]{1,0:T(8,128)}, u32[]{:S(2)}) copy-start(s32[32,28]{1,0:T(8,128)} %mask_ref.4) | copy-start | bytes 10756
  14.5 25.9 %collective-permute-start.3 = (bf16[160,2048]{1,0:T(8,128)(2,1)S(1)}, bf16[160,2048]{1,0:T(8,128)(2,1)S(1)}, u32[]{:S(2)}, u32[]{:S(2)}) collective-permute-start(bf16[160,2048]{1,0:T(8,128)(2,1)S(1)} %get-tuple-element.72.refs_0_), channel_id=1, source_target_pairs={{0,1},{1,0},{2,3},{3,2},{4,5},{5,4},{6,7},{7,6},{8,9},{9,8},{10,11... | collective-permute-start | bytes 1966088 | tf_op jit(solution)/shard_map/ppermute | solution.py:253
  16.5 30.3 %collective-permute-start.4 = (bf16[160,2048]{1,0:T(8,128)(2,1)S(1)}, bf16[160,2048]{1,0:T(8,128)(2,1)S(1)}, u32[]{:S(2)}, u32[]{:S(2)}) collective-permute-start(bf16[160,2048]{1,0:T(8,128)(2,1)S(1)} %get-tuple-element.72.refs_0_), channel_id=1, source_target_pairs={{0,2},{1,3},{2,0},{3,1},{4,6},{5,7},{6,4},{7,5},{8,10},{9,11},{10,... | collective-permute-start | bytes 1966088 | tf_op jit(solution)/shard_map/ppermute | solution.py:253
  18.1 38.2 %collective-permute-start.7 = (bf16[160,2048]{1,0:T(8,128)(2,1)S(1)}, bf16[160,2048]{1,0:T(8,128)(2,1)S(1)}, u32[]{:S(2)}, u32[]{:S(2)}) collective-permute-start(bf16[160,2048]{1,0:T(8,128)(2,1)S(1)} %get-tuple-element.72.refs_0_), channel_id=1, source_target_pairs={{0,4},{1,5},{2,6},{3,7},{4,0},{5,1},{6,2},{7,3},{8,12},{9,13},{10,... | collective-permute-start | bytes 1966088 | tf_op jit(solution)/shard_map/ppermute | solution.py:253
  20.7 3.1 %copy-start.1 = (bf16[2048,1792]{1,0:T(8,128)(2,1)S(1)}, bf16[2048,1792]{1,0:T(8,128)(2,1)}, u32[]{:S(2)}) copy-start(bf16[2048,1792]{1,0:T(8,128)(2,1)} %copy-done) | copy-start | bytes 22020100
  23.7 6.4 %copy-start.2 = (bf16[2048,1792]{1,0:T(8,128)(2,1)S(1)}, bf16[2048,1792]{1,0:T(8,128)(2,1)}, u32[]{:S(2)}) copy-start(bf16[2048,1792]{1,0:T(8,128)(2,1)} %copy-done) | copy-start | bytes 22020100
  23.7 6.5 %copy-start.4 = (s32[28,128]{1,0:T(8,128)S(1)}, s32[28,128]{1,0:T(8,128)}, u32[]{:S(2)}) copy-start(s32[28,128]{1,0:T(8,128)} %mask_ref.5) | copy-start | bytes 43012
  46.8 15.5 %collective-permute-start.9 = (bf16[160,2048]{1,0:T(8,128)(2,1)S(1)}, bf16[160,2048]{1,0:T(8,128)(2,1)S(1)}, u32[]{:S(2)}, u32[]{:S(2)}) collective-permute-start(bf16[160,2048]{1,0:T(8,128)(2,1)S(1)} %collective-permute-done.4.refs_5_.refs_0_), channel_id=1, source_target_pairs={{0,1},{1,0},{2,3},{3,2},{4,5},{5,4},{6,7},{7,6},{8,9},{9,8},{10,11... | collective-permute-start | bytes 1966088 | tf_op jit(solution)/shard_map/ppermute | solution.py:253
  53.2 2.0 %collective-permute-start.5 = (bf16[2,2,40,1792]{3,2,1,0:T(8,128)(2,1)S(1)}, bf16[2,2,40,1792]{3,2,1,0:T(8,128)(2,1)S(1)}, u32[]{:S(2)}, u32[]{:S(2)}) collective-permute-start(bf16[2,2,40,1792]{3,2,1,0:T(8,128)(2,1)S(1)} %get-tuple-element.78), channel_id=1, source_target_pairs={{0,8},{8,0},{16,24},{24,16},{1,9},{9,1},{17,25},{25,17},{2,10},{10... | collective-permute-start | bytes 1720328 | tf_op jit(solution)/shard_map/ppermute | solution.py:253
  53.3 2.8 %collective-permute-start.6 = (bf16[2,2,1,40,1792]{4,3,2,1,0:T(8,128)(2,1)S(1)}, bf16[2,2,1,40,1792]{4,3,2,1,0:T(8,128)(2,1)S(1)}, u32[]{:S(2)}, u32[]{:S(2)}) collective-permute-start(bf16[2,2,1,40,1792]{4,3,2,1,0:T(8,128)(2,1)S(1)} %get-tuple-element.79), channel_id=1, source_target_pairs={{0,8},{8,0},{16,24},{24,16},{1,9},{9,1},{17,25},{25,17},{2,10},{10... | collective-permute-start | bytes 1720328 | tf_op jit(solution)/shard_map/ppermute | solution.py:253
  56.2 17.1 %collective-permute-start.8 = (bf16[160,2048]{1,0:T(8,128)(2,1)S(1)}, bf16[160,2048]{1,0:T(8,128)(2,1)S(1)}, u32[]{:S(2)}, u32[]{:S(2)}) collective-permute-start(bf16[160,2048]{1,0:T(8,128)(2,1)S(1)} %collective-permute-done.7.refs_5_.refs_0_), channel_id=1, source_target_pairs={{0,2},{1,3},{2,0},{3,1},{4,6},{5,7},{6,4},{7,5},{8,10},{9,11},{10,... | collective-permute-start | bytes 1966088 | tf_op jit(solution)/shard_map/ppermute | solution.py:253
  62.2 14.9 %collective-permute-start.10 = (bf16[160,2048]{1,0:T(8,128)(2,1)S(1)}, bf16[160,2048]{1,0:T(8,128)(2,1)S(1)}, u32[]{:S(2)}, u32[]{:S(2)}) collective-permute-start(bf16[160,2048]{1,0:T(8,128)(2,1)S(1)} %collective-permute-done.7.refs_5_.refs_0_), channel_id=1, source_target_pairs={{0,1},{1,0},{2,3},{3,2},{4,5},{5,4},{6,7},{7,6},{8,9},{9,8},{10,11... | collective-permute-start | bytes 1966088 | tf_op jit(solution)/shard_map/ppermute | solution.py:253
  69.0 2.0 %collective-permute-start.12 = (bf16[2,2,1,40,1792]{4,3,2,1,0:T(8,128)(2,1)S(1)}, bf16[2,2,1,40,1792]{4,3,2,1,0:T(8,128)(2,1)S(1)}, u32[]{:S(2)}, u32[]{:S(2)}) collective-permute-start(bf16[2,2,1,40,1792]{4,3,2,1,0:T(8,128)(2,1)S(1)} %get-tuple-element.88), channel_id=1, source_target_pairs={{0,8},{8,0},{16,24},{24,16},{1,9},{9,1},{17,25},{25,17},{2,10},{10... | collective-permute-start | bytes 1720328 | tf_op jit(solution)/shard_map/ppermute | solution.py:253
  69.1 2.8 %collective-permute-start.13 = (bf16[2,2,40,1792]{3,2,1,0:T(8,128)(2,1)S(1)}, bf16[2,2,40,1792]{3,2,1,0:T(8,128)(2,1)S(1)}, u32[]{:S(2)}, u32[]{:S(2)}) collective-permute-start(bf16[2,2,40,1792]{3,2,1,0:T(8,128)(2,1)S(1)} %get-tuple-element.90), channel_id=1, source_target_pairs={{0,8},{8,0},{16,24},{24,16},{1,9},{9,1},{17,25},{25,17},{2,10},{10... | collective-permute-start | bytes 1720328 | tf_op jit(solution)/shard_map/ppermute | solution.py:253
  72.0 15.1 %collective-permute-start.15 = (bf16[2,2,40,1792]{3,2,1,0:T(8,128)(2,1)S(1)}, bf16[2,2,40,1792]{3,2,1,0:T(8,128)(2,1)S(1)}, u32[]{:S(2)}, u32[]{:S(2)}) collective-permute-start(bf16[2,2,40,1792]{3,2,1,0:T(8,128)(2,1)S(1)} %get-tuple-element.94), channel_id=1, source_target_pairs={{0,16},{8,24},{16,0},{24,8},{1,17},{9,25},{17,1},{25,9},{2,18},{10... | collective-permute-start | bytes 1720328 | tf_op jit(solution)/shard_map/ppermute | solution.py:253
  77.1 13.7 %collective-permute-start.11 = (bf16[160,2048]{1,0:T(8,128)(2,1)S(1)}, bf16[160,2048]{1,0:T(8,128)(2,1)S(1)}, u32[]{:S(2)}, u32[]{:S(2)}) collective-permute-start(bf16[160,2048]{1,0:T(8,128)(2,1)S(1)} %collective-permute-done.8.refs_5_.refs_0_), channel_id=1, source_target_pairs={{0,1},{1,0},{2,3},{3,2},{4,5},{5,4},{6,7},{7,6},{8,9},{9,8},{10,11... | collective-permute-start | bytes 1966088 | tf_op jit(solution)/shard_map/ppermute | solution.py:253
  83.9 3.5 %collective-permute-start.14 = (bf16[2,2,1,40,1792]{4,3,2,1,0:T(8,128)(2,1)S(1)}, bf16[2,2,1,40,1792]{4,3,2,1,0:T(8,128)(2,1)S(1)}, u32[]{:S(2)}, u32[]{:S(2)}) collective-permute-start(bf16[2,2,1,40,1792]{4,3,2,1,0:T(8,128)(2,1)S(1)} %get-tuple-element.93), channel_id=1, source_target_pairs={{0,8},{8,0},{16,24},{24,16},{1,9},{9,1},{17,25},{25,17},{2,10},{10... | collective-permute-start | bytes 1720328 | tf_op jit(solution)/shard_map/ppermute | solution.py:253
  84.0 3.4 %collective-permute-start.16 = (bf16[2,2,40,1792]{3,2,1,0:T(8,128)(2,1)S(1)}, bf16[2,2,40,1792]{3,2,1,0:T(8,128)(2,1)S(1)}, u32[]{:S(2)}, u32[]{:S(2)}) collective-permute-start(bf16[2,2,40,1792]{3,2,1,0:T(8,128)(2,1)S(1)} %get-tuple-element.97), channel_id=1, source_target_pairs={{0,8},{8,0},{16,24},{24,16},{1,9},{9,1},{17,25},{25,17},{2,10},{10... | collective-permute-start | bytes 1720328 | tf_op jit(solution)/shard_map/ppermute | solution.py:253
  87.6 16.5 %collective-permute-start.19 = (bf16[2,2,40,1792]{3,2,1,0:T(8,128)(2,1)S(1)}, bf16[2,2,40,1792]{3,2,1,0:T(8,128)(2,1)S(1)}, u32[]{:S(2)}, u32[]{:S(2)}) collective-permute-start(bf16[2,2,40,1792]{3,2,1,0:T(8,128)(2,1)S(1)} %get-tuple-element.102), channel_id=1, source_target_pairs={{0,16},{8,24},{16,0},{24,8},{1,17},{9,25},{17,1},{25,9},{2,18},{10... | collective-permute-start | bytes 1720328 | tf_op jit(solution)/shard_map/ppermute | solution.py:253
  96.9 7.7 %collective-permute-start.17 = (bf16[2,2,40,1792]{3,2,1,0:T(8,128)(2,1)S(1)}, bf16[2,2,40,1792]{3,2,1,0:T(8,128)(2,1)S(1)}, u32[]{:S(2)}, u32[]{:S(2)}) collective-permute-start(bf16[2,2,40,1792]{3,2,1,0:T(8,128)(2,1)S(1)} %get-tuple-element.100), channel_id=1, source_target_pairs={{0,8},{8,0},{16,24},{24,16},{1,9},{9,1},{17,25},{25,17},{2,10},{10... | collective-permute-start | bytes 1720328 | tf_op jit(solution)/shard_map/ppermute | solution.py:253
  97.0 7.6 %collective-permute-start.18 = (bf16[2,2,1,40,1792]{4,3,2,1,0:T(8,128)(2,1)S(1)}, bf16[2,2,1,40,1792]{4,3,2,1,0:T(8,128)(2,1)S(1)}, u32[]{:S(2)}, u32[]{:S(2)}) collective-permute-start(bf16[2,2,1,40,1792]{4,3,2,1,0:T(8,128)(2,1)S(1)} %get-tuple-element.101), channel_id=1, source_target_pairs={{0,8},{8,0},{16,24},{24,16},{1,9},{9,1},{17,25},{25,17},{2,10},{10... | collective-permute-start | bytes 1720328 | tf_op jit(solution)/shard_map/ppermute | solution.py:253
  97.5 2.7 %collective-permute-start.20 = (bf16[2,40,1792]{2,1,0:T(8,128)(2,1)S(1)}, bf16[2,40,1792]{2,1,0:T(8,128)(2,1)S(1)}, u32[]{:S(2)}, u32[]{:S(2)}) collective-permute-start(bf16[2,40,1792]{2,1,0:T(8,128)(2,1)S(1)} %get-tuple-element.103.own_ref), channel_id=1, source_target_pairs={{0,8},{8,0},{16,24},{24,16},{1,9},{9,1},{17,25},{25,17},{2,10},{10... | collective-permute-start | bytes 860168 | tf_op jit(solution)/shard_map/ppermute | solution.py:253
  104.4 1.9 %collective-permute-start.22 = (bf16[2,40,1792]{2,1,0:T(8,128)(2,1)S(1)}, bf16[2,40,1792]{2,1,0:T(8,128)(2,1)S(1)}, u32[]{:S(2)}, u32[]{:S(2)}) collective-permute-start(bf16[2,40,1792]{2,1,0:T(8,128)(2,1)S(1)} %get-tuple-element.109.own_ref), channel_id=1, source_target_pairs={{0,8},{8,0},{16,24},{24,16},{1,9},{9,1},{17,25},{25,17},{2,10},{10... | collective-permute-start | bytes 860168 | tf_op jit(solution)/shard_map/ppermute | solution.py:253
  104.7 15.3 %collective-permute-start.21 = (bf16[2,2,40,1792]{3,2,1,0:T(8,128)(2,1)S(1)}, bf16[2,2,40,1792]{3,2,1,0:T(8,128)(2,1)S(1)}, u32[]{:S(2)}, u32[]{:S(2)}) collective-permute-start(bf16[2,2,40,1792]{3,2,1,0:T(8,128)(2,1)S(1)} %get-tuple-element.108), channel_id=1, source_target_pairs={{0,16},{8,24},{16,0},{24,8},{1,17},{9,25},{17,1},{25,9},{2,18},{10... | collective-permute-start | bytes 1720328 | tf_op jit(solution)/shard_map/ppermute | solution.py:253
  110.2 16.8 %collective-permute-start.24 = (bf16[2,40,4096]{2,1,0:T(8,128)(2,1)S(1)}, bf16[2,40,4096]{2,1,0:T(8,128)(2,1)S(1)}, u32[]{:S(2)}, u32[]{:S(2)}) collective-permute-start(bf16[2,40,4096]{2,1,0:T(8,128)(2,1)S(1)} %get-tuple-element.115), channel_id=1, source_target_pairs={{0,1},{1,0},{2,3},{3,2},{4,5},{5,4},{6,7},{7,6},{8,9},{9,8},{10,11... | collective-permute-start | bytes 1966088 | tf_op jit(solution)/shard_map/ppermute | solution.py:253
  120.4 1.6 collective-permute-start.25
  120.4 15.4 %collective-permute-start.23 = (bf16[2,2,40,1792]{3,2,1,0:T(8,128)(2,1)S(1)}, bf16[2,2,40,1792]{3,2,1,0:T(8,128)(2,1)S(1)}, u32[]{:S(2)}, u32[]{:S(2)}) collective-permute-start(bf16[2,2,40,1792]{3,2,1,0:T(8,128)(2,1)S(1)} %get-tuple-element.113), channel_id=1, source_target_pairs={{0,16},{8,24},{16,0},{24,8},{1,17},{9,25},{17,1},{25,9},{2,18},{10... | collective-permute-start | bytes 1720328 | tf_op jit(solution)/shard_map/ppermute | solution.py:253
  127.0 15.9 %collective-permute-start.27 = (bf16[2,40,4096]{2,1,0:T(8,128)(2,1)S(1)}, bf16[2,40,4096]{2,1,0:T(8,128)(2,1)S(1)}, u32[]{:S(2)}, u32[]{:S(2)}) collective-permute-start(bf16[2,40,4096]{2,1,0:T(8,128)(2,1)S(1)} %get-tuple-element.125), channel_id=1, source_target_pairs={{0,1},{1,0},{2,3},{3,2},{4,5},{5,4},{6,7},{7,6},{8,9},{9,8},{10,11... | collective-permute-start | bytes 1966088 | tf_op jit(solution)/shard_map/ppermute | solution.py:253
  136.1 1.6 collective-permute-start.26
  136.2 17.1 %collective-permute-start.30 = (bf16[2,40,4096]{2,1,0:T(8,128)(2,1)S(1)}, bf16[2,40,4096]{2,1,0:T(8,128)(2,1)S(1)}, u32[]{:S(2)}, u32[]{:S(2)}) collective-permute-start(bf16[2,40,4096]{2,1,0:T(8,128)(2,1)S(1)} %get-tuple-element.131), channel_id=1, source_target_pairs={{0,2},{1,3},{2,0},{3,1},{4,6},{5,7},{6,4},{7,5},{8,10},{9,11},{10,... | collective-permute-start | bytes 1966088 | tf_op jit(solution)/shard_map/ppermute | solution.py:253
  142.8 15.7 %collective-permute-start.28 = (bf16[2,40,4096]{2,1,0:T(8,128)(2,1)S(1)}, bf16[2,40,4096]{2,1,0:T(8,128)(2,1)S(1)}, u32[]{:S(2)}, u32[]{:S(2)}) collective-permute-start(bf16[2,40,4096]{2,1,0:T(8,128)(2,1)S(1)} %get-tuple-element.127), channel_id=1, source_target_pairs={{0,1},{1,0},{2,3},{3,2},{4,5},{5,4},{6,7},{7,6},{8,9},{9,8},{10,11... | collective-permute-start | bytes 1966088 | tf_op jit(solution)/shard_map/ppermute | solution.py:253
  153.6 19.6 %collective-permute-start.32 = (bf16[2,40,4096]{2,1,0:T(8,128)(2,1)S(1)}, bf16[2,40,4096]{2,1,0:T(8,128)(2,1)S(1)}, u32[]{:S(2)}, u32[]{:S(2)}) collective-permute-start(bf16[2,40,4096]{2,1,0:T(8,128)(2,1)S(1)} %get-tuple-element.134), channel_id=1, source_target_pairs={{0,6},{1,7},{2,4},{3,5},{4,2},{5,3},{6,0},{7,1},{8,14},{9,15},{10,... | collective-permute-start | bytes 1966088 | tf_op jit(solution)/shard_map/ppermute | solution.py:253
  158.5 14.7 %collective-permute-start.29 = (bf16[2,40,4096]{2,1,0:T(8,128)(2,1)S(1)}, bf16[2,40,4096]{2,1,0:T(8,128)(2,1)S(1)}, u32[]{:S(2)}, u32[]{:S(2)}) collective-permute-start(bf16[2,40,4096]{2,1,0:T(8,128)(2,1)S(1)} %get-tuple-element.128), channel_id=1, source_target_pairs={{0,1},{1,0},{2,3},{3,2},{4,5},{5,4},{6,7},{7,6},{8,9},{9,8},{10,11... | collective-permute-start | bytes 1966088 | tf_op jit(solution)/shard_map/ppermute | solution.py:253
  160.2 25.7 %collective-permute-start.31 = (bf16[2,40,4096]{2,1,0:T(8,128)(2,1)S(1)}, bf16[2,40,4096]{2,1,0:T(8,128)(2,1)S(1)}, u32[]{:S(2)}, u32[]{:S(2)}) collective-permute-start(bf16[2,40,4096]{2,1,0:T(8,128)(2,1)S(1)} %get-tuple-element.133), channel_id=1, source_target_pairs={{0,2},{1,3},{2,0},{3,1},{4,6},{5,7},{6,4},{7,5},{8,10},{9,11},{10,... | collective-permute-start | bytes 1966088 | tf_op jit(solution)/shard_map/ppermute | solution.py:253
  186.3 1.7 collective-permute-start.33

commit v6 on v5

--- a/solution.py
+++ b/solution.py
@@ -10,6 +10,10 @@
 BLOCK = 64
 CORES = 2
 PLANES = 4
+NEXT = ((0, 1), (1, 0), (2, 3), (3, 2))
+MIRROR = ((0, 3), (3, 0), (1, 2), (2, 1))
+ACROSS = ((1, 2), (2, 1))
+OUTWARD = ((1, 0), (2, 3))
 VMEM = 12 * 1024 * 1024
 F32 = jnp.float32
 BF16 = jnp.bfloat16
@@ -54,7 +58,7 @@
     @pl.when(step == 0)
     def _():
         marks = mask_ref.shape[1]
-        first = core_ref[0] * (width // BLOCK)
+        first = core_ref[0] * (width // BLOCK) if marks * BLOCK > width else 0
         owner = lax.broadcasted_iota(jnp.int32, (marks, width), 1) // BLOCK + first
         chosen = (owner == lax.broadcasted_iota(jnp.int32, (marks, width), 0)).astype(F32)
         spread[...] = jnp.dot(mask_ref[...].astype(F32), chosen, preferred_element_type=F32)
@@ -74,7 +78,7 @@
             num_scalar_prefetch=1,
             grid=(depth // rows,),
             in_specs=[
-                pl.BlockSpec((rows, width), lambda i, core: (i, core[0])),
+                pl.BlockSpec((rows, width), lambda i, core: (i, core[0] if shares > 1 else 0)),
                 pl.BlockSpec(mask.shape, lambda i, core: (0, 0)),
             ]
             + [ANYWHERE] * len(after),
@@ -117,7 +121,8 @@
 
 def gate_up_kernel(part_count, after_count, *refs):
     parts, (gate_ref, up_ref) = refs[:part_count], refs[part_count : part_count + 2]
-    keep_ref, near_ref, far_ref, token_ref, all_rows = refs[part_count + 2 + after_count :]
+    keep_ref, near_ref, *far_refs, token_ref, all_rows = refs[part_count + 2 + after_count :]
+    far_places = [(far_ref, which) for far_ref in far_refs for which in range(far_ref.shape[0])]
     token_ref[...] = jnp.zeros_like(token_ref)
     half = parts[0].shape[0] // 2
     kept = half * len(parts)
@@ -134,14 +139,16 @@
             total = total.reshape(2, *keep_ref.shape[1:4], tile).astype(BF16)
             keep_ref[which, :, :, :, columns] = total[0]
             near_ref[which, :, :, columns] = total[1, :, 0]
-            far_ref[which, :, :, :, columns] = total[1, :, 1:]
-
-
-def gate_up(parts, gate_kept, up_kept, chips, after):
+            far_ref, place = far_places[which]
+            far_ref[place, :, :, :, columns] = total[1, :, 1:]
+
+
+def gate_up(parts, gate_kept, up_kept, chips, far_parts, after):
     rows = sum(part.shape[0] for part in parts)
     depth, width = gate_kept.shape
     groups, own = len(parts), rows // (2 * len(parts) * chips)
-    shapes = [(2, groups, chips, own, width), (2, groups, own, width), (2, groups, chips - 1, own, width)]
+    shapes = [(2, groups, chips, own, width), (2, groups, own, width)]
+    shapes += [(2 // far_parts, groups, chips - 1, own, width)] * far_parts
     return pl.pallas_call(
         functools.partial(gate_up_kernel, len(parts), len(after)),
         in_specs=[INSIDE] * (len(parts) + 2) + [ANYWHERE] * len(after),
@@ -149,12 +156,12 @@
         out_shape=[jax.ShapeDtypeStruct(shape, BF16) for shape in shapes] + [TOKEN],
         scratch_shapes=[pltpu.VMEM((rows, depth), BF16)],
         compiler_params=pltpu.CompilerParams(vmem_limit_bytes=VMEM // 2),
-        cost_estimate=cost(4 * rows * depth * width, 0),
+        cost_estimate=cost(HURRY * 4 * rows * depth * width, 0),
         name="gate_up",
     )(*parts, resident(gate_kept), resident(up_kept), *after)
 
 
-def down_kernel(after_count, own_ref, other_ref, weight_ref, *refs):
+def down_kernel(pieces, after_count, own_ref, other_ref, weight_ref, *refs):
     *partial_refs, token_ref, both = refs[after_count:]
     token_ref[...] = jnp.zeros_like(token_ref)
     groups, own, depth = own_ref.shape
@@ -167,20 +174,20 @@
     def _(number):
         columns = pl.ds(pl.multiple_of(number * tile, tile), tile)
         total = jnp.dot(both[...], weight_ref[:, columns], preferred_element_type=F32)
-        total = total.reshape(CORES, groups, own, tile)
+        total = total.reshape(pieces, CORES // pieces, groups, own, tile)
         for place, partial_ref in enumerate(partial_refs):
-            partial_ref[:, :, columns] = total[:, place].astype(BF16)
-
-
-def down(own, other, down_kept, after):
+            partial_ref[:, :, columns] = total[place % pieces, :, place // pieces].astype(BF16)
+
+
+def down(own, other, down_kept, pieces, after):
     groups, rows, depth = own.shape
     width = down_kept.shape[1]
-    shape = (CORES, rows, width)
+    shape = (CORES // pieces, rows, width)
     return pl.pallas_call(
-        functools.partial(down_kernel, len(after)),
+        functools.partial(down_kernel, pieces, len(after)),
         in_specs=[INSIDE] * 3 + [ANYWHERE] * len(after),
-        out_specs=[INSIDE] * (groups + 1),
-        out_shape=[jax.ShapeDtypeStruct(shape, BF16)] * groups + [TOKEN],
+        out_specs=[INSIDE] * (groups * pieces + 1),
+        out_shape=[jax.ShapeDtypeStruct(shape, BF16)] * (groups * pieces) + [TOKEN],
         scratch_shapes=[pltpu.VMEM((CORES * groups * rows, depth), BF16)],
         compiler_params=pltpu.CompilerParams(vmem_limit_bytes=VMEM // 2),
         cost_estimate=cost(2 * CORES * groups * rows * depth * width, 0),
@@ -188,7 +195,7 @@
     )(own, other, resident(down_kept), *after)
 
 
-def sums_kernel(sizes, after_count, *refs):
+def sums_kernel(sizes, first_core, after_count, *refs):
     to_chips, to_hidden, *to_rows = sizes
     refs = list(refs)
     refs.pop()[...] = jnp.zeros(TOKEN.shape, F32)
@@ -196,12 +203,13 @@
     del refs[:after_count]
 
     if to_chips:
-        keep_ref, came_ref = ins[0]
+        keep_ref, *came_refs = ins[0]
+        came_places = [came_ref.at[which] for came_ref in came_refs for which in range(came_ref.shape[0])]
         for chip in range(1, keep_ref.shape[2]):
             sent_ref = refs.pop(0)
             for which in range(2):
                 for group in range(keep_ref.shape[1]):
-                    came = came_ref[which, group, chip - 1].astype(F32)
+                    came = came_places[which][group, chip - 1].astype(F32)
                     sent_ref[which, group] = (keep_ref[which, group, chip].astype(F32) + came).astype(BF16)
     if to_hidden:
         keep_ref, came_ref, *chip_refs = ins[1]
@@ -216,14 +224,15 @@
             hidden_ref[group] = (jax.nn.silu(both[0]) * both[1]).astype(BF16)
     for part_refs in ins[2:]:
         summed_ref = refs.pop(0)
-        for core in range(CORES):
-            total = part_refs[0][core].astype(F32)
-            for part_ref in part_refs[1:]:
-                total = total + part_ref[core].astype(F32)
+        for core in range(summed_ref.shape[0]):
+            places = [core + first_core * (part_ref.shape[0] > summed_ref.shape[0]) for part_ref in part_refs]
+            total = part_refs[0][places[0]].astype(F32)
+            for part_ref, place in zip(part_refs[1:], places[1:]):
+                total = total + part_ref[place].astype(F32)
             summed_ref[core] = total.astype(BF16)
 
 
-def sums(to_chips, to_hidden, to_rows, after):
+def sums(to_chips, to_hidden, to_rows, first_core, after):
     shapes = []
     if to_chips:
         two, groups, chips, own, width = to_chips[0].shape
@@ -235,7 +244,7 @@
     sizes = tuple(len(parts) for parts in given)
     given = [part for parts in given for part in parts]
     results = list(pl.pallas_call(
-        functools.partial(sums_kernel, sizes, len(after)),
+        functools.partial(sums_kernel, sizes, first_core, len(after)),
         in_specs=[INSIDE] * len(given) + [ANYWHERE] * len(after),
         out_specs=[INSIDE] * (len(shapes) + 1),
         out_shape=[jax.ShapeDtypeStruct(shape, BF16) for shape in shapes] + [TOKEN],
@@ -260,21 +269,21 @@
     row = lax.axis_index("rows")
     core = row % CORES
     place = jnp.reshape(core, (1,)).astype(jnp.int32)
-    nowhere = jnp.zeros((1,), jnp.int32)
 
     normed = rms_normed(tokens, norm_gain)
     blocks = []
     for step in [chip * CORES + other for other in range(CORES) for chip in range(chips)]:
         block = lax.dynamic_slice_in_dim(normed, (row ^ step) * features, features, 1)
         blocks.append(swap(block, "rows", row_count, step) if step else block)
-    gate_kept, token = masked(gate_weight, gate_mask, tile_of(features, 256), nowhere, 1, [normed])
-    mine, token = assemble(blocks, [token, resident(gate_kept)])
+    gate_kept, token = masked(gate_weight, gate_mask, tile_of(features, 256), place, 1, [normed])
+    mine, token = assemble(blocks, [token])
 
     def behind(values, after):
         return lax.optimization_barrier((values, *after))[0] if after else values
 
-    def by_plane(values, plane, after=()):
-        return swap(behind(values, after), "cols", col_count, plane * per_plane)
+    def by_plane(values, planes, after=()):
+        pairs = [(a * per_plane + b, c * per_plane + b) for a, c in planes for b in range(per_plane)]
+        return lax.ppermute(behind(values, after), "cols", pairs)
 
     def by_row_of_plane(values, step, after=()):
         return swap(behind(values, after), "cols", col_count, step)
@@ -293,87 +302,99 @@
         for step in range(1, per_plane):
             parts[plane].append(by_row_of_plane(values, step, after))
 
-    def multiply_in(plane, after=()):
-        *halves[plane], last[0] = gate_up(parts[plane], gate_kept, up_kept, chips, last + list(after))
+    def multiply_in(plane, far_parts=1, after=()):
+        parts_after = last + list(after)
+        *halves[plane], last[0] = gate_up(parts[plane], gate_kept, up_kept, chips, far_parts, parts_after)
 
     def exchange(plane, after=()):
-        far[plane] = by_core(halves[plane][2], after)
+        far[plane] = [by_core(part, after) for part in halves[plane][2:]]
+
+    def exchange_near(plane, after=()):
         near[plane] = by_core(halves[plane][1], after)
 
-    def multiply_out(plane):
-        *partials[plane], last[0] = down(hiddens[plane], others[plane], down_kept, last)
-
-    def send_rows(plane, after=()):
-        rows_in[plane] = [partials[plane][0]]
-        for step in range(1, per_plane):
-            rows_in[plane].append(by_row_of_plane(partials[plane][step], step, after))
-
-    def to_chips(plane):
-        sent[plane], _, _, last[0] = sums([halves[plane][0], far[plane]], [], [], last + [near[plane]])
+    def multiply_out(plane, pieces=1):
+        *partials[plane], last[0] = down(hiddens[plane], others[plane], down_kept, pieces, last)
+
+    def send_rows(plane, after=(), pieces=1):
+        for piece in reversed(range(pieces)):
+            mine_and_others = partials[plane][piece::pieces]
+            rows_in[plane, piece] = mine_and_others[:1]
+            for step in range(1, per_plane):
+                rows_in[plane, piece].append(by_row_of_plane(mine_and_others[step], step, after))
+            after = rows_in[plane, piece][1:]
+
+    def to_chips(plane, after=()):
+        given = [halves[plane][0], *far[plane]]
+        sent[plane], _, _, last[0] = sums(given, [], [], 0, last + list(after))
 
     def send_chips(plane, after=()):
         chip_sums[plane] = [by_chip(part, number + 1, after) for number, part in enumerate(sent[plane])]
 
     def to_hidden(plane):
-        _, hiddens[plane], _, last[0] = sums([], [halves[plane][0], near[plane], *chip_sums[plane]], [], last)
+        _, hiddens[plane], _, last[0] = sums([], [halves[plane][0], near[plane], *chip_sums[plane]], [], 0, last)
         others[plane] = by_core(hiddens[plane])
 
-    def to_rows(*parts, after=()):
-        _, _, (summed,), last[0] = sums([], [], [parts], last + list(after))
+    def to_rows(*parts, first_core=0, after=()):
+        _, _, (summed,), last[0] = sums([], [], [parts], first_core, last + list(after))
         return summed
 
-    one_away = by_plane(mine, 1)
-    two_away = by_plane(mine, 2)
+    one_away = by_plane(mine, NEXT)
+    inner_three = by_plane(mine, ACROSS)
     forward(0, mine)
-    up_kept, last[0] = masked(up_weight, up_mask, tile_of(features, 256), nowhere, 1, last + [resident(gate_kept)])
-    down_kept, last[0] = masked(
-        down_weight, down_mask, 2 * BLOCK, place, CORES, last + [resident(gate_kept), resident(up_kept)]
-    )
+    up_kept, last[0] = masked(up_weight, up_mask, tile_of(features, 256), place, 1, last)
+    down_kept, last[0] = masked(down_weight, down_mask, 2 * BLOCK, place, CORES, last)
+    inner_two = by_plane(one_away, ACROSS, last)
+    outer_two = by_plane(inner_three, OUTWARD, last)
     forward(1, one_away, [*parts[0][1:], *last])
-    multiply_in(0, [one_away])
-    exchange(0)
-    to_chips(0)
-    three_away = by_plane(two_away, 1, last)
-    forward(2, two_away, [*parts[1][1:], *last])
-    multiply_in(1, [two_away])
+    multiply_in(0, after=[one_away, inner_three])
+    exchange(0, [inner_two, outer_two])
+    exchange_near(0, [inner_two, outer_two])
+    outer_three = by_plane(inner_two, OUTWARD, last)
+    forward(2, inner_two + outer_two, [*parts[1][1:], *last])
+    to_chips(0, [near[0]])
+    multiply_in(1)
     exchange(1)
-    to_chips(1)
+    exchange_near(1)
+    to_chips(1, [near[1]])
     send_chips(1)
-    forward(3, three_away, parts[2][1:])
-    multiply_in(2, [three_away])
+    forward(3, inner_three + behind(outer_three, last), [*parts[2][1:], *last])
+    multiply_in(2, after=[outer_three])
     exchange(2)
+    exchange_near(2)
     to_hidden(1)
-    to_chips(2)
+    to_chips(2, [near[2]])
     send_chips(2)
-    multiply_in(3)
+    multiply_out(1)
+    send_rows(1, parts[3][1:])
+    multiply_in(3, far_parts=2)
     exchange(3)
-    multiply_out(1)
     to_hidden(2)
     to_chips(3)
     send_chips(3)
+    exchange_near(3, last)
     multiply_out(2)
-    send_rows(2)
+    send_rows(2, rows_in[1, 0][1:])
+    one = to_rows(*rows_in[1, 0])
+    one_out = by_plane(one, NEXT)
     to_hidden(3)
-    send_chips(0, [last[0], *chip_sums[3]])
-    multiply_out(3)
-    send_rows(3, rows_in[2][1:])
-    two = to_rows(*rows_in[2])
-    two_out = by_plane(two, 1)
+    multiply_out(3, pieces=CORES)
+    send_chips(0, chip_sums[3])
+    send_rows(3, rows_in[2, 0][1:], pieces=CORES)
+    two = to_rows(*rows_in[2, 0], after=[one_out])
+    two_out = by_plane(two, NEXT)
     to_hidden(0)
     multiply_out(0)
-    send_rows(1, [*rows_in[3][1:], *last])
-    three = to_rows(*rows_in[3], two_out)
-    three_out = by_plane(three, 3)
-    send_rows(0, rows_in[1][1:])
-    one = to_rows(*rows_in[1])
-    one_out = by_plane(one, 1)
-    arrived = [*rows_in[0], one_out, three_out]
-
-    total = arrived[0].astype(F32)
-    for part in arrived[1:]:
-        total = total + part.astype(F32)
-    mine_now = total[0].astype(BF16)
-    other = by_core(total[1].astype(BF16))
+    three_out = {}
+    for piece in reversed(range(CORES)):
+        three = to_rows(*rows_in[3, piece], two_out, first_core=piece)
+        three_out[piece] = by_plane(three, MIRROR)
+    send_rows(0, rows_in[3, 0][1:])
+
+    def total(piece):
+        whole = [part[piece].astype(F32) for part in (*rows_in[0, 0], one_out)]
+        return (sum(whole[1:], whole[0]) + three_out[piece][0].astype(F32)).astype(BF16)
+
+    mine_now, other = total(0), by_core(total(1))
     left = jnp.where(core == 0, mine_now, other)
     right = jnp.where(core == 0, other, mine_now)
     return jnp.concatenate([left, right], 1)

time: 189 us -> 170 us (0.90)
  the two profiles are of different devices: /device:TPU:0 before, /device:TPU:8 now
where the time goes in v6:
time: 170 us; the launch traced here: 169 us
  Pallas kernels  64.1 us (38%)
  waiting for transfers between devices  62.2 us (37%)
  starting transfers between devices  38 us (22%)
  other arithmetic  4.35 us (3%)
    ppermute x9, waiting for transfers between devices, by_plane(): return lax.ppermute(behind(values, after), 'cols', pairs)  38.7 us
    pallas_call x4, Pallas kernels, gate_up(): pl.pallas_call(functools.partial(gate_up_kernel, len(parts), len(after)),...  24.3 us
    ppermute x30, waiting for transfers between devices, swap(): lax.ppermute(values, axis, [(place, place ^ step) for place in range(size)])  23.6 us
    ppermute x30, starting transfers between devices, swap(): lax.ppermute(values, axis, [(place, place ^ step) for place in range(size)])  22.2 us
    pallas_call x3, Pallas kernels, masked(): pl.pallas_call(functools.partial(mask_kernel, len(after)), grid_spec=pltp...  21.5 us
    ppermute x9, starting transfers between devices, by_plane(): return lax.ppermute(behind(values, after), 'cols', pairs)  15.8 us
    pallas_call x4, Pallas kernels, down(): pl.pallas_call(functools.partial(down_kernel, pieces, len(after)), in_spe...  15.5 us
  transfers between devices with their start and end apart: 39, of which 19 were waited for; matrix products, arithmetic and copies ran while one was open for 0% of the time, Pallas kernels for 38%

profile of v6, /device:TPU:8, one launch (start us, length us, event | category | flops | bytes accessed | tf_op | source)
XLA Modules:
  0.0 169.2 jit_solution(814141400966759025)
XLA Ops:
  0.0 1.3 fusion
  1.3 1.3 fusion.2.refs_0_
  2.7 1.6 collective-permute-start
  5.0 5.6 %masked.3 = (bf16[2048,1792]{1,0:T(8,128)(2,1)S(1)}, f32[8,128]{1,0:T(8,128)S(1)}) custom-call(s32[1]{0:T(128)} %bitcast.core_ref, bf16[2048,1792]{1,0:T(8,128)(2,1)} %weight_ref.3, s32[32,28]{1,0:T(8,128)S(1)} %copy-done, bf16[40,8192]{1,0:T(8,128)(2,1)S(1)} %fusion.2.refs_0_), custom_call_target="tpu_custom_call" | custom-call | bytes 14680 | tf_op jit(solution)/shard_map/masked/pallas_call | solution.py:75
  11.3 3.5 %collective-permute-start.5 = (bf16[160,2048]{1,0:T(8,128)(2,1)S(1)}, bf16[160,2048]{1,0:T(8,128)(2,1)S(1)}, u32[]{:S(2)}, u32[]{:S(2)}) collective-permute-start(bf16[160,2048]{1,0:T(8,128)(2,1)S(1)} %get-tuple-element.84.refs_0_), channel_id=1, source_target_pairs={{2,4},{3,5},{4,2},{5,3},{10,12},{11,13},{12,10},{13,11},{18,20},{1... | collective-permute-start | bytes 1966088 | tf_op jit(solution)/shard_map/ppermute | solution.py:286
  14.9 1.6 collective-permute-start.3
  16.5 5.6 %masked.4 = (bf16[2048,1792]{1,0:T(8,128)(2,1)S(1)}, f32[8,128]{1,0:T(8,128)S(1)}) custom-call(s32[1]{0:T(128)} %bitcast.core_ref, bf16[2048,1792]{1,0:T(8,128)(2,1)} %weight_ref.4, s32[32,28]{1,0:T(8,128)S(1)} %copy-done.1, f32[8,128]{1,0:T(8,128)S(1)} %get-tuple-element.86.refs_0_), custom_call_target="tpu_custom_call" | custom-call | bytes 14680 | tf_op jit(solution)/shard_map/masked/pallas_call | solution.py:75
  22.1 10.2 %masked.5 = (bf16[1792,4096]{1,0:T(8,128)(2,1)S(1)}, f32[8,128]{1,0:T(8,128)S(1)}) custom-call(s32[1]{0:T(128)} %bitcast.core_ref, bf16[1792,8192]{1,0:T(8,128)(2,1)} %weight_ref.5, s32[28,128]{1,0:T(8,128)S(1)} %copy-done.2, f32[8,128]{1,0:T(8,128)S(1)} %get-tuple-element.88.refs_0_), custom_call_target="tpu_custom_call" | custom-call | bytes 29360 | tf_op jit(solution)/shard_map/masked/pallas_call | solution.py:75
  32.4 3.9 %collective-permute-start.7 = (bf16[160,2048]{1,0:T(8,128)(2,1)S(1)}, bf16[160,2048]{1,0:T(8,128)(2,1)S(1)}, u32[]{:S(2)}, u32[]{:S(2)}) collective-permute-start(bf16[160,2048]{1,0:T(8,128)(2,1)S(1)} %collective-permute-done.5.refs_6_), channel_id=1, source_target_pairs={{2,0},{3,1},{4,6},{5,7},{10,8},{11,9},{12,14},{13,15},{18,16},{19,... | collective-permute-start | bytes 1966088 | tf_op jit(solution)/shard_map/ppermute | solution.py:286
  36.3 2.4 %collective-permute-start.6 = (bf16[160,2048]{1,0:T(8,128)(2,1)S(1)}, bf16[160,2048]{1,0:T(8,128)(2,1)S(1)}, u32[]{:S(2)}, u32[]{:S(2)}) collective-permute-start(bf16[160,2048]{1,0:T(8,128)(2,1)S(1)} %collective-permute-done.4.refs_5_.refs_0_), channel_id=1, source_target_pairs={{2,4},{3,5},{4,2},{5,3},{10,12},{11,13},{12,10},{13,11},{18,20},{1... | collective-permute-start | bytes 1966088 | tf_op jit(solution)/shard_map/ppermute | solution.py:286
  39.2 6.1 %gate_up.4 = (bf16[2,2,2,40,1792]{4,3,2,1,0:T(8,128)(2,1)S(1)}, bf16[2,2,40,1792]{3,2,1,0:T(8,128)(2,1)S(1)}, bf16[2,2,1,40,1792]{4,3,2,1,0:T(8,128)(2,1)S(1)}, f32[8,128]{1,0:T(8,128)S(1)}) custom-call(bf16[160,2048]{1,0:T(8,128)(2,1)S(1)} %get-tuple-element.84.refs_0_, bf16[160,2048]{1,0:T(8,128)(2,1)S(1)} %collective-permute-done.3.refs_1_, ...), custom_call_target="tpu_custom_call" | custom-call | flops 4697620480 | tf_op jit(solution)/shard_map/gate_up/pallas_call | solution.py:152
  45.3 5.0 %collective-permute-done.7 = bf16[160,2048]{1,0:T(8,128)(2,1)S(1)} collective-permute-done((bf16[160,2048]{1,0:T(8,128)(2,1)S(1)}, bf16[160,2048]{1,0:T(8,128)(2,1)S(1)}, u32[]{:S(2)}, u32[]{:S(2)}) %collective-permute-start.7) | collective-permute-done | bytes 655392 | tf_op jit(solution)/shard_map/ppermute | solution.py:286
  50.4 4.2 %collective-permute-done.6 = bf16[160,2048]{1,0:T(8,128)(2,1)S(1)} collective-permute-done((bf16[160,2048]{1,0:T(8,128)(2,1)S(1)}, bf16[160,2048]{1,0:T(8,128)(2,1)S(1)}, u32[]{:S(2)}, u32[]{:S(2)}) %collective-permute-start.6) | collective-permute-done | bytes 655392 | tf_op jit(solution)/shard_map/ppermute | solution.py:286
  55.8 1.3 collective-permute-start.10
  57.5 6.1 %gate_up.5 = (bf16[2,2,2,40,1792]{4,3,2,1,0:T(8,128)(2,1)S(1)}, bf16[2,2,40,1792]{3,2,1,0:T(8,128)(2,1)S(1)}, bf16[2,2,1,40,1792]{4,3,2,1,0:T(8,128)(2,1)S(1)}, f32[8,128]{1,0:T(8,128)S(1)}) custom-call(bf16[160,2048]{1,0:T(8,128)(2,1)S(1)} %collective-permute-done.4.refs_5_.refs_0_, bf16[160,2048]{1,0:T(8,128)(2,1)S(1)} %collective-permute-done.11.refs_1_, ...), custom_call_target="tpu_custom_call" | custom-call | flops 4697620480 | tf_op jit(solution)/shard_map/gate_up/pallas_call | solution.py:152
  64.1 1.5 collective-permute-done.12.refs_1_
  65.6 0.8 collective-permute-done.13.refs_3_.refs_1_
  66.6 1.6 collective-permute-start.16
  68.1 3.1 %collective-permute-done.10.refs_5_ = bf16[160,2048]{1,0:T(8,128)(2,1)S(1)} collective-permute-done((bf16[160,2048]{1,0:T(8,128)(2,1)S(1)}, bf16[160,2048]{1,0:T(8,128)(2,1)S(1)}, u32[]{:S(2)}, u32[]{:S(2)}) %collective-permute-start.10) | collective-permute-done | bytes 655392 | tf_op jit(solution)/shard_map/ppermute | solution.py:286
  72.0 1.1 collective-permute-start.15
  73.0 6.1 %gate_up.6 = (bf16[2,2,2,40,1792]{4,3,2,1,0:T(8,128)(2,1)S(1)}, bf16[2,2,40,1792]{3,2,1,0:T(8,128)(2,1)S(1)}, bf16[2,2,1,40,1792]{4,3,2,1,0:T(8,128)(2,1)S(1)}, f32[8,128]{1,0:T(8,128)S(1)}) custom-call(bf16[160,2048]{1,0:T(8,128)(2,1)S(1)} %add.69.refs_0_, bf16[160,2048]{1,0:T(8,128)(2,1)S(1)} %collective-permute-done.14.refs_1_, ...), custom_call_target="tpu_custom_call" | custom-call | flops 4697620480 | tf_op jit(solution)/shard_map/gate_up/pallas_call | solution.py:152
  79.7 2.0 %collective-permute-done.16.refs_2_ = bf16[2,2,40,1792]{3,2,1,0:T(8,128)(2,1)S(1)} collective-permute-done((bf16[2,2,40,1792]{3,2,1,0:T(8,128)(2,1)S(1)}, bf16[2,2,40,1792]{3,2,1,0:T(8,128)(2,1)S(1)}, u32[]{:S(2)}, u32[]{:S(2)}) %collective-permute-start.16) | collective-permute-done | bytes 573472 | tf_op jit(solution)/shard_map/ppermute | solution.py:262
  82.2 1.6 collective-permute-start.22
  83.8 3.9 %down.4 = (bf16[2,40,4096]{2,1,0:T(8,128)(2,1)S(1)}, bf16[2,40,4096]{2,1,0:T(8,128)(2,1)S(1)}, f32[8,128]{1,0:T(8,128)S(1)}) custom-call(bf16[2,40,1792]{2,1,0:T(8,128)(2,1)S(1)} %get-tuple-element.112.own_ref, bf16[2,40,1792]{2,1,0:T(8,128)(2,1)S(1)} %collective-permute-done.17.other_ref, bf16[1792,4096]{1,0:T(8,128)(2,1)S(1)} %get-tuple-element.113.weight_ref, ...), custom_call_target="tpu_custom_call" | custom-call | flops 2348810 | tf_op jit(solution)/shard_map/down/pallas_call | solution.py:186
  87.7 1.3 collective-permute-start.26
  89.1 6.1 %gate_up.7 = (bf16[2,2,2,40,1792]{4,3,2,1,0:T(8,128)(2,1)S(1)}, bf16[2,2,40,1792]{3,2,1,0:T(8,128)(2,1)S(1)}, bf16[1,2,1,40,1792]{4,3,2,1,0:T(8,128)(2,1)S(1)}, ...) custom-call(bf16[160,2048]{1,0:T(8,128)(2,1)S(1)} %add.68.refs_0_, ...), custom_call_target="tpu_custom_call" | custom-call | flops 4697620480 | tf_op jit(solution)/shard_map/gate_up/pallas_call | solution.py:152
  95.7 1.9 %collective-permute-done.22.refs_2_ = bf16[2,2,40,1792]{3,2,1,0:T(8,128)(2,1)S(1)} collective-permute-done((bf16[2,2,40,1792]{3,2,1,0:T(8,128)(2,1)S(1)}, bf16[2,2,40,1792]{3,2,1,0:T(8,128)(2,1)S(1)}, u32[]{:S(2)}, u32[]{:S(2)}) %collective-permute-start.22) | collective-permute-done | bytes 573472 | tf_op jit(solution)/shard_map/ppermute | solution.py:262
  98.7 1.5 collective-permute-start.23
  100.2 3.9 %down.5 = (bf16[2,40,4096]{2,1,0:T(8,128)(2,1)S(1)}, bf16[2,40,4096]{2,1,0:T(8,128)(2,1)S(1)}, f32[8,128]{1,0:T(8,128)S(1)}) custom-call(bf16[2,40,1792]{2,1,0:T(8,128)(2,1)S(1)} %get-tuple-element.128.own_ref, bf16[2,40,1792]{2,1,0:T(8,128)(2,1)S(1)} %collective-permute-done.25.other_ref, bf16[1792,4096]{1,0:T(8,128)(2,1)S(1)} %get-tuple-element.113.weight_ref, ...), custom_call_target="tpu_custom_call" | custom-call | flops 2348810 | tf_op jit(solution)/shard_map/down/pallas_call | solution.py:186
  104.6 1.4 collective-permute-start.27
  106.1 1.3 collective-permute-start.30
  107.4 6.3 %collective-permute-done.23.refs_2_ = bf16[2,2,40,1792]{3,2,1,0:T(8,128)(2,1)S(1)} collective-permute-done((bf16[2,2,40,1792]{3,2,1,0:T(8,128)(2,1)S(1)}, bf16[2,2,40,1792]{3,2,1,0:T(8,128)(2,1)S(1)}, u32[]{:S(2)}, u32[]{:S(2)}) %collective-permute-start.23) | collective-permute-done | bytes 573472 | tf_op jit(solution)/shard_map/ppermute | solution.py:262
  114.1 1.6 collective-permute-start.24
  115.6 3.9 %down.6 = (bf16[1,40,4096]{2,1,0:T(8,128)(2,1)S(1)}, bf16[1,40,4096]{2,1,0:T(8,128)(2,1)S(1)}, bf16[1,40,4096]{2,1,0:T(8,128)(2,1)S(1)}, bf16[1,40,4096]{2,1,0:T(8,128)(2,1)S(1)}, f32[8,128]{1,0:T(8,128)S(1)}) custom-call(bf16[2,40,1792]{2,1,0:T(8,128)(2,1)S(1)} %get-tuple-element.140.own_ref, bf16[2,40,1792]{2,1,0:T(8,128)(2,1)S(1)} %collective-permute-done.29.other_ref, ...), custom_call_target="tpu_custom_call" | custom-call | flops 2348810 | tf_op jit(solution)/shard_map/down/pallas_call | solution.py:186
  119.5 1.1 collective-permute-done.27.refs_1_
  120.6 1.4 collective-permute-start.32
  122.2 1.3 collective-permute-start.35
  123.4 5.9 %collective-permute-done.32.refs_1_ = bf16[1,40,4096]{2,1,0:T(8,128)(2,1)S(1)} collective-permute-done((bf16[1,40,4096]{2,1,0:T(8,128)(2,1)S(1)}, bf16[1,40,4096]{2,1,0:T(8,128)(2,1)S(1)}, u32[]{:S(2)}, u32[]{:S(2)}) %collective-permute-start.32) | collective-permute-done | bytes 327712 | tf_op jit(solution)/shard_map/ppermute | solution.py:262
  129.4 1.4 collective-permute-start.33
  131.1 1.6 collective-permute-done.31.other_ref
  132.7 3.9 %down.7 = (bf16[2,40,4096]{2,1,0:T(8,128)(2,1)S(1)}, bf16[2,40,4096]{2,1,0:T(8,128)(2,1)S(1)}, f32[8,128]{1,0:T(8,128)S(1)}) custom-call(bf16[2,40,1792]{2,1,0:T(8,128)(2,1)S(1)} %get-tuple-element.145.own_ref, bf16[2,40,1792]{2,1,0:T(8,128)(2,1)S(1)} %collective-permute-done.31.other_ref, bf16[1792,4096]{1,0:T(8,128)(2,1)S(1)} %get-tuple-element.113.weight_ref, ...), custom_call_target="tpu_custom_call" | custom-call | flops 2348810 | tf_op jit(solution)/shard_map/down/pallas_call | solution.py:186
  136.5 0.7 collective-permute-done.33.refs_1_
  137.2 1.3 collective-permute-start.34
  138.7 1.2 collective-permute-start.37
  140.5 0.9 collective-permute-start.36
  141.4 22.0 %collective-permute-done.37 = bf16[1,40,4096]{2,1,0:T(8,128)(2,1)S(1)} collective-permute-done((bf16[1,40,4096]{2,1,0:T(8,128)(2,1)S(1)}, bf16[1,40,4096]{2,1,0:T(8,128)(2,1)S(1)}, u32[]{:S(2)}, u32[]{:S(2)}) %collective-permute-start.37) | collective-permute-done | bytes 327712 | tf_op jit(solution)/shard_map/ppermute | solution.py:286
  163.7 4.3 %collective-permute-done.36 = bf16[1,40,4096]{2,1,0:T(8,128)(2,1)S(1)} collective-permute-done((bf16[1,40,4096]{2,1,0:T(8,128)(2,1)S(1)}, bf16[1,40,4096]{2,1,0:T(8,128)(2,1)S(1)}, u32[]{:S(2)}, u32[]{:S(2)}) %collective-permute-start.36) | collective-permute-done | bytes 327712 | tf_op jit(solution)/shard_map/ppermute | solution.py:286
  168.3 0.9 pad_maximum_fusion
  (70 shorter events, 10.6 us)
Async XLA Ops:
  1.3 3.6 %copy-start = (s32[32,28]{1,0:T(8,128)S(1)}, s32[32,28]{1,0:T(8,128)}, u32[]{:S(2)}) copy-start(s32[32,28]{1,0:T(8,128)} %mask_ref.3) | copy-start | bytes 10756
  2.7 7.9 %collective-permute-start = (bf16[40,2048]{1,0:T(8,128)(2,1)S(1)}, bf16[40,2048]{1,0:T(8,128)(2,1)S(1)}, u32[]{:S(2)}, u32[]{:S(2)}) collective-permute-start(bf16[40,2048]{1,0:T(8,128)(2,1)S(1)} %get-tuple-element.165), channel_id=1, source_target_pairs={{0,16},{8,24},{16,0},{24,8},{1,17},{9,25},{17,1},{25,9},{2,18},{10... | collective-permute-start | bytes 491528 | tf_op jit(solution)/shard_map/ppermute | solution.py:262
  4.3 6.3 %collective-permute-start.1 = (bf16[40,2048]{1,0:T(8,128)(2,1)S(1)}, bf16[40,2048]{1,0:T(8,128)(2,1)S(1)}, u32[]{:S(2)}, u32[]{:S(2)}) collective-permute-start(bf16[40,2048]{1,0:T(8,128)(2,1)S(1)} %get-tuple-element.164), channel_id=1, source_target_pairs={{0,8},{8,0},{16,24},{24,16},{1,9},{9,1},{17,25},{25,17},{2,10},{10... | collective-permute-start | bytes 491528 | tf_op jit(solution)/shard_map/ppermute | solution.py:262
  4.3 7.0 %collective-permute-start.2 = (bf16[40,2048]{1,0:T(8,128)(2,1)S(1)}, bf16[40,2048]{1,0:T(8,128)(2,1)S(1)}, u32[]{:S(2)}, u32[]{:S(2)}) collective-permute-start(bf16[40,2048]{1,0:T(8,128)(2,1)S(1)} %get-tuple-element.163), channel_id=1, source_target_pairs={{0,24},{8,16},{16,8},{24,0},{1,25},{9,17},{17,9},{25,1},{2,26},{10... | collective-permute-start | bytes 491528 | tf_op jit(solution)/shard_map/ppermute | solution.py:262
  5.0 11.5 %copy-start.1 = (s32[32,28]{1,0:T(8,128)S(1)}, s32[32,28]{1,0:T(8,128)}, u32[]{:S(2)}) copy-start(s32[32,28]{1,0:T(8,128)} %mask_ref.4) | copy-start | bytes 10756
  11.3 21.1 %collective-permute-start.5 = (bf16[160,2048]{1,0:T(8,128)(2,1)S(1)}, bf16[160,2048]{1,0:T(8,128)(2,1)S(1)}, u32[]{:S(2)}, u32[]{:S(2)}) collective-permute-start(bf16[160,2048]{1,0:T(8,128)(2,1)S(1)} %get-tuple-element.84.refs_0_), channel_id=1, source_target_pairs={{2,4},{3,5},{4,2},{5,3},{10,12},{11,13},{12,10},{13,11},{18,20},{1... | collective-permute-start | bytes 1966088 | tf_op jit(solution)/shard_map/ppermute | solution.py:286
  14.8 21.5 %collective-permute-start.4 = (bf16[160,2048]{1,0:T(8,128)(2,1)S(1)}, bf16[160,2048]{1,0:T(8,128)(2,1)S(1)}, u32[]{:S(2)}, u32[]{:S(2)}) collective-permute-start(bf16[160,2048]{1,0:T(8,128)(2,1)S(1)} %get-tuple-element.84.refs_0_), channel_id=1, source_target_pairs={{0,2},{1,3},{2,0},{3,1},{4,6},{5,7},{6,4},{7,5},{8,10},{9,11},{10,... | collective-permute-start | bytes 1966088 | tf_op jit(solution)/shard_map/ppermute | solution.py:286
  14.9 23.8 %collective-permute-start.3 = (bf16[160,2048]{1,0:T(8,128)(2,1)S(1)}, bf16[160,2048]{1,0:T(8,128)(2,1)S(1)}, u32[]{:S(2)}, u32[]{:S(2)}) collective-permute-start(bf16[160,2048]{1,0:T(8,128)(2,1)S(1)} %get-tuple-element.84.refs_0_), channel_id=1, source_target_pairs={{0,1},{1,0},{2,3},{3,2},{4,5},{5,4},{6,7},{7,6},{8,9},{9,8},{10,11... | collective-permute-start | bytes 1966088 | tf_op jit(solution)/shard_map/ppermute | solution.py:262
  16.5 5.7 %copy-start.2 = (s32[28,128]{1,0:T(8,128)S(1)}, s32[28,128]{1,0:T(8,128)}, u32[]{:S(2)}) copy-start(s32[28,128]{1,0:T(8,128)} %mask_ref.5) | copy-start | bytes 43012
  32.4 18.0 %collective-permute-start.7 = (bf16[160,2048]{1,0:T(8,128)(2,1)S(1)}, bf16[160,2048]{1,0:T(8,128)(2,1)S(1)}, u32[]{:S(2)}, u32[]{:S(2)}) collective-permute-start(bf16[160,2048]{1,0:T(8,128)(2,1)S(1)} %collective-permute-done.5.refs_6_), channel_id=1, source_target_pairs={{2,0},{3,1},{4,6},{5,7},{10,8},{11,9},{12,14},{13,15},{18,16},{19,... | collective-permute-start | bytes 1966088 | tf_op jit(solution)/shard_map/ppermute | solution.py:286
  36.3 18.2 %collective-permute-start.6 = (bf16[160,2048]{1,0:T(8,128)(2,1)S(1)}, bf16[160,2048]{1,0:T(8,128)(2,1)S(1)}, u32[]{:S(2)}, u32[]{:S(2)}) collective-permute-start(bf16[160,2048]{1,0:T(8,128)(2,1)S(1)} %collective-permute-done.4.refs_5_.refs_0_), channel_id=1, source_target_pairs={{2,4},{3,5},{4,2},{5,3},{10,12},{11,13},{12,10},{13,11},{18,20},{1... | collective-permute-start | bytes 1966088 | tf_op jit(solution)/shard_map/ppermute | solution.py:286
  38.7 16.6 %collective-permute-start.11 = (bf16[160,2048]{1,0:T(8,128)(2,1)S(1)}, bf16[160,2048]{1,0:T(8,128)(2,1)S(1)}, u32[]{:S(2)}, u32[]{:S(2)}) collective-permute-start(bf16[160,2048]{1,0:T(8,128)(2,1)S(1)} %collective-permute-done.4.refs_5_.refs_0_), channel_id=1, source_target_pairs={{0,1},{1,0},{2,3},{3,2},{4,5},{5,4},{6,7},{7,6},{8,9},{9,8},{10,11... | collective-permute-start | bytes 1966088 | tf_op jit(solution)/shard_map/ppermute | solution.py:262
  54.5 2.6 %collective-permute-start.8 = (bf16[2,2,40,1792]{3,2,1,0:T(8,128)(2,1)S(1)}, bf16[2,2,40,1792]{3,2,1,0:T(8,128)(2,1)S(1)}, u32[]{:S(2)}, u32[]{:S(2)}) collective-permute-start(bf16[2,2,40,1792]{3,2,1,0:T(8,128)(2,1)S(1)} %get-tuple-element.94), channel_id=1, source_target_pairs={{0,8},{8,0},{16,24},{24,16},{1,9},{9,1},{17,25},{25,17},{2,10},{10... | collective-permute-start | bytes 1720328 | tf_op jit(solution)/shard_map/ppermute | solution.py:262
  54.5 2.8 %collective-permute-start.9 = (bf16[2,2,1,40,1792]{4,3,2,1,0:T(8,128)(2,1)S(1)}, bf16[2,2,1,40,1792]{4,3,2,1,0:T(8,128)(2,1)S(1)}, u32[]{:S(2)}, u32[]{:S(2)}) collective-permute-start(bf16[2,2,1,40,1792]{4,3,2,1,0:T(8,128)(2,1)S(1)} %get-tuple-element.96), channel_id=1, source_target_pairs={{0,8},{8,0},{16,24},{24,16},{1,9},{9,1},{17,25},{25,17},{2,10},{10... | collective-permute-start | bytes 1720328 | tf_op jit(solution)/shard_map/ppermute | solution.py:262
  55.2 16.7 %collective-permute-start.14 = (bf16[160,2048]{1,0:T(8,128)(2,1)S(1)}, bf16[160,2048]{1,0:T(8,128)(2,1)S(1)}, u32[]{:S(2)}, u32[]{:S(2)}) collective-permute-start(bf16[160,2048]{1,0:T(8,128)(2,1)S(1)} %add.69.refs_0_), channel_id=1, source_target_pairs={{0,1},{1,0},{2,3},{3,2},{4,5},{5,4},{6,7},{7,6},{8,9},{9,8},{10,11... | collective-permute-start | bytes 1966088 | tf_op jit(solution)/shard_map/ppermute | solution.py:262
  55.8 15.4 %collective-permute-start.10 = (bf16[160,2048]{1,0:T(8,128)(2,1)S(1)}, bf16[160,2048]{1,0:T(8,128)(2,1)S(1)}, u32[]{:S(2)}, u32[]{:S(2)}) collective-permute-start(bf16[160,2048]{1,0:T(8,128)(2,1)S(1)} %collective-permute-done.6), channel_id=1, source_target_pairs={{2,0},{3,1},{4,6},{5,7},{10,8},{11,9},{12,14},{13,15},{18,16},{19,... | collective-permute-start | bytes 1966088 | tf_op jit(solution)/shard_map/ppermute | solution.py:286
  63.6 2.0 %collective-permute-start.12 = (bf16[2,2,1,40,1792]{4,3,2,1,0:T(8,128)(2,1)S(1)}, bf16[2,2,1,40,1792]{4,3,2,1,0:T(8,128)(2,1)S(1)}, u32[]{:S(2)}, u32[]{:S(2)}) collective-permute-start(bf16[2,2,1,40,1792]{4,3,2,1,0:T(8,128)(2,1)S(1)} %get-tuple-element.103), channel_id=1, source_target_pairs={{0,8},{8,0},{16,24},{24,16},{1,9},{9,1},{17,25},{25,17},{2,10},{10... | collective-permute-start | bytes 1720328 | tf_op jit(solution)/shard_map/ppermute | solution.py:262
  63.8 2.7 %collective-permute-start.13 = (bf16[2,2,40,1792]{3,2,1,0:T(8,128)(2,1)S(1)}, bf16[2,2,40,1792]{3,2,1,0:T(8,128)(2,1)S(1)}, u32[]{:S(2)}, u32[]{:S(2)}) collective-permute-start(bf16[2,2,40,1792]{3,2,1,0:T(8,128)(2,1)S(1)} %get-tuple-element.105), channel_id=1, source_target_pairs={{0,8},{8,0},{16,24},{24,16},{1,9},{9,1},{17,25},{25,17},{2,10},{10... | collective-permute-start | bytes 1720328 | tf_op jit(solution)/shard_map/ppermute | solution.py:262
  66.6 15.1 %collective-permute-start.16 = (bf16[2,2,40,1792]{3,2,1,0:T(8,128)(2,1)S(1)}, bf16[2,2,40,1792]{3,2,1,0:T(8,128)(2,1)S(1)}, u32[]{:S(2)}, u32[]{:S(2)}) collective-permute-start(bf16[2,2,40,1792]{3,2,1,0:T(8,128)(2,1)S(1)} %get-tuple-element.110), channel_id=1, source_target_pairs={{0,16},{8,24},{16,0},{24,8},{1,17},{9,25},{17,1},{25,9},{2,18},{10... | collective-permute-start | bytes 1720328 | tf_op jit(solution)/shard_map/ppermute | solution.py:262
  72.0 15.8 %collective-permute-start.15 = (bf16[160,2048]{1,0:T(8,128)(2,1)S(1)}, bf16[160,2048]{1,0:T(8,128)(2,1)S(1)}, u32[]{:S(2)}, u32[]{:S(2)}) collective-permute-start(bf16[160,2048]{1,0:T(8,128)(2,1)S(1)} %add.68.refs_0_), channel_id=1, source_target_pairs={{0,1},{1,0},{2,3},{3,2},{4,5},{5,4},{6,7},{7,6},{8,9},{9,8},{10,11... | collective-permute-start | bytes 1966088 | tf_op jit(solution)/shard_map/ppermute | solution.py:262
  79.1 2.9 %collective-permute-start.18 = (bf16[2,2,1,40,1792]{4,3,2,1,0:T(8,128)(2,1)S(1)}, bf16[2,2,1,40,1792]{4,3,2,1,0:T(8,128)(2,1)S(1)}, u32[]{:S(2)}, u32[]{:S(2)}) collective-permute-start(bf16[2,2,1,40,1792]{4,3,2,1,0:T(8,128)(2,1)S(1)} %get-tuple-element.115), channel_id=1, source_target_pairs={{0,8},{8,0},{16,24},{24,16},{1,9},{9,1},{17,25},{25,17},{2,10},{10... | collective-permute-start | bytes 1720328 | tf_op jit(solution)/shard_map/ppermute | solution.py:262
  79.2 2.8 %collective-permute-start.19 = (bf16[2,2,40,1792]{3,2,1,0:T(8,128)(2,1)S(1)}, bf16[2,2,40,1792]{3,2,1,0:T(8,128)(2,1)S(1)}, u32[]{:S(2)}, u32[]{:S(2)}) collective-permute-start(bf16[2,2,40,1792]{3,2,1,0:T(8,128)(2,1)S(1)} %get-tuple-element.117), channel_id=1, source_target_pairs={{0,8},{8,0},{16,24},{24,16},{1,9},{9,1},{17,25},{25,17},{2,10},{10... | collective-permute-start | bytes 1720328 | tf_op jit(solution)/shard_map/ppermute | solution.py:262
  82.0 1.8 %collective-permute-start.17 = (bf16[2,40,1792]{2,1,0:T(8,128)(2,1)S(1)}, bf16[2,40,1792]{2,1,0:T(8,128)(2,1)S(1)}, u32[]{:S(2)}, u32[]{:S(2)}) collective-permute-start(bf16[2,40,1792]{2,1,0:T(8,128)(2,1)S(1)} %get-tuple-element.112.own_ref), channel_id=1, source_target_pairs={{0,8},{8,0},{16,24},{24,16},{1,9},{9,1},{17,25},{25,17},{2,10},{10... | collective-permute-start | bytes 860168 | tf_op jit(solution)/shard_map/ppermute | solution.py:262
  82.2 15.4 %collective-permute-start.22 = (bf16[2,2,40,1792]{3,2,1,0:T(8,128)(2,1)S(1)}, bf16[2,2,40,1792]{3,2,1,0:T(8,128)(2,1)S(1)}, u32[]{:S(2)}, u32[]{:S(2)}) collective-permute-start(bf16[2,2,40,1792]{3,2,1,0:T(8,128)(2,1)S(1)} %get-tuple-element.123), channel_id=1, source_target_pairs={{0,16},{8,24},{16,0},{24,8},{1,17},{9,25},{17,1},{25,9},{2,18},{10... | collective-permute-start | bytes 1720328 | tf_op jit(solution)/shard_map/ppermute | solution.py:262
  87.7 16.8 %collective-permute-start.26 = (bf16[2,40,4096]{2,1,0:T(8,128)(2,1)S(1)}, bf16[2,40,4096]{2,1,0:T(8,128)(2,1)S(1)}, u32[]{:S(2)}, u32[]{:S(2)}) collective-permute-start(bf16[2,40,4096]{2,1,0:T(8,128)(2,1)S(1)} %get-tuple-element.133), channel_id=1, source_target_pairs={{0,1},{1,0},{2,3},{3,2},{4,5},{5,4},{6,7},{7,6},{8,9},{9,8},{10,11... | collective-permute-start | bytes 1966088 | tf_op jit(solution)/shard_map/ppermute | solution.py:262
  95.2 2.8 %collective-permute-start.20 = (bf16[1,2,1,40,1792]{4,3,2,1,0:T(8,128)(2,1)S(1)}, bf16[1,2,1,40,1792]{4,3,2,1,0:T(8,128)(2,1)S(1)}, u32[]{:S(2)}, u32[]{:S(2)}) collective-permute-start(bf16[1,2,1,40,1792]{4,3,2,1,0:T(8,128)(2,1)S(1)} %get-tuple-element.121), channel_id=1, source_target_pairs={{0,8},{8,0},{16,24},{24,16},{1,9},{9,1},{17,25},{25,17},{2,10},{10... | collective-permute-start | bytes 860168 | tf_op jit(solution)/shard_map/ppermute | solution.py:262
  95.2 2.8 %collective-permute-start.21 = (bf16[1,2,1,40,1792]{4,3,2,1,0:T(8,128)(2,1)S(1)}, bf16[1,2,1,40,1792]{4,3,2,1,0:T(8,128)(2,1)S(1)}, u32[]{:S(2)}, u32[]{:S(2)}) collective-permute-start(bf16[1,2,1,40,1792]{4,3,2,1,0:T(8,128)(2,1)S(1)} %get-tuple-element.122), channel_id=1, source_target_pairs={{0,8},{8,0},{16,24},{24,16},{1,9},{9,1},{17,25},{25,17},{2,10},{10... | collective-permute-start | bytes 860168 | tf_op jit(solution)/shard_map/ppermute | solution.py:262
  97.9 2.3 %collective-permute-start.25 = (bf16[2,40,1792]{2,1,0:T(8,128)(2,1)S(1)}, bf16[2,40,1792]{2,1,0:T(8,128)(2,1)S(1)}, u32[]{:S(2)}, u32[]{:S(2)}) collective-permute-start(bf16[2,40,1792]{2,1,0:T(8,128)(2,1)S(1)} %get-tuple-element.128.own_ref), channel_id=1, source_target_pairs={{0,8},{8,0},{16,24},{24,16},{1,9},{9,1},{17,25},{25,17},{2,10},{10... | collective-permute-start | bytes 860168 | tf_op jit(solution)/shard_map/ppermute | solution.py:262
  98.2 9.2 %collective-permute-start.28 = (bf16[2,2,40,1792]{3,2,1,0:T(8,128)(2,1)S(1)}, bf16[2,2,40,1792]{3,2,1,0:T(8,128)(2,1)S(1)}, u32[]{:S(2)}, u32[]{:S(2)}) collective-permute-start(bf16[2,2,40,1792]{3,2,1,0:T(8,128)(2,1)S(1)} %get-tuple-element.136), channel_id=1, source_target_pairs={{0,8},{8,0},{16,24},{24,16},{1,9},{9,1},{17,25},{25,17},{2,10},{10... | collective-permute-start | bytes 1720328 | tf_op jit(solution)/shard_map/ppermute | solution.py:262
  98.7 15.0 %collective-permute-start.23 = (bf16[2,2,40,1792]{3,2,1,0:T(8,128)(2,1)S(1)}, bf16[2,2,40,1792]{3,2,1,0:T(8,128)(2,1)S(1)}, u32[]{:S(2)}, u32[]{:S(2)}) collective-permute-start(bf16[2,2,40,1792]{3,2,1,0:T(8,128)(2,1)S(1)} %get-tuple-element.126), channel_id=1, source_target_pairs={{0,16},{8,24},{16,0},{24,8},{1,17},{9,25},{17,1},{25,9},{2,18},{10... | collective-permute-start | bytes 1720328 | tf_op jit(solution)/shard_map/ppermute | solution.py:262
  104.6 16.1 %collective-permute-start.27 = (bf16[2,40,4096]{2,1,0:T(8,128)(2,1)S(1)}, bf16[2,40,4096]{2,1,0:T(8,128)(2,1)S(1)}, u32[]{:S(2)}, u32[]{:S(2)}) collective-permute-start(bf16[2,40,4096]{2,1,0:T(8,128)(2,1)S(1)} %get-tuple-element.134), channel_id=1, source_target_pairs={{0,1},{1,0},{2,3},{3,2},{4,5},{5,4},{6,7},{7,6},{8,9},{9,8},{10,11... | collective-permute-start | bytes 1966088 | tf_op jit(solution)/shard_map/ppermute | solution.py:262
  106.1 15.9 %collective-permute-start.30 = (bf16[2,40,4096]{2,1,0:T(8,128)(2,1)S(1)}, bf16[2,40,4096]{2,1,0:T(8,128)(2,1)S(1)}, u32[]{:S(2)}, u32[]{:S(2)}) collective-permute-start(bf16[2,40,4096]{2,1,0:T(8,128)(2,1)S(1)} %get-tuple-element.143), channel_id=1, source_target_pairs={{0,2},{1,3},{2,0},{3,1},{4,6},{5,7},{6,4},{7,5},{8,10},{9,11},{10,... | collective-permute-start | bytes 1966088 | tf_op jit(solution)/shard_map/ppermute | solution.py:286
  114.0 1.7 collective-permute-start.29
  114.1 16.7 %collective-permute-start.24 = (bf16[2,2,40,1792]{3,2,1,0:T(8,128)(2,1)S(1)}, bf16[2,2,40,1792]{3,2,1,0:T(8,128)(2,1)S(1)}, u32[]{:S(2)}, u32[]{:S(2)}) collective-permute-start(bf16[2,2,40,1792]{3,2,1,0:T(8,128)(2,1)S(1)} %get-tuple-element.127), channel_id=1, source_target_pairs={{0,16},{8,24},{16,0},{24,8},{1,17},{9,25},{17,1},{25,9},{2,18},{10... | collective-permute-start | bytes 1720328 | tf_op jit(solution)/shard_map/ppermute | solution.py:262
  120.6 8.7 %collective-permute-start.32 = (bf16[1,40,4096]{2,1,0:T(8,128)(2,1)S(1)}, bf16[1,40,4096]{2,1,0:T(8,128)(2,1)S(1)}, u32[]{:S(2)}, u32[]{:S(2)}) collective-permute-start(bf16[1,40,4096]{2,1,0:T(8,128)(2,1)S(1)} %get-tuple-element.151), channel_id=1, source_target_pairs={{0,1},{1,0},{2,3},{3,2},{4,5},{5,4},{6,7},{7,6},{8,9},{9,8},{10,11... | collective-permute-start | bytes 983048 | tf_op jit(solution)/shard_map/ppermute | solution.py:262
  122.2 16.4 %collective-permute-start.35 = (bf16[2,40,4096]{2,1,0:T(8,128)(2,1)S(1)}, bf16[2,40,4096]{2,1,0:T(8,128)(2,1)S(1)}, u32[]{:S(2)}, u32[]{:S(2)}) collective-permute-start(bf16[2,40,4096]{2,1,0:T(8,128)(2,1)S(1)} %get-tuple-element.155), channel_id=1, source_target_pairs={{0,2},{1,3},{2,0},{3,1},{4,6},{5,7},{6,4},{7,5},{8,10},{9,11},{10,... | collective-permute-start | bytes 1966088 | tf_op jit(solution)/shard_map/ppermute | solution.py:286
  129.4 7.8 %collective-permute-start.33 = (bf16[1,40,4096]{2,1,0:T(8,128)(2,1)S(1)}, bf16[1,40,4096]{2,1,0:T(8,128)(2,1)S(1)}, u32[]{:S(2)}, u32[]{:S(2)}) collective-permute-start(bf16[1,40,4096]{2,1,0:T(8,128)(2,1)S(1)} %get-tuple-element.152), channel_id=1, source_target_pairs={{0,1},{1,0},{2,3},{3,2},{4,5},{5,4},{6,7},{7,6},{8,9},{9,8},{10,11... | collective-permute-start | bytes 983048 | tf_op jit(solution)/shard_map/ppermute | solution.py:262
  131.0 1.6 collective-permute-start.31
  137.2 26.2 %collective-permute-start.34 = (bf16[2,40,4096]{2,1,0:T(8,128)(2,1)S(1)}, bf16[2,40,4096]{2,1,0:T(8,128)(2,1)S(1)}, u32[]{:S(2)}, u32[]{:S(2)}) collective-permute-start(bf16[2,40,4096]{2,1,0:T(8,128)(2,1)S(1)} %get-tuple-element.153), channel_id=1, source_target_pairs={{0,1},{1,0},{2,3},{3,2},{4,5},{5,4},{6,7},{7,6},{8,9},{9,8},{10,11... | collective-permute-start | bytes 1966088 | tf_op jit(solution)/shard_map/ppermute | solution.py:262
  138.7 24.8 %collective-permute-start.37 = (bf16[1,40,4096]{2,1,0:T(8,128)(2,1)S(1)}, bf16[1,40,4096]{2,1,0:T(8,128)(2,1)S(1)}, u32[]{:S(2)}, u32[]{:S(2)}) collective-permute-start(bf16[1,40,4096]{2,1,0:T(8,128)(2,1)S(1)} %get-tuple-element.160), channel_id=1, source_target_pairs={{0,6},{1,7},{6,0},{7,1},{2,4},{3,5},{4,2},{5,3},{8,14},{9,15},{14,... | collective-permute-start | bytes 983048 | tf_op jit(solution)/shard_map/ppermute | solution.py:286
  140.5 27.5 %collective-permute-start.36 = (bf16[1,40,4096]{2,1,0:T(8,128)(2,1)S(1)}, bf16[1,40,4096]{2,1,0:T(8,128)(2,1)S(1)}, u32[]{:S(2)}, u32[]{:S(2)}) collective-permute-start(bf16[1,40,4096]{2,1,0:T(8,128)(2,1)S(1)} %get-tuple-element.159), channel_id=1, source_target_pairs={{0,6},{1,7},{6,0},{7,1},{2,4},{3,5},{4,2},{5,3},{8,14},{9,15},{14,... | collective-permute-start | bytes 983048 | tf_op jit(solution)/shard_map/ppermute | solution.py:286
  163.6 4.4 %collective-permute-start.38 = (bf16[40,4096]{1,0:T(8,128)(2,1)S(1)}, bf16[40,4096]{1,0:T(8,128)(2,1)S(1)}, u32[]{:S(2)}, u32[]{:S(2)}) collective-permute-start(bf16[40,4096]{1,0:T(8,128)(2,1)S(1)} %fusion.4), channel_id=1, source_target_pairs={{0,8},{8,0},{16,24},{24,16},{1,9},{9,1},{17,25},{25,17},{2,10},{10... | collective-permute-start | bytes 983048 | tf_op jit(solution)/shard_map/ppermute | solution.py:262

commit v7 on v6

--- a/solution.py
+++ b/solution.py
@@ -43,12 +43,16 @@
     return pl.CostEstimate(flops=flops // HURRY, bytes_accessed=moved // HURRY, transcendentals=0)
 
 
+def as_if(microseconds):
+    return cost(int(HURRY * 1.15e9 * microseconds), 0)
+
+
 ANYWHERE = pl.BlockSpec(memory_space=pl.ANY)
 TOKEN = jax.ShapeDtypeStruct((8, 128), F32)
 INSIDE = pl.BlockSpec(memory_space=pltpu.VMEM)
 
 
-def mask_kernel(after_count, core_ref, weight_ref, mask_ref, *refs):
+def mask_kernel(share, after_count, core_ref, weight_ref, mask_ref, *refs):
     kept_ref, token_ref, spread = refs[after_count:]
     token_ref[...] = jnp.zeros_like(token_ref)
     depth, width = weight_ref.shape
@@ -58,7 +62,7 @@
     @pl.when(step == 0)
     def _():
         marks = mask_ref.shape[1]
-        first = core_ref[0] * (width // BLOCK) if marks * BLOCK > width else 0
+        first = share(core_ref[0]) * (width // BLOCK)
         owner = lax.broadcasted_iota(jnp.int32, (marks, width), 1) // BLOCK + first
         chosen = (owner == lax.broadcasted_iota(jnp.int32, (marks, width), 0)).astype(F32)
         spread[...] = jnp.dot(mask_ref[...].astype(F32), chosen, preferred_element_type=F32)
@@ -69,16 +73,16 @@
         kept_ref[rows, :] = weight_ref[rows, :] * keep.astype(BF16)
 
 
-def masked(weight, mask, rows, core, shares, after):
+def masked(weight, mask, rows, core, shares, share, after, hint=0.0):
     depth, width = weight.shape
     width = width // shares
     return pl.pallas_call(
-        functools.partial(mask_kernel, len(after)),
+        functools.partial(mask_kernel, share, len(after)),
         grid_spec=pltpu.PrefetchScalarGridSpec(
             num_scalar_prefetch=1,
             grid=(depth // rows,),
             in_specs=[
-                pl.BlockSpec((rows, width), lambda i, core: (i, core[0] if shares > 1 else 0)),
+                pl.BlockSpec((rows, width), lambda i, core: (i, share(core[0]))),
                 pl.BlockSpec(mask.shape, lambda i, core: (0, 0)),
             ]
             + [ANYWHERE] * len(after),
@@ -90,29 +94,45 @@
         ),
         out_shape=[jax.ShapeDtypeStruct((depth, width), weight.dtype), TOKEN],
         compiler_params=params("arbitrary"),
-        cost_estimate=cost(0, 4 * depth * width),
+        cost_estimate=as_if(hint),
         name="masked",
     )(core, pltpu.with_memory_space_constraint(weight, pltpu.HBM), mask, *after)
 
 
-def assemble_kernel(after_count, *refs):
-    block_refs, (mine_ref, token_ref) = refs[: -2 - after_count], refs[-2:]
+def stack_kernel(after_count, *refs):
+    block_refs, (stacked_ref, token_ref) = refs[: -2 - after_count], refs[-2:]
     token_ref[...] = jnp.zeros_like(token_ref)
-    rows = jnp.concatenate([block_ref[...].astype(F32) for block_ref in block_refs], 0)
-    mine_ref[...] = rows.astype(BF16)
-
-
-def assemble(blocks, after):
-    shape = (sum(block.shape[0] for block in blocks), blocks[0].shape[1])
+    for number, block_ref in enumerate(block_refs):
+        stacked_ref[number // stacked_ref.shape[1], number % stacked_ref.shape[1]] = block_ref[...]
+
+
+def join_kernel(after_count, *refs):
+    stacked_refs, (joined_ref, token_ref) = refs[: -2 - after_count], refs[-2:]
+    token_ref[...] = jnp.zeros_like(token_ref)
+    blocks = [ref[core, chip] for core in range(CORES) for ref in stacked_refs for chip in range(ref.shape[1])]
+    joined_ref[...] = jnp.concatenate([block.astype(F32) for block in blocks], 0).astype(BF16)
+
+
+def rearranged(kernel, name, shape, blocks, after):
     return pl.pallas_call(
-        functools.partial(assemble_kernel, len(after)),
+        functools.partial(kernel, len(after)),
         in_specs=[INSIDE] * len(blocks) + [ANYWHERE] * len(after),
         out_specs=[INSIDE] * 2,
         out_shape=[jax.ShapeDtypeStruct(shape, BF16), TOKEN],
         compiler_params=pltpu.CompilerParams(vmem_limit_bytes=VMEM // 2),
         cost_estimate=cost(0, 1000000),
-        name="assemble",
+        name=name,
     )(*blocks, *after)
+
+
+def stack(blocks, after):
+    shape = (CORES, len(blocks) // CORES, *blocks[0].shape)
+    return rearranged(stack_kernel, "stack", shape, blocks, after)
+
+
+def join(stacks, after):
+    rows = sum(part.shape[1] for part in stacks) * CORES * stacks[0].shape[2]
+    return rearranged(join_kernel, "join", (rows, stacks[0].shape[3]), stacks, after)
 
 
 def resident(values):
@@ -143,7 +163,7 @@
             far_ref[place, :, :, :, columns] = total[1, :, 1:]
 
 
-def gate_up(parts, gate_kept, up_kept, chips, far_parts, after):
+def gate_up(parts, gate_kept, up_kept, chips, far_parts, hint, after):
     rows = sum(part.shape[0] for part in parts)
     depth, width = gate_kept.shape
     groups, own = len(parts), rows // (2 * len(parts) * chips)
@@ -156,46 +176,54 @@
         out_shape=[jax.ShapeDtypeStruct(shape, BF16) for shape in shapes] + [TOKEN],
         scratch_shapes=[pltpu.VMEM((rows, depth), BF16)],
         compiler_params=pltpu.CompilerParams(vmem_limit_bytes=VMEM // 2),
-        cost_estimate=cost(HURRY * 4 * rows * depth * width, 0),
+        cost_estimate=cost(hint * 4 * rows * depth * width, 0),
         name="gate_up",
     )(*parts, resident(gate_kept), resident(up_kept), *after)
 
 
-def down_kernel(pieces, after_count, own_ref, other_ref, weight_ref, *refs):
+def down_kernel(pieces, weight_count, after_count, own_ref, other_ref, *refs):
+    weight_refs, refs = refs[:weight_count], refs[weight_count:]
     *partial_refs, token_ref, both = refs[after_count:]
     token_ref[...] = jnp.zeros_like(token_ref)
     groups, own, depth = own_ref.shape
     rows = groups * own
     both[:rows, :] = own_ref[...].astype(F32).reshape(rows, depth).astype(BF16)
     both[rows:, :] = other_ref[...].astype(F32).reshape(rows, depth).astype(BF16)
-    tile = tile_of(weight_ref.shape[1], 512)
+    for number, weight_ref in enumerate(weight_refs):
+        width = weight_ref.shape[1]
+        down_columns(pieces, both, weight_ref, partial_refs, number * width, tile_of(width, 512))
+
+
+def down_columns(pieces, both, weight_ref, partial_refs, first, tile):
+    own = partial_refs[0].shape[1]
 
     @pl.loop(0, weight_ref.shape[1] // tile)
     def _(number):
-        columns = pl.ds(pl.multiple_of(number * tile, tile), tile)
-        total = jnp.dot(both[...], weight_ref[:, columns], preferred_element_type=F32)
-        total = total.reshape(pieces, CORES // pieces, groups, own, tile)
+        start = pl.multiple_of(number * tile, tile)
+        total = jnp.dot(both[...], weight_ref[:, pl.ds(start, tile)], preferred_element_type=F32)
+        total = total.reshape(pieces, CORES // pieces, len(partial_refs) // pieces, own, tile)
+        columns = pl.ds(pl.multiple_of(first + start, tile), tile)
         for place, partial_ref in enumerate(partial_refs):
             partial_ref[:, :, columns] = total[place % pieces, :, place // pieces].astype(BF16)
 
 
 def down(own, other, down_kept, pieces, after):
     groups, rows, depth = own.shape
-    width = down_kept.shape[1]
+    width = sum(weight.shape[1] for weight in down_kept)
     shape = (CORES // pieces, rows, width)
     return pl.pallas_call(
-        functools.partial(down_kernel, pieces, len(after)),
-        in_specs=[INSIDE] * 3 + [ANYWHERE] * len(after),
+        functools.partial(down_kernel, pieces, len(down_kept), len(after)),
+        in_specs=[INSIDE] * (2 + len(down_kept)) + [ANYWHERE] * len(after),
         out_specs=[INSIDE] * (groups * pieces + 1),
         out_shape=[jax.ShapeDtypeStruct(shape, BF16)] * (groups * pieces) + [TOKEN],
         scratch_shapes=[pltpu.VMEM((CORES * groups * rows, depth), BF16)],
         compiler_params=pltpu.CompilerParams(vmem_limit_bytes=VMEM // 2),
         cost_estimate=cost(2 * CORES * groups * rows * depth * width, 0),
         name="down",
-    )(own, other, resident(down_kept), *after)
-
-
-def sums_kernel(sizes, first_core, after_count, *refs):
+    )(own, other, *(resident(weight) for weight in down_kept), *after)
+
+
+def sums_kernel(sizes, after_count, *refs):
     to_chips, to_hidden, *to_rows = sizes
     refs = list(refs)
     refs.pop()[...] = jnp.zeros(TOKEN.shape, F32)
@@ -224,15 +252,15 @@
             hidden_ref[group] = (jax.nn.silu(both[0]) * both[1]).astype(BF16)
     for part_refs in ins[2:]:
         summed_ref = refs.pop(0)
-        for core in range(summed_ref.shape[0]):
-            places = [core + first_core * (part_ref.shape[0] > summed_ref.shape[0]) for part_ref in part_refs]
-            total = part_refs[0][places[0]].astype(F32)
-            for part_ref, place in zip(part_refs[1:], places[1:]):
-                total = total + part_ref[place].astype(F32)
+        cores = summed_ref.shape[0]
+        for core in range(cores):
+            total = part_refs[0][core].astype(F32)
+            for part_ref in part_refs[1:]:
+                total = total + part_ref[part_ref.shape[0] - cores + core].astype(F32)
             summed_ref[core] = total.astype(BF16)
 
 
-def sums(to_chips, to_hidden, to_rows, first_core, after):
+def sums(to_chips, to_hidden, to_rows, after, hint=0.0):
     shapes = []
     if to_chips:
         two, groups, chips, own, width = to_chips[0].shape
@@ -244,12 +272,12 @@
     sizes = tuple(len(parts) for parts in given)
     given = [part for parts in given for part in parts]
     results = list(pl.pallas_call(
-        functools.partial(sums_kernel, sizes, first_core, len(after)),
+        functools.partial(sums_kernel, sizes, len(after)),
         in_specs=[INSIDE] * len(given) + [ANYWHERE] * len(after),
         out_specs=[INSIDE] * (len(shapes) + 1),
         out_shape=[jax.ShapeDtypeStruct(shape, BF16) for shape in shapes] + [TOKEN],
         compiler_params=pltpu.CompilerParams(vmem_limit_bytes=VMEM // 2),
-        cost_estimate=cost(0, 4000000),
+        cost_estimate=as_if(hint),
         name="sums",
     )(*given, *after))
     token = results.pop()
@@ -271,12 +299,15 @@
     place = jnp.reshape(core, (1,)).astype(jnp.int32)
 
     normed = rms_normed(tokens, norm_gain)
-    blocks = []
-    for step in [chip * CORES + other for other in range(CORES) for chip in range(chips)]:
-        block = lax.dynamic_slice_in_dim(normed, (row ^ step) * features, features, 1)
-        blocks.append(swap(block, "rows", row_count, step) if step else block)
-    gate_kept, token = masked(gate_weight, gate_mask, tile_of(features, 256), place, 1, [normed])
-    mine, token = assemble(blocks, [token])
+    def block(step):
+        values = lax.dynamic_slice_in_dim(normed, (row ^ step) * features, features, 1)
+        return swap(values, "rows", row_count, step) if step else values
+
+    first, token = stack([block(core_step) for core_step in range(CORES)], [])
+    gate_kept, token = masked(gate_weight, gate_mask, tile_of(features, 256), place, 1, lambda core: 0, [token])
+    second = [block(chip * CORES + core_step) for core_step in range(CORES) for chip in range(1, chips)]
+    second, token = stack(second, [token])
+    mine, token = join([first, second], [token])
 
     def behind(values, after):
         return lax.optimization_barrier((values, *after))[0] if after else values
@@ -302,9 +333,9 @@
         for step in range(1, per_plane):
             parts[plane].append(by_row_of_plane(values, step, after))
 
-    def multiply_in(plane, far_parts=1, after=()):
+    def multiply_in(plane, far_parts=1, hint=HURRY, after=()):
         parts_after = last + list(after)
-        *halves[plane], last[0] = gate_up(parts[plane], gate_kept, up_kept, chips, far_parts, parts_after)
+        *halves[plane], last[0] = gate_up(parts[plane], gate_kept, up_kept, chips, far_parts, hint, parts_after)
 
     def exchange(plane, after=()):
         far[plane] = [by_core(part, after) for part in halves[plane][2:]]
@@ -315,38 +346,46 @@
     def multiply_out(plane, pieces=1):
         *partials[plane], last[0] = down(hiddens[plane], others[plane], down_kept, pieces, last)
 
-    def send_rows(plane, after=(), pieces=1):
-        for piece in reversed(range(pieces)):
-            mine_and_others = partials[plane][piece::pieces]
-            rows_in[plane, piece] = mine_and_others[:1]
-            for step in range(1, per_plane):
-                rows_in[plane, piece].append(by_row_of_plane(mine_and_others[step], step, after))
-            after = rows_in[plane, piece][1:]
+    def send_rows(plane, after=(), pieces=1, piece=0):
+        mine_and_others = partials[plane][piece::pieces]
+        rows_in[plane, piece] = mine_and_others[:1]
+        for step in range(1, per_plane):
+            rows_in[plane, piece].append(by_row_of_plane(mine_and_others[step], step, after))
 
     def to_chips(plane, after=()):
         given = [halves[plane][0], *far[plane]]
-        sent[plane], _, _, last[0] = sums(given, [], [], 0, last + list(after))
+        sent[plane], _, _, last[0] = sums(given, [], [], last + list(after))
 
     def send_chips(plane, after=()):
         chip_sums[plane] = [by_chip(part, number + 1, after) for number, part in enumerate(sent[plane])]
 
-    def to_hidden(plane):
-        _, hiddens[plane], _, last[0] = sums([], [halves[plane][0], near[plane], *chip_sums[plane]], [], 0, last)
+    def to_hidden(plane, after=()):
+        given = [halves[plane][0], near[plane], *chip_sums[plane]]
+        _, hiddens[plane], _, last[0] = sums([], given, [], last + list(after))
         others[plane] = by_core(hiddens[plane])
 
-    def to_rows(*parts, first_core=0, after=()):
-        _, _, (summed,), last[0] = sums([], [], [parts], first_core, last + list(after))
+    def to_rows(*parts, after=(), hint=0.0):
+        _, _, (summed,), last[0] = sums([], [], [parts], last + list(after), hint)
         return summed
 
-    one_away = by_plane(mine, NEXT)
+    next_stacks = [by_plane(first, NEXT), by_plane(second, NEXT)]
     inner_three = by_plane(mine, ACROSS)
     forward(0, mine)
-    up_kept, last[0] = masked(up_weight, up_mask, tile_of(features, 256), place, 1, last)
-    down_kept, last[0] = masked(down_weight, down_mask, 2 * BLOCK, place, CORES, last)
-    inner_two = by_plane(one_away, ACROSS, last)
-    outer_two = by_plane(inner_three, OUTWARD, last)
-    forward(1, one_away, [*parts[0][1:], *last])
-    multiply_in(0, after=[one_away, inner_three])
+    up_kept, last[0] = masked(
+        up_weight, up_mask, tile_of(features, 256), place, 1, lambda core: 0, last + next_stacks[:1], 0.15
+    )
+    one_away, last[0] = join(next_stacks, last)
+    inner_two = by_plane(one_away, ACROSS)
+    down_kept = []
+    for share in range(2):
+        part, last[0] = masked(
+            down_weight, down_mask, 2 * BLOCK, place, 2 * CORES, lambda core, share=share: 2 * core + share, last, 8 - 8 * share
+        )
+        down_kept.append(part)
+        if share == 0:
+            forward(1, one_away, [*parts[0][1:], *last])
+            outer_two = by_plane(inner_three, OUTWARD, last)
+    multiply_in(0, hint=0)
     exchange(0, [inner_two, outer_two])
     exchange_near(0, [inner_two, outer_two])
     outer_three = by_plane(inner_two, OUTWARD, last)
@@ -372,29 +411,35 @@
     to_chips(3)
     send_chips(3)
     exchange_near(3, last)
-    multiply_out(2)
-    send_rows(2, rows_in[1, 0][1:])
+    multiply_out(2, pieces=CORES)
+    send_rows(2, rows_in[1, 0][1:], CORES, 1)
     one = to_rows(*rows_in[1, 0])
     one_out = by_plane(one, NEXT)
+    two = to_rows(*rows_in[2, 1])
+    send_rows(2, [two], CORES, 0)
+    two_out, three_out = {1: by_plane(two, NEXT)}, {}
     to_hidden(3)
+    send_chips(0, chip_sums[3])
     multiply_out(3, pieces=CORES)
-    send_chips(0, chip_sums[3])
-    send_rows(3, rows_in[2, 0][1:], pieces=CORES)
     two = to_rows(*rows_in[2, 0], after=[one_out])
-    two_out = by_plane(two, NEXT)
-    to_hidden(0)
+    two_out[0] = by_plane(two, NEXT)
+    send_rows(3, [two], CORES, 1)
+    three = to_rows(*rows_in[3, 1], two_out[1])
+    three_out[1] = by_plane(three, MIRROR)
+    send_rows(3, [three], CORES, 0)
+    to_hidden(0, [two_out[0]])
     multiply_out(0)
-    three_out = {}
-    for piece in reversed(range(CORES)):
-        three = to_rows(*rows_in[3, piece], two_out, first_core=piece)
-        three_out[piece] = by_plane(three, MIRROR)
+    three = to_rows(*rows_in[3, 0], two_out[0])
+    three_out[0] = by_plane(three, MIRROR)
     send_rows(0, rows_in[3, 0][1:])
 
-    def total(piece):
-        whole = [part[piece].astype(F32) for part in (*rows_in[0, 0], one_out)]
-        return (sum(whole[1:], whole[0]) + three_out[piece][0].astype(F32)).astype(BF16)
-
-    mine_now, other = total(0), by_core(total(1))
+    joined = to_rows(three_out[1], one_out, hint=10.0)
+
+    def total(piece, *parts):
+        whole = [part[piece].astype(F32) for part in rows_in[0, 0]] + [part.astype(F32) for part in parts]
+        return sum(whole[1:], whole[0]).astype(BF16)
+
+    mine_now, other = total(0, one_out[0], three_out[0][0]), by_core(total(1, joined[0]))
     left = jnp.where(core == 0, mine_now, other)
     right = jnp.where(core == 0, other, mine_now)
     return jnp.concatenate([left, right], 1)

time: 170 us -> 164 us (0.965)
  the two profiles are of different devices: /device:TPU:8 before, /device:TPU:0 now
where the time goes in v7:
time: 164 us
  Pallas kernels  70.7 us (43%)
  waiting for transfers between devices  47.1 us (29%)
  starting transfers between devices  41.1 us (25%)
  other arithmetic  4.29 us (3%)
    ppermute x31, waiting for transfers between devices, swap(): lax.ppermute(values, axis, [(place, place ^ step) for place in range(size)])  30.6 us
    pallas_call x4, Pallas kernels, masked(): pl.pallas_call(functools.partial(mask_kernel, share, len(after)), grid_sp...  27.9 us
    pallas_call x4, Pallas kernels, gate_up(): pl.pallas_call(functools.partial(gate_up_kernel, len(parts), len(after)),...  24.3 us
    ppermute x31, starting transfers between devices, swap(): lax.ppermute(values, axis, [(place, place ^ step) for place in range(size)])  22.2 us
    ppermute x11, starting transfers between devices, by_plane(): return lax.ppermute(behind(values, after), 'cols', pairs)  18.8 us
    ppermute x11, waiting for transfers between devices, by_plane(): return lax.ppermute(behind(values, after), 'cols', pairs)  16.5 us
    pallas_call x4, Pallas kernels, down(): pl.pallas_call(functools.partial(down_kernel, pieces, len(down_kept), len...  15.5 us
  transfers between devices with their start and end apart: 42, of which 20 were waited for; matrix products, arithmetic and copies ran while one was open for 0% of the time, Pallas kernels for 43%

profile of v7, /device:TPU:0, one launch (start us, length us, event | category | flops | bytes accessed | tf_op | source)
XLA Modules:
  0.0 163.7 jit_solution(4568931103966320552)
XLA Ops:
  0.0 1.3 fusion
  1.4 1.3 fusion.2
  3.3 2.6 %collective-permute-start.1 = (bf16[40,2048]{1,0:T(8,128)(2,1)S(1)}, bf16[40,2048]{1,0:T(8,128)(2,1)S(1)}, u32[]{:S(2)}, u32[]{:S(2)}) collective-permute-start(bf16[40,2048]{1,0:T(8,128)(2,1)S(1)} %get-tuple-element.192), channel_id=1, source_target_pairs={{0,16},{8,24},{16,0},{24,8},{1,17},{9,25},{17,1},{25,9},{2,18},{10... | collective-permute-start | bytes 491528 | tf_op jit(solution)/shard_map/ppermute | solution.py:290
  5.9 1.9 %collective-permute-start.4 = (bf16[2,1,40,2048]{3,2,1,0:T(8,128)(2,1)S(1)}, bf16[2,1,40,2048]{3,2,1,0:T(8,128)(2,1)S(1)}, u32[]{:S(2)}, u32[]{:S(2)}) collective-permute-start(bf16[2,1,40,2048]{3,2,1,0:T(8,128)(2,1)S(1)} %get-tuple-element.97.refs_0_), channel_id=1, source_target_pairs={{0,2},{1,3},{2,0},{3,1},{4,6},{5,7},{6,4},{7,5},{8,10},{9,11},{10,... | collective-permute-start | bytes 983048 | tf_op jit(solution)/shard_map/ppermute | solution.py:317
  7.8 5.6 %masked.4 = (bf16[2048,1792]{1,0:T(8,128)(2,1)S(1)}, f32[8,128]{1,0:T(8,128)S(1)}) custom-call(s32[1]{0:T(128)} %bitcast.core_ref, bf16[2048,1792]{1,0:T(8,128)(2,1)} %weight_ref.4, s32[32,28]{1,0:T(8,128)S(1)} %copy-done, f32[8,128]{1,0:T(8,128)S(1)} %get-tuple-element.98.refs_0_), custom_call_target="tpu_custom_call" | custom-call | tf_op jit(solution)/shard_map/masked/pallas_call | solution.py:79
  13.9 1.7 %collective-permute-start.5 = (bf16[2,1,40,2048]{3,2,1,0:T(8,128)(2,1)S(1)}, bf16[2,1,40,2048]{3,2,1,0:T(8,128)(2,1)S(1)}, u32[]{:S(2)}, u32[]{:S(2)}) collective-permute-start(bf16[2,1,40,2048]{3,2,1,0:T(8,128)(2,1)S(1)} %get-tuple-element.100.refs_1_), channel_id=1, source_target_pairs={{0,2},{1,3},{2,0},{3,1},{4,6},{5,7},{6,4},{7,5},{8,10},{9,11},{10,... | collective-permute-start | bytes 983048 | tf_op jit(solution)/shard_map/ppermute | solution.py:317
  16.4 1.6 collective-permute-start.3
  18.0 5.7 %masked.5 = (bf16[2048,1792]{1,0:T(8,128)(2,1)S(1)}, f32[8,128]{1,0:T(8,128)S(1)}) custom-call(s32[1]{0:T(128)} %bitcast.core_ref, bf16[2048,1792]{1,0:T(8,128)(2,1)} %weight_ref.5, s32[32,28]{1,0:T(8,128)S(1)} %copy-done.1, f32[8,128]{1,0:T(8,128)S(1)} %get-tuple-element.104.refs_0_, bf16[2,1,40,2048]{3,2,1,0:T(8,128)(2,1)S(1)} %collective-permute-done.4.refs_1_.refs_0_), custom_call_target="tpu_custom_call" | custom-call | flops 172500000 | tf_op jit(solution)/shard_map/masked/pallas_call | solution.py:79
  24.8 8.3 %masked.6 = (bf16[1792,2048]{1,0:T(8,128)(2,1)S(1)}, f32[8,128]{1,0:T(8,128)S(1)}) custom-call(s32[1]{0:T(128)} %bitcast.core_ref, bf16[1792,8192]{1,0:T(8,128)(2,1)} %weight_ref.7, s32[28,128]{1,0:T(8,128)S(1)} %copy-done.2, f32[8,128]{1,0:T(8,128)S(1)} %get-tuple-element.107.refs_0_), custom_call_target="tpu_custom_call" | custom-call | flops 9200000000 | tf_op jit(solution)/shard_map/masked/pallas_call | solution.py:79
  33.1 1.3 collective-permute-start.8
  34.4 1.7 %collective-permute-start.12 = (bf16[160,2048]{1,0:T(8,128)(2,1)S(1)}, bf16[160,2048]{1,0:T(8,128)(2,1)S(1)}, u32[]{:S(2)}, u32[]{:S(2)}) collective-permute-start(bf16[160,2048]{1,0:T(8,128)(2,1)S(1)} %get-tuple-element.120.refs_0_), channel_id=1, source_target_pairs={{0,1},{1,0},{2,3},{3,2},{4,5},{5,4},{6,7},{7,6},{8,9},{9,8},{10,11... | collective-permute-start | bytes 1966088 | tf_op jit(solution)/shard_map/ppermute | solution.py:290
  36.2 8.3 %masked.7 = (bf16[1792,2048]{1,0:T(8,128)(2,1)S(1)}, f32[8,128]{1,0:T(8,128)S(1)}) custom-call(s32[1]{0:T(128)} %bitcast.core_ref, bf16[1792,8192]{1,0:T(8,128)(2,1)} %weight_ref.7, s32[28,128]{1,0:T(8,128)S(1)} %copy-done.2, f32[8,128]{1,0:T(8,128)S(1)} %get-tuple-element.108.refs_0_), custom_call_target="tpu_custom_call" | custom-call | tf_op jit(solution)/shard_map/masked/pallas_call | solution.py:79
  44.5 6.1 %gate_up.4 = (bf16[2,2,2,40,1792]{4,3,2,1,0:T(8,128)(2,1)S(1)}, bf16[2,2,40,1792]{3,2,1,0:T(8,128)(2,1)S(1)}, bf16[2,2,1,40,1792]{4,3,2,1,0:T(8,128)(2,1)S(1)}, f32[8,128]{1,0:T(8,128)S(1)}) custom-call(bf16[160,2048]{1,0:T(8,128)(2,1)S(1)} %get-tuple-element.102.refs_0_, bf16[160,2048]{1,0:T(8,128)(2,1)S(1)} %collective-permute-done.3.refs_1_, ...), custom_call_target="tpu_custom_call" | custom-call | tf_op jit(solution)/shard_map/gate_up/pallas_call | solution.py:172
  50.6 3.6 %collective-permute-done.8 = bf16[160,2048]{1,0:T(8,128)(2,1)S(1)} collective-permute-done((bf16[160,2048]{1,0:T(8,128)(2,1)S(1)}, bf16[160,2048]{1,0:T(8,128)(2,1)S(1)}, u32[]{:S(2)}, u32[]{:S(2)}) %collective-permute-start.8) | collective-permute-done | bytes 655392 | tf_op jit(solution)/shard_map/ppermute | solution.py:317
  54.7 1.5 collective-permute-start.11
  57.3 6.1 %gate_up.5 = (bf16[2,2,2,40,1792]{4,3,2,1,0:T(8,128)(2,1)S(1)}, bf16[2,2,40,1792]{3,2,1,0:T(8,128)(2,1)S(1)}, bf16[2,2,1,40,1792]{4,3,2,1,0:T(8,128)(2,1)S(1)}, f32[8,128]{1,0:T(8,128)S(1)}) custom-call(bf16[160,2048]{1,0:T(8,128)(2,1)S(1)} %get-tuple-element.120.refs_0_, bf16[160,2048]{1,0:T(8,128)(2,1)S(1)} %collective-permute-done.12.refs_1_, ...), custom_call_target="tpu_custom_call" | custom-call | flops 4697620480 | tf_op jit(solution)/shard_map/gate_up/pallas_call | solution.py:172
  64.0 1.5 collective-permute-done.13.refs_1_
  65.4 0.8 collective-permute-done.14.refs_3_.refs_1_
  66.4 1.6 collective-permute-start.17
  68.0 5.3 %collective-permute-done.11.refs_5_ = bf16[160,2048]{1,0:T(8,128)(2,1)S(1)} collective-permute-done((bf16[160,2048]{1,0:T(8,128)(2,1)S(1)}, bf16[160,2048]{1,0:T(8,128)(2,1)S(1)}, u32[]{:S(2)}, u32[]{:S(2)}) %collective-permute-start.11) | collective-permute-done | bytes 655392 | tf_op jit(solution)/shard_map/ppermute | solution.py:317
  74.2 6.1 %gate_up.6 = (bf16[2,2,2,40,1792]{4,3,2,1,0:T(8,128)(2,1)S(1)}, bf16[2,2,40,1792]{3,2,1,0:T(8,128)(2,1)S(1)}, bf16[2,2,1,40,1792]{4,3,2,1,0:T(8,128)(2,1)S(1)}, f32[8,128]{1,0:T(8,128)S(1)}) custom-call(bf16[160,2048]{1,0:T(8,128)(2,1)S(1)} %add.63.refs_0_, bf16[160,2048]{1,0:T(8,128)(2,1)S(1)} %collective-permute-done.15.refs_1_, ...), custom_call_target="tpu_custom_call" | custom-call | flops 4697620480 | tf_op jit(solution)/shard_map/gate_up/pallas_call | solution.py:172
  82.3 0.8 collective-permute-done.20.refs_3_.refs_1_
  83.3 1.6 collective-permute-start.23
  84.8 3.9 %down.4 = (bf16[2,40,4096]{2,1,0:T(8,128)(2,1)S(1)}, bf16[2,40,4096]{2,1,0:T(8,128)(2,1)S(1)}, f32[8,128]{1,0:T(8,128)S(1)}) custom-call(bf16[2,40,1792]{2,1,0:T(8,128)(2,1)S(1)} %get-tuple-element.132.own_ref, bf16[2,40,1792]{2,1,0:T(8,128)(2,1)S(1)} %collective-permute-done.18.other_ref, bf16[1792,2048]{1,0:T(8,128)(2,1)S(1)} %get-tuple-element.133.refs_0_, ...), custom_call_target="tpu_custom_call" | custom-call | flops 2348810 | tf_op jit(solution)/shard_map/down/pallas_call | solution.py:214
  89.3 0.9 collective-permute-start.28
  90.2 6.1 %gate_up.7 = (bf16[2,2,2,40,1792]{4,3,2,1,0:T(8,128)(2,1)S(1)}, bf16[2,2,40,1792]{3,2,1,0:T(8,128)(2,1)S(1)}, bf16[1,2,1,40,1792]{4,3,2,1,0:T(8,128)(2,1)S(1)}, ...) custom-call(bf16[160,2048]{1,0:T(8,128)(2,1)S(1)} %add.62.refs_0_, ...), custom_call_target="tpu_custom_call" | custom-call | flops 4697620480 | tf_op jit(solution)/shard_map/gate_up/pallas_call | solution.py:172
  96.8 1.5 collective-permute-done.23.refs_2_
  98.9 1.6 collective-permute-start.24
  100.7 3.9 %down.5 = (bf16[1,40,4096]{2,1,0:T(8,128)(2,1)S(1)}, bf16[1,40,4096]{2,1,0:T(8,128)(2,1)S(1)}, bf16[1,40,4096]{2,1,0:T(8,128)(2,1)S(1)}, bf16[1,40,4096]{2,1,0:T(8,128)(2,1)S(1)}, f32[8,128]{1,0:T(8,128)S(1)}) custom-call(bf16[2,40,1792]{2,1,0:T(8,128)(2,1)S(1)} %get-tuple-element.152.own_ref, bf16[2,40,1792]{2,1,0:T(8,128)(2,1)S(1)} %collective-permute-done.27.other_ref, ...), custom_call_target="tpu_custom_call" | custom-call | flops 2348810 | tf_op jit(solution)/shard_map/down/pallas_call | solution.py:214
  105.3 1.3 collective-permute-start.29
  106.8 2.1 %collective-permute-start.32 = (bf16[2,40,4096]{2,1,0:T(8,128)(2,1)S(1)}, bf16[2,40,4096]{2,1,0:T(8,128)(2,1)S(1)}, u32[]{:S(2)}, u32[]{:S(2)}) collective-permute-start(bf16[2,40,4096]{2,1,0:T(8,128)(2,1)S(1)} %get-tuple-element.171), channel_id=1, source_target_pairs={{0,2},{1,3},{2,0},{3,1},{4,6},{5,7},{6,4},{7,5},{8,10},{9,11},{10,... | collective-permute-start | bytes 1966088 | tf_op jit(solution)/shard_map/ppermute | solution.py:317
  108.9 5.7 %collective-permute-done.29.refs_1_ = bf16[1,40,4096]{2,1,0:T(8,128)(2,1)S(1)} collective-permute-done((bf16[1,40,4096]{2,1,0:T(8,128)(2,1)S(1)}, bf16[1,40,4096]{2,1,0:T(8,128)(2,1)S(1)}, u32[]{:S(2)}, u32[]{:S(2)}) %collective-permute-start.29) | collective-permute-done | bytes 327712 | tf_op jit(solution)/shard_map/ppermute | solution.py:290
  114.6 1.4 collective-permute-start.31
  116.4 1.0 collective-permute-start.25
  117.4 2.0 %collective-permute-start.34 = (bf16[1,40,4096]{2,1,0:T(8,128)(2,1)S(1)}, bf16[1,40,4096]{2,1,0:T(8,128)(2,1)S(1)}, u32[]{:S(2)}, u32[]{:S(2)}) collective-permute-start(bf16[1,40,4096]{2,1,0:T(8,128)(2,1)S(1)} %get-tuple-element.168), channel_id=1, source_target_pairs={{0,2},{1,3},{2,0},{3,1},{4,6},{5,7},{6,4},{7,5},{8,10},{9,11},{10,... | collective-permute-start | bytes 983048 | tf_op jit(solution)/shard_map/ppermute | solution.py:317
  119.4 3.9 %down.6 = (bf16[1,40,4096]{2,1,0:T(8,128)(2,1)S(1)}, bf16[1,40,4096]{2,1,0:T(8,128)(2,1)S(1)}, bf16[1,40,4096]{2,1,0:T(8,128)(2,1)S(1)}, bf16[1,40,4096]{2,1,0:T(8,128)(2,1)S(1)}, f32[8,128]{1,0:T(8,128)S(1)}) custom-call(bf16[2,40,1792]{2,1,0:T(8,128)(2,1)S(1)} %get-tuple-element.162.own_ref, bf16[2,40,1792]{2,1,0:T(8,128)(2,1)S(1)} %collective-permute-done.30.other_ref, ...), custom_call_target="tpu_custom_call" | custom-call | flops 2348810 | tf_op jit(solution)/shard_map/down/pallas_call | solution.py:214
  123.3 1.2 collective-permute-done.32.refs_3_.refs_1_
  125.3 2.0 %collective-permute-start.35 = (bf16[1,40,4096]{2,1,0:T(8,128)(2,1)S(1)}, bf16[1,40,4096]{2,1,0:T(8,128)(2,1)S(1)}, u32[]{:S(2)}, u32[]{:S(2)}) collective-permute-start(bf16[1,40,4096]{2,1,0:T(8,128)(2,1)S(1)} %get-tuple-element.172), channel_id=1, source_target_pairs={{0,2},{1,3},{2,0},{3,1},{4,6},{5,7},{6,4},{7,5},{8,10},{9,11},{10,... | collective-permute-start | bytes 983048 | tf_op jit(solution)/shard_map/ppermute | solution.py:317
  127.3 4.2 %collective-permute-done.34.refs_2_ = bf16[1,40,4096]{2,1,0:T(8,128)(2,1)S(1)} collective-permute-done((bf16[1,40,4096]{2,1,0:T(8,128)(2,1)S(1)}, bf16[1,40,4096]{2,1,0:T(8,128)(2,1)S(1)}, u32[]{:S(2)}, u32[]{:S(2)}) %collective-permute-start.34) | collective-permute-done | bytes 327712 | tf_op jit(solution)/shard_map/ppermute | solution.py:317
  131.5 1.4 collective-permute-done.33.refs_1_
  133.8 2.5 %collective-permute-start.40 = (bf16[1,40,4096]{2,1,0:T(8,128)(2,1)S(1)}, bf16[1,40,4096]{2,1,0:T(8,128)(2,1)S(1)}, u32[]{:S(2)}, u32[]{:S(2)}) collective-permute-start(bf16[1,40,4096]{2,1,0:T(8,128)(2,1)S(1)} %get-tuple-element.181), channel_id=1, source_target_pairs={{0,6},{1,7},{6,0},{7,1},{2,4},{3,5},{4,2},{5,3},{8,14},{9,15},{14,... | collective-permute-start | bytes 983048 | tf_op jit(solution)/shard_map/ppermute | solution.py:317
  136.3 1.8 %collective-permute-done.35.refs_4_.refs_2_ = bf16[1,40,4096]{2,1,0:T(8,128)(2,1)S(1)} collective-permute-done((bf16[1,40,4096]{2,1,0:T(8,128)(2,1)S(1)}, bf16[1,40,4096]{2,1,0:T(8,128)(2,1)S(1)}, u32[]{:S(2)}, u32[]{:S(2)}) %collective-permute-start.35) | collective-permute-done | bytes 327712 | tf_op jit(solution)/shard_map/ppermute | solution.py:317
  138.5 1.6 collective-permute-done.36.other_ref
  140.0 3.9 %down.7 = (bf16[2,40,4096]{2,1,0:T(8,128)(2,1)S(1)}, bf16[2,40,4096]{2,1,0:T(8,128)(2,1)S(1)}, f32[8,128]{1,0:T(8,128)S(1)}) custom-call(bf16[2,40,1792]{2,1,0:T(8,128)(2,1)S(1)} %get-tuple-element.176.own_ref, bf16[2,40,1792]{2,1,0:T(8,128)(2,1)S(1)} %collective-permute-done.36.other_ref, bf16[1792,2048]{1,0:T(8,128)(2,1)S(1)} %get-tuple-element.133.refs_0_, ...), custom_call_target="tpu_custom_call" | custom-call | flops 2348810 | tf_op jit(solution)/shard_map/down/pallas_call | solution.py:214
  144.7 2.5 %collective-permute-start.39 = (bf16[1,40,4096]{2,1,0:T(8,128)(2,1)S(1)}, bf16[1,40,4096]{2,1,0:T(8,128)(2,1)S(1)}, u32[]{:S(2)}, u32[]{:S(2)}) collective-permute-start(bf16[1,40,4096]{2,1,0:T(8,128)(2,1)S(1)} %get-tuple-element.186), channel_id=1, source_target_pairs={{0,6},{1,7},{6,0},{7,1},{2,4},{3,5},{4,2},{5,3},{8,14},{9,15},{14,... | collective-permute-start | bytes 983048 | tf_op jit(solution)/shard_map/ppermute | solution.py:317
  147.9 12.8 %collective-permute-done.38 = bf16[2,40,4096]{2,1,0:T(8,128)(2,1)S(1)} collective-permute-done((bf16[2,40,4096]{2,1,0:T(8,128)(2,1)S(1)}, bf16[2,40,4096]{2,1,0:T(8,128)(2,1)S(1)}, u32[]{:S(2)}, u32[]{:S(2)}) %collective-permute-start.38) | collective-permute-done | bytes 655392 | tf_op jit(solution)/shard_map/ppermute | solution.py:290
  160.9 1.6 collective-permute-done.41
  162.8 0.9 pad_maximum_fusion
  (82 shorter events, 15.6 us)
Async XLA Ops:
  1.3 6.5 %copy-start = (s32[32,28]{1,0:T(8,128)S(1)}, s32[32,28]{1,0:T(8,128)}, u32[]{:S(2)}) copy-start(s32[32,28]{1,0:T(8,128)} %mask_ref.4) | copy-start | bytes 10756
  2.7 3.2 %collective-permute-start = (bf16[40,2048]{1,0:T(8,128)(2,1)S(1)}, bf16[40,2048]{1,0:T(8,128)(2,1)S(1)}, u32[]{:S(2)}, u32[]{:S(2)}) collective-permute-start(bf16[40,2048]{1,0:T(8,128)(2,1)S(1)} %get-tuple-element.193), channel_id=1, source_target_pairs={{0,8},{8,0},{16,24},{24,16},{1,9},{9,1},{17,25},{25,17},{2,10},{10... | collective-permute-start | bytes 491528 | tf_op jit(solution)/shard_map/ppermute | solution.py:290
  3.3 10.2 %collective-permute-start.1 = (bf16[40,2048]{1,0:T(8,128)(2,1)S(1)}, bf16[40,2048]{1,0:T(8,128)(2,1)S(1)}, u32[]{:S(2)}, u32[]{:S(2)}) collective-permute-start(bf16[40,2048]{1,0:T(8,128)(2,1)S(1)} %get-tuple-element.192), channel_id=1, source_target_pairs={{0,16},{8,24},{16,0},{24,8},{1,17},{9,25},{17,1},{25,9},{2,18},{10... | collective-permute-start | bytes 491528 | tf_op jit(solution)/shard_map/ppermute | solution.py:290
  5.8 8.0 %collective-permute-start.2 = (bf16[40,2048]{1,0:T(8,128)(2,1)S(1)}, bf16[40,2048]{1,0:T(8,128)(2,1)S(1)}, u32[]{:S(2)}, u32[]{:S(2)}) collective-permute-start(bf16[40,2048]{1,0:T(8,128)(2,1)S(1)} %get-tuple-element.191), channel_id=1, source_target_pairs={{0,24},{8,16},{16,8},{24,0},{1,25},{9,17},{17,9},{25,1},{2,26},{10... | collective-permute-start | bytes 491528 | tf_op jit(solution)/shard_map/ppermute | solution.py:290
  5.9 12.0 %collective-permute-start.4 = (bf16[2,1,40,2048]{3,2,1,0:T(8,128)(2,1)S(1)}, bf16[2,1,40,2048]{3,2,1,0:T(8,128)(2,1)S(1)}, u32[]{:S(2)}, u32[]{:S(2)}) collective-permute-start(bf16[2,1,40,2048]{3,2,1,0:T(8,128)(2,1)S(1)} %get-tuple-element.97.refs_0_), channel_id=1, source_target_pairs={{0,2},{1,3},{2,0},{3,1},{4,6},{5,7},{6,4},{7,5},{8,10},{9,11},{10,... | collective-permute-start | bytes 983048 | tf_op jit(solution)/shard_map/ppermute | solution.py:317
  7.8 10.2 %copy-start.1 = (s32[32,28]{1,0:T(8,128)S(1)}, s32[32,28]{1,0:T(8,128)}, u32[]{:S(2)}) copy-start(s32[32,28]{1,0:T(8,128)} %mask_ref.5) | copy-start | bytes 10756
  13.9 10.2 %collective-permute-start.5 = (bf16[2,1,40,2048]{3,2,1,0:T(8,128)(2,1)S(1)}, bf16[2,1,40,2048]{3,2,1,0:T(8,128)(2,1)S(1)}, u32[]{:S(2)}, u32[]{:S(2)}) collective-permute-start(bf16[2,1,40,2048]{3,2,1,0:T(8,128)(2,1)S(1)} %get-tuple-element.100.refs_1_), channel_id=1, source_target_pairs={{0,2},{1,3},{2,0},{3,1},{4,6},{5,7},{6,4},{7,5},{8,10},{9,11},{10,... | collective-permute-start | bytes 983048 | tf_op jit(solution)/shard_map/ppermute | solution.py:317
  15.7 17.5 %collective-permute-start.7 = (bf16[160,2048]{1,0:T(8,128)(2,1)S(1)}, bf16[160,2048]{1,0:T(8,128)(2,1)S(1)}, u32[]{:S(2)}, u32[]{:S(2)}) collective-permute-start(bf16[160,2048]{1,0:T(8,128)(2,1)S(1)} %get-tuple-element.102.refs_0_), channel_id=1, source_target_pairs={{2,4},{3,5},{4,2},{5,3},{10,12},{11,13},{12,10},{13,11},{18,20},{1... | collective-permute-start | bytes 1966088 | tf_op jit(solution)/shard_map/ppermute | solution.py:317
  16.4 18.1 %collective-permute-start.3 = (bf16[160,2048]{1,0:T(8,128)(2,1)S(1)}, bf16[160,2048]{1,0:T(8,128)(2,1)S(1)}, u32[]{:S(2)}, u32[]{:S(2)}) collective-permute-start(bf16[160,2048]{1,0:T(8,128)(2,1)S(1)} %get-tuple-element.102.refs_0_), channel_id=1, source_target_pairs={{0,1},{1,0},{2,3},{3,2},{4,5},{5,4},{6,7},{7,6},{8,9},{9,8},{10,11... | collective-permute-start | bytes 1966088 | tf_op jit(solution)/shard_map/ppermute | solution.py:290
  18.0 6.9 %copy-start.2 = (s32[28,128]{1,0:T(8,128)S(1)}, s32[28,128]{1,0:T(8,128)}, u32[]{:S(2)}) copy-start(s32[28,128]{1,0:T(8,128)} %mask_ref.7) | copy-start | bytes 43012
  24.1 26.5 %collective-permute-start.6 = (bf16[160,2048]{1,0:T(8,128)(2,1)S(1)}, bf16[160,2048]{1,0:T(8,128)(2,1)S(1)}, u32[]{:S(2)}, u32[]{:S(2)}) collective-permute-start(bf16[160,2048]{1,0:T(8,128)(2,1)S(1)} %get-tuple-element.120.refs_0_), channel_id=1, source_target_pairs={{2,4},{3,5},{4,2},{5,3},{10,12},{11,13},{12,10},{13,11},{18,20},{1... | collective-permute-start | bytes 1966088 | tf_op jit(solution)/shard_map/ppermute | solution.py:317
  33.1 21.1 %collective-permute-start.8 = (bf16[160,2048]{1,0:T(8,128)(2,1)S(1)}, bf16[160,2048]{1,0:T(8,128)(2,1)S(1)}, u32[]{:S(2)}, u32[]{:S(2)}) collective-permute-start(bf16[160,2048]{1,0:T(8,128)(2,1)S(1)} %collective-permute-done.7), channel_id=1, source_target_pairs={{2,0},{3,1},{4,6},{5,7},{10,8},{11,9},{12,14},{13,15},{18,16},{19,... | collective-permute-start | bytes 1966088 | tf_op jit(solution)/shard_map/ppermute | solution.py:317
  34.4 21.9 %collective-permute-start.12 = (bf16[160,2048]{1,0:T(8,128)(2,1)S(1)}, bf16[160,2048]{1,0:T(8,128)(2,1)S(1)}, u32[]{:S(2)}, u32[]{:S(2)}) collective-permute-start(bf16[160,2048]{1,0:T(8,128)(2,1)S(1)} %get-tuple-element.120.refs_0_), channel_id=1, source_target_pairs={{0,1},{1,0},{2,3},{3,2},{4,5},{5,4},{6,7},{7,6},{8,9},{9,8},{10,11... | collective-permute-start | bytes 1966088 | tf_op jit(solution)/shard_map/ppermute | solution.py:290
  54.2 2.9 %collective-permute-start.9 = (bf16[2,2,40,1792]{3,2,1,0:T(8,128)(2,1)S(1)}, bf16[2,2,40,1792]{3,2,1,0:T(8,128)(2,1)S(1)}, u32[]{:S(2)}, u32[]{:S(2)}) collective-permute-start(bf16[2,2,40,1792]{3,2,1,0:T(8,128)(2,1)S(1)} %get-tuple-element.114), channel_id=1, source_target_pairs={{0,8},{8,0},{16,24},{24,16},{1,9},{9,1},{17,25},{25,17},{2,10},{10... | collective-permute-start | bytes 1720328 | tf_op jit(solution)/shard_map/ppermute | solution.py:290
  54.2 2.9 %collective-permute-start.10 = (bf16[2,2,1,40,1792]{4,3,2,1,0:T(8,128)(2,1)S(1)}, bf16[2,2,1,40,1792]{4,3,2,1,0:T(8,128)(2,1)S(1)}, u32[]{:S(2)}, u32[]{:S(2)}) collective-permute-start(bf16[2,2,1,40,1792]{4,3,2,1,0:T(8,128)(2,1)S(1)} %get-tuple-element.116), channel_id=1, source_target_pairs={{0,8},{8,0},{16,24},{24,16},{1,9},{9,1},{17,25},{25,17},{2,10},{10... | collective-permute-start | bytes 1720328 | tf_op jit(solution)/shard_map/ppermute | solution.py:290
  54.7 18.5 %collective-permute-start.11 = (bf16[160,2048]{1,0:T(8,128)(2,1)S(1)}, bf16[160,2048]{1,0:T(8,128)(2,1)S(1)}, u32[]{:S(2)}, u32[]{:S(2)}) collective-permute-start(bf16[160,2048]{1,0:T(8,128)(2,1)S(1)} %collective-permute-done.6), channel_id=1, source_target_pairs={{2,0},{3,1},{4,6},{5,7},{10,8},{11,9},{12,14},{13,15},{18,16},{19,... | collective-permute-start | bytes 1966088 | tf_op jit(solution)/shard_map/ppermute | solution.py:317
  56.4 17.0 %collective-permute-start.15 = (bf16[160,2048]{1,0:T(8,128)(2,1)S(1)}, bf16[160,2048]{1,0:T(8,128)(2,1)S(1)}, u32[]{:S(2)}, u32[]{:S(2)}) collective-permute-start(bf16[160,2048]{1,0:T(8,128)(2,1)S(1)} %add.63.refs_0_), channel_id=1, source_target_pairs={{0,1},{1,0},{2,3},{3,2},{4,5},{5,4},{6,7},{7,6},{8,9},{9,8},{10,11... | collective-permute-start | bytes 1966088 | tf_op jit(solution)/shard_map/ppermute | solution.py:290
  63.4 2.0 %collective-permute-start.13 = (bf16[2,2,1,40,1792]{4,3,2,1,0:T(8,128)(2,1)S(1)}, bf16[2,2,1,40,1792]{4,3,2,1,0:T(8,128)(2,1)S(1)}, u32[]{:S(2)}, u32[]{:S(2)}) collective-permute-start(bf16[2,2,1,40,1792]{4,3,2,1,0:T(8,128)(2,1)S(1)} %get-tuple-element.123), channel_id=1, source_target_pairs={{0,8},{8,0},{16,24},{24,16},{1,9},{9,1},{17,25},{25,17},{2,10},{10... | collective-permute-start | bytes 1720328 | tf_op jit(solution)/shard_map/ppermute | solution.py:290
  63.5 2.8 %collective-permute-start.14 = (bf16[2,2,40,1792]{3,2,1,0:T(8,128)(2,1)S(1)}, bf16[2,2,40,1792]{3,2,1,0:T(8,128)(2,1)S(1)}, u32[]{:S(2)}, u32[]{:S(2)}) collective-permute-start(bf16[2,2,40,1792]{3,2,1,0:T(8,128)(2,1)S(1)} %get-tuple-element.125), channel_id=1, source_target_pairs={{0,8},{8,0},{16,24},{24,16},{1,9},{9,1},{17,25},{25,17},{2,10},{10... | collective-permute-start | bytes 1720328 | tf_op jit(solution)/shard_map/ppermute | solution.py:290
  66.4 15.1 %collective-permute-start.17 = (bf16[2,2,40,1792]{3,2,1,0:T(8,128)(2,1)S(1)}, bf16[2,2,40,1792]{3,2,1,0:T(8,128)(2,1)S(1)}, u32[]{:S(2)}, u32[]{:S(2)}) collective-permute-start(bf16[2,2,40,1792]{3,2,1,0:T(8,128)(2,1)S(1)} %get-tuple-element.130), channel_id=1, source_target_pairs={{0,16},{8,24},{16,0},{24,8},{1,17},{9,25},{17,1},{25,9},{2,18},{10... | collective-permute-start | bytes 1720328 | tf_op jit(solution)/shard_map/ppermute | solution.py:290
  73.4 15.9 %collective-permute-start.16 = (bf16[160,2048]{1,0:T(8,128)(2,1)S(1)}, bf16[160,2048]{1,0:T(8,128)(2,1)S(1)}, u32[]{:S(2)}, u32[]{:S(2)}) collective-permute-start(bf16[160,2048]{1,0:T(8,128)(2,1)S(1)} %add.62.refs_0_), channel_id=1, source_target_pairs={{0,1},{1,0},{2,3},{3,2},{4,5},{5,4},{6,7},{7,6},{8,9},{9,8},{10,11... | collective-permute-start | bytes 1966088 | tf_op jit(solution)/shard_map/ppermute | solution.py:290
  80.3 2.0 %collective-permute-start.19 = (bf16[2,2,1,40,1792]{4,3,2,1,0:T(8,128)(2,1)S(1)}, bf16[2,2,1,40,1792]{4,3,2,1,0:T(8,128)(2,1)S(1)}, u32[]{:S(2)}, u32[]{:S(2)}) collective-permute-start(bf16[2,2,1,40,1792]{4,3,2,1,0:T(8,128)(2,1)S(1)} %get-tuple-element.136), channel_id=1, source_target_pairs={{0,8},{8,0},{16,24},{24,16},{1,9},{9,1},{17,25},{25,17},{2,10},{10... | collective-permute-start | bytes 1720328 | tf_op jit(solution)/shard_map/ppermute | solution.py:290
  80.3 2.8 %collective-permute-start.20 = (bf16[2,2,40,1792]{3,2,1,0:T(8,128)(2,1)S(1)}, bf16[2,2,40,1792]{3,2,1,0:T(8,128)(2,1)S(1)}, u32[]{:S(2)}, u32[]{:S(2)}) collective-permute-start(bf16[2,2,40,1792]{3,2,1,0:T(8,128)(2,1)S(1)} %get-tuple-element.138), channel_id=1, source_target_pairs={{0,8},{8,0},{16,24},{24,16},{1,9},{9,1},{17,25},{25,17},{2,10},{10... | collective-permute-start | bytes 1720328 | tf_op jit(solution)/shard_map/ppermute | solution.py:290
  81.8 3.1 %collective-permute-start.18 = (bf16[2,40,1792]{2,1,0:T(8,128)(2,1)S(1)}, bf16[2,40,1792]{2,1,0:T(8,128)(2,1)S(1)}, u32[]{:S(2)}, u32[]{:S(2)}) collective-permute-start(bf16[2,40,1792]{2,1,0:T(8,128)(2,1)S(1)} %get-tuple-element.132.own_ref), channel_id=1, source_target_pairs={{0,8},{8,0},{16,24},{24,16},{1,9},{9,1},{17,25},{25,17},{2,10},{10... | collective-permute-start | bytes 860168 | tf_op jit(solution)/shard_map/ppermute | solution.py:290
  83.3 15.1 %collective-permute-start.23 = (bf16[2,2,40,1792]{3,2,1,0:T(8,128)(2,1)S(1)}, bf16[2,2,40,1792]{3,2,1,0:T(8,128)(2,1)S(1)}, u32[]{:S(2)}, u32[]{:S(2)}) collective-permute-start(bf16[2,2,40,1792]{3,2,1,0:T(8,128)(2,1)S(1)} %get-tuple-element.144), channel_id=1, source_target_pairs={{0,16},{8,24},{16,0},{24,8},{1,17},{9,25},{17,1},{25,9},{2,18},{10... | collective-permute-start | bytes 1720328 | tf_op jit(solution)/shard_map/ppermute | solution.py:290
  89.3 16.0 %collective-permute-start.28 = (bf16[2,40,4096]{2,1,0:T(8,128)(2,1)S(1)}, bf16[2,40,4096]{2,1,0:T(8,128)(2,1)S(1)}, u32[]{:S(2)}, u32[]{:S(2)}) collective-permute-start(bf16[2,40,4096]{2,1,0:T(8,128)(2,1)S(1)} %get-tuple-element.156), channel_id=1, source_target_pairs={{0,1},{1,0},{2,3},{3,2},{4,5},{5,4},{6,7},{7,6},{8,9},{9,8},{10,11... | collective-permute-start | bytes 1966088 | tf_op jit(solution)/shard_map/ppermute | solution.py:290
  96.3 2.5 %collective-permute-start.21 = (bf16[1,2,1,40,1792]{4,3,2,1,0:T(8,128)(2,1)S(1)}, bf16[1,2,1,40,1792]{4,3,2,1,0:T(8,128)(2,1)S(1)}, u32[]{:S(2)}, u32[]{:S(2)}) collective-permute-start(bf16[1,2,1,40,1792]{4,3,2,1,0:T(8,128)(2,1)S(1)} %get-tuple-element.142), channel_id=1, source_target_pairs={{0,8},{8,0},{16,24},{24,16},{1,9},{9,1},{17,25},{25,17},{2,10},{10... | collective-permute-start | bytes 860168 | tf_op jit(solution)/shard_map/ppermute | solution.py:290
  96.3 2.4 %collective-permute-start.22 = (bf16[1,2,1,40,1792]{4,3,2,1,0:T(8,128)(2,1)S(1)}, bf16[1,2,1,40,1792]{4,3,2,1,0:T(8,128)(2,1)S(1)}, u32[]{:S(2)}, u32[]{:S(2)}) collective-permute-start(bf16[1,2,1,40,1792]{4,3,2,1,0:T(8,128)(2,1)S(1)} %get-tuple-element.143), channel_id=1, source_target_pairs={{0,8},{8,0},{16,24},{24,16},{1,9},{9,1},{17,25},{25,17},{2,10},{10... | collective-permute-start | bytes 860168 | tf_op jit(solution)/shard_map/ppermute | solution.py:290
  98.7 2.0 %collective-permute-start.27 = (bf16[2,40,1792]{2,1,0:T(8,128)(2,1)S(1)}, bf16[2,40,1792]{2,1,0:T(8,128)(2,1)S(1)}, u32[]{:S(2)}, u32[]{:S(2)}) collective-permute-start(bf16[2,40,1792]{2,1,0:T(8,128)(2,1)S(1)} %get-tuple-element.152.own_ref), channel_id=1, source_target_pairs={{0,8},{8,0},{16,24},{24,16},{1,9},{9,1},{17,25},{25,17},{2,10},{10... | collective-permute-start | bytes 860168 | tf_op jit(solution)/shard_map/ppermute | solution.py:290
  98.9 17.1 %collective-permute-start.24 = (bf16[2,2,40,1792]{3,2,1,0:T(8,128)(2,1)S(1)}, bf16[2,2,40,1792]{3,2,1,0:T(8,128)(2,1)S(1)}, u32[]{:S(2)}, u32[]{:S(2)}) collective-permute-start(bf16[2,2,40,1792]{3,2,1,0:T(8,128)(2,1)S(1)} %get-tuple-element.147), channel_id=1, source_target_pairs={{0,16},{8,24},{16,0},{24,8},{1,17},{9,25},{17,1},{25,9},{2,18},{10... | collective-permute-start | bytes 1720328 | tf_op jit(solution)/shard_map/ppermute | solution.py:290
  100.5 15.6 %collective-permute-start.26 = (bf16[2,2,40,1792]{3,2,1,0:T(8,128)(2,1)S(1)}, bf16[2,2,40,1792]{3,2,1,0:T(8,128)(2,1)S(1)}, u32[]{:S(2)}, u32[]{:S(2)}) collective-permute-start(bf16[2,2,40,1792]{3,2,1,0:T(8,128)(2,1)S(1)} %get-tuple-element.151), channel_id=1, source_target_pairs={{0,8},{8,0},{16,24},{24,16},{1,9},{9,1},{17,25},{25,17},{2,10},{10... | collective-permute-start | bytes 1720328 | tf_op jit(solution)/shard_map/ppermute | solution.py:290
  105.3 9.3 %collective-permute-start.29 = (bf16[1,40,4096]{2,1,0:T(8,128)(2,1)S(1)}, bf16[1,40,4096]{2,1,0:T(8,128)(2,1)S(1)}, u32[]{:S(2)}, u32[]{:S(2)}) collective-permute-start(bf16[1,40,4096]{2,1,0:T(8,128)(2,1)S(1)} %get-tuple-element.157), channel_id=1, source_target_pairs={{0,1},{1,0},{2,3},{3,2},{4,5},{5,4},{6,7},{7,6},{8,9},{9,8},{10,11... | collective-permute-start | bytes 983048 | tf_op jit(solution)/shard_map/ppermute | solution.py:290
  106.8 17.7 %collective-permute-start.32 = (bf16[2,40,4096]{2,1,0:T(8,128)(2,1)S(1)}, bf16[2,40,4096]{2,1,0:T(8,128)(2,1)S(1)}, u32[]{:S(2)}, u32[]{:S(2)}) collective-permute-start(bf16[2,40,4096]{2,1,0:T(8,128)(2,1)S(1)} %get-tuple-element.171), channel_id=1, source_target_pairs={{0,2},{1,3},{2,0},{3,1},{4,6},{5,7},{6,4},{7,5},{8,10},{9,11},{10,... | collective-permute-start | bytes 1966088 | tf_op jit(solution)/shard_map/ppermute | solution.py:317
  114.6 9.9 %collective-permute-start.31 = (bf16[1,40,4096]{2,1,0:T(8,128)(2,1)S(1)}, bf16[1,40,4096]{2,1,0:T(8,128)(2,1)S(1)}, u32[]{:S(2)}, u32[]{:S(2)}) collective-permute-start(bf16[1,40,4096]{2,1,0:T(8,128)(2,1)S(1)} %get-tuple-element.169), channel_id=1, source_target_pairs={{0,1},{1,0},{2,3},{3,2},{4,5},{5,4},{6,7},{7,6},{8,9},{9,8},{10,11... | collective-permute-start | bytes 983048 | tf_op jit(solution)/shard_map/ppermute | solution.py:290
  116.3 3.1 %collective-permute-start.30 = (bf16[2,40,1792]{2,1,0:T(8,128)(2,1)S(1)}, bf16[2,40,1792]{2,1,0:T(8,128)(2,1)S(1)}, u32[]{:S(2)}, u32[]{:S(2)}) collective-permute-start(bf16[2,40,1792]{2,1,0:T(8,128)(2,1)S(1)} %get-tuple-element.162.own_ref), channel_id=1, source_target_pairs={{0,8},{8,0},{16,24},{24,16},{1,9},{9,1},{17,25},{25,17},{2,10},{10... | collective-permute-start | bytes 860168 | tf_op jit(solution)/shard_map/ppermute | solution.py:290
  116.4 19.9 %collective-permute-start.25 = (bf16[2,2,40,1792]{3,2,1,0:T(8,128)(2,1)S(1)}, bf16[2,2,40,1792]{3,2,1,0:T(8,128)(2,1)S(1)}, u32[]{:S(2)}, u32[]{:S(2)}) collective-permute-start(bf16[2,2,40,1792]{3,2,1,0:T(8,128)(2,1)S(1)} %get-tuple-element.148), channel_id=1, source_target_pairs={{0,16},{8,24},{16,0},{24,8},{1,17},{9,25},{17,1},{25,9},{2,18},{10... | collective-permute-start | bytes 1720328 | tf_op jit(solution)/shard_map/ppermute | solution.py:290
  117.4 14.1 %collective-permute-start.34 = (bf16[1,40,4096]{2,1,0:T(8,128)(2,1)S(1)}, bf16[1,40,4096]{2,1,0:T(8,128)(2,1)S(1)}, u32[]{:S(2)}, u32[]{:S(2)}) collective-permute-start(bf16[1,40,4096]{2,1,0:T(8,128)(2,1)S(1)} %get-tuple-element.168), channel_id=1, source_target_pairs={{0,2},{1,3},{2,0},{3,1},{4,6},{5,7},{6,4},{7,5},{8,10},{9,11},{10,... | collective-permute-start | bytes 983048 | tf_op jit(solution)/shard_map/ppermute | solution.py:317
  124.6 8.4 %collective-permute-start.33 = (bf16[1,40,4096]{2,1,0:T(8,128)(2,1)S(1)}, bf16[1,40,4096]{2,1,0:T(8,128)(2,1)S(1)}, u32[]{:S(2)}, u32[]{:S(2)}) collective-permute-start(bf16[1,40,4096]{2,1,0:T(8,128)(2,1)S(1)} %get-tuple-element.173), channel_id=1, source_target_pairs={{0,1},{1,0},{2,3},{3,2},{4,5},{5,4},{6,7},{7,6},{8,9},{9,8},{10,11... | collective-permute-start | bytes 983048 | tf_op jit(solution)/shard_map/ppermute | solution.py:290
  125.3 12.8 %collective-permute-start.35 = (bf16[1,40,4096]{2,1,0:T(8,128)(2,1)S(1)}, bf16[1,40,4096]{2,1,0:T(8,128)(2,1)S(1)}, u32[]{:S(2)}, u32[]{:S(2)}) collective-permute-start(bf16[1,40,4096]{2,1,0:T(8,128)(2,1)S(1)} %get-tuple-element.172), channel_id=1, source_target_pairs={{0,2},{1,3},{2,0},{3,1},{4,6},{5,7},{6,4},{7,5},{8,10},{9,11},{10,... | collective-permute-start | bytes 983048 | tf_op jit(solution)/shard_map/ppermute | solution.py:317
  133.1 10.8 %collective-permute-start.37 = (bf16[1,40,4096]{2,1,0:T(8,128)(2,1)S(1)}, bf16[1,40,4096]{2,1,0:T(8,128)(2,1)S(1)}, u32[]{:S(2)}, u32[]{:S(2)}) collective-permute-start(bf16[1,40,4096]{2,1,0:T(8,128)(2,1)S(1)} %get-tuple-element.182), channel_id=1, source_target_pairs={{0,1},{1,0},{2,3},{3,2},{4,5},{5,4},{6,7},{7,6},{8,9},{9,8},{10,11... | collective-permute-start | bytes 983048 | tf_op jit(solution)/shard_map/ppermute | solution.py:290
  133.8 13.4 %collective-permute-start.40 = (bf16[1,40,4096]{2,1,0:T(8,128)(2,1)S(1)}, bf16[1,40,4096]{2,1,0:T(8,128)(2,1)S(1)}, u32[]{:S(2)}, u32[]{:S(2)}) collective-permute-start(bf16[1,40,4096]{2,1,0:T(8,128)(2,1)S(1)} %get-tuple-element.181), channel_id=1, source_target_pairs={{0,6},{1,7},{6,0},{7,1},{2,4},{3,5},{4,2},{5,3},{8,14},{9,15},{14,... | collective-permute-start | bytes 983048 | tf_op jit(solution)/shard_map/ppermute | solution.py:317
  138.4 1.6 collective-permute-start.36
  143.9 16.8 %collective-permute-start.38 = (bf16[2,40,4096]{2,1,0:T(8,128)(2,1)S(1)}, bf16[2,40,4096]{2,1,0:T(8,128)(2,1)S(1)}, u32[]{:S(2)}, u32[]{:S(2)}) collective-permute-start(bf16[2,40,4096]{2,1,0:T(8,128)(2,1)S(1)} %get-tuple-element.183), channel_id=1, source_target_pairs={{0,1},{1,0},{2,3},{3,2},{4,5},{5,4},{6,7},{7,6},{8,9},{9,8},{10,11... | collective-permute-start | bytes 1966088 | tf_op jit(solution)/shard_map/ppermute | solution.py:290
  144.7 16.2 %collective-permute-start.39 = (bf16[1,40,4096]{2,1,0:T(8,128)(2,1)S(1)}, bf16[1,40,4096]{2,1,0:T(8,128)(2,1)S(1)}, u32[]{:S(2)}, u32[]{:S(2)}) collective-permute-start(bf16[1,40,4096]{2,1,0:T(8,128)(2,1)S(1)} %get-tuple-element.186), channel_id=1, source_target_pairs={{0,6},{1,7},{6,0},{7,1},{2,4},{3,5},{4,2},{5,3},{8,14},{9,15},{14,... | collective-permute-start | bytes 983048 | tf_op jit(solution)/shard_map/ppermute | solution.py:317
  160.9 1.7 %collective-permute-start.41 = (bf16[40,4096]{1,0:T(8,128)(2,1)S(1)}, bf16[40,4096]{1,0:T(8,128)(2,1)S(1)}, u32[]{:S(2)}, u32[]{:S(2)}) collective-permute-start(bf16[40,4096]{1,0:T(8,128)(2,1)S(1)} %fusion.4), channel_id=1, source_target_pairs={{0,8},{8,0},{16,24},{24,16},{1,9},{9,1},{17,25},{25,17},{2,10},{10... | collective-permute-start | bytes 983048 | tf_op jit(solution)/shard_map/ppermute | solution.py:290

commit v8 on v7

--- a/solution.py
+++ b/solution.py
@@ -32,10 +32,6 @@
     return (values * lax.rsqrt(meansq + 1e-05) * norm_gain).astype(BF16)
 
 
-def params(*semantics):
-    return pltpu.CompilerParams(dimension_semantics=semantics, vmem_limit_bytes=VMEM)
-
-
 HURRY = 1000
 
 
@@ -52,48 +48,42 @@
 INSIDE = pl.BlockSpec(memory_space=pltpu.VMEM)
 
 
-def mask_kernel(share, after_count, core_ref, weight_ref, mask_ref, *refs):
-    kept_ref, token_ref, spread = refs[after_count:]
+def mask_kernel(share, rows, after_count, core_ref, weight_ref, mask_ref, *refs):
+    kept_ref, token_ref, spread, semaphores = refs[after_count:]
     token_ref[...] = jnp.zeros_like(token_ref)
-    depth, width = weight_ref.shape
-    blocks = depth // BLOCK
-    step = pl.program_id(0)
-
-    @pl.when(step == 0)
-    def _():
-        marks = mask_ref.shape[1]
-        first = share(core_ref[0]) * (width // BLOCK)
-        owner = lax.broadcasted_iota(jnp.int32, (marks, width), 1) // BLOCK + first
-        chosen = (owner == lax.broadcasted_iota(jnp.int32, (marks, width), 0)).astype(F32)
-        spread[...] = jnp.dot(mask_ref[...].astype(F32), chosen, preferred_element_type=F32)
-
-    for block in range(blocks):
-        rows = pl.ds(block * BLOCK, BLOCK)
-        keep = jnp.broadcast_to(spread[pl.ds(step * blocks + block, 1), :], (BLOCK, width))
-        kept_ref[rows, :] = weight_ref[rows, :] * keep.astype(BF16)
+    depth, width = kept_ref.shape
+    number = share(core_ref[0])
+    columns = pl.ds(pl.multiple_of(number * width, width), width)
+    copies = [
+        pltpu.make_async_copy(
+            weight_ref.at[pl.ds(step * rows, rows), columns], kept_ref.at[pl.ds(step * rows, rows)], semaphores.at[step]
+        )
+        for step in range(depth // rows)
+    ]
+    for copy in copies:
+        copy.start()
+    marks = mask_ref.shape[1]
+    owner = lax.broadcasted_iota(jnp.int32, (marks, width), 1) // BLOCK + number * (width // BLOCK)
+    chosen = (owner == lax.broadcasted_iota(jnp.int32, (marks, width), 0)).astype(F32)
+    spread[...] = jnp.dot(mask_ref[...].astype(F32), chosen, preferred_element_type=F32)
+    for step, copy in enumerate(copies):
+        copy.wait()
+        for block in range(step * rows // BLOCK, (step + 1) * rows // BLOCK):
+            part = pl.ds(block * BLOCK, BLOCK)
+            keep = jnp.broadcast_to(spread[pl.ds(block, 1), :], (BLOCK, width))
+            kept_ref[part, :] = kept_ref[part, :] * keep.astype(BF16)
 
 
 def masked(weight, mask, rows, core, shares, share, after, hint=0.0):
     depth, width = weight.shape
     width = width // shares
     return pl.pallas_call(
-        functools.partial(mask_kernel, share, len(after)),
-        grid_spec=pltpu.PrefetchScalarGridSpec(
-            num_scalar_prefetch=1,
-            grid=(depth // rows,),
-            in_specs=[
-                pl.BlockSpec((rows, width), lambda i, core: (i, share(core[0]))),
-                pl.BlockSpec(mask.shape, lambda i, core: (0, 0)),
-            ]
-            + [ANYWHERE] * len(after),
-            out_specs=[
-                pl.BlockSpec((rows, width), lambda i, core: (i, 0)),
-                pl.BlockSpec(TOKEN.shape, lambda i, core: (0, 0)),
-            ],
-            scratch_shapes=[pltpu.VMEM((mask.shape[0], width), F32)],
-        ),
+        functools.partial(mask_kernel, share, rows, len(after)),
+        in_specs=[pl.BlockSpec(memory_space=pltpu.SMEM), ANYWHERE, INSIDE] + [ANYWHERE] * len(after),
+        out_specs=[INSIDE] * 2,
         out_shape=[jax.ShapeDtypeStruct((depth, width), weight.dtype), TOKEN],
-        compiler_params=params("arbitrary"),
+        scratch_shapes=[pltpu.VMEM((mask.shape[0], width), F32), pltpu.SemaphoreType.DMA((depth // rows,))],
+        compiler_params=pltpu.CompilerParams(vmem_limit_bytes=VMEM),
         cost_estimate=as_if(hint),
         name="masked",
     )(core, pltpu.with_memory_space_constraint(weight, pltpu.HBM), mask, *after)
@@ -382,9 +372,8 @@
             down_weight, down_mask, 2 * BLOCK, place, 2 * CORES, lambda core, share=share: 2 * core + share, last, 8 - 8 * share
         )
         down_kept.append(part)
-        if share == 0:
-            forward(1, one_away, [*parts[0][1:], *last])
-            outer_two = by_plane(inner_three, OUTWARD, last)
+    outer_two = by_plane(inner_three, OUTWARD, last)
+    forward(1, one_away, [*parts[0][1:], *last])
     multiply_in(0, hint=0)
     exchange(0, [inner_two, outer_two])
     exchange_near(0, [inner_two, outer_two])

time: 164 us -> 162 us (0.988)
  Pallas kernels: 70.7 us -> 55.9 us
  waiting for transfers between devices: 47.1 us -> 57.3 us
  starting transfers between devices: 41.1 us -> 43.4 us
    pallas_call x4, Pallas kernels: 27.9 us -> 13 us  [masked(): pl.pallas_call(functools.partial(mask_kernel, share, rows, len(after)), i...]
    ppermute x11, waiting for transfers between devices: 16.5 us -> 23.8 us  [by_plane(): return lax.ppermute(behind(values, after), 'cols', pairs)]
    ppermute x31, waiting for transfers between devices: 30.6 us -> 33.4 us  [swap(): lax.ppermute(values, axis, [(place, place ^ step) for place in range(size)])]
    ppermute x31, starting transfers between devices: 22.2 us -> 25 us  [swap(): lax.ppermute(values, axis, [(place, place ^ step) for place in range(size)])]
  transfers between devices with their start and end apart: 42 -> 42, of which waited for: 20 -> 20; matrix products, arithmetic and copies ran while one was open for 0% -> 0% of each run, Pallas kernels for 43% -> 35%
where the time goes in v8:
time: 162 us; the launch traced here: 161 us
  waiting for transfers between devices  57.3 us (35%)
  Pallas kernels  55.9 us (35%)
  starting transfers between devices  43.4 us (27%)
  other arithmetic  4.29 us (3%)
    ppermute x31, waiting for transfers between devices, swap(): lax.ppermute(values, axis, [(place, place ^ step) for place in range(size)])  33.4 us
    ppermute x31, starting transfers between devices, swap(): lax.ppermute(values, axis, [(place, place ^ step) for place in range(size)])  25 us
    pallas_call x4, Pallas kernels, gate_up(): pl.pallas_call(functools.partial(gate_up_kernel, len(parts), len(after)),...  24.3 us
    ppermute x11, waiting for transfers between devices, by_plane(): return lax.ppermute(behind(values, after), 'cols', pairs)  23.8 us
    ppermute x11, starting transfers between devices, by_plane(): return lax.ppermute(behind(values, after), 'cols', pairs)  18.4 us
    pallas_call x4, Pallas kernels, down(): pl.pallas_call(functools.partial(down_kernel, pieces, len(down_kept), len...  15.5 us
    pallas_call x4, Pallas kernels, masked(): pl.pallas_call(functools.partial(mask_kernel, share, rows, len(after)), i...  13 us
  transfers between devices with their start and end apart: 42, of which 20 were waited for; matrix products, arithmetic and copies ran while one was open for 0% of the time, Pallas kernels for 35%

profile of v8, /device:TPU:0, one launch (start us, length us, event | category | flops | bytes accessed | tf_op | source)
XLA Modules:
  0.0 161.3 jit_solution(8674695807656576350)
XLA Ops:
  0.0 1.3 fusion
  1.4 1.3 fusion.2
  3.3 2.6 %collective-permute-start.1 = (bf16[40,2048]{1,0:T(8,128)(2,1)S(1)}, bf16[40,2048]{1,0:T(8,128)(2,1)S(1)}, u32[]{:S(2)}, u32[]{:S(2)}) collective-permute-start(bf16[40,2048]{1,0:T(8,128)(2,1)S(1)} %get-tuple-element.192), channel_id=1, source_target_pairs={{0,16},{8,24},{16,0},{24,8},{1,17},{9,25},{17,1},{25,9},{2,18},{10... | collective-permute-start | bytes 491528 | tf_op jit(solution)/shard_map/ppermute | solution.py:280
  5.9 1.9 %collective-permute-start.4 = (bf16[2,1,40,2048]{3,2,1,0:T(8,128)(2,1)S(1)}, bf16[2,1,40,2048]{3,2,1,0:T(8,128)(2,1)S(1)}, u32[]{:S(2)}, u32[]{:S(2)}) collective-permute-start(bf16[2,1,40,2048]{3,2,1,0:T(8,128)(2,1)S(1)} %get-tuple-element.97.refs_0_), channel_id=1, source_target_pairs={{0,2},{1,3},{2,0},{3,1},{4,6},{5,7},{6,4},{7,5},{8,10},{9,11},{10,... | collective-permute-start | bytes 983048 | tf_op jit(solution)/shard_map/ppermute | solution.py:307
  7.8 3.3 %masked.4 = (bf16[2048,1792]{1,0:T(8,128)(2,1)S(1)}, f32[8,128]{1,0:T(8,128)S(1)}) custom-call(s32[1]{0:T(128)} %bitcast.core_ref, bf16[2048,1792]{1,0:T(8,128)(2,1)} %weight_ref.4, s32[32,28]{1,0:T(8,128)S(1)} %copy-done, f32[8,128]{1,0:T(8,128)S(1)} %get-tuple-element.98.refs_0_), custom_call_target="tpu_custom_call" | custom-call | tf_op jit(solution)/shard_map/masked/pallas_call | solution.py:80
  11.1 2.8 %collective-permute-done.2.refs_1_ = bf16[40,2048]{1,0:T(8,128)(2,1)S(1)} collective-permute-done((bf16[40,2048]{1,0:T(8,128)(2,1)S(1)}, bf16[40,2048]{1,0:T(8,128)(2,1)S(1)}, u32[]{:S(2)}, u32[]{:S(2)}) %collective-permute-start.2) | collective-permute-done | bytes 163872 | tf_op jit(solution)/shard_map/ppermute | solution.py:280
  13.9 1.7 %collective-permute-start.5 = (bf16[2,1,40,2048]{3,2,1,0:T(8,128)(2,1)S(1)}, bf16[2,1,40,2048]{3,2,1,0:T(8,128)(2,1)S(1)}, u32[]{:S(2)}, u32[]{:S(2)}) collective-permute-start(bf16[2,1,40,2048]{3,2,1,0:T(8,128)(2,1)S(1)} %get-tuple-element.100.refs_1_), channel_id=1, source_target_pairs={{0,2},{1,3},{2,0},{3,1},{4,6},{5,7},{6,4},{7,5},{8,10},{9,11},{10,... | collective-permute-start | bytes 983048 | tf_op jit(solution)/shard_map/ppermute | solution.py:307
  16.4 1.6 collective-permute-start.3
  18.0 3.3 %masked.5 = (bf16[2048,1792]{1,0:T(8,128)(2,1)S(1)}, f32[8,128]{1,0:T(8,128)S(1)}) custom-call(s32[1]{0:T(128)} %bitcast.core_ref, bf16[2048,1792]{1,0:T(8,128)(2,1)} %weight_ref.5, s32[32,28]{1,0:T(8,128)S(1)} %copy-done.1, f32[8,128]{1,0:T(8,128)S(1)} %get-tuple-element.104.refs_0_, bf16[2,1,40,2048]{3,2,1,0:T(8,128)(2,1)S(1)} %collective-permute-done.4.refs_1_.refs_0_), custom_call_target="tpu_custom_call" | custom-call | flops 172500000 | tf_op jit(solution)/shard_map/masked/pallas_call | solution.py:80
  21.2 2.8 %collective-permute-done.5.refs_1_ = bf16[2,1,40,2048]{3,2,1,0:T(8,128)(2,1)S(1)} collective-permute-done((bf16[2,1,40,2048]{3,2,1,0:T(8,128)(2,1)S(1)}, bf16[2,1,40,2048]{3,2,1,0:T(8,128)(2,1)S(1)}, u32[]{:S(2)}, u32[]{:S(2)}) %collective-permute-start.5) | collective-permute-done | bytes 327712 | tf_op jit(solution)/shard_map/ppermute | solution.py:307
  24.1 3.3 %masked.6 = (bf16[1792,2048]{1,0:T(8,128)(2,1)S(1)}, f32[8,128]{1,0:T(8,128)S(1)}) custom-call(s32[1]{0:T(128)} %bitcast.core_ref, bf16[1792,8192]{1,0:T(8,128)(2,1)} %weight_ref.7, s32[28,128]{1,0:T(8,128)S(1)} %copy-done.2, f32[8,128]{1,0:T(8,128)S(1)} %get-tuple-element.107.refs_0_), custom_call_target="tpu_custom_call" | custom-call | flops 9200000000 | tf_op jit(solution)/shard_map/masked/pallas_call | solution.py:80
  27.4 3.3 %masked.7 = (bf16[1792,2048]{1,0:T(8,128)(2,1)S(1)}, f32[8,128]{1,0:T(8,128)S(1)}) custom-call(s32[1]{0:T(128)} %bitcast.core_ref, bf16[1792,8192]{1,0:T(8,128)(2,1)} %weight_ref.7, s32[28,128]{1,0:T(8,128)S(1)} %copy-done.2, f32[8,128]{1,0:T(8,128)S(1)} %get-tuple-element.108.refs_0_), custom_call_target="tpu_custom_call" | custom-call | tf_op jit(solution)/shard_map/masked/pallas_call | solution.py:80
  31.4 1.3 collective-permute-start.8
  33.4 1.5 collective-permute-start.12
  34.9 6.1 %gate_up.4 = (bf16[2,2,2,40,1792]{4,3,2,1,0:T(8,128)(2,1)S(1)}, bf16[2,2,40,1792]{3,2,1,0:T(8,128)(2,1)S(1)}, bf16[2,2,1,40,1792]{4,3,2,1,0:T(8,128)(2,1)S(1)}, f32[8,128]{1,0:T(8,128)S(1)}) custom-call(bf16[160,2048]{1,0:T(8,128)(2,1)S(1)} %get-tuple-element.102.refs_0_, bf16[160,2048]{1,0:T(8,128)(2,1)S(1)} %collective-permute-done.3.refs_1_, ...), custom_call_target="tpu_custom_call" | custom-call | tf_op jit(solution)/shard_map/gate_up/pallas_call | solution.py:162
  41.0 10.9 %collective-permute-done.8 = bf16[160,2048]{1,0:T(8,128)(2,1)S(1)} collective-permute-done((bf16[160,2048]{1,0:T(8,128)(2,1)S(1)}, bf16[160,2048]{1,0:T(8,128)(2,1)S(1)}, u32[]{:S(2)}, u32[]{:S(2)}) %collective-permute-start.8) | collective-permute-done | bytes 655392 | tf_op jit(solution)/shard_map/ppermute | solution.py:307
  52.4 1.5 collective-permute-start.11
  54.1 1.6 collective-permute-start.15
  55.8 6.1 %gate_up.5 = (bf16[2,2,2,40,1792]{4,3,2,1,0:T(8,128)(2,1)S(1)}, bf16[2,2,40,1792]{3,2,1,0:T(8,128)(2,1)S(1)}, bf16[2,2,1,40,1792]{4,3,2,1,0:T(8,128)(2,1)S(1)}, f32[8,128]{1,0:T(8,128)S(1)}) custom-call(bf16[160,2048]{1,0:T(8,128)(2,1)S(1)} %get-tuple-element.120.refs_0_, bf16[160,2048]{1,0:T(8,128)(2,1)S(1)} %collective-permute-done.12.refs_1_, ...), custom_call_target="tpu_custom_call" | custom-call | flops 4697620480 | tf_op jit(solution)/shard_map/gate_up/pallas_call | solution.py:162
  62.5 1.5 collective-permute-done.13.refs_1_
  64.9 1.6 collective-permute-start.17
  66.5 4.4 %collective-permute-done.11.refs_5_ = bf16[160,2048]{1,0:T(8,128)(2,1)S(1)} collective-permute-done((bf16[160,2048]{1,0:T(8,128)(2,1)S(1)}, bf16[160,2048]{1,0:T(8,128)(2,1)S(1)}, u32[]{:S(2)}, u32[]{:S(2)}) %collective-permute-start.11) | collective-permute-done | bytes 655392 | tf_op jit(solution)/shard_map/ppermute | solution.py:307
  71.1 1.6 collective-permute-start.16
  72.7 6.1 %gate_up.6 = (bf16[2,2,2,40,1792]{4,3,2,1,0:T(8,128)(2,1)S(1)}, bf16[2,2,40,1792]{3,2,1,0:T(8,128)(2,1)S(1)}, bf16[2,2,1,40,1792]{4,3,2,1,0:T(8,128)(2,1)S(1)}, f32[8,128]{1,0:T(8,128)S(1)}) custom-call(bf16[160,2048]{1,0:T(8,128)(2,1)S(1)} %add.63.refs_0_, bf16[160,2048]{1,0:T(8,128)(2,1)S(1)} %collective-permute-done.15.refs_1_, ...), custom_call_target="tpu_custom_call" | custom-call | flops 4697620480 | tf_op jit(solution)/shard_map/gate_up/pallas_call | solution.py:162
  81.8 1.6 collective-permute-start.23
  83.4 3.9 %down.4 = (bf16[2,40,4096]{2,1,0:T(8,128)(2,1)S(1)}, bf16[2,40,4096]{2,1,0:T(8,128)(2,1)S(1)}, f32[8,128]{1,0:T(8,128)S(1)}) custom-call(bf16[2,40,1792]{2,1,0:T(8,128)(2,1)S(1)} %get-tuple-element.132.own_ref, bf16[2,40,1792]{2,1,0:T(8,128)(2,1)S(1)} %collective-permute-done.18.other_ref, bf16[1792,2048]{1,0:T(8,128)(2,1)S(1)} %get-tuple-element.133.refs_0_, ...), custom_call_target="tpu_custom_call" | custom-call | flops 2348810 | tf_op jit(solution)/shard_map/down/pallas_call | solution.py:204
  87.3 1.2 collective-permute-start.28
  88.5 6.1 %gate_up.7 = (bf16[2,2,2,40,1792]{4,3,2,1,0:T(8,128)(2,1)S(1)}, bf16[2,2,40,1792]{3,2,1,0:T(8,128)(2,1)S(1)}, bf16[1,2,1,40,1792]{4,3,2,1,0:T(8,128)(2,1)S(1)}, ...) custom-call(bf16[160,2048]{1,0:T(8,128)(2,1)S(1)} %add.62.refs_0_, ...), custom_call_target="tpu_custom_call" | custom-call | flops 4697620480 | tf_op jit(solution)/shard_map/gate_up/pallas_call | solution.py:162
  95.2 1.7 %collective-permute-done.23.refs_2_ = bf16[2,2,40,1792]{3,2,1,0:T(8,128)(2,1)S(1)} collective-permute-done((bf16[2,2,40,1792]{3,2,1,0:T(8,128)(2,1)S(1)}, bf16[2,2,40,1792]{3,2,1,0:T(8,128)(2,1)S(1)}, u32[]{:S(2)}, u32[]{:S(2)}) %collective-permute-start.23) | collective-permute-done | bytes 573472 | tf_op jit(solution)/shard_map/ppermute | solution.py:280
  97.4 1.6 collective-permute-start.24
  99.2 3.9 %down.5 = (bf16[1,40,4096]{2,1,0:T(8,128)(2,1)S(1)}, bf16[1,40,4096]{2,1,0:T(8,128)(2,1)S(1)}, bf16[1,40,4096]{2,1,0:T(8,128)(2,1)S(1)}, bf16[1,40,4096]{2,1,0:T(8,128)(2,1)S(1)}, f32[8,128]{1,0:T(8,128)S(1)}) custom-call(bf16[2,40,1792]{2,1,0:T(8,128)(2,1)S(1)} %get-tuple-element.152.own_ref, bf16[2,40,1792]{2,1,0:T(8,128)(2,1)S(1)} %collective-permute-done.27.other_ref, ...), custom_call_target="tpu_custom_call" | custom-call | flops 2348810 | tf_op jit(solution)/shard_map/down/pallas_call | solution.py:204
  104.5 2.0 %collective-permute-start.32 = (bf16[2,40,4096]{2,1,0:T(8,128)(2,1)S(1)}, bf16[2,40,4096]{2,1,0:T(8,128)(2,1)S(1)}, u32[]{:S(2)}, u32[]{:S(2)}) collective-permute-start(bf16[2,40,4096]{2,1,0:T(8,128)(2,1)S(1)} %get-tuple-element.171), channel_id=1, source_target_pairs={{0,2},{1,3},{2,0},{3,1},{4,6},{5,7},{6,4},{7,5},{8,10},{9,11},{10,... | collective-permute-start | bytes 1966088 | tf_op jit(solution)/shard_map/ppermute | solution.py:307
  106.5 6.6 %collective-permute-done.29.refs_1_ = bf16[1,40,4096]{2,1,0:T(8,128)(2,1)S(1)} collective-permute-done((bf16[1,40,4096]{2,1,0:T(8,128)(2,1)S(1)}, bf16[1,40,4096]{2,1,0:T(8,128)(2,1)S(1)}, u32[]{:S(2)}, u32[]{:S(2)}) %collective-permute-start.29) | collective-permute-done | bytes 327712 | tf_op jit(solution)/shard_map/ppermute | solution.py:280
  115.1 2.0 %collective-permute-start.34 = (bf16[1,40,4096]{2,1,0:T(8,128)(2,1)S(1)}, bf16[1,40,4096]{2,1,0:T(8,128)(2,1)S(1)}, u32[]{:S(2)}, u32[]{:S(2)}) collective-permute-start(bf16[1,40,4096]{2,1,0:T(8,128)(2,1)S(1)} %get-tuple-element.168), channel_id=1, source_target_pairs={{0,2},{1,3},{2,0},{3,1},{4,6},{5,7},{6,4},{7,5},{8,10},{9,11},{10,... | collective-permute-start | bytes 983048 | tf_op jit(solution)/shard_map/ppermute | solution.py:307
  117.1 3.9 %down.6 = (bf16[1,40,4096]{2,1,0:T(8,128)(2,1)S(1)}, bf16[1,40,4096]{2,1,0:T(8,128)(2,1)S(1)}, bf16[1,40,4096]{2,1,0:T(8,128)(2,1)S(1)}, bf16[1,40,4096]{2,1,0:T(8,128)(2,1)S(1)}, f32[8,128]{1,0:T(8,128)S(1)}) custom-call(bf16[2,40,1792]{2,1,0:T(8,128)(2,1)S(1)} %get-tuple-element.162.own_ref, bf16[2,40,1792]{2,1,0:T(8,128)(2,1)S(1)} %collective-permute-done.30.other_ref, ...), custom_call_target="tpu_custom_call" | custom-call | flops 2348810 | tf_op jit(solution)/shard_map/down/pallas_call | solution.py:204
  121.0 1.2 collective-permute-done.32.refs_3_.refs_1_
  122.3 1.6 collective-permute-start.33
  123.9 2.0 %collective-permute-start.35 = (bf16[1,40,4096]{2,1,0:T(8,128)(2,1)S(1)}, bf16[1,40,4096]{2,1,0:T(8,128)(2,1)S(1)}, u32[]{:S(2)}, u32[]{:S(2)}) collective-permute-start(bf16[1,40,4096]{2,1,0:T(8,128)(2,1)S(1)} %get-tuple-element.172), channel_id=1, source_target_pairs={{0,2},{1,3},{2,0},{3,1},{4,6},{5,7},{6,4},{7,5},{8,10},{9,11},{10,... | collective-permute-start | bytes 983048 | tf_op jit(solution)/shard_map/ppermute | solution.py:307
  125.9 3.4 %collective-permute-done.34.refs_2_ = bf16[1,40,4096]{2,1,0:T(8,128)(2,1)S(1)} collective-permute-done((bf16[1,40,4096]{2,1,0:T(8,128)(2,1)S(1)}, bf16[1,40,4096]{2,1,0:T(8,128)(2,1)S(1)}, u32[]{:S(2)}, u32[]{:S(2)}) %collective-permute-start.34) | collective-permute-done | bytes 327712 | tf_op jit(solution)/shard_map/ppermute | solution.py:307
  129.2 1.4 collective-permute-done.33.refs_1_
  130.7 1.6 collective-permute-start.37
  132.3 2.3 %collective-permute-start.40 = (bf16[1,40,4096]{2,1,0:T(8,128)(2,1)S(1)}, bf16[1,40,4096]{2,1,0:T(8,128)(2,1)S(1)}, u32[]{:S(2)}, u32[]{:S(2)}) collective-permute-start(bf16[1,40,4096]{2,1,0:T(8,128)(2,1)S(1)} %get-tuple-element.181), channel_id=1, source_target_pairs={{0,6},{1,7},{6,0},{7,1},{2,4},{3,5},{4,2},{5,3},{8,14},{9,15},{14,... | collective-permute-start | bytes 983048 | tf_op jit(solution)/shard_map/ppermute | solution.py:307
  136.1 1.6 collective-permute-done.36.other_ref
  137.7 3.9 %down.7 = (bf16[2,40,4096]{2,1,0:T(8,128)(2,1)S(1)}, bf16[2,40,4096]{2,1,0:T(8,128)(2,1)S(1)}, f32[8,128]{1,0:T(8,128)S(1)}) custom-call(bf16[2,40,1792]{2,1,0:T(8,128)(2,1)S(1)} %get-tuple-element.176.own_ref, bf16[2,40,1792]{2,1,0:T(8,128)(2,1)S(1)} %collective-permute-done.36.other_ref, bf16[1792,2048]{1,0:T(8,128)(2,1)S(1)} %get-tuple-element.133.refs_0_, ...), custom_call_target="tpu_custom_call" | custom-call | flops 2348810 | tf_op jit(solution)/shard_map/down/pallas_call | solution.py:204
  141.5 1.6 collective-permute-start.38
  143.3 2.4 %collective-permute-start.39 = (bf16[1,40,4096]{2,1,0:T(8,128)(2,1)S(1)}, bf16[1,40,4096]{2,1,0:T(8,128)(2,1)S(1)}, u32[]{:S(2)}, u32[]{:S(2)}) collective-permute-start(bf16[1,40,4096]{2,1,0:T(8,128)(2,1)S(1)} %get-tuple-element.186), channel_id=1, source_target_pairs={{0,6},{1,7},{6,0},{7,1},{2,4},{3,5},{4,2},{5,3},{8,14},{9,15},{14,... | collective-permute-start | bytes 983048 | tf_op jit(solution)/shard_map/ppermute | solution.py:307
  146.3 12.1 %collective-permute-done.38 = bf16[2,40,4096]{2,1,0:T(8,128)(2,1)S(1)} collective-permute-done((bf16[2,40,4096]{2,1,0:T(8,128)(2,1)S(1)}, bf16[2,40,4096]{2,1,0:T(8,128)(2,1)S(1)}, u32[]{:S(2)}, u32[]{:S(2)}) %collective-permute-start.38) | collective-permute-done | bytes 655392 | tf_op jit(solution)/shard_map/ppermute | solution.py:280
  158.6 1.6 collective-permute-done.41
  (82 shorter events, 16.9 us)
Async XLA Ops:
  1.3 6.5 %copy-start = (s32[32,28]{1,0:T(8,128)S(1)}, s32[32,28]{1,0:T(8,128)}, u32[]{:S(2)}) copy-start(s32[32,28]{1,0:T(8,128)} %mask_ref.4) | copy-start | bytes 10756
  2.7 3.2 %collective-permute-start = (bf16[40,2048]{1,0:T(8,128)(2,1)S(1)}, bf16[40,2048]{1,0:T(8,128)(2,1)S(1)}, u32[]{:S(2)}, u32[]{:S(2)}) collective-permute-start(bf16[40,2048]{1,0:T(8,128)(2,1)S(1)} %get-tuple-element.193), channel_id=1, source_target_pairs={{0,8},{8,0},{16,24},{24,16},{1,9},{9,1},{17,25},{25,17},{2,10},{10... | collective-permute-start | bytes 491528 | tf_op jit(solution)/shard_map/ppermute | solution.py:280
  3.3 7.8 %collective-permute-start.1 = (bf16[40,2048]{1,0:T(8,128)(2,1)S(1)}, bf16[40,2048]{1,0:T(8,128)(2,1)S(1)}, u32[]{:S(2)}, u32[]{:S(2)}) collective-permute-start(bf16[40,2048]{1,0:T(8,128)(2,1)S(1)} %get-tuple-element.192), channel_id=1, source_target_pairs={{0,16},{8,24},{16,0},{24,8},{1,17},{9,25},{17,1},{25,9},{2,18},{10... | collective-permute-start | bytes 491528 | tf_op jit(solution)/shard_map/ppermute | solution.py:280
  5.8 8.0 %collective-permute-start.2 = (bf16[40,2048]{1,0:T(8,128)(2,1)S(1)}, bf16[40,2048]{1,0:T(8,128)(2,1)S(1)}, u32[]{:S(2)}, u32[]{:S(2)}) collective-permute-start(bf16[40,2048]{1,0:T(8,128)(2,1)S(1)} %get-tuple-element.191), channel_id=1, source_target_pairs={{0,24},{8,16},{16,8},{24,0},{1,25},{9,17},{17,9},{25,1},{2,26},{10... | collective-permute-start | bytes 491528 | tf_op jit(solution)/shard_map/ppermute | solution.py:280
  5.9 12.0 %collective-permute-start.4 = (bf16[2,1,40,2048]{3,2,1,0:T(8,128)(2,1)S(1)}, bf16[2,1,40,2048]{3,2,1,0:T(8,128)(2,1)S(1)}, u32[]{:S(2)}, u32[]{:S(2)}) collective-permute-start(bf16[2,1,40,2048]{3,2,1,0:T(8,128)(2,1)S(1)} %get-tuple-element.97.refs_0_), channel_id=1, source_target_pairs={{0,2},{1,3},{2,0},{3,1},{4,6},{5,7},{6,4},{7,5},{8,10},{9,11},{10,... | collective-permute-start | bytes 983048 | tf_op jit(solution)/shard_map/ppermute | solution.py:307
  7.8 10.2 %copy-start.1 = (s32[32,28]{1,0:T(8,128)S(1)}, s32[32,28]{1,0:T(8,128)}, u32[]{:S(2)}) copy-start(s32[32,28]{1,0:T(8,128)} %mask_ref.5) | copy-start | bytes 10756
  13.9 10.2 %collective-permute-start.5 = (bf16[2,1,40,2048]{3,2,1,0:T(8,128)(2,1)S(1)}, bf16[2,1,40,2048]{3,2,1,0:T(8,128)(2,1)S(1)}, u32[]{:S(2)}, u32[]{:S(2)}) collective-permute-start(bf16[2,1,40,2048]{3,2,1,0:T(8,128)(2,1)S(1)} %get-tuple-element.100.refs_1_), channel_id=1, source_target_pairs={{0,2},{1,3},{2,0},{3,1},{4,6},{5,7},{6,4},{7,5},{8,10},{9,11},{10,... | collective-permute-start | bytes 983048 | tf_op jit(solution)/shard_map/ppermute | solution.py:307
  15.7 15.7 %collective-permute-start.7 = (bf16[160,2048]{1,0:T(8,128)(2,1)S(1)}, bf16[160,2048]{1,0:T(8,128)(2,1)S(1)}, u32[]{:S(2)}, u32[]{:S(2)}) collective-permute-start(bf16[160,2048]{1,0:T(8,128)(2,1)S(1)} %get-tuple-element.102.refs_0_), channel_id=1, source_target_pairs={{2,4},{3,5},{4,2},{5,3},{10,12},{11,13},{12,10},{13,11},{18,20},{1... | collective-permute-start | bytes 1966088 | tf_op jit(solution)/shard_map/ppermute | solution.py:307
  16.4 17.0 %collective-permute-start.3 = (bf16[160,2048]{1,0:T(8,128)(2,1)S(1)}, bf16[160,2048]{1,0:T(8,128)(2,1)S(1)}, u32[]{:S(2)}, u32[]{:S(2)}) collective-permute-start(bf16[160,2048]{1,0:T(8,128)(2,1)S(1)} %get-tuple-element.102.refs_0_), channel_id=1, source_target_pairs={{0,1},{1,0},{2,3},{3,2},{4,5},{5,4},{6,7},{7,6},{8,9},{9,8},{10,11... | collective-permute-start | bytes 1966088 | tf_op jit(solution)/shard_map/ppermute | solution.py:280
  18.0 6.1 %copy-start.2 = (s32[28,128]{1,0:T(8,128)S(1)}, s32[28,128]{1,0:T(8,128)}, u32[]{:S(2)}) copy-start(s32[28,128]{1,0:T(8,128)} %mask_ref.7) | copy-start | bytes 43012
  30.7 10.3 %collective-permute-start.6 = (bf16[160,2048]{1,0:T(8,128)(2,1)S(1)}, bf16[160,2048]{1,0:T(8,128)(2,1)S(1)}, u32[]{:S(2)}, u32[]{:S(2)}) collective-permute-start(bf16[160,2048]{1,0:T(8,128)(2,1)S(1)} %get-tuple-element.120.refs_0_), channel_id=1, source_target_pairs={{2,4},{3,5},{4,2},{5,3},{10,12},{11,13},{12,10},{13,11},{18,20},{1... | collective-permute-start | bytes 1966088 | tf_op jit(solution)/shard_map/ppermute | solution.py:307
  31.4 20.5 %collective-permute-start.8 = (bf16[160,2048]{1,0:T(8,128)(2,1)S(1)}, bf16[160,2048]{1,0:T(8,128)(2,1)S(1)}, u32[]{:S(2)}, u32[]{:S(2)}) collective-permute-start(bf16[160,2048]{1,0:T(8,128)(2,1)S(1)} %collective-permute-done.7), channel_id=1, source_target_pairs={{2,0},{3,1},{4,6},{5,7},{10,8},{11,9},{12,14},{13,15},{18,16},{19,... | collective-permute-start | bytes 1966088 | tf_op jit(solution)/shard_map/ppermute | solution.py:307
  33.4 20.7 %collective-permute-start.12 = (bf16[160,2048]{1,0:T(8,128)(2,1)S(1)}, bf16[160,2048]{1,0:T(8,128)(2,1)S(1)}, u32[]{:S(2)}, u32[]{:S(2)}) collective-permute-start(bf16[160,2048]{1,0:T(8,128)(2,1)S(1)} %get-tuple-element.120.refs_0_), channel_id=1, source_target_pairs={{0,1},{1,0},{2,3},{3,2},{4,5},{5,4},{6,7},{7,6},{8,9},{9,8},{10,11... | collective-permute-start | bytes 1966088 | tf_op jit(solution)/shard_map/ppermute | solution.py:280
  51.9 3.8 %collective-permute-start.9 = (bf16[2,2,40,1792]{3,2,1,0:T(8,128)(2,1)S(1)}, bf16[2,2,40,1792]{3,2,1,0:T(8,128)(2,1)S(1)}, u32[]{:S(2)}, u32[]{:S(2)}) collective-permute-start(bf16[2,2,40,1792]{3,2,1,0:T(8,128)(2,1)S(1)} %get-tuple-element.114), channel_id=1, source_target_pairs={{0,8},{8,0},{16,24},{24,16},{1,9},{9,1},{17,25},{25,17},{2,10},{10... | collective-permute-start | bytes 1720328 | tf_op jit(solution)/shard_map/ppermute | solution.py:280
  51.9 3.8 %collective-permute-start.10 = (bf16[2,2,1,40,1792]{4,3,2,1,0:T(8,128)(2,1)S(1)}, bf16[2,2,1,40,1792]{4,3,2,1,0:T(8,128)(2,1)S(1)}, u32[]{:S(2)}, u32[]{:S(2)}) collective-permute-start(bf16[2,2,1,40,1792]{4,3,2,1,0:T(8,128)(2,1)S(1)} %get-tuple-element.116), channel_id=1, source_target_pairs={{0,8},{8,0},{16,24},{24,16},{1,9},{9,1},{17,25},{25,17},{2,10},{10... | collective-permute-start | bytes 1720328 | tf_op jit(solution)/shard_map/ppermute | solution.py:280
  52.4 18.5 %collective-permute-start.11 = (bf16[160,2048]{1,0:T(8,128)(2,1)S(1)}, bf16[160,2048]{1,0:T(8,128)(2,1)S(1)}, u32[]{:S(2)}, u32[]{:S(2)}) collective-permute-start(bf16[160,2048]{1,0:T(8,128)(2,1)S(1)} %collective-permute-done.6), channel_id=1, source_target_pairs={{2,0},{3,1},{4,6},{5,7},{10,8},{11,9},{12,14},{13,15},{18,16},{19,... | collective-permute-start | bytes 1966088 | tf_op jit(solution)/shard_map/ppermute | solution.py:307
  54.1 17.0 %collective-permute-start.15 = (bf16[160,2048]{1,0:T(8,128)(2,1)S(1)}, bf16[160,2048]{1,0:T(8,128)(2,1)S(1)}, u32[]{:S(2)}, u32[]{:S(2)}) collective-permute-start(bf16[160,2048]{1,0:T(8,128)(2,1)S(1)} %add.63.refs_0_), channel_id=1, source_target_pairs={{0,1},{1,0},{2,3},{3,2},{4,5},{5,4},{6,7},{7,6},{8,9},{9,8},{10,11... | collective-permute-start | bytes 1966088 | tf_op jit(solution)/shard_map/ppermute | solution.py:280
  61.9 2.0 %collective-permute-start.13 = (bf16[2,2,1,40,1792]{4,3,2,1,0:T(8,128)(2,1)S(1)}, bf16[2,2,1,40,1792]{4,3,2,1,0:T(8,128)(2,1)S(1)}, u32[]{:S(2)}, u32[]{:S(2)}) collective-permute-start(bf16[2,2,1,40,1792]{4,3,2,1,0:T(8,128)(2,1)S(1)} %get-tuple-element.123), channel_id=1, source_target_pairs={{0,8},{8,0},{16,24},{24,16},{1,9},{9,1},{17,25},{25,17},{2,10},{10... | collective-permute-start | bytes 1720328 | tf_op jit(solution)/shard_map/ppermute | solution.py:280
  62.0 2.8 %collective-permute-start.14 = (bf16[2,2,40,1792]{3,2,1,0:T(8,128)(2,1)S(1)}, bf16[2,2,40,1792]{3,2,1,0:T(8,128)(2,1)S(1)}, u32[]{:S(2)}, u32[]{:S(2)}) collective-permute-start(bf16[2,2,40,1792]{3,2,1,0:T(8,128)(2,1)S(1)} %get-tuple-element.125), channel_id=1, source_target_pairs={{0,8},{8,0},{16,24},{24,16},{1,9},{9,1},{17,25},{25,17},{2,10},{10... | collective-permute-start | bytes 1720328 | tf_op jit(solution)/shard_map/ppermute | solution.py:280
  64.9 15.1 %collective-permute-start.17 = (bf16[2,2,40,1792]{3,2,1,0:T(8,128)(2,1)S(1)}, bf16[2,2,40,1792]{3,2,1,0:T(8,128)(2,1)S(1)}, u32[]{:S(2)}, u32[]{:S(2)}) collective-permute-start(bf16[2,2,40,1792]{3,2,1,0:T(8,128)(2,1)S(1)} %get-tuple-element.130), channel_id=1, source_target_pairs={{0,16},{8,24},{16,0},{24,8},{1,17},{9,25},{17,1},{25,9},{2,18},{10... | collective-permute-start | bytes 1720328 | tf_op jit(solution)/shard_map/ppermute | solution.py:280
  71.1 16.1 %collective-permute-start.16 = (bf16[160,2048]{1,0:T(8,128)(2,1)S(1)}, bf16[160,2048]{1,0:T(8,128)(2,1)S(1)}, u32[]{:S(2)}, u32[]{:S(2)}) collective-permute-start(bf16[160,2048]{1,0:T(8,128)(2,1)S(1)} %add.62.refs_0_), channel_id=1, source_target_pairs={{0,1},{1,0},{2,3},{3,2},{4,5},{5,4},{6,7},{7,6},{8,9},{9,8},{10,11... | collective-permute-start | bytes 1966088 | tf_op jit(solution)/shard_map/ppermute | solution.py:280
  78.8 2.0 %collective-permute-start.19 = (bf16[2,2,1,40,1792]{4,3,2,1,0:T(8,128)(2,1)S(1)}, bf16[2,2,1,40,1792]{4,3,2,1,0:T(8,128)(2,1)S(1)}, u32[]{:S(2)}, u32[]{:S(2)}) collective-permute-start(bf16[2,2,1,40,1792]{4,3,2,1,0:T(8,128)(2,1)S(1)} %get-tuple-element.136), channel_id=1, source_target_pairs={{0,8},{8,0},{16,24},{24,16},{1,9},{9,1},{17,25},{25,17},{2,10},{10... | collective-permute-start | bytes 1720328 | tf_op jit(solution)/shard_map/ppermute | solution.py:280
  78.9 2.8 %collective-permute-start.20 = (bf16[2,2,40,1792]{3,2,1,0:T(8,128)(2,1)S(1)}, bf16[2,2,40,1792]{3,2,1,0:T(8,128)(2,1)S(1)}, u32[]{:S(2)}, u32[]{:S(2)}) collective-permute-start(bf16[2,2,40,1792]{3,2,1,0:T(8,128)(2,1)S(1)} %get-tuple-element.138), channel_id=1, source_target_pairs={{0,8},{8,0},{16,24},{24,16},{1,9},{9,1},{17,25},{25,17},{2,10},{10... | collective-permute-start | bytes 1720328 | tf_op jit(solution)/shard_map/ppermute | solution.py:280
  80.3 3.1 %collective-permute-start.18 = (bf16[2,40,1792]{2,1,0:T(8,128)(2,1)S(1)}, bf16[2,40,1792]{2,1,0:T(8,128)(2,1)S(1)}, u32[]{:S(2)}, u32[]{:S(2)}) collective-permute-start(bf16[2,40,1792]{2,1,0:T(8,128)(2,1)S(1)} %get-tuple-element.132.own_ref), channel_id=1, source_target_pairs={{0,8},{8,0},{16,24},{24,16},{1,9},{9,1},{17,25},{25,17},{2,10},{10... | collective-permute-start | bytes 860168 | tf_op jit(solution)/shard_map/ppermute | solution.py:280
  81.8 15.1 %collective-permute-start.23 = (bf16[2,2,40,1792]{3,2,1,0:T(8,128)(2,1)S(1)}, bf16[2,2,40,1792]{3,2,1,0:T(8,128)(2,1)S(1)}, u32[]{:S(2)}, u32[]{:S(2)}) collective-permute-start(bf16[2,2,40,1792]{3,2,1,0:T(8,128)(2,1)S(1)} %get-tuple-element.144), channel_id=1, source_target_pairs={{0,16},{8,24},{16,0},{24,8},{1,17},{9,25},{17,1},{25,9},{2,18},{10... | collective-permute-start | bytes 1720328 | tf_op jit(solution)/shard_map/ppermute | solution.py:280
  87.3 16.6 %collective-permute-start.28 = (bf16[2,40,4096]{2,1,0:T(8,128)(2,1)S(1)}, bf16[2,40,4096]{2,1,0:T(8,128)(2,1)S(1)}, u32[]{:S(2)}, u32[]{:S(2)}) collective-permute-start(bf16[2,40,4096]{2,1,0:T(8,128)(2,1)S(1)} %get-tuple-element.156), channel_id=1, source_target_pairs={{0,1},{1,0},{2,3},{3,2},{4,5},{5,4},{6,7},{7,6},{8,9},{9,8},{10,11... | collective-permute-start | bytes 1966088 | tf_op jit(solution)/shard_map/ppermute | solution.py:280
  94.6 2.7 %collective-permute-start.21 = (bf16[1,2,1,40,1792]{4,3,2,1,0:T(8,128)(2,1)S(1)}, bf16[1,2,1,40,1792]{4,3,2,1,0:T(8,128)(2,1)S(1)}, u32[]{:S(2)}, u32[]{:S(2)}) collective-permute-start(bf16[1,2,1,40,1792]{4,3,2,1,0:T(8,128)(2,1)S(1)} %get-tuple-element.142), channel_id=1, source_target_pairs={{0,8},{8,0},{16,24},{24,16},{1,9},{9,1},{17,25},{25,17},{2,10},{10... | collective-permute-start | bytes 860168 | tf_op jit(solution)/shard_map/ppermute | solution.py:280
  94.7 2.6 %collective-permute-start.22 = (bf16[1,2,1,40,1792]{4,3,2,1,0:T(8,128)(2,1)S(1)}, bf16[1,2,1,40,1792]{4,3,2,1,0:T(8,128)(2,1)S(1)}, u32[]{:S(2)}, u32[]{:S(2)}) collective-permute-start(bf16[1,2,1,40,1792]{4,3,2,1,0:T(8,128)(2,1)S(1)} %get-tuple-element.143), channel_id=1, source_target_pairs={{0,8},{8,0},{16,24},{24,16},{1,9},{9,1},{17,25},{25,17},{2,10},{10... | collective-permute-start | bytes 860168 | tf_op jit(solution)/shard_map/ppermute | solution.py:280
  97.2 2.0 %collective-permute-start.27 = (bf16[2,40,1792]{2,1,0:T(8,128)(2,1)S(1)}, bf16[2,40,1792]{2,1,0:T(8,128)(2,1)S(1)}, u32[]{:S(2)}, u32[]{:S(2)}) collective-permute-start(bf16[2,40,1792]{2,1,0:T(8,128)(2,1)S(1)} %get-tuple-element.152.own_ref), channel_id=1, source_target_pairs={{0,8},{8,0},{16,24},{24,16},{1,9},{9,1},{17,25},{25,17},{2,10},{10... | collective-permute-start | bytes 860168 | tf_op jit(solution)/shard_map/ppermute | solution.py:280
  97.4 16.3 %collective-permute-start.24 = (bf16[2,2,40,1792]{3,2,1,0:T(8,128)(2,1)S(1)}, bf16[2,2,40,1792]{3,2,1,0:T(8,128)(2,1)S(1)}, u32[]{:S(2)}, u32[]{:S(2)}) collective-permute-start(bf16[2,2,40,1792]{3,2,1,0:T(8,128)(2,1)S(1)} %get-tuple-element.147), channel_id=1, source_target_pairs={{0,16},{8,24},{16,0},{24,8},{1,17},{9,25},{17,1},{25,9},{2,18},{10... | collective-permute-start | bytes 1720328 | tf_op jit(solution)/shard_map/ppermute | solution.py:280
  99.0 14.7 %collective-permute-start.26 = (bf16[2,2,40,1792]{3,2,1,0:T(8,128)(2,1)S(1)}, bf16[2,2,40,1792]{3,2,1,0:T(8,128)(2,1)S(1)}, u32[]{:S(2)}, u32[]{:S(2)}) collective-permute-start(bf16[2,2,40,1792]{3,2,1,0:T(8,128)(2,1)S(1)} %get-tuple-element.151), channel_id=1, source_target_pairs={{0,8},{8,0},{16,24},{24,16},{1,9},{9,1},{17,25},{25,17},{2,10},{10... | collective-permute-start | bytes 1720328 | tf_op jit(solution)/shard_map/ppermute | solution.py:280
  103.8 9.2 %collective-permute-start.29 = (bf16[1,40,4096]{2,1,0:T(8,128)(2,1)S(1)}, bf16[1,40,4096]{2,1,0:T(8,128)(2,1)S(1)}, u32[]{:S(2)}, u32[]{:S(2)}) collective-permute-start(bf16[1,40,4096]{2,1,0:T(8,128)(2,1)S(1)} %get-tuple-element.157), channel_id=1, source_target_pairs={{0,1},{1,0},{2,3},{3,2},{4,5},{5,4},{6,7},{7,6},{8,9},{9,8},{10,11... | collective-permute-start | bytes 983048 | tf_op jit(solution)/shard_map/ppermute | solution.py:280
  104.5 17.7 %collective-permute-start.32 = (bf16[2,40,4096]{2,1,0:T(8,128)(2,1)S(1)}, bf16[2,40,4096]{2,1,0:T(8,128)(2,1)S(1)}, u32[]{:S(2)}, u32[]{:S(2)}) collective-permute-start(bf16[2,40,4096]{2,1,0:T(8,128)(2,1)S(1)} %get-tuple-element.171), channel_id=1, source_target_pairs={{0,2},{1,3},{2,0},{3,1},{4,6},{5,7},{6,4},{7,5},{8,10},{9,11},{10,... | collective-permute-start | bytes 1966088 | tf_op jit(solution)/shard_map/ppermute | solution.py:307
  113.1 9.1 %collective-permute-start.31 = (bf16[1,40,4096]{2,1,0:T(8,128)(2,1)S(1)}, bf16[1,40,4096]{2,1,0:T(8,128)(2,1)S(1)}, u32[]{:S(2)}, u32[]{:S(2)}) collective-permute-start(bf16[1,40,4096]{2,1,0:T(8,128)(2,1)S(1)} %get-tuple-element.169), channel_id=1, source_target_pairs={{0,1},{1,0},{2,3},{3,2},{4,5},{5,4},{6,7},{7,6},{8,9},{9,8},{10,11... | collective-permute-start | bytes 983048 | tf_op jit(solution)/shard_map/ppermute | solution.py:280
  114.0 3.1 %collective-permute-start.30 = (bf16[2,40,1792]{2,1,0:T(8,128)(2,1)S(1)}, bf16[2,40,1792]{2,1,0:T(8,128)(2,1)S(1)}, u32[]{:S(2)}, u32[]{:S(2)}) collective-permute-start(bf16[2,40,1792]{2,1,0:T(8,128)(2,1)S(1)} %get-tuple-element.162.own_ref), channel_id=1, source_target_pairs={{0,8},{8,0},{16,24},{24,16},{1,9},{9,1},{17,25},{25,17},{2,10},{10... | collective-permute-start | bytes 860168 | tf_op jit(solution)/shard_map/ppermute | solution.py:280
  114.1 20.6 %collective-permute-start.25 = (bf16[2,2,40,1792]{3,2,1,0:T(8,128)(2,1)S(1)}, bf16[2,2,40,1792]{3,2,1,0:T(8,128)(2,1)S(1)}, u32[]{:S(2)}, u32[]{:S(2)}) collective-permute-start(bf16[2,2,40,1792]{3,2,1,0:T(8,128)(2,1)S(1)} %get-tuple-element.148), channel_id=1, source_target_pairs={{0,16},{8,24},{16,0},{24,8},{1,17},{9,25},{17,1},{25,9},{2,18},{10... | collective-permute-start | bytes 1720328 | tf_op jit(solution)/shard_map/ppermute | solution.py:280
  115.1 14.1 %collective-permute-start.34 = (bf16[1,40,4096]{2,1,0:T(8,128)(2,1)S(1)}, bf16[1,40,4096]{2,1,0:T(8,128)(2,1)S(1)}, u32[]{:S(2)}, u32[]{:S(2)}) collective-permute-start(bf16[1,40,4096]{2,1,0:T(8,128)(2,1)S(1)} %get-tuple-element.168), channel_id=1, source_target_pairs={{0,2},{1,3},{2,0},{3,1},{4,6},{5,7},{6,4},{7,5},{8,10},{9,11},{10,... | collective-permute-start | bytes 983048 | tf_op jit(solution)/shard_map/ppermute | solution.py:307
  122.3 8.3 %collective-permute-start.33 = (bf16[1,40,4096]{2,1,0:T(8,128)(2,1)S(1)}, bf16[1,40,4096]{2,1,0:T(8,128)(2,1)S(1)}, u32[]{:S(2)}, u32[]{:S(2)}) collective-permute-start(bf16[1,40,4096]{2,1,0:T(8,128)(2,1)S(1)} %get-tuple-element.173), channel_id=1, source_target_pairs={{0,1},{1,0},{2,3},{3,2},{4,5},{5,4},{6,7},{7,6},{8,9},{9,8},{10,11... | collective-permute-start | bytes 983048 | tf_op jit(solution)/shard_map/ppermute | solution.py:280
  123.9 11.9 %collective-permute-start.35 = (bf16[1,40,4096]{2,1,0:T(8,128)(2,1)S(1)}, bf16[1,40,4096]{2,1,0:T(8,128)(2,1)S(1)}, u32[]{:S(2)}, u32[]{:S(2)}) collective-permute-start(bf16[1,40,4096]{2,1,0:T(8,128)(2,1)S(1)} %get-tuple-element.172), channel_id=1, source_target_pairs={{0,2},{1,3},{2,0},{3,1},{4,6},{5,7},{6,4},{7,5},{8,10},{9,11},{10,... | collective-permute-start | bytes 983048 | tf_op jit(solution)/shard_map/ppermute | solution.py:307
  130.7 10.8 %collective-permute-start.37 = (bf16[1,40,4096]{2,1,0:T(8,128)(2,1)S(1)}, bf16[1,40,4096]{2,1,0:T(8,128)(2,1)S(1)}, u32[]{:S(2)}, u32[]{:S(2)}) collective-permute-start(bf16[1,40,4096]{2,1,0:T(8,128)(2,1)S(1)} %get-tuple-element.182), channel_id=1, source_target_pairs={{0,1},{1,0},{2,3},{3,2},{4,5},{5,4},{6,7},{7,6},{8,9},{9,8},{10,11... | collective-permute-start | bytes 983048 | tf_op jit(solution)/shard_map/ppermute | solution.py:280
  132.3 13.3 %collective-permute-start.40 = (bf16[1,40,4096]{2,1,0:T(8,128)(2,1)S(1)}, bf16[1,40,4096]{2,1,0:T(8,128)(2,1)S(1)}, u32[]{:S(2)}, u32[]{:S(2)}) collective-permute-start(bf16[1,40,4096]{2,1,0:T(8,128)(2,1)S(1)} %get-tuple-element.181), channel_id=1, source_target_pairs={{0,6},{1,7},{6,0},{7,1},{2,4},{3,5},{4,2},{5,3},{8,14},{9,15},{14,... | collective-permute-start | bytes 983048 | tf_op jit(solution)/shard_map/ppermute | solution.py:307
  136.0 1.6 %collective-permute-start.36 = (bf16[2,40,1792]{2,1,0:T(8,128)(2,1)S(1)}, bf16[2,40,1792]{2,1,0:T(8,128)(2,1)S(1)}, u32[]{:S(2)}, u32[]{:S(2)}) collective-permute-start(bf16[2,40,1792]{2,1,0:T(8,128)(2,1)S(1)} %get-tuple-element.176.own_ref), channel_id=1, source_target_pairs={{0,8},{8,0},{16,24},{24,16},{1,9},{9,1},{17,25},{25,17},{2,10},{10... | collective-permute-start | bytes 860168 | tf_op jit(solution)/shard_map/ppermute | solution.py:280
  141.5 16.8 %collective-permute-start.38 = (bf16[2,40,4096]{2,1,0:T(8,128)(2,1)S(1)}, bf16[2,40,4096]{2,1,0:T(8,128)(2,1)S(1)}, u32[]{:S(2)}, u32[]{:S(2)}) collective-permute-start(bf16[2,40,4096]{2,1,0:T(8,128)(2,1)S(1)} %get-tuple-element.183), channel_id=1, source_target_pairs={{0,1},{1,0},{2,3},{3,2},{4,5},{5,4},{6,7},{7,6},{8,9},{9,8},{10,11... | collective-permute-start | bytes 1966088 | tf_op jit(solution)/shard_map/ppermute | solution.py:280
  143.3 15.3 %collective-permute-start.39 = (bf16[1,40,4096]{2,1,0:T(8,128)(2,1)S(1)}, bf16[1,40,4096]{2,1,0:T(8,128)(2,1)S(1)}, u32[]{:S(2)}, u32[]{:S(2)}) collective-permute-start(bf16[1,40,4096]{2,1,0:T(8,128)(2,1)S(1)} %get-tuple-element.186), channel_id=1, source_target_pairs={{0,6},{1,7},{6,0},{7,1},{2,4},{3,5},{4,2},{5,3},{8,14},{9,15},{14,... | collective-permute-start | bytes 983048 | tf_op jit(solution)/shard_map/ppermute | solution.py:307
  158.5 1.7 %collective-permute-start.41 = (bf16[40,4096]{1,0:T(8,128)(2,1)S(1)}, bf16[40,4096]{1,0:T(8,128)(2,1)S(1)}, u32[]{:S(2)}, u32[]{:S(2)}) collective-permute-start(bf16[40,4096]{1,0:T(8,128)(2,1)S(1)} %fusion.4), channel_id=1, source_target_pairs={{0,8},{8,0},{16,24},{24,16},{1,9},{9,1},{17,25},{25,17},{2,10},{10... | collective-permute-start | bytes 983048 | tf_op jit(solution)/shard_map/ppermute | solution.py:280

commit v9 on v8

--- a/solution.py
+++ b/solution.py
@@ -11,9 +11,9 @@
 CORES = 2
 PLANES = 4
 NEXT = ((0, 1), (1, 0), (2, 3), (3, 2))
+SECOND = ((0, 2), (2, 0), (1, 3), (3, 1))
 MIRROR = ((0, 3), (3, 0), (1, 2), (2, 1))
-ACROSS = ((1, 2), (2, 1))
-OUTWARD = ((1, 0), (2, 3))
+CYCLE = ((0, 2), (2, 3), (3, 1), (1, 0))
 VMEM = 12 * 1024 * 1024
 F32 = jnp.float32
 BF16 = jnp.bfloat16
@@ -123,6 +123,32 @@
 def join(stacks, after):
     rows = sum(part.shape[1] for part in stacks) * CORES * stacks[0].shape[2]
     return rearranged(join_kernel, "join", (rows, stacks[0].shape[3]), stacks, after)
+
+
+def pick_kernel(after_count, place_ref, *refs):
+    inner_ref, outer_ref = refs[:2]
+    picked_ref, token_ref = refs[2 + after_count :]
+    token_ref[...] = jnp.zeros_like(token_ref)
+
+    @pl.when(place_ref[1] == 1)
+    def _():
+        picked_ref[...] = inner_ref[...]
+
+    @pl.when(place_ref[1] == 0)
+    def _():
+        picked_ref[...] = outer_ref[...]
+
+
+def pick(place, on_inner, on_outer, after):
+    return pl.pallas_call(
+        functools.partial(pick_kernel, len(after)),
+        in_specs=[pl.BlockSpec(memory_space=pltpu.SMEM)] + [INSIDE] * 2 + [ANYWHERE] * len(after),
+        out_specs=[INSIDE] * 2,
+        out_shape=[jax.ShapeDtypeStruct(on_inner.shape, BF16), TOKEN],
+        compiler_params=pltpu.CompilerParams(vmem_limit_bytes=VMEM // 2),
+        cost_estimate=as_if(0),
+        name="pick",
+    )(place, on_inner, on_outer, *after)
 
 
 def resident(values):
@@ -286,7 +312,8 @@
     features, width = gate_weight.shape
     row = lax.axis_index("rows")
     core = row % CORES
-    place = jnp.reshape(core, (1,)).astype(jnp.int32)
+    inner = (lax.axis_index("cols") // per_plane) % (PLANES - 1) != 0
+    place = jnp.stack([core, inner.astype(core.dtype)])
 
     normed = rms_normed(tokens, norm_gain)
     def block(step):
@@ -359,76 +386,75 @@
         return summed
 
     next_stacks = [by_plane(first, NEXT), by_plane(second, NEXT)]
-    inner_three = by_plane(mine, ACROSS)
+    three_away = by_plane(mine, MIRROR)
     forward(0, mine)
     up_kept, last[0] = masked(
         up_weight, up_mask, tile_of(features, 256), place, 1, lambda core: 0, last + next_stacks[:1], 0.15
     )
     one_away, last[0] = join(next_stacks, last)
-    inner_two = by_plane(one_away, ACROSS)
     down_kept = []
-    for share in range(2):
+    for share, hint in ((0, 8), (1, 0)):
         part, last[0] = masked(
-            down_weight, down_mask, 2 * BLOCK, place, 2 * CORES, lambda core, share=share: 2 * core + share, last, 8 - 8 * share
+            down_weight, down_mask, 2 * BLOCK, place, 2 * CORES, lambda core, share=share: 2 * core + share, last, hint
         )
         down_kept.append(part)
-    outer_two = by_plane(inner_three, OUTWARD, last)
     forward(1, one_away, [*parts[0][1:], *last])
     multiply_in(0, hint=0)
-    exchange(0, [inner_two, outer_two])
-    exchange_near(0, [inner_two, outer_two])
-    outer_three = by_plane(inner_two, OUTWARD, last)
-    forward(2, inner_two + outer_two, [*parts[1][1:], *last])
+    exchange(0)
+    exchange_near(0)
     to_chips(0, [near[0]])
+    passed, last[0] = pick(place, three_away, mine, last)
+    two_away = by_plane(passed, CYCLE)
+    forward(3, three_away, [*parts[1][1:], *last])
     multiply_in(1)
     exchange(1)
     exchange_near(1)
     to_chips(1, [near[1]])
     send_chips(1)
-    forward(3, inner_three + behind(outer_three, last), [*parts[2][1:], *last])
-    multiply_in(2, after=[outer_three])
+    forward(2, two_away, [*parts[3][1:], *last])
+    multiply_in(3, after=[two_away])
+    exchange(3)
+    exchange_near(3)
+    to_hidden(1)
+    to_chips(3, [near[3]])
+    send_chips(3)
+    multiply_out(1)
+    send_rows(1, parts[2][1:])
+    multiply_in(2, far_parts=2)
     exchange(2)
-    exchange_near(2)
-    to_hidden(1)
-    to_chips(2, [near[2]])
+    to_hidden(3)
+    to_chips(2)
     send_chips(2)
-    multiply_out(1)
-    send_rows(1, parts[3][1:])
-    multiply_in(3, far_parts=2)
-    exchange(3)
-    to_hidden(2)
-    to_chips(3)
-    send_chips(3)
-    exchange_near(3, last)
-    multiply_out(2, pieces=CORES)
-    send_rows(2, rows_in[1, 0][1:], CORES, 1)
+    exchange_near(2, last)
+    multiply_out(3, pieces=CORES)
+    send_rows(3, rows_in[1, 0][1:], CORES, 1)
     one = to_rows(*rows_in[1, 0])
     one_out = by_plane(one, NEXT)
-    two = to_rows(*rows_in[2, 1])
+    three = to_rows(*rows_in[3, 1])
+    send_rows(3, [three], CORES, 0)
+    three_out, two_out = {1: by_plane(three, NEXT)}, {}
+    to_hidden(2)
+    send_chips(0, chip_sums[2])
+    multiply_out(2, pieces=CORES)
+    three = to_rows(*rows_in[3, 0], after=[one_out])
+    three_out[0] = by_plane(three, NEXT)
+    send_rows(2, [three], CORES, 1)
+    two = to_rows(*rows_in[2, 1], three_out[1])
+    two_out[1] = by_plane(two, SECOND)
     send_rows(2, [two], CORES, 0)
-    two_out, three_out = {1: by_plane(two, NEXT)}, {}
-    to_hidden(3)
-    send_chips(0, chip_sums[3])
-    multiply_out(3, pieces=CORES)
-    two = to_rows(*rows_in[2, 0], after=[one_out])
-    two_out[0] = by_plane(two, NEXT)
-    send_rows(3, [two], CORES, 1)
-    three = to_rows(*rows_in[3, 1], two_out[1])
-    three_out[1] = by_plane(three, MIRROR)
-    send_rows(3, [three], CORES, 0)
-    to_hidden(0, [two_out[0]])
+    to_hidden(0, [three_out[0]])
     multiply_out(0)
-    three = to_rows(*rows_in[3, 0], two_out[0])
-    three_out[0] = by_plane(three, MIRROR)
-    send_rows(0, rows_in[3, 0][1:])
-
-    joined = to_rows(three_out[1], one_out, hint=10.0)
+    two = to_rows(*rows_in[2, 0], three_out[0])
+    two_out[0] = by_plane(two, SECOND)
+    send_rows(0, rows_in[2, 0][1:])
+
+    joined = to_rows(two_out[1], one_out, hint=10.0)
 
     def total(piece, *parts):
         whole = [part[piece].astype(F32) for part in rows_in[0, 0]] + [part.astype(F32) for part in parts]
         return sum(whole[1:], whole[0]).astype(BF16)
 
-    mine_now, other = total(0, one_out[0], three_out[0][0]), by_core(total(1, joined[0]))
+    mine_now, other = total(0, one_out[0], two_out[0][0]), by_core(total(1, joined[0]))
     left = jnp.where(core == 0, mine_now, other)
     right = jnp.where(core == 0, other, mine_now)
     return jnp.concatenate([left, right], 1)

time: 162 us -> 169 us (1.043)
  starting transfers between devices: 43.4 us -> 56.8 us
  waiting for transfers between devices: 57.3 us -> 48.5 us
  Pallas kernels: 55.9 us -> 58.8 us
    ppermute x11 -> x9, starting transfers between devices: 18.4 us -> 34.7 us  [by_plane(): return lax.ppermute(behind(values, after), 'cols', pairs)]
    ppermute x11 -> x9, waiting for transfers between devices: 23.8 us -> 12 us  [by_plane(): return lax.ppermute(behind(values, after), 'cols', pairs)]
    ppermute x31, waiting for transfers between devices: 33.4 us -> 36.5 us  [swap(): lax.ppermute(values, axis, [(place, place ^ step) for place in range(size)])]
    ppermute x31, starting transfers between devices: 25 us -> 22.1 us  [swap(): lax.ppermute(values, axis, [(place, place ^ step) for place in range(size)])]
    pallas_call x4, Pallas kernels: 13 us -> 15.4 us  [masked(): pl.pallas_call(functools.partial(mask_kernel, share, rows, len(after)), i...]
  transfers between devices with their start and end apart: 42 -> 40, of which waited for: 20 -> 20; matrix products, arithmetic and copies ran while one was open for 0% -> 0% of each run, Pallas kernels for 35% -> 35%
where the time goes in v9:
time: 169 us; the launch traced here: 168 us
  Pallas kernels  58.8 us (35%)
  starting transfers between devices  56.8 us (34%)
  waiting for transfers between devices  48.5 us (29%)
  other arithmetic  3.97 us (2%)
    ppermute x31, waiting for transfers between devices, swap(): lax.ppermute(values, axis, [(place, place ^ step) for place in range(size)])  36.5 us
    ppermute x9, starting transfers between devices, by_plane(): return lax.ppermute(behind(values, after), 'cols', pairs)  34.7 us
    pallas_call x4, Pallas kernels, gate_up(): pl.pallas_call(functools.partial(gate_up_kernel, len(parts), len(after)),...  24.3 us
    ppermute x31, starting transfers between devices, swap(): lax.ppermute(values, axis, [(place, place ^ step) for place in range(size)])  22.1 us
    pallas_call x4, Pallas kernels, down(): pl.pallas_call(functools.partial(down_kernel, pieces, len(down_kept), len...  15.5 us
    pallas_call x4, Pallas kernels, masked(): pl.pallas_call(functools.partial(mask_kernel, share, rows, len(after)), i...  15.4 us
    ppermute x9, waiting for transfers between devices, by_plane(): return lax.ppermute(behind(values, after), 'cols', pairs)  12 us
  transfers between devices with their start and end apart: 40, of which 20 were waited for; matrix products, arithmetic and copies ran while one was open for 0% of the time, Pallas kernels for 35%

profile of v9, /device:TPU:0, one launch (start us, length us, event | category | flops | bytes accessed | tf_op | source)
XLA Modules:
  0.0 168.5 jit_solution(591867249971661491)
XLA Ops:
  0.0 1.3 fusion
  1.4 1.3 fusion.2
  3.3 2.6 %collective-permute-start.2 = (bf16[40,2048]{1,0:T(8,128)(2,1)S(1)}, bf16[40,2048]{1,0:T(8,128)(2,1)S(1)}, u32[]{:S(2)}, u32[]{:S(2)}) collective-permute-start(bf16[40,2048]{1,0:T(8,128)(2,1)S(1)} %get-tuple-element.185), channel_id=1, source_target_pairs={{0,24},{8,16},{16,8},{24,0},{1,25},{9,17},{17,9},{25,1},{2,26},{10... | collective-permute-start | bytes 491528 | tf_op jit(solution)/shard_map/ppermute | solution.py:306
  6.0 2.1 %collective-permute-start.4 = (bf16[2,1,40,2048]{3,2,1,0:T(8,128)(2,1)S(1)}, bf16[2,1,40,2048]{3,2,1,0:T(8,128)(2,1)S(1)}, u32[]{:S(2)}, u32[]{:S(2)}) collective-permute-start(bf16[2,1,40,2048]{3,2,1,0:T(8,128)(2,1)S(1)} %get-tuple-element.94.refs_0_), channel_id=1, source_target_pairs={{0,2},{1,3},{2,0},{3,1},{4,6},{5,7},{6,4},{7,5},{8,10},{9,11},{10,... | collective-permute-start | bytes 983048 | tf_op jit(solution)/shard_map/ppermute | solution.py:334
  8.2 3.8 %masked.4 = (bf16[2048,1792]{1,0:T(8,128)(2,1)S(1)}, f32[8,128]{1,0:T(8,128)S(1)}) custom-call(s32[2]{0:T(128)S(1)} %pad_add_fusion.core_ref.place_ref, bf16[2048,1792]{1,0:T(8,128)(2,1)} %weight_ref.4, s32[32,28]{1,0:T(8,128)S(1)} %copy-done, f32[8,128]{1,0:T(8,128)S(1)} %get-tuple-element.95.refs_0_), custom_call_target="tpu_custom_call" | custom-call | tf_op jit(solution)/shard_map/masked/pallas_call | solution.py:80
  12.0 2.2 %collective-permute-done.1.refs_0_ = bf16[40,2048]{1,0:T(8,128)(2,1)S(1)} collective-permute-done((bf16[40,2048]{1,0:T(8,128)(2,1)S(1)}, bf16[40,2048]{1,0:T(8,128)(2,1)S(1)}, u32[]{:S(2)}, u32[]{:S(2)}) %collective-permute-start.1) | collective-permute-done | bytes 163872 | tf_op jit(solution)/shard_map/ppermute | solution.py:306
  14.2 1.9 %collective-permute-start.5 = (bf16[2,1,40,2048]{3,2,1,0:T(8,128)(2,1)S(1)}, bf16[2,1,40,2048]{3,2,1,0:T(8,128)(2,1)S(1)}, u32[]{:S(2)}, u32[]{:S(2)}) collective-permute-start(bf16[2,1,40,2048]{3,2,1,0:T(8,128)(2,1)S(1)} %get-tuple-element.97.refs_1_), channel_id=1, source_target_pairs={{0,2},{1,3},{2,0},{3,1},{4,6},{5,7},{6,4},{7,5},{8,10},{9,11},{10,... | collective-permute-start | bytes 983048 | tf_op jit(solution)/shard_map/ppermute | solution.py:334
  16.1 2.5 %collective-permute-start.8 = (bf16[160,2048]{1,0:T(8,128)(2,1)S(1)}, bf16[160,2048]{1,0:T(8,128)(2,1)S(1)}, u32[]{:S(2)}, u32[]{:S(2)}) collective-permute-start(bf16[160,2048]{1,0:T(8,128)(2,1)S(1)} %get-tuple-element.99.refs_0_.refs_1_), channel_id=1, source_target_pairs={{0,6},{1,7},{6,0},{7,1},{2,4},{3,5},{4,2},{5,3},{8,14},{9,15},{14,... | collective-permute-start | bytes 1966088 | tf_op jit(solution)/shard_map/ppermute | solution.py:334
  18.6 1.5 collective-permute-start.3
  20.1 3.8 %masked.5 = (bf16[2048,1792]{1,0:T(8,128)(2,1)S(1)}, f32[8,128]{1,0:T(8,128)S(1)}) custom-call(s32[2]{0:T(128)S(1)} %pad_add_fusion.core_ref.place_ref, bf16[2048,1792]{1,0:T(8,128)(2,1)} %weight_ref.5, s32[32,28]{1,0:T(8,128)S(1)} %copy-done.1, f32[8,128]{1,0:T(8,128)S(1)} %get-tuple-element.101.refs_0_, ...), custom_call_target="tpu_custom_call" | custom-call | flops 172500000 | tf_op jit(solution)/shard_map/masked/pallas_call | solution.py:80
  24.2 3.9 %masked.6 = (bf16[1792,2048]{1,0:T(8,128)(2,1)S(1)}, f32[8,128]{1,0:T(8,128)S(1)}) custom-call(s32[2]{0:T(128)S(1)} %pad_add_fusion.core_ref.place_ref, bf16[1792,8192]{1,0:T(8,128)(2,1)} %weight_ref.7, s32[28,128]{1,0:T(8,128)S(1)} %copy-done.2, f32[8,128]{1,0:T(8,128)S(1)} %get-tuple-element.104.refs_0_), custom_call_target="tpu_custom_call" | custom-call | flops 9200000000 | tf_op jit(solution)/shard_map/masked/pallas_call | solution.py:80
  28.1 3.9 %masked.7 = (bf16[1792,2048]{1,0:T(8,128)(2,1)S(1)}, f32[8,128]{1,0:T(8,128)S(1)}) custom-call(s32[2]{0:T(128)S(1)} %pad_add_fusion.core_ref.place_ref, bf16[1792,8192]{1,0:T(8,128)(2,1)} %weight_ref.7, s32[28,128]{1,0:T(8,128)S(1)} %copy-done.2, f32[8,128]{1,0:T(8,128)S(1)} %get-tuple-element.105.refs_0_), custom_call_target="tpu_custom_call" | custom-call | tf_op jit(solution)/shard_map/masked/pallas_call | solution.py:80
  32.1 2.2 %collective-permute-done.3.refs_1_ = bf16[160,2048]{1,0:T(8,128)(2,1)S(1)} collective-permute-done((bf16[160,2048]{1,0:T(8,128)(2,1)S(1)}, bf16[160,2048]{1,0:T(8,128)(2,1)S(1)}, u32[]{:S(2)}, u32[]{:S(2)}) %collective-permute-start.3) | collective-permute-done | bytes 655392 | tf_op jit(solution)/shard_map/ppermute | solution.py:306
  34.2 1.5 collective-permute-start.10
  35.7 6.1 %gate_up.4 = (bf16[2,2,2,40,1792]{4,3,2,1,0:T(8,128)(2,1)S(1)}, bf16[2,2,40,1792]{3,2,1,0:T(8,128)(2,1)S(1)}, bf16[2,2,1,40,1792]{4,3,2,1,0:T(8,128)(2,1)S(1)}, f32[8,128]{1,0:T(8,128)S(1)}) custom-call(bf16[160,2048]{1,0:T(8,128)(2,1)S(1)} %get-tuple-element.99.refs_0_.refs_1_, bf16[160,2048]{1,0:T(8,128)(2,1)S(1)} %collective-permute-done.3.refs_1_, ...), custom_call_target="tpu_custom_call" | custom-call | tf_op jit(solution)/shard_map/gate_up/pallas_call | solution.py:188
  42.4 1.5 collective-permute-done.6.refs_3_.refs_1_
  43.9 0.8 collective-permute-done.7.refs_1_
  45.5 4.0 %collective-permute-start.9 = (bf16[160,2048]{1,0:T(8,128)(2,1)S(1)}, bf16[160,2048]{1,0:T(8,128)(2,1)S(1)}, u32[]{:S(2)}, u32[]{:S(2)}) collective-permute-start(bf16[160,2048]{1,0:T(8,128)(2,1)S(1)} %get-tuple-element.113), channel_id=1, source_target_pairs={{0,4},{1,5},{4,6},{5,7},{6,2},{7,3},{2,0},{3,1},{8,12},{9,13},{12,... | collective-permute-start | bytes 1966088 | tf_op jit(solution)/shard_map/ppermute | solution.py:334
  49.5 1.5 collective-permute-start.11
  51.0 6.1 %gate_up.5 = (bf16[2,2,2,40,1792]{4,3,2,1,0:T(8,128)(2,1)S(1)}, bf16[2,2,40,1792]{3,2,1,0:T(8,128)(2,1)S(1)}, bf16[2,2,1,40,1792]{4,3,2,1,0:T(8,128)(2,1)S(1)}, f32[8,128]{1,0:T(8,128)S(1)}) custom-call(bf16[160,2048]{1,0:T(8,128)(2,1)S(1)} %get-tuple-element.115.refs_0_, bf16[160,2048]{1,0:T(8,128)(2,1)S(1)} %collective-permute-done.10.refs_1_, ...), custom_call_target="tpu_custom_call" | custom-call | flops 4697620480 | tf_op jit(solution)/shard_map/gate_up/pallas_call | solution.py:188
  57.7 1.5 collective-permute-done.12.refs_1_
  59.2 0.8 collective-permute-done.13.refs_3_.refs_1_
  60.1 1.6 collective-permute-start.15
  62.5 1.7 %collective-permute-done.11.refs_1_ = bf16[160,2048]{1,0:T(8,128)(2,1)S(1)} collective-permute-done((bf16[160,2048]{1,0:T(8,128)(2,1)S(1)}, bf16[160,2048]{1,0:T(8,128)(2,1)S(1)}, u32[]{:S(2)}, u32[]{:S(2)}) %collective-permute-start.11) | collective-permute-done | bytes 655392 | tf_op jit(solution)/shard_map/ppermute | solution.py:306
  64.2 1.7 %collective-permute-start.14 = (bf16[160,2048]{1,0:T(8,128)(2,1)S(1)}, bf16[160,2048]{1,0:T(8,128)(2,1)S(1)}, u32[]{:S(2)}, u32[]{:S(2)}) collective-permute-start(bf16[160,2048]{1,0:T(8,128)(2,1)S(1)} %collective-permute-done.9.refs_5_.refs_0_), channel_id=1, source_target_pairs={{0,1},{1,0},{2,3},{3,2},{4,5},{5,4},{6,7},{7,6},{8,9},{9,8},{10,11... | collective-permute-start | bytes 1966088 | tf_op jit(solution)/shard_map/ppermute | solution.py:306
  65.9 6.1 %gate_up.6 = (bf16[2,2,2,40,1792]{4,3,2,1,0:T(8,128)(2,1)S(1)}, bf16[2,2,40,1792]{3,2,1,0:T(8,128)(2,1)S(1)}, bf16[2,2,1,40,1792]{4,3,2,1,0:T(8,128)(2,1)S(1)}, f32[8,128]{1,0:T(8,128)S(1)}) custom-call(bf16[160,2048]{1,0:T(8,128)(2,1)S(1)} %collective-permute-done.8.refs_0_, bf16[160,2048]{1,0:T(8,128)(2,1)S(1)} %collective-permute-done.11.refs_1_, ...), custom_call_target="tpu_custom_call" | custom-call | flops 4697620480 | tf_op jit(solution)/shard_map/gate_up/pallas_call | solution.py:188
  72.6 2.6 %collective-permute-done.15.refs_2_ = bf16[2,2,40,1792]{3,2,1,0:T(8,128)(2,1)S(1)} collective-permute-done((bf16[2,2,40,1792]{3,2,1,0:T(8,128)(2,1)S(1)}, bf16[2,2,40,1792]{3,2,1,0:T(8,128)(2,1)S(1)}, u32[]{:S(2)}, u32[]{:S(2)}) %collective-permute-start.15) | collective-permute-done | bytes 573472 | tf_op jit(solution)/shard_map/ppermute | solution.py:306
  75.7 1.6 collective-permute-start.21
  77.3 3.9 %down.4 = (bf16[2,40,4096]{2,1,0:T(8,128)(2,1)S(1)}, bf16[2,40,4096]{2,1,0:T(8,128)(2,1)S(1)}, f32[8,128]{1,0:T(8,128)S(1)}) custom-call(bf16[2,40,1792]{2,1,0:T(8,128)(2,1)S(1)} %get-tuple-element.126.own_ref, bf16[2,40,1792]{2,1,0:T(8,128)(2,1)S(1)} %collective-permute-done.16.other_ref, bf16[1792,2048]{1,0:T(8,128)(2,1)S(1)} %get-tuple-element.127.refs_0_, ...), custom_call_target="tpu_custom_call" | custom-call | flops 2348810 | tf_op jit(solution)/shard_map/down/pallas_call | solution.py:230
  81.8 6.1 %gate_up.7 = (bf16[2,2,2,40,1792]{4,3,2,1,0:T(8,128)(2,1)S(1)}, bf16[2,2,40,1792]{3,2,1,0:T(8,128)(2,1)S(1)}, bf16[1,2,1,40,1792]{4,3,2,1,0:T(8,128)(2,1)S(1)}, ...) custom-call(bf16[160,2048]{1,0:T(8,128)(2,1)S(1)} %collective-permute-done.9.refs_5_.refs_0_, ...), custom_call_target="tpu_custom_call" | custom-call | flops 4697620480 | tf_op jit(solution)/shard_map/gate_up/pallas_call | solution.py:188
  88.4 2.7 %collective-permute-done.21.refs_2_ = bf16[2,2,40,1792]{3,2,1,0:T(8,128)(2,1)S(1)} collective-permute-done((bf16[2,2,40,1792]{3,2,1,0:T(8,128)(2,1)S(1)}, bf16[2,2,40,1792]{3,2,1,0:T(8,128)(2,1)S(1)}, u32[]{:S(2)}, u32[]{:S(2)}) %collective-permute-start.21) | collective-permute-done | bytes 573472 | tf_op jit(solution)/shard_map/ppermute | solution.py:306
  92.3 1.5 collective-permute-start.22
  93.7 3.9 %down.5 = (bf16[1,40,4096]{2,1,0:T(8,128)(2,1)S(1)}, bf16[1,40,4096]{2,1,0:T(8,128)(2,1)S(1)}, bf16[1,40,4096]{2,1,0:T(8,128)(2,1)S(1)}, bf16[1,40,4096]{2,1,0:T(8,128)(2,1)S(1)}, f32[8,128]{1,0:T(8,128)S(1)}) custom-call(bf16[2,40,1792]{2,1,0:T(8,128)(2,1)S(1)} %get-tuple-element.146.own_ref, bf16[2,40,1792]{2,1,0:T(8,128)(2,1)S(1)} %collective-permute-done.25.other_ref, ...), custom_call_target="tpu_custom_call" | custom-call | flops 2348810 | tf_op jit(solution)/shard_map/down/pallas_call | solution.py:230
  98.8 10.9 %collective-permute-start.30 = (bf16[2,40,4096]{2,1,0:T(8,128)(2,1)S(1)}, bf16[2,40,4096]{2,1,0:T(8,128)(2,1)S(1)}, u32[]{:S(2)}, u32[]{:S(2)}) collective-permute-start(bf16[2,40,4096]{2,1,0:T(8,128)(2,1)S(1)} %get-tuple-element.165), channel_id=1, source_target_pairs={{0,2},{1,3},{2,0},{3,1},{4,6},{5,7},{6,4},{7,5},{8,10},{9,11},{10,... | collective-permute-start | bytes 1966088 | tf_op jit(solution)/shard_map/ppermute | solution.py:334
  110.7 1.6 collective-permute-start.23
  112.2 8.0 %collective-permute-start.32 = (bf16[1,40,4096]{2,1,0:T(8,128)(2,1)S(1)}, bf16[1,40,4096]{2,1,0:T(8,128)(2,1)S(1)}, u32[]{:S(2)}, u32[]{:S(2)}) collective-permute-start(bf16[1,40,4096]{2,1,0:T(8,128)(2,1)S(1)} %get-tuple-element.162), channel_id=1, source_target_pairs={{0,2},{1,3},{2,0},{3,1},{4,6},{5,7},{6,4},{7,5},{8,10},{9,11},{10,... | collective-permute-start | bytes 983048 | tf_op jit(solution)/shard_map/ppermute | solution.py:334
  120.2 3.9 %down.6 = (bf16[1,40,4096]{2,1,0:T(8,128)(2,1)S(1)}, bf16[1,40,4096]{2,1,0:T(8,128)(2,1)S(1)}, bf16[1,40,4096]{2,1,0:T(8,128)(2,1)S(1)}, bf16[1,40,4096]{2,1,0:T(8,128)(2,1)S(1)}, f32[8,128]{1,0:T(8,128)S(1)}) custom-call(bf16[2,40,1792]{2,1,0:T(8,128)(2,1)S(1)} %get-tuple-element.156.own_ref, bf16[2,40,1792]{2,1,0:T(8,128)(2,1)S(1)} %collective-permute-done.28.other_ref, ...), custom_call_target="tpu_custom_call" | custom-call | flops 2348810 | tf_op jit(solution)/shard_map/down/pallas_call | solution.py:230
  124.1 1.2 collective-permute-done.30.refs_3_.refs_1_
  126.0 2.0 %collective-permute-start.33 = (bf16[1,40,4096]{2,1,0:T(8,128)(2,1)S(1)}, bf16[1,40,4096]{2,1,0:T(8,128)(2,1)S(1)}, u32[]{:S(2)}, u32[]{:S(2)}) collective-permute-start(bf16[1,40,4096]{2,1,0:T(8,128)(2,1)S(1)} %get-tuple-element.166), channel_id=1, source_target_pairs={{0,2},{1,3},{2,0},{3,1},{4,6},{5,7},{6,4},{7,5},{8,10},{9,11},{10,... | collective-permute-start | bytes 983048 | tf_op jit(solution)/shard_map/ppermute | solution.py:334
  128.0 4.3 %collective-permute-done.32.refs_2_ = bf16[1,40,4096]{2,1,0:T(8,128)(2,1)S(1)} collective-permute-done((bf16[1,40,4096]{2,1,0:T(8,128)(2,1)S(1)}, bf16[1,40,4096]{2,1,0:T(8,128)(2,1)S(1)}, u32[]{:S(2)}, u32[]{:S(2)}) %collective-permute-start.32) | collective-permute-done | bytes 327712 | tf_op jit(solution)/shard_map/ppermute | solution.py:334
  132.3 1.5 collective-permute-done.31.refs_1_
  134.5 3.0 %collective-permute-start.38 = (bf16[1,40,4096]{2,1,0:T(8,128)(2,1)S(1)}, bf16[1,40,4096]{2,1,0:T(8,128)(2,1)S(1)}, u32[]{:S(2)}, u32[]{:S(2)}) collective-permute-start(bf16[1,40,4096]{2,1,0:T(8,128)(2,1)S(1)} %get-tuple-element.175), channel_id=1, source_target_pairs={{0,4},{1,5},{4,0},{5,1},{2,6},{3,7},{6,2},{7,3},{8,12},{9,13},{12,... | collective-permute-start | bytes 983048 | tf_op jit(solution)/shard_map/ppermute | solution.py:334
  137.5 5.2 %collective-permute-done.33.refs_4_.refs_2_ = bf16[1,40,4096]{2,1,0:T(8,128)(2,1)S(1)} collective-permute-done((bf16[1,40,4096]{2,1,0:T(8,128)(2,1)S(1)}, bf16[1,40,4096]{2,1,0:T(8,128)(2,1)S(1)}, u32[]{:S(2)}, u32[]{:S(2)}) %collective-permute-start.33) | collective-permute-done | bytes 327712 | tf_op jit(solution)/shard_map/ppermute | solution.py:334
  143.0 1.6 collective-permute-done.34.other_ref
  144.6 3.9 %down.7 = (bf16[2,40,4096]{2,1,0:T(8,128)(2,1)S(1)}, bf16[2,40,4096]{2,1,0:T(8,128)(2,1)S(1)}, f32[8,128]{1,0:T(8,128)S(1)}) custom-call(bf16[2,40,1792]{2,1,0:T(8,128)(2,1)S(1)} %get-tuple-element.170.own_ref, bf16[2,40,1792]{2,1,0:T(8,128)(2,1)S(1)} %collective-permute-done.34.other_ref, bf16[1792,2048]{1,0:T(8,128)(2,1)S(1)} %get-tuple-element.127.refs_0_, ...), custom_call_target="tpu_custom_call" | custom-call | flops 2348810 | tf_op jit(solution)/shard_map/down/pallas_call | solution.py:230
  150.2 15.3 %collective-permute-done.36 = bf16[2,40,4096]{2,1,0:T(8,128)(2,1)S(1)} collective-permute-done((bf16[2,40,4096]{2,1,0:T(8,128)(2,1)S(1)}, bf16[2,40,4096]{2,1,0:T(8,128)(2,1)S(1)}, u32[]{:S(2)}, u32[]{:S(2)}) %collective-permute-start.36) | collective-permute-done | bytes 655392 | tf_op jit(solution)/shard_map/ppermute | solution.py:306
  165.7 1.6 collective-permute-done.39
  167.6 0.9 pad_maximum_fusion
  (78 shorter events, 13.2 us)
Async XLA Ops:
  1.3 6.8 %copy-start = (s32[32,28]{1,0:T(8,128)S(1)}, s32[32,28]{1,0:T(8,128)}, u32[]{:S(2)}) copy-start(s32[32,28]{1,0:T(8,128)} %mask_ref.4) | copy-start | bytes 10756
  2.7 3.2 %collective-permute-start = (bf16[40,2048]{1,0:T(8,128)(2,1)S(1)}, bf16[40,2048]{1,0:T(8,128)(2,1)S(1)}, u32[]{:S(2)}, u32[]{:S(2)}) collective-permute-start(bf16[40,2048]{1,0:T(8,128)(2,1)S(1)} %get-tuple-element.187), channel_id=1, source_target_pairs={{0,8},{8,0},{16,24},{24,16},{1,9},{9,1},{17,25},{25,17},{2,10},{10... | collective-permute-start | bytes 491528 | tf_op jit(solution)/shard_map/ppermute | solution.py:306
  3.3 8.7 %collective-permute-start.2 = (bf16[40,2048]{1,0:T(8,128)(2,1)S(1)}, bf16[40,2048]{1,0:T(8,128)(2,1)S(1)}, u32[]{:S(2)}, u32[]{:S(2)}) collective-permute-start(bf16[40,2048]{1,0:T(8,128)(2,1)S(1)} %get-tuple-element.185), channel_id=1, source_target_pairs={{0,24},{8,16},{16,8},{24,0},{1,25},{9,17},{17,9},{25,1},{2,26},{10... | collective-permute-start | bytes 491528 | tf_op jit(solution)/shard_map/ppermute | solution.py:306
  5.9 8.3 %collective-permute-start.1 = (bf16[40,2048]{1,0:T(8,128)(2,1)S(1)}, bf16[40,2048]{1,0:T(8,128)(2,1)S(1)}, u32[]{:S(2)}, u32[]{:S(2)}) collective-permute-start(bf16[40,2048]{1,0:T(8,128)(2,1)S(1)} %get-tuple-element.186), channel_id=1, source_target_pairs={{0,16},{8,24},{16,0},{24,8},{1,17},{9,25},{17,1},{25,9},{2,18},{10... | collective-permute-start | bytes 491528 | tf_op jit(solution)/shard_map/ppermute | solution.py:306
  6.0 14.2 %collective-permute-start.4 = (bf16[2,1,40,2048]{3,2,1,0:T(8,128)(2,1)S(1)}, bf16[2,1,40,2048]{3,2,1,0:T(8,128)(2,1)S(1)}, u32[]{:S(2)}, u32[]{:S(2)}) collective-permute-start(bf16[2,1,40,2048]{3,2,1,0:T(8,128)(2,1)S(1)} %get-tuple-element.94.refs_0_), channel_id=1, source_target_pairs={{0,2},{1,3},{2,0},{3,1},{4,6},{5,7},{6,4},{7,5},{8,10},{9,11},{10,... | collective-permute-start | bytes 983048 | tf_op jit(solution)/shard_map/ppermute | solution.py:334
  8.2 12.0 %copy-start.1 = (s32[32,28]{1,0:T(8,128)S(1)}, s32[32,28]{1,0:T(8,128)}, u32[]{:S(2)}) copy-start(s32[32,28]{1,0:T(8,128)} %mask_ref.5) | copy-start | bytes 10756
  14.2 10.0 %collective-permute-start.5 = (bf16[2,1,40,2048]{3,2,1,0:T(8,128)(2,1)S(1)}, bf16[2,1,40,2048]{3,2,1,0:T(8,128)(2,1)S(1)}, u32[]{:S(2)}, u32[]{:S(2)}) collective-permute-start(bf16[2,1,40,2048]{3,2,1,0:T(8,128)(2,1)S(1)} %get-tuple-element.97.refs_1_), channel_id=1, source_target_pairs={{0,2},{1,3},{2,0},{3,1},{4,6},{5,7},{6,4},{7,5},{8,10},{9,11},{10,... | collective-permute-start | bytes 983048 | tf_op jit(solution)/shard_map/ppermute | solution.py:334
  16.1 28.8 %collective-permute-start.8 = (bf16[160,2048]{1,0:T(8,128)(2,1)S(1)}, bf16[160,2048]{1,0:T(8,128)(2,1)S(1)}, u32[]{:S(2)}, u32[]{:S(2)}) collective-permute-start(bf16[160,2048]{1,0:T(8,128)(2,1)S(1)} %get-tuple-element.99.refs_0_.refs_1_), channel_id=1, source_target_pairs={{0,6},{1,7},{6,0},{7,1},{2,4},{3,5},{4,2},{5,3},{8,14},{9,15},{14,... | collective-permute-start | bytes 1966088 | tf_op jit(solution)/shard_map/ppermute | solution.py:334
  18.6 15.6 %collective-permute-start.3 = (bf16[160,2048]{1,0:T(8,128)(2,1)S(1)}, bf16[160,2048]{1,0:T(8,128)(2,1)S(1)}, u32[]{:S(2)}, u32[]{:S(2)}) collective-permute-start(bf16[160,2048]{1,0:T(8,128)(2,1)S(1)} %get-tuple-element.99.refs_0_.refs_1_), channel_id=1, source_target_pairs={{0,1},{1,0},{2,3},{3,2},{4,5},{5,4},{6,7},{7,6},{8,9},{9,8},{10,11... | collective-permute-start | bytes 1966088 | tf_op jit(solution)/shard_map/ppermute | solution.py:306
  20.1 4.1 %copy-start.2 = (s32[28,128]{1,0:T(8,128)S(1)}, s32[28,128]{1,0:T(8,128)}, u32[]{:S(2)}) copy-start(s32[28,128]{1,0:T(8,128)} %mask_ref.7) | copy-start | bytes 43012
  34.2 15.3 %collective-permute-start.10 = (bf16[160,2048]{1,0:T(8,128)(2,1)S(1)}, bf16[160,2048]{1,0:T(8,128)(2,1)S(1)}, u32[]{:S(2)}, u32[]{:S(2)}) collective-permute-start(bf16[160,2048]{1,0:T(8,128)(2,1)S(1)} %get-tuple-element.115.refs_0_), channel_id=1, source_target_pairs={{0,1},{1,0},{2,3},{3,2},{4,5},{5,4},{6,7},{7,6},{8,9},{9,8},{10,11... | collective-permute-start | bytes 1966088 | tf_op jit(solution)/shard_map/ppermute | solution.py:306
  41.8 2.0 %collective-permute-start.6 = (bf16[2,2,40,1792]{3,2,1,0:T(8,128)(2,1)S(1)}, bf16[2,2,40,1792]{3,2,1,0:T(8,128)(2,1)S(1)}, u32[]{:S(2)}, u32[]{:S(2)}) collective-permute-start(bf16[2,2,40,1792]{3,2,1,0:T(8,128)(2,1)S(1)} %get-tuple-element.108), channel_id=1, source_target_pairs={{0,8},{8,0},{16,24},{24,16},{1,9},{9,1},{17,25},{25,17},{2,10},{10... | collective-permute-start | bytes 1720328 | tf_op jit(solution)/shard_map/ppermute | solution.py:306
  41.9 2.8 %collective-permute-start.7 = (bf16[2,2,1,40,1792]{4,3,2,1,0:T(8,128)(2,1)S(1)}, bf16[2,2,1,40,1792]{4,3,2,1,0:T(8,128)(2,1)S(1)}, u32[]{:S(2)}, u32[]{:S(2)}) collective-permute-start(bf16[2,2,1,40,1792]{4,3,2,1,0:T(8,128)(2,1)S(1)} %get-tuple-element.109), channel_id=1, source_target_pairs={{0,8},{8,0},{16,24},{24,16},{1,9},{9,1},{17,25},{25,17},{2,10},{10... | collective-permute-start | bytes 1720328 | tf_op jit(solution)/shard_map/ppermute | solution.py:306
  45.5 17.0 %collective-permute-start.9 = (bf16[160,2048]{1,0:T(8,128)(2,1)S(1)}, bf16[160,2048]{1,0:T(8,128)(2,1)S(1)}, u32[]{:S(2)}, u32[]{:S(2)}) collective-permute-start(bf16[160,2048]{1,0:T(8,128)(2,1)S(1)} %get-tuple-element.113), channel_id=1, source_target_pairs={{0,4},{1,5},{4,6},{5,7},{6,2},{7,3},{2,0},{3,1},{8,12},{9,13},{12,... | collective-permute-start | bytes 1966088 | tf_op jit(solution)/shard_map/ppermute | solution.py:334
  49.5 14.7 %collective-permute-start.11 = (bf16[160,2048]{1,0:T(8,128)(2,1)S(1)}, bf16[160,2048]{1,0:T(8,128)(2,1)S(1)}, u32[]{:S(2)}, u32[]{:S(2)}) collective-permute-start(bf16[160,2048]{1,0:T(8,128)(2,1)S(1)} %collective-permute-done.8.refs_0_), channel_id=1, source_target_pairs={{0,1},{1,0},{2,3},{3,2},{4,5},{5,4},{6,7},{7,6},{8,9},{9,8},{10,11... | collective-permute-start | bytes 1966088 | tf_op jit(solution)/shard_map/ppermute | solution.py:306
  57.1 2.0 %collective-permute-start.12 = (bf16[2,2,1,40,1792]{4,3,2,1,0:T(8,128)(2,1)S(1)}, bf16[2,2,1,40,1792]{4,3,2,1,0:T(8,128)(2,1)S(1)}, u32[]{:S(2)}, u32[]{:S(2)}) collective-permute-start(bf16[2,2,1,40,1792]{4,3,2,1,0:T(8,128)(2,1)S(1)} %get-tuple-element.119), channel_id=1, source_target_pairs={{0,8},{8,0},{16,24},{24,16},{1,9},{9,1},{17,25},{25,17},{2,10},{10... | collective-permute-start | bytes 1720328 | tf_op jit(solution)/shard_map/ppermute | solution.py:306
  57.2 2.8 %collective-permute-start.13 = (bf16[2,2,40,1792]{3,2,1,0:T(8,128)(2,1)S(1)}, bf16[2,2,40,1792]{3,2,1,0:T(8,128)(2,1)S(1)}, u32[]{:S(2)}, u32[]{:S(2)}) collective-permute-start(bf16[2,2,40,1792]{3,2,1,0:T(8,128)(2,1)S(1)} %get-tuple-element.121), channel_id=1, source_target_pairs={{0,8},{8,0},{16,24},{24,16},{1,9},{9,1},{17,25},{25,17},{2,10},{10... | collective-permute-start | bytes 1720328 | tf_op jit(solution)/shard_map/ppermute | solution.py:306
  60.1 15.1 %collective-permute-start.15 = (bf16[2,2,40,1792]{3,2,1,0:T(8,128)(2,1)S(1)}, bf16[2,2,40,1792]{3,2,1,0:T(8,128)(2,1)S(1)}, u32[]{:S(2)}, u32[]{:S(2)}) collective-permute-start(bf16[2,2,40,1792]{3,2,1,0:T(8,128)(2,1)S(1)} %get-tuple-element.124), channel_id=1, source_target_pairs={{0,16},{8,24},{16,0},{24,8},{1,17},{9,25},{17,1},{25,9},{2,18},{10... | collective-permute-start | bytes 1720328 | tf_op jit(solution)/shard_map/ppermute | solution.py:306
  64.2 17.0 %collective-permute-start.14 = (bf16[160,2048]{1,0:T(8,128)(2,1)S(1)}, bf16[160,2048]{1,0:T(8,128)(2,1)S(1)}, u32[]{:S(2)}, u32[]{:S(2)}) collective-permute-start(bf16[160,2048]{1,0:T(8,128)(2,1)S(1)} %collective-permute-done.9.refs_5_.refs_0_), channel_id=1, source_target_pairs={{0,1},{1,0},{2,3},{3,2},{4,5},{5,4},{6,7},{7,6},{8,9},{9,8},{10,11... | collective-permute-start | bytes 1966088 | tf_op jit(solution)/shard_map/ppermute | solution.py:306
  72.0 3.5 %collective-permute-start.17 = (bf16[2,2,1,40,1792]{4,3,2,1,0:T(8,128)(2,1)S(1)}, bf16[2,2,1,40,1792]{4,3,2,1,0:T(8,128)(2,1)S(1)}, u32[]{:S(2)}, u32[]{:S(2)}) collective-permute-start(bf16[2,2,1,40,1792]{4,3,2,1,0:T(8,128)(2,1)S(1)} %get-tuple-element.130), channel_id=1, source_target_pairs={{0,8},{8,0},{16,24},{24,16},{1,9},{9,1},{17,25},{25,17},{2,10},{10... | collective-permute-start | bytes 1720328 | tf_op jit(solution)/shard_map/ppermute | solution.py:306
  72.1 3.5 %collective-permute-start.18 = (bf16[2,2,40,1792]{3,2,1,0:T(8,128)(2,1)S(1)}, bf16[2,2,40,1792]{3,2,1,0:T(8,128)(2,1)S(1)}, u32[]{:S(2)}, u32[]{:S(2)}) collective-permute-start(bf16[2,2,40,1792]{3,2,1,0:T(8,128)(2,1)S(1)} %get-tuple-element.132), channel_id=1, source_target_pairs={{0,8},{8,0},{16,24},{24,16},{1,9},{9,1},{17,25},{25,17},{2,10},{10... | collective-permute-start | bytes 1720328 | tf_op jit(solution)/shard_map/ppermute | solution.py:306
  75.5 1.8 %collective-permute-start.16 = (bf16[2,40,1792]{2,1,0:T(8,128)(2,1)S(1)}, bf16[2,40,1792]{2,1,0:T(8,128)(2,1)S(1)}, u32[]{:S(2)}, u32[]{:S(2)}) collective-permute-start(bf16[2,40,1792]{2,1,0:T(8,128)(2,1)S(1)} %get-tuple-element.126.own_ref), channel_id=1, source_target_pairs={{0,8},{8,0},{16,24},{24,16},{1,9},{9,1},{17,25},{25,17},{2,10},{10... | collective-permute-start | bytes 860168 | tf_op jit(solution)/shard_map/ppermute | solution.py:306
  75.7 15.4 %collective-permute-start.21 = (bf16[2,2,40,1792]{3,2,1,0:T(8,128)(2,1)S(1)}, bf16[2,2,40,1792]{3,2,1,0:T(8,128)(2,1)S(1)}, u32[]{:S(2)}, u32[]{:S(2)}) collective-permute-start(bf16[2,2,40,1792]{3,2,1,0:T(8,128)(2,1)S(1)} %get-tuple-element.138), channel_id=1, source_target_pairs={{0,16},{8,24},{16,0},{24,8},{1,17},{9,25},{17,1},{25,9},{2,18},{10... | collective-permute-start | bytes 1720328 | tf_op jit(solution)/shard_map/ppermute | solution.py:306
  81.2 16.9 %collective-permute-start.26 = (bf16[2,40,4096]{2,1,0:T(8,128)(2,1)S(1)}, bf16[2,40,4096]{2,1,0:T(8,128)(2,1)S(1)}, u32[]{:S(2)}, u32[]{:S(2)}) collective-permute-start(bf16[2,40,4096]{2,1,0:T(8,128)(2,1)S(1)} %get-tuple-element.150), channel_id=1, source_target_pairs={{0,1},{1,0},{2,3},{3,2},{4,5},{5,4},{6,7},{7,6},{8,9},{9,8},{10,11... | collective-permute-start | bytes 1966088 | tf_op jit(solution)/shard_map/ppermute | solution.py:306
  87.9 3.7 %collective-permute-start.19 = (bf16[1,2,1,40,1792]{4,3,2,1,0:T(8,128)(2,1)S(1)}, bf16[1,2,1,40,1792]{4,3,2,1,0:T(8,128)(2,1)S(1)}, u32[]{:S(2)}, u32[]{:S(2)}) collective-permute-start(bf16[1,2,1,40,1792]{4,3,2,1,0:T(8,128)(2,1)S(1)} %get-tuple-element.136), channel_id=1, source_target_pairs={{0,8},{8,0},{16,24},{24,16},{1,9},{9,1},{17,25},{25,17},{2,10},{10... | collective-permute-start | bytes 860168 | tf_op jit(solution)/shard_map/ppermute | solution.py:306
  87.9 3.6 %collective-permute-start.20 = (bf16[1,2,1,40,1792]{4,3,2,1,0:T(8,128)(2,1)S(1)}, bf16[1,2,1,40,1792]{4,3,2,1,0:T(8,128)(2,1)S(1)}, u32[]{:S(2)}, u32[]{:S(2)}) collective-permute-start(bf16[1,2,1,40,1792]{4,3,2,1,0:T(8,128)(2,1)S(1)} %get-tuple-element.137), channel_id=1, source_target_pairs={{0,8},{8,0},{16,24},{24,16},{1,9},{9,1},{17,25},{25,17},{2,10},{10... | collective-permute-start | bytes 860168 | tf_op jit(solution)/shard_map/ppermute | solution.py:306
  91.5 2.3 %collective-permute-start.25 = (bf16[2,40,1792]{2,1,0:T(8,128)(2,1)S(1)}, bf16[2,40,1792]{2,1,0:T(8,128)(2,1)S(1)}, u32[]{:S(2)}, u32[]{:S(2)}) collective-permute-start(bf16[2,40,1792]{2,1,0:T(8,128)(2,1)S(1)} %get-tuple-element.146.own_ref), channel_id=1, source_target_pairs={{0,8},{8,0},{16,24},{24,16},{1,9},{9,1},{17,25},{25,17},{2,10},{10... | collective-permute-start | bytes 860168 | tf_op jit(solution)/shard_map/ppermute | solution.py:306
  91.7 18.6 %collective-permute-start.24 = (bf16[2,2,40,1792]{3,2,1,0:T(8,128)(2,1)S(1)}, bf16[2,2,40,1792]{3,2,1,0:T(8,128)(2,1)S(1)}, u32[]{:S(2)}, u32[]{:S(2)}) collective-permute-start(bf16[2,2,40,1792]{3,2,1,0:T(8,128)(2,1)S(1)} %get-tuple-element.145), channel_id=1, source_target_pairs={{0,8},{8,0},{16,24},{24,16},{1,9},{9,1},{17,25},{25,17},{2,10},{10... | collective-permute-start | bytes 1720328 | tf_op jit(solution)/shard_map/ppermute | solution.py:306
  92.3 18.1 %collective-permute-start.22 = (bf16[2,2,40,1792]{3,2,1,0:T(8,128)(2,1)S(1)}, bf16[2,2,40,1792]{3,2,1,0:T(8,128)(2,1)S(1)}, u32[]{:S(2)}, u32[]{:S(2)}) collective-permute-start(bf16[2,2,40,1792]{3,2,1,0:T(8,128)(2,1)S(1)} %get-tuple-element.141), channel_id=1, source_target_pairs={{0,16},{8,24},{16,0},{24,8},{1,17},{9,25},{17,1},{25,9},{2,18},{10... | collective-permute-start | bytes 1720328 | tf_op jit(solution)/shard_map/ppermute | solution.py:306
  98.1 11.6 %collective-permute-start.27 = (bf16[1,40,4096]{2,1,0:T(8,128)(2,1)S(1)}, bf16[1,40,4096]{2,1,0:T(8,128)(2,1)S(1)}, u32[]{:S(2)}, u32[]{:S(2)}) collective-permute-start(bf16[1,40,4096]{2,1,0:T(8,128)(2,1)S(1)} %get-tuple-element.151), channel_id=1, source_target_pairs={{0,1},{1,0},{2,3},{3,2},{4,5},{5,4},{6,7},{7,6},{8,9},{9,8},{10,11... | collective-permute-start | bytes 983048 | tf_op jit(solution)/shard_map/ppermute | solution.py:306
  98.8 26.5 %collective-permute-start.30 = (bf16[2,40,4096]{2,1,0:T(8,128)(2,1)S(1)}, bf16[2,40,4096]{2,1,0:T(8,128)(2,1)S(1)}, u32[]{:S(2)}, u32[]{:S(2)}) collective-permute-start(bf16[2,40,4096]{2,1,0:T(8,128)(2,1)S(1)} %get-tuple-element.165), channel_id=1, source_target_pairs={{0,2},{1,3},{2,0},{3,1},{4,6},{5,7},{6,4},{7,5},{8,10},{9,11},{10,... | collective-permute-start | bytes 1966088 | tf_op jit(solution)/shard_map/ppermute | solution.py:334
  109.7 15.6 %collective-permute-start.29 = (bf16[1,40,4096]{2,1,0:T(8,128)(2,1)S(1)}, bf16[1,40,4096]{2,1,0:T(8,128)(2,1)S(1)}, u32[]{:S(2)}, u32[]{:S(2)}) collective-permute-start(bf16[1,40,4096]{2,1,0:T(8,128)(2,1)S(1)} %get-tuple-element.163), channel_id=1, source_target_pairs={{0,1},{1,0},{2,3},{3,2},{4,5},{5,4},{6,7},{7,6},{8,9},{9,8},{10,11... | collective-permute-start | bytes 983048 | tf_op jit(solution)/shard_map/ppermute | solution.py:306
  110.6 9.6 %collective-permute-start.28 = (bf16[2,40,1792]{2,1,0:T(8,128)(2,1)S(1)}, bf16[2,40,1792]{2,1,0:T(8,128)(2,1)S(1)}, u32[]{:S(2)}, u32[]{:S(2)}) collective-permute-start(bf16[2,40,1792]{2,1,0:T(8,128)(2,1)S(1)} %get-tuple-element.156.own_ref), channel_id=1, source_target_pairs={{0,8},{8,0},{16,24},{24,16},{1,9},{9,1},{17,25},{25,17},{2,10},{10... | collective-permute-start | bytes 860168 | tf_op jit(solution)/shard_map/ppermute | solution.py:306
  110.7 26.8 %collective-permute-start.23 = (bf16[2,2,40,1792]{3,2,1,0:T(8,128)(2,1)S(1)}, bf16[2,2,40,1792]{3,2,1,0:T(8,128)(2,1)S(1)}, u32[]{:S(2)}, u32[]{:S(2)}) collective-permute-start(bf16[2,2,40,1792]{3,2,1,0:T(8,128)(2,1)S(1)} %get-tuple-element.142), channel_id=1, source_target_pairs={{0,16},{8,24},{16,0},{24,8},{1,17},{9,25},{17,1},{25,9},{2,18},{10... | collective-permute-start | bytes 1720328 | tf_op jit(solution)/shard_map/ppermute | solution.py:306
  112.2 20.1 %collective-permute-start.32 = (bf16[1,40,4096]{2,1,0:T(8,128)(2,1)S(1)}, bf16[1,40,4096]{2,1,0:T(8,128)(2,1)S(1)}, u32[]{:S(2)}, u32[]{:S(2)}) collective-permute-start(bf16[1,40,4096]{2,1,0:T(8,128)(2,1)S(1)} %get-tuple-element.162), channel_id=1, source_target_pairs={{0,2},{1,3},{2,0},{3,1},{4,6},{5,7},{6,4},{7,5},{8,10},{9,11},{10,... | collective-permute-start | bytes 983048 | tf_op jit(solution)/shard_map/ppermute | solution.py:334
  125.4 8.4 %collective-permute-start.31 = (bf16[1,40,4096]{2,1,0:T(8,128)(2,1)S(1)}, bf16[1,40,4096]{2,1,0:T(8,128)(2,1)S(1)}, u32[]{:S(2)}, u32[]{:S(2)}) collective-permute-start(bf16[1,40,4096]{2,1,0:T(8,128)(2,1)S(1)} %get-tuple-element.167), channel_id=1, source_target_pairs={{0,1},{1,0},{2,3},{3,2},{4,5},{5,4},{6,7},{7,6},{8,9},{9,8},{10,11... | collective-permute-start | bytes 983048 | tf_op jit(solution)/shard_map/ppermute | solution.py:306
  126.0 16.7 %collective-permute-start.33 = (bf16[1,40,4096]{2,1,0:T(8,128)(2,1)S(1)}, bf16[1,40,4096]{2,1,0:T(8,128)(2,1)S(1)}, u32[]{:S(2)}, u32[]{:S(2)}) collective-permute-start(bf16[1,40,4096]{2,1,0:T(8,128)(2,1)S(1)} %get-tuple-element.166), channel_id=1, source_target_pairs={{0,2},{1,3},{2,0},{3,1},{4,6},{5,7},{6,4},{7,5},{8,10},{9,11},{10,... | collective-permute-start | bytes 983048 | tf_op jit(solution)/shard_map/ppermute | solution.py:334
  133.9 14.5 %collective-permute-start.35 = (bf16[1,40,4096]{2,1,0:T(8,128)(2,1)S(1)}, bf16[1,40,4096]{2,1,0:T(8,128)(2,1)S(1)}, u32[]{:S(2)}, u32[]{:S(2)}) collective-permute-start(bf16[1,40,4096]{2,1,0:T(8,128)(2,1)S(1)} %get-tuple-element.176), channel_id=1, source_target_pairs={{0,1},{1,0},{2,3},{3,2},{4,5},{5,4},{6,7},{7,6},{8,9},{9,8},{10,11... | collective-permute-start | bytes 983048 | tf_op jit(solution)/shard_map/ppermute | solution.py:306
  134.5 15.1 %collective-permute-start.38 = (bf16[1,40,4096]{2,1,0:T(8,128)(2,1)S(1)}, bf16[1,40,4096]{2,1,0:T(8,128)(2,1)S(1)}, u32[]{:S(2)}, u32[]{:S(2)}) collective-permute-start(bf16[1,40,4096]{2,1,0:T(8,128)(2,1)S(1)} %get-tuple-element.175), channel_id=1, source_target_pairs={{0,4},{1,5},{4,0},{5,1},{2,6},{3,7},{6,2},{7,3},{8,12},{9,13},{12,... | collective-permute-start | bytes 983048 | tf_op jit(solution)/shard_map/ppermute | solution.py:334
  143.0 1.6 collective-permute-start.34
  148.6 17.1 %collective-permute-start.37 = (bf16[1,40,4096]{2,1,0:T(8,128)(2,1)S(1)}, bf16[1,40,4096]{2,1,0:T(8,128)(2,1)S(1)}, u32[]{:S(2)}, u32[]{:S(2)}) collective-permute-start(bf16[1,40,4096]{2,1,0:T(8,128)(2,1)S(1)} %get-tuple-element.180), channel_id=1, source_target_pairs={{0,4},{1,5},{4,0},{5,1},{2,6},{3,7},{6,2},{7,3},{8,12},{9,13},{12,... | collective-permute-start | bytes 983048 | tf_op jit(solution)/shard_map/ppermute | solution.py:334
  148.8 16.7 %collective-permute-start.36 = (bf16[2,40,4096]{2,1,0:T(8,128)(2,1)S(1)}, bf16[2,40,4096]{2,1,0:T(8,128)(2,1)S(1)}, u32[]{:S(2)}, u32[]{:S(2)}) collective-permute-start(bf16[2,40,4096]{2,1,0:T(8,128)(2,1)S(1)} %get-tuple-element.177), channel_id=1, source_target_pairs={{0,1},{1,0},{2,3},{3,2},{4,5},{5,4},{6,7},{7,6},{8,9},{9,8},{10,11... | collective-permute-start | bytes 1966088 | tf_op jit(solution)/shard_map/ppermute | solution.py:306
  165.7 1.7 %collective-permute-start.39 = (bf16[40,4096]{1,0:T(8,128)(2,1)S(1)}, bf16[40,4096]{1,0:T(8,128)(2,1)S(1)}, u32[]{:S(2)}, u32[]{:S(2)}) collective-permute-start(bf16[40,4096]{1,0:T(8,128)(2,1)S(1)} %fusion.4), channel_id=1, source_target_pairs={{0,8},{8,0},{16,24},{24,16},{1,9},{9,1},{17,25},{25,17},{2,10},{10... | collective-permute-start | bytes 983048 | tf_op jit(solution)/shard_map/ppermute | solution.py:306

commit v10 on v9

--- a/solution.py
+++ b/solution.py
@@ -12,7 +12,8 @@
 PLANES = 4
 NEXT = ((0, 1), (1, 0), (2, 3), (3, 2))
 SECOND = ((0, 2), (2, 0), (1, 3), (3, 1))
-MIRROR = ((0, 3), (3, 0), (1, 2), (2, 1))
+ACROSS = ((1, 2), (2, 1))
+AROUND = ((0, 3), (3, 0))
 CYCLE = ((0, 2), (2, 3), (3, 1), (1, 0))
 VMEM = 12 * 1024 * 1024
 F32 = jnp.float32
@@ -125,30 +126,31 @@
     return rearranged(join_kernel, "join", (rows, stacks[0].shape[3]), stacks, after)
 
 
-def pick_kernel(after_count, place_ref, *refs):
-    inner_ref, outer_ref = refs[:2]
-    picked_ref, token_ref = refs[2 + after_count :]
+def pick_kernel(after_count, place_ref, inner_three_ref, outer_three_ref, mine_ref, *refs):
+    three_ref, passed_ref, token_ref = refs[after_count:]
     token_ref[...] = jnp.zeros_like(token_ref)
 
     @pl.when(place_ref[1] == 1)
     def _():
-        picked_ref[...] = inner_ref[...]
+        three_ref[...] = inner_three_ref[...]
+        passed_ref[...] = inner_three_ref[...]
 
     @pl.when(place_ref[1] == 0)
     def _():
-        picked_ref[...] = outer_ref[...]
-
-
-def pick(place, on_inner, on_outer, after):
+        three_ref[...] = outer_three_ref[...]
+        passed_ref[...] = mine_ref[...]
+
+
+def pick(place, inner_three, outer_three, mine, after):
     return pl.pallas_call(
         functools.partial(pick_kernel, len(after)),
-        in_specs=[pl.BlockSpec(memory_space=pltpu.SMEM)] + [INSIDE] * 2 + [ANYWHERE] * len(after),
-        out_specs=[INSIDE] * 2,
-        out_shape=[jax.ShapeDtypeStruct(on_inner.shape, BF16), TOKEN],
+        in_specs=[pl.BlockSpec(memory_space=pltpu.SMEM)] + [INSIDE] * 3 + [ANYWHERE] * len(after),
+        out_specs=[INSIDE] * 3,
+        out_shape=[jax.ShapeDtypeStruct(mine.shape, BF16)] * 2 + [TOKEN],
         compiler_params=pltpu.CompilerParams(vmem_limit_bytes=VMEM // 2),
         cost_estimate=as_if(0),
         name="pick",
-    )(place, on_inner, on_outer, *after)
+    )(place, inner_three, outer_three, mine, *after)
 
 
 def resident(values):
@@ -386,12 +388,13 @@
         return summed
 
     next_stacks = [by_plane(first, NEXT), by_plane(second, NEXT)]
-    three_away = by_plane(mine, MIRROR)
+    inner_three = by_plane(mine, ACROSS)
     forward(0, mine)
     up_kept, last[0] = masked(
         up_weight, up_mask, tile_of(features, 256), place, 1, lambda core: 0, last + next_stacks[:1], 0.15
     )
     one_away, last[0] = join(next_stacks, last)
+    outer_three = by_plane(mine, AROUND, [one_away])
     down_kept = []
     for share, hint in ((0, 8), (1, 0)):
         part, last[0] = masked(
@@ -399,11 +402,11 @@
         )
         down_kept.append(part)
     forward(1, one_away, [*parts[0][1:], *last])
-    multiply_in(0, hint=0)
+    multiply_in(0, hint=0, after=[inner_three])
     exchange(0)
     exchange_near(0)
     to_chips(0, [near[0]])
-    passed, last[0] = pick(place, three_away, mine, last)
+    three_away, passed, last[0] = pick(place, inner_three, outer_three, mine, last)
     two_away = by_plane(passed, CYCLE)
     forward(3, three_away, [*parts[1][1:], *last])
     multiply_in(1)
@@ -429,20 +432,20 @@
     multiply_out(3, pieces=CORES)
     send_rows(3, rows_in[1, 0][1:], CORES, 1)
     one = to_rows(*rows_in[1, 0])
-    one_out = by_plane(one, NEXT)
     three = to_rows(*rows_in[3, 1])
     send_rows(3, [three], CORES, 0)
     three_out, two_out = {1: by_plane(three, NEXT)}, {}
     to_hidden(2)
     send_chips(0, chip_sums[2])
     multiply_out(2, pieces=CORES)
-    three = to_rows(*rows_in[3, 0], after=[one_out])
+    three = to_rows(*rows_in[3, 0], after=[three_out[1]])
     three_out[0] = by_plane(three, NEXT)
+    one_out = by_plane(one, NEXT, [three_out[0]])
     send_rows(2, [three], CORES, 1)
-    two = to_rows(*rows_in[2, 1], three_out[1])
+    two = to_rows(*rows_in[2, 1], three_out[1], after=chip_sums[0])
     two_out[1] = by_plane(two, SECOND)
     send_rows(2, [two], CORES, 0)
-    to_hidden(0, [three_out[0]])
+    to_hidden(0)
     multiply_out(0)
     two = to_rows(*rows_in[2, 0], three_out[0])
     two_out[0] = by_plane(two, SECOND)

time: 169 us -> 175 us (1.036)
  waiting for transfers between devices: 48.5 us -> 59.7 us
  starting transfers between devices: 56.8 us -> 51.9 us
    ppermute x9 -> x10, waiting for transfers between devices: 12 us -> 27.7 us  [by_plane(): return lax.ppermute(behind(values, after), 'cols', pairs)]
    ppermute x9 -> x10, starting transfers between devices: 34.7 us -> 27.3 us  [by_plane(): return lax.ppermute(behind(values, after), 'cols', pairs)]
    ppermute x31, waiting for transfers between devices: 36.5 us -> 31.9 us  [swap(): lax.ppermute(values, axis, [(place, place ^ step) for place in range(size)])]
    ppermute x31, starting transfers between devices: 22.1 us -> 24.6 us  [swap(): lax.ppermute(values, axis, [(place, place ^ step) for place in range(size)])]
  transfers between devices with their start and end apart: 40 -> 41, of which waited for: 20 -> 23; matrix products, arithmetic and copies ran while one was open for 0% -> 0% of each run, Pallas kernels for 35% -> 34%
where the time goes in v10:
time: 175 us
  waiting for transfers between devices  59.7 us (34%)
  Pallas kernels  58.9 us (34%)
  starting transfers between devices  51.9 us (30%)
  other arithmetic  3.97 us (2%)
    ppermute x31, waiting for transfers between devices, swap(): lax.ppermute(values, axis, [(place, place ^ step) for place in range(size)])  31.9 us
    ppermute x10, waiting for transfers between devices, by_plane(): return lax.ppermute(behind(values, after), 'cols', pairs)  27.7 us
    ppermute x10, starting transfers between devices, by_plane(): return lax.ppermute(behind(values, after), 'cols', pairs)  27.3 us
    ppermute x31, starting transfers between devices, swap(): lax.ppermute(values, axis, [(place, place ^ step) for place in range(size)])  24.6 us
    pallas_call x4, Pallas kernels, gate_up(): pl.pallas_call(functools.partial(gate_up_kernel, len(parts), len(after)),...  24.3 us
    pallas_call x4, Pallas kernels, down(): pl.pallas_call(functools.partial(down_kernel, pieces, len(down_kept), len...  15.5 us
    pallas_call x4, Pallas kernels, masked(): pl.pallas_call(functools.partial(mask_kernel, share, rows, len(after)), i...  15.4 us
  transfers between devices with their start and end apart: 41, of which 23 were waited for; matrix products, arithmetic and copies ran while one was open for 0% of the time, Pallas kernels for 34%

profile of v10, /device:TPU:0, one launch (start us, length us, event | category | flops | bytes accessed | tf_op | source)
XLA Modules:
  0.0 174.9 jit_solution(13862822128066019473)
XLA Ops:
  0.0 1.3 fusion
  1.4 1.3 fusion.2
  3.3 2.6 %collective-permute-start.2 = (bf16[40,2048]{1,0:T(8,128)(2,1)S(1)}, bf16[40,2048]{1,0:T(8,128)(2,1)S(1)}, u32[]{:S(2)}, u32[]{:S(2)}) collective-permute-start(bf16[40,2048]{1,0:T(8,128)(2,1)S(1)} %get-tuple-element.191), channel_id=1, source_target_pairs={{0,24},{8,16},{16,8},{24,0},{1,25},{9,17},{17,9},{25,1},{2,26},{10... | collective-permute-start | bytes 491528 | tf_op jit(solution)/shard_map/ppermute | solution.py:308
  6.0 2.1 %collective-permute-start.4 = (bf16[2,1,40,2048]{3,2,1,0:T(8,128)(2,1)S(1)}, bf16[2,1,40,2048]{3,2,1,0:T(8,128)(2,1)S(1)}, u32[]{:S(2)}, u32[]{:S(2)}) collective-permute-start(bf16[2,1,40,2048]{3,2,1,0:T(8,128)(2,1)S(1)} %get-tuple-element.97.refs_0_), channel_id=1, source_target_pairs={{0,2},{1,3},{2,0},{3,1},{4,6},{5,7},{6,4},{7,5},{8,10},{9,11},{10,... | collective-permute-start | bytes 983048 | tf_op jit(solution)/shard_map/ppermute | solution.py:336
  8.2 3.8 %masked.4 = (bf16[2048,1792]{1,0:T(8,128)(2,1)S(1)}, f32[8,128]{1,0:T(8,128)S(1)}) custom-call(s32[2]{0:T(128)S(1)} %pad_add_fusion.core_ref.place_ref, bf16[2048,1792]{1,0:T(8,128)(2,1)} %weight_ref.4, s32[32,28]{1,0:T(8,128)S(1)} %copy-done, f32[8,128]{1,0:T(8,128)S(1)} %get-tuple-element.98.refs_0_), custom_call_target="tpu_custom_call" | custom-call | tf_op jit(solution)/shard_map/masked/pallas_call | solution.py:81
  12.0 2.2 %collective-permute-done.1.refs_0_ = bf16[40,2048]{1,0:T(8,128)(2,1)S(1)} collective-permute-done((bf16[40,2048]{1,0:T(8,128)(2,1)S(1)}, bf16[40,2048]{1,0:T(8,128)(2,1)S(1)}, u32[]{:S(2)}, u32[]{:S(2)}) %collective-permute-start.1) | collective-permute-done | bytes 163872 | tf_op jit(solution)/shard_map/ppermute | solution.py:308
  14.2 1.9 %collective-permute-start.5 = (bf16[2,1,40,2048]{3,2,1,0:T(8,128)(2,1)S(1)}, bf16[2,1,40,2048]{3,2,1,0:T(8,128)(2,1)S(1)}, u32[]{:S(2)}, u32[]{:S(2)}) collective-permute-start(bf16[2,1,40,2048]{3,2,1,0:T(8,128)(2,1)S(1)} %get-tuple-element.100.refs_1_), channel_id=1, source_target_pairs={{0,2},{1,3},{2,0},{3,1},{4,6},{5,7},{6,4},{7,5},{8,10},{9,11},{10,... | collective-permute-start | bytes 983048 | tf_op jit(solution)/shard_map/ppermute | solution.py:336
  16.8 1.6 collective-permute-start.3
  18.4 3.8 %masked.5 = (bf16[2048,1792]{1,0:T(8,128)(2,1)S(1)}, f32[8,128]{1,0:T(8,128)S(1)}) custom-call(s32[2]{0:T(128)S(1)} %pad_add_fusion.core_ref.place_ref, bf16[2048,1792]{1,0:T(8,128)(2,1)} %weight_ref.5, s32[32,28]{1,0:T(8,128)S(1)} %copy-done.1, f32[8,128]{1,0:T(8,128)S(1)} %get-tuple-element.104.refs_0_, ...), custom_call_target="tpu_custom_call" | custom-call | flops 172500000 | tf_op jit(solution)/shard_map/masked/pallas_call | solution.py:81
  22.2 1.5 collective-permute-done.5.refs_1_
  23.7 5.4 %collective-permute-start.9 = (bf16[160,2048]{1,0:T(8,128)(2,1)S(1)}, bf16[160,2048]{1,0:T(8,128)(2,1)S(1)}, u32[]{:S(2)}, u32[]{:S(2)}) collective-permute-start(bf16[160,2048]{1,0:T(8,128)(2,1)S(1)} %get-tuple-element.116.refs_0_.mine_ref), channel_id=1, source_target_pairs={{0,6},{1,7},{6,0},{7,1},{8,14},{9,15},{14,8},{15,9},{16,22},{17,23... | collective-permute-start | bytes 1966088 | tf_op jit(solution)/shard_map/ppermute | solution.py:336
  29.2 3.9 %masked.6 = (bf16[1792,2048]{1,0:T(8,128)(2,1)S(1)}, f32[8,128]{1,0:T(8,128)S(1)}) custom-call(s32[2]{0:T(128)S(1)} %pad_add_fusion.core_ref.place_ref, bf16[1792,8192]{1,0:T(8,128)(2,1)} %weight_ref.7, s32[28,128]{1,0:T(8,128)S(1)} %copy-done.2, f32[8,128]{1,0:T(8,128)S(1)} %get-tuple-element.107.refs_0_), custom_call_target="tpu_custom_call" | custom-call | flops 9200000000 | tf_op jit(solution)/shard_map/masked/pallas_call | solution.py:81
  33.1 3.9 %masked.7 = (bf16[1792,2048]{1,0:T(8,128)(2,1)S(1)}, f32[8,128]{1,0:T(8,128)S(1)}) custom-call(s32[2]{0:T(128)S(1)} %pad_add_fusion.core_ref.place_ref, bf16[1792,8192]{1,0:T(8,128)(2,1)} %weight_ref.7, s32[28,128]{1,0:T(8,128)S(1)} %copy-done.2, f32[8,128]{1,0:T(8,128)S(1)} %get-tuple-element.108.refs_0_), custom_call_target="tpu_custom_call" | custom-call | tf_op jit(solution)/shard_map/masked/pallas_call | solution.py:81
  37.0 1.6 collective-permute-start.11
  38.6 6.1 %gate_up.4 = (bf16[2,2,2,40,1792]{4,3,2,1,0:T(8,128)(2,1)S(1)}, bf16[2,2,40,1792]{3,2,1,0:T(8,128)(2,1)S(1)}, bf16[2,2,1,40,1792]{4,3,2,1,0:T(8,128)(2,1)S(1)}, f32[8,128]{1,0:T(8,128)S(1)}) custom-call(bf16[160,2048]{1,0:T(8,128)(2,1)S(1)} %get-tuple-element.116.refs_0_.mine_ref, bf16[160,2048]{1,0:T(8,128)(2,1)S(1)} %collective-permute-done.3.refs_1_, ...), custom_call_target="tpu_custom_call" | custom-call | tf_op jit(solution)/shard_map/gate_up/pallas_call | solution.py:190
  45.3 1.5 collective-permute-done.7.refs_3_.refs_1_
  48.4 12.1 %collective-permute-start.10 = (bf16[160,2048]{1,0:T(8,128)(2,1)S(1)}, bf16[160,2048]{1,0:T(8,128)(2,1)S(1)}, u32[]{:S(2)}, u32[]{:S(2)}) collective-permute-start(bf16[160,2048]{1,0:T(8,128)(2,1)S(1)} %get-tuple-element.118), channel_id=1, source_target_pairs={{0,4},{1,5},{4,6},{5,7},{6,2},{7,3},{2,0},{3,1},{8,12},{9,13},{12,... | collective-permute-start | bytes 1966088 | tf_op jit(solution)/shard_map/ppermute | solution.py:336
  60.5 1.5 collective-permute-start.12
  62.0 6.1 %gate_up.5 = (bf16[2,2,2,40,1792]{4,3,2,1,0:T(8,128)(2,1)S(1)}, bf16[2,2,40,1792]{3,2,1,0:T(8,128)(2,1)S(1)}, bf16[2,2,1,40,1792]{4,3,2,1,0:T(8,128)(2,1)S(1)}, f32[8,128]{1,0:T(8,128)S(1)}) custom-call(bf16[160,2048]{1,0:T(8,128)(2,1)S(1)} %get-tuple-element.120.refs_0_, bf16[160,2048]{1,0:T(8,128)(2,1)S(1)} %collective-permute-done.11.refs_1_, ...), custom_call_target="tpu_custom_call" | custom-call | flops 4697620480 | tf_op jit(solution)/shard_map/gate_up/pallas_call | solution.py:190
  68.7 1.5 collective-permute-done.13.refs_1_
  71.1 1.5 collective-permute-start.16
  72.7 2.1 %collective-permute-done.10.refs_5_.refs_0_ = bf16[160,2048]{1,0:T(8,128)(2,1)S(1)} collective-permute-done((bf16[160,2048]{1,0:T(8,128)(2,1)S(1)}, bf16[160,2048]{1,0:T(8,128)(2,1)S(1)}, u32[]{:S(2)}, u32[]{:S(2)}) %collective-permute-start.10) | collective-permute-done | bytes 655392 | tf_op jit(solution)/shard_map/ppermute | solution.py:336
  74.8 2.2 %collective-permute-done.12.refs_1_ = bf16[160,2048]{1,0:T(8,128)(2,1)S(1)} collective-permute-done((bf16[160,2048]{1,0:T(8,128)(2,1)S(1)}, bf16[160,2048]{1,0:T(8,128)(2,1)S(1)}, u32[]{:S(2)}, u32[]{:S(2)}) %collective-permute-start.12) | collective-permute-done | bytes 655392 | tf_op jit(solution)/shard_map/ppermute | solution.py:308
  77.0 1.5 collective-permute-start.15
  78.5 6.1 %gate_up.6 = (bf16[2,2,2,40,1792]{4,3,2,1,0:T(8,128)(2,1)S(1)}, bf16[2,2,40,1792]{3,2,1,0:T(8,128)(2,1)S(1)}, bf16[2,2,1,40,1792]{4,3,2,1,0:T(8,128)(2,1)S(1)}, f32[8,128]{1,0:T(8,128)S(1)}) custom-call(bf16[160,2048]{1,0:T(8,128)(2,1)S(1)} %get-tuple-element.122.refs_0_, bf16[160,2048]{1,0:T(8,128)(2,1)S(1)} %collective-permute-done.12.refs_1_, ...), custom_call_target="tpu_custom_call" | custom-call | flops 4697620480 | tf_op jit(solution)/shard_map/gate_up/pallas_call | solution.py:190
  87.6 1.5 collective-permute-start.22
  89.2 3.9 %down.4 = (bf16[2,40,4096]{2,1,0:T(8,128)(2,1)S(1)}, bf16[2,40,4096]{2,1,0:T(8,128)(2,1)S(1)}, f32[8,128]{1,0:T(8,128)S(1)}) custom-call(bf16[2,40,1792]{2,1,0:T(8,128)(2,1)S(1)} %get-tuple-element.131.own_ref, bf16[2,40,1792]{2,1,0:T(8,128)(2,1)S(1)} %collective-permute-done.17.other_ref, bf16[1792,2048]{1,0:T(8,128)(2,1)S(1)} %get-tuple-element.132.refs_0_, ...), custom_call_target="tpu_custom_call" | custom-call | flops 2348810 | tf_op jit(solution)/shard_map/down/pallas_call | solution.py:232
  93.1 1.1 collective-permute-start.27
  94.1 6.1 %gate_up.7 = (bf16[2,2,2,40,1792]{4,3,2,1,0:T(8,128)(2,1)S(1)}, bf16[2,2,40,1792]{3,2,1,0:T(8,128)(2,1)S(1)}, bf16[1,2,1,40,1792]{4,3,2,1,0:T(8,128)(2,1)S(1)}, ...) custom-call(bf16[160,2048]{1,0:T(8,128)(2,1)S(1)} %collective-permute-done.10.refs_5_.refs_0_, ...), custom_call_target="tpu_custom_call" | custom-call | flops 4697620480 | tf_op jit(solution)/shard_map/gate_up/pallas_call | solution.py:190
  100.8 1.9 %collective-permute-done.22.refs_2_ = bf16[2,2,40,1792]{3,2,1,0:T(8,128)(2,1)S(1)} collective-permute-done((bf16[2,2,40,1792]{3,2,1,0:T(8,128)(2,1)S(1)}, bf16[2,2,40,1792]{3,2,1,0:T(8,128)(2,1)S(1)}, u32[]{:S(2)}, u32[]{:S(2)}) %collective-permute-start.22) | collective-permute-done | bytes 573472 | tf_op jit(solution)/shard_map/ppermute | solution.py:308
  103.8 1.5 collective-permute-start.23
  105.3 3.9 %down.5 = (bf16[1,40,4096]{2,1,0:T(8,128)(2,1)S(1)}, bf16[1,40,4096]{2,1,0:T(8,128)(2,1)S(1)}, bf16[1,40,4096]{2,1,0:T(8,128)(2,1)S(1)}, bf16[1,40,4096]{2,1,0:T(8,128)(2,1)S(1)}, f32[8,128]{1,0:T(8,128)S(1)}) custom-call(bf16[2,40,1792]{2,1,0:T(8,128)(2,1)S(1)} %get-tuple-element.151.own_ref, bf16[2,40,1792]{2,1,0:T(8,128)(2,1)S(1)} %collective-permute-done.26.other_ref, ...), custom_call_target="tpu_custom_call" | custom-call | flops 2348810 | tf_op jit(solution)/shard_map/down/pallas_call | solution.py:232
  110.3 8.3 %collective-permute-done.28.refs_1_ = bf16[1,40,4096]{2,1,0:T(8,128)(2,1)S(1)} collective-permute-done((bf16[1,40,4096]{2,1,0:T(8,128)(2,1)S(1)}, bf16[1,40,4096]{2,1,0:T(8,128)(2,1)S(1)}, u32[]{:S(2)}, u32[]{:S(2)}) %collective-permute-start.28) | collective-permute-done | bytes 327712 | tf_op jit(solution)/shard_map/ppermute | solution.py:308
  119.7 1.6 collective-permute-done.29.other_ref
  121.2 3.9 %down.6 = (bf16[1,40,4096]{2,1,0:T(8,128)(2,1)S(1)}, bf16[1,40,4096]{2,1,0:T(8,128)(2,1)S(1)}, bf16[1,40,4096]{2,1,0:T(8,128)(2,1)S(1)}, bf16[1,40,4096]{2,1,0:T(8,128)(2,1)S(1)}, f32[8,128]{1,0:T(8,128)S(1)}) custom-call(bf16[2,40,1792]{2,1,0:T(8,128)(2,1)S(1)} %get-tuple-element.161.own_ref, bf16[2,40,1792]{2,1,0:T(8,128)(2,1)S(1)} %collective-permute-done.29.other_ref, ...), custom_call_target="tpu_custom_call" | custom-call | flops 2348810 | tf_op jit(solution)/shard_map/down/pallas_call | solution.py:232
  125.1 1.7 collective-permute-done.30.refs_1_
  127.5 1.7 collective-permute-start.24
  129.2 1.5 collective-permute-start.32
  130.7 4.6 %collective-permute-done.36.refs_2_ = bf16[1,40,4096]{2,1,0:T(8,128)(2,1)S(1)} collective-permute-done((bf16[1,40,4096]{2,1,0:T(8,128)(2,1)S(1)}, bf16[1,40,4096]{2,1,0:T(8,128)(2,1)S(1)}, u32[]{:S(2)}, u32[]{:S(2)}) %collective-permute-start.36) | collective-permute-done | bytes 327712 | tf_op jit(solution)/shard_map/ppermute | solution.py:336
  135.3 1.7 collective-permute-start.37
  137.0 5.0 %collective-permute-done.24.refs_4_.refs_2_ = bf16[2,2,40,1792]{3,2,1,0:T(8,128)(2,1)S(1)} collective-permute-done((bf16[2,2,40,1792]{3,2,1,0:T(8,128)(2,1)S(1)}, bf16[2,2,40,1792]{3,2,1,0:T(8,128)(2,1)S(1)}, u32[]{:S(2)}, u32[]{:S(2)}) %collective-permute-start.24) | collective-permute-done | bytes 573472 | tf_op jit(solution)/shard_map/ppermute | solution.py:308
  142.2 1.6 collective-permute-start.34
  143.7 1.2 collective-permute-start.39
  145.3 1.6 collective-permute-done.33.other_ref
  146.8 3.9 %down.7 = (bf16[2,40,4096]{2,1,0:T(8,128)(2,1)S(1)}, bf16[2,40,4096]{2,1,0:T(8,128)(2,1)S(1)}, f32[8,128]{1,0:T(8,128)S(1)}) custom-call(bf16[2,40,1792]{2,1,0:T(8,128)(2,1)S(1)} %get-tuple-element.174.own_ref, bf16[2,40,1792]{2,1,0:T(8,128)(2,1)S(1)} %collective-permute-done.33.other_ref, bf16[1792,2048]{1,0:T(8,128)(2,1)S(1)} %get-tuple-element.132.refs_0_, ...), custom_call_target="tpu_custom_call" | custom-call | flops 2348810 | tf_op jit(solution)/shard_map/down/pallas_call | solution.py:232
  150.9 1.8 %collective-permute-start.38 = (bf16[1,40,4096]{2,1,0:T(8,128)(2,1)S(1)}, bf16[1,40,4096]{2,1,0:T(8,128)(2,1)S(1)}, u32[]{:S(2)}, u32[]{:S(2)}) collective-permute-start(bf16[1,40,4096]{2,1,0:T(8,128)(2,1)S(1)} %get-tuple-element.186), channel_id=1, source_target_pairs={{0,4},{1,5},{4,0},{5,1},{2,6},{3,7},{6,2},{7,3},{8,12},{9,13},{12,... | collective-permute-start | bytes 983048 | tf_op jit(solution)/shard_map/ppermute | solution.py:336
  153.2 14.8 %collective-permute-done.39.refs_0_ = bf16[1,40,4096]{2,1,0:T(8,128)(2,1)S(1)} collective-permute-done((bf16[1,40,4096]{2,1,0:T(8,128)(2,1)S(1)}, bf16[1,40,4096]{2,1,0:T(8,128)(2,1)S(1)}, u32[]{:S(2)}, u32[]{:S(2)}) %collective-permute-start.39) | collective-permute-done | bytes 327712 | tf_op jit(solution)/shard_map/ppermute | solution.py:336
  169.3 4.4 %collective-permute-done.38 = bf16[1,40,4096]{2,1,0:T(8,128)(2,1)S(1)} collective-permute-done((bf16[1,40,4096]{2,1,0:T(8,128)(2,1)S(1)}, bf16[1,40,4096]{2,1,0:T(8,128)(2,1)S(1)}, u32[]{:S(2)}, u32[]{:S(2)}) %collective-permute-start.38) | collective-permute-done | bytes 327712 | tf_op jit(solution)/shard_map/ppermute | solution.py:336
  (80 shorter events, 16.3 us)
Async XLA Ops:
  1.3 6.8 %copy-start = (s32[32,28]{1,0:T(8,128)S(1)}, s32[32,28]{1,0:T(8,128)}, u32[]{:S(2)}) copy-start(s32[32,28]{1,0:T(8,128)} %mask_ref.4) | copy-start | bytes 10756
  2.7 3.2 %collective-permute-start = (bf16[40,2048]{1,0:T(8,128)(2,1)S(1)}, bf16[40,2048]{1,0:T(8,128)(2,1)S(1)}, u32[]{:S(2)}, u32[]{:S(2)}) collective-permute-start(bf16[40,2048]{1,0:T(8,128)(2,1)S(1)} %get-tuple-element.193), channel_id=1, source_target_pairs={{0,8},{8,0},{16,24},{24,16},{1,9},{9,1},{17,25},{25,17},{2,10},{10... | collective-permute-start | bytes 491528 | tf_op jit(solution)/shard_map/ppermute | solution.py:308
  3.3 8.7 %collective-permute-start.2 = (bf16[40,2048]{1,0:T(8,128)(2,1)S(1)}, bf16[40,2048]{1,0:T(8,128)(2,1)S(1)}, u32[]{:S(2)}, u32[]{:S(2)}) collective-permute-start(bf16[40,2048]{1,0:T(8,128)(2,1)S(1)} %get-tuple-element.191), channel_id=1, source_target_pairs={{0,24},{8,16},{16,8},{24,0},{1,25},{9,17},{17,9},{25,1},{2,26},{10... | collective-permute-start | bytes 491528 | tf_op jit(solution)/shard_map/ppermute | solution.py:308
  5.9 8.3 %collective-permute-start.1 = (bf16[40,2048]{1,0:T(8,128)(2,1)S(1)}, bf16[40,2048]{1,0:T(8,128)(2,1)S(1)}, u32[]{:S(2)}, u32[]{:S(2)}) collective-permute-start(bf16[40,2048]{1,0:T(8,128)(2,1)S(1)} %get-tuple-element.192), channel_id=1, source_target_pairs={{0,16},{8,24},{16,0},{24,8},{1,17},{9,25},{17,1},{25,9},{2,18},{10... | collective-permute-start | bytes 491528 | tf_op jit(solution)/shard_map/ppermute | solution.py:308
  6.0 12.4 %collective-permute-start.4 = (bf16[2,1,40,2048]{3,2,1,0:T(8,128)(2,1)S(1)}, bf16[2,1,40,2048]{3,2,1,0:T(8,128)(2,1)S(1)}, u32[]{:S(2)}, u32[]{:S(2)}) collective-permute-start(bf16[2,1,40,2048]{3,2,1,0:T(8,128)(2,1)S(1)} %get-tuple-element.97.refs_0_), channel_id=1, source_target_pairs={{0,2},{1,3},{2,0},{3,1},{4,6},{5,7},{6,4},{7,5},{8,10},{9,11},{10,... | collective-permute-start | bytes 983048 | tf_op jit(solution)/shard_map/ppermute | solution.py:336
  8.2 10.2 %copy-start.1 = (s32[32,28]{1,0:T(8,128)S(1)}, s32[32,28]{1,0:T(8,128)}, u32[]{:S(2)}) copy-start(s32[32,28]{1,0:T(8,128)} %mask_ref.5) | copy-start | bytes 10756
  14.2 9.5 %collective-permute-start.5 = (bf16[2,1,40,2048]{3,2,1,0:T(8,128)(2,1)S(1)}, bf16[2,1,40,2048]{3,2,1,0:T(8,128)(2,1)S(1)}, u32[]{:S(2)}, u32[]{:S(2)}) collective-permute-start(bf16[2,1,40,2048]{3,2,1,0:T(8,128)(2,1)S(1)} %get-tuple-element.100.refs_1_), channel_id=1, source_target_pairs={{0,2},{1,3},{2,0},{3,1},{4,6},{5,7},{6,4},{7,5},{8,10},{9,11},{10,... | collective-permute-start | bytes 983048 | tf_op jit(solution)/shard_map/ppermute | solution.py:336
  16.1 22.5 %collective-permute-start.6 = (bf16[160,2048]{1,0:T(8,128)(2,1)S(1)}, bf16[160,2048]{1,0:T(8,128)(2,1)S(1)}, u32[]{:S(2)}, u32[]{:S(2)}) collective-permute-start(bf16[160,2048]{1,0:T(8,128)(2,1)S(1)} %get-tuple-element.116.refs_0_.mine_ref), channel_id=1, source_target_pairs={{2,4},{3,5},{4,2},{5,3},{10,12},{11,13},{12,10},{13,11},{18,20},{1... | collective-permute-start | bytes 1966088 | tf_op jit(solution)/shard_map/ppermute | solution.py:336
  16.8 20.2 %collective-permute-start.3 = (bf16[160,2048]{1,0:T(8,128)(2,1)S(1)}, bf16[160,2048]{1,0:T(8,128)(2,1)S(1)}, u32[]{:S(2)}, u32[]{:S(2)}) collective-permute-start(bf16[160,2048]{1,0:T(8,128)(2,1)S(1)} %get-tuple-element.116.refs_0_.mine_ref), channel_id=1, source_target_pairs={{0,1},{1,0},{2,3},{3,2},{4,5},{5,4},{6,7},{7,6},{8,9},{9,8},{10,11... | collective-permute-start | bytes 1966088 | tf_op jit(solution)/shard_map/ppermute | solution.py:308
  18.4 10.8 %copy-start.2 = (s32[28,128]{1,0:T(8,128)S(1)}, s32[28,128]{1,0:T(8,128)}, u32[]{:S(2)}) copy-start(s32[28,128]{1,0:T(8,128)} %mask_ref.7) | copy-start | bytes 43012
  23.7 24.0 %collective-permute-start.9 = (bf16[160,2048]{1,0:T(8,128)(2,1)S(1)}, bf16[160,2048]{1,0:T(8,128)(2,1)S(1)}, u32[]{:S(2)}, u32[]{:S(2)}) collective-permute-start(bf16[160,2048]{1,0:T(8,128)(2,1)S(1)} %get-tuple-element.116.refs_0_.mine_ref), channel_id=1, source_target_pairs={{0,6},{1,7},{6,0},{7,1},{8,14},{9,15},{14,8},{15,9},{16,22},{17,23... | collective-permute-start | bytes 1966088 | tf_op jit(solution)/shard_map/ppermute | solution.py:336
  37.0 23.5 %collective-permute-start.11 = (bf16[160,2048]{1,0:T(8,128)(2,1)S(1)}, bf16[160,2048]{1,0:T(8,128)(2,1)S(1)}, u32[]{:S(2)}, u32[]{:S(2)}) collective-permute-start(bf16[160,2048]{1,0:T(8,128)(2,1)S(1)} %get-tuple-element.120.refs_0_), channel_id=1, source_target_pairs={{0,1},{1,0},{2,3},{3,2},{4,5},{5,4},{6,7},{7,6},{8,9},{9,8},{10,11... | collective-permute-start | bytes 1966088 | tf_op jit(solution)/shard_map/ppermute | solution.py:308
  44.7 2.0 %collective-permute-start.7 = (bf16[2,2,40,1792]{3,2,1,0:T(8,128)(2,1)S(1)}, bf16[2,2,40,1792]{3,2,1,0:T(8,128)(2,1)S(1)}, u32[]{:S(2)}, u32[]{:S(2)}) collective-permute-start(bf16[2,2,40,1792]{3,2,1,0:T(8,128)(2,1)S(1)} %get-tuple-element.111), channel_id=1, source_target_pairs={{0,8},{8,0},{16,24},{24,16},{1,9},{9,1},{17,25},{25,17},{2,10},{10... | collective-permute-start | bytes 1720328 | tf_op jit(solution)/shard_map/ppermute | solution.py:308
  44.8 2.8 %collective-permute-start.8 = (bf16[2,2,1,40,1792]{4,3,2,1,0:T(8,128)(2,1)S(1)}, bf16[2,2,1,40,1792]{4,3,2,1,0:T(8,128)(2,1)S(1)}, u32[]{:S(2)}, u32[]{:S(2)}) collective-permute-start(bf16[2,2,1,40,1792]{4,3,2,1,0:T(8,128)(2,1)S(1)} %get-tuple-element.112), channel_id=1, source_target_pairs={{0,8},{8,0},{16,24},{24,16},{1,9},{9,1},{17,25},{25,17},{2,10},{10... | collective-permute-start | bytes 1720328 | tf_op jit(solution)/shard_map/ppermute | solution.py:308
  48.4 26.4 %collective-permute-start.10 = (bf16[160,2048]{1,0:T(8,128)(2,1)S(1)}, bf16[160,2048]{1,0:T(8,128)(2,1)S(1)}, u32[]{:S(2)}, u32[]{:S(2)}) collective-permute-start(bf16[160,2048]{1,0:T(8,128)(2,1)S(1)} %get-tuple-element.118), channel_id=1, source_target_pairs={{0,4},{1,5},{4,6},{5,7},{6,2},{7,3},{2,0},{3,1},{8,12},{9,13},{12,... | collective-permute-start | bytes 1966088 | tf_op jit(solution)/shard_map/ppermute | solution.py:336
  60.5 16.5 %collective-permute-start.12 = (bf16[160,2048]{1,0:T(8,128)(2,1)S(1)}, bf16[160,2048]{1,0:T(8,128)(2,1)S(1)}, u32[]{:S(2)}, u32[]{:S(2)}) collective-permute-start(bf16[160,2048]{1,0:T(8,128)(2,1)S(1)} %get-tuple-element.122.refs_0_), channel_id=1, source_target_pairs={{0,1},{1,0},{2,3},{3,2},{4,5},{5,4},{6,7},{7,6},{8,9},{9,8},{10,11... | collective-permute-start | bytes 1966088 | tf_op jit(solution)/shard_map/ppermute | solution.py:308
  68.1 2.0 %collective-permute-start.13 = (bf16[2,2,1,40,1792]{4,3,2,1,0:T(8,128)(2,1)S(1)}, bf16[2,2,1,40,1792]{4,3,2,1,0:T(8,128)(2,1)S(1)}, u32[]{:S(2)}, u32[]{:S(2)}) collective-permute-start(bf16[2,2,1,40,1792]{4,3,2,1,0:T(8,128)(2,1)S(1)} %get-tuple-element.124), channel_id=1, source_target_pairs={{0,8},{8,0},{16,24},{24,16},{1,9},{9,1},{17,25},{25,17},{2,10},{10... | collective-permute-start | bytes 1720328 | tf_op jit(solution)/shard_map/ppermute | solution.py:308
  68.2 2.8 %collective-permute-start.14 = (bf16[2,2,40,1792]{3,2,1,0:T(8,128)(2,1)S(1)}, bf16[2,2,40,1792]{3,2,1,0:T(8,128)(2,1)S(1)}, u32[]{:S(2)}, u32[]{:S(2)}) collective-permute-start(bf16[2,2,40,1792]{3,2,1,0:T(8,128)(2,1)S(1)} %get-tuple-element.126), channel_id=1, source_target_pairs={{0,8},{8,0},{16,24},{24,16},{1,9},{9,1},{17,25},{25,17},{2,10},{10... | collective-permute-start | bytes 1720328 | tf_op jit(solution)/shard_map/ppermute | solution.py:308
  71.1 15.1 %collective-permute-start.16 = (bf16[2,2,40,1792]{3,2,1,0:T(8,128)(2,1)S(1)}, bf16[2,2,40,1792]{3,2,1,0:T(8,128)(2,1)S(1)}, u32[]{:S(2)}, u32[]{:S(2)}) collective-permute-start(bf16[2,2,40,1792]{3,2,1,0:T(8,128)(2,1)S(1)} %get-tuple-element.129), channel_id=1, source_target_pairs={{0,16},{8,24},{16,0},{24,8},{1,17},{9,25},{17,1},{25,9},{2,18},{10... | collective-permute-start | bytes 1720328 | tf_op jit(solution)/shard_map/ppermute | solution.py:308
  77.0 16.1 %collective-permute-start.15 = (bf16[160,2048]{1,0:T(8,128)(2,1)S(1)}, bf16[160,2048]{1,0:T(8,128)(2,1)S(1)}, u32[]{:S(2)}, u32[]{:S(2)}) collective-permute-start(bf16[160,2048]{1,0:T(8,128)(2,1)S(1)} %collective-permute-done.10.refs_5_.refs_0_), channel_id=1, source_target_pairs={{0,1},{1,0},{2,3},{3,2},{4,5},{5,4},{6,7},{7,6},{8,9},{9,8},{10,11... | collective-permute-start | bytes 1966088 | tf_op jit(solution)/shard_map/ppermute | solution.py:308
  84.6 2.0 %collective-permute-start.18 = (bf16[2,2,1,40,1792]{4,3,2,1,0:T(8,128)(2,1)S(1)}, bf16[2,2,1,40,1792]{4,3,2,1,0:T(8,128)(2,1)S(1)}, u32[]{:S(2)}, u32[]{:S(2)}) collective-permute-start(bf16[2,2,1,40,1792]{4,3,2,1,0:T(8,128)(2,1)S(1)} %get-tuple-element.135), channel_id=1, source_target_pairs={{0,8},{8,0},{16,24},{24,16},{1,9},{9,1},{17,25},{25,17},{2,10},{10... | collective-permute-start | bytes 1720328 | tf_op jit(solution)/shard_map/ppermute | solution.py:308
  84.7 2.8 %collective-permute-start.19 = (bf16[2,2,40,1792]{3,2,1,0:T(8,128)(2,1)S(1)}, bf16[2,2,40,1792]{3,2,1,0:T(8,128)(2,1)S(1)}, u32[]{:S(2)}, u32[]{:S(2)}) collective-permute-start(bf16[2,2,40,1792]{3,2,1,0:T(8,128)(2,1)S(1)} %get-tuple-element.137), channel_id=1, source_target_pairs={{0,8},{8,0},{16,24},{24,16},{1,9},{9,1},{17,25},{25,17},{2,10},{10... | collective-permute-start | bytes 1720328 | tf_op jit(solution)/shard_map/ppermute | solution.py:308
  86.5 2.7 %collective-permute-start.17 = (bf16[2,40,1792]{2,1,0:T(8,128)(2,1)S(1)}, bf16[2,40,1792]{2,1,0:T(8,128)(2,1)S(1)}, u32[]{:S(2)}, u32[]{:S(2)}) collective-permute-start(bf16[2,40,1792]{2,1,0:T(8,128)(2,1)S(1)} %get-tuple-element.131.own_ref), channel_id=1, source_target_pairs={{0,8},{8,0},{16,24},{24,16},{1,9},{9,1},{17,25},{25,17},{2,10},{10... | collective-permute-start | bytes 860168 | tf_op jit(solution)/shard_map/ppermute | solution.py:308
  87.6 15.1 %collective-permute-start.22 = (bf16[2,2,40,1792]{3,2,1,0:T(8,128)(2,1)S(1)}, bf16[2,2,40,1792]{3,2,1,0:T(8,128)(2,1)S(1)}, u32[]{:S(2)}, u32[]{:S(2)}) collective-permute-start(bf16[2,2,40,1792]{3,2,1,0:T(8,128)(2,1)S(1)} %get-tuple-element.143), channel_id=1, source_target_pairs={{0,16},{8,24},{16,0},{24,8},{1,17},{9,25},{17,1},{25,9},{2,18},{10... | collective-permute-start | bytes 1720328 | tf_op jit(solution)/shard_map/ppermute | solution.py:308
  93.1 16.5 %collective-permute-start.27 = (bf16[2,40,4096]{2,1,0:T(8,128)(2,1)S(1)}, bf16[2,40,4096]{2,1,0:T(8,128)(2,1)S(1)}, u32[]{:S(2)}, u32[]{:S(2)}) collective-permute-start(bf16[2,40,4096]{2,1,0:T(8,128)(2,1)S(1)} %get-tuple-element.155), channel_id=1, source_target_pairs={{0,1},{1,0},{2,3},{3,2},{4,5},{5,4},{6,7},{7,6},{8,9},{9,8},{10,11... | collective-permute-start | bytes 1966088 | tf_op jit(solution)/shard_map/ppermute | solution.py:308
  100.2 2.8 %collective-permute-start.20 = (bf16[1,2,1,40,1792]{4,3,2,1,0:T(8,128)(2,1)S(1)}, bf16[1,2,1,40,1792]{4,3,2,1,0:T(8,128)(2,1)S(1)}, u32[]{:S(2)}, u32[]{:S(2)}) collective-permute-start(bf16[1,2,1,40,1792]{4,3,2,1,0:T(8,128)(2,1)S(1)} %get-tuple-element.141), channel_id=1, source_target_pairs={{0,8},{8,0},{16,24},{24,16},{1,9},{9,1},{17,25},{25,17},{2,10},{10... | collective-permute-start | bytes 860168 | tf_op jit(solution)/shard_map/ppermute | solution.py:308
  100.3 2.8 %collective-permute-start.21 = (bf16[1,2,1,40,1792]{4,3,2,1,0:T(8,128)(2,1)S(1)}, bf16[1,2,1,40,1792]{4,3,2,1,0:T(8,128)(2,1)S(1)}, u32[]{:S(2)}, u32[]{:S(2)}) collective-permute-start(bf16[1,2,1,40,1792]{4,3,2,1,0:T(8,128)(2,1)S(1)} %get-tuple-element.142), channel_id=1, source_target_pairs={{0,8},{8,0},{16,24},{24,16},{1,9},{9,1},{17,25},{25,17},{2,10},{10... | collective-permute-start | bytes 860168 | tf_op jit(solution)/shard_map/ppermute | solution.py:308
  103.0 2.3 %collective-permute-start.26 = (bf16[2,40,1792]{2,1,0:T(8,128)(2,1)S(1)}, bf16[2,40,1792]{2,1,0:T(8,128)(2,1)S(1)}, u32[]{:S(2)}, u32[]{:S(2)}) collective-permute-start(bf16[2,40,1792]{2,1,0:T(8,128)(2,1)S(1)} %get-tuple-element.151.own_ref), channel_id=1, source_target_pairs={{0,8},{8,0},{16,24},{24,16},{1,9},{9,1},{17,25},{25,17},{2,10},{10... | collective-permute-start | bytes 860168 | tf_op jit(solution)/shard_map/ppermute | solution.py:308
  103.2 16.1 %collective-permute-start.25 = (bf16[2,2,40,1792]{3,2,1,0:T(8,128)(2,1)S(1)}, bf16[2,2,40,1792]{3,2,1,0:T(8,128)(2,1)S(1)}, u32[]{:S(2)}, u32[]{:S(2)}) collective-permute-start(bf16[2,2,40,1792]{3,2,1,0:T(8,128)(2,1)S(1)} %get-tuple-element.150), channel_id=1, source_target_pairs={{0,8},{8,0},{16,24},{24,16},{1,9},{9,1},{17,25},{25,17},{2,10},{10... | collective-permute-start | bytes 1720328 | tf_op jit(solution)/shard_map/ppermute | solution.py:308
  103.8 15.5 %collective-permute-start.23 = (bf16[2,2,40,1792]{3,2,1,0:T(8,128)(2,1)S(1)}, bf16[2,2,40,1792]{3,2,1,0:T(8,128)(2,1)S(1)}, u32[]{:S(2)}, u32[]{:S(2)}) collective-permute-start(bf16[2,2,40,1792]{3,2,1,0:T(8,128)(2,1)S(1)} %get-tuple-element.146), channel_id=1, source_target_pairs={{0,16},{8,24},{16,0},{24,8},{1,17},{9,25},{17,1},{25,9},{2,18},{10... | collective-permute-start | bytes 1720328 | tf_op jit(solution)/shard_map/ppermute | solution.py:308
  109.6 9.0 %collective-permute-start.28 = (bf16[1,40,4096]{2,1,0:T(8,128)(2,1)S(1)}, bf16[1,40,4096]{2,1,0:T(8,128)(2,1)S(1)}, u32[]{:S(2)}, u32[]{:S(2)}) collective-permute-start(bf16[1,40,4096]{2,1,0:T(8,128)(2,1)S(1)} %get-tuple-element.156), channel_id=1, source_target_pairs={{0,1},{1,0},{2,3},{3,2},{4,5},{5,4},{6,7},{7,6},{8,9},{9,8},{10,11... | collective-permute-start | bytes 983048 | tf_op jit(solution)/shard_map/ppermute | solution.py:308
  118.7 8.2 %collective-permute-start.30 = (bf16[1,40,4096]{2,1,0:T(8,128)(2,1)S(1)}, bf16[1,40,4096]{2,1,0:T(8,128)(2,1)S(1)}, u32[]{:S(2)}, u32[]{:S(2)}) collective-permute-start(bf16[1,40,4096]{2,1,0:T(8,128)(2,1)S(1)} %get-tuple-element.168), channel_id=1, source_target_pairs={{0,1},{1,0},{2,3},{3,2},{4,5},{5,4},{6,7},{7,6},{8,9},{9,8},{10,11... | collective-permute-start | bytes 983048 | tf_op jit(solution)/shard_map/ppermute | solution.py:308
  119.3 7.8 %collective-permute-start.31 = (bf16[1,40,4096]{2,1,0:T(8,128)(2,1)S(1)}, bf16[1,40,4096]{2,1,0:T(8,128)(2,1)S(1)}, u32[]{:S(2)}, u32[]{:S(2)}) collective-permute-start(bf16[1,40,4096]{2,1,0:T(8,128)(2,1)S(1)} %get-tuple-element.167), channel_id=1, source_target_pairs={{0,2},{1,3},{2,0},{3,1},{4,6},{5,7},{6,4},{7,5},{8,10},{9,11},{10,... | collective-permute-start | bytes 983048 | tf_op jit(solution)/shard_map/ppermute | solution.py:336
  119.6 1.6 collective-permute-start.29
  127.2 8.1 %collective-permute-start.36 = (bf16[1,40,4096]{2,1,0:T(8,128)(2,1)S(1)}, bf16[1,40,4096]{2,1,0:T(8,128)(2,1)S(1)}, u32[]{:S(2)}, u32[]{:S(2)}) collective-permute-start(bf16[1,40,4096]{2,1,0:T(8,128)(2,1)S(1)} %get-tuple-element.170), channel_id=1, source_target_pairs={{0,2},{1,3},{2,0},{3,1},{4,6},{5,7},{6,4},{7,5},{8,10},{9,11},{10,... | collective-permute-start | bytes 983048 | tf_op jit(solution)/shard_map/ppermute | solution.py:336
  127.5 14.5 %collective-permute-start.24 = (bf16[2,2,40,1792]{3,2,1,0:T(8,128)(2,1)S(1)}, bf16[2,2,40,1792]{3,2,1,0:T(8,128)(2,1)S(1)}, u32[]{:S(2)}, u32[]{:S(2)}) collective-permute-start(bf16[2,2,40,1792]{3,2,1,0:T(8,128)(2,1)S(1)} %get-tuple-element.147), channel_id=1, source_target_pairs={{0,16},{8,24},{16,0},{24,8},{1,17},{9,25},{17,1},{25,9},{2,18},{10... | collective-permute-start | bytes 1720328 | tf_op jit(solution)/shard_map/ppermute | solution.py:308
  129.2 12.8 %collective-permute-start.32 = (bf16[1,40,4096]{2,1,0:T(8,128)(2,1)S(1)}, bf16[1,40,4096]{2,1,0:T(8,128)(2,1)S(1)}, u32[]{:S(2)}, u32[]{:S(2)}) collective-permute-start(bf16[1,40,4096]{2,1,0:T(8,128)(2,1)S(1)} %get-tuple-element.171), channel_id=1, source_target_pairs={{0,1},{1,0},{2,3},{3,2},{4,5},{5,4},{6,7},{7,6},{8,9},{9,8},{10,11... | collective-permute-start | bytes 983048 | tf_op jit(solution)/shard_map/ppermute | solution.py:308
  135.3 32.7 %collective-permute-start.37 = (bf16[2,40,4096]{2,1,0:T(8,128)(2,1)S(1)}, bf16[2,40,4096]{2,1,0:T(8,128)(2,1)S(1)}, u32[]{:S(2)}, u32[]{:S(2)}) collective-permute-start(bf16[2,40,4096]{2,1,0:T(8,128)(2,1)S(1)} %get-tuple-element.183), channel_id=1, source_target_pairs={{0,2},{1,3},{2,0},{3,1},{4,6},{5,7},{6,4},{7,5},{8,10},{9,11},{10,... | collective-permute-start | bytes 1966088 | tf_op jit(solution)/shard_map/ppermute | solution.py:336
  142.2 8.6 %collective-permute-start.34 = (bf16[1,40,4096]{2,1,0:T(8,128)(2,1)S(1)}, bf16[1,40,4096]{2,1,0:T(8,128)(2,1)S(1)}, u32[]{:S(2)}, u32[]{:S(2)}) collective-permute-start(bf16[1,40,4096]{2,1,0:T(8,128)(2,1)S(1)} %get-tuple-element.180), channel_id=1, source_target_pairs={{0,1},{1,0},{2,3},{3,2},{4,5},{5,4},{6,7},{7,6},{8,9},{9,8},{10,11... | collective-permute-start | bytes 983048 | tf_op jit(solution)/shard_map/ppermute | solution.py:308
  143.7 24.3 %collective-permute-start.39 = (bf16[1,40,4096]{2,1,0:T(8,128)(2,1)S(1)}, bf16[1,40,4096]{2,1,0:T(8,128)(2,1)S(1)}, u32[]{:S(2)}, u32[]{:S(2)}) collective-permute-start(bf16[1,40,4096]{2,1,0:T(8,128)(2,1)S(1)} %get-tuple-element.179), channel_id=1, source_target_pairs={{0,4},{1,5},{4,0},{5,1},{2,6},{3,7},{6,2},{7,3},{8,12},{9,13},{12,... | collective-permute-start | bytes 983048 | tf_op jit(solution)/shard_map/ppermute | solution.py:336
  145.2 1.6 collective-permute-start.33
  150.9 22.9 %collective-permute-start.38 = (bf16[1,40,4096]{2,1,0:T(8,128)(2,1)S(1)}, bf16[1,40,4096]{2,1,0:T(8,128)(2,1)S(1)}, u32[]{:S(2)}, u32[]{:S(2)}) collective-permute-start(bf16[1,40,4096]{2,1,0:T(8,128)(2,1)S(1)} %get-tuple-element.186), channel_id=1, source_target_pairs={{0,4},{1,5},{4,0},{5,1},{2,6},{3,7},{6,2},{7,3},{8,12},{9,13},{12,... | collective-permute-start | bytes 983048 | tf_op jit(solution)/shard_map/ppermute | solution.py:336
  152.6 16.5 %collective-permute-start.35 = (bf16[2,40,4096]{2,1,0:T(8,128)(2,1)S(1)}, bf16[2,40,4096]{2,1,0:T(8,128)(2,1)S(1)}, u32[]{:S(2)}, u32[]{:S(2)}) collective-permute-start(bf16[2,40,4096]{2,1,0:T(8,128)(2,1)S(1)} %get-tuple-element.181), channel_id=1, source_target_pairs={{0,1},{1,0},{2,3},{3,2},{4,5},{5,4},{6,7},{7,6},{8,9},{9,8},{10,11... | collective-permute-start | bytes 1966088 | tf_op jit(solution)/shard_map/ppermute | solution.py:308
  169.3 4.5 %collective-permute-start.40 = (bf16[40,4096]{1,0:T(8,128)(2,1)S(1)}, bf16[40,4096]{1,0:T(8,128)(2,1)S(1)}, u32[]{:S(2)}, u32[]{:S(2)}) collective-permute-start(bf16[40,4096]{1,0:T(8,128)(2,1)S(1)} %fusion.4), channel_id=1, source_target_pairs={{0,8},{8,0},{16,24},{24,16},{1,9},{9,1},{17,25},{25,17},{2,10},{10... | collective-permute-start | bytes 983048 | tf_op jit(solution)/shard_map/ppermute | solution.py:308

commit v11 on v9

--- a/solution.py
+++ b/solution.py
@@ -103,14 +103,14 @@
     joined_ref[...] = jnp.concatenate([block.astype(F32) for block in blocks], 0).astype(BF16)
 
 
-def rearranged(kernel, name, shape, blocks, after):
+def rearranged(kernel, name, shape, blocks, after, hint=0.0):
     return pl.pallas_call(
         functools.partial(kernel, len(after)),
         in_specs=[INSIDE] * len(blocks) + [ANYWHERE] * len(after),
         out_specs=[INSIDE] * 2,
         out_shape=[jax.ShapeDtypeStruct(shape, BF16), TOKEN],
         compiler_params=pltpu.CompilerParams(vmem_limit_bytes=VMEM // 2),
-        cost_estimate=cost(0, 1000000),
+        cost_estimate=as_if(hint),
         name=name,
     )(*blocks, *after)
 
@@ -120,9 +120,9 @@
     return rearranged(stack_kernel, "stack", shape, blocks, after)
 
 
-def join(stacks, after):
+def join(stacks, after, hint=0.0):
     rows = sum(part.shape[1] for part in stacks) * CORES * stacks[0].shape[2]
-    return rearranged(join_kernel, "join", (rows, stacks[0].shape[3]), stacks, after)
+    return rearranged(join_kernel, "join", (rows, stacks[0].shape[3]), stacks, after, hint)
 
 
 def pick_kernel(after_count, place_ref, *refs):
@@ -360,8 +360,8 @@
     def exchange_near(plane, after=()):
         near[plane] = by_core(halves[plane][1], after)
 
-    def multiply_out(plane, pieces=1):
-        *partials[plane], last[0] = down(hiddens[plane], others[plane], down_kept, pieces, last)
+    def multiply_out(plane, pieces=1, after=()):
+        *partials[plane], last[0] = down(hiddens[plane], others[plane], down_kept, pieces, last + list(after))
 
     def send_rows(plane, after=(), pieces=1, piece=0):
         mine_and_others = partials[plane][piece::pieces]
@@ -386,25 +386,28 @@
         return summed
 
     next_stacks = [by_plane(first, NEXT), by_plane(second, NEXT)]
-    three_away = by_plane(mine, MIRROR)
+    mirror_stacks = [by_plane(first, MIRROR)]
     forward(0, mine)
     up_kept, last[0] = masked(
-        up_weight, up_mask, tile_of(features, 256), place, 1, lambda core: 0, last + next_stacks[:1], 0.15
+        up_weight, up_mask, tile_of(features, 256), place, 1, lambda core: 0, last + next_stacks[:1] + mirror_stacks, 0.15
     )
     one_away, last[0] = join(next_stacks, last)
+    mirror_stacks.append(by_plane(second, MIRROR, [one_away]))
     down_kept = []
     for share, hint in ((0, 8), (1, 0)):
         part, last[0] = masked(
-            down_weight, down_mask, 2 * BLOCK, place, 2 * CORES, lambda core, share=share: 2 * core + share, last, hint
+            down_weight, down_mask, 2 * BLOCK, place, 2 * CORES, lambda core, share=share: 2 * core + share,
+            last, hint
         )
         down_kept.append(part)
     forward(1, one_away, [*parts[0][1:], *last])
     multiply_in(0, hint=0)
     exchange(0)
     exchange_near(0)
-    to_chips(0, [near[0]])
+    three_away, last[0] = join(mirror_stacks, last, 8)
     passed, last[0] = pick(place, three_away, mine, last)
     two_away = by_plane(passed, CYCLE)
+    to_chips(0, [near[0]])
     forward(3, three_away, [*parts[1][1:], *last])
     multiply_in(1)
     exchange(1)
@@ -442,8 +445,8 @@
     two = to_rows(*rows_in[2, 1], three_out[1])
     two_out[1] = by_plane(two, SECOND)
     send_rows(2, [two], CORES, 0)
-    to_hidden(0, [three_out[0]])
-    multiply_out(0)
+    to_hidden(0)
+    multiply_out(0, after=[three_out[0]])
     two = to_rows(*rows_in[2, 0], three_out[0])
     two_out[0] = by_plane(two, SECOND)
     send_rows(0, rows_in[2, 0][1:])

time: 169 us -> 164 us (0.970)
  starting transfers between devices: 56.8 us -> 40 us
  waiting for transfers between devices: 48.5 us -> 60.2 us
    ppermute x9 -> x10, waiting for transfers between devices: 12 us -> 35.5 us  [by_plane(): return lax.ppermute(behind(values, after), 'cols', pairs)]
    ppermute x9 -> x10, starting transfers between devices: 34.7 us -> 14.3 us  [by_plane(): return lax.ppermute(behind(values, after), 'cols', pairs)]
    ppermute x31, waiting for transfers between devices: 36.5 us -> 24.7 us  [swap(): lax.ppermute(values, axis, [(place, place ^ step) for place in range(size)])]
    ppermute x31, starting transfers between devices: 22.1 us -> 25.7 us  [swap(): lax.ppermute(values, axis, [(place, place ^ step) for place in range(size)])]
  transfers between devices with their start and end apart: 40 -> 41, of which waited for: 20 -> 19; matrix products, arithmetic and copies ran while one was open for 0% -> 0% of each run, Pallas kernels for 35% -> 36%
where the time goes in v11:
time: 164 us; the launch traced here: 163 us
  waiting for transfers between devices  60.2 us (37%)
  Pallas kernels  58.9 us (36%)
  starting transfers between devices  40 us (24%)
  other arithmetic  3.97 us (2%)
    ppermute x10, waiting for transfers between devices, by_plane(): return lax.ppermute(behind(values, after), 'cols', pairs)  35.5 us
    ppermute x31, starting transfers between devices, swap(): lax.ppermute(values, axis, [(place, place ^ step) for place in range(size)])  25.7 us
    ppermute x31, waiting for transfers between devices, swap(): lax.ppermute(values, axis, [(place, place ^ step) for place in range(size)])  24.7 us
    pallas_call x4, Pallas kernels, gate_up(): pl.pallas_call(functools.partial(gate_up_kernel, len(parts), len(after)),...  24.3 us
    pallas_call x4, Pallas kernels, down(): pl.pallas_call(functools.partial(down_kernel, pieces, len(down_kept), len...  15.5 us
    pallas_call x4, Pallas kernels, masked(): pl.pallas_call(functools.partial(mask_kernel, share, rows, len(after)), i...  15.4 us
    ppermute x10, starting transfers between devices, by_plane(): return lax.ppermute(behind(values, after), 'cols', pairs)  14.3 us
  transfers between devices with their start and end apart: 41, of which 19 were waited for; matrix products, arithmetic and copies ran while one was open for 0% of the time, Pallas kernels for 36%

profile of v11, /device:TPU:0, one launch (start us, length us, event | category | flops | bytes accessed | tf_op | source)
XLA Modules:
  0.0 163.5 jit_solution(8324071905930140171)
XLA Ops:
  0.0 1.3 fusion
  1.4 1.3 fusion.2
  3.3 2.6 %collective-permute-start.2 = (bf16[40,2048]{1,0:T(8,128)(2,1)S(1)}, bf16[40,2048]{1,0:T(8,128)(2,1)S(1)}, u32[]{:S(2)}, u32[]{:S(2)}) collective-permute-start(bf16[40,2048]{1,0:T(8,128)(2,1)S(1)} %get-tuple-element.191), channel_id=1, source_target_pairs={{0,24},{8,16},{16,8},{24,0},{1,25},{9,17},{17,9},{25,1},{2,26},{10... | collective-permute-start | bytes 491528 | tf_op jit(solution)/shard_map/ppermute | solution.py:306
  6.0 4.2 %collective-permute-start.5 = (bf16[2,1,40,2048]{3,2,1,0:T(8,128)(2,1)S(1)}, bf16[2,1,40,2048]{3,2,1,0:T(8,128)(2,1)S(1)}, u32[]{:S(2)}, u32[]{:S(2)}) collective-permute-start(bf16[2,1,40,2048]{3,2,1,0:T(8,128)(2,1)S(1)} %get-tuple-element.97.refs_0_), channel_id=1, source_target_pairs={{0,6},{1,7},{6,0},{7,1},{2,4},{3,5},{4,2},{5,3},{8,14},{9,15},{14,... | collective-permute-start | bytes 983048 | tf_op jit(solution)/shard_map/ppermute | solution.py:334
  10.2 3.8 %masked.4 = (bf16[2048,1792]{1,0:T(8,128)(2,1)S(1)}, f32[8,128]{1,0:T(8,128)S(1)}) custom-call(s32[2]{0:T(128)S(1)} %pad_add_fusion.core_ref.place_ref, bf16[2048,1792]{1,0:T(8,128)(2,1)} %weight_ref.4, s32[32,28]{1,0:T(8,128)S(1)} %copy-done, f32[8,128]{1,0:T(8,128)S(1)} %get-tuple-element.98.refs_0_), custom_call_target="tpu_custom_call" | custom-call | tf_op jit(solution)/shard_map/masked/pallas_call | solution.py:80
  14.2 2.0 %collective-permute-start.6 = (bf16[2,1,40,2048]{3,2,1,0:T(8,128)(2,1)S(1)}, bf16[2,1,40,2048]{3,2,1,0:T(8,128)(2,1)S(1)}, u32[]{:S(2)}, u32[]{:S(2)}) collective-permute-start(bf16[2,1,40,2048]{3,2,1,0:T(8,128)(2,1)S(1)} %get-tuple-element.114.refs_1_), channel_id=1, source_target_pairs={{0,2},{1,3},{2,0},{3,1},{4,6},{5,7},{6,4},{7,5},{8,10},{9,11},{10,... | collective-permute-start | bytes 983048 | tf_op jit(solution)/shard_map/ppermute | solution.py:334
  16.2 1.6 collective-permute-start.3
  17.8 1.0 collective-permute-done.5.refs_2_.refs_0_
  18.8 6.5 %collective-permute-done.4.refs_1_.refs_0_ = bf16[2,1,40,2048]{3,2,1,0:T(8,128)(2,1)S(1)} collective-permute-done((bf16[2,1,40,2048]{3,2,1,0:T(8,128)(2,1)S(1)}, bf16[2,1,40,2048]{3,2,1,0:T(8,128)(2,1)S(1)}, u32[]{:S(2)}, u32[]{:S(2)}) %collective-permute-start.4) | collective-permute-done | bytes 327712 | tf_op jit(solution)/shard_map/ppermute | solution.py:334
  25.3 3.8 %masked.5 = (bf16[2048,1792]{1,0:T(8,128)(2,1)S(1)}, f32[8,128]{1,0:T(8,128)S(1)}) custom-call(s32[2]{0:T(128)S(1)} %pad_add_fusion.core_ref.place_ref, bf16[2048,1792]{1,0:T(8,128)(2,1)} %weight_ref.5, s32[32,28]{1,0:T(8,128)S(1)} %copy-done.1, f32[8,128]{1,0:T(8,128)S(1)} %get-tuple-element.104.refs_0_, ...), custom_call_target="tpu_custom_call" | custom-call | flops 172500000 | tf_op jit(solution)/shard_map/masked/pallas_call | solution.py:80
  29.1 2.9 %collective-permute-done.6.refs_1_ = bf16[2,1,40,2048]{3,2,1,0:T(8,128)(2,1)S(1)} collective-permute-done((bf16[2,1,40,2048]{3,2,1,0:T(8,128)(2,1)S(1)}, bf16[2,1,40,2048]{3,2,1,0:T(8,128)(2,1)S(1)}, u32[]{:S(2)}, u32[]{:S(2)}) %collective-permute-start.6) | collective-permute-done | bytes 327712 | tf_op jit(solution)/shard_map/ppermute | solution.py:334
  32.0 1.8 %collective-permute-start.9 = (bf16[2,1,40,2048]{3,2,1,0:T(8,128)(2,1)S(1)}, bf16[2,1,40,2048]{3,2,1,0:T(8,128)(2,1)S(1)}, u32[]{:S(2)}, u32[]{:S(2)}) collective-permute-start(bf16[2,1,40,2048]{3,2,1,0:T(8,128)(2,1)S(1)} %get-tuple-element.114.refs_1_), channel_id=1, source_target_pairs={{0,6},{1,7},{6,0},{7,1},{2,4},{3,5},{4,2},{5,3},{8,14},{9,15},{14,... | collective-permute-start | bytes 983048 | tf_op jit(solution)/shard_map/ppermute | solution.py:334
  33.8 3.9 %masked.6 = (bf16[1792,2048]{1,0:T(8,128)(2,1)S(1)}, f32[8,128]{1,0:T(8,128)S(1)}) custom-call(s32[2]{0:T(128)S(1)} %pad_add_fusion.core_ref.place_ref, bf16[1792,8192]{1,0:T(8,128)(2,1)} %weight_ref.7, s32[28,128]{1,0:T(8,128)S(1)} %copy-done.2, f32[8,128]{1,0:T(8,128)S(1)} %get-tuple-element.107.refs_0_), custom_call_target="tpu_custom_call" | custom-call | flops 9200000000 | tf_op jit(solution)/shard_map/masked/pallas_call | solution.py:80
  37.7 3.9 %masked.7 = (bf16[1792,2048]{1,0:T(8,128)(2,1)S(1)}, f32[8,128]{1,0:T(8,128)S(1)}) custom-call(s32[2]{0:T(128)S(1)} %pad_add_fusion.core_ref.place_ref, bf16[1792,8192]{1,0:T(8,128)(2,1)} %weight_ref.7, s32[28,128]{1,0:T(8,128)S(1)} %copy-done.2, f32[8,128]{1,0:T(8,128)S(1)} %get-tuple-element.108.refs_0_), custom_call_target="tpu_custom_call" | custom-call | tf_op jit(solution)/shard_map/masked/pallas_call | solution.py:80
  41.6 1.6 collective-permute-start.11
  43.2 6.1 %gate_up.4 = (bf16[2,2,2,40,1792]{4,3,2,1,0:T(8,128)(2,1)S(1)}, bf16[2,2,40,1792]{3,2,1,0:T(8,128)(2,1)S(1)}, bf16[2,2,1,40,1792]{4,3,2,1,0:T(8,128)(2,1)S(1)}, f32[8,128]{1,0:T(8,128)S(1)}) custom-call(bf16[160,2048]{1,0:T(8,128)(2,1)S(1)} %get-tuple-element.102.refs_0_.refs_1_, bf16[160,2048]{1,0:T(8,128)(2,1)S(1)} %collective-permute-done.3.refs_1_, ...), custom_call_target="tpu_custom_call" | custom-call | tf_op jit(solution)/shard_map/gate_up/pallas_call | solution.py:188
  50.5 1.7 %collective-permute-start.10 = (bf16[160,2048]{1,0:T(8,128)(2,1)S(1)}, bf16[160,2048]{1,0:T(8,128)(2,1)S(1)}, u32[]{:S(2)}, u32[]{:S(2)}) collective-permute-start(bf16[160,2048]{1,0:T(8,128)(2,1)S(1)} %get-tuple-element.120), channel_id=1, source_target_pairs={{0,4},{1,5},{4,6},{5,7},{6,2},{7,3},{2,0},{3,1},{8,12},{9,13},{12,... | collective-permute-start | bytes 1966088 | tf_op jit(solution)/shard_map/ppermute | solution.py:334
  52.3 4.6 %collective-permute-done.11.refs_1_ = bf16[160,2048]{1,0:T(8,128)(2,1)S(1)} collective-permute-done((bf16[160,2048]{1,0:T(8,128)(2,1)S(1)}, bf16[160,2048]{1,0:T(8,128)(2,1)S(1)}, u32[]{:S(2)}, u32[]{:S(2)}) %collective-permute-start.11) | collective-permute-done | bytes 655392 | tf_op jit(solution)/shard_map/ppermute | solution.py:306
  56.9 1.4 collective-permute-start.12
  58.3 6.1 %gate_up.5 = (bf16[2,2,2,40,1792]{4,3,2,1,0:T(8,128)(2,1)S(1)}, bf16[2,2,40,1792]{3,2,1,0:T(8,128)(2,1)S(1)}, bf16[2,2,1,40,1792]{4,3,2,1,0:T(8,128)(2,1)S(1)}, f32[8,128]{1,0:T(8,128)S(1)}) custom-call(bf16[160,2048]{1,0:T(8,128)(2,1)S(1)} %get-tuple-element.121.refs_0_, bf16[160,2048]{1,0:T(8,128)(2,1)S(1)} %collective-permute-done.11.refs_1_, ...), custom_call_target="tpu_custom_call" | custom-call | flops 4697620480 | tf_op jit(solution)/shard_map/gate_up/pallas_call | solution.py:188
  64.9 1.5 collective-permute-done.13.refs_1_
  66.4 0.8 collective-permute-done.14.refs_3_.refs_1_
  67.4 1.6 collective-permute-start.16
  68.9 2.3 %collective-permute-done.12.refs_1_ = bf16[160,2048]{1,0:T(8,128)(2,1)S(1)} collective-permute-done((bf16[160,2048]{1,0:T(8,128)(2,1)S(1)}, bf16[160,2048]{1,0:T(8,128)(2,1)S(1)}, u32[]{:S(2)}, u32[]{:S(2)}) %collective-permute-start.12) | collective-permute-done | bytes 655392 | tf_op jit(solution)/shard_map/ppermute | solution.py:306
  71.3 1.7 %collective-permute-start.15 = (bf16[160,2048]{1,0:T(8,128)(2,1)S(1)}, bf16[160,2048]{1,0:T(8,128)(2,1)S(1)}, u32[]{:S(2)}, u32[]{:S(2)}) collective-permute-start(bf16[160,2048]{1,0:T(8,128)(2,1)S(1)} %collective-permute-done.10.refs_5_.refs_0_), channel_id=1, source_target_pairs={{0,1},{1,0},{2,3},{3,2},{4,5},{5,4},{6,7},{7,6},{8,9},{9,8},{10,11... | collective-permute-start | bytes 1966088 | tf_op jit(solution)/shard_map/ppermute | solution.py:306
  72.9 6.1 %gate_up.6 = (bf16[2,2,2,40,1792]{4,3,2,1,0:T(8,128)(2,1)S(1)}, bf16[2,2,40,1792]{3,2,1,0:T(8,128)(2,1)S(1)}, bf16[2,2,1,40,1792]{4,3,2,1,0:T(8,128)(2,1)S(1)}, f32[8,128]{1,0:T(8,128)S(1)}) custom-call(bf16[160,2048]{1,0:T(8,128)(2,1)S(1)} %get-tuple-element.123.refs_0_, bf16[160,2048]{1,0:T(8,128)(2,1)S(1)} %collective-permute-done.12.refs_1_, ...), custom_call_target="tpu_custom_call" | custom-call | flops 4697620480 | tf_op jit(solution)/shard_map/gate_up/pallas_call | solution.py:188
  79.6 2.9 %collective-permute-done.16.refs_2_ = bf16[2,2,40,1792]{3,2,1,0:T(8,128)(2,1)S(1)} collective-permute-done((bf16[2,2,40,1792]{3,2,1,0:T(8,128)(2,1)S(1)}, bf16[2,2,40,1792]{3,2,1,0:T(8,128)(2,1)S(1)}, u32[]{:S(2)}, u32[]{:S(2)}) %collective-permute-start.16) | collective-permute-done | bytes 573472 | tf_op jit(solution)/shard_map/ppermute | solution.py:306
  83.0 1.6 collective-permute-start.22
  84.6 3.9 %down.4 = (bf16[2,40,4096]{2,1,0:T(8,128)(2,1)S(1)}, bf16[2,40,4096]{2,1,0:T(8,128)(2,1)S(1)}, f32[8,128]{1,0:T(8,128)S(1)}) custom-call(bf16[2,40,1792]{2,1,0:T(8,128)(2,1)S(1)} %get-tuple-element.132.own_ref, bf16[2,40,1792]{2,1,0:T(8,128)(2,1)S(1)} %collective-permute-done.17.other_ref, bf16[1792,2048]{1,0:T(8,128)(2,1)S(1)} %get-tuple-element.133.refs_0_, ...), custom_call_target="tpu_custom_call" | custom-call | flops 2348810 | tf_op jit(solution)/shard_map/down/pallas_call | solution.py:230
  89.0 6.1 %gate_up.7 = (bf16[2,2,2,40,1792]{4,3,2,1,0:T(8,128)(2,1)S(1)}, bf16[2,2,40,1792]{3,2,1,0:T(8,128)(2,1)S(1)}, bf16[1,2,1,40,1792]{4,3,2,1,0:T(8,128)(2,1)S(1)}, ...) custom-call(bf16[160,2048]{1,0:T(8,128)(2,1)S(1)} %collective-permute-done.10.refs_5_.refs_0_, ...), custom_call_target="tpu_custom_call" | custom-call | flops 4697620480 | tf_op jit(solution)/shard_map/gate_up/pallas_call | solution.py:188
  95.7 2.8 %collective-permute-done.22.refs_2_ = bf16[2,2,40,1792]{3,2,1,0:T(8,128)(2,1)S(1)} collective-permute-done((bf16[2,2,40,1792]{3,2,1,0:T(8,128)(2,1)S(1)}, bf16[2,2,40,1792]{3,2,1,0:T(8,128)(2,1)S(1)}, u32[]{:S(2)}, u32[]{:S(2)}) %collective-permute-start.22) | collective-permute-done | bytes 573472 | tf_op jit(solution)/shard_map/ppermute | solution.py:306
  99.5 1.5 collective-permute-start.23
  101.0 3.9 %down.5 = (bf16[1,40,4096]{2,1,0:T(8,128)(2,1)S(1)}, bf16[1,40,4096]{2,1,0:T(8,128)(2,1)S(1)}, bf16[1,40,4096]{2,1,0:T(8,128)(2,1)S(1)}, bf16[1,40,4096]{2,1,0:T(8,128)(2,1)S(1)}, f32[8,128]{1,0:T(8,128)S(1)}) custom-call(bf16[2,40,1792]{2,1,0:T(8,128)(2,1)S(1)} %get-tuple-element.152.own_ref, bf16[2,40,1792]{2,1,0:T(8,128)(2,1)S(1)} %collective-permute-done.26.other_ref, ...), custom_call_target="tpu_custom_call" | custom-call | flops 2348810 | tf_op jit(solution)/shard_map/down/pallas_call | solution.py:230
  106.6 7.8 %collective-permute-done.28.refs_1_ = bf16[1,40,4096]{2,1,0:T(8,128)(2,1)S(1)} collective-permute-done((bf16[1,40,4096]{2,1,0:T(8,128)(2,1)S(1)}, bf16[1,40,4096]{2,1,0:T(8,128)(2,1)S(1)}, u32[]{:S(2)}, u32[]{:S(2)}) %collective-permute-start.28) | collective-permute-done | bytes 327712 | tf_op jit(solution)/shard_map/ppermute | solution.py:306
  115.4 1.2 collective-permute-start.24
  117.1 3.9 %down.6 = (bf16[1,40,4096]{2,1,0:T(8,128)(2,1)S(1)}, bf16[1,40,4096]{2,1,0:T(8,128)(2,1)S(1)}, bf16[1,40,4096]{2,1,0:T(8,128)(2,1)S(1)}, bf16[1,40,4096]{2,1,0:T(8,128)(2,1)S(1)}, f32[8,128]{1,0:T(8,128)S(1)}) custom-call(bf16[2,40,1792]{2,1,0:T(8,128)(2,1)S(1)} %get-tuple-element.162.own_ref, bf16[2,40,1792]{2,1,0:T(8,128)(2,1)S(1)} %collective-permute-done.29.other_ref, ...), custom_call_target="tpu_custom_call" | custom-call | flops 2348810 | tf_op jit(solution)/shard_map/down/pallas_call | solution.py:230
  121.0 2.7 %collective-permute-done.31.refs_3_.refs_1_ = bf16[2,40,4096]{2,1,0:T(8,128)(2,1)S(1)} collective-permute-done((bf16[2,40,4096]{2,1,0:T(8,128)(2,1)S(1)}, bf16[2,40,4096]{2,1,0:T(8,128)(2,1)S(1)}, u32[]{:S(2)}, u32[]{:S(2)}) %collective-permute-start.31) | collective-permute-done | bytes 655392 | tf_op jit(solution)/shard_map/ppermute | solution.py:334
  123.8 1.6 collective-permute-start.32
  125.9 4.8 %collective-permute-done.33.refs_2_ = bf16[1,40,4096]{2,1,0:T(8,128)(2,1)S(1)} collective-permute-done((bf16[1,40,4096]{2,1,0:T(8,128)(2,1)S(1)}, bf16[1,40,4096]{2,1,0:T(8,128)(2,1)S(1)}, u32[]{:S(2)}, u32[]{:S(2)}) %collective-permute-start.33) | collective-permute-done | bytes 327712 | tf_op jit(solution)/shard_map/ppermute | solution.py:334
  130.8 0.9 collective-permute-done.32.refs_1_
  131.9 1.6 collective-permute-start.36
  133.4 2.4 %collective-permute-start.39 = (bf16[1,40,4096]{2,1,0:T(8,128)(2,1)S(1)}, bf16[1,40,4096]{2,1,0:T(8,128)(2,1)S(1)}, u32[]{:S(2)}, u32[]{:S(2)}) collective-permute-start(bf16[1,40,4096]{2,1,0:T(8,128)(2,1)S(1)} %get-tuple-element.181), channel_id=1, source_target_pairs={{0,4},{1,5},{4,0},{5,1},{2,6},{3,7},{6,2},{7,3},{8,12},{9,13},{12,... | collective-permute-start | bytes 983048 | tf_op jit(solution)/shard_map/ppermute | solution.py:334
  136.2 3.1 %collective-permute-done.35.refs_3_.refs_2_ = bf16[1,40,4096]{2,1,0:T(8,128)(2,1)S(1)} collective-permute-done((bf16[1,40,4096]{2,1,0:T(8,128)(2,1)S(1)}, bf16[1,40,4096]{2,1,0:T(8,128)(2,1)S(1)}, u32[]{:S(2)}, u32[]{:S(2)}) %collective-permute-start.35) | collective-permute-done | bytes 327712 | tf_op jit(solution)/shard_map/ppermute | solution.py:334
  139.3 3.9 %down.7 = (bf16[2,40,4096]{2,1,0:T(8,128)(2,1)S(1)}, bf16[2,40,4096]{2,1,0:T(8,128)(2,1)S(1)}, f32[8,128]{1,0:T(8,128)S(1)}) custom-call(bf16[2,40,1792]{2,1,0:T(8,128)(2,1)S(1)} %get-tuple-element.176.own_ref, bf16[2,40,1792]{2,1,0:T(8,128)(2,1)S(1)} %collective-permute-done.34.other_ref, bf16[1792,2048]{1,0:T(8,128)(2,1)S(1)} %get-tuple-element.133.refs_0_, ...), custom_call_target="tpu_custom_call" | custom-call | flops 2348810 | tf_op jit(solution)/shard_map/down/pallas_call | solution.py:230
  144.0 2.5 %collective-permute-start.37 = (bf16[2,40,4096]{2,1,0:T(8,128)(2,1)S(1)}, bf16[2,40,4096]{2,1,0:T(8,128)(2,1)S(1)}, u32[]{:S(2)}, u32[]{:S(2)}) collective-permute-start(bf16[2,40,4096]{2,1,0:T(8,128)(2,1)S(1)} %get-tuple-element.183), channel_id=1, source_target_pairs={{0,1},{1,0},{2,3},{3,2},{4,5},{5,4},{6,7},{7,6},{8,9},{9,8},{10,11... | collective-permute-start | bytes 1966088 | tf_op jit(solution)/shard_map/ppermute | solution.py:306
  146.5 11.5 %collective-permute-done.39.refs_0_ = bf16[1,40,4096]{2,1,0:T(8,128)(2,1)S(1)} collective-permute-done((bf16[1,40,4096]{2,1,0:T(8,128)(2,1)S(1)}, bf16[1,40,4096]{2,1,0:T(8,128)(2,1)S(1)}, u32[]{:S(2)}, u32[]{:S(2)}) %collective-permute-start.39) | collective-permute-done | bytes 327712 | tf_op jit(solution)/shard_map/ppermute | solution.py:334
  159.4 2.9 %collective-permute-done.38 = bf16[1,40,4096]{2,1,0:T(8,128)(2,1)S(1)} collective-permute-done((bf16[1,40,4096]{2,1,0:T(8,128)(2,1)S(1)}, bf16[1,40,4096]{2,1,0:T(8,128)(2,1)S(1)}, u32[]{:S(2)}, u32[]{:S(2)}) %collective-permute-start.38) | collective-permute-done | bytes 327712 | tf_op jit(solution)/shard_map/ppermute | solution.py:334
  162.6 0.9 pad_maximum_fusion
  (81 shorter events, 13.0 us)
Async XLA Ops:
  1.3 8.8 %copy-start = (s32[32,28]{1,0:T(8,128)S(1)}, s32[32,28]{1,0:T(8,128)}, u32[]{:S(2)}) copy-start(s32[32,28]{1,0:T(8,128)} %mask_ref.4) | copy-start | bytes 10756
  2.7 3.2 %collective-permute-start = (bf16[40,2048]{1,0:T(8,128)(2,1)S(1)}, bf16[40,2048]{1,0:T(8,128)(2,1)S(1)}, u32[]{:S(2)}, u32[]{:S(2)}) collective-permute-start(bf16[40,2048]{1,0:T(8,128)(2,1)S(1)} %get-tuple-element.193), channel_id=1, source_target_pairs={{0,8},{8,0},{16,24},{24,16},{1,9},{9,1},{17,25},{25,17},{2,10},{10... | collective-permute-start | bytes 491528 | tf_op jit(solution)/shard_map/ppermute | solution.py:306
  3.3 10.7 %collective-permute-start.2 = (bf16[40,2048]{1,0:T(8,128)(2,1)S(1)}, bf16[40,2048]{1,0:T(8,128)(2,1)S(1)}, u32[]{:S(2)}, u32[]{:S(2)}) collective-permute-start(bf16[40,2048]{1,0:T(8,128)(2,1)S(1)} %get-tuple-element.191), channel_id=1, source_target_pairs={{0,24},{8,16},{16,8},{24,0},{1,25},{9,17},{17,9},{25,1},{2,26},{10... | collective-permute-start | bytes 491528 | tf_op jit(solution)/shard_map/ppermute | solution.py:306
  5.9 8.3 %collective-permute-start.1 = (bf16[40,2048]{1,0:T(8,128)(2,1)S(1)}, bf16[40,2048]{1,0:T(8,128)(2,1)S(1)}, u32[]{:S(2)}, u32[]{:S(2)}) collective-permute-start(bf16[40,2048]{1,0:T(8,128)(2,1)S(1)} %get-tuple-element.192), channel_id=1, source_target_pairs={{0,16},{8,24},{16,0},{24,8},{1,17},{9,25},{17,1},{25,9},{2,18},{10... | collective-permute-start | bytes 491528 | tf_op jit(solution)/shard_map/ppermute | solution.py:306
  6.0 12.8 %collective-permute-start.5 = (bf16[2,1,40,2048]{3,2,1,0:T(8,128)(2,1)S(1)}, bf16[2,1,40,2048]{3,2,1,0:T(8,128)(2,1)S(1)}, u32[]{:S(2)}, u32[]{:S(2)}) collective-permute-start(bf16[2,1,40,2048]{3,2,1,0:T(8,128)(2,1)S(1)} %get-tuple-element.97.refs_0_), channel_id=1, source_target_pairs={{0,6},{1,7},{6,0},{7,1},{2,4},{3,5},{4,2},{5,3},{8,14},{9,15},{14,... | collective-permute-start | bytes 983048 | tf_op jit(solution)/shard_map/ppermute | solution.py:334
  10.1 15.1 %collective-permute-start.4 = (bf16[2,1,40,2048]{3,2,1,0:T(8,128)(2,1)S(1)}, bf16[2,1,40,2048]{3,2,1,0:T(8,128)(2,1)S(1)}, u32[]{:S(2)}, u32[]{:S(2)}) collective-permute-start(bf16[2,1,40,2048]{3,2,1,0:T(8,128)(2,1)S(1)} %get-tuple-element.97.refs_0_), channel_id=1, source_target_pairs={{0,2},{1,3},{2,0},{3,1},{4,6},{5,7},{6,4},{7,5},{8,10},{9,11},{10,... | collective-permute-start | bytes 983048 | tf_op jit(solution)/shard_map/ppermute | solution.py:334
  10.2 15.1 %copy-start.1 = (s32[32,28]{1,0:T(8,128)S(1)}, s32[32,28]{1,0:T(8,128)}, u32[]{:S(2)}) copy-start(s32[32,28]{1,0:T(8,128)} %mask_ref.5) | copy-start | bytes 10756
  14.2 17.8 %collective-permute-start.6 = (bf16[2,1,40,2048]{3,2,1,0:T(8,128)(2,1)S(1)}, bf16[2,1,40,2048]{3,2,1,0:T(8,128)(2,1)S(1)}, u32[]{:S(2)}, u32[]{:S(2)}) collective-permute-start(bf16[2,1,40,2048]{3,2,1,0:T(8,128)(2,1)S(1)} %get-tuple-element.114.refs_1_), channel_id=1, source_target_pairs={{0,2},{1,3},{2,0},{3,1},{4,6},{5,7},{6,4},{7,5},{8,10},{9,11},{10,... | collective-permute-start | bytes 983048 | tf_op jit(solution)/shard_map/ppermute | solution.py:334
  16.2 25.4 %collective-permute-start.3 = (bf16[160,2048]{1,0:T(8,128)(2,1)S(1)}, bf16[160,2048]{1,0:T(8,128)(2,1)S(1)}, u32[]{:S(2)}, u32[]{:S(2)}) collective-permute-start(bf16[160,2048]{1,0:T(8,128)(2,1)S(1)} %get-tuple-element.102.refs_0_.refs_1_), channel_id=1, source_target_pairs={{0,1},{1,0},{2,3},{3,2},{4,5},{5,4},{6,7},{7,6},{8,9},{9,8},{10,11... | collective-permute-start | bytes 1966088 | tf_op jit(solution)/shard_map/ppermute | solution.py:306
  25.3 8.5 %copy-start.2 = (s32[28,128]{1,0:T(8,128)S(1)}, s32[28,128]{1,0:T(8,128)}, u32[]{:S(2)}) copy-start(s32[28,128]{1,0:T(8,128)} %mask_ref.7) | copy-start | bytes 43012
  32.0 17.9 %collective-permute-start.9 = (bf16[2,1,40,2048]{3,2,1,0:T(8,128)(2,1)S(1)}, bf16[2,1,40,2048]{3,2,1,0:T(8,128)(2,1)S(1)}, u32[]{:S(2)}, u32[]{:S(2)}) collective-permute-start(bf16[2,1,40,2048]{3,2,1,0:T(8,128)(2,1)S(1)} %get-tuple-element.114.refs_1_), channel_id=1, source_target_pairs={{0,6},{1,7},{6,0},{7,1},{2,4},{3,5},{4,2},{5,3},{8,14},{9,15},{14,... | collective-permute-start | bytes 983048 | tf_op jit(solution)/shard_map/ppermute | solution.py:334
  41.6 15.3 %collective-permute-start.11 = (bf16[160,2048]{1,0:T(8,128)(2,1)S(1)}, bf16[160,2048]{1,0:T(8,128)(2,1)S(1)}, u32[]{:S(2)}, u32[]{:S(2)}) collective-permute-start(bf16[160,2048]{1,0:T(8,128)(2,1)S(1)} %get-tuple-element.121.refs_0_), channel_id=1, source_target_pairs={{0,1},{1,0},{2,3},{3,2},{4,5},{5,4},{6,7},{7,6},{8,9},{9,8},{10,11... | collective-permute-start | bytes 1966088 | tf_op jit(solution)/shard_map/ppermute | solution.py:306
  49.3 2.9 %collective-permute-start.7 = (bf16[2,2,40,1792]{3,2,1,0:T(8,128)(2,1)S(1)}, bf16[2,2,40,1792]{3,2,1,0:T(8,128)(2,1)S(1)}, u32[]{:S(2)}, u32[]{:S(2)}) collective-permute-start(bf16[2,2,40,1792]{3,2,1,0:T(8,128)(2,1)S(1)} %get-tuple-element.111), channel_id=1, source_target_pairs={{0,8},{8,0},{16,24},{24,16},{1,9},{9,1},{17,25},{25,17},{2,10},{10... | collective-permute-start | bytes 1720328 | tf_op jit(solution)/shard_map/ppermute | solution.py:306
  49.3 2.8 %collective-permute-start.8 = (bf16[2,2,1,40,1792]{4,3,2,1,0:T(8,128)(2,1)S(1)}, bf16[2,2,1,40,1792]{4,3,2,1,0:T(8,128)(2,1)S(1)}, u32[]{:S(2)}, u32[]{:S(2)}) collective-permute-start(bf16[2,2,1,40,1792]{4,3,2,1,0:T(8,128)(2,1)S(1)} %get-tuple-element.112), channel_id=1, source_target_pairs={{0,8},{8,0},{16,24},{24,16},{1,9},{9,1},{17,25},{25,17},{2,10},{10... | collective-permute-start | bytes 1720328 | tf_op jit(solution)/shard_map/ppermute | solution.py:306
  50.5 18.4 %collective-permute-start.10 = (bf16[160,2048]{1,0:T(8,128)(2,1)S(1)}, bf16[160,2048]{1,0:T(8,128)(2,1)S(1)}, u32[]{:S(2)}, u32[]{:S(2)}) collective-permute-start(bf16[160,2048]{1,0:T(8,128)(2,1)S(1)} %get-tuple-element.120), channel_id=1, source_target_pairs={{0,4},{1,5},{4,6},{5,7},{6,2},{7,3},{2,0},{3,1},{8,12},{9,13},{12,... | collective-permute-start | bytes 1966088 | tf_op jit(solution)/shard_map/ppermute | solution.py:334
  56.9 14.3 %collective-permute-start.12 = (bf16[160,2048]{1,0:T(8,128)(2,1)S(1)}, bf16[160,2048]{1,0:T(8,128)(2,1)S(1)}, u32[]{:S(2)}, u32[]{:S(2)}) collective-permute-start(bf16[160,2048]{1,0:T(8,128)(2,1)S(1)} %get-tuple-element.123.refs_0_), channel_id=1, source_target_pairs={{0,1},{1,0},{2,3},{3,2},{4,5},{5,4},{6,7},{7,6},{8,9},{9,8},{10,11... | collective-permute-start | bytes 1966088 | tf_op jit(solution)/shard_map/ppermute | solution.py:306
  64.3 2.0 %collective-permute-start.13 = (bf16[2,2,1,40,1792]{4,3,2,1,0:T(8,128)(2,1)S(1)}, bf16[2,2,1,40,1792]{4,3,2,1,0:T(8,128)(2,1)S(1)}, u32[]{:S(2)}, u32[]{:S(2)}) collective-permute-start(bf16[2,2,1,40,1792]{4,3,2,1,0:T(8,128)(2,1)S(1)} %get-tuple-element.125), channel_id=1, source_target_pairs={{0,8},{8,0},{16,24},{24,16},{1,9},{9,1},{17,25},{25,17},{2,10},{10... | collective-permute-start | bytes 1720328 | tf_op jit(solution)/shard_map/ppermute | solution.py:306
  64.4 2.8 %collective-permute-start.14 = (bf16[2,2,40,1792]{3,2,1,0:T(8,128)(2,1)S(1)}, bf16[2,2,40,1792]{3,2,1,0:T(8,128)(2,1)S(1)}, u32[]{:S(2)}, u32[]{:S(2)}) collective-permute-start(bf16[2,2,40,1792]{3,2,1,0:T(8,128)(2,1)S(1)} %get-tuple-element.127), channel_id=1, source_target_pairs={{0,8},{8,0},{16,24},{24,16},{1,9},{9,1},{17,25},{25,17},{2,10},{10... | collective-permute-start | bytes 1720328 | tf_op jit(solution)/shard_map/ppermute | solution.py:306
  67.4 15.1 %collective-permute-start.16 = (bf16[2,2,40,1792]{3,2,1,0:T(8,128)(2,1)S(1)}, bf16[2,2,40,1792]{3,2,1,0:T(8,128)(2,1)S(1)}, u32[]{:S(2)}, u32[]{:S(2)}) collective-permute-start(bf16[2,2,40,1792]{3,2,1,0:T(8,128)(2,1)S(1)} %get-tuple-element.130), channel_id=1, source_target_pairs={{0,16},{8,24},{16,0},{24,8},{1,17},{9,25},{17,1},{25,9},{2,18},{10... | collective-permute-start | bytes 1720328 | tf_op jit(solution)/shard_map/ppermute | solution.py:306
  71.3 17.2 %collective-permute-start.15 = (bf16[160,2048]{1,0:T(8,128)(2,1)S(1)}, bf16[160,2048]{1,0:T(8,128)(2,1)S(1)}, u32[]{:S(2)}, u32[]{:S(2)}) collective-permute-start(bf16[160,2048]{1,0:T(8,128)(2,1)S(1)} %collective-permute-done.10.refs_5_.refs_0_), channel_id=1, source_target_pairs={{0,1},{1,0},{2,3},{3,2},{4,5},{5,4},{6,7},{7,6},{8,9},{9,8},{10,11... | collective-permute-start | bytes 1966088 | tf_op jit(solution)/shard_map/ppermute | solution.py:306
  79.0 3.8 %collective-permute-start.18 = (bf16[2,2,1,40,1792]{4,3,2,1,0:T(8,128)(2,1)S(1)}, bf16[2,2,1,40,1792]{4,3,2,1,0:T(8,128)(2,1)S(1)}, u32[]{:S(2)}, u32[]{:S(2)}) collective-permute-start(bf16[2,2,1,40,1792]{4,3,2,1,0:T(8,128)(2,1)S(1)} %get-tuple-element.136), channel_id=1, source_target_pairs={{0,8},{8,0},{16,24},{24,16},{1,9},{9,1},{17,25},{25,17},{2,10},{10... | collective-permute-start | bytes 1720328 | tf_op jit(solution)/shard_map/ppermute | solution.py:306
  79.1 3.8 %collective-permute-start.19 = (bf16[2,2,40,1792]{3,2,1,0:T(8,128)(2,1)S(1)}, bf16[2,2,40,1792]{3,2,1,0:T(8,128)(2,1)S(1)}, u32[]{:S(2)}, u32[]{:S(2)}) collective-permute-start(bf16[2,2,40,1792]{3,2,1,0:T(8,128)(2,1)S(1)} %get-tuple-element.138), channel_id=1, source_target_pairs={{0,8},{8,0},{16,24},{24,16},{1,9},{9,1},{17,25},{25,17},{2,10},{10... | collective-permute-start | bytes 1720328 | tf_op jit(solution)/shard_map/ppermute | solution.py:306
  82.7 1.8 %collective-permute-start.17 = (bf16[2,40,1792]{2,1,0:T(8,128)(2,1)S(1)}, bf16[2,40,1792]{2,1,0:T(8,128)(2,1)S(1)}, u32[]{:S(2)}, u32[]{:S(2)}) collective-permute-start(bf16[2,40,1792]{2,1,0:T(8,128)(2,1)S(1)} %get-tuple-element.132.own_ref), channel_id=1, source_target_pairs={{0,8},{8,0},{16,24},{24,16},{1,9},{9,1},{17,25},{25,17},{2,10},{10... | collective-permute-start | bytes 860168 | tf_op jit(solution)/shard_map/ppermute | solution.py:306
  83.0 15.4 %collective-permute-start.22 = (bf16[2,2,40,1792]{3,2,1,0:T(8,128)(2,1)S(1)}, bf16[2,2,40,1792]{3,2,1,0:T(8,128)(2,1)S(1)}, u32[]{:S(2)}, u32[]{:S(2)}) collective-permute-start(bf16[2,2,40,1792]{3,2,1,0:T(8,128)(2,1)S(1)} %get-tuple-element.144), channel_id=1, source_target_pairs={{0,16},{8,24},{16,0},{24,8},{1,17},{9,25},{17,1},{25,9},{2,18},{10... | collective-permute-start | bytes 1720328 | tf_op jit(solution)/shard_map/ppermute | solution.py:306
  88.4 16.9 %collective-permute-start.27 = (bf16[2,40,4096]{2,1,0:T(8,128)(2,1)S(1)}, bf16[2,40,4096]{2,1,0:T(8,128)(2,1)S(1)}, u32[]{:S(2)}, u32[]{:S(2)}) collective-permute-start(bf16[2,40,4096]{2,1,0:T(8,128)(2,1)S(1)} %get-tuple-element.156), channel_id=1, source_target_pairs={{0,1},{1,0},{2,3},{3,2},{4,5},{5,4},{6,7},{7,6},{8,9},{9,8},{10,11... | collective-permute-start | bytes 1966088 | tf_op jit(solution)/shard_map/ppermute | solution.py:306
  95.1 3.7 %collective-permute-start.20 = (bf16[1,2,1,40,1792]{4,3,2,1,0:T(8,128)(2,1)S(1)}, bf16[1,2,1,40,1792]{4,3,2,1,0:T(8,128)(2,1)S(1)}, u32[]{:S(2)}, u32[]{:S(2)}) collective-permute-start(bf16[1,2,1,40,1792]{4,3,2,1,0:T(8,128)(2,1)S(1)} %get-tuple-element.142), channel_id=1, source_target_pairs={{0,8},{8,0},{16,24},{24,16},{1,9},{9,1},{17,25},{25,17},{2,10},{10... | collective-permute-start | bytes 860168 | tf_op jit(solution)/shard_map/ppermute | solution.py:306
  95.2 3.6 %collective-permute-start.21 = (bf16[1,2,1,40,1792]{4,3,2,1,0:T(8,128)(2,1)S(1)}, bf16[1,2,1,40,1792]{4,3,2,1,0:T(8,128)(2,1)S(1)}, u32[]{:S(2)}, u32[]{:S(2)}) collective-permute-start(bf16[1,2,1,40,1792]{4,3,2,1,0:T(8,128)(2,1)S(1)} %get-tuple-element.143), channel_id=1, source_target_pairs={{0,8},{8,0},{16,24},{24,16},{1,9},{9,1},{17,25},{25,17},{2,10},{10... | collective-permute-start | bytes 860168 | tf_op jit(solution)/shard_map/ppermute | solution.py:306
  98.7 2.3 %collective-permute-start.26 = (bf16[2,40,1792]{2,1,0:T(8,128)(2,1)S(1)}, bf16[2,40,1792]{2,1,0:T(8,128)(2,1)S(1)}, u32[]{:S(2)}, u32[]{:S(2)}) collective-permute-start(bf16[2,40,1792]{2,1,0:T(8,128)(2,1)S(1)} %get-tuple-element.152.own_ref), channel_id=1, source_target_pairs={{0,8},{8,0},{16,24},{24,16},{1,9},{9,1},{17,25},{25,17},{2,10},{10... | collective-permute-start | bytes 860168 | tf_op jit(solution)/shard_map/ppermute | solution.py:306
  99.0 16.1 %collective-permute-start.25 = (bf16[2,2,40,1792]{3,2,1,0:T(8,128)(2,1)S(1)}, bf16[2,2,40,1792]{3,2,1,0:T(8,128)(2,1)S(1)}, u32[]{:S(2)}, u32[]{:S(2)}) collective-permute-start(bf16[2,2,40,1792]{3,2,1,0:T(8,128)(2,1)S(1)} %get-tuple-element.151), channel_id=1, source_target_pairs={{0,8},{8,0},{16,24},{24,16},{1,9},{9,1},{17,25},{25,17},{2,10},{10... | collective-permute-start | bytes 1720328 | tf_op jit(solution)/shard_map/ppermute | solution.py:306
  99.5 15.5 %collective-permute-start.23 = (bf16[2,2,40,1792]{3,2,1,0:T(8,128)(2,1)S(1)}, bf16[2,2,40,1792]{3,2,1,0:T(8,128)(2,1)S(1)}, u32[]{:S(2)}, u32[]{:S(2)}) collective-permute-start(bf16[2,2,40,1792]{3,2,1,0:T(8,128)(2,1)S(1)} %get-tuple-element.147), channel_id=1, source_target_pairs={{0,16},{8,24},{16,0},{24,8},{1,17},{9,25},{17,1},{25,9},{2,18},{10... | collective-permute-start | bytes 1720328 | tf_op jit(solution)/shard_map/ppermute | solution.py:306
  105.4 9.0 %collective-permute-start.28 = (bf16[1,40,4096]{2,1,0:T(8,128)(2,1)S(1)}, bf16[1,40,4096]{2,1,0:T(8,128)(2,1)S(1)}, u32[]{:S(2)}, u32[]{:S(2)}) collective-permute-start(bf16[1,40,4096]{2,1,0:T(8,128)(2,1)S(1)} %get-tuple-element.157), channel_id=1, source_target_pairs={{0,1},{1,0},{2,3},{3,2},{4,5},{5,4},{6,7},{7,6},{8,9},{9,8},{10,11... | collective-permute-start | bytes 983048 | tf_op jit(solution)/shard_map/ppermute | solution.py:306
  106.0 17.7 %collective-permute-start.31 = (bf16[2,40,4096]{2,1,0:T(8,128)(2,1)S(1)}, bf16[2,40,4096]{2,1,0:T(8,128)(2,1)S(1)}, u32[]{:S(2)}, u32[]{:S(2)}) collective-permute-start(bf16[2,40,4096]{2,1,0:T(8,128)(2,1)S(1)} %get-tuple-element.171), channel_id=1, source_target_pairs={{0,2},{1,3},{2,0},{3,1},{4,6},{5,7},{6,4},{7,5},{8,10},{9,11},{10,... | collective-permute-start | bytes 1966088 | tf_op jit(solution)/shard_map/ppermute | solution.py:334
  114.5 9.3 %collective-permute-start.30 = (bf16[1,40,4096]{2,1,0:T(8,128)(2,1)S(1)}, bf16[1,40,4096]{2,1,0:T(8,128)(2,1)S(1)}, u32[]{:S(2)}, u32[]{:S(2)}) collective-permute-start(bf16[1,40,4096]{2,1,0:T(8,128)(2,1)S(1)} %get-tuple-element.169), channel_id=1, source_target_pairs={{0,1},{1,0},{2,3},{3,2},{4,5},{5,4},{6,7},{7,6},{8,9},{9,8},{10,11... | collective-permute-start | bytes 983048 | tf_op jit(solution)/shard_map/ppermute | solution.py:306
  115.3 1.8 %collective-permute-start.29 = (bf16[2,40,1792]{2,1,0:T(8,128)(2,1)S(1)}, bf16[2,40,1792]{2,1,0:T(8,128)(2,1)S(1)}, u32[]{:S(2)}, u32[]{:S(2)}) collective-permute-start(bf16[2,40,1792]{2,1,0:T(8,128)(2,1)S(1)} %get-tuple-element.162.own_ref), channel_id=1, source_target_pairs={{0,8},{8,0},{16,24},{24,16},{1,9},{9,1},{17,25},{25,17},{2,10},{10... | collective-permute-start | bytes 860168 | tf_op jit(solution)/shard_map/ppermute | solution.py:306
  115.4 20.5 %collective-permute-start.24 = (bf16[2,2,40,1792]{3,2,1,0:T(8,128)(2,1)S(1)}, bf16[2,2,40,1792]{3,2,1,0:T(8,128)(2,1)S(1)}, u32[]{:S(2)}, u32[]{:S(2)}) collective-permute-start(bf16[2,2,40,1792]{3,2,1,0:T(8,128)(2,1)S(1)} %get-tuple-element.148), channel_id=1, source_target_pairs={{0,16},{8,24},{16,0},{24,8},{1,17},{9,25},{17,1},{25,9},{2,18},{10... | collective-permute-start | bytes 1720328 | tf_op jit(solution)/shard_map/ppermute | solution.py:306
  116.7 14.1 %collective-permute-start.33 = (bf16[1,40,4096]{2,1,0:T(8,128)(2,1)S(1)}, bf16[1,40,4096]{2,1,0:T(8,128)(2,1)S(1)}, u32[]{:S(2)}, u32[]{:S(2)}) collective-permute-start(bf16[1,40,4096]{2,1,0:T(8,128)(2,1)S(1)} %get-tuple-element.168), channel_id=1, source_target_pairs={{0,2},{1,3},{2,0},{3,1},{4,6},{5,7},{6,4},{7,5},{8,10},{9,11},{10,... | collective-permute-start | bytes 983048 | tf_op jit(solution)/shard_map/ppermute | solution.py:334
  123.8 7.9 %collective-permute-start.32 = (bf16[1,40,4096]{2,1,0:T(8,128)(2,1)S(1)}, bf16[1,40,4096]{2,1,0:T(8,128)(2,1)S(1)}, u32[]{:S(2)}, u32[]{:S(2)}) collective-permute-start(bf16[1,40,4096]{2,1,0:T(8,128)(2,1)S(1)} %get-tuple-element.173), channel_id=1, source_target_pairs={{0,1},{1,0},{2,3},{3,2},{4,5},{5,4},{6,7},{7,6},{8,9},{9,8},{10,11... | collective-permute-start | bytes 983048 | tf_op jit(solution)/shard_map/ppermute | solution.py:306
  125.4 13.9 %collective-permute-start.35 = (bf16[1,40,4096]{2,1,0:T(8,128)(2,1)S(1)}, bf16[1,40,4096]{2,1,0:T(8,128)(2,1)S(1)}, u32[]{:S(2)}, u32[]{:S(2)}) collective-permute-start(bf16[1,40,4096]{2,1,0:T(8,128)(2,1)S(1)} %get-tuple-element.172), channel_id=1, source_target_pairs={{0,2},{1,3},{2,0},{3,1},{4,6},{5,7},{6,4},{7,5},{8,10},{9,11},{10,... | collective-permute-start | bytes 983048 | tf_op jit(solution)/shard_map/ppermute | solution.py:334
  131.9 11.3 %collective-permute-start.36 = (bf16[1,40,4096]{2,1,0:T(8,128)(2,1)S(1)}, bf16[1,40,4096]{2,1,0:T(8,128)(2,1)S(1)}, u32[]{:S(2)}, u32[]{:S(2)}) collective-permute-start(bf16[1,40,4096]{2,1,0:T(8,128)(2,1)S(1)} %get-tuple-element.182), channel_id=1, source_target_pairs={{0,1},{1,0},{2,3},{3,2},{4,5},{5,4},{6,7},{7,6},{8,9},{9,8},{10,11... | collective-permute-start | bytes 983048 | tf_op jit(solution)/shard_map/ppermute | solution.py:306
  133.4 24.6 %collective-permute-start.39 = (bf16[1,40,4096]{2,1,0:T(8,128)(2,1)S(1)}, bf16[1,40,4096]{2,1,0:T(8,128)(2,1)S(1)}, u32[]{:S(2)}, u32[]{:S(2)}) collective-permute-start(bf16[1,40,4096]{2,1,0:T(8,128)(2,1)S(1)} %get-tuple-element.181), channel_id=1, source_target_pairs={{0,4},{1,5},{4,0},{5,1},{2,6},{3,7},{6,2},{7,3},{8,12},{9,13},{12,... | collective-permute-start | bytes 983048 | tf_op jit(solution)/shard_map/ppermute | solution.py:334
  136.1 3.2 %collective-permute-start.34 = (bf16[2,40,1792]{2,1,0:T(8,128)(2,1)S(1)}, bf16[2,40,1792]{2,1,0:T(8,128)(2,1)S(1)}, u32[]{:S(2)}, u32[]{:S(2)}) collective-permute-start(bf16[2,40,1792]{2,1,0:T(8,128)(2,1)S(1)} %get-tuple-element.176.own_ref), channel_id=1, source_target_pairs={{0,8},{8,0},{16,24},{24,16},{1,9},{9,1},{17,25},{25,17},{2,10},{10... | collective-permute-start | bytes 860168 | tf_op jit(solution)/shard_map/ppermute | solution.py:306
  143.3 19.0 %collective-permute-start.38 = (bf16[1,40,4096]{2,1,0:T(8,128)(2,1)S(1)}, bf16[1,40,4096]{2,1,0:T(8,128)(2,1)S(1)}, u32[]{:S(2)}, u32[]{:S(2)}) collective-permute-start(bf16[1,40,4096]{2,1,0:T(8,128)(2,1)S(1)} %get-tuple-element.186), channel_id=1, source_target_pairs={{0,4},{1,5},{4,0},{5,1},{2,6},{3,7},{6,2},{7,3},{8,12},{9,13},{12,... | collective-permute-start | bytes 983048 | tf_op jit(solution)/shard_map/ppermute | solution.py:334
  144.0 15.1 %collective-permute-start.37 = (bf16[2,40,4096]{2,1,0:T(8,128)(2,1)S(1)}, bf16[2,40,4096]{2,1,0:T(8,128)(2,1)S(1)}, u32[]{:S(2)}, u32[]{:S(2)}) collective-permute-start(bf16[2,40,4096]{2,1,0:T(8,128)(2,1)S(1)} %get-tuple-element.183), channel_id=1, source_target_pairs={{0,1},{1,0},{2,3},{3,2},{4,5},{5,4},{6,7},{7,6},{8,9},{9,8},{10,11... | collective-permute-start | bytes 1966088 | tf_op jit(solution)/shard_map/ppermute | solution.py:306
  159.3 3.0 %collective-permute-start.40 = (bf16[40,4096]{1,0:T(8,128)(2,1)S(1)}, bf16[40,4096]{1,0:T(8,128)(2,1)S(1)}, u32[]{:S(2)}, u32[]{:S(2)}) collective-permute-start(bf16[40,4096]{1,0:T(8,128)(2,1)S(1)} %fusion.4), channel_id=1, source_target_pairs={{0,8},{8,0},{16,24},{24,16},{1,9},{9,1},{17,25},{25,17},{2,10},{10... | collective-permute-start | bytes 983048 | tf_op jit(solution)/shard_map/ppermute | solution.py:306

commit v12 on v11

--- a/solution.py
+++ b/solution.py
@@ -12,7 +12,8 @@
 PLANES = 4
 NEXT = ((0, 1), (1, 0), (2, 3), (3, 2))
 SECOND = ((0, 2), (2, 0), (1, 3), (3, 1))
-MIRROR = ((0, 3), (3, 0), (1, 2), (2, 1))
+ACROSS = ((1, 2), (2, 1))
+AROUND = ((0, 3), (3, 0))
 CYCLE = ((0, 2), (2, 3), (3, 1), (1, 0))
 VMEM = 12 * 1024 * 1024
 F32 = jnp.float32
@@ -125,30 +126,31 @@
     return rearranged(join_kernel, "join", (rows, stacks[0].shape[3]), stacks, after, hint)
 
 
-def pick_kernel(after_count, place_ref, *refs):
-    inner_ref, outer_ref = refs[:2]
-    picked_ref, token_ref = refs[2 + after_count :]
+def pick_kernel(after_count, place_ref, inner_three_ref, outer_three_ref, mine_ref, *refs):
+    three_ref, passed_ref, token_ref = refs[after_count:]
     token_ref[...] = jnp.zeros_like(token_ref)
 
     @pl.when(place_ref[1] == 1)
     def _():
-        picked_ref[...] = inner_ref[...]
+        three_ref[...] = inner_three_ref[...]
+        passed_ref[...] = inner_three_ref[...]
 
     @pl.when(place_ref[1] == 0)
     def _():
-        picked_ref[...] = outer_ref[...]
-
-
-def pick(place, on_inner, on_outer, after):
+        three_ref[...] = outer_three_ref[...]
+        passed_ref[...] = mine_ref[...]
+
+
+def pick(place, inner_three, outer_three, mine, after):
     return pl.pallas_call(
         functools.partial(pick_kernel, len(after)),
-        in_specs=[pl.BlockSpec(memory_space=pltpu.SMEM)] + [INSIDE] * 2 + [ANYWHERE] * len(after),
-        out_specs=[INSIDE] * 2,
-        out_shape=[jax.ShapeDtypeStruct(on_inner.shape, BF16), TOKEN],
+        in_specs=[pl.BlockSpec(memory_space=pltpu.SMEM)] + [INSIDE] * 3 + [ANYWHERE] * len(after),
+        out_specs=[INSIDE] * 3,
+        out_shape=[jax.ShapeDtypeStruct(mine.shape, BF16)] * 2 + [TOKEN],
         compiler_params=pltpu.CompilerParams(vmem_limit_bytes=VMEM // 2),
-        cost_estimate=as_if(0),
+        cost_estimate=as_if(8),
         name="pick",
-    )(place, on_inner, on_outer, *after)
+    )(place, inner_three, outer_three, mine, *after)
 
 
 def resident(values):
@@ -386,13 +388,15 @@
         return summed
 
     next_stacks = [by_plane(first, NEXT), by_plane(second, NEXT)]
-    mirror_stacks = [by_plane(first, MIRROR)]
-    forward(0, mine)
+    across_stacks = [by_plane(first, ACROSS), by_plane(second, ACROSS)]
+    forward(0, mine, [next_stacks[0], across_stacks[0]])
     up_kept, last[0] = masked(
-        up_weight, up_mask, tile_of(features, 256), place, 1, lambda core: 0, last + next_stacks[:1] + mirror_stacks, 0.15
+        up_weight, up_mask, tile_of(features, 256), place, 1, lambda core: 0,
+        last + [next_stacks[0], across_stacks[0]], 0.15
     )
     one_away, last[0] = join(next_stacks, last)
-    mirror_stacks.append(by_plane(second, MIRROR, [one_away]))
+    inner_three, last[0] = join(across_stacks, last)
+    outer_three = by_plane(mine, AROUND, last)
     down_kept = []
     for share, hint in ((0, 8), (1, 0)):
         part, last[0] = masked(
@@ -404,8 +408,7 @@
     multiply_in(0, hint=0)
     exchange(0)
     exchange_near(0)
-    three_away, last[0] = join(mirror_stacks, last, 8)
-    passed, last[0] = pick(place, three_away, mine, last)
+    three_away, passed, last[0] = pick(place, inner_three, outer_three, mine, last)
     two_away = by_plane(passed, CYCLE)
     to_chips(0, [near[0]])
     forward(3, three_away, [*parts[1][1:], *last])

time: 164 us -> 159 us (0.970)
  waiting for transfers between devices: 60.2 us -> 55.9 us
    ppermute x10 -> x11, waiting for transfers between devices: 35.5 us -> 29.8 us  [by_plane(): return lax.ppermute(behind(values, after), 'cols', pairs)]
    ppermute x10 -> x11, starting transfers between devices: 14.3 us -> 13.2 us  [by_plane(): return lax.ppermute(behind(values, after), 'cols', pairs)]
  transfers between devices with their start and end apart: 41 -> 42, of which waited for: 19 -> 19; matrix products, arithmetic and copies ran while one was open for 0% -> 0% of each run, Pallas kernels for 36% -> 37%
where the time goes in v12:
time: 159 us; the launch traced here: 158 us
  Pallas kernels  58.9 us (37%)
  waiting for transfers between devices  55.9 us (35%)
  starting transfers between devices  39.1 us (25%)
  other arithmetic  3.97 us (2%)
    ppermute x11, waiting for transfers between devices, by_plane(): return lax.ppermute(behind(values, after), 'cols', pairs)  29.8 us
    ppermute x31, waiting for transfers between devices, swap(): lax.ppermute(values, axis, [(place, place ^ step) for place in range(size)])  26.1 us
    ppermute x31, starting transfers between devices, swap(): lax.ppermute(values, axis, [(place, place ^ step) for place in range(size)])  25.8 us
    pallas_call x4, Pallas kernels, gate_up(): pl.pallas_call(functools.partial(gate_up_kernel, len(parts), len(after)),...  24.3 us
    pallas_call x4, Pallas kernels, down(): pl.pallas_call(functools.partial(down_kernel, pieces, len(down_kept), len...  15.5 us
    pallas_call x4, Pallas kernels, masked(): pl.pallas_call(functools.partial(mask_kernel, share, rows, len(after)), i...  15.4 us
    ppermute x11, starting transfers between devices, by_plane(): return lax.ppermute(behind(values, after), 'cols', pairs)  13.2 us
  transfers between devices with their start and end apart: 42, of which 19 were waited for; matrix products, arithmetic and copies ran while one was open for 0% of the time, Pallas kernels for 37%

profile of v12, /device:TPU:0, one launch (start us, length us, event | category | flops | bytes accessed | tf_op | source)
XLA Modules:
  0.0 158.3 jit_solution(11413089462769842204)
XLA Ops:
  0.0 1.3 fusion
  1.4 1.3 fusion.2
  3.3 2.6 %collective-permute-start.2 = (bf16[40,2048]{1,0:T(8,128)(2,1)S(1)}, bf16[40,2048]{1,0:T(8,128)(2,1)S(1)}, u32[]{:S(2)}, u32[]{:S(2)}) collective-permute-start(bf16[40,2048]{1,0:T(8,128)(2,1)S(1)} %get-tuple-element.195), channel_id=1, source_target_pairs={{0,24},{8,16},{16,8},{24,0},{1,25},{9,17},{17,9},{25,1},{2,26},{10... | collective-permute-start | bytes 491528 | tf_op jit(solution)/shard_map/ppermute | solution.py:308
  6.0 0.7 collective-permute-start.4
  6.6 4.9 %collective-permute-start.3 = (bf16[2,1,40,2048]{3,2,1,0:T(8,128)(2,1)S(1)}, bf16[2,1,40,2048]{3,2,1,0:T(8,128)(2,1)S(1)}, u32[]{:S(2)}, u32[]{:S(2)}) collective-permute-start(bf16[2,1,40,2048]{3,2,1,0:T(8,128)(2,1)S(1)} %get-tuple-element.99.refs_0_), channel_id=1, source_target_pairs={{0,2},{1,3},{2,0},{3,1},{4,6},{5,7},{6,4},{7,5},{8,10},{9,11},{10,... | collective-permute-start | bytes 983048 | tf_op jit(solution)/shard_map/ppermute | solution.py:336
  11.7 3.8 %masked.4 = (bf16[2048,1792]{1,0:T(8,128)(2,1)S(1)}, f32[8,128]{1,0:T(8,128)S(1)}) custom-call(s32[2]{0:T(128)S(1)} %pad_add_fusion.core_ref.place_ref, bf16[2048,1792]{1,0:T(8,128)(2,1)} %weight_ref.4, s32[32,28]{1,0:T(8,128)S(1)} %copy-done, f32[8,128]{1,0:T(8,128)S(1)} %get-tuple-element.100.refs_0_), custom_call_target="tpu_custom_call" | custom-call | tf_op jit(solution)/shard_map/masked/pallas_call | solution.py:81
  16.0 0.7 collective-permute-start.6
  16.8 3.4 %collective-permute-done.3.refs_1_.refs_0_ = bf16[2,1,40,2048]{3,2,1,0:T(8,128)(2,1)S(1)} collective-permute-done((bf16[2,1,40,2048]{3,2,1,0:T(8,128)(2,1)S(1)}, bf16[2,1,40,2048]{3,2,1,0:T(8,128)(2,1)S(1)}, u32[]{:S(2)}, u32[]{:S(2)}) %collective-permute-start.3) | collective-permute-done | bytes 327712 | tf_op jit(solution)/shard_map/ppermute | solution.py:336
  20.2 1.5 collective-permute-start.5
  21.7 3.8 %masked.5 = (bf16[2048,1792]{1,0:T(8,128)(2,1)S(1)}, f32[8,128]{1,0:T(8,128)S(1)}) custom-call(s32[2]{0:T(128)S(1)} %pad_add_fusion.core_ref.place_ref, bf16[2048,1792]{1,0:T(8,128)(2,1)} %weight_ref.5, s32[32,28]{1,0:T(8,128)S(1)} %copy-done.1, f32[8,128]{1,0:T(8,128)S(1)} %get-tuple-element.107.refs_0_, ...), custom_call_target="tpu_custom_call" | custom-call | flops 172500000 | tf_op jit(solution)/shard_map/masked/pallas_call | solution.py:81
  26.1 3.3 %collective-permute-start.10 = (bf16[160,2048]{1,0:T(8,128)(2,1)S(1)}, bf16[160,2048]{1,0:T(8,128)(2,1)S(1)}, u32[]{:S(2)}, u32[]{:S(2)}) collective-permute-start(bf16[160,2048]{1,0:T(8,128)(2,1)S(1)} %get-tuple-element.105.refs_0_.mine_ref), channel_id=1, source_target_pairs={{0,6},{1,7},{6,0},{7,1},{8,14},{9,15},{14,8},{15,9},{16,22},{17,23... | collective-permute-start | bytes 1966088 | tf_op jit(solution)/shard_map/ppermute | solution.py:336
  29.4 3.9 %masked.6 = (bf16[1792,2048]{1,0:T(8,128)(2,1)S(1)}, f32[8,128]{1,0:T(8,128)S(1)}) custom-call(s32[2]{0:T(128)S(1)} %pad_add_fusion.core_ref.place_ref, bf16[1792,8192]{1,0:T(8,128)(2,1)} %weight_ref.7, s32[28,128]{1,0:T(8,128)S(1)} %copy-done.2, f32[8,128]{1,0:T(8,128)S(1)} %get-tuple-element.111.refs_0_), custom_call_target="tpu_custom_call" | custom-call | flops 9200000000 | tf_op jit(solution)/shard_map/masked/pallas_call | solution.py:81
  33.3 3.9 %masked.7 = (bf16[1792,2048]{1,0:T(8,128)(2,1)S(1)}, f32[8,128]{1,0:T(8,128)S(1)}) custom-call(s32[2]{0:T(128)S(1)} %pad_add_fusion.core_ref.place_ref, bf16[1792,8192]{1,0:T(8,128)(2,1)} %weight_ref.7, s32[28,128]{1,0:T(8,128)S(1)} %copy-done.2, f32[8,128]{1,0:T(8,128)S(1)} %get-tuple-element.112.refs_0_), custom_call_target="tpu_custom_call" | custom-call | tf_op jit(solution)/shard_map/masked/pallas_call | solution.py:81
  37.2 1.6 %collective-permute-start.12 = (bf16[160,2048]{1,0:T(8,128)(2,1)S(1)}, bf16[160,2048]{1,0:T(8,128)(2,1)S(1)}, u32[]{:S(2)}, u32[]{:S(2)}) collective-permute-start(bf16[160,2048]{1,0:T(8,128)(2,1)S(1)} %get-tuple-element.125.refs_0_), channel_id=1, source_target_pairs={{0,1},{1,0},{2,3},{3,2},{4,5},{5,4},{6,7},{7,6},{8,9},{9,8},{10,11... | collective-permute-start | bytes 1966088 | tf_op jit(solution)/shard_map/ppermute | solution.py:308
  38.8 6.1 %gate_up.4 = (bf16[2,2,2,40,1792]{4,3,2,1,0:T(8,128)(2,1)S(1)}, bf16[2,2,40,1792]{3,2,1,0:T(8,128)(2,1)S(1)}, bf16[2,2,1,40,1792]{4,3,2,1,0:T(8,128)(2,1)S(1)}, f32[8,128]{1,0:T(8,128)S(1)}) custom-call(bf16[160,2048]{1,0:T(8,128)(2,1)S(1)} %get-tuple-element.105.refs_0_.mine_ref, bf16[160,2048]{1,0:T(8,128)(2,1)S(1)} %collective-permute-done.5.refs_1_, ...), custom_call_target="tpu_custom_call" | custom-call | tf_op jit(solution)/shard_map/gate_up/pallas_call | solution.py:190
  46.1 1.0 collective-permute-start.11
  47.9 4.5 %collective-permute-done.12.refs_1_ = bf16[160,2048]{1,0:T(8,128)(2,1)S(1)} collective-permute-done((bf16[160,2048]{1,0:T(8,128)(2,1)S(1)}, bf16[160,2048]{1,0:T(8,128)(2,1)S(1)}, u32[]{:S(2)}, u32[]{:S(2)}) %collective-permute-start.12) | collective-permute-done | bytes 655392 | tf_op jit(solution)/shard_map/ppermute | solution.py:308
  52.4 1.5 collective-permute-start.13
  53.9 6.1 %gate_up.5 = (bf16[2,2,2,40,1792]{4,3,2,1,0:T(8,128)(2,1)S(1)}, bf16[2,2,40,1792]{3,2,1,0:T(8,128)(2,1)S(1)}, bf16[2,2,1,40,1792]{4,3,2,1,0:T(8,128)(2,1)S(1)}, f32[8,128]{1,0:T(8,128)S(1)}) custom-call(bf16[160,2048]{1,0:T(8,128)(2,1)S(1)} %get-tuple-element.125.refs_0_, bf16[160,2048]{1,0:T(8,128)(2,1)S(1)} %collective-permute-done.12.refs_1_, ...), custom_call_target="tpu_custom_call" | custom-call | flops 4697620480 | tf_op jit(solution)/shard_map/gate_up/pallas_call | solution.py:190
  60.6 1.5 collective-permute-done.14.refs_1_
  62.0 0.8 collective-permute-done.15.refs_3_.refs_1_
  63.0 1.6 collective-permute-start.17
  64.6 2.0 %collective-permute-done.13.refs_1_ = bf16[160,2048]{1,0:T(8,128)(2,1)S(1)} collective-permute-done((bf16[160,2048]{1,0:T(8,128)(2,1)S(1)}, bf16[160,2048]{1,0:T(8,128)(2,1)S(1)}, u32[]{:S(2)}, u32[]{:S(2)}) %collective-permute-start.13) | collective-permute-done | bytes 655392 | tf_op jit(solution)/shard_map/ppermute | solution.py:308
  66.6 2.0 %collective-permute-start.16 = (bf16[160,2048]{1,0:T(8,128)(2,1)S(1)}, bf16[160,2048]{1,0:T(8,128)(2,1)S(1)}, u32[]{:S(2)}, u32[]{:S(2)}) collective-permute-start(bf16[160,2048]{1,0:T(8,128)(2,1)S(1)} %collective-permute-done.11.refs_5_.refs_0_), channel_id=1, source_target_pairs={{0,1},{1,0},{2,3},{3,2},{4,5},{5,4},{6,7},{7,6},{8,9},{9,8},{10,11... | collective-permute-start | bytes 1966088 | tf_op jit(solution)/shard_map/ppermute | solution.py:308
  68.6 6.1 %gate_up.6 = (bf16[2,2,2,40,1792]{4,3,2,1,0:T(8,128)(2,1)S(1)}, bf16[2,2,40,1792]{3,2,1,0:T(8,128)(2,1)S(1)}, bf16[2,2,1,40,1792]{4,3,2,1,0:T(8,128)(2,1)S(1)}, f32[8,128]{1,0:T(8,128)S(1)}) custom-call(bf16[160,2048]{1,0:T(8,128)(2,1)S(1)} %get-tuple-element.127.refs_0_, bf16[160,2048]{1,0:T(8,128)(2,1)S(1)} %collective-permute-done.13.refs_1_, ...), custom_call_target="tpu_custom_call" | custom-call | flops 4697620480 | tf_op jit(solution)/shard_map/gate_up/pallas_call | solution.py:190
  75.3 2.8 %collective-permute-done.17.refs_2_ = bf16[2,2,40,1792]{3,2,1,0:T(8,128)(2,1)S(1)} collective-permute-done((bf16[2,2,40,1792]{3,2,1,0:T(8,128)(2,1)S(1)}, bf16[2,2,40,1792]{3,2,1,0:T(8,128)(2,1)S(1)}, u32[]{:S(2)}, u32[]{:S(2)}) %collective-permute-start.17) | collective-permute-done | bytes 573472 | tf_op jit(solution)/shard_map/ppermute | solution.py:308
  78.6 1.6 collective-permute-start.23
  80.2 3.9 %down.4 = (bf16[2,40,4096]{2,1,0:T(8,128)(2,1)S(1)}, bf16[2,40,4096]{2,1,0:T(8,128)(2,1)S(1)}, f32[8,128]{1,0:T(8,128)S(1)}) custom-call(bf16[2,40,1792]{2,1,0:T(8,128)(2,1)S(1)} %get-tuple-element.136.own_ref, bf16[2,40,1792]{2,1,0:T(8,128)(2,1)S(1)} %collective-permute-done.18.other_ref, bf16[1792,2048]{1,0:T(8,128)(2,1)S(1)} %get-tuple-element.137.refs_0_, ...), custom_call_target="tpu_custom_call" | custom-call | flops 2348810 | tf_op jit(solution)/shard_map/down/pallas_call | solution.py:232
  84.6 6.1 %gate_up.7 = (bf16[2,2,2,40,1792]{4,3,2,1,0:T(8,128)(2,1)S(1)}, bf16[2,2,40,1792]{3,2,1,0:T(8,128)(2,1)S(1)}, bf16[1,2,1,40,1792]{4,3,2,1,0:T(8,128)(2,1)S(1)}, ...) custom-call(bf16[160,2048]{1,0:T(8,128)(2,1)S(1)} %collective-permute-done.11.refs_5_.refs_0_, ...), custom_call_target="tpu_custom_call" | custom-call | flops 4697620480 | tf_op jit(solution)/shard_map/gate_up/pallas_call | solution.py:190
  91.3 2.8 %collective-permute-done.23.refs_2_ = bf16[2,2,40,1792]{3,2,1,0:T(8,128)(2,1)S(1)} collective-permute-done((bf16[2,2,40,1792]{3,2,1,0:T(8,128)(2,1)S(1)}, bf16[2,2,40,1792]{3,2,1,0:T(8,128)(2,1)S(1)}, u32[]{:S(2)}, u32[]{:S(2)}) %collective-permute-start.23) | collective-permute-done | bytes 573472 | tf_op jit(solution)/shard_map/ppermute | solution.py:308
  95.1 1.5 collective-permute-start.24
  96.6 3.9 %down.5 = (bf16[1,40,4096]{2,1,0:T(8,128)(2,1)S(1)}, bf16[1,40,4096]{2,1,0:T(8,128)(2,1)S(1)}, bf16[1,40,4096]{2,1,0:T(8,128)(2,1)S(1)}, bf16[1,40,4096]{2,1,0:T(8,128)(2,1)S(1)}, f32[8,128]{1,0:T(8,128)S(1)}) custom-call(bf16[2,40,1792]{2,1,0:T(8,128)(2,1)S(1)} %get-tuple-element.156.own_ref, bf16[2,40,1792]{2,1,0:T(8,128)(2,1)S(1)} %collective-permute-done.27.other_ref, ...), custom_call_target="tpu_custom_call" | custom-call | flops 2348810 | tf_op jit(solution)/shard_map/down/pallas_call | solution.py:232
  101.7 8.3 %collective-permute-done.29.refs_1_ = bf16[1,40,4096]{2,1,0:T(8,128)(2,1)S(1)} collective-permute-done((bf16[1,40,4096]{2,1,0:T(8,128)(2,1)S(1)}, bf16[1,40,4096]{2,1,0:T(8,128)(2,1)S(1)}, u32[]{:S(2)}, u32[]{:S(2)}) %collective-permute-start.29) | collective-permute-done | bytes 327712 | tf_op jit(solution)/shard_map/ppermute | solution.py:308
  111.1 1.2 collective-permute-start.25
  112.6 3.9 %down.6 = (bf16[1,40,4096]{2,1,0:T(8,128)(2,1)S(1)}, bf16[1,40,4096]{2,1,0:T(8,128)(2,1)S(1)}, bf16[1,40,4096]{2,1,0:T(8,128)(2,1)S(1)}, bf16[1,40,4096]{2,1,0:T(8,128)(2,1)S(1)}, f32[8,128]{1,0:T(8,128)S(1)}) custom-call(bf16[2,40,1792]{2,1,0:T(8,128)(2,1)S(1)} %get-tuple-element.166.own_ref, bf16[2,40,1792]{2,1,0:T(8,128)(2,1)S(1)} %collective-permute-done.30.other_ref, ...), custom_call_target="tpu_custom_call" | custom-call | flops 2348810 | tf_op jit(solution)/shard_map/down/pallas_call | solution.py:232
  116.5 2.9 %collective-permute-done.32.refs_3_.refs_1_ = bf16[2,40,4096]{2,1,0:T(8,128)(2,1)S(1)} collective-permute-done((bf16[2,40,4096]{2,1,0:T(8,128)(2,1)S(1)}, bf16[2,40,4096]{2,1,0:T(8,128)(2,1)S(1)}, u32[]{:S(2)}, u32[]{:S(2)}) %collective-permute-start.32) | collective-permute-done | bytes 655392 | tf_op jit(solution)/shard_map/ppermute | solution.py:336
  119.5 1.6 %collective-permute-start.33 = (bf16[1,40,4096]{2,1,0:T(8,128)(2,1)S(1)}, bf16[1,40,4096]{2,1,0:T(8,128)(2,1)S(1)}, u32[]{:S(2)}, u32[]{:S(2)}) collective-permute-start(bf16[1,40,4096]{2,1,0:T(8,128)(2,1)S(1)} %get-tuple-element.177), channel_id=1, source_target_pairs={{0,1},{1,0},{2,3},{3,2},{4,5},{5,4},{6,7},{7,6},{8,9},{9,8},{10,11... | collective-permute-start | bytes 983048 | tf_op jit(solution)/shard_map/ppermute | solution.py:308
  121.1 5.3 %collective-permute-done.34.refs_2_ = bf16[1,40,4096]{2,1,0:T(8,128)(2,1)S(1)} collective-permute-done((bf16[1,40,4096]{2,1,0:T(8,128)(2,1)S(1)}, bf16[1,40,4096]{2,1,0:T(8,128)(2,1)S(1)}, u32[]{:S(2)}, u32[]{:S(2)}) %collective-permute-start.34) | collective-permute-done | bytes 327712 | tf_op jit(solution)/shard_map/ppermute | solution.py:336
  126.4 0.9 collective-permute-done.33.refs_1_
  127.5 1.6 collective-permute-start.37
  129.0 1.7 %collective-permute-start.40 = (bf16[1,40,4096]{2,1,0:T(8,128)(2,1)S(1)}, bf16[1,40,4096]{2,1,0:T(8,128)(2,1)S(1)}, u32[]{:S(2)}, u32[]{:S(2)}) collective-permute-start(bf16[1,40,4096]{2,1,0:T(8,128)(2,1)S(1)} %get-tuple-element.185), channel_id=1, source_target_pairs={{0,4},{1,5},{4,0},{5,1},{2,6},{3,7},{6,2},{7,3},{8,12},{9,13},{12,... | collective-permute-start | bytes 983048 | tf_op jit(solution)/shard_map/ppermute | solution.py:336
  131.1 3.9 %collective-permute-done.36.refs_3_.refs_2_ = bf16[1,40,4096]{2,1,0:T(8,128)(2,1)S(1)} collective-permute-done((bf16[1,40,4096]{2,1,0:T(8,128)(2,1)S(1)}, bf16[1,40,4096]{2,1,0:T(8,128)(2,1)S(1)}, u32[]{:S(2)}, u32[]{:S(2)}) %collective-permute-start.36) | collective-permute-done | bytes 327712 | tf_op jit(solution)/shard_map/ppermute | solution.py:336
  135.0 3.9 %down.7 = (bf16[2,40,4096]{2,1,0:T(8,128)(2,1)S(1)}, bf16[2,40,4096]{2,1,0:T(8,128)(2,1)S(1)}, f32[8,128]{1,0:T(8,128)S(1)}) custom-call(bf16[2,40,1792]{2,1,0:T(8,128)(2,1)S(1)} %get-tuple-element.180.own_ref, bf16[2,40,1792]{2,1,0:T(8,128)(2,1)S(1)} %collective-permute-done.35.other_ref, bf16[1792,2048]{1,0:T(8,128)(2,1)S(1)} %get-tuple-element.137.refs_0_, ...), custom_call_target="tpu_custom_call" | custom-call | flops 2348810 | tf_op jit(solution)/shard_map/down/pallas_call | solution.py:232
  139.4 2.2 %collective-permute-start.38 = (bf16[2,40,4096]{2,1,0:T(8,128)(2,1)S(1)}, bf16[2,40,4096]{2,1,0:T(8,128)(2,1)S(1)}, u32[]{:S(2)}, u32[]{:S(2)}) collective-permute-start(bf16[2,40,4096]{2,1,0:T(8,128)(2,1)S(1)} %get-tuple-element.187), channel_id=1, source_target_pairs={{0,1},{1,0},{2,3},{3,2},{4,5},{5,4},{6,7},{7,6},{8,9},{9,8},{10,11... | collective-permute-start | bytes 1966088 | tf_op jit(solution)/shard_map/ppermute | solution.py:308
  141.6 11.2 %collective-permute-done.40.refs_0_ = bf16[1,40,4096]{2,1,0:T(8,128)(2,1)S(1)} collective-permute-done((bf16[1,40,4096]{2,1,0:T(8,128)(2,1)S(1)}, bf16[1,40,4096]{2,1,0:T(8,128)(2,1)S(1)}, u32[]{:S(2)}, u32[]{:S(2)}) %collective-permute-start.40) | collective-permute-done | bytes 327712 | tf_op jit(solution)/shard_map/ppermute | solution.py:336
  153.5 1.0 collective-permute-done.38
  154.7 2.5 %collective-permute-done.39 = bf16[1,40,4096]{2,1,0:T(8,128)(2,1)S(1)} collective-permute-done((bf16[1,40,4096]{2,1,0:T(8,128)(2,1)S(1)}, bf16[1,40,4096]{2,1,0:T(8,128)(2,1)S(1)}, u32[]{:S(2)}, u32[]{:S(2)}) %collective-permute-start.39) | collective-permute-done | bytes 327712 | tf_op jit(solution)/shard_map/ppermute | solution.py:336
  157.4 0.9 pad_maximum_fusion
  (83 shorter events, 12.7 us)
Async XLA Ops:
  1.3 10.3 %copy-start = (s32[32,28]{1,0:T(8,128)S(1)}, s32[32,28]{1,0:T(8,128)}, u32[]{:S(2)}) copy-start(s32[32,28]{1,0:T(8,128)} %mask_ref.4) | copy-start | bytes 10756
  2.7 3.2 %collective-permute-start = (bf16[40,2048]{1,0:T(8,128)(2,1)S(1)}, bf16[40,2048]{1,0:T(8,128)(2,1)S(1)}, u32[]{:S(2)}, u32[]{:S(2)}) collective-permute-start(bf16[40,2048]{1,0:T(8,128)(2,1)S(1)} %get-tuple-element.197), channel_id=1, source_target_pairs={{0,8},{8,0},{16,24},{24,16},{1,9},{9,1},{17,25},{25,17},{2,10},{10... | collective-permute-start | bytes 491528 | tf_op jit(solution)/shard_map/ppermute | solution.py:308
  3.3 12.2 %collective-permute-start.2 = (bf16[40,2048]{1,0:T(8,128)(2,1)S(1)}, bf16[40,2048]{1,0:T(8,128)(2,1)S(1)}, u32[]{:S(2)}, u32[]{:S(2)}) collective-permute-start(bf16[40,2048]{1,0:T(8,128)(2,1)S(1)} %get-tuple-element.195), channel_id=1, source_target_pairs={{0,24},{8,16},{16,8},{24,0},{1,25},{9,17},{17,9},{25,1},{2,26},{10... | collective-permute-start | bytes 491528 | tf_op jit(solution)/shard_map/ppermute | solution.py:308
  5.9 9.6 %collective-permute-start.1 = (bf16[40,2048]{1,0:T(8,128)(2,1)S(1)}, bf16[40,2048]{1,0:T(8,128)(2,1)S(1)}, u32[]{:S(2)}, u32[]{:S(2)}) collective-permute-start(bf16[40,2048]{1,0:T(8,128)(2,1)S(1)} %get-tuple-element.196), channel_id=1, source_target_pairs={{0,16},{8,24},{16,0},{24,8},{1,17},{9,25},{17,1},{25,9},{2,18},{10... | collective-permute-start | bytes 491528 | tf_op jit(solution)/shard_map/ppermute | solution.py:308
  6.0 10.8 %collective-permute-start.4 = (bf16[2,1,40,2048]{3,2,1,0:T(8,128)(2,1)S(1)}, bf16[2,1,40,2048]{3,2,1,0:T(8,128)(2,1)S(1)}, u32[]{:S(2)}, u32[]{:S(2)}) collective-permute-start(bf16[2,1,40,2048]{3,2,1,0:T(8,128)(2,1)S(1)} %get-tuple-element.99.refs_0_), channel_id=1, source_target_pairs={{2,4},{3,5},{4,2},{5,3},{10,12},{11,13},{12,10},{13,11},{18,20},{1... | collective-permute-start | bytes 983048 | tf_op jit(solution)/shard_map/ppermute | solution.py:336
  6.6 13.5 %collective-permute-start.3 = (bf16[2,1,40,2048]{3,2,1,0:T(8,128)(2,1)S(1)}, bf16[2,1,40,2048]{3,2,1,0:T(8,128)(2,1)S(1)}, u32[]{:S(2)}, u32[]{:S(2)}) collective-permute-start(bf16[2,1,40,2048]{3,2,1,0:T(8,128)(2,1)S(1)} %get-tuple-element.99.refs_0_), channel_id=1, source_target_pairs={{0,2},{1,3},{2,0},{3,1},{4,6},{5,7},{6,4},{7,5},{8,10},{9,11},{10,... | collective-permute-start | bytes 983048 | tf_op jit(solution)/shard_map/ppermute | solution.py:336
  11.7 10.0 %copy-start.1 = (s32[32,28]{1,0:T(8,128)S(1)}, s32[32,28]{1,0:T(8,128)}, u32[]{:S(2)}) copy-start(s32[32,28]{1,0:T(8,128)} %mask_ref.5) | copy-start | bytes 10756
  15.5 10.5 %collective-permute-start.7 = (bf16[2,1,40,2048]{3,2,1,0:T(8,128)(2,1)S(1)}, bf16[2,1,40,2048]{3,2,1,0:T(8,128)(2,1)S(1)}, u32[]{:S(2)}, u32[]{:S(2)}) collective-permute-start(bf16[2,1,40,2048]{3,2,1,0:T(8,128)(2,1)S(1)} %get-tuple-element.102.refs_1_), channel_id=1, source_target_pairs={{0,2},{1,3},{2,0},{3,1},{4,6},{5,7},{6,4},{7,5},{8,10},{9,11},{10,... | collective-permute-start | bytes 983048 | tf_op jit(solution)/shard_map/ppermute | solution.py:336
  16.0 10.0 %collective-permute-start.6 = (bf16[2,1,40,2048]{3,2,1,0:T(8,128)(2,1)S(1)}, bf16[2,1,40,2048]{3,2,1,0:T(8,128)(2,1)S(1)}, u32[]{:S(2)}, u32[]{:S(2)}) collective-permute-start(bf16[2,1,40,2048]{3,2,1,0:T(8,128)(2,1)S(1)} %get-tuple-element.102.refs_1_), channel_id=1, source_target_pairs={{2,4},{3,5},{4,2},{5,3},{10,12},{11,13},{12,10},{13,11},{18,20},{1... | collective-permute-start | bytes 983048 | tf_op jit(solution)/shard_map/ppermute | solution.py:336
  20.2 17.0 %collective-permute-start.5 = (bf16[160,2048]{1,0:T(8,128)(2,1)S(1)}, bf16[160,2048]{1,0:T(8,128)(2,1)S(1)}, u32[]{:S(2)}, u32[]{:S(2)}) collective-permute-start(bf16[160,2048]{1,0:T(8,128)(2,1)S(1)} %get-tuple-element.105.refs_0_.mine_ref), channel_id=1, source_target_pairs={{0,1},{1,0},{2,3},{3,2},{4,5},{5,4},{6,7},{7,6},{8,9},{9,8},{10,11... | collective-permute-start | bytes 1966088 | tf_op jit(solution)/shard_map/ppermute | solution.py:308
  25.5 3.9 %copy-start.2 = (s32[28,128]{1,0:T(8,128)S(1)}, s32[28,128]{1,0:T(8,128)}, u32[]{:S(2)}) copy-start(s32[28,128]{1,0:T(8,128)} %mask_ref.7) | copy-start | bytes 43012
  26.1 19.4 %collective-permute-start.10 = (bf16[160,2048]{1,0:T(8,128)(2,1)S(1)}, bf16[160,2048]{1,0:T(8,128)(2,1)S(1)}, u32[]{:S(2)}, u32[]{:S(2)}) collective-permute-start(bf16[160,2048]{1,0:T(8,128)(2,1)S(1)} %get-tuple-element.105.refs_0_.mine_ref), channel_id=1, source_target_pairs={{0,6},{1,7},{6,0},{7,1},{8,14},{9,15},{14,8},{15,9},{16,22},{17,23... | collective-permute-start | bytes 1966088 | tf_op jit(solution)/shard_map/ppermute | solution.py:336
  37.2 15.2 %collective-permute-start.12 = (bf16[160,2048]{1,0:T(8,128)(2,1)S(1)}, bf16[160,2048]{1,0:T(8,128)(2,1)S(1)}, u32[]{:S(2)}, u32[]{:S(2)}) collective-permute-start(bf16[160,2048]{1,0:T(8,128)(2,1)S(1)} %get-tuple-element.125.refs_0_), channel_id=1, source_target_pairs={{0,1},{1,0},{2,3},{3,2},{4,5},{5,4},{6,7},{7,6},{8,9},{9,8},{10,11... | collective-permute-start | bytes 1966088 | tf_op jit(solution)/shard_map/ppermute | solution.py:308
  44.9 2.2 %collective-permute-start.8 = (bf16[2,2,40,1792]{3,2,1,0:T(8,128)(2,1)S(1)}, bf16[2,2,40,1792]{3,2,1,0:T(8,128)(2,1)S(1)}, u32[]{:S(2)}, u32[]{:S(2)}) collective-permute-start(bf16[2,2,40,1792]{3,2,1,0:T(8,128)(2,1)S(1)} %get-tuple-element.115), channel_id=1, source_target_pairs={{0,8},{8,0},{16,24},{24,16},{1,9},{9,1},{17,25},{25,17},{2,10},{10... | collective-permute-start | bytes 1720328 | tf_op jit(solution)/shard_map/ppermute | solution.py:308
  45.0 2.8 %collective-permute-start.9 = (bf16[2,2,1,40,1792]{4,3,2,1,0:T(8,128)(2,1)S(1)}, bf16[2,2,1,40,1792]{4,3,2,1,0:T(8,128)(2,1)S(1)}, u32[]{:S(2)}, u32[]{:S(2)}) collective-permute-start(bf16[2,2,1,40,1792]{4,3,2,1,0:T(8,128)(2,1)S(1)} %get-tuple-element.116), channel_id=1, source_target_pairs={{0,8},{8,0},{16,24},{24,16},{1,9},{9,1},{17,25},{25,17},{2,10},{10... | collective-permute-start | bytes 1720328 | tf_op jit(solution)/shard_map/ppermute | solution.py:308
  46.1 18.5 %collective-permute-start.11 = (bf16[160,2048]{1,0:T(8,128)(2,1)S(1)}, bf16[160,2048]{1,0:T(8,128)(2,1)S(1)}, u32[]{:S(2)}, u32[]{:S(2)}) collective-permute-start(bf16[160,2048]{1,0:T(8,128)(2,1)S(1)} %get-tuple-element.122), channel_id=1, source_target_pairs={{0,4},{1,5},{4,6},{5,7},{6,2},{7,3},{2,0},{3,1},{8,12},{9,13},{12,... | collective-permute-start | bytes 1966088 | tf_op jit(solution)/shard_map/ppermute | solution.py:336
  52.4 14.2 %collective-permute-start.13 = (bf16[160,2048]{1,0:T(8,128)(2,1)S(1)}, bf16[160,2048]{1,0:T(8,128)(2,1)S(1)}, u32[]{:S(2)}, u32[]{:S(2)}) collective-permute-start(bf16[160,2048]{1,0:T(8,128)(2,1)S(1)} %get-tuple-element.127.refs_0_), channel_id=1, source_target_pairs={{0,1},{1,0},{2,3},{3,2},{4,5},{5,4},{6,7},{7,6},{8,9},{9,8},{10,11... | collective-permute-start | bytes 1966088 | tf_op jit(solution)/shard_map/ppermute | solution.py:308
  60.0 2.0 %collective-permute-start.14 = (bf16[2,2,1,40,1792]{4,3,2,1,0:T(8,128)(2,1)S(1)}, bf16[2,2,1,40,1792]{4,3,2,1,0:T(8,128)(2,1)S(1)}, u32[]{:S(2)}, u32[]{:S(2)}) collective-permute-start(bf16[2,2,1,40,1792]{4,3,2,1,0:T(8,128)(2,1)S(1)} %get-tuple-element.129), channel_id=1, source_target_pairs={{0,8},{8,0},{16,24},{24,16},{1,9},{9,1},{17,25},{25,17},{2,10},{10... | collective-permute-start | bytes 1720328 | tf_op jit(solution)/shard_map/ppermute | solution.py:308
  60.1 2.8 %collective-permute-start.15 = (bf16[2,2,40,1792]{3,2,1,0:T(8,128)(2,1)S(1)}, bf16[2,2,40,1792]{3,2,1,0:T(8,128)(2,1)S(1)}, u32[]{:S(2)}, u32[]{:S(2)}) collective-permute-start(bf16[2,2,40,1792]{3,2,1,0:T(8,128)(2,1)S(1)} %get-tuple-element.131), channel_id=1, source_target_pairs={{0,8},{8,0},{16,24},{24,16},{1,9},{9,1},{17,25},{25,17},{2,10},{10... | collective-permute-start | bytes 1720328 | tf_op jit(solution)/shard_map/ppermute | solution.py:308
  63.0 15.1 %collective-permute-start.17 = (bf16[2,2,40,1792]{3,2,1,0:T(8,128)(2,1)S(1)}, bf16[2,2,40,1792]{3,2,1,0:T(8,128)(2,1)S(1)}, u32[]{:S(2)}, u32[]{:S(2)}) collective-permute-start(bf16[2,2,40,1792]{3,2,1,0:T(8,128)(2,1)S(1)} %get-tuple-element.134), channel_id=1, source_target_pairs={{0,16},{8,24},{16,0},{24,8},{1,17},{9,25},{17,1},{25,9},{2,18},{10... | collective-permute-start | bytes 1720328 | tf_op jit(solution)/shard_map/ppermute | solution.py:308
  66.6 17.5 %collective-permute-start.16 = (bf16[160,2048]{1,0:T(8,128)(2,1)S(1)}, bf16[160,2048]{1,0:T(8,128)(2,1)S(1)}, u32[]{:S(2)}, u32[]{:S(2)}) collective-permute-start(bf16[160,2048]{1,0:T(8,128)(2,1)S(1)} %collective-permute-done.11.refs_5_.refs_0_), channel_id=1, source_target_pairs={{0,1},{1,0},{2,3},{3,2},{4,5},{5,4},{6,7},{7,6},{8,9},{9,8},{10,11... | collective-permute-start | bytes 1966088 | tf_op jit(solution)/shard_map/ppermute | solution.py:308
  74.7 3.8 %collective-permute-start.19 = (bf16[2,2,1,40,1792]{4,3,2,1,0:T(8,128)(2,1)S(1)}, bf16[2,2,1,40,1792]{4,3,2,1,0:T(8,128)(2,1)S(1)}, u32[]{:S(2)}, u32[]{:S(2)}) collective-permute-start(bf16[2,2,1,40,1792]{4,3,2,1,0:T(8,128)(2,1)S(1)} %get-tuple-element.140), channel_id=1, source_target_pairs={{0,8},{8,0},{16,24},{24,16},{1,9},{9,1},{17,25},{25,17},{2,10},{10... | collective-permute-start | bytes 1720328 | tf_op jit(solution)/shard_map/ppermute | solution.py:308
  74.8 3.7 %collective-permute-start.20 = (bf16[2,2,40,1792]{3,2,1,0:T(8,128)(2,1)S(1)}, bf16[2,2,40,1792]{3,2,1,0:T(8,128)(2,1)S(1)}, u32[]{:S(2)}, u32[]{:S(2)}) collective-permute-start(bf16[2,2,40,1792]{3,2,1,0:T(8,128)(2,1)S(1)} %get-tuple-element.142), channel_id=1, source_target_pairs={{0,8},{8,0},{16,24},{24,16},{1,9},{9,1},{17,25},{25,17},{2,10},{10... | collective-permute-start | bytes 1720328 | tf_op jit(solution)/shard_map/ppermute | solution.py:308
  78.4 1.8 %collective-permute-start.18 = (bf16[2,40,1792]{2,1,0:T(8,128)(2,1)S(1)}, bf16[2,40,1792]{2,1,0:T(8,128)(2,1)S(1)}, u32[]{:S(2)}, u32[]{:S(2)}) collective-permute-start(bf16[2,40,1792]{2,1,0:T(8,128)(2,1)S(1)} %get-tuple-element.136.own_ref), channel_id=1, source_target_pairs={{0,8},{8,0},{16,24},{24,16},{1,9},{9,1},{17,25},{25,17},{2,10},{10... | collective-permute-start | bytes 860168 | tf_op jit(solution)/shard_map/ppermute | solution.py:308
  78.6 15.4 %collective-permute-start.23 = (bf16[2,2,40,1792]{3,2,1,0:T(8,128)(2,1)S(1)}, bf16[2,2,40,1792]{3,2,1,0:T(8,128)(2,1)S(1)}, u32[]{:S(2)}, u32[]{:S(2)}) collective-permute-start(bf16[2,2,40,1792]{3,2,1,0:T(8,128)(2,1)S(1)} %get-tuple-element.148), channel_id=1, source_target_pairs={{0,16},{8,24},{16,0},{24,8},{1,17},{9,25},{17,1},{25,9},{2,18},{10... | collective-permute-start | bytes 1720328 | tf_op jit(solution)/shard_map/ppermute | solution.py:308
  84.1 16.9 %collective-permute-start.28 = (bf16[2,40,4096]{2,1,0:T(8,128)(2,1)S(1)}, bf16[2,40,4096]{2,1,0:T(8,128)(2,1)S(1)}, u32[]{:S(2)}, u32[]{:S(2)}) collective-permute-start(bf16[2,40,4096]{2,1,0:T(8,128)(2,1)S(1)} %get-tuple-element.160), channel_id=1, source_target_pairs={{0,1},{1,0},{2,3},{3,2},{4,5},{5,4},{6,7},{7,6},{8,9},{9,8},{10,11... | collective-permute-start | bytes 1966088 | tf_op jit(solution)/shard_map/ppermute | solution.py:308
  90.7 3.7 %collective-permute-start.21 = (bf16[1,2,1,40,1792]{4,3,2,1,0:T(8,128)(2,1)S(1)}, bf16[1,2,1,40,1792]{4,3,2,1,0:T(8,128)(2,1)S(1)}, u32[]{:S(2)}, u32[]{:S(2)}) collective-permute-start(bf16[1,2,1,40,1792]{4,3,2,1,0:T(8,128)(2,1)S(1)} %get-tuple-element.146), channel_id=1, source_target_pairs={{0,8},{8,0},{16,24},{24,16},{1,9},{9,1},{17,25},{25,17},{2,10},{10... | collective-permute-start | bytes 860168 | tf_op jit(solution)/shard_map/ppermute | solution.py:308
  90.8 3.6 %collective-permute-start.22 = (bf16[1,2,1,40,1792]{4,3,2,1,0:T(8,128)(2,1)S(1)}, bf16[1,2,1,40,1792]{4,3,2,1,0:T(8,128)(2,1)S(1)}, u32[]{:S(2)}, u32[]{:S(2)}) collective-permute-start(bf16[1,2,1,40,1792]{4,3,2,1,0:T(8,128)(2,1)S(1)} %get-tuple-element.147), channel_id=1, source_target_pairs={{0,8},{8,0},{16,24},{24,16},{1,9},{9,1},{17,25},{25,17},{2,10},{10... | collective-permute-start | bytes 860168 | tf_op jit(solution)/shard_map/ppermute | solution.py:308
  94.3 2.3 %collective-permute-start.27 = (bf16[2,40,1792]{2,1,0:T(8,128)(2,1)S(1)}, bf16[2,40,1792]{2,1,0:T(8,128)(2,1)S(1)}, u32[]{:S(2)}, u32[]{:S(2)}) collective-permute-start(bf16[2,40,1792]{2,1,0:T(8,128)(2,1)S(1)} %get-tuple-element.156.own_ref), channel_id=1, source_target_pairs={{0,8},{8,0},{16,24},{24,16},{1,9},{9,1},{17,25},{25,17},{2,10},{10... | collective-permute-start | bytes 860168 | tf_op jit(solution)/shard_map/ppermute | solution.py:308
  94.6 16.1 %collective-permute-start.26 = (bf16[2,2,40,1792]{3,2,1,0:T(8,128)(2,1)S(1)}, bf16[2,2,40,1792]{3,2,1,0:T(8,128)(2,1)S(1)}, u32[]{:S(2)}, u32[]{:S(2)}) collective-permute-start(bf16[2,2,40,1792]{3,2,1,0:T(8,128)(2,1)S(1)} %get-tuple-element.155), channel_id=1, source_target_pairs={{0,8},{8,0},{16,24},{24,16},{1,9},{9,1},{17,25},{25,17},{2,10},{10... | collective-permute-start | bytes 1720328 | tf_op jit(solution)/shard_map/ppermute | solution.py:308
  95.1 15.5 %collective-permute-start.24 = (bf16[2,2,40,1792]{3,2,1,0:T(8,128)(2,1)S(1)}, bf16[2,2,40,1792]{3,2,1,0:T(8,128)(2,1)S(1)}, u32[]{:S(2)}, u32[]{:S(2)}) collective-permute-start(bf16[2,2,40,1792]{3,2,1,0:T(8,128)(2,1)S(1)} %get-tuple-element.151), channel_id=1, source_target_pairs={{0,16},{8,24},{16,0},{24,8},{1,17},{9,25},{17,1},{25,9},{2,18},{10... | collective-permute-start | bytes 1720328 | tf_op jit(solution)/shard_map/ppermute | solution.py:308
  101.0 9.0 %collective-permute-start.29 = (bf16[1,40,4096]{2,1,0:T(8,128)(2,1)S(1)}, bf16[1,40,4096]{2,1,0:T(8,128)(2,1)S(1)}, u32[]{:S(2)}, u32[]{:S(2)}) collective-permute-start(bf16[1,40,4096]{2,1,0:T(8,128)(2,1)S(1)} %get-tuple-element.161), channel_id=1, source_target_pairs={{0,1},{1,0},{2,3},{3,2},{4,5},{5,4},{6,7},{7,6},{8,9},{9,8},{10,11... | collective-permute-start | bytes 983048 | tf_op jit(solution)/shard_map/ppermute | solution.py:308
  101.6 17.7 %collective-permute-start.32 = (bf16[2,40,4096]{2,1,0:T(8,128)(2,1)S(1)}, bf16[2,40,4096]{2,1,0:T(8,128)(2,1)S(1)}, u32[]{:S(2)}, u32[]{:S(2)}) collective-permute-start(bf16[2,40,4096]{2,1,0:T(8,128)(2,1)S(1)} %get-tuple-element.175), channel_id=1, source_target_pairs={{0,2},{1,3},{2,0},{3,1},{4,6},{5,7},{6,4},{7,5},{8,10},{9,11},{10,... | collective-permute-start | bytes 1966088 | tf_op jit(solution)/shard_map/ppermute | solution.py:336
  110.1 9.3 %collective-permute-start.31 = (bf16[1,40,4096]{2,1,0:T(8,128)(2,1)S(1)}, bf16[1,40,4096]{2,1,0:T(8,128)(2,1)S(1)}, u32[]{:S(2)}, u32[]{:S(2)}) collective-permute-start(bf16[1,40,4096]{2,1,0:T(8,128)(2,1)S(1)} %get-tuple-element.173), channel_id=1, source_target_pairs={{0,1},{1,0},{2,3},{3,2},{4,5},{5,4},{6,7},{7,6},{8,9},{9,8},{10,11... | collective-permute-start | bytes 983048 | tf_op jit(solution)/shard_map/ppermute | solution.py:308
  111.0 1.6 %collective-permute-start.30 = (bf16[2,40,1792]{2,1,0:T(8,128)(2,1)S(1)}, bf16[2,40,1792]{2,1,0:T(8,128)(2,1)S(1)}, u32[]{:S(2)}, u32[]{:S(2)}) collective-permute-start(bf16[2,40,1792]{2,1,0:T(8,128)(2,1)S(1)} %get-tuple-element.166.own_ref), channel_id=1, source_target_pairs={{0,8},{8,0},{16,24},{24,16},{1,9},{9,1},{17,25},{25,17},{2,10},{10... | collective-permute-start | bytes 860168 | tf_op jit(solution)/shard_map/ppermute | solution.py:308
  111.1 19.7 %collective-permute-start.25 = (bf16[2,2,40,1792]{3,2,1,0:T(8,128)(2,1)S(1)}, bf16[2,2,40,1792]{3,2,1,0:T(8,128)(2,1)S(1)}, u32[]{:S(2)}, u32[]{:S(2)}) collective-permute-start(bf16[2,2,40,1792]{3,2,1,0:T(8,128)(2,1)S(1)} %get-tuple-element.152), channel_id=1, source_target_pairs={{0,16},{8,24},{16,0},{24,8},{1,17},{9,25},{17,1},{25,9},{2,18},{10... | collective-permute-start | bytes 1720328 | tf_op jit(solution)/shard_map/ppermute | solution.py:308
  112.3 14.1 %collective-permute-start.34 = (bf16[1,40,4096]{2,1,0:T(8,128)(2,1)S(1)}, bf16[1,40,4096]{2,1,0:T(8,128)(2,1)S(1)}, u32[]{:S(2)}, u32[]{:S(2)}) collective-permute-start(bf16[1,40,4096]{2,1,0:T(8,128)(2,1)S(1)} %get-tuple-element.172), channel_id=1, source_target_pairs={{0,2},{1,3},{2,0},{3,1},{4,6},{5,7},{6,4},{7,5},{8,10},{9,11},{10,... | collective-permute-start | bytes 983048 | tf_op jit(solution)/shard_map/ppermute | solution.py:336
  119.5 7.9 %collective-permute-start.33 = (bf16[1,40,4096]{2,1,0:T(8,128)(2,1)S(1)}, bf16[1,40,4096]{2,1,0:T(8,128)(2,1)S(1)}, u32[]{:S(2)}, u32[]{:S(2)}) collective-permute-start(bf16[1,40,4096]{2,1,0:T(8,128)(2,1)S(1)} %get-tuple-element.177), channel_id=1, source_target_pairs={{0,1},{1,0},{2,3},{3,2},{4,5},{5,4},{6,7},{7,6},{8,9},{9,8},{10,11... | collective-permute-start | bytes 983048 | tf_op jit(solution)/shard_map/ppermute | solution.py:308
  121.1 13.9 %collective-permute-start.36 = (bf16[1,40,4096]{2,1,0:T(8,128)(2,1)S(1)}, bf16[1,40,4096]{2,1,0:T(8,128)(2,1)S(1)}, u32[]{:S(2)}, u32[]{:S(2)}) collective-permute-start(bf16[1,40,4096]{2,1,0:T(8,128)(2,1)S(1)} %get-tuple-element.176), channel_id=1, source_target_pairs={{0,2},{1,3},{2,0},{3,1},{4,6},{5,7},{6,4},{7,5},{8,10},{9,11},{10,... | collective-permute-start | bytes 983048 | tf_op jit(solution)/shard_map/ppermute | solution.py:336
  127.5 11.4 %collective-permute-start.37 = (bf16[1,40,4096]{2,1,0:T(8,128)(2,1)S(1)}, bf16[1,40,4096]{2,1,0:T(8,128)(2,1)S(1)}, u32[]{:S(2)}, u32[]{:S(2)}) collective-permute-start(bf16[1,40,4096]{2,1,0:T(8,128)(2,1)S(1)} %get-tuple-element.186), channel_id=1, source_target_pairs={{0,1},{1,0},{2,3},{3,2},{4,5},{5,4},{6,7},{7,6},{8,9},{9,8},{10,11... | collective-permute-start | bytes 983048 | tf_op jit(solution)/shard_map/ppermute | solution.py:308
  129.0 23.8 %collective-permute-start.40 = (bf16[1,40,4096]{2,1,0:T(8,128)(2,1)S(1)}, bf16[1,40,4096]{2,1,0:T(8,128)(2,1)S(1)}, u32[]{:S(2)}, u32[]{:S(2)}) collective-permute-start(bf16[1,40,4096]{2,1,0:T(8,128)(2,1)S(1)} %get-tuple-element.185), channel_id=1, source_target_pairs={{0,4},{1,5},{4,0},{5,1},{2,6},{3,7},{6,2},{7,3},{8,12},{9,13},{12,... | collective-permute-start | bytes 983048 | tf_op jit(solution)/shard_map/ppermute | solution.py:336
  131.0 4.0 %collective-permute-start.35 = (bf16[2,40,1792]{2,1,0:T(8,128)(2,1)S(1)}, bf16[2,40,1792]{2,1,0:T(8,128)(2,1)S(1)}, u32[]{:S(2)}, u32[]{:S(2)}) collective-permute-start(bf16[2,40,1792]{2,1,0:T(8,128)(2,1)S(1)} %get-tuple-element.180.own_ref), channel_id=1, source_target_pairs={{0,8},{8,0},{16,24},{24,16},{1,9},{9,1},{17,25},{25,17},{2,10},{10... | collective-permute-start | bytes 860168 | tf_op jit(solution)/shard_map/ppermute | solution.py:308
  139.0 18.2 %collective-permute-start.39 = (bf16[1,40,4096]{2,1,0:T(8,128)(2,1)S(1)}, bf16[1,40,4096]{2,1,0:T(8,128)(2,1)S(1)}, u32[]{:S(2)}, u32[]{:S(2)}) collective-permute-start(bf16[1,40,4096]{2,1,0:T(8,128)(2,1)S(1)} %get-tuple-element.190), channel_id=1, source_target_pairs={{0,4},{1,5},{4,0},{5,1},{2,6},{3,7},{6,2},{7,3},{8,12},{9,13},{12,... | collective-permute-start | bytes 983048 | tf_op jit(solution)/shard_map/ppermute | solution.py:336
  139.4 15.1 %collective-permute-start.38 = (bf16[2,40,4096]{2,1,0:T(8,128)(2,1)S(1)}, bf16[2,40,4096]{2,1,0:T(8,128)(2,1)S(1)}, u32[]{:S(2)}, u32[]{:S(2)}) collective-permute-start(bf16[2,40,4096]{2,1,0:T(8,128)(2,1)S(1)} %get-tuple-element.187), channel_id=1, source_target_pairs={{0,1},{1,0},{2,3},{3,2},{4,5},{5,4},{6,7},{7,6},{8,9},{9,8},{10,11... | collective-permute-start | bytes 1966088 | tf_op jit(solution)/shard_map/ppermute | solution.py:308
  154.6 2.6 %collective-permute-start.41 = (bf16[40,4096]{1,0:T(8,128)(2,1)S(1)}, bf16[40,4096]{1,0:T(8,128)(2,1)S(1)}, u32[]{:S(2)}, u32[]{:S(2)}) collective-permute-start(bf16[40,4096]{1,0:T(8,128)(2,1)S(1)} %fusion.4), channel_id=1, source_target_pairs={{0,8},{8,0},{16,24},{24,16},{1,9},{9,1},{17,25},{25,17},{2,10},{10... | collective-permute-start | bytes 983048 | tf_op jit(solution)/shard_map/ppermute | solution.py:308

commit v13 on v12

--- a/solution.py
+++ b/solution.py
@@ -387,8 +387,8 @@
         _, _, (summed,), last[0] = sums([], [], [parts], last + list(after), hint)
         return summed
 
+    across_stacks = [by_plane(first, ACROSS), by_plane(second, ACROSS)]
     next_stacks = [by_plane(first, NEXT), by_plane(second, NEXT)]
-    across_stacks = [by_plane(first, ACROSS), by_plane(second, ACROSS)]
     forward(0, mine, [next_stacks[0], across_stacks[0]])
     up_kept, last[0] = masked(
         up_weight, up_mask, tile_of(features, 256), place, 1, lambda core: 0,
@@ -398,16 +398,19 @@
     inner_three, last[0] = join(across_stacks, last)
     outer_three = by_plane(mine, AROUND, last)
     down_kept = []
-    for share, hint in ((0, 8), (1, 0)):
+
+    def keep_down(share, hint=0.0):
         part, last[0] = masked(
-            down_weight, down_mask, 2 * BLOCK, place, 2 * CORES, lambda core, share=share: 2 * core + share,
-            last, hint
+            down_weight, down_mask, 2 * BLOCK, place, 2 * CORES, lambda core: 2 * core + share, last, hint
         )
         down_kept.append(part)
+
+    keep_down(0, 8)
     forward(1, one_away, [*parts[0][1:], *last])
     multiply_in(0, hint=0)
     exchange(0)
     exchange_near(0)
+    keep_down(1)
     three_away, passed, last[0] = pick(place, inner_three, outer_three, mine, last)
     two_away = by_plane(passed, CYCLE)
     to_chips(0, [near[0]])
@@ -449,8 +452,9 @@
     two_out[1] = by_plane(two, SECOND)
     send_rows(2, [two], CORES, 0)
     to_hidden(0)
-    multiply_out(0, after=[three_out[0]])
-    two = to_rows(*rows_in[2, 0], three_out[0])
+    multiply_out(0)
+    two = to_rows(rows_in[2, 0][0], three_out[0], hint=0.5)
+    two = to_rows(two, *rows_in[2, 0][1:])
     two_out[0] = by_plane(two, SECOND)
     send_rows(0, rows_in[2, 0][1:])
 

time: 159 us -> 160 us (level)
  starting transfers between devices: 39.1 us -> 42.7 us
  waiting for transfers between devices: 55.9 us -> 53.2 us
    ppermute x11, starting transfers between devices: 13.2 us -> 20.4 us  [by_plane(): return lax.ppermute(behind(values, after), 'cols', pairs)]
    ppermute x31, waiting for transfers between devices: 26.1 us -> 21.2 us  [swap(): lax.ppermute(values, axis, [(place, place ^ step) for place in range(size)])]
    ppermute x31, starting transfers between devices: 25.8 us -> 22.3 us  [swap(): lax.ppermute(values, axis, [(place, place ^ step) for place in range(size)])]
    ppermute x11, waiting for transfers between devices: 29.8 us -> 32 us  [by_plane(): return lax.ppermute(behind(values, after), 'cols', pairs)]
  transfers between devices with their start and end apart: 42 -> 42, of which waited for: 19 -> 20; matrix products, arithmetic and copies ran while one was open for 0% -> 0% of each run, Pallas kernels for 37% -> 37%
where the time goes in v13:
time: 160 us; the launch traced here: 159 us
  Pallas kernels  59 us (37%)
  waiting for transfers between devices  53.2 us (33%)
  starting transfers between devices  42.7 us (27%)
  other arithmetic  3.97 us (2%)
    ppermute x11, waiting for transfers between devices, by_plane(): return lax.ppermute(behind(values, after), 'cols', pairs)  32 us
    pallas_call x4, Pallas kernels, gate_up(): pl.pallas_call(functools.partial(gate_up_kernel, len(parts), len(after)),...  24.3 us
    ppermute x31, starting transfers between devices, swap(): lax.ppermute(values, axis, [(place, place ^ step) for place in range(size)])  22.3 us
    ppermute x31, waiting for transfers between devices, swap(): lax.ppermute(values, axis, [(place, place ^ step) for place in range(size)])  21.2 us
    ppermute x11, starting transfers between devices, by_plane(): return lax.ppermute(behind(values, after), 'cols', pairs)  20.4 us
    pallas_call x4, Pallas kernels, down(): pl.pallas_call(functools.partial(down_kernel, pieces, len(down_kept), len...  15.5 us
    pallas_call x4, Pallas kernels, masked(): pl.pallas_call(functools.partial(mask_kernel, share, rows, len(after)), i...  15.4 us
  transfers between devices with their start and end apart: 42, of which 20 were waited for; matrix products, arithmetic and copies ran while one was open for 0% of the time, Pallas kernels for 37%

profile of v13, /device:TPU:0, one launch (start us, length us, event | category | flops | bytes accessed | tf_op | source)
XLA Modules:
  0.0 159.3 jit_solution(14101503928979745102)
XLA Ops:
  0.0 1.3 fusion
  1.4 1.3 fusion.2
  3.3 2.6 %collective-permute-start.2 = (bf16[40,2048]{1,0:T(8,128)(2,1)S(1)}, bf16[40,2048]{1,0:T(8,128)(2,1)S(1)}, u32[]{:S(2)}, u32[]{:S(2)}) collective-permute-start(bf16[40,2048]{1,0:T(8,128)(2,1)S(1)} %get-tuple-element.199), channel_id=1, source_target_pairs={{0,24},{8,16},{16,8},{24,0},{1,25},{9,17},{17,9},{25,1},{2,26},{10... | collective-permute-start | bytes 491528 | tf_op jit(solution)/shard_map/ppermute | solution.py:308
  6.6 4.9 %collective-permute-start.3 = (bf16[2,1,40,2048]{3,2,1,0:T(8,128)(2,1)S(1)}, bf16[2,1,40,2048]{3,2,1,0:T(8,128)(2,1)S(1)}, u32[]{:S(2)}, u32[]{:S(2)}) collective-permute-start(bf16[2,1,40,2048]{3,2,1,0:T(8,128)(2,1)S(1)} %get-tuple-element.101.refs_0_), channel_id=1, source_target_pairs={{0,2},{1,3},{2,0},{3,1},{4,6},{5,7},{6,4},{7,5},{8,10},{9,11},{10,... | collective-permute-start | bytes 983048 | tf_op jit(solution)/shard_map/ppermute | solution.py:336
  11.7 3.8 %masked.4 = (bf16[2048,1792]{1,0:T(8,128)(2,1)S(1)}, f32[8,128]{1,0:T(8,128)S(1)}) custom-call(s32[2]{0:T(128)S(1)} %pad_add_fusion.core_ref.place_ref, bf16[2048,1792]{1,0:T(8,128)(2,1)} %weight_ref.4, s32[32,28]{1,0:T(8,128)S(1)} %copy-done, f32[8,128]{1,0:T(8,128)S(1)} %get-tuple-element.102.refs_0_), custom_call_target="tpu_custom_call" | custom-call | tf_op jit(solution)/shard_map/masked/pallas_call | solution.py:81
  16.8 3.4 %collective-permute-done.3.refs_1_.refs_0_ = bf16[2,1,40,2048]{3,2,1,0:T(8,128)(2,1)S(1)} collective-permute-done((bf16[2,1,40,2048]{3,2,1,0:T(8,128)(2,1)S(1)}, bf16[2,1,40,2048]{3,2,1,0:T(8,128)(2,1)S(1)}, u32[]{:S(2)}, u32[]{:S(2)}) %collective-permute-start.3) | collective-permute-done | bytes 327712 | tf_op jit(solution)/shard_map/ppermute | solution.py:336
  20.2 1.5 collective-permute-start.5
  21.7 3.8 %masked.5 = (bf16[2048,1792]{1,0:T(8,128)(2,1)S(1)}, f32[8,128]{1,0:T(8,128)S(1)}) custom-call(s32[2]{0:T(128)S(1)} %pad_add_fusion.core_ref.place_ref, bf16[2048,1792]{1,0:T(8,128)(2,1)} %weight_ref.5, s32[32,28]{1,0:T(8,128)S(1)} %copy-done.1, f32[8,128]{1,0:T(8,128)S(1)} %get-tuple-element.109.refs_0_, ...), custom_call_target="tpu_custom_call" | custom-call | flops 172500000 | tf_op jit(solution)/shard_map/masked/pallas_call | solution.py:81
  26.1 3.3 %collective-permute-start.10 = (bf16[160,2048]{1,0:T(8,128)(2,1)S(1)}, bf16[160,2048]{1,0:T(8,128)(2,1)S(1)}, u32[]{:S(2)}, u32[]{:S(2)}) collective-permute-start(bf16[160,2048]{1,0:T(8,128)(2,1)S(1)} %get-tuple-element.107.refs_0_.mine_ref), channel_id=1, source_target_pairs={{0,6},{1,7},{6,0},{7,1},{8,14},{9,15},{14,8},{15,9},{16,22},{17,23... | collective-permute-start | bytes 1966088 | tf_op jit(solution)/shard_map/ppermute | solution.py:336
  29.4 3.9 %masked.6 = (bf16[1792,2048]{1,0:T(8,128)(2,1)S(1)}, f32[8,128]{1,0:T(8,128)S(1)}) custom-call(s32[2]{0:T(128)S(1)} %pad_add_fusion.core_ref.place_ref, bf16[1792,8192]{1,0:T(8,128)(2,1)} %weight_ref.7, s32[28,128]{1,0:T(8,128)S(1)} %copy-done.2, f32[8,128]{1,0:T(8,128)S(1)} %get-tuple-element.113.refs_0_), custom_call_target="tpu_custom_call" | custom-call | flops 9200000000 | tf_op jit(solution)/shard_map/masked/pallas_call | solution.py:81
  33.3 1.2 collective-permute-done.5.refs_1_
  34.5 1.5 collective-permute-start.12
  36.0 6.1 %gate_up.4 = (bf16[2,2,2,40,1792]{4,3,2,1,0:T(8,128)(2,1)S(1)}, bf16[2,2,40,1792]{3,2,1,0:T(8,128)(2,1)S(1)}, bf16[2,2,1,40,1792]{4,3,2,1,0:T(8,128)(2,1)S(1)}, f32[8,128]{1,0:T(8,128)S(1)}) custom-call(bf16[160,2048]{1,0:T(8,128)(2,1)S(1)} %get-tuple-element.107.refs_0_.mine_ref, bf16[160,2048]{1,0:T(8,128)(2,1)S(1)} %collective-permute-done.5.refs_1_, ...), custom_call_target="tpu_custom_call" | custom-call | tf_op jit(solution)/shard_map/gate_up/pallas_call | solution.py:190
  42.7 3.9 %masked.7 = (bf16[1792,2048]{1,0:T(8,128)(2,1)S(1)}, f32[8,128]{1,0:T(8,128)S(1)}) custom-call(s32[2]{0:T(128)S(1)} %pad_add_fusion.core_ref.place_ref, bf16[1792,8192]{1,0:T(8,128)(2,1)} %weight_ref.7, s32[28,128]{1,0:T(8,128)S(1)} %copy-done.2, f32[8,128]{1,0:T(8,128)S(1)} %get-tuple-element.120.refs_0_), custom_call_target="tpu_custom_call" | custom-call | tf_op jit(solution)/shard_map/masked/pallas_call | solution.py:81
  47.3 2.6 %collective-permute-start.11 = (bf16[160,2048]{1,0:T(8,128)(2,1)S(1)}, bf16[160,2048]{1,0:T(8,128)(2,1)S(1)}, u32[]{:S(2)}, u32[]{:S(2)}) collective-permute-start(bf16[160,2048]{1,0:T(8,128)(2,1)S(1)} %get-tuple-element.124), channel_id=1, source_target_pairs={{0,4},{1,5},{4,6},{5,7},{6,2},{7,3},{2,0},{3,1},{8,12},{9,13},{12,... | collective-permute-start | bytes 1966088 | tf_op jit(solution)/shard_map/ppermute | solution.py:336
  50.6 6.1 %gate_up.5 = (bf16[2,2,2,40,1792]{4,3,2,1,0:T(8,128)(2,1)S(1)}, bf16[2,2,40,1792]{3,2,1,0:T(8,128)(2,1)S(1)}, bf16[2,2,1,40,1792]{4,3,2,1,0:T(8,128)(2,1)S(1)}, f32[8,128]{1,0:T(8,128)S(1)}) custom-call(bf16[160,2048]{1,0:T(8,128)(2,1)S(1)} %get-tuple-element.127.refs_0_, bf16[160,2048]{1,0:T(8,128)(2,1)S(1)} %collective-permute-done.12.refs_1_, ...), custom_call_target="tpu_custom_call" | custom-call | flops 4697620480 | tf_op jit(solution)/shard_map/gate_up/pallas_call | solution.py:190
  57.2 1.5 collective-permute-done.14.refs_1_
  58.7 0.8 collective-permute-done.15.refs_3_.refs_1_
  59.7 1.6 collective-permute-start.17
  61.2 3.8 %collective-permute-done.11.refs_5_.refs_0_ = bf16[160,2048]{1,0:T(8,128)(2,1)S(1)} collective-permute-done((bf16[160,2048]{1,0:T(8,128)(2,1)S(1)}, bf16[160,2048]{1,0:T(8,128)(2,1)S(1)}, u32[]{:S(2)}, u32[]{:S(2)}) %collective-permute-start.11) | collective-permute-done | bytes 655392 | tf_op jit(solution)/shard_map/ppermute | solution.py:336
  65.1 1.4 collective-permute-done.13.refs_1_
  67.0 6.1 %gate_up.6 = (bf16[2,2,2,40,1792]{4,3,2,1,0:T(8,128)(2,1)S(1)}, bf16[2,2,40,1792]{3,2,1,0:T(8,128)(2,1)S(1)}, bf16[2,2,1,40,1792]{4,3,2,1,0:T(8,128)(2,1)S(1)}, f32[8,128]{1,0:T(8,128)S(1)}) custom-call(bf16[160,2048]{1,0:T(8,128)(2,1)S(1)} %get-tuple-element.129.refs_0_, bf16[160,2048]{1,0:T(8,128)(2,1)S(1)} %collective-permute-done.13.refs_1_, ...), custom_call_target="tpu_custom_call" | custom-call | flops 4697620480 | tf_op jit(solution)/shard_map/gate_up/pallas_call | solution.py:190
  73.7 1.1 collective-permute-done.17.refs_2_
  76.1 1.6 collective-permute-start.23
  77.7 3.9 %down.4 = (bf16[2,40,4096]{2,1,0:T(8,128)(2,1)S(1)}, bf16[2,40,4096]{2,1,0:T(8,128)(2,1)S(1)}, f32[8,128]{1,0:T(8,128)S(1)}) custom-call(bf16[2,40,1792]{2,1,0:T(8,128)(2,1)S(1)} %get-tuple-element.138.own_ref, bf16[2,40,1792]{2,1,0:T(8,128)(2,1)S(1)} %collective-permute-done.18.other_ref, bf16[1792,2048]{1,0:T(8,128)(2,1)S(1)} %get-tuple-element.139.refs_0_, ...), custom_call_target="tpu_custom_call" | custom-call | flops 2348810 | tf_op jit(solution)/shard_map/down/pallas_call | solution.py:232
  82.1 1.1 collective-permute-start.28
  83.2 6.1 %gate_up.7 = (bf16[2,2,2,40,1792]{4,3,2,1,0:T(8,128)(2,1)S(1)}, bf16[2,2,40,1792]{3,2,1,0:T(8,128)(2,1)S(1)}, bf16[1,2,1,40,1792]{4,3,2,1,0:T(8,128)(2,1)S(1)}, ...) custom-call(bf16[160,2048]{1,0:T(8,128)(2,1)S(1)} %collective-permute-done.11.refs_5_.refs_0_, ...), custom_call_target="tpu_custom_call" | custom-call | flops 4697620480 | tf_op jit(solution)/shard_map/gate_up/pallas_call | solution.py:190
  89.8 1.4 collective-permute-done.23.refs_2_
  92.3 1.5 collective-permute-start.24
  93.8 3.9 %down.5 = (bf16[1,40,4096]{2,1,0:T(8,128)(2,1)S(1)}, bf16[1,40,4096]{2,1,0:T(8,128)(2,1)S(1)}, bf16[1,40,4096]{2,1,0:T(8,128)(2,1)S(1)}, bf16[1,40,4096]{2,1,0:T(8,128)(2,1)S(1)}, f32[8,128]{1,0:T(8,128)S(1)}) custom-call(bf16[2,40,1792]{2,1,0:T(8,128)(2,1)S(1)} %get-tuple-element.158.own_ref, bf16[2,40,1792]{2,1,0:T(8,128)(2,1)S(1)} %collective-permute-done.27.other_ref, ...), custom_call_target="tpu_custom_call" | custom-call | flops 2348810 | tf_op jit(solution)/shard_map/down/pallas_call | solution.py:232
  98.1 1.5 collective-permute-start.29
  99.8 1.3 collective-permute-start.32
  101.1 6.0 %collective-permute-done.29.refs_1_ = bf16[1,40,4096]{2,1,0:T(8,128)(2,1)S(1)} collective-permute-done((bf16[1,40,4096]{2,1,0:T(8,128)(2,1)S(1)}, bf16[1,40,4096]{2,1,0:T(8,128)(2,1)S(1)}, u32[]{:S(2)}, u32[]{:S(2)}) %collective-permute-start.29) | collective-permute-done | bytes 327712 | tf_op jit(solution)/shard_map/ppermute | solution.py:308
  107.2 1.6 collective-permute-start.31
  109.2 1.2 collective-permute-start.25
  110.4 1.2 collective-permute-start.34
  111.7 3.9 %down.6 = (bf16[1,40,4096]{2,1,0:T(8,128)(2,1)S(1)}, bf16[1,40,4096]{2,1,0:T(8,128)(2,1)S(1)}, bf16[1,40,4096]{2,1,0:T(8,128)(2,1)S(1)}, bf16[1,40,4096]{2,1,0:T(8,128)(2,1)S(1)}, f32[8,128]{1,0:T(8,128)S(1)}) custom-call(bf16[2,40,1792]{2,1,0:T(8,128)(2,1)S(1)} %get-tuple-element.168.own_ref, bf16[2,40,1792]{2,1,0:T(8,128)(2,1)S(1)} %collective-permute-done.30.other_ref, ...), custom_call_target="tpu_custom_call" | custom-call | flops 2348810 | tf_op jit(solution)/shard_map/down/pallas_call | solution.py:232
  115.5 2.0 %collective-permute-done.32.refs_3_.refs_1_ = bf16[2,40,4096]{2,1,0:T(8,128)(2,1)S(1)} collective-permute-done((bf16[2,40,4096]{2,1,0:T(8,128)(2,1)S(1)}, bf16[2,40,4096]{2,1,0:T(8,128)(2,1)S(1)}, u32[]{:S(2)}, u32[]{:S(2)}) %collective-permute-start.32) | collective-permute-done | bytes 655392 | tf_op jit(solution)/shard_map/ppermute | solution.py:336
  118.2 1.4 collective-permute-start.38
  119.6 5.0 %collective-permute-done.34.refs_2_ = bf16[1,40,4096]{2,1,0:T(8,128)(2,1)S(1)} collective-permute-done((bf16[1,40,4096]{2,1,0:T(8,128)(2,1)S(1)}, bf16[1,40,4096]{2,1,0:T(8,128)(2,1)S(1)}, u32[]{:S(2)}, u32[]{:S(2)}) %collective-permute-start.34) | collective-permute-done | bytes 327712 | tf_op jit(solution)/shard_map/ppermute | solution.py:336
  126.4 1.9 %collective-permute-start.40 = (bf16[1,40,4096]{2,1,0:T(8,128)(2,1)S(1)}, bf16[1,40,4096]{2,1,0:T(8,128)(2,1)S(1)}, u32[]{:S(2)}, u32[]{:S(2)}) collective-permute-start(bf16[1,40,4096]{2,1,0:T(8,128)(2,1)S(1)} %get-tuple-element.187), channel_id=1, source_target_pairs={{0,4},{1,5},{4,0},{5,1},{2,6},{3,7},{6,2},{7,3},{8,12},{9,13},{12,... | collective-permute-start | bytes 983048 | tf_op jit(solution)/shard_map/ppermute | solution.py:336
  128.3 3.9 %down.7 = (bf16[2,40,4096]{2,1,0:T(8,128)(2,1)S(1)}, bf16[2,40,4096]{2,1,0:T(8,128)(2,1)S(1)}, f32[8,128]{1,0:T(8,128)S(1)}) custom-call(bf16[2,40,1792]{2,1,0:T(8,128)(2,1)S(1)} %get-tuple-element.182.own_ref, bf16[2,40,1792]{2,1,0:T(8,128)(2,1)S(1)} %collective-permute-done.35.other_ref, bf16[1792,2048]{1,0:T(8,128)(2,1)S(1)} %get-tuple-element.139.refs_0_, ...), custom_call_target="tpu_custom_call" | custom-call | flops 2348810 | tf_op jit(solution)/shard_map/down/pallas_call | solution.py:232
  132.3 3.6 %collective-permute-done.36.refs_1_ = bf16[1,40,4096]{2,1,0:T(8,128)(2,1)S(1)} collective-permute-done((bf16[1,40,4096]{2,1,0:T(8,128)(2,1)S(1)}, bf16[1,40,4096]{2,1,0:T(8,128)(2,1)S(1)}, u32[]{:S(2)}, u32[]{:S(2)}) %collective-permute-start.36) | collective-permute-done | bytes 327712 | tf_op jit(solution)/shard_map/ppermute | solution.py:308
  136.0 2.0 %collective-permute-start.39 = (bf16[1,40,4096]{2,1,0:T(8,128)(2,1)S(1)}, bf16[1,40,4096]{2,1,0:T(8,128)(2,1)S(1)}, u32[]{:S(2)}, u32[]{:S(2)}) collective-permute-start(bf16[1,40,4096]{2,1,0:T(8,128)(2,1)S(1)} %get-tuple-element.194), channel_id=1, source_target_pairs={{0,4},{1,5},{4,0},{5,1},{2,6},{3,7},{6,2},{7,3},{8,12},{9,13},{12,... | collective-permute-start | bytes 983048 | tf_op jit(solution)/shard_map/ppermute | solution.py:336
  138.5 13.2 %collective-permute-done.40.refs_0_ = bf16[1,40,4096]{2,1,0:T(8,128)(2,1)S(1)} collective-permute-done((bf16[1,40,4096]{2,1,0:T(8,128)(2,1)S(1)}, bf16[1,40,4096]{2,1,0:T(8,128)(2,1)S(1)}, u32[]{:S(2)}, u32[]{:S(2)}) %collective-permute-start.40) | collective-permute-done | bytes 327712 | tf_op jit(solution)/shard_map/ppermute | solution.py:336
  152.3 1.6 %collective-permute-done.37 = bf16[2,40,4096]{2,1,0:T(8,128)(2,1)S(1)} collective-permute-done((bf16[2,40,4096]{2,1,0:T(8,128)(2,1)S(1)}, bf16[2,40,4096]{2,1,0:T(8,128)(2,1)S(1)}, u32[]{:S(2)}, u32[]{:S(2)}) %collective-permute-start.37) | collective-permute-done | bytes 655392 | tf_op jit(solution)/shard_map/ppermute | solution.py:308
  154.2 4.0 %collective-permute-done.39 = bf16[1,40,4096]{2,1,0:T(8,128)(2,1)S(1)} collective-permute-done((bf16[1,40,4096]{2,1,0:T(8,128)(2,1)S(1)}, bf16[1,40,4096]{2,1,0:T(8,128)(2,1)S(1)}, u32[]{:S(2)}, u32[]{:S(2)}) %collective-permute-start.39) | collective-permute-done | bytes 327712 | tf_op jit(solution)/shard_map/ppermute | solution.py:336
  158.4 0.9 pad_maximum_fusion
  (84 shorter events, 15.7 us)
Async XLA Ops:
  1.3 10.3 %copy-start = (s32[32,28]{1,0:T(8,128)S(1)}, s32[32,28]{1,0:T(8,128)}, u32[]{:S(2)}) copy-start(s32[32,28]{1,0:T(8,128)} %mask_ref.4) | copy-start | bytes 10756
  2.7 3.2 %collective-permute-start = (bf16[40,2048]{1,0:T(8,128)(2,1)S(1)}, bf16[40,2048]{1,0:T(8,128)(2,1)S(1)}, u32[]{:S(2)}, u32[]{:S(2)}) collective-permute-start(bf16[40,2048]{1,0:T(8,128)(2,1)S(1)} %get-tuple-element.201), channel_id=1, source_target_pairs={{0,8},{8,0},{16,24},{24,16},{1,9},{9,1},{17,25},{25,17},{2,10},{10... | collective-permute-start | bytes 491528 | tf_op jit(solution)/shard_map/ppermute | solution.py:308
  3.3 12.2 %collective-permute-start.2 = (bf16[40,2048]{1,0:T(8,128)(2,1)S(1)}, bf16[40,2048]{1,0:T(8,128)(2,1)S(1)}, u32[]{:S(2)}, u32[]{:S(2)}) collective-permute-start(bf16[40,2048]{1,0:T(8,128)(2,1)S(1)} %get-tuple-element.199), channel_id=1, source_target_pairs={{0,24},{8,16},{16,8},{24,0},{1,25},{9,17},{17,9},{25,1},{2,26},{10... | collective-permute-start | bytes 491528 | tf_op jit(solution)/shard_map/ppermute | solution.py:308
  5.9 9.6 %collective-permute-start.1 = (bf16[40,2048]{1,0:T(8,128)(2,1)S(1)}, bf16[40,2048]{1,0:T(8,128)(2,1)S(1)}, u32[]{:S(2)}, u32[]{:S(2)}) collective-permute-start(bf16[40,2048]{1,0:T(8,128)(2,1)S(1)} %get-tuple-element.200), channel_id=1, source_target_pairs={{0,16},{8,24},{16,0},{24,8},{1,17},{9,25},{17,1},{25,9},{2,18},{10... | collective-permute-start | bytes 491528 | tf_op jit(solution)/shard_map/ppermute | solution.py:308
  6.0 10.8 %collective-permute-start.4 = (bf16[2,1,40,2048]{3,2,1,0:T(8,128)(2,1)S(1)}, bf16[2,1,40,2048]{3,2,1,0:T(8,128)(2,1)S(1)}, u32[]{:S(2)}, u32[]{:S(2)}) collective-permute-start(bf16[2,1,40,2048]{3,2,1,0:T(8,128)(2,1)S(1)} %get-tuple-element.101.refs_0_), channel_id=1, source_target_pairs={{2,4},{3,5},{4,2},{5,3},{10,12},{11,13},{12,10},{13,11},{18,20},{1... | collective-permute-start | bytes 983048 | tf_op jit(solution)/shard_map/ppermute | solution.py:336
  6.6 13.5 %collective-permute-start.3 = (bf16[2,1,40,2048]{3,2,1,0:T(8,128)(2,1)S(1)}, bf16[2,1,40,2048]{3,2,1,0:T(8,128)(2,1)S(1)}, u32[]{:S(2)}, u32[]{:S(2)}) collective-permute-start(bf16[2,1,40,2048]{3,2,1,0:T(8,128)(2,1)S(1)} %get-tuple-element.101.refs_0_), channel_id=1, source_target_pairs={{0,2},{1,3},{2,0},{3,1},{4,6},{5,7},{6,4},{7,5},{8,10},{9,11},{10,... | collective-permute-start | bytes 983048 | tf_op jit(solution)/shard_map/ppermute | solution.py:336
  11.7 10.0 %copy-start.1 = (s32[32,28]{1,0:T(8,128)S(1)}, s32[32,28]{1,0:T(8,128)}, u32[]{:S(2)}) copy-start(s32[32,28]{1,0:T(8,128)} %mask_ref.5) | copy-start | bytes 10756
  15.5 10.5 %collective-permute-start.7 = (bf16[2,1,40,2048]{3,2,1,0:T(8,128)(2,1)S(1)}, bf16[2,1,40,2048]{3,2,1,0:T(8,128)(2,1)S(1)}, u32[]{:S(2)}, u32[]{:S(2)}) collective-permute-start(bf16[2,1,40,2048]{3,2,1,0:T(8,128)(2,1)S(1)} %get-tuple-element.104.refs_1_), channel_id=1, source_target_pairs={{0,2},{1,3},{2,0},{3,1},{4,6},{5,7},{6,4},{7,5},{8,10},{9,11},{10,... | collective-permute-start | bytes 983048 | tf_op jit(solution)/shard_map/ppermute | solution.py:336
  16.0 10.0 %collective-permute-start.6 = (bf16[2,1,40,2048]{3,2,1,0:T(8,128)(2,1)S(1)}, bf16[2,1,40,2048]{3,2,1,0:T(8,128)(2,1)S(1)}, u32[]{:S(2)}, u32[]{:S(2)}) collective-permute-start(bf16[2,1,40,2048]{3,2,1,0:T(8,128)(2,1)S(1)} %get-tuple-element.104.refs_1_), channel_id=1, source_target_pairs={{2,4},{3,5},{4,2},{5,3},{10,12},{11,13},{12,10},{13,11},{18,20},{1... | collective-permute-start | bytes 983048 | tf_op jit(solution)/shard_map/ppermute | solution.py:336
  20.2 14.3 %collective-permute-start.5 = (bf16[160,2048]{1,0:T(8,128)(2,1)S(1)}, bf16[160,2048]{1,0:T(8,128)(2,1)S(1)}, u32[]{:S(2)}, u32[]{:S(2)}) collective-permute-start(bf16[160,2048]{1,0:T(8,128)(2,1)S(1)} %get-tuple-element.107.refs_0_.mine_ref), channel_id=1, source_target_pairs={{0,1},{1,0},{2,3},{3,2},{4,5},{5,4},{6,7},{7,6},{8,9},{9,8},{10,11... | collective-permute-start | bytes 1966088 | tf_op jit(solution)/shard_map/ppermute | solution.py:308
  25.5 3.9 %copy-start.2 = (s32[28,128]{1,0:T(8,128)S(1)}, s32[28,128]{1,0:T(8,128)}, u32[]{:S(2)}) copy-start(s32[28,128]{1,0:T(8,128)} %mask_ref.7) | copy-start | bytes 43012
  26.1 20.5 %collective-permute-start.10 = (bf16[160,2048]{1,0:T(8,128)(2,1)S(1)}, bf16[160,2048]{1,0:T(8,128)(2,1)S(1)}, u32[]{:S(2)}, u32[]{:S(2)}) collective-permute-start(bf16[160,2048]{1,0:T(8,128)(2,1)S(1)} %get-tuple-element.107.refs_0_.mine_ref), channel_id=1, source_target_pairs={{0,6},{1,7},{6,0},{7,1},{8,14},{9,15},{14,8},{15,9},{16,22},{17,23... | collective-permute-start | bytes 1966088 | tf_op jit(solution)/shard_map/ppermute | solution.py:336
  34.5 15.5 %collective-permute-start.12 = (bf16[160,2048]{1,0:T(8,128)(2,1)S(1)}, bf16[160,2048]{1,0:T(8,128)(2,1)S(1)}, u32[]{:S(2)}, u32[]{:S(2)}) collective-permute-start(bf16[160,2048]{1,0:T(8,128)(2,1)S(1)} %get-tuple-element.127.refs_0_), channel_id=1, source_target_pairs={{0,1},{1,0},{2,3},{3,2},{4,5},{5,4},{6,7},{7,6},{8,9},{9,8},{10,11... | collective-permute-start | bytes 1966088 | tf_op jit(solution)/shard_map/ppermute | solution.py:308
  42.1 7.7 %collective-permute-start.8 = (bf16[2,2,40,1792]{3,2,1,0:T(8,128)(2,1)S(1)}, bf16[2,2,40,1792]{3,2,1,0:T(8,128)(2,1)S(1)}, u32[]{:S(2)}, u32[]{:S(2)}) collective-permute-start(bf16[2,2,40,1792]{3,2,1,0:T(8,128)(2,1)S(1)} %get-tuple-element.116), channel_id=1, source_target_pairs={{0,8},{8,0},{16,24},{24,16},{1,9},{9,1},{17,25},{25,17},{2,10},{10... | collective-permute-start | bytes 1720328 | tf_op jit(solution)/shard_map/ppermute | solution.py:308
  42.2 7.6 %collective-permute-start.9 = (bf16[2,2,1,40,1792]{4,3,2,1,0:T(8,128)(2,1)S(1)}, bf16[2,2,1,40,1792]{4,3,2,1,0:T(8,128)(2,1)S(1)}, u32[]{:S(2)}, u32[]{:S(2)}) collective-permute-start(bf16[2,2,1,40,1792]{4,3,2,1,0:T(8,128)(2,1)S(1)} %get-tuple-element.117), channel_id=1, source_target_pairs={{0,8},{8,0},{16,24},{24,16},{1,9},{9,1},{17,25},{25,17},{2,10},{10... | collective-permute-start | bytes 1720328 | tf_op jit(solution)/shard_map/ppermute | solution.py:308
  47.3 17.8 %collective-permute-start.11 = (bf16[160,2048]{1,0:T(8,128)(2,1)S(1)}, bf16[160,2048]{1,0:T(8,128)(2,1)S(1)}, u32[]{:S(2)}, u32[]{:S(2)}) collective-permute-start(bf16[160,2048]{1,0:T(8,128)(2,1)S(1)} %get-tuple-element.124), channel_id=1, source_target_pairs={{0,4},{1,5},{4,6},{5,7},{6,2},{7,3},{2,0},{3,1},{8,12},{9,13},{12,... | collective-permute-start | bytes 1966088 | tf_op jit(solution)/shard_map/ppermute | solution.py:336
  50.0 16.5 %collective-permute-start.13 = (bf16[160,2048]{1,0:T(8,128)(2,1)S(1)}, bf16[160,2048]{1,0:T(8,128)(2,1)S(1)}, u32[]{:S(2)}, u32[]{:S(2)}) collective-permute-start(bf16[160,2048]{1,0:T(8,128)(2,1)S(1)} %get-tuple-element.129.refs_0_), channel_id=1, source_target_pairs={{0,1},{1,0},{2,3},{3,2},{4,5},{5,4},{6,7},{7,6},{8,9},{9,8},{10,11... | collective-permute-start | bytes 1966088 | tf_op jit(solution)/shard_map/ppermute | solution.py:308
  56.7 2.0 %collective-permute-start.14 = (bf16[2,2,1,40,1792]{4,3,2,1,0:T(8,128)(2,1)S(1)}, bf16[2,2,1,40,1792]{4,3,2,1,0:T(8,128)(2,1)S(1)}, u32[]{:S(2)}, u32[]{:S(2)}) collective-permute-start(bf16[2,2,1,40,1792]{4,3,2,1,0:T(8,128)(2,1)S(1)} %get-tuple-element.131), channel_id=1, source_target_pairs={{0,8},{8,0},{16,24},{24,16},{1,9},{9,1},{17,25},{25,17},{2,10},{10... | collective-permute-start | bytes 1720328 | tf_op jit(solution)/shard_map/ppermute | solution.py:308
  56.7 2.8 %collective-permute-start.15 = (bf16[2,2,40,1792]{3,2,1,0:T(8,128)(2,1)S(1)}, bf16[2,2,40,1792]{3,2,1,0:T(8,128)(2,1)S(1)}, u32[]{:S(2)}, u32[]{:S(2)}) collective-permute-start(bf16[2,2,40,1792]{3,2,1,0:T(8,128)(2,1)S(1)} %get-tuple-element.133), channel_id=1, source_target_pairs={{0,8},{8,0},{16,24},{24,16},{1,9},{9,1},{17,25},{25,17},{2,10},{10... | collective-permute-start | bytes 1720328 | tf_op jit(solution)/shard_map/ppermute | solution.py:308
  59.7 15.1 %collective-permute-start.17 = (bf16[2,2,40,1792]{3,2,1,0:T(8,128)(2,1)S(1)}, bf16[2,2,40,1792]{3,2,1,0:T(8,128)(2,1)S(1)}, u32[]{:S(2)}, u32[]{:S(2)}) collective-permute-start(bf16[2,2,40,1792]{3,2,1,0:T(8,128)(2,1)S(1)} %get-tuple-element.136), channel_id=1, source_target_pairs={{0,16},{8,24},{16,0},{24,8},{1,17},{9,25},{17,1},{25,9},{2,18},{10... | collective-permute-start | bytes 1720328 | tf_op jit(solution)/shard_map/ppermute | solution.py:308
  66.5 15.6 %collective-permute-start.16 = (bf16[160,2048]{1,0:T(8,128)(2,1)S(1)}, bf16[160,2048]{1,0:T(8,128)(2,1)S(1)}, u32[]{:S(2)}, u32[]{:S(2)}) collective-permute-start(bf16[160,2048]{1,0:T(8,128)(2,1)S(1)} %collective-permute-done.11.refs_5_.refs_0_), channel_id=1, source_target_pairs={{0,1},{1,0},{2,3},{3,2},{4,5},{5,4},{6,7},{7,6},{8,9},{9,8},{10,11... | collective-permute-start | bytes 1966088 | tf_op jit(solution)/shard_map/ppermute | solution.py:308
  73.1 2.0 %collective-permute-start.19 = (bf16[2,2,1,40,1792]{4,3,2,1,0:T(8,128)(2,1)S(1)}, bf16[2,2,1,40,1792]{4,3,2,1,0:T(8,128)(2,1)S(1)}, u32[]{:S(2)}, u32[]{:S(2)}) collective-permute-start(bf16[2,2,1,40,1792]{4,3,2,1,0:T(8,128)(2,1)S(1)} %get-tuple-element.142), channel_id=1, source_target_pairs={{0,8},{8,0},{16,24},{24,16},{1,9},{9,1},{17,25},{25,17},{2,10},{10... | collective-permute-start | bytes 1720328 | tf_op jit(solution)/shard_map/ppermute | solution.py:308
  73.2 2.8 %collective-permute-start.20 = (bf16[2,2,40,1792]{3,2,1,0:T(8,128)(2,1)S(1)}, bf16[2,2,40,1792]{3,2,1,0:T(8,128)(2,1)S(1)}, u32[]{:S(2)}, u32[]{:S(2)}) collective-permute-start(bf16[2,2,40,1792]{3,2,1,0:T(8,128)(2,1)S(1)} %get-tuple-element.144), channel_id=1, source_target_pairs={{0,8},{8,0},{16,24},{24,16},{1,9},{9,1},{17,25},{25,17},{2,10},{10... | collective-permute-start | bytes 1720328 | tf_op jit(solution)/shard_map/ppermute | solution.py:308
  75.1 2.6 %collective-permute-start.18 = (bf16[2,40,1792]{2,1,0:T(8,128)(2,1)S(1)}, bf16[2,40,1792]{2,1,0:T(8,128)(2,1)S(1)}, u32[]{:S(2)}, u32[]{:S(2)}) collective-permute-start(bf16[2,40,1792]{2,1,0:T(8,128)(2,1)S(1)} %get-tuple-element.138.own_ref), channel_id=1, source_target_pairs={{0,8},{8,0},{16,24},{24,16},{1,9},{9,1},{17,25},{25,17},{2,10},{10... | collective-permute-start | bytes 860168 | tf_op jit(solution)/shard_map/ppermute | solution.py:308
  76.1 15.1 %collective-permute-start.23 = (bf16[2,2,40,1792]{3,2,1,0:T(8,128)(2,1)S(1)}, bf16[2,2,40,1792]{3,2,1,0:T(8,128)(2,1)S(1)}, u32[]{:S(2)}, u32[]{:S(2)}) collective-permute-start(bf16[2,2,40,1792]{3,2,1,0:T(8,128)(2,1)S(1)} %get-tuple-element.150), channel_id=1, source_target_pairs={{0,16},{8,24},{16,0},{24,8},{1,17},{9,25},{17,1},{25,9},{2,18},{10... | collective-permute-start | bytes 1720328 | tf_op jit(solution)/shard_map/ppermute | solution.py:308
  82.1 16.1 %collective-permute-start.28 = (bf16[2,40,4096]{2,1,0:T(8,128)(2,1)S(1)}, bf16[2,40,4096]{2,1,0:T(8,128)(2,1)S(1)}, u32[]{:S(2)}, u32[]{:S(2)}) collective-permute-start(bf16[2,40,4096]{2,1,0:T(8,128)(2,1)S(1)} %get-tuple-element.162), channel_id=1, source_target_pairs={{0,1},{1,0},{2,3},{3,2},{4,5},{5,4},{6,7},{7,6},{8,9},{9,8},{10,11... | collective-permute-start | bytes 1966088 | tf_op jit(solution)/shard_map/ppermute | solution.py:308
  89.3 2.3 %collective-permute-start.21 = (bf16[1,2,1,40,1792]{4,3,2,1,0:T(8,128)(2,1)S(1)}, bf16[1,2,1,40,1792]{4,3,2,1,0:T(8,128)(2,1)S(1)}, u32[]{:S(2)}, u32[]{:S(2)}) collective-permute-start(bf16[1,2,1,40,1792]{4,3,2,1,0:T(8,128)(2,1)S(1)} %get-tuple-element.148), channel_id=1, source_target_pairs={{0,8},{8,0},{16,24},{24,16},{1,9},{9,1},{17,25},{25,17},{2,10},{10... | collective-permute-start | bytes 860168 | tf_op jit(solution)/shard_map/ppermute | solution.py:308
  89.3 2.2 %collective-permute-start.22 = (bf16[1,2,1,40,1792]{4,3,2,1,0:T(8,128)(2,1)S(1)}, bf16[1,2,1,40,1792]{4,3,2,1,0:T(8,128)(2,1)S(1)}, u32[]{:S(2)}, u32[]{:S(2)}) collective-permute-start(bf16[1,2,1,40,1792]{4,3,2,1,0:T(8,128)(2,1)S(1)} %get-tuple-element.149), channel_id=1, source_target_pairs={{0,8},{8,0},{16,24},{24,16},{1,9},{9,1},{17,25},{25,17},{2,10},{10... | collective-permute-start | bytes 860168 | tf_op jit(solution)/shard_map/ppermute | solution.py:308
  91.5 2.3 %collective-permute-start.27 = (bf16[2,40,1792]{2,1,0:T(8,128)(2,1)S(1)}, bf16[2,40,1792]{2,1,0:T(8,128)(2,1)S(1)}, u32[]{:S(2)}, u32[]{:S(2)}) collective-permute-start(bf16[2,40,1792]{2,1,0:T(8,128)(2,1)S(1)} %get-tuple-element.158.own_ref), channel_id=1, source_target_pairs={{0,8},{8,0},{16,24},{24,16},{1,9},{9,1},{17,25},{25,17},{2,10},{10... | collective-permute-start | bytes 860168 | tf_op jit(solution)/shard_map/ppermute | solution.py:308
  91.7 17.1 %collective-permute-start.26 = (bf16[2,2,40,1792]{3,2,1,0:T(8,128)(2,1)S(1)}, bf16[2,2,40,1792]{3,2,1,0:T(8,128)(2,1)S(1)}, u32[]{:S(2)}, u32[]{:S(2)}) collective-permute-start(bf16[2,2,40,1792]{3,2,1,0:T(8,128)(2,1)S(1)} %get-tuple-element.157), channel_id=1, source_target_pairs={{0,8},{8,0},{16,24},{24,16},{1,9},{9,1},{17,25},{25,17},{2,10},{10... | collective-permute-start | bytes 1720328 | tf_op jit(solution)/shard_map/ppermute | solution.py:308
  92.3 16.5 %collective-permute-start.24 = (bf16[2,2,40,1792]{3,2,1,0:T(8,128)(2,1)S(1)}, bf16[2,2,40,1792]{3,2,1,0:T(8,128)(2,1)S(1)}, u32[]{:S(2)}, u32[]{:S(2)}) collective-permute-start(bf16[2,2,40,1792]{3,2,1,0:T(8,128)(2,1)S(1)} %get-tuple-element.153), channel_id=1, source_target_pairs={{0,16},{8,24},{16,0},{24,8},{1,17},{9,25},{17,1},{25,9},{2,18},{10... | collective-permute-start | bytes 1720328 | tf_op jit(solution)/shard_map/ppermute | solution.py:308
  98.1 9.0 %collective-permute-start.29 = (bf16[1,40,4096]{2,1,0:T(8,128)(2,1)S(1)}, bf16[1,40,4096]{2,1,0:T(8,128)(2,1)S(1)}, u32[]{:S(2)}, u32[]{:S(2)}) collective-permute-start(bf16[1,40,4096]{2,1,0:T(8,128)(2,1)S(1)} %get-tuple-element.163), channel_id=1, source_target_pairs={{0,1},{1,0},{2,3},{3,2},{4,5},{5,4},{6,7},{7,6},{8,9},{9,8},{10,11... | collective-permute-start | bytes 983048 | tf_op jit(solution)/shard_map/ppermute | solution.py:308
  99.8 17.7 %collective-permute-start.32 = (bf16[2,40,4096]{2,1,0:T(8,128)(2,1)S(1)}, bf16[2,40,4096]{2,1,0:T(8,128)(2,1)S(1)}, u32[]{:S(2)}, u32[]{:S(2)}) collective-permute-start(bf16[2,40,4096]{2,1,0:T(8,128)(2,1)S(1)} %get-tuple-element.177), channel_id=1, source_target_pairs={{0,2},{1,3},{2,0},{3,1},{4,6},{5,7},{6,4},{7,5},{8,10},{9,11},{10,... | collective-permute-start | bytes 1966088 | tf_op jit(solution)/shard_map/ppermute | solution.py:336
  107.2 10.3 %collective-permute-start.31 = (bf16[1,40,4096]{2,1,0:T(8,128)(2,1)S(1)}, bf16[1,40,4096]{2,1,0:T(8,128)(2,1)S(1)}, u32[]{:S(2)}, u32[]{:S(2)}) collective-permute-start(bf16[1,40,4096]{2,1,0:T(8,128)(2,1)S(1)} %get-tuple-element.175), channel_id=1, source_target_pairs={{0,1},{1,0},{2,3},{3,2},{4,5},{5,4},{6,7},{7,6},{8,9},{9,8},{10,11... | collective-permute-start | bytes 983048 | tf_op jit(solution)/shard_map/ppermute | solution.py:308
  109.1 2.5 %collective-permute-start.30 = (bf16[2,40,1792]{2,1,0:T(8,128)(2,1)S(1)}, bf16[2,40,1792]{2,1,0:T(8,128)(2,1)S(1)}, u32[]{:S(2)}, u32[]{:S(2)}) collective-permute-start(bf16[2,40,1792]{2,1,0:T(8,128)(2,1)S(1)} %get-tuple-element.168.own_ref), channel_id=1, source_target_pairs={{0,8},{8,0},{16,24},{24,16},{1,9},{9,1},{17,25},{25,17},{2,10},{10... | collective-permute-start | bytes 860168 | tf_op jit(solution)/shard_map/ppermute | solution.py:308
  109.2 16.2 %collective-permute-start.25 = (bf16[2,2,40,1792]{3,2,1,0:T(8,128)(2,1)S(1)}, bf16[2,2,40,1792]{3,2,1,0:T(8,128)(2,1)S(1)}, u32[]{:S(2)}, u32[]{:S(2)}) collective-permute-start(bf16[2,2,40,1792]{3,2,1,0:T(8,128)(2,1)S(1)} %get-tuple-element.154), channel_id=1, source_target_pairs={{0,16},{8,24},{16,0},{24,8},{1,17},{9,25},{17,1},{25,9},{2,18},{10... | collective-permute-start | bytes 1720328 | tf_op jit(solution)/shard_map/ppermute | solution.py:308
  110.4 14.2 %collective-permute-start.34 = (bf16[1,40,4096]{2,1,0:T(8,128)(2,1)S(1)}, bf16[1,40,4096]{2,1,0:T(8,128)(2,1)S(1)}, u32[]{:S(2)}, u32[]{:S(2)}) collective-permute-start(bf16[1,40,4096]{2,1,0:T(8,128)(2,1)S(1)} %get-tuple-element.174), channel_id=1, source_target_pairs={{0,2},{1,3},{2,0},{3,1},{4,6},{5,7},{6,4},{7,5},{8,10},{9,11},{10,... | collective-permute-start | bytes 983048 | tf_op jit(solution)/shard_map/ppermute | solution.py:336
  117.6 7.6 %collective-permute-start.33 = (bf16[1,40,4096]{2,1,0:T(8,128)(2,1)S(1)}, bf16[1,40,4096]{2,1,0:T(8,128)(2,1)S(1)}, u32[]{:S(2)}, u32[]{:S(2)}) collective-permute-start(bf16[1,40,4096]{2,1,0:T(8,128)(2,1)S(1)} %get-tuple-element.179), channel_id=1, source_target_pairs={{0,1},{1,0},{2,3},{3,2},{4,5},{5,4},{6,7},{7,6},{8,9},{9,8},{10,11... | collective-permute-start | bytes 983048 | tf_op jit(solution)/shard_map/ppermute | solution.py:308
  118.2 13.9 %collective-permute-start.38 = (bf16[1,40,4096]{2,1,0:T(8,128)(2,1)S(1)}, bf16[1,40,4096]{2,1,0:T(8,128)(2,1)S(1)}, u32[]{:S(2)}, u32[]{:S(2)}) collective-permute-start(bf16[1,40,4096]{2,1,0:T(8,128)(2,1)S(1)} %get-tuple-element.178), channel_id=1, source_target_pairs={{0,2},{1,3},{2,0},{3,1},{4,6},{5,7},{6,4},{7,5},{8,10},{9,11},{10,... | collective-permute-start | bytes 983048 | tf_op jit(solution)/shard_map/ppermute | solution.py:336
  125.7 2.6 %collective-permute-start.35 = (bf16[2,40,1792]{2,1,0:T(8,128)(2,1)S(1)}, bf16[2,40,1792]{2,1,0:T(8,128)(2,1)S(1)}, u32[]{:S(2)}, u32[]{:S(2)}) collective-permute-start(bf16[2,40,1792]{2,1,0:T(8,128)(2,1)S(1)} %get-tuple-element.182.own_ref), channel_id=1, source_target_pairs={{0,8},{8,0},{16,24},{24,16},{1,9},{9,1},{17,25},{25,17},{2,10},{10... | collective-permute-start | bytes 860168 | tf_op jit(solution)/shard_map/ppermute | solution.py:308
  125.8 10.1 %collective-permute-start.36 = (bf16[1,40,4096]{2,1,0:T(8,128)(2,1)S(1)}, bf16[1,40,4096]{2,1,0:T(8,128)(2,1)S(1)}, u32[]{:S(2)}, u32[]{:S(2)}) collective-permute-start(bf16[1,40,4096]{2,1,0:T(8,128)(2,1)S(1)} %get-tuple-element.188), channel_id=1, source_target_pairs={{0,1},{1,0},{2,3},{3,2},{4,5},{5,4},{6,7},{7,6},{8,9},{9,8},{10,11... | collective-permute-start | bytes 983048 | tf_op jit(solution)/shard_map/ppermute | solution.py:308
  126.4 25.3 %collective-permute-start.40 = (bf16[1,40,4096]{2,1,0:T(8,128)(2,1)S(1)}, bf16[1,40,4096]{2,1,0:T(8,128)(2,1)S(1)}, u32[]{:S(2)}, u32[]{:S(2)}) collective-permute-start(bf16[1,40,4096]{2,1,0:T(8,128)(2,1)S(1)} %get-tuple-element.187), channel_id=1, source_target_pairs={{0,4},{1,5},{4,0},{5,1},{2,6},{3,7},{6,2},{7,3},{8,12},{9,13},{12,... | collective-permute-start | bytes 983048 | tf_op jit(solution)/shard_map/ppermute | solution.py:336
  136.0 22.2 %collective-permute-start.39 = (bf16[1,40,4096]{2,1,0:T(8,128)(2,1)S(1)}, bf16[1,40,4096]{2,1,0:T(8,128)(2,1)S(1)}, u32[]{:S(2)}, u32[]{:S(2)}) collective-permute-start(bf16[1,40,4096]{2,1,0:T(8,128)(2,1)S(1)} %get-tuple-element.194), channel_id=1, source_target_pairs={{0,4},{1,5},{4,0},{5,1},{2,6},{3,7},{6,2},{7,3},{8,12},{9,13},{12,... | collective-permute-start | bytes 983048 | tf_op jit(solution)/shard_map/ppermute | solution.py:336
  138.0 16.0 %collective-permute-start.37 = (bf16[2,40,4096]{2,1,0:T(8,128)(2,1)S(1)}, bf16[2,40,4096]{2,1,0:T(8,128)(2,1)S(1)}, u32[]{:S(2)}, u32[]{:S(2)}) collective-permute-start(bf16[2,40,4096]{2,1,0:T(8,128)(2,1)S(1)} %get-tuple-element.189), channel_id=1, source_target_pairs={{0,1},{1,0},{2,3},{3,2},{4,5},{5,4},{6,7},{7,6},{8,9},{9,8},{10,11... | collective-permute-start | bytes 1966088 | tf_op jit(solution)/shard_map/ppermute | solution.py:308
  154.1 4.1 %collective-permute-start.41 = (bf16[40,4096]{1,0:T(8,128)(2,1)S(1)}, bf16[40,4096]{1,0:T(8,128)(2,1)S(1)}, u32[]{:S(2)}, u32[]{:S(2)}) collective-permute-start(bf16[40,4096]{1,0:T(8,128)(2,1)S(1)} %fusion.4), channel_id=1, source_target_pairs={{0,8},{8,0},{16,24},{24,16},{1,9},{9,1},{17,25},{25,17},{2,10},{10... | collective-permute-start | bytes 983048 | tf_op jit(solution)/shard_map/ppermute | solution.py:308

commit v14 on v13

--- a/solution.py
+++ b/solution.py
@@ -114,6 +114,22 @@
         cost_estimate=as_if(hint),
         name=name,
     )(*blocks, *after)
+
+
+def wait_kernel(*refs):
+    refs[-1][...] = jnp.zeros_like(refs[-1])
+
+
+def waited(after, hint):
+    return pl.pallas_call(
+        wait_kernel,
+        in_specs=[ANYWHERE] * len(after),
+        out_specs=INSIDE,
+        out_shape=TOKEN,
+        compiler_params=pltpu.CompilerParams(vmem_limit_bytes=VMEM // 2),
+        cost_estimate=as_if(hint),
+        name="waited",
+    )(*after)
 
 
 def stack(blocks, after):
@@ -319,13 +335,15 @@
 
     normed = rms_normed(tokens, norm_gain)
     def block(step):
-        values = lax.dynamic_slice_in_dim(normed, (row ^ step) * features, features, 1)
-        return swap(values, "rows", row_count, step) if step else values
-
-    first, token = stack([block(core_step) for core_step in range(CORES)], [])
+        return lax.dynamic_slice_in_dim(normed, (row ^ step) * features, features, 1)
+
+    from_core = swap(jnp.stack([block(chip * CORES + 1) for chip in range(chips)]), "rows", row_count, 1)
+    to_chips_rows = [stack([block(chip * CORES), from_core[chip]], [])[0] for chip in range(1, chips)]
+    first, token = stack([block(0), from_core[0]], to_chips_rows[:1])
     gate_kept, token = masked(gate_weight, gate_mask, tile_of(features, 256), place, 1, lambda core: 0, [token])
-    second = [block(chip * CORES + core_step) for core_step in range(CORES) for chip in range(1, chips)]
-    second, token = stack(second, [token])
+    second = [swap(part, "rows", row_count, (chip + 1) * CORES) for chip, part in enumerate(to_chips_rows)]
+    second = jnp.concatenate(second, 1) if len(second) > 1 else second[0]
+    second = lax.optimization_barrier((second, token))[0]
     mine, token = join([first, second], [token])
 
     def behind(values, after):
@@ -387,13 +405,15 @@
         _, _, (summed,), last[0] = sums([], [], [parts], last + list(after), hint)
         return summed
 
+    next_stacks = [by_plane(first, NEXT), by_plane(second, NEXT)]
     across_stacks = [by_plane(first, ACROSS), by_plane(second, ACROSS)]
-    next_stacks = [by_plane(first, NEXT), by_plane(second, NEXT)]
-    forward(0, mine, [next_stacks[0], across_stacks[0]])
+    row_stacks = {
+        step: [by_row_of_plane(first, step), by_row_of_plane(second, step)] for step in range(1, per_plane)
+    }
     up_kept, last[0] = masked(
-        up_weight, up_mask, tile_of(features, 256), place, 1, lambda core: 0,
-        last + [next_stacks[0], across_stacks[0]], 0.15
+        up_weight, up_mask, tile_of(features, 256), place, 1, lambda core: 0, last + next_stacks[:1], 0.15
     )
+    last[0] = waited([*last, across_stacks[0], *(stacks[0] for stacks in row_stacks.values())], 0.07)
     one_away, last[0] = join(next_stacks, last)
     inner_three, last[0] = join(across_stacks, last)
     outer_three = by_plane(mine, AROUND, last)
@@ -406,7 +426,11 @@
         down_kept.append(part)
 
     keep_down(0, 8)
-    forward(1, one_away, [*parts[0][1:], *last])
+    parts[0] = [mine]
+    for stacks in row_stacks.values():
+        part, last[0] = join(stacks, last)
+        parts[0].append(part)
+    forward(1, one_away, last)
     multiply_in(0, hint=0)
     exchange(0)
     exchange_near(0)

time: 160 us -> 160 us (level)
    ppermute x31, waiting for transfers between devices: 21.2 us -> 25.5 us  [swap(): lax.ppermute(values, axis, [(place, place ^ step) for place in range(size)])]
    ppermute x11, waiting for transfers between devices: 32 us -> 28 us  [by_plane(): return lax.ppermute(behind(values, after), 'cols', pairs)]
    ppermute x11, starting transfers between devices: 20.4 us -> 17.3 us  [by_plane(): return lax.ppermute(behind(values, after), 'cols', pairs)]
    ppermute x31, starting transfers between devices: 22.3 us -> 25.2 us  [swap(): lax.ppermute(values, axis, [(place, place ^ step) for place in range(size)])]
  transfers between devices with their start and end apart: 42 -> 42, of which waited for: 20 -> 19; matrix products, arithmetic and copies ran while one was open for 0% -> 0% of each run, Pallas kernels for 37% -> 37%
where the time goes in v14:
time: 160 us
  Pallas kernels  59.6 us (37%)
  waiting for transfers between devices  53.5 us (33%)
  starting transfers between devices  42.5 us (27%)
  other arithmetic  4 us (2%)
    ppermute x11, waiting for transfers between devices, by_plane(): return lax.ppermute(behind(values, after), 'cols', pairs)  28 us
    ppermute x31, waiting for transfers between devices, swap(): lax.ppermute(values, axis, [(place, place ^ step) for place in range(size)])  25.5 us
    ppermute x31, starting transfers between devices, swap(): lax.ppermute(values, axis, [(place, place ^ step) for place in range(size)])  25.2 us
    pallas_call x4, Pallas kernels, gate_up(): pl.pallas_call(functools.partial(gate_up_kernel, len(parts), len(after)),...  24.3 us
    ppermute x11, starting transfers between devices, by_plane(): return lax.ppermute(behind(values, after), 'cols', pairs)  17.3 us
    pallas_call x4, Pallas kernels, down(): pl.pallas_call(functools.partial(down_kernel, pieces, len(down_kept), len...  15.5 us
    pallas_call x4, Pallas kernels, masked(): pl.pallas_call(functools.partial(mask_kernel, share, rows, len(after)), i...  15.4 us
  transfers between devices with their start and end apart: 42, of which 19 were waited for; matrix products, arithmetic and copies ran while one was open for 0% of the time, Pallas kernels for 37%

profile of v14, /device:TPU:0, one launch (start us, length us, event | category | flops | bytes accessed | tf_op | source)
XLA Modules:
  0.0 160.2 jit_solution(4168131140422583778)
XLA Ops:
  0.0 1.3 fusion
  1.3 1.3 fusion.2
  3.3 1.3 collective-permute-done
  5.2 2.9 %collective-permute-start.1 = (bf16[2,1,40,2048]{3,2,1,0:T(8,128)(2,1)S(1)}, bf16[2,1,40,2048]{3,2,1,0:T(8,128)(2,1)S(1)}, u32[]{:S(2)}, u32[]{:S(2)}) collective-permute-start(bf16[2,1,40,2048]{3,2,1,0:T(8,128)(2,1)S(1)} %get-tuple-element.102.refs_2_), channel_id=1, source_target_pairs={{0,16},{8,24},{16,0},{24,8},{1,17},{9,25},{17,1},{25,9},{2,18},{10... | collective-permute-start | bytes 983048 | tf_op jit(solution)/shard_map/ppermute | solution.py:324
  8.1 1.6 %collective-permute-start.6 = (bf16[2,1,40,2048]{3,2,1,0:T(8,128)(2,1)S(1)}, bf16[2,1,40,2048]{3,2,1,0:T(8,128)(2,1)S(1)}, u32[]{:S(2)}, u32[]{:S(2)}) collective-permute-start(bf16[2,1,40,2048]{3,2,1,0:T(8,128)(2,1)S(1)} %get-tuple-element.103.refs_0_), channel_id=1, source_target_pairs={{0,2},{1,3},{2,0},{3,1},{4,6},{5,7},{6,4},{7,5},{8,10},{9,11},{10,... | collective-permute-start | bytes 983048 | tf_op jit(solution)/shard_map/ppermute | solution.py:354
  10.4 1.6 collective-permute-start.2
  12.1 3.8 %masked.4 = (bf16[2048,1792]{1,0:T(8,128)(2,1)S(1)}, f32[8,128]{1,0:T(8,128)S(1)}) custom-call(s32[2]{0:T(128)S(1)} %pad_add_fusion.core_ref.place_ref, bf16[2048,1792]{1,0:T(8,128)(2,1)} %weight_ref.4, s32[32,28]{1,0:T(8,128)S(1)} %copy-done, f32[8,128]{1,0:T(8,128)S(1)} %get-tuple-element.104.refs_0_), custom_call_target="tpu_custom_call" | custom-call | tf_op jit(solution)/shard_map/masked/pallas_call | solution.py:81
  16.1 4.2 %collective-permute-start.7 = (bf16[2,1,40,2048]{3,2,1,0:T(8,128)(2,1)S(1)}, bf16[2,1,40,2048]{3,2,1,0:T(8,128)(2,1)S(1)}, u32[]{:S(2)}, u32[]{:S(2)}) collective-permute-start(bf16[2,1,40,2048]{3,2,1,0:T(8,128)(2,1)S(1)} %collective-permute-done.1.refs_1_), channel_id=1, source_target_pairs={{0,2},{1,3},{2,0},{3,1},{4,6},{5,7},{6,4},{7,5},{8,10},{9,11},{10,... | collective-permute-start | bytes 983048 | tf_op jit(solution)/shard_map/ppermute | solution.py:354
  21.6 3.8 %masked.5 = (bf16[2048,1792]{1,0:T(8,128)(2,1)S(1)}, f32[8,128]{1,0:T(8,128)S(1)}) custom-call(s32[2]{0:T(128)S(1)} %pad_add_fusion.core_ref.place_ref, bf16[2048,1792]{1,0:T(8,128)(2,1)} %weight_ref.5, s32[32,28]{1,0:T(8,128)S(1)} %copy-done.1, f32[8,128]{1,0:T(8,128)S(1)} %get-tuple-element.108.refs_0_, ...), custom_call_target="tpu_custom_call" | custom-call | flops 172500000 | tf_op jit(solution)/shard_map/masked/pallas_call | solution.py:81
  25.5 1.7 %collective-permute-done.7.refs_1_ = bf16[2,1,40,2048]{3,2,1,0:T(8,128)(2,1)S(1)} collective-permute-done((bf16[2,1,40,2048]{3,2,1,0:T(8,128)(2,1)S(1)}, bf16[2,1,40,2048]{3,2,1,0:T(8,128)(2,1)S(1)}, u32[]{:S(2)}, u32[]{:S(2)}) %collective-permute-start.7) | collective-permute-done | bytes 327712 | tf_op jit(solution)/shard_map/ppermute | solution.py:354
  27.3 3.5 %collective-permute-start.10 = (bf16[160,2048]{1,0:T(8,128)(2,1)S(1)}, bf16[160,2048]{1,0:T(8,128)(2,1)S(1)}, u32[]{:S(2)}, u32[]{:S(2)}) collective-permute-start(bf16[160,2048]{1,0:T(8,128)(2,1)S(1)} %get-tuple-element.121.refs_0_.mine_ref), channel_id=1, source_target_pairs={{0,6},{1,7},{6,0},{7,1},{8,14},{9,15},{14,8},{15,9},{16,22},{17,23... | collective-permute-start | bytes 1966088 | tf_op jit(solution)/shard_map/ppermute | solution.py:354
  30.9 3.9 %masked.6 = (bf16[1792,2048]{1,0:T(8,128)(2,1)S(1)}, f32[8,128]{1,0:T(8,128)S(1)}) custom-call(s32[2]{0:T(128)S(1)} %pad_add_fusion.core_ref.place_ref, bf16[1792,8192]{1,0:T(8,128)(2,1)} %weight_ref.7, s32[28,128]{1,0:T(8,128)S(1)} %copy-done.2, f32[8,128]{1,0:T(8,128)S(1)} %get-tuple-element.111.refs_0_), custom_call_target="tpu_custom_call" | custom-call | flops 9200000000 | tf_op jit(solution)/shard_map/masked/pallas_call | solution.py:81
  34.9 1.6 collective-permute-start.12
  36.4 6.1 %gate_up.4 = (bf16[2,2,2,40,1792]{4,3,2,1,0:T(8,128)(2,1)S(1)}, bf16[2,2,40,1792]{3,2,1,0:T(8,128)(2,1)S(1)}, bf16[2,2,1,40,1792]{4,3,2,1,0:T(8,128)(2,1)S(1)}, f32[8,128]{1,0:T(8,128)S(1)}) custom-call(bf16[160,2048]{1,0:T(8,128)(2,1)S(1)} %get-tuple-element.121.refs_0_.mine_ref, bf16[160,2048]{1,0:T(8,128)(2,1)S(1)} %get-tuple-element.113.refs_1_, ...), custom_call_target="tpu_custom_call" | custom-call | tf_op jit(solution)/shard_map/gate_up/pallas_call | solution.py:206
  43.1 3.9 %masked.7 = (bf16[1792,2048]{1,0:T(8,128)(2,1)S(1)}, f32[8,128]{1,0:T(8,128)S(1)}) custom-call(s32[2]{0:T(128)S(1)} %pad_add_fusion.core_ref.place_ref, bf16[1792,8192]{1,0:T(8,128)(2,1)} %weight_ref.7, s32[28,128]{1,0:T(8,128)S(1)} %copy-done.2, f32[8,128]{1,0:T(8,128)S(1)} %get-tuple-element.122.refs_0_), custom_call_target="tpu_custom_call" | custom-call | tf_op jit(solution)/shard_map/masked/pallas_call | solution.py:81
  47.8 1.8 %collective-permute-done.12.refs_1_ = bf16[160,2048]{1,0:T(8,128)(2,1)S(1)} collective-permute-done((bf16[160,2048]{1,0:T(8,128)(2,1)S(1)}, bf16[160,2048]{1,0:T(8,128)(2,1)S(1)}, u32[]{:S(2)}, u32[]{:S(2)}) %collective-permute-start.12) | collective-permute-done | bytes 655392 | tf_op jit(solution)/shard_map/ppermute | solution.py:324
  49.7 1.5 collective-permute-start.13
  51.2 0.9 collective-permute-start.11
  52.1 6.1 %gate_up.5 = (bf16[2,2,2,40,1792]{4,3,2,1,0:T(8,128)(2,1)S(1)}, bf16[2,2,40,1792]{3,2,1,0:T(8,128)(2,1)S(1)}, bf16[2,2,1,40,1792]{4,3,2,1,0:T(8,128)(2,1)S(1)}, f32[8,128]{1,0:T(8,128)S(1)}) custom-call(bf16[160,2048]{1,0:T(8,128)(2,1)S(1)} %get-tuple-element.129.refs_0_, bf16[160,2048]{1,0:T(8,128)(2,1)S(1)} %collective-permute-done.12.refs_1_, ...), custom_call_target="tpu_custom_call" | custom-call | flops 4697620480 | tf_op jit(solution)/shard_map/gate_up/pallas_call | solution.py:206
  58.8 1.5 collective-permute-done.14.refs_1_
  61.2 1.5 collective-permute-start.17
  62.8 1.9 %collective-permute-done.13.refs_1_ = bf16[160,2048]{1,0:T(8,128)(2,1)S(1)} collective-permute-done((bf16[160,2048]{1,0:T(8,128)(2,1)S(1)}, bf16[160,2048]{1,0:T(8,128)(2,1)S(1)}, u32[]{:S(2)}, u32[]{:S(2)}) %collective-permute-start.13) | collective-permute-done | bytes 655392 | tf_op jit(solution)/shard_map/ppermute | solution.py:324
  64.9 1.5 collective-permute-start.16
  66.4 6.1 %gate_up.6 = (bf16[2,2,2,40,1792]{4,3,2,1,0:T(8,128)(2,1)S(1)}, bf16[2,2,40,1792]{3,2,1,0:T(8,128)(2,1)S(1)}, bf16[2,2,1,40,1792]{4,3,2,1,0:T(8,128)(2,1)S(1)}, f32[8,128]{1,0:T(8,128)S(1)}) custom-call(bf16[160,2048]{1,0:T(8,128)(2,1)S(1)} %get-tuple-element.131.refs_0_, bf16[160,2048]{1,0:T(8,128)(2,1)S(1)} %collective-permute-done.13.refs_1_, ...), custom_call_target="tpu_custom_call" | custom-call | flops 4697620480 | tf_op jit(solution)/shard_map/gate_up/pallas_call | solution.py:206
  73.0 3.2 %collective-permute-done.17.refs_2_ = bf16[2,2,40,1792]{3,2,1,0:T(8,128)(2,1)S(1)} collective-permute-done((bf16[2,2,40,1792]{3,2,1,0:T(8,128)(2,1)S(1)}, bf16[2,2,40,1792]{3,2,1,0:T(8,128)(2,1)S(1)}, u32[]{:S(2)}, u32[]{:S(2)}) %collective-permute-start.17) | collective-permute-done | bytes 573472 | tf_op jit(solution)/shard_map/ppermute | solution.py:324
  76.8 1.5 collective-permute-start.23
  78.4 3.9 %down.4 = (bf16[2,40,4096]{2,1,0:T(8,128)(2,1)S(1)}, bf16[2,40,4096]{2,1,0:T(8,128)(2,1)S(1)}, f32[8,128]{1,0:T(8,128)S(1)}) custom-call(bf16[2,40,1792]{2,1,0:T(8,128)(2,1)S(1)} %get-tuple-element.140.own_ref, bf16[2,40,1792]{2,1,0:T(8,128)(2,1)S(1)} %collective-permute-done.18.other_ref, bf16[1792,2048]{1,0:T(8,128)(2,1)S(1)} %get-tuple-element.141.refs_0_, ...), custom_call_target="tpu_custom_call" | custom-call | flops 2348810 | tf_op jit(solution)/shard_map/down/pallas_call | solution.py:248
  82.9 6.1 %gate_up.7 = (bf16[2,2,2,40,1792]{4,3,2,1,0:T(8,128)(2,1)S(1)}, bf16[2,2,40,1792]{3,2,1,0:T(8,128)(2,1)S(1)}, bf16[1,2,1,40,1792]{4,3,2,1,0:T(8,128)(2,1)S(1)}, ...) custom-call(bf16[160,2048]{1,0:T(8,128)(2,1)S(1)} %collective-permute-done.11.refs_5_.refs_0_, ...), custom_call_target="tpu_custom_call" | custom-call | flops 4697620480 | tf_op jit(solution)/shard_map/gate_up/pallas_call | solution.py:206
  89.5 2.7 %collective-permute-done.23.refs_2_ = bf16[2,2,40,1792]{3,2,1,0:T(8,128)(2,1)S(1)} collective-permute-done((bf16[2,2,40,1792]{3,2,1,0:T(8,128)(2,1)S(1)}, bf16[2,2,40,1792]{3,2,1,0:T(8,128)(2,1)S(1)}, u32[]{:S(2)}, u32[]{:S(2)}) %collective-permute-start.23) | collective-permute-done | bytes 573472 | tf_op jit(solution)/shard_map/ppermute | solution.py:324
  93.4 1.5 collective-permute-start.24
  94.8 3.9 %down.5 = (bf16[1,40,4096]{2,1,0:T(8,128)(2,1)S(1)}, bf16[1,40,4096]{2,1,0:T(8,128)(2,1)S(1)}, bf16[1,40,4096]{2,1,0:T(8,128)(2,1)S(1)}, bf16[1,40,4096]{2,1,0:T(8,128)(2,1)S(1)}, f32[8,128]{1,0:T(8,128)S(1)}) custom-call(bf16[2,40,1792]{2,1,0:T(8,128)(2,1)S(1)} %get-tuple-element.160.own_ref, bf16[2,40,1792]{2,1,0:T(8,128)(2,1)S(1)} %collective-permute-done.27.other_ref, ...), custom_call_target="tpu_custom_call" | custom-call | flops 2348810 | tf_op jit(solution)/shard_map/down/pallas_call | solution.py:248
  99.8 1.2 collective-permute-start.32
  101.0 7.2 %collective-permute-done.29.refs_1_ = bf16[1,40,4096]{2,1,0:T(8,128)(2,1)S(1)} collective-permute-done((bf16[1,40,4096]{2,1,0:T(8,128)(2,1)S(1)}, bf16[1,40,4096]{2,1,0:T(8,128)(2,1)S(1)}, u32[]{:S(2)}, u32[]{:S(2)}) %collective-permute-start.29) | collective-permute-done | bytes 327712 | tf_op jit(solution)/shard_map/ppermute | solution.py:324
  109.2 1.3 collective-permute-start.25
  110.5 1.1 collective-permute-start.34
  111.6 3.9 %down.6 = (bf16[1,40,4096]{2,1,0:T(8,128)(2,1)S(1)}, bf16[1,40,4096]{2,1,0:T(8,128)(2,1)S(1)}, bf16[1,40,4096]{2,1,0:T(8,128)(2,1)S(1)}, bf16[1,40,4096]{2,1,0:T(8,128)(2,1)S(1)}, f32[8,128]{1,0:T(8,128)S(1)}) custom-call(bf16[2,40,1792]{2,1,0:T(8,128)(2,1)S(1)} %get-tuple-element.170.own_ref, bf16[2,40,1792]{2,1,0:T(8,128)(2,1)S(1)} %collective-permute-done.30.other_ref, ...), custom_call_target="tpu_custom_call" | custom-call | flops 2348810 | tf_op jit(solution)/shard_map/down/pallas_call | solution.py:248
  115.5 2.1 %collective-permute-done.32.refs_3_.refs_1_ = bf16[2,40,4096]{2,1,0:T(8,128)(2,1)S(1)} collective-permute-done((bf16[2,40,4096]{2,1,0:T(8,128)(2,1)S(1)}, bf16[2,40,4096]{2,1,0:T(8,128)(2,1)S(1)}, u32[]{:S(2)}, u32[]{:S(2)}) %collective-permute-start.32) | collective-permute-done | bytes 655392 | tf_op jit(solution)/shard_map/ppermute | solution.py:354
  117.7 1.6 collective-permute-start.33
  119.3 1.1 collective-permute-start.38
  120.4 4.2 %collective-permute-done.34.refs_2_ = bf16[1,40,4096]{2,1,0:T(8,128)(2,1)S(1)} collective-permute-done((bf16[1,40,4096]{2,1,0:T(8,128)(2,1)S(1)}, bf16[1,40,4096]{2,1,0:T(8,128)(2,1)S(1)}, u32[]{:S(2)}, u32[]{:S(2)}) %collective-permute-start.34) | collective-permute-done | bytes 327712 | tf_op jit(solution)/shard_map/ppermute | solution.py:354
  125.7 1.6 collective-permute-start.36
  128.2 3.9 %down.7 = (bf16[2,40,4096]{2,1,0:T(8,128)(2,1)S(1)}, bf16[2,40,4096]{2,1,0:T(8,128)(2,1)S(1)}, f32[8,128]{1,0:T(8,128)S(1)}) custom-call(bf16[2,40,1792]{2,1,0:T(8,128)(2,1)S(1)} %get-tuple-element.184.own_ref, bf16[2,40,1792]{2,1,0:T(8,128)(2,1)S(1)} %collective-permute-done.35.other_ref, bf16[1792,2048]{1,0:T(8,128)(2,1)S(1)} %get-tuple-element.141.refs_0_, ...), custom_call_target="tpu_custom_call" | custom-call | flops 2348810 | tf_op jit(solution)/shard_map/down/pallas_call | solution.py:248
  132.2 3.7 %collective-permute-done.36.refs_1_ = bf16[1,40,4096]{2,1,0:T(8,128)(2,1)S(1)} collective-permute-done((bf16[1,40,4096]{2,1,0:T(8,128)(2,1)S(1)}, bf16[1,40,4096]{2,1,0:T(8,128)(2,1)S(1)}, u32[]{:S(2)}, u32[]{:S(2)}) %collective-permute-start.36) | collective-permute-done | bytes 327712 | tf_op jit(solution)/shard_map/ppermute | solution.py:324
  135.9 1.3 collective-permute-start.39
  137.2 1.2 collective-permute-start.37
  138.4 14.0 %collective-permute-done.40.refs_0_ = bf16[1,40,4096]{2,1,0:T(8,128)(2,1)S(1)} collective-permute-done((bf16[1,40,4096]{2,1,0:T(8,128)(2,1)S(1)}, bf16[1,40,4096]{2,1,0:T(8,128)(2,1)S(1)}, u32[]{:S(2)}, u32[]{:S(2)}) %collective-permute-start.40) | collective-permute-done | bytes 327712 | tf_op jit(solution)/shard_map/ppermute | solution.py:354
  153.4 5.6 %collective-permute-done.39 = bf16[1,40,4096]{2,1,0:T(8,128)(2,1)S(1)} collective-permute-done((bf16[1,40,4096]{2,1,0:T(8,128)(2,1)S(1)}, bf16[1,40,4096]{2,1,0:T(8,128)(2,1)S(1)}, u32[]{:S(2)}, u32[]{:S(2)}) %collective-permute-start.39) | collective-permute-done | bytes 327712 | tf_op jit(solution)/shard_map/ppermute | solution.py:354
  159.3 0.9 pad_maximum_fusion
  (88 shorter events, 15.7 us)
Async XLA Ops:
  2.7 9.3 %copy-start = (s32[32,28]{1,0:T(8,128)S(1)}, s32[32,28]{1,0:T(8,128)}, u32[]{:S(2)}) copy-start(s32[32,28]{1,0:T(8,128)} %mask_ref.4) | copy-start | bytes 10756
  2.8 1.8 %collective-permute-start = (bf16[2,40,2048]{2,1,0:T(8,128)(2,1)S(1)}, bf16[2,40,2048]{2,1,0:T(8,128)(2,1)S(1)}, u32[]{:S(2)}, u32[]{:S(2)}) collective-permute-start(bf16[2,40,2048]{2,1,0:T(8,128)(2,1)S(1)} %pad_maximum_fusion.1), channel_id=1, source_target_pairs={{0,8},{8,0},{16,24},{24,16},{1,9},{9,1},{17,25},{25,17},{2,10},{10... | collective-permute-start | bytes 983048 | tf_op jit(solution)/shard_map/ppermute | solution.py:324
  5.2 10.9 %collective-permute-start.1 = (bf16[2,1,40,2048]{3,2,1,0:T(8,128)(2,1)S(1)}, bf16[2,1,40,2048]{3,2,1,0:T(8,128)(2,1)S(1)}, u32[]{:S(2)}, u32[]{:S(2)}) collective-permute-start(bf16[2,1,40,2048]{3,2,1,0:T(8,128)(2,1)S(1)} %get-tuple-element.102.refs_2_), channel_id=1, source_target_pairs={{0,16},{8,24},{16,0},{24,8},{1,17},{9,25},{17,1},{25,9},{2,18},{10... | collective-permute-start | bytes 983048 | tf_op jit(solution)/shard_map/ppermute | solution.py:324
  8.1 13.0 %collective-permute-start.6 = (bf16[2,1,40,2048]{3,2,1,0:T(8,128)(2,1)S(1)}, bf16[2,1,40,2048]{3,2,1,0:T(8,128)(2,1)S(1)}, u32[]{:S(2)}, u32[]{:S(2)}) collective-permute-start(bf16[2,1,40,2048]{3,2,1,0:T(8,128)(2,1)S(1)} %get-tuple-element.103.refs_0_), channel_id=1, source_target_pairs={{0,2},{1,3},{2,0},{3,1},{4,6},{5,7},{6,4},{7,5},{8,10},{9,11},{10,... | collective-permute-start | bytes 983048 | tf_op jit(solution)/shard_map/ppermute | solution.py:354
  9.7 15.7 %collective-permute-start.4 = (bf16[2,1,40,2048]{3,2,1,0:T(8,128)(2,1)S(1)}, bf16[2,1,40,2048]{3,2,1,0:T(8,128)(2,1)S(1)}, u32[]{:S(2)}, u32[]{:S(2)}) collective-permute-start(bf16[2,1,40,2048]{3,2,1,0:T(8,128)(2,1)S(1)} %get-tuple-element.103.refs_0_), channel_id=1, source_target_pairs={{2,4},{3,5},{4,2},{5,3},{10,12},{11,13},{12,10},{13,11},{18,20},{1... | collective-permute-start | bytes 983048 | tf_op jit(solution)/shard_map/ppermute | solution.py:354
  10.4 15.0 %collective-permute-start.2 = (bf16[2,1,40,2048]{3,2,1,0:T(8,128)(2,1)S(1)}, bf16[2,1,40,2048]{3,2,1,0:T(8,128)(2,1)S(1)}, u32[]{:S(2)}, u32[]{:S(2)}) collective-permute-start(bf16[2,1,40,2048]{3,2,1,0:T(8,128)(2,1)S(1)} %get-tuple-element.103.refs_0_), channel_id=1, source_target_pairs={{0,1},{1,0},{2,3},{3,2},{4,5},{5,4},{6,7},{7,6},{8,9},{9,8},{10,11... | collective-permute-start | bytes 983048 | tf_op jit(solution)/shard_map/ppermute | solution.py:324
  12.1 9.6 %copy-start.1 = (s32[32,28]{1,0:T(8,128)S(1)}, s32[32,28]{1,0:T(8,128)}, u32[]{:S(2)}) copy-start(s32[32,28]{1,0:T(8,128)} %mask_ref.5) | copy-start | bytes 10756
  16.1 11.1 %collective-permute-start.7 = (bf16[2,1,40,2048]{3,2,1,0:T(8,128)(2,1)S(1)}, bf16[2,1,40,2048]{3,2,1,0:T(8,128)(2,1)S(1)}, u32[]{:S(2)}, u32[]{:S(2)}) collective-permute-start(bf16[2,1,40,2048]{3,2,1,0:T(8,128)(2,1)S(1)} %collective-permute-done.1.refs_1_), channel_id=1, source_target_pairs={{0,2},{1,3},{2,0},{3,1},{4,6},{5,7},{6,4},{7,5},{8,10},{9,11},{10,... | collective-permute-start | bytes 983048 | tf_op jit(solution)/shard_map/ppermute | solution.py:354
  20.3 6.9 %collective-permute-start.5 = (bf16[2,1,40,2048]{3,2,1,0:T(8,128)(2,1)S(1)}, bf16[2,1,40,2048]{3,2,1,0:T(8,128)(2,1)S(1)}, u32[]{:S(2)}, u32[]{:S(2)}) collective-permute-start(bf16[2,1,40,2048]{3,2,1,0:T(8,128)(2,1)S(1)} %collective-permute-done.1.refs_1_), channel_id=1, source_target_pairs={{2,4},{3,5},{4,2},{5,3},{10,12},{11,13},{12,10},{13,11},{18,20},{1... | collective-permute-start | bytes 983048 | tf_op jit(solution)/shard_map/ppermute | solution.py:354
  21.1 13.7 %collective-permute-start.3 = (bf16[2,1,40,2048]{3,2,1,0:T(8,128)(2,1)S(1)}, bf16[2,1,40,2048]{3,2,1,0:T(8,128)(2,1)S(1)}, u32[]{:S(2)}, u32[]{:S(2)}) collective-permute-start(bf16[2,1,40,2048]{3,2,1,0:T(8,128)(2,1)S(1)} %collective-permute-done.1.refs_1_), channel_id=1, source_target_pairs={{0,1},{1,0},{2,3},{3,2},{4,5},{5,4},{6,7},{7,6},{8,9},{9,8},{10,11... | collective-permute-start | bytes 983048 | tf_op jit(solution)/shard_map/ppermute | solution.py:324
  25.4 5.5 %copy-start.2 = (s32[28,128]{1,0:T(8,128)S(1)}, s32[28,128]{1,0:T(8,128)}, u32[]{:S(2)}) copy-start(s32[28,128]{1,0:T(8,128)} %mask_ref.7) | copy-start | bytes 43012
  27.3 19.7 %collective-permute-start.10 = (bf16[160,2048]{1,0:T(8,128)(2,1)S(1)}, bf16[160,2048]{1,0:T(8,128)(2,1)S(1)}, u32[]{:S(2)}, u32[]{:S(2)}) collective-permute-start(bf16[160,2048]{1,0:T(8,128)(2,1)S(1)} %get-tuple-element.121.refs_0_.mine_ref), channel_id=1, source_target_pairs={{0,6},{1,7},{6,0},{7,1},{8,14},{9,15},{14,8},{15,9},{16,22},{17,23... | collective-permute-start | bytes 1966088 | tf_op jit(solution)/shard_map/ppermute | solution.py:354
  34.9 14.8 %collective-permute-start.12 = (bf16[160,2048]{1,0:T(8,128)(2,1)S(1)}, bf16[160,2048]{1,0:T(8,128)(2,1)S(1)}, u32[]{:S(2)}, u32[]{:S(2)}) collective-permute-start(bf16[160,2048]{1,0:T(8,128)(2,1)S(1)} %get-tuple-element.129.refs_0_), channel_id=1, source_target_pairs={{0,1},{1,0},{2,3},{3,2},{4,5},{5,4},{6,7},{7,6},{8,9},{9,8},{10,11... | collective-permute-start | bytes 1966088 | tf_op jit(solution)/shard_map/ppermute | solution.py:324
  42.5 5.1 %collective-permute-start.8 = (bf16[2,2,40,1792]{3,2,1,0:T(8,128)(2,1)S(1)}, bf16[2,2,40,1792]{3,2,1,0:T(8,128)(2,1)S(1)}, u32[]{:S(2)}, u32[]{:S(2)}) collective-permute-start(bf16[2,2,40,1792]{3,2,1,0:T(8,128)(2,1)S(1)} %get-tuple-element.118), channel_id=1, source_target_pairs={{0,8},{8,0},{16,24},{24,16},{1,9},{9,1},{17,25},{25,17},{2,10},{10... | collective-permute-start | bytes 1720328 | tf_op jit(solution)/shard_map/ppermute | solution.py:324
  42.6 5.1 %collective-permute-start.9 = (bf16[2,2,1,40,1792]{4,3,2,1,0:T(8,128)(2,1)S(1)}, bf16[2,2,1,40,1792]{4,3,2,1,0:T(8,128)(2,1)S(1)}, u32[]{:S(2)}, u32[]{:S(2)}) collective-permute-start(bf16[2,2,1,40,1792]{4,3,2,1,0:T(8,128)(2,1)S(1)} %get-tuple-element.119), channel_id=1, source_target_pairs={{0,8},{8,0},{16,24},{24,16},{1,9},{9,1},{17,25},{25,17},{2,10},{10... | collective-permute-start | bytes 1720328 | tf_op jit(solution)/shard_map/ppermute | solution.py:324
  49.7 15.0 %collective-permute-start.13 = (bf16[160,2048]{1,0:T(8,128)(2,1)S(1)}, bf16[160,2048]{1,0:T(8,128)(2,1)S(1)}, u32[]{:S(2)}, u32[]{:S(2)}) collective-permute-start(bf16[160,2048]{1,0:T(8,128)(2,1)S(1)} %get-tuple-element.131.refs_0_), channel_id=1, source_target_pairs={{0,1},{1,0},{2,3},{3,2},{4,5},{5,4},{6,7},{7,6},{8,9},{9,8},{10,11... | collective-permute-start | bytes 1966088 | tf_op jit(solution)/shard_map/ppermute | solution.py:324
  51.2 13.7 %collective-permute-start.11 = (bf16[160,2048]{1,0:T(8,128)(2,1)S(1)}, bf16[160,2048]{1,0:T(8,128)(2,1)S(1)}, u32[]{:S(2)}, u32[]{:S(2)}) collective-permute-start(bf16[160,2048]{1,0:T(8,128)(2,1)S(1)} %get-tuple-element.126), channel_id=1, source_target_pairs={{0,4},{1,5},{4,6},{5,7},{6,2},{7,3},{2,0},{3,1},{8,12},{9,13},{12,... | collective-permute-start | bytes 1966088 | tf_op jit(solution)/shard_map/ppermute | solution.py:354
  58.2 2.0 %collective-permute-start.14 = (bf16[2,2,1,40,1792]{4,3,2,1,0:T(8,128)(2,1)S(1)}, bf16[2,2,1,40,1792]{4,3,2,1,0:T(8,128)(2,1)S(1)}, u32[]{:S(2)}, u32[]{:S(2)}) collective-permute-start(bf16[2,2,1,40,1792]{4,3,2,1,0:T(8,128)(2,1)S(1)} %get-tuple-element.133), channel_id=1, source_target_pairs={{0,8},{8,0},{16,24},{24,16},{1,9},{9,1},{17,25},{25,17},{2,10},{10... | collective-permute-start | bytes 1720328 | tf_op jit(solution)/shard_map/ppermute | solution.py:324
  58.3 2.8 %collective-permute-start.15 = (bf16[2,2,40,1792]{3,2,1,0:T(8,128)(2,1)S(1)}, bf16[2,2,40,1792]{3,2,1,0:T(8,128)(2,1)S(1)}, u32[]{:S(2)}, u32[]{:S(2)}) collective-permute-start(bf16[2,2,40,1792]{3,2,1,0:T(8,128)(2,1)S(1)} %get-tuple-element.135), channel_id=1, source_target_pairs={{0,8},{8,0},{16,24},{24,16},{1,9},{9,1},{17,25},{25,17},{2,10},{10... | collective-permute-start | bytes 1720328 | tf_op jit(solution)/shard_map/ppermute | solution.py:324
  61.2 15.1 %collective-permute-start.17 = (bf16[2,2,40,1792]{3,2,1,0:T(8,128)(2,1)S(1)}, bf16[2,2,40,1792]{3,2,1,0:T(8,128)(2,1)S(1)}, u32[]{:S(2)}, u32[]{:S(2)}) collective-permute-start(bf16[2,2,40,1792]{3,2,1,0:T(8,128)(2,1)S(1)} %get-tuple-element.138), channel_id=1, source_target_pairs={{0,16},{8,24},{16,0},{24,8},{1,17},{9,25},{17,1},{25,9},{2,18},{10... | collective-permute-start | bytes 1720328 | tf_op jit(solution)/shard_map/ppermute | solution.py:324
  64.9 17.4 %collective-permute-start.16 = (bf16[160,2048]{1,0:T(8,128)(2,1)S(1)}, bf16[160,2048]{1,0:T(8,128)(2,1)S(1)}, u32[]{:S(2)}, u32[]{:S(2)}) collective-permute-start(bf16[160,2048]{1,0:T(8,128)(2,1)S(1)} %collective-permute-done.11.refs_5_.refs_0_), channel_id=1, source_target_pairs={{0,1},{1,0},{2,3},{3,2},{4,5},{5,4},{6,7},{7,6},{8,9},{9,8},{10,11... | collective-permute-start | bytes 1966088 | tf_op jit(solution)/shard_map/ppermute | solution.py:324
  72.5 4.2 %collective-permute-start.19 = (bf16[2,2,1,40,1792]{4,3,2,1,0:T(8,128)(2,1)S(1)}, bf16[2,2,1,40,1792]{4,3,2,1,0:T(8,128)(2,1)S(1)}, u32[]{:S(2)}, u32[]{:S(2)}) collective-permute-start(bf16[2,2,1,40,1792]{4,3,2,1,0:T(8,128)(2,1)S(1)} %get-tuple-element.144), channel_id=1, source_target_pairs={{0,8},{8,0},{16,24},{24,16},{1,9},{9,1},{17,25},{25,17},{2,10},{10... | collective-permute-start | bytes 1720328 | tf_op jit(solution)/shard_map/ppermute | solution.py:324
  72.5 4.1 %collective-permute-start.20 = (bf16[2,2,40,1792]{3,2,1,0:T(8,128)(2,1)S(1)}, bf16[2,2,40,1792]{3,2,1,0:T(8,128)(2,1)S(1)}, u32[]{:S(2)}, u32[]{:S(2)}) collective-permute-start(bf16[2,2,40,1792]{3,2,1,0:T(8,128)(2,1)S(1)} %get-tuple-element.146), channel_id=1, source_target_pairs={{0,8},{8,0},{16,24},{24,16},{1,9},{9,1},{17,25},{25,17},{2,10},{10... | collective-permute-start | bytes 1720328 | tf_op jit(solution)/shard_map/ppermute | solution.py:324
  76.6 1.8 %collective-permute-start.18 = (bf16[2,40,1792]{2,1,0:T(8,128)(2,1)S(1)}, bf16[2,40,1792]{2,1,0:T(8,128)(2,1)S(1)}, u32[]{:S(2)}, u32[]{:S(2)}) collective-permute-start(bf16[2,40,1792]{2,1,0:T(8,128)(2,1)S(1)} %get-tuple-element.140.own_ref), channel_id=1, source_target_pairs={{0,8},{8,0},{16,24},{24,16},{1,9},{9,1},{17,25},{25,17},{2,10},{10... | collective-permute-start | bytes 860168 | tf_op jit(solution)/shard_map/ppermute | solution.py:324
  76.8 15.4 %collective-permute-start.23 = (bf16[2,2,40,1792]{3,2,1,0:T(8,128)(2,1)S(1)}, bf16[2,2,40,1792]{3,2,1,0:T(8,128)(2,1)S(1)}, u32[]{:S(2)}, u32[]{:S(2)}) collective-permute-start(bf16[2,2,40,1792]{3,2,1,0:T(8,128)(2,1)S(1)} %get-tuple-element.152), channel_id=1, source_target_pairs={{0,16},{8,24},{16,0},{24,8},{1,17},{9,25},{17,1},{25,9},{2,18},{10... | collective-permute-start | bytes 1720328 | tf_op jit(solution)/shard_map/ppermute | solution.py:324
  82.3 16.9 %collective-permute-start.28 = (bf16[2,40,4096]{2,1,0:T(8,128)(2,1)S(1)}, bf16[2,40,4096]{2,1,0:T(8,128)(2,1)S(1)}, u32[]{:S(2)}, u32[]{:S(2)}) collective-permute-start(bf16[2,40,4096]{2,1,0:T(8,128)(2,1)S(1)} %get-tuple-element.164), channel_id=1, source_target_pairs={{0,1},{1,0},{2,3},{3,2},{4,5},{5,4},{6,7},{7,6},{8,9},{9,8},{10,11... | collective-permute-start | bytes 1966088 | tf_op jit(solution)/shard_map/ppermute | solution.py:324
  89.0 3.7 %collective-permute-start.21 = (bf16[1,2,1,40,1792]{4,3,2,1,0:T(8,128)(2,1)S(1)}, bf16[1,2,1,40,1792]{4,3,2,1,0:T(8,128)(2,1)S(1)}, u32[]{:S(2)}, u32[]{:S(2)}) collective-permute-start(bf16[1,2,1,40,1792]{4,3,2,1,0:T(8,128)(2,1)S(1)} %get-tuple-element.150), channel_id=1, source_target_pairs={{0,8},{8,0},{16,24},{24,16},{1,9},{9,1},{17,25},{25,17},{2,10},{10... | collective-permute-start | bytes 860168 | tf_op jit(solution)/shard_map/ppermute | solution.py:324
  89.0 3.6 %collective-permute-start.22 = (bf16[1,2,1,40,1792]{4,3,2,1,0:T(8,128)(2,1)S(1)}, bf16[1,2,1,40,1792]{4,3,2,1,0:T(8,128)(2,1)S(1)}, u32[]{:S(2)}, u32[]{:S(2)}) collective-permute-start(bf16[1,2,1,40,1792]{4,3,2,1,0:T(8,128)(2,1)S(1)} %get-tuple-element.151), channel_id=1, source_target_pairs={{0,8},{8,0},{16,24},{24,16},{1,9},{9,1},{17,25},{25,17},{2,10},{10... | collective-permute-start | bytes 860168 | tf_op jit(solution)/shard_map/ppermute | solution.py:324
  92.6 2.3 %collective-permute-start.27 = (bf16[2,40,1792]{2,1,0:T(8,128)(2,1)S(1)}, bf16[2,40,1792]{2,1,0:T(8,128)(2,1)S(1)}, u32[]{:S(2)}, u32[]{:S(2)}) collective-permute-start(bf16[2,40,1792]{2,1,0:T(8,128)(2,1)S(1)} %get-tuple-element.160.own_ref), channel_id=1, source_target_pairs={{0,8},{8,0},{16,24},{24,16},{1,9},{9,1},{17,25},{25,17},{2,10},{10... | collective-permute-start | bytes 860168 | tf_op jit(solution)/shard_map/ppermute | solution.py:324
  92.8 16.0 %collective-permute-start.26 = (bf16[2,2,40,1792]{3,2,1,0:T(8,128)(2,1)S(1)}, bf16[2,2,40,1792]{3,2,1,0:T(8,128)(2,1)S(1)}, u32[]{:S(2)}, u32[]{:S(2)}) collective-permute-start(bf16[2,2,40,1792]{3,2,1,0:T(8,128)(2,1)S(1)} %get-tuple-element.159), channel_id=1, source_target_pairs={{0,8},{8,0},{16,24},{24,16},{1,9},{9,1},{17,25},{25,17},{2,10},{10... | collective-permute-start | bytes 1720328 | tf_op jit(solution)/shard_map/ppermute | solution.py:324
  93.4 15.5 %collective-permute-start.24 = (bf16[2,2,40,1792]{3,2,1,0:T(8,128)(2,1)S(1)}, bf16[2,2,40,1792]{3,2,1,0:T(8,128)(2,1)S(1)}, u32[]{:S(2)}, u32[]{:S(2)}) collective-permute-start(bf16[2,2,40,1792]{3,2,1,0:T(8,128)(2,1)S(1)} %get-tuple-element.155), channel_id=1, source_target_pairs={{0,16},{8,24},{16,0},{24,8},{1,17},{9,25},{17,1},{25,9},{2,18},{10... | collective-permute-start | bytes 1720328 | tf_op jit(solution)/shard_map/ppermute | solution.py:324
  99.2 9.0 %collective-permute-start.29 = (bf16[1,40,4096]{2,1,0:T(8,128)(2,1)S(1)}, bf16[1,40,4096]{2,1,0:T(8,128)(2,1)S(1)}, u32[]{:S(2)}, u32[]{:S(2)}) collective-permute-start(bf16[1,40,4096]{2,1,0:T(8,128)(2,1)S(1)} %get-tuple-element.165), channel_id=1, source_target_pairs={{0,1},{1,0},{2,3},{3,2},{4,5},{5,4},{6,7},{7,6},{8,9},{9,8},{10,11... | collective-permute-start | bytes 983048 | tf_op jit(solution)/shard_map/ppermute | solution.py:324
  99.8 17.7 %collective-permute-start.32 = (bf16[2,40,4096]{2,1,0:T(8,128)(2,1)S(1)}, bf16[2,40,4096]{2,1,0:T(8,128)(2,1)S(1)}, u32[]{:S(2)}, u32[]{:S(2)}) collective-permute-start(bf16[2,40,4096]{2,1,0:T(8,128)(2,1)S(1)} %get-tuple-element.179), channel_id=1, source_target_pairs={{0,2},{1,3},{2,0},{3,1},{4,6},{5,7},{6,4},{7,5},{8,10},{9,11},{10,... | collective-permute-start | bytes 1966088 | tf_op jit(solution)/shard_map/ppermute | solution.py:354
  108.3 9.3 %collective-permute-start.31 = (bf16[1,40,4096]{2,1,0:T(8,128)(2,1)S(1)}, bf16[1,40,4096]{2,1,0:T(8,128)(2,1)S(1)}, u32[]{:S(2)}, u32[]{:S(2)}) collective-permute-start(bf16[1,40,4096]{2,1,0:T(8,128)(2,1)S(1)} %get-tuple-element.177), channel_id=1, source_target_pairs={{0,1},{1,0},{2,3},{3,2},{4,5},{5,4},{6,7},{7,6},{8,9},{9,8},{10,11... | collective-permute-start | bytes 983048 | tf_op jit(solution)/shard_map/ppermute | solution.py:324
  109.1 2.5 %collective-permute-start.30 = (bf16[2,40,1792]{2,1,0:T(8,128)(2,1)S(1)}, bf16[2,40,1792]{2,1,0:T(8,128)(2,1)S(1)}, u32[]{:S(2)}, u32[]{:S(2)}) collective-permute-start(bf16[2,40,1792]{2,1,0:T(8,128)(2,1)S(1)} %get-tuple-element.170.own_ref), channel_id=1, source_target_pairs={{0,8},{8,0},{16,24},{24,16},{1,9},{9,1},{17,25},{25,17},{2,10},{10... | collective-permute-start | bytes 860168 | tf_op jit(solution)/shard_map/ppermute | solution.py:324
  109.2 16.1 %collective-permute-start.25 = (bf16[2,2,40,1792]{3,2,1,0:T(8,128)(2,1)S(1)}, bf16[2,2,40,1792]{3,2,1,0:T(8,128)(2,1)S(1)}, u32[]{:S(2)}, u32[]{:S(2)}) collective-permute-start(bf16[2,2,40,1792]{3,2,1,0:T(8,128)(2,1)S(1)} %get-tuple-element.156), channel_id=1, source_target_pairs={{0,16},{8,24},{16,0},{24,8},{1,17},{9,25},{17,1},{25,9},{2,18},{10... | collective-permute-start | bytes 1720328 | tf_op jit(solution)/shard_map/ppermute | solution.py:324
  110.5 14.1 %collective-permute-start.34 = (bf16[1,40,4096]{2,1,0:T(8,128)(2,1)S(1)}, bf16[1,40,4096]{2,1,0:T(8,128)(2,1)S(1)}, u32[]{:S(2)}, u32[]{:S(2)}) collective-permute-start(bf16[1,40,4096]{2,1,0:T(8,128)(2,1)S(1)} %get-tuple-element.176), channel_id=1, source_target_pairs={{0,2},{1,3},{2,0},{3,1},{4,6},{5,7},{6,4},{7,5},{8,10},{9,11},{10,... | collective-permute-start | bytes 983048 | tf_op jit(solution)/shard_map/ppermute | solution.py:354
  117.7 7.5 %collective-permute-start.33 = (bf16[1,40,4096]{2,1,0:T(8,128)(2,1)S(1)}, bf16[1,40,4096]{2,1,0:T(8,128)(2,1)S(1)}, u32[]{:S(2)}, u32[]{:S(2)}) collective-permute-start(bf16[1,40,4096]{2,1,0:T(8,128)(2,1)S(1)} %get-tuple-element.181), channel_id=1, source_target_pairs={{0,1},{1,0},{2,3},{3,2},{4,5},{5,4},{6,7},{7,6},{8,9},{9,8},{10,11... | collective-permute-start | bytes 983048 | tf_op jit(solution)/shard_map/ppermute | solution.py:324
  119.3 12.8 %collective-permute-start.38 = (bf16[1,40,4096]{2,1,0:T(8,128)(2,1)S(1)}, bf16[1,40,4096]{2,1,0:T(8,128)(2,1)S(1)}, u32[]{:S(2)}, u32[]{:S(2)}) collective-permute-start(bf16[1,40,4096]{2,1,0:T(8,128)(2,1)S(1)} %get-tuple-element.180), channel_id=1, source_target_pairs={{0,2},{1,3},{2,0},{3,1},{4,6},{5,7},{6,4},{7,5},{8,10},{9,11},{10,... | collective-permute-start | bytes 983048 | tf_op jit(solution)/shard_map/ppermute | solution.py:354
  125.6 2.6 %collective-permute-start.35 = (bf16[2,40,1792]{2,1,0:T(8,128)(2,1)S(1)}, bf16[2,40,1792]{2,1,0:T(8,128)(2,1)S(1)}, u32[]{:S(2)}, u32[]{:S(2)}) collective-permute-start(bf16[2,40,1792]{2,1,0:T(8,128)(2,1)S(1)} %get-tuple-element.184.own_ref), channel_id=1, source_target_pairs={{0,8},{8,0},{16,24},{24,16},{1,9},{9,1},{17,25},{25,17},{2,10},{10... | collective-permute-start | bytes 860168 | tf_op jit(solution)/shard_map/ppermute | solution.py:324
  125.7 10.1 %collective-permute-start.36 = (bf16[1,40,4096]{2,1,0:T(8,128)(2,1)S(1)}, bf16[1,40,4096]{2,1,0:T(8,128)(2,1)S(1)}, u32[]{:S(2)}, u32[]{:S(2)}) collective-permute-start(bf16[1,40,4096]{2,1,0:T(8,128)(2,1)S(1)} %get-tuple-element.190), channel_id=1, source_target_pairs={{0,1},{1,0},{2,3},{3,2},{4,5},{5,4},{6,7},{7,6},{8,9},{9,8},{10,11... | collective-permute-start | bytes 983048 | tf_op jit(solution)/shard_map/ppermute | solution.py:324
  127.3 25.1 %collective-permute-start.40 = (bf16[1,40,4096]{2,1,0:T(8,128)(2,1)S(1)}, bf16[1,40,4096]{2,1,0:T(8,128)(2,1)S(1)}, u32[]{:S(2)}, u32[]{:S(2)}) collective-permute-start(bf16[1,40,4096]{2,1,0:T(8,128)(2,1)S(1)} %get-tuple-element.189), channel_id=1, source_target_pairs={{0,4},{1,5},{4,0},{5,1},{2,6},{3,7},{6,2},{7,3},{8,12},{9,13},{12,... | collective-permute-start | bytes 983048 | tf_op jit(solution)/shard_map/ppermute | solution.py:354
  135.9 23.1 %collective-permute-start.39 = (bf16[1,40,4096]{2,1,0:T(8,128)(2,1)S(1)}, bf16[1,40,4096]{2,1,0:T(8,128)(2,1)S(1)}, u32[]{:S(2)}, u32[]{:S(2)}) collective-permute-start(bf16[1,40,4096]{2,1,0:T(8,128)(2,1)S(1)} %get-tuple-element.196), channel_id=1, source_target_pairs={{0,4},{1,5},{4,0},{5,1},{2,6},{3,7},{6,2},{7,3},{8,12},{9,13},{12,... | collective-permute-start | bytes 983048 | tf_op jit(solution)/shard_map/ppermute | solution.py:354
  137.2 16.0 %collective-permute-start.37 = (bf16[2,40,4096]{2,1,0:T(8,128)(2,1)S(1)}, bf16[2,40,4096]{2,1,0:T(8,128)(2,1)S(1)}, u32[]{:S(2)}, u32[]{:S(2)}) collective-permute-start(bf16[2,40,4096]{2,1,0:T(8,128)(2,1)S(1)} %get-tuple-element.191), channel_id=1, source_target_pairs={{0,1},{1,0},{2,3},{3,2},{4,5},{5,4},{6,7},{7,6},{8,9},{9,8},{10,11... | collective-permute-start | bytes 1966088 | tf_op jit(solution)/shard_map/ppermute | solution.py:324
  153.4 5.7 %collective-permute-start.41 = (bf16[40,4096]{1,0:T(8,128)(2,1)S(1)}, bf16[40,4096]{1,0:T(8,128)(2,1)S(1)}, u32[]{:S(2)}, u32[]{:S(2)}) collective-permute-start(bf16[40,4096]{1,0:T(8,128)(2,1)S(1)} %fusion.4), channel_id=1, source_target_pairs={{0,8},{8,0},{16,24},{24,16},{1,9},{9,1},{17,25},{25,17},{2,10},{10... | collective-permute-start | bytes 983048 | tf_op jit(solution)/shard_map/ppermute | solution.py:324

commit v15 on v14

--- a/solution.py
+++ b/solution.py
@@ -415,7 +415,7 @@
     )
     last[0] = waited([*last, across_stacks[0], *(stacks[0] for stacks in row_stacks.values())], 0.07)
     one_away, last[0] = join(next_stacks, last)
-    inner_three, last[0] = join(across_stacks, last)
+    inner_three, last[0] = join(across_stacks, last + [stacks[1] for stacks in row_stacks.values()])
     outer_three = by_plane(mine, AROUND, last)
     down_kept = []
 
@@ -425,7 +425,6 @@
         )
         down_kept.append(part)
 
-    keep_down(0, 8)
     parts[0] = [mine]
     for stacks in row_stacks.values():
         part, last[0] = join(stacks, last)
@@ -434,6 +433,7 @@
     multiply_in(0, hint=0)
     exchange(0)
     exchange_near(0)
+    keep_down(0)
     keep_down(1)
     three_away, passed, last[0] = pick(place, inner_three, outer_three, mine, last)
     two_away = by_plane(passed, CYCLE)

time: 160 us -> 160 us (level)
  starting transfers between devices: 42.5 us -> 39.8 us
  waiting for transfers between devices: 53.5 us -> 55.5 us
    ppermute x31, starting transfers between devices: 25.2 us -> 22 us  [swap(): lax.ppermute(values, axis, [(place, place ^ step) for place in range(size)])]
    ppermute x31, waiting for transfers between devices: 25.5 us -> 28.7 us  [swap(): lax.ppermute(values, axis, [(place, place ^ step) for place in range(size)])]
  transfers between devices with their start and end apart: 42 -> 42, of which waited for: 19 -> 22; matrix products, arithmetic and copies ran while one was open for 0% -> 0% of each run, Pallas kernels for 37% -> 37%
where the time goes in v15:
time: 160 us
  Pallas kernels  59.6 us (37%)
  waiting for transfers between devices  55.5 us (35%)
  starting transfers between devices  39.8 us (25%)
  other arithmetic  4 us (2%)
    ppermute x31, waiting for transfers between devices, swap(): lax.ppermute(values, axis, [(place, place ^ step) for place in range(size)])  28.7 us
    ppermute x11, waiting for transfers between devices, by_plane(): return lax.ppermute(behind(values, after), 'cols', pairs)  26.8 us
    pallas_call x4, Pallas kernels, gate_up(): pl.pallas_call(functools.partial(gate_up_kernel, len(parts), len(after)),...  24.3 us
    ppermute x31, starting transfers between devices, swap(): lax.ppermute(values, axis, [(place, place ^ step) for place in range(size)])  22 us
    ppermute x11, starting transfers between devices, by_plane(): return lax.ppermute(behind(values, after), 'cols', pairs)  17.9 us
    pallas_call x4, Pallas kernels, down(): pl.pallas_call(functools.partial(down_kernel, pieces, len(down_kept), len...  15.5 us
    pallas_call x4, Pallas kernels, masked(): pl.pallas_call(functools.partial(mask_kernel, share, rows, len(after)), i...  15.4 us
  transfers between devices with their start and end apart: 42, of which 22 were waited for; matrix products, arithmetic and copies ran while one was open for 0% of the time, Pallas kernels for 37%

profile of v15, /device:TPU:0, one launch (start us, length us, event | category | flops | bytes accessed | tf_op | source)
XLA Modules:
  0.0 159.5 jit_solution(10986546594331413000)
XLA Ops:
  0.0 1.3 fusion
  1.3 1.3 fusion.2
  3.3 1.3 collective-permute-done
  5.2 2.9 %collective-permute-start.1 = (bf16[2,1,40,2048]{3,2,1,0:T(8,128)(2,1)S(1)}, bf16[2,1,40,2048]{3,2,1,0:T(8,128)(2,1)S(1)}, u32[]{:S(2)}, u32[]{:S(2)}) collective-permute-start(bf16[2,1,40,2048]{3,2,1,0:T(8,128)(2,1)S(1)} %get-tuple-element.102.refs_2_), channel_id=1, source_target_pairs={{0,16},{8,24},{16,0},{24,8},{1,17},{9,25},{17,1},{25,9},{2,18},{10... | collective-permute-start | bytes 983048 | tf_op jit(solution)/shard_map/ppermute | solution.py:324
  8.1 1.6 %collective-permute-start.6 = (bf16[2,1,40,2048]{3,2,1,0:T(8,128)(2,1)S(1)}, bf16[2,1,40,2048]{3,2,1,0:T(8,128)(2,1)S(1)}, u32[]{:S(2)}, u32[]{:S(2)}) collective-permute-start(bf16[2,1,40,2048]{3,2,1,0:T(8,128)(2,1)S(1)} %get-tuple-element.103.refs_0_), channel_id=1, source_target_pairs={{0,2},{1,3},{2,0},{3,1},{4,6},{5,7},{6,4},{7,5},{8,10},{9,11},{10,... | collective-permute-start | bytes 983048 | tf_op jit(solution)/shard_map/ppermute | solution.py:354
  10.4 1.6 collective-permute-start.2
  12.1 3.8 %masked.4 = (bf16[2048,1792]{1,0:T(8,128)(2,1)S(1)}, f32[8,128]{1,0:T(8,128)S(1)}) custom-call(s32[2]{0:T(128)S(1)} %pad_add_fusion.core_ref.place_ref, bf16[2048,1792]{1,0:T(8,128)(2,1)} %weight_ref.4, s32[32,28]{1,0:T(8,128)S(1)} %copy-done.1, f32[8,128]{1,0:T(8,128)S(1)} %get-tuple-element.104.refs_0_), custom_call_target="tpu_custom_call" | custom-call | tf_op jit(solution)/shard_map/masked/pallas_call | solution.py:81
  16.1 4.2 %collective-permute-start.7 = (bf16[2,1,40,2048]{3,2,1,0:T(8,128)(2,1)S(1)}, bf16[2,1,40,2048]{3,2,1,0:T(8,128)(2,1)S(1)}, u32[]{:S(2)}, u32[]{:S(2)}) collective-permute-start(bf16[2,1,40,2048]{3,2,1,0:T(8,128)(2,1)S(1)} %collective-permute-done.1.refs_1_), channel_id=1, source_target_pairs={{0,2},{1,3},{2,0},{3,1},{4,6},{5,7},{6,4},{7,5},{8,10},{9,11},{10,... | collective-permute-start | bytes 983048 | tf_op jit(solution)/shard_map/ppermute | solution.py:354
  21.6 3.8 %masked.5 = (bf16[2048,1792]{1,0:T(8,128)(2,1)S(1)}, f32[8,128]{1,0:T(8,128)S(1)}) custom-call(s32[2]{0:T(128)S(1)} %pad_add_fusion.core_ref.place_ref, bf16[2048,1792]{1,0:T(8,128)(2,1)} %weight_ref.5, s32[32,28]{1,0:T(8,128)S(1)} %copy-done.2, f32[8,128]{1,0:T(8,128)S(1)} %get-tuple-element.108.refs_0_, ...), custom_call_target="tpu_custom_call" | custom-call | flops 172500000 | tf_op jit(solution)/shard_map/masked/pallas_call | solution.py:81
  25.5 1.7 %collective-permute-done.7.refs_1_ = bf16[2,1,40,2048]{3,2,1,0:T(8,128)(2,1)S(1)} collective-permute-done((bf16[2,1,40,2048]{3,2,1,0:T(8,128)(2,1)S(1)}, bf16[2,1,40,2048]{3,2,1,0:T(8,128)(2,1)S(1)}, u32[]{:S(2)}, u32[]{:S(2)}) %collective-permute-start.7) | collective-permute-done | bytes 327712 | tf_op jit(solution)/shard_map/ppermute | solution.py:354
  27.3 2.2 %collective-permute-done.3.refs_3_.refs_1_ = bf16[2,1,40,2048]{3,2,1,0:T(8,128)(2,1)S(1)} collective-permute-done((bf16[2,1,40,2048]{3,2,1,0:T(8,128)(2,1)S(1)}, bf16[2,1,40,2048]{3,2,1,0:T(8,128)(2,1)S(1)}, u32[]{:S(2)}, u32[]{:S(2)}) %collective-permute-start.3) | collective-permute-done | bytes 327712 | tf_op jit(solution)/shard_map/ppermute | solution.py:324
  29.5 3.1 %collective-permute-start.10 = (bf16[160,2048]{1,0:T(8,128)(2,1)S(1)}, bf16[160,2048]{1,0:T(8,128)(2,1)S(1)}, u32[]{:S(2)}, u32[]{:S(2)}) collective-permute-start(bf16[160,2048]{1,0:T(8,128)(2,1)S(1)} %get-tuple-element.120.refs_0_.mine_ref), channel_id=1, source_target_pairs={{0,6},{1,7},{6,0},{7,1},{8,14},{9,15},{14,8},{15,9},{16,22},{17,23... | collective-permute-start | bytes 1966088 | tf_op jit(solution)/shard_map/ppermute | solution.py:354
  33.4 6.1 %gate_up.4 = (bf16[2,2,2,40,1792]{4,3,2,1,0:T(8,128)(2,1)S(1)}, bf16[2,2,40,1792]{3,2,1,0:T(8,128)(2,1)S(1)}, bf16[2,2,1,40,1792]{4,3,2,1,0:T(8,128)(2,1)S(1)}, f32[8,128]{1,0:T(8,128)S(1)}) custom-call(bf16[160,2048]{1,0:T(8,128)(2,1)S(1)} %get-tuple-element.120.refs_0_.mine_ref, bf16[160,2048]{1,0:T(8,128)(2,1)S(1)} %get-tuple-element.112.refs_1_, ...), custom_call_target="tpu_custom_call" | custom-call | tf_op jit(solution)/shard_map/gate_up/pallas_call | solution.py:206
  40.1 3.9 %masked.6 = (bf16[1792,2048]{1,0:T(8,128)(2,1)S(1)}, f32[8,128]{1,0:T(8,128)S(1)}) custom-call(s32[2]{0:T(128)S(1)} %pad_add_fusion.core_ref.place_ref, bf16[1792,8192]{1,0:T(8,128)(2,1)} %weight_ref.7, s32[28,128]{1,0:T(8,128)S(1)} %copy-done, f32[8,128]{1,0:T(8,128)S(1)} %get-tuple-element.121.refs_0_), custom_call_target="tpu_custom_call" | custom-call | tf_op jit(solution)/shard_map/masked/pallas_call | solution.py:81
  44.0 3.9 %masked.7 = (bf16[1792,2048]{1,0:T(8,128)(2,1)S(1)}, f32[8,128]{1,0:T(8,128)S(1)}) custom-call(s32[2]{0:T(128)S(1)} %pad_add_fusion.core_ref.place_ref, bf16[1792,8192]{1,0:T(8,128)(2,1)} %weight_ref.7, s32[28,128]{1,0:T(8,128)S(1)} %copy-done, f32[8,128]{1,0:T(8,128)S(1)} %get-tuple-element.122.refs_0_), custom_call_target="tpu_custom_call" | custom-call | tf_op jit(solution)/shard_map/masked/pallas_call | solution.py:81
  48.8 1.4 collective-permute-start.13
  50.4 6.1 %gate_up.5 = (bf16[2,2,2,40,1792]{4,3,2,1,0:T(8,128)(2,1)S(1)}, bf16[2,2,40,1792]{3,2,1,0:T(8,128)(2,1)S(1)}, bf16[2,2,1,40,1792]{4,3,2,1,0:T(8,128)(2,1)S(1)}, f32[8,128]{1,0:T(8,128)S(1)}) custom-call(bf16[160,2048]{1,0:T(8,128)(2,1)S(1)} %get-tuple-element.129.refs_0_, bf16[160,2048]{1,0:T(8,128)(2,1)S(1)} %collective-permute-done.12.refs_1_, ...), custom_call_target="tpu_custom_call" | custom-call | flops 4697620480 | tf_op jit(solution)/shard_map/gate_up/pallas_call | solution.py:206
  57.1 1.5 collective-permute-done.14.refs_1_
  58.6 0.8 collective-permute-done.15.refs_3_.refs_1_
  60.1 5.4 %collective-permute-done.13.refs_1_ = bf16[160,2048]{1,0:T(8,128)(2,1)S(1)} collective-permute-done((bf16[160,2048]{1,0:T(8,128)(2,1)S(1)}, bf16[160,2048]{1,0:T(8,128)(2,1)S(1)}, u32[]{:S(2)}, u32[]{:S(2)}) %collective-permute-start.13) | collective-permute-done | bytes 655392 | tf_op jit(solution)/shard_map/ppermute | solution.py:324
  65.5 1.0 collective-permute-done.11.refs_5_.refs_0_
  67.3 6.1 %gate_up.6 = (bf16[2,2,2,40,1792]{4,3,2,1,0:T(8,128)(2,1)S(1)}, bf16[2,2,40,1792]{3,2,1,0:T(8,128)(2,1)S(1)}, bf16[2,2,1,40,1792]{4,3,2,1,0:T(8,128)(2,1)S(1)}, f32[8,128]{1,0:T(8,128)S(1)}) custom-call(bf16[160,2048]{1,0:T(8,128)(2,1)S(1)} %get-tuple-element.131.refs_0_, bf16[160,2048]{1,0:T(8,128)(2,1)S(1)} %collective-permute-done.13.refs_1_, ...), custom_call_target="tpu_custom_call" | custom-call | flops 4697620480 | tf_op jit(solution)/shard_map/gate_up/pallas_call | solution.py:206
  76.4 1.5 collective-permute-start.23
  77.9 3.9 %down.4 = (bf16[2,40,4096]{2,1,0:T(8,128)(2,1)S(1)}, bf16[2,40,4096]{2,1,0:T(8,128)(2,1)S(1)}, f32[8,128]{1,0:T(8,128)S(1)}) custom-call(bf16[2,40,1792]{2,1,0:T(8,128)(2,1)S(1)} %get-tuple-element.140.own_ref, bf16[2,40,1792]{2,1,0:T(8,128)(2,1)S(1)} %collective-permute-done.18.other_ref, bf16[1792,2048]{1,0:T(8,128)(2,1)S(1)} %get-tuple-element.141.refs_0_, ...), custom_call_target="tpu_custom_call" | custom-call | flops 2348810 | tf_op jit(solution)/shard_map/down/pallas_call | solution.py:248
  82.9 6.1 %gate_up.7 = (bf16[2,2,2,40,1792]{4,3,2,1,0:T(8,128)(2,1)S(1)}, bf16[2,2,40,1792]{3,2,1,0:T(8,128)(2,1)S(1)}, bf16[1,2,1,40,1792]{4,3,2,1,0:T(8,128)(2,1)S(1)}, ...) custom-call(bf16[160,2048]{1,0:T(8,128)(2,1)S(1)} %collective-permute-done.11.refs_5_.refs_0_, ...), custom_call_target="tpu_custom_call" | custom-call | flops 4697620480 | tf_op jit(solution)/shard_map/gate_up/pallas_call | solution.py:206
  89.5 2.0 %collective-permute-done.23.refs_2_ = bf16[2,2,40,1792]{3,2,1,0:T(8,128)(2,1)S(1)} collective-permute-done((bf16[2,2,40,1792]{3,2,1,0:T(8,128)(2,1)S(1)}, bf16[2,2,40,1792]{3,2,1,0:T(8,128)(2,1)S(1)}, u32[]{:S(2)}, u32[]{:S(2)}) %collective-permute-start.23) | collective-permute-done | bytes 573472 | tf_op jit(solution)/shard_map/ppermute | solution.py:324
  92.6 1.4 collective-permute-start.24
  94.0 3.9 %down.5 = (bf16[1,40,4096]{2,1,0:T(8,128)(2,1)S(1)}, bf16[1,40,4096]{2,1,0:T(8,128)(2,1)S(1)}, bf16[1,40,4096]{2,1,0:T(8,128)(2,1)S(1)}, bf16[1,40,4096]{2,1,0:T(8,128)(2,1)S(1)}, f32[8,128]{1,0:T(8,128)S(1)}) custom-call(bf16[2,40,1792]{2,1,0:T(8,128)(2,1)S(1)} %get-tuple-element.160.own_ref, bf16[2,40,1792]{2,1,0:T(8,128)(2,1)S(1)} %collective-permute-done.27.other_ref, ...), custom_call_target="tpu_custom_call" | custom-call | flops 2348810 | tf_op jit(solution)/shard_map/down/pallas_call | solution.py:248
  99.0 1.4 collective-permute-start.32
  100.4 7.0 %collective-permute-done.29.refs_1_ = bf16[1,40,4096]{2,1,0:T(8,128)(2,1)S(1)} collective-permute-done((bf16[1,40,4096]{2,1,0:T(8,128)(2,1)S(1)}, bf16[1,40,4096]{2,1,0:T(8,128)(2,1)S(1)}, u32[]{:S(2)}, u32[]{:S(2)}) %collective-permute-start.29) | collective-permute-done | bytes 327712 | tf_op jit(solution)/shard_map/ppermute | solution.py:324
  107.5 1.1 collective-permute-start.31
  108.9 0.9 collective-permute-start.25
  109.8 1.5 collective-permute-start.34
  111.3 3.9 %down.6 = (bf16[1,40,4096]{2,1,0:T(8,128)(2,1)S(1)}, bf16[1,40,4096]{2,1,0:T(8,128)(2,1)S(1)}, bf16[1,40,4096]{2,1,0:T(8,128)(2,1)S(1)}, bf16[1,40,4096]{2,1,0:T(8,128)(2,1)S(1)}, f32[8,128]{1,0:T(8,128)S(1)}) custom-call(bf16[2,40,1792]{2,1,0:T(8,128)(2,1)S(1)} %get-tuple-element.170.own_ref, bf16[2,40,1792]{2,1,0:T(8,128)(2,1)S(1)} %collective-permute-done.30.other_ref, ...), custom_call_target="tpu_custom_call" | custom-call | flops 2348810 | tf_op jit(solution)/shard_map/down/pallas_call | solution.py:248
  115.2 1.6 collective-permute-done.32.refs_3_.refs_1_
  116.9 1.6 collective-permute-start.33
  118.4 1.3 collective-permute-start.38
  119.7 4.1 %collective-permute-done.34.refs_2_ = bf16[1,40,4096]{2,1,0:T(8,128)(2,1)S(1)} collective-permute-done((bf16[1,40,4096]{2,1,0:T(8,128)(2,1)S(1)}, bf16[1,40,4096]{2,1,0:T(8,128)(2,1)S(1)}, u32[]{:S(2)}, u32[]{:S(2)}) %collective-permute-start.34) | collective-permute-done | bytes 327712 | tf_op jit(solution)/shard_map/ppermute | solution.py:354
  123.8 1.1 collective-permute-done.33.refs_1_
  125.4 1.3 collective-permute-start.36
  126.6 1.3 collective-permute-start.40
  127.9 3.9 %down.7 = (bf16[2,40,4096]{2,1,0:T(8,128)(2,1)S(1)}, bf16[2,40,4096]{2,1,0:T(8,128)(2,1)S(1)}, f32[8,128]{1,0:T(8,128)S(1)}) custom-call(bf16[2,40,1792]{2,1,0:T(8,128)(2,1)S(1)} %get-tuple-element.184.own_ref, bf16[2,40,1792]{2,1,0:T(8,128)(2,1)S(1)} %collective-permute-done.35.other_ref, bf16[1792,2048]{1,0:T(8,128)(2,1)S(1)} %get-tuple-element.141.refs_0_, ...), custom_call_target="tpu_custom_call" | custom-call | flops 2348810 | tf_op jit(solution)/shard_map/down/pallas_call | solution.py:248
  131.9 3.6 %collective-permute-done.36.refs_1_ = bf16[1,40,4096]{2,1,0:T(8,128)(2,1)S(1)} collective-permute-done((bf16[1,40,4096]{2,1,0:T(8,128)(2,1)S(1)}, bf16[1,40,4096]{2,1,0:T(8,128)(2,1)S(1)}, u32[]{:S(2)}, u32[]{:S(2)}) %collective-permute-start.36) | collective-permute-done | bytes 327712 | tf_op jit(solution)/shard_map/ppermute | solution.py:324
  135.6 1.8 %collective-permute-start.39 = (bf16[1,40,4096]{2,1,0:T(8,128)(2,1)S(1)}, bf16[1,40,4096]{2,1,0:T(8,128)(2,1)S(1)}, u32[]{:S(2)}, u32[]{:S(2)}) collective-permute-start(bf16[1,40,4096]{2,1,0:T(8,128)(2,1)S(1)} %get-tuple-element.196), channel_id=1, source_target_pairs={{0,4},{1,5},{4,0},{5,1},{2,6},{3,7},{6,2},{7,3},{8,12},{9,13},{12,... | collective-permute-start | bytes 983048 | tf_op jit(solution)/shard_map/ppermute | solution.py:354
  138.1 13.6 %collective-permute-done.40.refs_0_ = bf16[1,40,4096]{2,1,0:T(8,128)(2,1)S(1)} collective-permute-done((bf16[1,40,4096]{2,1,0:T(8,128)(2,1)S(1)}, bf16[1,40,4096]{2,1,0:T(8,128)(2,1)S(1)}, u32[]{:S(2)}, u32[]{:S(2)}) %collective-permute-start.40) | collective-permute-done | bytes 327712 | tf_op jit(solution)/shard_map/ppermute | solution.py:354
  152.4 1.1 collective-permute-done.37
  153.6 4.8 %collective-permute-done.39 = bf16[1,40,4096]{2,1,0:T(8,128)(2,1)S(1)} collective-permute-done((bf16[1,40,4096]{2,1,0:T(8,128)(2,1)S(1)}, bf16[1,40,4096]{2,1,0:T(8,128)(2,1)S(1)}, u32[]{:S(2)}, u32[]{:S(2)}) %collective-permute-start.39) | collective-permute-done | bytes 327712 | tf_op jit(solution)/shard_map/ppermute | solution.py:354
  158.7 0.9 pad_maximum_fusion
  (88 shorter events, 18.0 us)
Async XLA Ops:
  2.7 9.3 %copy-start.1 = (s32[32,28]{1,0:T(8,128)S(1)}, s32[32,28]{1,0:T(8,128)}, u32[]{:S(2)}) copy-start(s32[32,28]{1,0:T(8,128)} %mask_ref.4) | copy-start | bytes 10756
  2.8 1.8 %collective-permute-start = (bf16[2,40,2048]{2,1,0:T(8,128)(2,1)S(1)}, bf16[2,40,2048]{2,1,0:T(8,128)(2,1)S(1)}, u32[]{:S(2)}, u32[]{:S(2)}) collective-permute-start(bf16[2,40,2048]{2,1,0:T(8,128)(2,1)S(1)} %pad_maximum_fusion.1), channel_id=1, source_target_pairs={{0,8},{8,0},{16,24},{24,16},{1,9},{9,1},{17,25},{25,17},{2,10},{10... | collective-permute-start | bytes 983048 | tf_op jit(solution)/shard_map/ppermute | solution.py:324
  5.2 10.9 %collective-permute-start.1 = (bf16[2,1,40,2048]{3,2,1,0:T(8,128)(2,1)S(1)}, bf16[2,1,40,2048]{3,2,1,0:T(8,128)(2,1)S(1)}, u32[]{:S(2)}, u32[]{:S(2)}) collective-permute-start(bf16[2,1,40,2048]{3,2,1,0:T(8,128)(2,1)S(1)} %get-tuple-element.102.refs_2_), channel_id=1, source_target_pairs={{0,16},{8,24},{16,0},{24,8},{1,17},{9,25},{17,1},{25,9},{2,18},{10... | collective-permute-start | bytes 983048 | tf_op jit(solution)/shard_map/ppermute | solution.py:324
  8.1 12.9 %collective-permute-start.6 = (bf16[2,1,40,2048]{3,2,1,0:T(8,128)(2,1)S(1)}, bf16[2,1,40,2048]{3,2,1,0:T(8,128)(2,1)S(1)}, u32[]{:S(2)}, u32[]{:S(2)}) collective-permute-start(bf16[2,1,40,2048]{3,2,1,0:T(8,128)(2,1)S(1)} %get-tuple-element.103.refs_0_), channel_id=1, source_target_pairs={{0,2},{1,3},{2,0},{3,1},{4,6},{5,7},{6,4},{7,5},{8,10},{9,11},{10,... | collective-permute-start | bytes 983048 | tf_op jit(solution)/shard_map/ppermute | solution.py:354
  9.7 15.7 %collective-permute-start.4 = (bf16[2,1,40,2048]{3,2,1,0:T(8,128)(2,1)S(1)}, bf16[2,1,40,2048]{3,2,1,0:T(8,128)(2,1)S(1)}, u32[]{:S(2)}, u32[]{:S(2)}) collective-permute-start(bf16[2,1,40,2048]{3,2,1,0:T(8,128)(2,1)S(1)} %get-tuple-element.103.refs_0_), channel_id=1, source_target_pairs={{2,4},{3,5},{4,2},{5,3},{10,12},{11,13},{12,10},{13,11},{18,20},{1... | collective-permute-start | bytes 983048 | tf_op jit(solution)/shard_map/ppermute | solution.py:354
  10.4 15.0 %collective-permute-start.2 = (bf16[2,1,40,2048]{3,2,1,0:T(8,128)(2,1)S(1)}, bf16[2,1,40,2048]{3,2,1,0:T(8,128)(2,1)S(1)}, u32[]{:S(2)}, u32[]{:S(2)}) collective-permute-start(bf16[2,1,40,2048]{3,2,1,0:T(8,128)(2,1)S(1)} %get-tuple-element.103.refs_0_), channel_id=1, source_target_pairs={{0,1},{1,0},{2,3},{3,2},{4,5},{5,4},{6,7},{7,6},{8,9},{9,8},{10,11... | collective-permute-start | bytes 983048 | tf_op jit(solution)/shard_map/ppermute | solution.py:324
  12.1 9.6 %copy-start.2 = (s32[32,28]{1,0:T(8,128)S(1)}, s32[32,28]{1,0:T(8,128)}, u32[]{:S(2)}) copy-start(s32[32,28]{1,0:T(8,128)} %mask_ref.5) | copy-start | bytes 10756
  16.1 11.1 %collective-permute-start.7 = (bf16[2,1,40,2048]{3,2,1,0:T(8,128)(2,1)S(1)}, bf16[2,1,40,2048]{3,2,1,0:T(8,128)(2,1)S(1)}, u32[]{:S(2)}, u32[]{:S(2)}) collective-permute-start(bf16[2,1,40,2048]{3,2,1,0:T(8,128)(2,1)S(1)} %collective-permute-done.1.refs_1_), channel_id=1, source_target_pairs={{0,2},{1,3},{2,0},{3,1},{4,6},{5,7},{6,4},{7,5},{8,10},{9,11},{10,... | collective-permute-start | bytes 983048 | tf_op jit(solution)/shard_map/ppermute | solution.py:354
  20.3 6.9 %collective-permute-start.5 = (bf16[2,1,40,2048]{3,2,1,0:T(8,128)(2,1)S(1)}, bf16[2,1,40,2048]{3,2,1,0:T(8,128)(2,1)S(1)}, u32[]{:S(2)}, u32[]{:S(2)}) collective-permute-start(bf16[2,1,40,2048]{3,2,1,0:T(8,128)(2,1)S(1)} %collective-permute-done.1.refs_1_), channel_id=1, source_target_pairs={{2,4},{3,5},{4,2},{5,3},{10,12},{11,13},{12,10},{13,11},{18,20},{1... | collective-permute-start | bytes 983048 | tf_op jit(solution)/shard_map/ppermute | solution.py:354
  21.0 8.4 %collective-permute-start.3 = (bf16[2,1,40,2048]{3,2,1,0:T(8,128)(2,1)S(1)}, bf16[2,1,40,2048]{3,2,1,0:T(8,128)(2,1)S(1)}, u32[]{:S(2)}, u32[]{:S(2)}) collective-permute-start(bf16[2,1,40,2048]{3,2,1,0:T(8,128)(2,1)S(1)} %collective-permute-done.1.refs_1_), channel_id=1, source_target_pairs={{0,1},{1,0},{2,3},{3,2},{4,5},{5,4},{6,7},{7,6},{8,9},{9,8},{10,11... | collective-permute-start | bytes 983048 | tf_op jit(solution)/shard_map/ppermute | solution.py:324
  29.5 18.5 %collective-permute-start.10 = (bf16[160,2048]{1,0:T(8,128)(2,1)S(1)}, bf16[160,2048]{1,0:T(8,128)(2,1)S(1)}, u32[]{:S(2)}, u32[]{:S(2)}) collective-permute-start(bf16[160,2048]{1,0:T(8,128)(2,1)S(1)} %get-tuple-element.120.refs_0_.mine_ref), channel_id=1, source_target_pairs={{0,6},{1,7},{6,0},{7,1},{8,14},{9,15},{14,8},{15,9},{16,22},{17,23... | collective-permute-start | bytes 1966088 | tf_op jit(solution)/shard_map/ppermute | solution.py:354
  32.6 16.1 %collective-permute-start.12 = (bf16[160,2048]{1,0:T(8,128)(2,1)S(1)}, bf16[160,2048]{1,0:T(8,128)(2,1)S(1)}, u32[]{:S(2)}, u32[]{:S(2)}) collective-permute-start(bf16[160,2048]{1,0:T(8,128)(2,1)S(1)} %get-tuple-element.129.refs_0_), channel_id=1, source_target_pairs={{0,1},{1,0},{2,3},{3,2},{4,5},{5,4},{6,7},{7,6},{8,9},{9,8},{10,11... | collective-permute-start | bytes 1966088 | tf_op jit(solution)/shard_map/ppermute | solution.py:324
  33.4 6.7 %copy-start = (s32[28,128]{1,0:T(8,128)S(1)}, s32[28,128]{1,0:T(8,128)}, u32[]{:S(2)}) copy-start(s32[28,128]{1,0:T(8,128)} %mask_ref.7) | copy-start | bytes 43012
  39.5 9.1 %collective-permute-start.8 = (bf16[2,2,40,1792]{3,2,1,0:T(8,128)(2,1)S(1)}, bf16[2,2,40,1792]{3,2,1,0:T(8,128)(2,1)S(1)}, u32[]{:S(2)}, u32[]{:S(2)}) collective-permute-start(bf16[2,2,40,1792]{3,2,1,0:T(8,128)(2,1)S(1)} %get-tuple-element.117), channel_id=1, source_target_pairs={{0,8},{8,0},{16,24},{24,16},{1,9},{9,1},{17,25},{25,17},{2,10},{10... | collective-permute-start | bytes 1720328 | tf_op jit(solution)/shard_map/ppermute | solution.py:324
  39.6 9.0 %collective-permute-start.9 = (bf16[2,2,1,40,1792]{4,3,2,1,0:T(8,128)(2,1)S(1)}, bf16[2,2,1,40,1792]{4,3,2,1,0:T(8,128)(2,1)S(1)}, u32[]{:S(2)}, u32[]{:S(2)}) collective-permute-start(bf16[2,2,1,40,1792]{4,3,2,1,0:T(8,128)(2,1)S(1)} %get-tuple-element.118), channel_id=1, source_target_pairs={{0,8},{8,0},{16,24},{24,16},{1,9},{9,1},{17,25},{25,17},{2,10},{10... | collective-permute-start | bytes 1720328 | tf_op jit(solution)/shard_map/ppermute | solution.py:324
  48.8 16.8 %collective-permute-start.13 = (bf16[160,2048]{1,0:T(8,128)(2,1)S(1)}, bf16[160,2048]{1,0:T(8,128)(2,1)S(1)}, u32[]{:S(2)}, u32[]{:S(2)}) collective-permute-start(bf16[160,2048]{1,0:T(8,128)(2,1)S(1)} %get-tuple-element.131.refs_0_), channel_id=1, source_target_pairs={{0,1},{1,0},{2,3},{3,2},{4,5},{5,4},{6,7},{7,6},{8,9},{9,8},{10,11... | collective-permute-start | bytes 1966088 | tf_op jit(solution)/shard_map/ppermute | solution.py:324
  50.1 16.4 %collective-permute-start.11 = (bf16[160,2048]{1,0:T(8,128)(2,1)S(1)}, bf16[160,2048]{1,0:T(8,128)(2,1)S(1)}, u32[]{:S(2)}, u32[]{:S(2)}) collective-permute-start(bf16[160,2048]{1,0:T(8,128)(2,1)S(1)} %get-tuple-element.126), channel_id=1, source_target_pairs={{0,4},{1,5},{4,6},{5,7},{6,2},{7,3},{2,0},{3,1},{8,12},{9,13},{12,... | collective-permute-start | bytes 1966088 | tf_op jit(solution)/shard_map/ppermute | solution.py:354
  56.5 2.0 %collective-permute-start.14 = (bf16[2,2,1,40,1792]{4,3,2,1,0:T(8,128)(2,1)S(1)}, bf16[2,2,1,40,1792]{4,3,2,1,0:T(8,128)(2,1)S(1)}, u32[]{:S(2)}, u32[]{:S(2)}) collective-permute-start(bf16[2,2,1,40,1792]{4,3,2,1,0:T(8,128)(2,1)S(1)} %get-tuple-element.133), channel_id=1, source_target_pairs={{0,8},{8,0},{16,24},{24,16},{1,9},{9,1},{17,25},{25,17},{2,10},{10... | collective-permute-start | bytes 1720328 | tf_op jit(solution)/shard_map/ppermute | solution.py:324
  56.6 2.8 %collective-permute-start.15 = (bf16[2,2,40,1792]{3,2,1,0:T(8,128)(2,1)S(1)}, bf16[2,2,40,1792]{3,2,1,0:T(8,128)(2,1)S(1)}, u32[]{:S(2)}, u32[]{:S(2)}) collective-permute-start(bf16[2,2,40,1792]{3,2,1,0:T(8,128)(2,1)S(1)} %get-tuple-element.135), channel_id=1, source_target_pairs={{0,8},{8,0},{16,24},{24,16},{1,9},{9,1},{17,25},{25,17},{2,10},{10... | collective-permute-start | bytes 1720328 | tf_op jit(solution)/shard_map/ppermute | solution.py:324
  59.5 15.1 %collective-permute-start.17 = (bf16[2,2,40,1792]{3,2,1,0:T(8,128)(2,1)S(1)}, bf16[2,2,40,1792]{3,2,1,0:T(8,128)(2,1)S(1)}, u32[]{:S(2)}, u32[]{:S(2)}) collective-permute-start(bf16[2,2,40,1792]{3,2,1,0:T(8,128)(2,1)S(1)} %get-tuple-element.138), channel_id=1, source_target_pairs={{0,16},{8,24},{16,0},{24,8},{1,17},{9,25},{17,1},{25,9},{2,18},{10... | collective-permute-start | bytes 1720328 | tf_op jit(solution)/shard_map/ppermute | solution.py:324
  66.6 15.6 %collective-permute-start.16 = (bf16[160,2048]{1,0:T(8,128)(2,1)S(1)}, bf16[160,2048]{1,0:T(8,128)(2,1)S(1)}, u32[]{:S(2)}, u32[]{:S(2)}) collective-permute-start(bf16[160,2048]{1,0:T(8,128)(2,1)S(1)} %collective-permute-done.11.refs_5_.refs_0_), channel_id=1, source_target_pairs={{0,1},{1,0},{2,3},{3,2},{4,5},{5,4},{6,7},{7,6},{8,9},{9,8},{10,11... | collective-permute-start | bytes 1966088 | tf_op jit(solution)/shard_map/ppermute | solution.py:324
  73.4 2.0 %collective-permute-start.19 = (bf16[2,2,1,40,1792]{4,3,2,1,0:T(8,128)(2,1)S(1)}, bf16[2,2,1,40,1792]{4,3,2,1,0:T(8,128)(2,1)S(1)}, u32[]{:S(2)}, u32[]{:S(2)}) collective-permute-start(bf16[2,2,1,40,1792]{4,3,2,1,0:T(8,128)(2,1)S(1)} %get-tuple-element.144), channel_id=1, source_target_pairs={{0,8},{8,0},{16,24},{24,16},{1,9},{9,1},{17,25},{25,17},{2,10},{10... | collective-permute-start | bytes 1720328 | tf_op jit(solution)/shard_map/ppermute | solution.py:324
  73.5 2.8 %collective-permute-start.20 = (bf16[2,2,40,1792]{3,2,1,0:T(8,128)(2,1)S(1)}, bf16[2,2,40,1792]{3,2,1,0:T(8,128)(2,1)S(1)}, u32[]{:S(2)}, u32[]{:S(2)}) collective-permute-start(bf16[2,2,40,1792]{3,2,1,0:T(8,128)(2,1)S(1)} %get-tuple-element.146), channel_id=1, source_target_pairs={{0,8},{8,0},{16,24},{24,16},{1,9},{9,1},{17,25},{25,17},{2,10},{10... | collective-permute-start | bytes 1720328 | tf_op jit(solution)/shard_map/ppermute | solution.py:324
  74.9 3.0 %collective-permute-start.18 = (bf16[2,40,1792]{2,1,0:T(8,128)(2,1)S(1)}, bf16[2,40,1792]{2,1,0:T(8,128)(2,1)S(1)}, u32[]{:S(2)}, u32[]{:S(2)}) collective-permute-start(bf16[2,40,1792]{2,1,0:T(8,128)(2,1)S(1)} %get-tuple-element.140.own_ref), channel_id=1, source_target_pairs={{0,8},{8,0},{16,24},{24,16},{1,9},{9,1},{17,25},{25,17},{2,10},{10... | collective-permute-start | bytes 860168 | tf_op jit(solution)/shard_map/ppermute | solution.py:324
  76.4 15.1 %collective-permute-start.23 = (bf16[2,2,40,1792]{3,2,1,0:T(8,128)(2,1)S(1)}, bf16[2,2,40,1792]{3,2,1,0:T(8,128)(2,1)S(1)}, u32[]{:S(2)}, u32[]{:S(2)}) collective-permute-start(bf16[2,2,40,1792]{3,2,1,0:T(8,128)(2,1)S(1)} %get-tuple-element.152), channel_id=1, source_target_pairs={{0,16},{8,24},{16,0},{24,8},{1,17},{9,25},{17,1},{25,9},{2,18},{10... | collective-permute-start | bytes 1720328 | tf_op jit(solution)/shard_map/ppermute | solution.py:324
  82.1 16.2 %collective-permute-start.28 = (bf16[2,40,4096]{2,1,0:T(8,128)(2,1)S(1)}, bf16[2,40,4096]{2,1,0:T(8,128)(2,1)S(1)}, u32[]{:S(2)}, u32[]{:S(2)}) collective-permute-start(bf16[2,40,4096]{2,1,0:T(8,128)(2,1)S(1)} %get-tuple-element.164), channel_id=1, source_target_pairs={{0,1},{1,0},{2,3},{3,2},{4,5},{5,4},{6,7},{7,6},{8,9},{9,8},{10,11... | collective-permute-start | bytes 1966088 | tf_op jit(solution)/shard_map/ppermute | solution.py:324
  88.9 2.9 %collective-permute-start.21 = (bf16[1,2,1,40,1792]{4,3,2,1,0:T(8,128)(2,1)S(1)}, bf16[1,2,1,40,1792]{4,3,2,1,0:T(8,128)(2,1)S(1)}, u32[]{:S(2)}, u32[]{:S(2)}) collective-permute-start(bf16[1,2,1,40,1792]{4,3,2,1,0:T(8,128)(2,1)S(1)} %get-tuple-element.150), channel_id=1, source_target_pairs={{0,8},{8,0},{16,24},{24,16},{1,9},{9,1},{17,25},{25,17},{2,10},{10... | collective-permute-start | bytes 860168 | tf_op jit(solution)/shard_map/ppermute | solution.py:324
  89.0 2.8 %collective-permute-start.22 = (bf16[1,2,1,40,1792]{4,3,2,1,0:T(8,128)(2,1)S(1)}, bf16[1,2,1,40,1792]{4,3,2,1,0:T(8,128)(2,1)S(1)}, u32[]{:S(2)}, u32[]{:S(2)}) collective-permute-start(bf16[1,2,1,40,1792]{4,3,2,1,0:T(8,128)(2,1)S(1)} %get-tuple-element.151), channel_id=1, source_target_pairs={{0,8},{8,0},{16,24},{24,16},{1,9},{9,1},{17,25},{25,17},{2,10},{10... | collective-permute-start | bytes 860168 | tf_op jit(solution)/shard_map/ppermute | solution.py:324
  91.8 2.2 %collective-permute-start.27 = (bf16[2,40,1792]{2,1,0:T(8,128)(2,1)S(1)}, bf16[2,40,1792]{2,1,0:T(8,128)(2,1)S(1)}, u32[]{:S(2)}, u32[]{:S(2)}) collective-permute-start(bf16[2,40,1792]{2,1,0:T(8,128)(2,1)S(1)} %get-tuple-element.160.own_ref), channel_id=1, source_target_pairs={{0,8},{8,0},{16,24},{24,16},{1,9},{9,1},{17,25},{25,17},{2,10},{10... | collective-permute-start | bytes 860168 | tf_op jit(solution)/shard_map/ppermute | solution.py:324
  92.0 16.5 %collective-permute-start.26 = (bf16[2,2,40,1792]{3,2,1,0:T(8,128)(2,1)S(1)}, bf16[2,2,40,1792]{3,2,1,0:T(8,128)(2,1)S(1)}, u32[]{:S(2)}, u32[]{:S(2)}) collective-permute-start(bf16[2,2,40,1792]{3,2,1,0:T(8,128)(2,1)S(1)} %get-tuple-element.159), channel_id=1, source_target_pairs={{0,8},{8,0},{16,24},{24,16},{1,9},{9,1},{17,25},{25,17},{2,10},{10... | collective-permute-start | bytes 1720328 | tf_op jit(solution)/shard_map/ppermute | solution.py:324
  92.6 16.0 %collective-permute-start.24 = (bf16[2,2,40,1792]{3,2,1,0:T(8,128)(2,1)S(1)}, bf16[2,2,40,1792]{3,2,1,0:T(8,128)(2,1)S(1)}, u32[]{:S(2)}, u32[]{:S(2)}) collective-permute-start(bf16[2,2,40,1792]{3,2,1,0:T(8,128)(2,1)S(1)} %get-tuple-element.155), channel_id=1, source_target_pairs={{0,16},{8,24},{16,0},{24,8},{1,17},{9,25},{17,1},{25,9},{2,18},{10... | collective-permute-start | bytes 1720328 | tf_op jit(solution)/shard_map/ppermute | solution.py:324
  98.4 9.0 %collective-permute-start.29 = (bf16[1,40,4096]{2,1,0:T(8,128)(2,1)S(1)}, bf16[1,40,4096]{2,1,0:T(8,128)(2,1)S(1)}, u32[]{:S(2)}, u32[]{:S(2)}) collective-permute-start(bf16[1,40,4096]{2,1,0:T(8,128)(2,1)S(1)} %get-tuple-element.165), channel_id=1, source_target_pairs={{0,1},{1,0},{2,3},{3,2},{4,5},{5,4},{6,7},{7,6},{8,9},{9,8},{10,11... | collective-permute-start | bytes 983048 | tf_op jit(solution)/shard_map/ppermute | solution.py:324
  99.0 17.7 %collective-permute-start.32 = (bf16[2,40,4096]{2,1,0:T(8,128)(2,1)S(1)}, bf16[2,40,4096]{2,1,0:T(8,128)(2,1)S(1)}, u32[]{:S(2)}, u32[]{:S(2)}) collective-permute-start(bf16[2,40,4096]{2,1,0:T(8,128)(2,1)S(1)} %get-tuple-element.179), channel_id=1, source_target_pairs={{0,2},{1,3},{2,0},{3,1},{4,6},{5,7},{6,4},{7,5},{8,10},{9,11},{10,... | collective-permute-start | bytes 1966088 | tf_op jit(solution)/shard_map/ppermute | solution.py:354
  107.5 9.3 %collective-permute-start.31 = (bf16[1,40,4096]{2,1,0:T(8,128)(2,1)S(1)}, bf16[1,40,4096]{2,1,0:T(8,128)(2,1)S(1)}, u32[]{:S(2)}, u32[]{:S(2)}) collective-permute-start(bf16[1,40,4096]{2,1,0:T(8,128)(2,1)S(1)} %get-tuple-element.177), channel_id=1, source_target_pairs={{0,1},{1,0},{2,3},{3,2},{4,5},{5,4},{6,7},{7,6},{8,9},{9,8},{10,11... | collective-permute-start | bytes 983048 | tf_op jit(solution)/shard_map/ppermute | solution.py:324
  108.8 2.5 %collective-permute-start.30 = (bf16[2,40,1792]{2,1,0:T(8,128)(2,1)S(1)}, bf16[2,40,1792]{2,1,0:T(8,128)(2,1)S(1)}, u32[]{:S(2)}, u32[]{:S(2)}) collective-permute-start(bf16[2,40,1792]{2,1,0:T(8,128)(2,1)S(1)} %get-tuple-element.170.own_ref), channel_id=1, source_target_pairs={{0,8},{8,0},{16,24},{24,16},{1,9},{9,1},{17,25},{25,17},{2,10},{10... | collective-permute-start | bytes 860168 | tf_op jit(solution)/shard_map/ppermute | solution.py:324
  108.9 16.1 %collective-permute-start.25 = (bf16[2,2,40,1792]{3,2,1,0:T(8,128)(2,1)S(1)}, bf16[2,2,40,1792]{3,2,1,0:T(8,128)(2,1)S(1)}, u32[]{:S(2)}, u32[]{:S(2)}) collective-permute-start(bf16[2,2,40,1792]{3,2,1,0:T(8,128)(2,1)S(1)} %get-tuple-element.156), channel_id=1, source_target_pairs={{0,16},{8,24},{16,0},{24,8},{1,17},{9,25},{17,1},{25,9},{2,18},{10... | collective-permute-start | bytes 1720328 | tf_op jit(solution)/shard_map/ppermute | solution.py:324
  109.8 13.9 %collective-permute-start.34 = (bf16[1,40,4096]{2,1,0:T(8,128)(2,1)S(1)}, bf16[1,40,4096]{2,1,0:T(8,128)(2,1)S(1)}, u32[]{:S(2)}, u32[]{:S(2)}) collective-permute-start(bf16[1,40,4096]{2,1,0:T(8,128)(2,1)S(1)} %get-tuple-element.176), channel_id=1, source_target_pairs={{0,2},{1,3},{2,0},{3,1},{4,6},{5,7},{6,4},{7,5},{8,10},{9,11},{10,... | collective-permute-start | bytes 983048 | tf_op jit(solution)/shard_map/ppermute | solution.py:354
  116.9 8.0 %collective-permute-start.33 = (bf16[1,40,4096]{2,1,0:T(8,128)(2,1)S(1)}, bf16[1,40,4096]{2,1,0:T(8,128)(2,1)S(1)}, u32[]{:S(2)}, u32[]{:S(2)}) collective-permute-start(bf16[1,40,4096]{2,1,0:T(8,128)(2,1)S(1)} %get-tuple-element.181), channel_id=1, source_target_pairs={{0,1},{1,0},{2,3},{3,2},{4,5},{5,4},{6,7},{7,6},{8,9},{9,8},{10,11... | collective-permute-start | bytes 983048 | tf_op jit(solution)/shard_map/ppermute | solution.py:324
  118.4 13.4 %collective-permute-start.38 = (bf16[1,40,4096]{2,1,0:T(8,128)(2,1)S(1)}, bf16[1,40,4096]{2,1,0:T(8,128)(2,1)S(1)}, u32[]{:S(2)}, u32[]{:S(2)}) collective-permute-start(bf16[1,40,4096]{2,1,0:T(8,128)(2,1)S(1)} %get-tuple-element.180), channel_id=1, source_target_pairs={{0,2},{1,3},{2,0},{3,1},{4,6},{5,7},{6,4},{7,5},{8,10},{9,11},{10,... | collective-permute-start | bytes 983048 | tf_op jit(solution)/shard_map/ppermute | solution.py:354
  125.3 2.6 %collective-permute-start.35 = (bf16[2,40,1792]{2,1,0:T(8,128)(2,1)S(1)}, bf16[2,40,1792]{2,1,0:T(8,128)(2,1)S(1)}, u32[]{:S(2)}, u32[]{:S(2)}) collective-permute-start(bf16[2,40,1792]{2,1,0:T(8,128)(2,1)S(1)} %get-tuple-element.184.own_ref), channel_id=1, source_target_pairs={{0,8},{8,0},{16,24},{24,16},{1,9},{9,1},{17,25},{25,17},{2,10},{10... | collective-permute-start | bytes 860168 | tf_op jit(solution)/shard_map/ppermute | solution.py:324
  125.4 10.1 %collective-permute-start.36 = (bf16[1,40,4096]{2,1,0:T(8,128)(2,1)S(1)}, bf16[1,40,4096]{2,1,0:T(8,128)(2,1)S(1)}, u32[]{:S(2)}, u32[]{:S(2)}) collective-permute-start(bf16[1,40,4096]{2,1,0:T(8,128)(2,1)S(1)} %get-tuple-element.190), channel_id=1, source_target_pairs={{0,1},{1,0},{2,3},{3,2},{4,5},{5,4},{6,7},{7,6},{8,9},{9,8},{10,11... | collective-permute-start | bytes 983048 | tf_op jit(solution)/shard_map/ppermute | solution.py:324
  126.6 25.1 %collective-permute-start.40 = (bf16[1,40,4096]{2,1,0:T(8,128)(2,1)S(1)}, bf16[1,40,4096]{2,1,0:T(8,128)(2,1)S(1)}, u32[]{:S(2)}, u32[]{:S(2)}) collective-permute-start(bf16[1,40,4096]{2,1,0:T(8,128)(2,1)S(1)} %get-tuple-element.189), channel_id=1, source_target_pairs={{0,4},{1,5},{4,0},{5,1},{2,6},{3,7},{6,2},{7,3},{8,12},{9,13},{12,... | collective-permute-start | bytes 983048 | tf_op jit(solution)/shard_map/ppermute | solution.py:354
  135.6 22.8 %collective-permute-start.39 = (bf16[1,40,4096]{2,1,0:T(8,128)(2,1)S(1)}, bf16[1,40,4096]{2,1,0:T(8,128)(2,1)S(1)}, u32[]{:S(2)}, u32[]{:S(2)}) collective-permute-start(bf16[1,40,4096]{2,1,0:T(8,128)(2,1)S(1)} %get-tuple-element.196), channel_id=1, source_target_pairs={{0,4},{1,5},{4,0},{5,1},{2,6},{3,7},{6,2},{7,3},{8,12},{9,13},{12,... | collective-permute-start | bytes 983048 | tf_op jit(solution)/shard_map/ppermute | solution.py:354
  137.4 16.0 %collective-permute-start.37 = (bf16[2,40,4096]{2,1,0:T(8,128)(2,1)S(1)}, bf16[2,40,4096]{2,1,0:T(8,128)(2,1)S(1)}, u32[]{:S(2)}, u32[]{:S(2)}) collective-permute-start(bf16[2,40,4096]{2,1,0:T(8,128)(2,1)S(1)} %get-tuple-element.191), channel_id=1, source_target_pairs={{0,1},{1,0},{2,3},{3,2},{4,5},{5,4},{6,7},{7,6},{8,9},{9,8},{10,11... | collective-permute-start | bytes 1966088 | tf_op jit(solution)/shard_map/ppermute | solution.py:324
  153.5 4.8 %collective-permute-start.41 = (bf16[40,4096]{1,0:T(8,128)(2,1)S(1)}, bf16[40,4096]{1,0:T(8,128)(2,1)S(1)}, u32[]{:S(2)}, u32[]{:S(2)}) collective-permute-start(bf16[40,4096]{1,0:T(8,128)(2,1)S(1)} %fusion.4), channel_id=1, source_target_pairs={{0,8},{8,0},{16,24},{24,16},{1,9},{9,1},{17,25},{25,17},{2,10},{10... | collective-permute-start | bytes 983048 | tf_op jit(solution)/shard_map/ppermute | solution.py:324

commit v16 on v15

--- a/solution.py
+++ b/solution.py
@@ -343,7 +343,6 @@
     gate_kept, token = masked(gate_weight, gate_mask, tile_of(features, 256), place, 1, lambda core: 0, [token])
     second = [swap(part, "rows", row_count, (chip + 1) * CORES) for chip, part in enumerate(to_chips_rows)]
     second = jnp.concatenate(second, 1) if len(second) > 1 else second[0]
-    second = lax.optimization_barrier((second, token))[0]
     mine, token = join([first, second], [token])
 
     def behind(values, after):
@@ -444,7 +443,7 @@
     exchange_near(1)
     to_chips(1, [near[1]])
     send_chips(1)
-    forward(2, two_away, [*parts[3][1:], *last])
+    forward(2, two_away, last)
     multiply_in(3, after=[two_away])
     exchange(3)
     exchange_near(3)

time: 160 us -> 160 us (level)
    ppermute x31, waiting for transfers between devices: 28.7 us -> 24 us  [swap(): lax.ppermute(values, axis, [(place, place ^ step) for place in range(size)])]
    ppermute x11, waiting for transfers between devices: 26.8 us -> 31.3 us  [by_plane(): return lax.ppermute(behind(values, after), 'cols', pairs)]
    ppermute x31, starting transfers between devices: 22 us -> 24.6 us  [swap(): lax.ppermute(values, axis, [(place, place ^ step) for place in range(size)])]
    ppermute x11, starting transfers between devices: 17.9 us -> 15.5 us  [by_plane(): return lax.ppermute(behind(values, after), 'cols', pairs)]
  transfers between devices with their start and end apart: 42 -> 42, of which waited for: 22 -> 19; matrix products, arithmetic and copies ran while one was open for 0% -> 0% of each run, Pallas kernels for 37% -> 37%
where the time goes in v16:
time: 160 us
  Pallas kernels  59.6 us (37%)
  waiting for transfers between devices  55.3 us (35%)
  starting transfers between devices  40 us (25%)
  other arithmetic  4 us (2%)
    ppermute x11, waiting for transfers between devices, by_plane(): return lax.ppermute(behind(values, after), 'cols', pairs)  31.3 us
    ppermute x31, starting transfers between devices, swap(): lax.ppermute(values, axis, [(place, place ^ step) for place in range(size)])  24.6 us
    pallas_call x4, Pallas kernels, gate_up(): pl.pallas_call(functools.partial(gate_up_kernel, len(parts), len(after)),...  24.3 us
    ppermute x31, waiting for transfers between devices, swap(): lax.ppermute(values, axis, [(place, place ^ step) for place in range(size)])  24 us
    pallas_call x4, Pallas kernels, down(): pl.pallas_call(functools.partial(down_kernel, pieces, len(down_kept), len...  15.5 us
    ppermute x11, starting transfers between devices, by_plane(): return lax.ppermute(behind(values, after), 'cols', pairs)  15.5 us
    pallas_call x4, Pallas kernels, masked(): pl.pallas_call(functools.partial(mask_kernel, share, rows, len(after)), i...  15.4 us
  transfers between devices with their start and end apart: 42, of which 19 were waited for; matrix products, arithmetic and copies ran while one was open for 0% of the time, Pallas kernels for 37%

profile of v16, /device:TPU:0, one launch (start us, length us, event | category | flops | bytes accessed | tf_op | source)
XLA Modules:
  0.0 159.5 jit_solution(5749982551562832392)
XLA Ops:
  0.0 1.3 fusion
  1.3 1.3 fusion.2
  3.3 1.3 collective-permute-done
  5.2 2.9 %collective-permute-start.1 = (bf16[2,1,40,2048]{3,2,1,0:T(8,128)(2,1)S(1)}, bf16[2,1,40,2048]{3,2,1,0:T(8,128)(2,1)S(1)}, u32[]{:S(2)}, u32[]{:S(2)}) collective-permute-start(bf16[2,1,40,2048]{3,2,1,0:T(8,128)(2,1)S(1)} %get-tuple-element.101.refs_2_), channel_id=1, source_target_pairs={{0,16},{8,24},{16,0},{24,8},{1,17},{9,25},{17,1},{25,9},{2,18},{10... | collective-permute-start | bytes 983048 | tf_op jit(solution)/shard_map/ppermute | solution.py:324
  8.1 1.6 %collective-permute-start.6 = (bf16[2,1,40,2048]{3,2,1,0:T(8,128)(2,1)S(1)}, bf16[2,1,40,2048]{3,2,1,0:T(8,128)(2,1)S(1)}, u32[]{:S(2)}, u32[]{:S(2)}) collective-permute-start(bf16[2,1,40,2048]{3,2,1,0:T(8,128)(2,1)S(1)} %get-tuple-element.102.refs_0_), channel_id=1, source_target_pairs={{0,2},{1,3},{2,0},{3,1},{4,6},{5,7},{6,4},{7,5},{8,10},{9,11},{10,... | collective-permute-start | bytes 983048 | tf_op jit(solution)/shard_map/ppermute | solution.py:353
  10.4 1.6 collective-permute-start.2
  12.0 4.1 %collective-permute-done.1.refs_1_ = bf16[2,1,40,2048]{3,2,1,0:T(8,128)(2,1)S(1)} collective-permute-done((bf16[2,1,40,2048]{3,2,1,0:T(8,128)(2,1)S(1)}, bf16[2,1,40,2048]{3,2,1,0:T(8,128)(2,1)S(1)}, u32[]{:S(2)}, u32[]{:S(2)}) %collective-permute-start.1) | collective-permute-done | bytes 327712 | tf_op jit(solution)/shard_map/ppermute | solution.py:324
  16.1 1.8 %collective-permute-start.7 = (bf16[2,1,40,2048]{3,2,1,0:T(8,128)(2,1)S(1)}, bf16[2,1,40,2048]{3,2,1,0:T(8,128)(2,1)S(1)}, u32[]{:S(2)}, u32[]{:S(2)}) collective-permute-start(bf16[2,1,40,2048]{3,2,1,0:T(8,128)(2,1)S(1)} %collective-permute-done.1.refs_1_), channel_id=1, source_target_pairs={{0,2},{1,3},{2,0},{3,1},{4,6},{5,7},{6,4},{7,5},{8,10},{9,11},{10,... | collective-permute-start | bytes 983048 | tf_op jit(solution)/shard_map/ppermute | solution.py:353
  18.6 1.6 collective-permute-start.3
  20.2 3.8 %masked.4 = (bf16[2048,1792]{1,0:T(8,128)(2,1)S(1)}, f32[8,128]{1,0:T(8,128)S(1)}) custom-call(s32[2]{0:T(128)S(1)} %pad_add_fusion.core_ref.place_ref, bf16[2048,1792]{1,0:T(8,128)(2,1)} %weight_ref.4, s32[32,28]{1,0:T(8,128)S(1)} %copy-done.1, f32[8,128]{1,0:T(8,128)S(1)} %get-tuple-element.103.refs_0_), custom_call_target="tpu_custom_call" | custom-call | tf_op jit(solution)/shard_map/masked/pallas_call | solution.py:81
  24.1 3.8 %masked.5 = (bf16[2048,1792]{1,0:T(8,128)(2,1)S(1)}, f32[8,128]{1,0:T(8,128)S(1)}) custom-call(s32[2]{0:T(128)S(1)} %pad_add_fusion.core_ref.place_ref, bf16[2048,1792]{1,0:T(8,128)(2,1)} %weight_ref.5, s32[32,28]{1,0:T(8,128)S(1)} %copy-done.2, f32[8,128]{1,0:T(8,128)S(1)} %get-tuple-element.106.refs_0_, ...), custom_call_target="tpu_custom_call" | custom-call | flops 172500000 | tf_op jit(solution)/shard_map/masked/pallas_call | solution.py:81
  28.1 4.5 %collective-permute-start.10 = (bf16[160,2048]{1,0:T(8,128)(2,1)S(1)}, bf16[160,2048]{1,0:T(8,128)(2,1)S(1)}, u32[]{:S(2)}, u32[]{:S(2)}) collective-permute-start(bf16[160,2048]{1,0:T(8,128)(2,1)S(1)} %get-tuple-element.118.refs_0_.mine_ref), channel_id=1, source_target_pairs={{0,6},{1,7},{6,0},{7,1},{8,14},{9,15},{14,8},{15,9},{16,22},{17,23... | collective-permute-start | bytes 1966088 | tf_op jit(solution)/shard_map/ppermute | solution.py:353
  33.4 6.1 %gate_up.4 = (bf16[2,2,2,40,1792]{4,3,2,1,0:T(8,128)(2,1)S(1)}, bf16[2,2,40,1792]{3,2,1,0:T(8,128)(2,1)S(1)}, bf16[2,2,1,40,1792]{4,3,2,1,0:T(8,128)(2,1)S(1)}, f32[8,128]{1,0:T(8,128)S(1)}) custom-call(bf16[160,2048]{1,0:T(8,128)(2,1)S(1)} %get-tuple-element.118.refs_0_.mine_ref, bf16[160,2048]{1,0:T(8,128)(2,1)S(1)} %get-tuple-element.110.refs_1_, ...), custom_call_target="tpu_custom_call" | custom-call | tf_op jit(solution)/shard_map/gate_up/pallas_call | solution.py:206
  40.1 3.9 %masked.6 = (bf16[1792,2048]{1,0:T(8,128)(2,1)S(1)}, f32[8,128]{1,0:T(8,128)S(1)}) custom-call(s32[2]{0:T(128)S(1)} %pad_add_fusion.core_ref.place_ref, bf16[1792,8192]{1,0:T(8,128)(2,1)} %weight_ref.7, s32[28,128]{1,0:T(8,128)S(1)} %copy-done, f32[8,128]{1,0:T(8,128)S(1)} %get-tuple-element.119.refs_0_), custom_call_target="tpu_custom_call" | custom-call | tf_op jit(solution)/shard_map/masked/pallas_call | solution.py:81
  44.0 3.9 %masked.7 = (bf16[1792,2048]{1,0:T(8,128)(2,1)S(1)}, f32[8,128]{1,0:T(8,128)S(1)}) custom-call(s32[2]{0:T(128)S(1)} %pad_add_fusion.core_ref.place_ref, bf16[1792,8192]{1,0:T(8,128)(2,1)} %weight_ref.7, s32[28,128]{1,0:T(8,128)S(1)} %copy-done, f32[8,128]{1,0:T(8,128)S(1)} %get-tuple-element.120.refs_0_), custom_call_target="tpu_custom_call" | custom-call | tf_op jit(solution)/shard_map/masked/pallas_call | solution.py:81
  48.8 1.3 collective-permute-start.17
  50.2 6.1 %gate_up.5 = (bf16[2,2,2,40,1792]{4,3,2,1,0:T(8,128)(2,1)S(1)}, bf16[2,2,40,1792]{3,2,1,0:T(8,128)(2,1)S(1)}, bf16[2,2,1,40,1792]{4,3,2,1,0:T(8,128)(2,1)S(1)}, f32[8,128]{1,0:T(8,128)S(1)}) custom-call(bf16[160,2048]{1,0:T(8,128)(2,1)S(1)} %get-tuple-element.126.refs_0_, bf16[160,2048]{1,0:T(8,128)(2,1)S(1)} %collective-permute-done.12.refs_1_, ...), custom_call_target="tpu_custom_call" | custom-call | flops 4697620480 | tf_op jit(solution)/shard_map/gate_up/pallas_call | solution.py:206
  56.8 1.5 collective-permute-done.13.refs_1_
  58.3 0.8 collective-permute-done.14.refs_3_.refs_1_
  59.3 1.6 collective-permute-start.16
  60.8 5.7 %collective-permute-done.11.refs_5_.refs_0_ = bf16[160,2048]{1,0:T(8,128)(2,1)S(1)} collective-permute-done((bf16[160,2048]{1,0:T(8,128)(2,1)S(1)}, bf16[160,2048]{1,0:T(8,128)(2,1)S(1)}, u32[]{:S(2)}, u32[]{:S(2)}) %collective-permute-start.11) | collective-permute-done | bytes 655392 | tf_op jit(solution)/shard_map/ppermute | solution.py:353
  67.3 6.1 %gate_up.6 = (bf16[2,2,2,40,1792]{4,3,2,1,0:T(8,128)(2,1)S(1)}, bf16[2,2,40,1792]{3,2,1,0:T(8,128)(2,1)S(1)}, bf16[2,2,1,40,1792]{4,3,2,1,0:T(8,128)(2,1)S(1)}, f32[8,128]{1,0:T(8,128)S(1)}) custom-call(bf16[160,2048]{1,0:T(8,128)(2,1)S(1)} %get-tuple-element.136.refs_0_, bf16[160,2048]{1,0:T(8,128)(2,1)S(1)} %collective-permute-done.17.refs_1_, ...), custom_call_target="tpu_custom_call" | custom-call | flops 4697620480 | tf_op jit(solution)/shard_map/gate_up/pallas_call | solution.py:206
  76.4 1.5 collective-permute-start.23
  77.9 3.9 %down.4 = (bf16[2,40,4096]{2,1,0:T(8,128)(2,1)S(1)}, bf16[2,40,4096]{2,1,0:T(8,128)(2,1)S(1)}, f32[8,128]{1,0:T(8,128)S(1)}) custom-call(bf16[2,40,1792]{2,1,0:T(8,128)(2,1)S(1)} %get-tuple-element.138.own_ref, bf16[2,40,1792]{2,1,0:T(8,128)(2,1)S(1)} %collective-permute-done.18.other_ref, bf16[1792,2048]{1,0:T(8,128)(2,1)S(1)} %get-tuple-element.139.refs_0_, ...), custom_call_target="tpu_custom_call" | custom-call | flops 2348810 | tf_op jit(solution)/shard_map/down/pallas_call | solution.py:248
  82.1 1.0 collective-permute-start.28
  83.1 6.1 %gate_up.7 = (bf16[2,2,2,40,1792]{4,3,2,1,0:T(8,128)(2,1)S(1)}, bf16[2,2,40,1792]{3,2,1,0:T(8,128)(2,1)S(1)}, bf16[1,2,1,40,1792]{4,3,2,1,0:T(8,128)(2,1)S(1)}, ...) custom-call(bf16[160,2048]{1,0:T(8,128)(2,1)S(1)} %collective-permute-done.11.refs_5_.refs_0_, ...), custom_call_target="tpu_custom_call" | custom-call | flops 4697620480 | tf_op jit(solution)/shard_map/gate_up/pallas_call | solution.py:206
  89.8 1.7 %collective-permute-done.23.refs_2_ = bf16[2,2,40,1792]{3,2,1,0:T(8,128)(2,1)S(1)} collective-permute-done((bf16[2,2,40,1792]{3,2,1,0:T(8,128)(2,1)S(1)}, bf16[2,2,40,1792]{3,2,1,0:T(8,128)(2,1)S(1)}, u32[]{:S(2)}, u32[]{:S(2)}) %collective-permute-start.23) | collective-permute-done | bytes 573472 | tf_op jit(solution)/shard_map/ppermute | solution.py:324
  92.6 1.4 collective-permute-start.24
  94.0 3.9 %down.5 = (bf16[1,40,4096]{2,1,0:T(8,128)(2,1)S(1)}, bf16[1,40,4096]{2,1,0:T(8,128)(2,1)S(1)}, bf16[1,40,4096]{2,1,0:T(8,128)(2,1)S(1)}, bf16[1,40,4096]{2,1,0:T(8,128)(2,1)S(1)}, f32[8,128]{1,0:T(8,128)S(1)}) custom-call(bf16[2,40,1792]{2,1,0:T(8,128)(2,1)S(1)} %get-tuple-element.158.own_ref, bf16[2,40,1792]{2,1,0:T(8,128)(2,1)S(1)} %collective-permute-done.27.other_ref, ...), custom_call_target="tpu_custom_call" | custom-call | flops 2348810 | tf_op jit(solution)/shard_map/down/pallas_call | solution.py:248
  98.3 1.2 collective-permute-start.29
  99.7 1.7 %collective-permute-start.32 = (bf16[2,40,4096]{2,1,0:T(8,128)(2,1)S(1)}, bf16[2,40,4096]{2,1,0:T(8,128)(2,1)S(1)}, u32[]{:S(2)}, u32[]{:S(2)}) collective-permute-start(bf16[2,40,4096]{2,1,0:T(8,128)(2,1)S(1)} %get-tuple-element.177), channel_id=1, source_target_pairs={{0,2},{1,3},{2,0},{3,1},{4,6},{5,7},{6,4},{7,5},{8,10},{9,11},{10,... | collective-permute-start | bytes 1966088 | tf_op jit(solution)/shard_map/ppermute | solution.py:353
  101.4 6.0 %collective-permute-done.29.refs_1_ = bf16[1,40,4096]{2,1,0:T(8,128)(2,1)S(1)} collective-permute-done((bf16[1,40,4096]{2,1,0:T(8,128)(2,1)S(1)}, bf16[1,40,4096]{2,1,0:T(8,128)(2,1)S(1)}, u32[]{:S(2)}, u32[]{:S(2)}) %collective-permute-start.29) | collective-permute-done | bytes 327712 | tf_op jit(solution)/shard_map/ppermute | solution.py:324
  107.5 1.3 collective-permute-start.31
  109.1 1.2 collective-permute-start.25
  110.4 1.6 collective-permute-start.34
  112.0 3.9 %down.6 = (bf16[1,40,4096]{2,1,0:T(8,128)(2,1)S(1)}, bf16[1,40,4096]{2,1,0:T(8,128)(2,1)S(1)}, bf16[1,40,4096]{2,1,0:T(8,128)(2,1)S(1)}, bf16[1,40,4096]{2,1,0:T(8,128)(2,1)S(1)}, f32[8,128]{1,0:T(8,128)S(1)}) custom-call(bf16[2,40,1792]{2,1,0:T(8,128)(2,1)S(1)} %get-tuple-element.168.own_ref, bf16[2,40,1792]{2,1,0:T(8,128)(2,1)S(1)} %collective-permute-done.30.other_ref, ...), custom_call_target="tpu_custom_call" | custom-call | flops 2348810 | tf_op jit(solution)/shard_map/down/pallas_call | solution.py:248
  115.8 1.6 %collective-permute-done.32.refs_3_.refs_1_ = bf16[2,40,4096]{2,1,0:T(8,128)(2,1)S(1)} collective-permute-done((bf16[2,40,4096]{2,1,0:T(8,128)(2,1)S(1)}, bf16[2,40,4096]{2,1,0:T(8,128)(2,1)S(1)}, u32[]{:S(2)}, u32[]{:S(2)}) %collective-permute-start.32) | collective-permute-done | bytes 655392 | tf_op jit(solution)/shard_map/ppermute | solution.py:353
  117.6 0.9 collective-permute-start.33
  118.4 1.3 collective-permute-start.38
  119.8 4.7 %collective-permute-done.34.refs_2_ = bf16[1,40,4096]{2,1,0:T(8,128)(2,1)S(1)} collective-permute-done((bf16[1,40,4096]{2,1,0:T(8,128)(2,1)S(1)}, bf16[1,40,4096]{2,1,0:T(8,128)(2,1)S(1)}, u32[]{:S(2)}, u32[]{:S(2)}) %collective-permute-start.34) | collective-permute-done | bytes 327712 | tf_op jit(solution)/shard_map/ppermute | solution.py:353
  124.5 1.0 collective-permute-done.33.refs_1_
  126.6 1.1 collective-permute-start.40
  127.7 3.9 %down.7 = (bf16[2,40,4096]{2,1,0:T(8,128)(2,1)S(1)}, bf16[2,40,4096]{2,1,0:T(8,128)(2,1)S(1)}, f32[8,128]{1,0:T(8,128)S(1)}) custom-call(bf16[2,40,1792]{2,1,0:T(8,128)(2,1)S(1)} %get-tuple-element.182.own_ref, bf16[2,40,1792]{2,1,0:T(8,128)(2,1)S(1)} %collective-permute-done.35.other_ref, bf16[1792,2048]{1,0:T(8,128)(2,1)S(1)} %get-tuple-element.139.refs_0_, ...), custom_call_target="tpu_custom_call" | custom-call | flops 2348810 | tf_op jit(solution)/shard_map/down/pallas_call | solution.py:248
  131.7 4.5 %collective-permute-done.36.refs_1_ = bf16[1,40,4096]{2,1,0:T(8,128)(2,1)S(1)} collective-permute-done((bf16[1,40,4096]{2,1,0:T(8,128)(2,1)S(1)}, bf16[1,40,4096]{2,1,0:T(8,128)(2,1)S(1)}, u32[]{:S(2)}, u32[]{:S(2)}) %collective-permute-start.36) | collective-permute-done | bytes 327712 | tf_op jit(solution)/shard_map/ppermute | solution.py:324
  136.7 1.2 collective-permute-start.37
  137.9 13.8 %collective-permute-done.40.refs_0_ = bf16[1,40,4096]{2,1,0:T(8,128)(2,1)S(1)} collective-permute-done((bf16[1,40,4096]{2,1,0:T(8,128)(2,1)S(1)}, bf16[1,40,4096]{2,1,0:T(8,128)(2,1)S(1)}, u32[]{:S(2)}, u32[]{:S(2)}) %collective-permute-start.40) | collective-permute-done | bytes 327712 | tf_op jit(solution)/shard_map/ppermute | solution.py:353
  152.9 5.5 %collective-permute-done.39 = bf16[1,40,4096]{2,1,0:T(8,128)(2,1)S(1)} collective-permute-done((bf16[1,40,4096]{2,1,0:T(8,128)(2,1)S(1)}, bf16[1,40,4096]{2,1,0:T(8,128)(2,1)S(1)}, u32[]{:S(2)}, u32[]{:S(2)}) %collective-permute-start.39) | collective-permute-done | bytes 327712 | tf_op jit(solution)/shard_map/ppermute | solution.py:353
  158.6 0.9 pad_maximum_fusion
  (88 shorter events, 15.8 us)
Async XLA Ops:
  2.7 17.5 %copy-start.1 = (s32[32,28]{1,0:T(8,128)S(1)}, s32[32,28]{1,0:T(8,128)}, u32[]{:S(2)}) copy-start(s32[32,28]{1,0:T(8,128)} %mask_ref.4) | copy-start | bytes 10756
  2.8 1.8 %collective-permute-start = (bf16[2,40,2048]{2,1,0:T(8,128)(2,1)S(1)}, bf16[2,40,2048]{2,1,0:T(8,128)(2,1)S(1)}, u32[]{:S(2)}, u32[]{:S(2)}) collective-permute-start(bf16[2,40,2048]{2,1,0:T(8,128)(2,1)S(1)} %pad_maximum_fusion.1), channel_id=1, source_target_pairs={{0,8},{8,0},{16,24},{24,16},{1,9},{9,1},{17,25},{25,17},{2,10},{10... | collective-permute-start | bytes 983048 | tf_op jit(solution)/shard_map/ppermute | solution.py:324
  5.2 10.9 %collective-permute-start.1 = (bf16[2,1,40,2048]{3,2,1,0:T(8,128)(2,1)S(1)}, bf16[2,1,40,2048]{3,2,1,0:T(8,128)(2,1)S(1)}, u32[]{:S(2)}, u32[]{:S(2)}) collective-permute-start(bf16[2,1,40,2048]{3,2,1,0:T(8,128)(2,1)S(1)} %get-tuple-element.101.refs_2_), channel_id=1, source_target_pairs={{0,16},{8,24},{16,0},{24,8},{1,17},{9,25},{17,1},{25,9},{2,18},{10... | collective-permute-start | bytes 983048 | tf_op jit(solution)/shard_map/ppermute | solution.py:324
  8.1 10.5 %collective-permute-start.6 = (bf16[2,1,40,2048]{3,2,1,0:T(8,128)(2,1)S(1)}, bf16[2,1,40,2048]{3,2,1,0:T(8,128)(2,1)S(1)}, u32[]{:S(2)}, u32[]{:S(2)}) collective-permute-start(bf16[2,1,40,2048]{3,2,1,0:T(8,128)(2,1)S(1)} %get-tuple-element.102.refs_0_), channel_id=1, source_target_pairs={{0,2},{1,3},{2,0},{3,1},{4,6},{5,7},{6,4},{7,5},{8,10},{9,11},{10,... | collective-permute-start | bytes 983048 | tf_op jit(solution)/shard_map/ppermute | solution.py:353
  9.7 18.2 %collective-permute-start.4 = (bf16[2,1,40,2048]{3,2,1,0:T(8,128)(2,1)S(1)}, bf16[2,1,40,2048]{3,2,1,0:T(8,128)(2,1)S(1)}, u32[]{:S(2)}, u32[]{:S(2)}) collective-permute-start(bf16[2,1,40,2048]{3,2,1,0:T(8,128)(2,1)S(1)} %get-tuple-element.102.refs_0_), channel_id=1, source_target_pairs={{2,4},{3,5},{4,2},{5,3},{10,12},{11,13},{12,10},{13,11},{18,20},{1... | collective-permute-start | bytes 983048 | tf_op jit(solution)/shard_map/ppermute | solution.py:353
  10.4 17.5 %collective-permute-start.2 = (bf16[2,1,40,2048]{3,2,1,0:T(8,128)(2,1)S(1)}, bf16[2,1,40,2048]{3,2,1,0:T(8,128)(2,1)S(1)}, u32[]{:S(2)}, u32[]{:S(2)}) collective-permute-start(bf16[2,1,40,2048]{3,2,1,0:T(8,128)(2,1)S(1)} %get-tuple-element.102.refs_0_), channel_id=1, source_target_pairs={{0,1},{1,0},{2,3},{3,2},{4,5},{5,4},{6,7},{7,6},{8,9},{9,8},{10,11... | collective-permute-start | bytes 983048 | tf_op jit(solution)/shard_map/ppermute | solution.py:324
  16.1 11.9 %collective-permute-start.7 = (bf16[2,1,40,2048]{3,2,1,0:T(8,128)(2,1)S(1)}, bf16[2,1,40,2048]{3,2,1,0:T(8,128)(2,1)S(1)}, u32[]{:S(2)}, u32[]{:S(2)}) collective-permute-start(bf16[2,1,40,2048]{3,2,1,0:T(8,128)(2,1)S(1)} %collective-permute-done.1.refs_1_), channel_id=1, source_target_pairs={{0,2},{1,3},{2,0},{3,1},{4,6},{5,7},{6,4},{7,5},{8,10},{9,11},{10,... | collective-permute-start | bytes 983048 | tf_op jit(solution)/shard_map/ppermute | solution.py:353
  17.9 10.1 %collective-permute-start.5 = (bf16[2,1,40,2048]{3,2,1,0:T(8,128)(2,1)S(1)}, bf16[2,1,40,2048]{3,2,1,0:T(8,128)(2,1)S(1)}, u32[]{:S(2)}, u32[]{:S(2)}) collective-permute-start(bf16[2,1,40,2048]{3,2,1,0:T(8,128)(2,1)S(1)} %collective-permute-done.1.refs_1_), channel_id=1, source_target_pairs={{2,4},{3,5},{4,2},{5,3},{10,12},{11,13},{12,10},{13,11},{18,20},{1... | collective-permute-start | bytes 983048 | tf_op jit(solution)/shard_map/ppermute | solution.py:353
  18.6 9.4 %collective-permute-start.3 = (bf16[2,1,40,2048]{3,2,1,0:T(8,128)(2,1)S(1)}, bf16[2,1,40,2048]{3,2,1,0:T(8,128)(2,1)S(1)}, u32[]{:S(2)}, u32[]{:S(2)}) collective-permute-start(bf16[2,1,40,2048]{3,2,1,0:T(8,128)(2,1)S(1)} %collective-permute-done.1.refs_1_), channel_id=1, source_target_pairs={{0,1},{1,0},{2,3},{3,2},{4,5},{5,4},{6,7},{7,6},{8,9},{9,8},{10,11... | collective-permute-start | bytes 983048 | tf_op jit(solution)/shard_map/ppermute | solution.py:324
  20.2 3.8 %copy-start.2 = (s32[32,28]{1,0:T(8,128)S(1)}, s32[32,28]{1,0:T(8,128)}, u32[]{:S(2)}) copy-start(s32[32,28]{1,0:T(8,128)} %mask_ref.5) | copy-start | bytes 10756
  28.1 19.8 %collective-permute-start.10 = (bf16[160,2048]{1,0:T(8,128)(2,1)S(1)}, bf16[160,2048]{1,0:T(8,128)(2,1)S(1)}, u32[]{:S(2)}, u32[]{:S(2)}) collective-permute-start(bf16[160,2048]{1,0:T(8,128)(2,1)S(1)} %get-tuple-element.118.refs_0_.mine_ref), channel_id=1, source_target_pairs={{0,6},{1,7},{6,0},{7,1},{8,14},{9,15},{14,8},{15,9},{16,22},{17,23... | collective-permute-start | bytes 1966088 | tf_op jit(solution)/shard_map/ppermute | solution.py:353
  32.6 16.1 %collective-permute-start.12 = (bf16[160,2048]{1,0:T(8,128)(2,1)S(1)}, bf16[160,2048]{1,0:T(8,128)(2,1)S(1)}, u32[]{:S(2)}, u32[]{:S(2)}) collective-permute-start(bf16[160,2048]{1,0:T(8,128)(2,1)S(1)} %get-tuple-element.126.refs_0_), channel_id=1, source_target_pairs={{0,1},{1,0},{2,3},{3,2},{4,5},{5,4},{6,7},{7,6},{8,9},{9,8},{10,11... | collective-permute-start | bytes 1966088 | tf_op jit(solution)/shard_map/ppermute | solution.py:324
  33.4 6.7 %copy-start = (s32[28,128]{1,0:T(8,128)S(1)}, s32[28,128]{1,0:T(8,128)}, u32[]{:S(2)}) copy-start(s32[28,128]{1,0:T(8,128)} %mask_ref.7) | copy-start | bytes 43012
  39.5 9.1 %collective-permute-start.8 = (bf16[2,2,40,1792]{3,2,1,0:T(8,128)(2,1)S(1)}, bf16[2,2,40,1792]{3,2,1,0:T(8,128)(2,1)S(1)}, u32[]{:S(2)}, u32[]{:S(2)}) collective-permute-start(bf16[2,2,40,1792]{3,2,1,0:T(8,128)(2,1)S(1)} %get-tuple-element.115), channel_id=1, source_target_pairs={{0,8},{8,0},{16,24},{24,16},{1,9},{9,1},{17,25},{25,17},{2,10},{10... | collective-permute-start | bytes 1720328 | tf_op jit(solution)/shard_map/ppermute | solution.py:324
  39.6 9.0 %collective-permute-start.9 = (bf16[2,2,1,40,1792]{4,3,2,1,0:T(8,128)(2,1)S(1)}, bf16[2,2,1,40,1792]{4,3,2,1,0:T(8,128)(2,1)S(1)}, u32[]{:S(2)}, u32[]{:S(2)}) collective-permute-start(bf16[2,2,1,40,1792]{4,3,2,1,0:T(8,128)(2,1)S(1)} %get-tuple-element.116), channel_id=1, source_target_pairs={{0,8},{8,0},{16,24},{24,16},{1,9},{9,1},{17,25},{25,17},{2,10},{10... | collective-permute-start | bytes 1720328 | tf_op jit(solution)/shard_map/ppermute | solution.py:324
  48.8 18.5 %collective-permute-start.17 = (bf16[160,2048]{1,0:T(8,128)(2,1)S(1)}, bf16[160,2048]{1,0:T(8,128)(2,1)S(1)}, u32[]{:S(2)}, u32[]{:S(2)}) collective-permute-start(bf16[160,2048]{1,0:T(8,128)(2,1)S(1)} %get-tuple-element.136.refs_0_), channel_id=1, source_target_pairs={{0,1},{1,0},{2,3},{3,2},{4,5},{5,4},{6,7},{7,6},{8,9},{9,8},{10,11... | collective-permute-start | bytes 1966088 | tf_op jit(solution)/shard_map/ppermute | solution.py:324
  50.1 16.4 %collective-permute-start.11 = (bf16[160,2048]{1,0:T(8,128)(2,1)S(1)}, bf16[160,2048]{1,0:T(8,128)(2,1)S(1)}, u32[]{:S(2)}, u32[]{:S(2)}) collective-permute-start(bf16[160,2048]{1,0:T(8,128)(2,1)S(1)} %get-tuple-element.124), channel_id=1, source_target_pairs={{0,4},{1,5},{4,6},{5,7},{6,2},{7,3},{2,0},{3,1},{8,12},{9,13},{12,... | collective-permute-start | bytes 1966088 | tf_op jit(solution)/shard_map/ppermute | solution.py:353
  56.2 2.0 %collective-permute-start.13 = (bf16[2,2,1,40,1792]{4,3,2,1,0:T(8,128)(2,1)S(1)}, bf16[2,2,1,40,1792]{4,3,2,1,0:T(8,128)(2,1)S(1)}, u32[]{:S(2)}, u32[]{:S(2)}) collective-permute-start(bf16[2,2,1,40,1792]{4,3,2,1,0:T(8,128)(2,1)S(1)} %get-tuple-element.129), channel_id=1, source_target_pairs={{0,8},{8,0},{16,24},{24,16},{1,9},{9,1},{17,25},{25,17},{2,10},{10... | collective-permute-start | bytes 1720328 | tf_op jit(solution)/shard_map/ppermute | solution.py:324
  56.3 2.8 %collective-permute-start.14 = (bf16[2,2,40,1792]{3,2,1,0:T(8,128)(2,1)S(1)}, bf16[2,2,40,1792]{3,2,1,0:T(8,128)(2,1)S(1)}, u32[]{:S(2)}, u32[]{:S(2)}) collective-permute-start(bf16[2,2,40,1792]{3,2,1,0:T(8,128)(2,1)S(1)} %get-tuple-element.131), channel_id=1, source_target_pairs={{0,8},{8,0},{16,24},{24,16},{1,9},{9,1},{17,25},{25,17},{2,10},{10... | collective-permute-start | bytes 1720328 | tf_op jit(solution)/shard_map/ppermute | solution.py:324
  59.3 15.1 %collective-permute-start.16 = (bf16[2,2,40,1792]{3,2,1,0:T(8,128)(2,1)S(1)}, bf16[2,2,40,1792]{3,2,1,0:T(8,128)(2,1)S(1)}, u32[]{:S(2)}, u32[]{:S(2)}) collective-permute-start(bf16[2,2,40,1792]{3,2,1,0:T(8,128)(2,1)S(1)} %get-tuple-element.134), channel_id=1, source_target_pairs={{0,16},{8,24},{16,0},{24,8},{1,17},{9,25},{17,1},{25,9},{2,18},{10... | collective-permute-start | bytes 1720328 | tf_op jit(solution)/shard_map/ppermute | solution.py:324
  66.5 15.6 %collective-permute-start.15 = (bf16[160,2048]{1,0:T(8,128)(2,1)S(1)}, bf16[160,2048]{1,0:T(8,128)(2,1)S(1)}, u32[]{:S(2)}, u32[]{:S(2)}) collective-permute-start(bf16[160,2048]{1,0:T(8,128)(2,1)S(1)} %collective-permute-done.11.refs_5_.refs_0_), channel_id=1, source_target_pairs={{0,1},{1,0},{2,3},{3,2},{4,5},{5,4},{6,7},{7,6},{8,9},{9,8},{10,11... | collective-permute-start | bytes 1966088 | tf_op jit(solution)/shard_map/ppermute | solution.py:324
  73.4 2.0 %collective-permute-start.19 = (bf16[2,2,1,40,1792]{4,3,2,1,0:T(8,128)(2,1)S(1)}, bf16[2,2,1,40,1792]{4,3,2,1,0:T(8,128)(2,1)S(1)}, u32[]{:S(2)}, u32[]{:S(2)}) collective-permute-start(bf16[2,2,1,40,1792]{4,3,2,1,0:T(8,128)(2,1)S(1)} %get-tuple-element.142), channel_id=1, source_target_pairs={{0,8},{8,0},{16,24},{24,16},{1,9},{9,1},{17,25},{25,17},{2,10},{10... | collective-permute-start | bytes 1720328 | tf_op jit(solution)/shard_map/ppermute | solution.py:324
  73.5 2.8 %collective-permute-start.20 = (bf16[2,2,40,1792]{3,2,1,0:T(8,128)(2,1)S(1)}, bf16[2,2,40,1792]{3,2,1,0:T(8,128)(2,1)S(1)}, u32[]{:S(2)}, u32[]{:S(2)}) collective-permute-start(bf16[2,2,40,1792]{3,2,1,0:T(8,128)(2,1)S(1)} %get-tuple-element.144), channel_id=1, source_target_pairs={{0,8},{8,0},{16,24},{24,16},{1,9},{9,1},{17,25},{25,17},{2,10},{10... | collective-permute-start | bytes 1720328 | tf_op jit(solution)/shard_map/ppermute | solution.py:324
  74.6 3.3 %collective-permute-start.18 = (bf16[2,40,1792]{2,1,0:T(8,128)(2,1)S(1)}, bf16[2,40,1792]{2,1,0:T(8,128)(2,1)S(1)}, u32[]{:S(2)}, u32[]{:S(2)}) collective-permute-start(bf16[2,40,1792]{2,1,0:T(8,128)(2,1)S(1)} %get-tuple-element.138.own_ref), channel_id=1, source_target_pairs={{0,8},{8,0},{16,24},{24,16},{1,9},{9,1},{17,25},{25,17},{2,10},{10... | collective-permute-start | bytes 860168 | tf_op jit(solution)/shard_map/ppermute | solution.py:324
  76.4 15.1 %collective-permute-start.23 = (bf16[2,2,40,1792]{3,2,1,0:T(8,128)(2,1)S(1)}, bf16[2,2,40,1792]{3,2,1,0:T(8,128)(2,1)S(1)}, u32[]{:S(2)}, u32[]{:S(2)}) collective-permute-start(bf16[2,2,40,1792]{3,2,1,0:T(8,128)(2,1)S(1)} %get-tuple-element.150), channel_id=1, source_target_pairs={{0,16},{8,24},{16,0},{24,8},{1,17},{9,25},{17,1},{25,9},{2,18},{10... | collective-permute-start | bytes 1720328 | tf_op jit(solution)/shard_map/ppermute | solution.py:324
  82.1 16.2 %collective-permute-start.28 = (bf16[2,40,4096]{2,1,0:T(8,128)(2,1)S(1)}, bf16[2,40,4096]{2,1,0:T(8,128)(2,1)S(1)}, u32[]{:S(2)}, u32[]{:S(2)}) collective-permute-start(bf16[2,40,4096]{2,1,0:T(8,128)(2,1)S(1)} %get-tuple-element.162), channel_id=1, source_target_pairs={{0,1},{1,0},{2,3},{3,2},{4,5},{5,4},{6,7},{7,6},{8,9},{9,8},{10,11... | collective-permute-start | bytes 1966088 | tf_op jit(solution)/shard_map/ppermute | solution.py:324
  89.2 2.7 %collective-permute-start.21 = (bf16[1,2,1,40,1792]{4,3,2,1,0:T(8,128)(2,1)S(1)}, bf16[1,2,1,40,1792]{4,3,2,1,0:T(8,128)(2,1)S(1)}, u32[]{:S(2)}, u32[]{:S(2)}) collective-permute-start(bf16[1,2,1,40,1792]{4,3,2,1,0:T(8,128)(2,1)S(1)} %get-tuple-element.148), channel_id=1, source_target_pairs={{0,8},{8,0},{16,24},{24,16},{1,9},{9,1},{17,25},{25,17},{2,10},{10... | collective-permute-start | bytes 860168 | tf_op jit(solution)/shard_map/ppermute | solution.py:324
  89.3 2.6 %collective-permute-start.22 = (bf16[1,2,1,40,1792]{4,3,2,1,0:T(8,128)(2,1)S(1)}, bf16[1,2,1,40,1792]{4,3,2,1,0:T(8,128)(2,1)S(1)}, u32[]{:S(2)}, u32[]{:S(2)}) collective-permute-start(bf16[1,2,1,40,1792]{4,3,2,1,0:T(8,128)(2,1)S(1)} %get-tuple-element.149), channel_id=1, source_target_pairs={{0,8},{8,0},{16,24},{24,16},{1,9},{9,1},{17,25},{25,17},{2,10},{10... | collective-permute-start | bytes 860168 | tf_op jit(solution)/shard_map/ppermute | solution.py:324
  91.8 2.3 %collective-permute-start.27 = (bf16[2,40,1792]{2,1,0:T(8,128)(2,1)S(1)}, bf16[2,40,1792]{2,1,0:T(8,128)(2,1)S(1)}, u32[]{:S(2)}, u32[]{:S(2)}) collective-permute-start(bf16[2,40,1792]{2,1,0:T(8,128)(2,1)S(1)} %get-tuple-element.158.own_ref), channel_id=1, source_target_pairs={{0,8},{8,0},{16,24},{24,16},{1,9},{9,1},{17,25},{25,17},{2,10},{10... | collective-permute-start | bytes 860168 | tf_op jit(solution)/shard_map/ppermute | solution.py:324
  92.0 16.8 %collective-permute-start.26 = (bf16[2,2,40,1792]{3,2,1,0:T(8,128)(2,1)S(1)}, bf16[2,2,40,1792]{3,2,1,0:T(8,128)(2,1)S(1)}, u32[]{:S(2)}, u32[]{:S(2)}) collective-permute-start(bf16[2,2,40,1792]{3,2,1,0:T(8,128)(2,1)S(1)} %get-tuple-element.157), channel_id=1, source_target_pairs={{0,8},{8,0},{16,24},{24,16},{1,9},{9,1},{17,25},{25,17},{2,10},{10... | collective-permute-start | bytes 1720328 | tf_op jit(solution)/shard_map/ppermute | solution.py:324
  92.6 16.2 %collective-permute-start.24 = (bf16[2,2,40,1792]{3,2,1,0:T(8,128)(2,1)S(1)}, bf16[2,2,40,1792]{3,2,1,0:T(8,128)(2,1)S(1)}, u32[]{:S(2)}, u32[]{:S(2)}) collective-permute-start(bf16[2,2,40,1792]{3,2,1,0:T(8,128)(2,1)S(1)} %get-tuple-element.153), channel_id=1, source_target_pairs={{0,16},{8,24},{16,0},{24,8},{1,17},{9,25},{17,1},{25,9},{2,18},{10... | collective-permute-start | bytes 1720328 | tf_op jit(solution)/shard_map/ppermute | solution.py:324
  98.3 9.0 %collective-permute-start.29 = (bf16[1,40,4096]{2,1,0:T(8,128)(2,1)S(1)}, bf16[1,40,4096]{2,1,0:T(8,128)(2,1)S(1)}, u32[]{:S(2)}, u32[]{:S(2)}) collective-permute-start(bf16[1,40,4096]{2,1,0:T(8,128)(2,1)S(1)} %get-tuple-element.163), channel_id=1, source_target_pairs={{0,1},{1,0},{2,3},{3,2},{4,5},{5,4},{6,7},{7,6},{8,9},{9,8},{10,11... | collective-permute-start | bytes 983048 | tf_op jit(solution)/shard_map/ppermute | solution.py:324
  99.7 17.7 %collective-permute-start.32 = (bf16[2,40,4096]{2,1,0:T(8,128)(2,1)S(1)}, bf16[2,40,4096]{2,1,0:T(8,128)(2,1)S(1)}, u32[]{:S(2)}, u32[]{:S(2)}) collective-permute-start(bf16[2,40,4096]{2,1,0:T(8,128)(2,1)S(1)} %get-tuple-element.177), channel_id=1, source_target_pairs={{0,2},{1,3},{2,0},{3,1},{4,6},{5,7},{6,4},{7,5},{8,10},{9,11},{10,... | collective-permute-start | bytes 1966088 | tf_op jit(solution)/shard_map/ppermute | solution.py:353
  107.5 10.0 %collective-permute-start.31 = (bf16[1,40,4096]{2,1,0:T(8,128)(2,1)S(1)}, bf16[1,40,4096]{2,1,0:T(8,128)(2,1)S(1)}, u32[]{:S(2)}, u32[]{:S(2)}) collective-permute-start(bf16[1,40,4096]{2,1,0:T(8,128)(2,1)S(1)} %get-tuple-element.175), channel_id=1, source_target_pairs={{0,1},{1,0},{2,3},{3,2},{4,5},{5,4},{6,7},{7,6},{8,9},{9,8},{10,11... | collective-permute-start | bytes 983048 | tf_op jit(solution)/shard_map/ppermute | solution.py:324
  109.1 2.9 %collective-permute-start.30 = (bf16[2,40,1792]{2,1,0:T(8,128)(2,1)S(1)}, bf16[2,40,1792]{2,1,0:T(8,128)(2,1)S(1)}, u32[]{:S(2)}, u32[]{:S(2)}) collective-permute-start(bf16[2,40,1792]{2,1,0:T(8,128)(2,1)S(1)} %get-tuple-element.168.own_ref), channel_id=1, source_target_pairs={{0,8},{8,0},{16,24},{24,16},{1,9},{9,1},{17,25},{25,17},{2,10},{10... | collective-permute-start | bytes 860168 | tf_op jit(solution)/shard_map/ppermute | solution.py:324
  109.1 16.5 %collective-permute-start.25 = (bf16[2,2,40,1792]{3,2,1,0:T(8,128)(2,1)S(1)}, bf16[2,2,40,1792]{3,2,1,0:T(8,128)(2,1)S(1)}, u32[]{:S(2)}, u32[]{:S(2)}) collective-permute-start(bf16[2,2,40,1792]{3,2,1,0:T(8,128)(2,1)S(1)} %get-tuple-element.154), channel_id=1, source_target_pairs={{0,16},{8,24},{16,0},{24,8},{1,17},{9,25},{17,1},{25,9},{2,18},{10... | collective-permute-start | bytes 1720328 | tf_op jit(solution)/shard_map/ppermute | solution.py:324
  110.4 14.1 %collective-permute-start.34 = (bf16[1,40,4096]{2,1,0:T(8,128)(2,1)S(1)}, bf16[1,40,4096]{2,1,0:T(8,128)(2,1)S(1)}, u32[]{:S(2)}, u32[]{:S(2)}) collective-permute-start(bf16[1,40,4096]{2,1,0:T(8,128)(2,1)S(1)} %get-tuple-element.174), channel_id=1, source_target_pairs={{0,2},{1,3},{2,0},{3,1},{4,6},{5,7},{6,4},{7,5},{8,10},{9,11},{10,... | collective-permute-start | bytes 983048 | tf_op jit(solution)/shard_map/ppermute | solution.py:353
  117.6 8.0 %collective-permute-start.33 = (bf16[1,40,4096]{2,1,0:T(8,128)(2,1)S(1)}, bf16[1,40,4096]{2,1,0:T(8,128)(2,1)S(1)}, u32[]{:S(2)}, u32[]{:S(2)}) collective-permute-start(bf16[1,40,4096]{2,1,0:T(8,128)(2,1)S(1)} %get-tuple-element.179), channel_id=1, source_target_pairs={{0,1},{1,0},{2,3},{3,2},{4,5},{5,4},{6,7},{7,6},{8,9},{9,8},{10,11... | collective-permute-start | bytes 983048 | tf_op jit(solution)/shard_map/ppermute | solution.py:324
  118.4 13.1 %collective-permute-start.38 = (bf16[1,40,4096]{2,1,0:T(8,128)(2,1)S(1)}, bf16[1,40,4096]{2,1,0:T(8,128)(2,1)S(1)}, u32[]{:S(2)}, u32[]{:S(2)}) collective-permute-start(bf16[1,40,4096]{2,1,0:T(8,128)(2,1)S(1)} %get-tuple-element.178), channel_id=1, source_target_pairs={{0,2},{1,3},{2,0},{3,1},{4,6},{5,7},{6,4},{7,5},{8,10},{9,11},{10,... | collective-permute-start | bytes 983048 | tf_op jit(solution)/shard_map/ppermute | solution.py:353
  126.0 1.7 %collective-permute-start.35 = (bf16[2,40,1792]{2,1,0:T(8,128)(2,1)S(1)}, bf16[2,40,1792]{2,1,0:T(8,128)(2,1)S(1)}, u32[]{:S(2)}, u32[]{:S(2)}) collective-permute-start(bf16[2,40,1792]{2,1,0:T(8,128)(2,1)S(1)} %get-tuple-element.182.own_ref), channel_id=1, source_target_pairs={{0,8},{8,0},{16,24},{24,16},{1,9},{9,1},{17,25},{25,17},{2,10},{10... | collective-permute-start | bytes 860168 | tf_op jit(solution)/shard_map/ppermute | solution.py:324
  126.0 10.1 %collective-permute-start.36 = (bf16[1,40,4096]{2,1,0:T(8,128)(2,1)S(1)}, bf16[1,40,4096]{2,1,0:T(8,128)(2,1)S(1)}, u32[]{:S(2)}, u32[]{:S(2)}) collective-permute-start(bf16[1,40,4096]{2,1,0:T(8,128)(2,1)S(1)} %get-tuple-element.188), channel_id=1, source_target_pairs={{0,1},{1,0},{2,3},{3,2},{4,5},{5,4},{6,7},{7,6},{8,9},{9,8},{10,11... | collective-permute-start | bytes 983048 | tf_op jit(solution)/shard_map/ppermute | solution.py:324
  126.6 25.1 %collective-permute-start.40 = (bf16[1,40,4096]{2,1,0:T(8,128)(2,1)S(1)}, bf16[1,40,4096]{2,1,0:T(8,128)(2,1)S(1)}, u32[]{:S(2)}, u32[]{:S(2)}) collective-permute-start(bf16[1,40,4096]{2,1,0:T(8,128)(2,1)S(1)} %get-tuple-element.187), channel_id=1, source_target_pairs={{0,4},{1,5},{4,0},{5,1},{2,6},{3,7},{6,2},{7,3},{8,12},{9,13},{12,... | collective-permute-start | bytes 983048 | tf_op jit(solution)/shard_map/ppermute | solution.py:353
  136.3 22.1 %collective-permute-start.39 = (bf16[1,40,4096]{2,1,0:T(8,128)(2,1)S(1)}, bf16[1,40,4096]{2,1,0:T(8,128)(2,1)S(1)}, u32[]{:S(2)}, u32[]{:S(2)}) collective-permute-start(bf16[1,40,4096]{2,1,0:T(8,128)(2,1)S(1)} %get-tuple-element.194), channel_id=1, source_target_pairs={{0,4},{1,5},{4,0},{5,1},{2,6},{3,7},{6,2},{7,3},{8,12},{9,13},{12,... | collective-permute-start | bytes 983048 | tf_op jit(solution)/shard_map/ppermute | solution.py:353
  136.7 16.0 %collective-permute-start.37 = (bf16[2,40,4096]{2,1,0:T(8,128)(2,1)S(1)}, bf16[2,40,4096]{2,1,0:T(8,128)(2,1)S(1)}, u32[]{:S(2)}, u32[]{:S(2)}) collective-permute-start(bf16[2,40,4096]{2,1,0:T(8,128)(2,1)S(1)} %get-tuple-element.189), channel_id=1, source_target_pairs={{0,1},{1,0},{2,3},{3,2},{4,5},{5,4},{6,7},{7,6},{8,9},{9,8},{10,11... | collective-permute-start | bytes 1966088 | tf_op jit(solution)/shard_map/ppermute | solution.py:324
  152.8 5.6 %collective-permute-start.41 = (bf16[40,4096]{1,0:T(8,128)(2,1)S(1)}, bf16[40,4096]{1,0:T(8,128)(2,1)S(1)}, u32[]{:S(2)}, u32[]{:S(2)}) collective-permute-start(bf16[40,4096]{1,0:T(8,128)(2,1)S(1)} %fusion.4), channel_id=1, source_target_pairs={{0,8},{8,0},{16,24},{24,16},{1,9},{9,1},{17,25},{25,17},{2,10},{10... | collective-permute-start | bytes 983048 | tf_op jit(solution)/shard_map/ppermute | solution.py:324

commit v17 on v16

--- a/solution.py
+++ b/solution.py
@@ -8,6 +8,7 @@
 from jax.sharding import PartitionSpec as P
 
 BLOCK = 64
+ROWS = 16
 CORES = 2
 PLANES = 4
 NEXT = ((0, 1), (1, 0), (2, 3), (3, 2))
@@ -65,14 +66,15 @@
         copy.start()
     marks = mask_ref.shape[1]
     owner = lax.broadcasted_iota(jnp.int32, (marks, width), 1) // BLOCK + number * (width // BLOCK)
-    chosen = (owner == lax.broadcasted_iota(jnp.int32, (marks, width), 0)).astype(F32)
-    spread[...] = jnp.dot(mask_ref[...].astype(F32), chosen, preferred_element_type=F32)
+    chosen = (owner == lax.broadcasted_iota(jnp.int32, (marks, width), 0)).astype(BF16)
+    spread[...] = jnp.dot(mask_ref[...].astype(BF16), chosen, preferred_element_type=F32)
     for step, copy in enumerate(copies):
         copy.wait()
         for block in range(step * rows // BLOCK, (step + 1) * rows // BLOCK):
-            part = pl.ds(block * BLOCK, BLOCK)
-            keep = jnp.broadcast_to(spread[pl.ds(block, 1), :], (BLOCK, width))
-            kept_ref[part, :] = kept_ref[part, :] * keep.astype(BF16)
+            keep = jnp.broadcast_to(spread[pl.ds(block, 1), :], (ROWS, width)).astype(BF16)
+            for first in range(block * BLOCK, (block + 1) * BLOCK, ROWS):
+                part = pl.ds(first, ROWS)
+                kept_ref[part, :] = kept_ref[part, :] * keep
 
 
 def masked(weight, mask, rows, core, shares, share, after, hint=0.0):
@@ -409,9 +411,7 @@
     row_stacks = {
         step: [by_row_of_plane(first, step), by_row_of_plane(second, step)] for step in range(1, per_plane)
     }
-    up_kept, last[0] = masked(
-        up_weight, up_mask, tile_of(features, 256), place, 1, lambda core: 0, last + next_stacks[:1], 0.15
-    )
+    last[0] = waited(last + next_stacks[:1], 0.15)
     last[0] = waited([*last, across_stacks[0], *(stacks[0] for stacks in row_stacks.values())], 0.07)
     one_away, last[0] = join(next_stacks, last)
     inner_three, last[0] = join(across_stacks, last + [stacks[1] for stacks in row_stacks.values()])
@@ -429,6 +429,7 @@
         part, last[0] = join(stacks, last)
         parts[0].append(part)
     forward(1, one_away, last)
+    up_kept, last[0] = masked(up_weight, up_mask, tile_of(features, 256), place, 1, lambda core: 0, last)
     multiply_in(0, hint=0)
     exchange(0)
     exchange_near(0)

time: 160 us -> 163 us (1.019)
  waiting for transfers between devices: 55.3 us -> 58.5 us
    ppermute x31, waiting for transfers between devices: 24 us -> 25.6 us  [swap(): lax.ppermute(values, axis, [(place, place ^ step) for place in range(size)])]
  transfers between devices with their start and end apart: 42 -> 42, of which waited for: 19 -> 19; matrix products, arithmetic and copies ran while one was open for 0% -> 0% of each run, Pallas kernels for 37% -> 36%
where the time goes in v17:
time: 163 us
  Pallas kernels  59.5 us (37%)
  waiting for transfers between devices  58.5 us (36%)
  starting transfers between devices  40.6 us (25%)
  other arithmetic  4 us (2%)
    ppermute x11, waiting for transfers between devices, by_plane(): return lax.ppermute(behind(values, after), 'cols', pairs)  32.9 us
    ppermute x31, waiting for transfers between devices, swap(): lax.ppermute(values, axis, [(place, place ^ step) for place in range(size)])  25.6 us
    ppermute x31, starting transfers between devices, swap(): lax.ppermute(values, axis, [(place, place ^ step) for place in range(size)])  25.6 us
    pallas_call x4, Pallas kernels, gate_up(): pl.pallas_call(functools.partial(gate_up_kernel, len(parts), len(after)),...  24.3 us
    pallas_call x4, Pallas kernels, down(): pl.pallas_call(functools.partial(down_kernel, pieces, len(down_kept), len...  15.5 us
    pallas_call x4, Pallas kernels, masked(): pl.pallas_call(functools.partial(mask_kernel, share, rows, len(after)), i...  15.2 us
    ppermute x11, starting transfers between devices, by_plane(): return lax.ppermute(behind(values, after), 'cols', pairs)  15 us
  transfers between devices with their start and end apart: 42, of which 19 were waited for; matrix products, arithmetic and copies ran while one was open for 0% of the time, Pallas kernels for 36%

profile of v17, /device:TPU:0, one launch (start us, length us, event | category | flops | bytes accessed | tf_op | source)
XLA Modules:
  0.0 163.1 jit_solution(15890788103085526375)
XLA Ops:
  0.0 1.3 fusion
  1.3 1.3 fusion.2
  3.3 1.3 collective-permute-done
  5.2 2.9 %collective-permute-start.1 = (bf16[2,1,40,2048]{3,2,1,0:T(8,128)(2,1)S(1)}, bf16[2,1,40,2048]{3,2,1,0:T(8,128)(2,1)S(1)}, u32[]{:S(2)}, u32[]{:S(2)}) collective-permute-start(bf16[2,1,40,2048]{3,2,1,0:T(8,128)(2,1)S(1)} %get-tuple-element.101.refs_2_), channel_id=1, source_target_pairs={{0,16},{8,24},{16,0},{24,8},{1,17},{9,25},{17,1},{25,9},{2,18},{10... | collective-permute-start | bytes 983048 | tf_op jit(solution)/shard_map/ppermute | solution.py:326
  8.1 1.6 %collective-permute-start.6 = (bf16[2,1,40,2048]{3,2,1,0:T(8,128)(2,1)S(1)}, bf16[2,1,40,2048]{3,2,1,0:T(8,128)(2,1)S(1)}, u32[]{:S(2)}, u32[]{:S(2)}) collective-permute-start(bf16[2,1,40,2048]{3,2,1,0:T(8,128)(2,1)S(1)} %get-tuple-element.102.refs_0_), channel_id=1, source_target_pairs={{0,2},{1,3},{2,0},{3,1},{4,6},{5,7},{6,4},{7,5},{8,10},{9,11},{10,... | collective-permute-start | bytes 983048 | tf_op jit(solution)/shard_map/ppermute | solution.py:355
  10.4 1.6 collective-permute-start.2
  12.0 4.1 %collective-permute-done.1.refs_1_ = bf16[2,1,40,2048]{3,2,1,0:T(8,128)(2,1)S(1)} collective-permute-done((bf16[2,1,40,2048]{3,2,1,0:T(8,128)(2,1)S(1)}, bf16[2,1,40,2048]{3,2,1,0:T(8,128)(2,1)S(1)}, u32[]{:S(2)}, u32[]{:S(2)}) %collective-permute-start.1) | collective-permute-done | bytes 327712 | tf_op jit(solution)/shard_map/ppermute | solution.py:326
  16.1 1.8 %collective-permute-start.7 = (bf16[2,1,40,2048]{3,2,1,0:T(8,128)(2,1)S(1)}, bf16[2,1,40,2048]{3,2,1,0:T(8,128)(2,1)S(1)}, u32[]{:S(2)}, u32[]{:S(2)}) collective-permute-start(bf16[2,1,40,2048]{3,2,1,0:T(8,128)(2,1)S(1)} %collective-permute-done.1.refs_1_), channel_id=1, source_target_pairs={{0,2},{1,3},{2,0},{3,1},{4,6},{5,7},{6,4},{7,5},{8,10},{9,11},{10,... | collective-permute-start | bytes 983048 | tf_op jit(solution)/shard_map/ppermute | solution.py:355
  18.6 1.6 collective-permute-start.3
  20.2 3.8 %masked.4 = (bf16[2048,1792]{1,0:T(8,128)(2,1)S(1)}, f32[8,128]{1,0:T(8,128)S(1)}) custom-call(s32[2]{0:T(128)S(1)} %pad_add_fusion.core_ref.place_ref, bf16[2048,1792]{1,0:T(8,128)(2,1)} %weight_ref.4, s32[32,28]{1,0:T(8,128)S(1)} %copy-done.1, f32[8,128]{1,0:T(8,128)S(1)} %get-tuple-element.103.refs_0_), custom_call_target="tpu_custom_call" | custom-call | tf_op jit(solution)/shard_map/masked/pallas_call | solution.py:83
  24.1 1.2 collective-permute-done.7.refs_1_
  25.4 1.9 %collective-permute-done.3.refs_3_.refs_1_ = bf16[2,1,40,2048]{3,2,1,0:T(8,128)(2,1)S(1)} collective-permute-done((bf16[2,1,40,2048]{3,2,1,0:T(8,128)(2,1)S(1)}, bf16[2,1,40,2048]{3,2,1,0:T(8,128)(2,1)S(1)}, u32[]{:S(2)}, u32[]{:S(2)}) %collective-permute-start.3) | collective-permute-done | bytes 327712 | tf_op jit(solution)/shard_map/ppermute | solution.py:326
  27.3 4.4 %collective-permute-start.10 = (bf16[160,2048]{1,0:T(8,128)(2,1)S(1)}, bf16[160,2048]{1,0:T(8,128)(2,1)S(1)}, u32[]{:S(2)}, u32[]{:S(2)}) collective-permute-start(bf16[160,2048]{1,0:T(8,128)(2,1)S(1)} %get-tuple-element.118.refs_0_.mine_ref), channel_id=1, source_target_pairs={{0,6},{1,7},{6,0},{7,1},{8,14},{9,15},{14,8},{15,9},{16,22},{17,23... | collective-permute-start | bytes 1966088 | tf_op jit(solution)/shard_map/ppermute | solution.py:355
  31.8 1.6 collective-permute-start.12
  33.4 3.8 %masked.5 = (bf16[2048,1792]{1,0:T(8,128)(2,1)S(1)}, f32[8,128]{1,0:T(8,128)S(1)}) custom-call(s32[2]{0:T(128)S(1)} %pad_add_fusion.core_ref.place_ref, bf16[2048,1792]{1,0:T(8,128)(2,1)} %weight_ref.5, s32[32,28]{1,0:T(8,128)S(1)} %copy-done.2, f32[8,128]{1,0:T(8,128)S(1)} %get-tuple-element.111.refs_0_), custom_call_target="tpu_custom_call" | custom-call | tf_op jit(solution)/shard_map/masked/pallas_call | solution.py:83
  37.2 6.1 %gate_up.4 = (bf16[2,2,2,40,1792]{4,3,2,1,0:T(8,128)(2,1)S(1)}, bf16[2,2,40,1792]{3,2,1,0:T(8,128)(2,1)S(1)}, bf16[2,2,1,40,1792]{4,3,2,1,0:T(8,128)(2,1)S(1)}, f32[8,128]{1,0:T(8,128)S(1)}) custom-call(bf16[160,2048]{1,0:T(8,128)(2,1)S(1)} %get-tuple-element.118.refs_0_.mine_ref, bf16[160,2048]{1,0:T(8,128)(2,1)S(1)} %get-tuple-element.109.refs_1_, ...), custom_call_target="tpu_custom_call" | custom-call | tf_op jit(solution)/shard_map/gate_up/pallas_call | solution.py:208
  43.9 3.8 %masked.6 = (bf16[1792,2048]{1,0:T(8,128)(2,1)S(1)}, f32[8,128]{1,0:T(8,128)S(1)}) custom-call(s32[2]{0:T(128)S(1)} %pad_add_fusion.core_ref.place_ref, bf16[1792,8192]{1,0:T(8,128)(2,1)} %weight_ref.7, s32[28,128]{1,0:T(8,128)S(1)} %copy-done, f32[8,128]{1,0:T(8,128)S(1)} %get-tuple-element.119.refs_0_), custom_call_target="tpu_custom_call" | custom-call | tf_op jit(solution)/shard_map/masked/pallas_call | solution.py:83
  47.7 3.8 %masked.7 = (bf16[1792,2048]{1,0:T(8,128)(2,1)S(1)}, f32[8,128]{1,0:T(8,128)S(1)}) custom-call(s32[2]{0:T(128)S(1)} %pad_add_fusion.core_ref.place_ref, bf16[1792,8192]{1,0:T(8,128)(2,1)} %weight_ref.7, s32[28,128]{1,0:T(8,128)S(1)} %copy-done, f32[8,128]{1,0:T(8,128)S(1)} %get-tuple-element.120.refs_0_), custom_call_target="tpu_custom_call" | custom-call | tf_op jit(solution)/shard_map/masked/pallas_call | solution.py:83
  53.1 6.1 %gate_up.5 = (bf16[2,2,2,40,1792]{4,3,2,1,0:T(8,128)(2,1)S(1)}, bf16[2,2,40,1792]{3,2,1,0:T(8,128)(2,1)S(1)}, bf16[2,2,1,40,1792]{4,3,2,1,0:T(8,128)(2,1)S(1)}, f32[8,128]{1,0:T(8,128)S(1)}) custom-call(bf16[160,2048]{1,0:T(8,128)(2,1)S(1)} %get-tuple-element.126.refs_0_, bf16[160,2048]{1,0:T(8,128)(2,1)S(1)} %collective-permute-done.12.refs_1_, ...), custom_call_target="tpu_custom_call" | custom-call | flops 4697620480 | tf_op jit(solution)/shard_map/gate_up/pallas_call | solution.py:208
  59.7 1.5 collective-permute-done.13.refs_1_
  62.2 1.6 collective-permute-start.16
  63.7 5.7 %collective-permute-done.11.refs_5_.refs_0_ = bf16[160,2048]{1,0:T(8,128)(2,1)S(1)} collective-permute-done((bf16[160,2048]{1,0:T(8,128)(2,1)S(1)}, bf16[160,2048]{1,0:T(8,128)(2,1)S(1)}, u32[]{:S(2)}, u32[]{:S(2)}) %collective-permute-start.11) | collective-permute-done | bytes 655392 | tf_op jit(solution)/shard_map/ppermute | solution.py:355
  69.4 1.5 collective-permute-start.15
  71.0 6.1 %gate_up.6 = (bf16[2,2,2,40,1792]{4,3,2,1,0:T(8,128)(2,1)S(1)}, bf16[2,2,40,1792]{3,2,1,0:T(8,128)(2,1)S(1)}, bf16[2,2,1,40,1792]{4,3,2,1,0:T(8,128)(2,1)S(1)}, f32[8,128]{1,0:T(8,128)S(1)}) custom-call(bf16[160,2048]{1,0:T(8,128)(2,1)S(1)} %get-tuple-element.136.refs_0_, bf16[160,2048]{1,0:T(8,128)(2,1)S(1)} %collective-permute-done.17.refs_1_, ...), custom_call_target="tpu_custom_call" | custom-call | flops 4697620480 | tf_op jit(solution)/shard_map/gate_up/pallas_call | solution.py:208
  78.0 1.0 collective-permute-done.19.refs_1_
  80.1 1.5 collective-permute-start.23
  81.6 3.9 %down.4 = (bf16[2,40,4096]{2,1,0:T(8,128)(2,1)S(1)}, bf16[2,40,4096]{2,1,0:T(8,128)(2,1)S(1)}, f32[8,128]{1,0:T(8,128)S(1)}) custom-call(bf16[2,40,1792]{2,1,0:T(8,128)(2,1)S(1)} %get-tuple-element.138.own_ref, bf16[2,40,1792]{2,1,0:T(8,128)(2,1)S(1)} %collective-permute-done.18.other_ref, bf16[1792,2048]{1,0:T(8,128)(2,1)S(1)} %get-tuple-element.139.refs_0_, ...), custom_call_target="tpu_custom_call" | custom-call | flops 2348810 | tf_op jit(solution)/shard_map/down/pallas_call | solution.py:250
  85.5 1.0 collective-permute-start.28
  86.5 6.1 %gate_up.7 = (bf16[2,2,2,40,1792]{4,3,2,1,0:T(8,128)(2,1)S(1)}, bf16[2,2,40,1792]{3,2,1,0:T(8,128)(2,1)S(1)}, bf16[1,2,1,40,1792]{4,3,2,1,0:T(8,128)(2,1)S(1)}, ...) custom-call(bf16[160,2048]{1,0:T(8,128)(2,1)S(1)} %collective-permute-done.11.refs_5_.refs_0_, ...), custom_call_target="tpu_custom_call" | custom-call | flops 4697620480 | tf_op jit(solution)/shard_map/gate_up/pallas_call | solution.py:208
  93.2 2.0 %collective-permute-done.23.refs_2_ = bf16[2,2,40,1792]{3,2,1,0:T(8,128)(2,1)S(1)} collective-permute-done((bf16[2,2,40,1792]{3,2,1,0:T(8,128)(2,1)S(1)}, bf16[2,2,40,1792]{3,2,1,0:T(8,128)(2,1)S(1)}, u32[]{:S(2)}, u32[]{:S(2)}) %collective-permute-start.23) | collective-permute-done | bytes 573472 | tf_op jit(solution)/shard_map/ppermute | solution.py:326
  96.2 1.4 collective-permute-start.24
  97.7 3.9 %down.5 = (bf16[1,40,4096]{2,1,0:T(8,128)(2,1)S(1)}, bf16[1,40,4096]{2,1,0:T(8,128)(2,1)S(1)}, bf16[1,40,4096]{2,1,0:T(8,128)(2,1)S(1)}, bf16[1,40,4096]{2,1,0:T(8,128)(2,1)S(1)}, f32[8,128]{1,0:T(8,128)S(1)}) custom-call(bf16[2,40,1792]{2,1,0:T(8,128)(2,1)S(1)} %get-tuple-element.158.own_ref, bf16[2,40,1792]{2,1,0:T(8,128)(2,1)S(1)} %collective-permute-done.27.other_ref, ...), custom_call_target="tpu_custom_call" | custom-call | flops 2348810 | tf_op jit(solution)/shard_map/down/pallas_call | solution.py:250
  102.7 1.4 collective-permute-start.32
  104.1 7.0 %collective-permute-done.29.refs_1_ = bf16[1,40,4096]{2,1,0:T(8,128)(2,1)S(1)} collective-permute-done((bf16[1,40,4096]{2,1,0:T(8,128)(2,1)S(1)}, bf16[1,40,4096]{2,1,0:T(8,128)(2,1)S(1)}, u32[]{:S(2)}, u32[]{:S(2)}) %collective-permute-start.29) | collective-permute-done | bytes 327712 | tf_op jit(solution)/shard_map/ppermute | solution.py:326
  112.1 1.2 collective-permute-start.25
  113.3 1.3 collective-permute-start.34
  114.6 3.9 %down.6 = (bf16[1,40,4096]{2,1,0:T(8,128)(2,1)S(1)}, bf16[1,40,4096]{2,1,0:T(8,128)(2,1)S(1)}, bf16[1,40,4096]{2,1,0:T(8,128)(2,1)S(1)}, bf16[1,40,4096]{2,1,0:T(8,128)(2,1)S(1)}, f32[8,128]{1,0:T(8,128)S(1)}) custom-call(bf16[2,40,1792]{2,1,0:T(8,128)(2,1)S(1)} %get-tuple-element.168.own_ref, bf16[2,40,1792]{2,1,0:T(8,128)(2,1)S(1)} %collective-permute-done.30.other_ref, ...), custom_call_target="tpu_custom_call" | custom-call | flops 2348810 | tf_op jit(solution)/shard_map/down/pallas_call | solution.py:250
  118.5 1.9 %collective-permute-done.32.refs_3_.refs_1_ = bf16[2,40,4096]{2,1,0:T(8,128)(2,1)S(1)} collective-permute-done((bf16[2,40,4096]{2,1,0:T(8,128)(2,1)S(1)}, bf16[2,40,4096]{2,1,0:T(8,128)(2,1)S(1)}, u32[]{:S(2)}, u32[]{:S(2)}) %collective-permute-start.32) | collective-permute-done | bytes 655392 | tf_op jit(solution)/shard_map/ppermute | solution.py:355
  120.5 1.6 collective-permute-start.33
  122.1 1.3 collective-permute-start.38
  123.4 4.1 %collective-permute-done.34.refs_2_ = bf16[1,40,4096]{2,1,0:T(8,128)(2,1)S(1)} collective-permute-done((bf16[1,40,4096]{2,1,0:T(8,128)(2,1)S(1)}, bf16[1,40,4096]{2,1,0:T(8,128)(2,1)S(1)}, u32[]{:S(2)}, u32[]{:S(2)}) %collective-permute-start.34) | collective-permute-done | bytes 327712 | tf_op jit(solution)/shard_map/ppermute | solution.py:355
  128.7 1.5 collective-permute-start.36
  130.9 3.9 %down.7 = (bf16[2,40,4096]{2,1,0:T(8,128)(2,1)S(1)}, bf16[2,40,4096]{2,1,0:T(8,128)(2,1)S(1)}, f32[8,128]{1,0:T(8,128)S(1)}) custom-call(bf16[2,40,1792]{2,1,0:T(8,128)(2,1)S(1)} %get-tuple-element.182.own_ref, bf16[2,40,1792]{2,1,0:T(8,128)(2,1)S(1)} %collective-permute-done.35.other_ref, bf16[1792,2048]{1,0:T(8,128)(2,1)S(1)} %get-tuple-element.139.refs_0_, ...), custom_call_target="tpu_custom_call" | custom-call | flops 2348810 | tf_op jit(solution)/shard_map/down/pallas_call | solution.py:250
  134.9 3.9 %collective-permute-done.36.refs_1_ = bf16[1,40,4096]{2,1,0:T(8,128)(2,1)S(1)} collective-permute-done((bf16[1,40,4096]{2,1,0:T(8,128)(2,1)S(1)}, bf16[1,40,4096]{2,1,0:T(8,128)(2,1)S(1)}, u32[]{:S(2)}, u32[]{:S(2)}) %collective-permute-start.36) | collective-permute-done | bytes 327712 | tf_op jit(solution)/shard_map/ppermute | solution.py:326
  138.9 1.1 collective-permute-start.39
  140.0 1.1 collective-permute-start.37
  141.1 14.2 %collective-permute-done.40.refs_0_ = bf16[1,40,4096]{2,1,0:T(8,128)(2,1)S(1)} collective-permute-done((bf16[1,40,4096]{2,1,0:T(8,128)(2,1)S(1)}, bf16[1,40,4096]{2,1,0:T(8,128)(2,1)S(1)}, u32[]{:S(2)}, u32[]{:S(2)}) %collective-permute-start.40) | collective-permute-done | bytes 327712 | tf_op jit(solution)/shard_map/ppermute | solution.py:355
  156.2 5.8 %collective-permute-done.39 = bf16[1,40,4096]{2,1,0:T(8,128)(2,1)S(1)} collective-permute-done((bf16[1,40,4096]{2,1,0:T(8,128)(2,1)S(1)}, bf16[1,40,4096]{2,1,0:T(8,128)(2,1)S(1)}, u32[]{:S(2)}, u32[]{:S(2)}) %collective-permute-start.39) | collective-permute-done | bytes 327712 | tf_op jit(solution)/shard_map/ppermute | solution.py:355
  (89 shorter events, 16.4 us)
Async XLA Ops:
  2.7 17.5 %copy-start.1 = (s32[32,28]{1,0:T(8,128)S(1)}, s32[32,28]{1,0:T(8,128)}, u32[]{:S(2)}) copy-start(s32[32,28]{1,0:T(8,128)} %mask_ref.4) | copy-start | bytes 10756
  2.8 1.8 %collective-permute-start = (bf16[2,40,2048]{2,1,0:T(8,128)(2,1)S(1)}, bf16[2,40,2048]{2,1,0:T(8,128)(2,1)S(1)}, u32[]{:S(2)}, u32[]{:S(2)}) collective-permute-start(bf16[2,40,2048]{2,1,0:T(8,128)(2,1)S(1)} %pad_maximum_fusion.1), channel_id=1, source_target_pairs={{0,8},{8,0},{16,24},{24,16},{1,9},{9,1},{17,25},{25,17},{2,10},{10... | collective-permute-start | bytes 983048 | tf_op jit(solution)/shard_map/ppermute | solution.py:326
  5.2 10.9 %collective-permute-start.1 = (bf16[2,1,40,2048]{3,2,1,0:T(8,128)(2,1)S(1)}, bf16[2,1,40,2048]{3,2,1,0:T(8,128)(2,1)S(1)}, u32[]{:S(2)}, u32[]{:S(2)}) collective-permute-start(bf16[2,1,40,2048]{3,2,1,0:T(8,128)(2,1)S(1)} %get-tuple-element.101.refs_2_), channel_id=1, source_target_pairs={{0,16},{8,24},{16,0},{24,8},{1,17},{9,25},{17,1},{25,9},{2,18},{10... | collective-permute-start | bytes 983048 | tf_op jit(solution)/shard_map/ppermute | solution.py:326
  8.1 10.5 %collective-permute-start.6 = (bf16[2,1,40,2048]{3,2,1,0:T(8,128)(2,1)S(1)}, bf16[2,1,40,2048]{3,2,1,0:T(8,128)(2,1)S(1)}, u32[]{:S(2)}, u32[]{:S(2)}) collective-permute-start(bf16[2,1,40,2048]{3,2,1,0:T(8,128)(2,1)S(1)} %get-tuple-element.102.refs_0_), channel_id=1, source_target_pairs={{0,2},{1,3},{2,0},{3,1},{4,6},{5,7},{6,4},{7,5},{8,10},{9,11},{10,... | collective-permute-start | bytes 983048 | tf_op jit(solution)/shard_map/ppermute | solution.py:355
  9.7 14.4 %collective-permute-start.4 = (bf16[2,1,40,2048]{3,2,1,0:T(8,128)(2,1)S(1)}, bf16[2,1,40,2048]{3,2,1,0:T(8,128)(2,1)S(1)}, u32[]{:S(2)}, u32[]{:S(2)}) collective-permute-start(bf16[2,1,40,2048]{3,2,1,0:T(8,128)(2,1)S(1)} %get-tuple-element.102.refs_0_), channel_id=1, source_target_pairs={{2,4},{3,5},{4,2},{5,3},{10,12},{11,13},{12,10},{13,11},{18,20},{1... | collective-permute-start | bytes 983048 | tf_op jit(solution)/shard_map/ppermute | solution.py:355
  10.4 13.7 %collective-permute-start.2 = (bf16[2,1,40,2048]{3,2,1,0:T(8,128)(2,1)S(1)}, bf16[2,1,40,2048]{3,2,1,0:T(8,128)(2,1)S(1)}, u32[]{:S(2)}, u32[]{:S(2)}) collective-permute-start(bf16[2,1,40,2048]{3,2,1,0:T(8,128)(2,1)S(1)} %get-tuple-element.102.refs_0_), channel_id=1, source_target_pairs={{0,1},{1,0},{2,3},{3,2},{4,5},{5,4},{6,7},{7,6},{8,9},{9,8},{10,11... | collective-permute-start | bytes 983048 | tf_op jit(solution)/shard_map/ppermute | solution.py:326
  16.1 9.2 %collective-permute-start.7 = (bf16[2,1,40,2048]{3,2,1,0:T(8,128)(2,1)S(1)}, bf16[2,1,40,2048]{3,2,1,0:T(8,128)(2,1)S(1)}, u32[]{:S(2)}, u32[]{:S(2)}) collective-permute-start(bf16[2,1,40,2048]{3,2,1,0:T(8,128)(2,1)S(1)} %collective-permute-done.1.refs_1_), channel_id=1, source_target_pairs={{0,2},{1,3},{2,0},{3,1},{4,6},{5,7},{6,4},{7,5},{8,10},{9,11},{10,... | collective-permute-start | bytes 983048 | tf_op jit(solution)/shard_map/ppermute | solution.py:355
  17.9 7.5 %collective-permute-start.5 = (bf16[2,1,40,2048]{3,2,1,0:T(8,128)(2,1)S(1)}, bf16[2,1,40,2048]{3,2,1,0:T(8,128)(2,1)S(1)}, u32[]{:S(2)}, u32[]{:S(2)}) collective-permute-start(bf16[2,1,40,2048]{3,2,1,0:T(8,128)(2,1)S(1)} %collective-permute-done.1.refs_1_), channel_id=1, source_target_pairs={{2,4},{3,5},{4,2},{5,3},{10,12},{11,13},{12,10},{13,11},{18,20},{1... | collective-permute-start | bytes 983048 | tf_op jit(solution)/shard_map/ppermute | solution.py:355
  18.6 8.7 %collective-permute-start.3 = (bf16[2,1,40,2048]{3,2,1,0:T(8,128)(2,1)S(1)}, bf16[2,1,40,2048]{3,2,1,0:T(8,128)(2,1)S(1)}, u32[]{:S(2)}, u32[]{:S(2)}) collective-permute-start(bf16[2,1,40,2048]{3,2,1,0:T(8,128)(2,1)S(1)} %collective-permute-done.1.refs_1_), channel_id=1, source_target_pairs={{0,1},{1,0},{2,3},{3,2},{4,5},{5,4},{6,7},{7,6},{8,9},{9,8},{10,11... | collective-permute-start | bytes 983048 | tf_op jit(solution)/shard_map/ppermute | solution.py:326
  24.1 9.3 %copy-start.2 = (s32[32,28]{1,0:T(8,128)S(1)}, s32[32,28]{1,0:T(8,128)}, u32[]{:S(2)}) copy-start(s32[32,28]{1,0:T(8,128)} %mask_ref.5) | copy-start | bytes 10756
  27.3 24.2 %collective-permute-start.10 = (bf16[160,2048]{1,0:T(8,128)(2,1)S(1)}, bf16[160,2048]{1,0:T(8,128)(2,1)S(1)}, u32[]{:S(2)}, u32[]{:S(2)}) collective-permute-start(bf16[160,2048]{1,0:T(8,128)(2,1)S(1)} %get-tuple-element.118.refs_0_.mine_ref), channel_id=1, source_target_pairs={{0,6},{1,7},{6,0},{7,1},{8,14},{9,15},{14,8},{15,9},{16,22},{17,23... | collective-permute-start | bytes 1966088 | tf_op jit(solution)/shard_map/ppermute | solution.py:355
  31.8 20.6 %collective-permute-start.12 = (bf16[160,2048]{1,0:T(8,128)(2,1)S(1)}, bf16[160,2048]{1,0:T(8,128)(2,1)S(1)}, u32[]{:S(2)}, u32[]{:S(2)}) collective-permute-start(bf16[160,2048]{1,0:T(8,128)(2,1)S(1)} %get-tuple-element.126.refs_0_), channel_id=1, source_target_pairs={{0,1},{1,0},{2,3},{3,2},{4,5},{5,4},{6,7},{7,6},{8,9},{9,8},{10,11... | collective-permute-start | bytes 1966088 | tf_op jit(solution)/shard_map/ppermute | solution.py:326
  37.2 6.7 %copy-start = (s32[28,128]{1,0:T(8,128)S(1)}, s32[28,128]{1,0:T(8,128)}, u32[]{:S(2)}) copy-start(s32[28,128]{1,0:T(8,128)} %mask_ref.7) | copy-start | bytes 43012
  43.3 8.9 %collective-permute-start.8 = (bf16[2,2,40,1792]{3,2,1,0:T(8,128)(2,1)S(1)}, bf16[2,2,40,1792]{3,2,1,0:T(8,128)(2,1)S(1)}, u32[]{:S(2)}, u32[]{:S(2)}) collective-permute-start(bf16[2,2,40,1792]{3,2,1,0:T(8,128)(2,1)S(1)} %get-tuple-element.115), channel_id=1, source_target_pairs={{0,8},{8,0},{16,24},{24,16},{1,9},{9,1},{17,25},{25,17},{2,10},{10... | collective-permute-start | bytes 1720328 | tf_op jit(solution)/shard_map/ppermute | solution.py:326
  43.4 8.8 %collective-permute-start.9 = (bf16[2,2,1,40,1792]{4,3,2,1,0:T(8,128)(2,1)S(1)}, bf16[2,2,1,40,1792]{4,3,2,1,0:T(8,128)(2,1)S(1)}, u32[]{:S(2)}, u32[]{:S(2)}) collective-permute-start(bf16[2,2,1,40,1792]{4,3,2,1,0:T(8,128)(2,1)S(1)} %get-tuple-element.116), channel_id=1, source_target_pairs={{0,8},{8,0},{16,24},{24,16},{1,9},{9,1},{17,25},{25,17},{2,10},{10... | collective-permute-start | bytes 1720328 | tf_op jit(solution)/shard_map/ppermute | solution.py:326
  52.4 18.5 %collective-permute-start.17 = (bf16[160,2048]{1,0:T(8,128)(2,1)S(1)}, bf16[160,2048]{1,0:T(8,128)(2,1)S(1)}, u32[]{:S(2)}, u32[]{:S(2)}) collective-permute-start(bf16[160,2048]{1,0:T(8,128)(2,1)S(1)} %get-tuple-element.136.refs_0_), channel_id=1, source_target_pairs={{0,1},{1,0},{2,3},{3,2},{4,5},{5,4},{6,7},{7,6},{8,9},{9,8},{10,11... | collective-permute-start | bytes 1966088 | tf_op jit(solution)/shard_map/ppermute | solution.py:326
  53.0 16.5 %collective-permute-start.11 = (bf16[160,2048]{1,0:T(8,128)(2,1)S(1)}, bf16[160,2048]{1,0:T(8,128)(2,1)S(1)}, u32[]{:S(2)}, u32[]{:S(2)}) collective-permute-start(bf16[160,2048]{1,0:T(8,128)(2,1)S(1)} %get-tuple-element.124), channel_id=1, source_target_pairs={{0,4},{1,5},{4,6},{5,7},{6,2},{7,3},{2,0},{3,1},{8,12},{9,13},{12,... | collective-permute-start | bytes 1966088 | tf_op jit(solution)/shard_map/ppermute | solution.py:355
  59.2 2.0 %collective-permute-start.13 = (bf16[2,2,1,40,1792]{4,3,2,1,0:T(8,128)(2,1)S(1)}, bf16[2,2,1,40,1792]{4,3,2,1,0:T(8,128)(2,1)S(1)}, u32[]{:S(2)}, u32[]{:S(2)}) collective-permute-start(bf16[2,2,1,40,1792]{4,3,2,1,0:T(8,128)(2,1)S(1)} %get-tuple-element.129), channel_id=1, source_target_pairs={{0,8},{8,0},{16,24},{24,16},{1,9},{9,1},{17,25},{25,17},{2,10},{10... | collective-permute-start | bytes 1720328 | tf_op jit(solution)/shard_map/ppermute | solution.py:326
  59.2 2.8 %collective-permute-start.14 = (bf16[2,2,40,1792]{3,2,1,0:T(8,128)(2,1)S(1)}, bf16[2,2,40,1792]{3,2,1,0:T(8,128)(2,1)S(1)}, u32[]{:S(2)}, u32[]{:S(2)}) collective-permute-start(bf16[2,2,40,1792]{3,2,1,0:T(8,128)(2,1)S(1)} %get-tuple-element.131), channel_id=1, source_target_pairs={{0,8},{8,0},{16,24},{24,16},{1,9},{9,1},{17,25},{25,17},{2,10},{10... | collective-permute-start | bytes 1720328 | tf_op jit(solution)/shard_map/ppermute | solution.py:326
  62.2 15.4 %collective-permute-start.16 = (bf16[2,2,40,1792]{3,2,1,0:T(8,128)(2,1)S(1)}, bf16[2,2,40,1792]{3,2,1,0:T(8,128)(2,1)S(1)}, u32[]{:S(2)}, u32[]{:S(2)}) collective-permute-start(bf16[2,2,40,1792]{3,2,1,0:T(8,128)(2,1)S(1)} %get-tuple-element.134), channel_id=1, source_target_pairs={{0,16},{8,24},{16,0},{24,8},{1,17},{9,25},{17,1},{25,9},{2,18},{10... | collective-permute-start | bytes 1720328 | tf_op jit(solution)/shard_map/ppermute | solution.py:326
  69.4 16.0 %collective-permute-start.15 = (bf16[160,2048]{1,0:T(8,128)(2,1)S(1)}, bf16[160,2048]{1,0:T(8,128)(2,1)S(1)}, u32[]{:S(2)}, u32[]{:S(2)}) collective-permute-start(bf16[160,2048]{1,0:T(8,128)(2,1)S(1)} %collective-permute-done.11.refs_5_.refs_0_), channel_id=1, source_target_pairs={{0,1},{1,0},{2,3},{3,2},{4,5},{5,4},{6,7},{7,6},{8,9},{9,8},{10,11... | collective-permute-start | bytes 1966088 | tf_op jit(solution)/shard_map/ppermute | solution.py:326
  77.0 2.0 %collective-permute-start.19 = (bf16[2,2,1,40,1792]{4,3,2,1,0:T(8,128)(2,1)S(1)}, bf16[2,2,1,40,1792]{4,3,2,1,0:T(8,128)(2,1)S(1)}, u32[]{:S(2)}, u32[]{:S(2)}) collective-permute-start(bf16[2,2,1,40,1792]{4,3,2,1,0:T(8,128)(2,1)S(1)} %get-tuple-element.142), channel_id=1, source_target_pairs={{0,8},{8,0},{16,24},{24,16},{1,9},{9,1},{17,25},{25,17},{2,10},{10... | collective-permute-start | bytes 1720328 | tf_op jit(solution)/shard_map/ppermute | solution.py:326
  77.1 2.8 %collective-permute-start.20 = (bf16[2,2,40,1792]{3,2,1,0:T(8,128)(2,1)S(1)}, bf16[2,2,40,1792]{3,2,1,0:T(8,128)(2,1)S(1)}, u32[]{:S(2)}, u32[]{:S(2)}) collective-permute-start(bf16[2,2,40,1792]{3,2,1,0:T(8,128)(2,1)S(1)} %get-tuple-element.144), channel_id=1, source_target_pairs={{0,8},{8,0},{16,24},{24,16},{1,9},{9,1},{17,25},{25,17},{2,10},{10... | collective-permute-start | bytes 1720328 | tf_op jit(solution)/shard_map/ppermute | solution.py:326
  77.9 3.7 %collective-permute-start.18 = (bf16[2,40,1792]{2,1,0:T(8,128)(2,1)S(1)}, bf16[2,40,1792]{2,1,0:T(8,128)(2,1)S(1)}, u32[]{:S(2)}, u32[]{:S(2)}) collective-permute-start(bf16[2,40,1792]{2,1,0:T(8,128)(2,1)S(1)} %get-tuple-element.138.own_ref), channel_id=1, source_target_pairs={{0,8},{8,0},{16,24},{24,16},{1,9},{9,1},{17,25},{25,17},{2,10},{10... | collective-permute-start | bytes 860168 | tf_op jit(solution)/shard_map/ppermute | solution.py:326
  80.1 15.1 %collective-permute-start.23 = (bf16[2,2,40,1792]{3,2,1,0:T(8,128)(2,1)S(1)}, bf16[2,2,40,1792]{3,2,1,0:T(8,128)(2,1)S(1)}, u32[]{:S(2)}, u32[]{:S(2)}) collective-permute-start(bf16[2,2,40,1792]{3,2,1,0:T(8,128)(2,1)S(1)} %get-tuple-element.150), channel_id=1, source_target_pairs={{0,16},{8,24},{16,0},{24,8},{1,17},{9,25},{17,1},{25,9},{2,18},{10... | collective-permute-start | bytes 1720328 | tf_op jit(solution)/shard_map/ppermute | solution.py:326
  85.5 16.5 %collective-permute-start.28 = (bf16[2,40,4096]{2,1,0:T(8,128)(2,1)S(1)}, bf16[2,40,4096]{2,1,0:T(8,128)(2,1)S(1)}, u32[]{:S(2)}, u32[]{:S(2)}) collective-permute-start(bf16[2,40,4096]{2,1,0:T(8,128)(2,1)S(1)} %get-tuple-element.162), channel_id=1, source_target_pairs={{0,1},{1,0},{2,3},{3,2},{4,5},{5,4},{6,7},{7,6},{8,9},{9,8},{10,11... | collective-permute-start | bytes 1966088 | tf_op jit(solution)/shard_map/ppermute | solution.py:326
  92.6 2.9 %collective-permute-start.21 = (bf16[1,2,1,40,1792]{4,3,2,1,0:T(8,128)(2,1)S(1)}, bf16[1,2,1,40,1792]{4,3,2,1,0:T(8,128)(2,1)S(1)}, u32[]{:S(2)}, u32[]{:S(2)}) collective-permute-start(bf16[1,2,1,40,1792]{4,3,2,1,0:T(8,128)(2,1)S(1)} %get-tuple-element.148), channel_id=1, source_target_pairs={{0,8},{8,0},{16,24},{24,16},{1,9},{9,1},{17,25},{25,17},{2,10},{10... | collective-permute-start | bytes 860168 | tf_op jit(solution)/shard_map/ppermute | solution.py:326
  92.7 2.8 %collective-permute-start.22 = (bf16[1,2,1,40,1792]{4,3,2,1,0:T(8,128)(2,1)S(1)}, bf16[1,2,1,40,1792]{4,3,2,1,0:T(8,128)(2,1)S(1)}, u32[]{:S(2)}, u32[]{:S(2)}) collective-permute-start(bf16[1,2,1,40,1792]{4,3,2,1,0:T(8,128)(2,1)S(1)} %get-tuple-element.149), channel_id=1, source_target_pairs={{0,8},{8,0},{16,24},{24,16},{1,9},{9,1},{17,25},{25,17},{2,10},{10... | collective-permute-start | bytes 860168 | tf_op jit(solution)/shard_map/ppermute | solution.py:326
  95.4 2.2 %collective-permute-start.27 = (bf16[2,40,1792]{2,1,0:T(8,128)(2,1)S(1)}, bf16[2,40,1792]{2,1,0:T(8,128)(2,1)S(1)}, u32[]{:S(2)}, u32[]{:S(2)}) collective-permute-start(bf16[2,40,1792]{2,1,0:T(8,128)(2,1)S(1)} %get-tuple-element.158.own_ref), channel_id=1, source_target_pairs={{0,8},{8,0},{16,24},{24,16},{1,9},{9,1},{17,25},{25,17},{2,10},{10... | collective-permute-start | bytes 860168 | tf_op jit(solution)/shard_map/ppermute | solution.py:326
  95.7 16.0 %collective-permute-start.26 = (bf16[2,2,40,1792]{3,2,1,0:T(8,128)(2,1)S(1)}, bf16[2,2,40,1792]{3,2,1,0:T(8,128)(2,1)S(1)}, u32[]{:S(2)}, u32[]{:S(2)}) collective-permute-start(bf16[2,2,40,1792]{3,2,1,0:T(8,128)(2,1)S(1)} %get-tuple-element.157), channel_id=1, source_target_pairs={{0,8},{8,0},{16,24},{24,16},{1,9},{9,1},{17,25},{25,17},{2,10},{10... | collective-permute-start | bytes 1720328 | tf_op jit(solution)/shard_map/ppermute | solution.py:326
  96.2 15.5 %collective-permute-start.24 = (bf16[2,2,40,1792]{3,2,1,0:T(8,128)(2,1)S(1)}, bf16[2,2,40,1792]{3,2,1,0:T(8,128)(2,1)S(1)}, u32[]{:S(2)}, u32[]{:S(2)}) collective-permute-start(bf16[2,2,40,1792]{3,2,1,0:T(8,128)(2,1)S(1)} %get-tuple-element.153), channel_id=1, source_target_pairs={{0,16},{8,24},{16,0},{24,8},{1,17},{9,25},{17,1},{25,9},{2,18},{10... | collective-permute-start | bytes 1720328 | tf_op jit(solution)/shard_map/ppermute | solution.py:326
  102.0 9.0 %collective-permute-start.29 = (bf16[1,40,4096]{2,1,0:T(8,128)(2,1)S(1)}, bf16[1,40,4096]{2,1,0:T(8,128)(2,1)S(1)}, u32[]{:S(2)}, u32[]{:S(2)}) collective-permute-start(bf16[1,40,4096]{2,1,0:T(8,128)(2,1)S(1)} %get-tuple-element.163), channel_id=1, source_target_pairs={{0,1},{1,0},{2,3},{3,2},{4,5},{5,4},{6,7},{7,6},{8,9},{9,8},{10,11... | collective-permute-start | bytes 983048 | tf_op jit(solution)/shard_map/ppermute | solution.py:326
  102.7 17.7 %collective-permute-start.32 = (bf16[2,40,4096]{2,1,0:T(8,128)(2,1)S(1)}, bf16[2,40,4096]{2,1,0:T(8,128)(2,1)S(1)}, u32[]{:S(2)}, u32[]{:S(2)}) collective-permute-start(bf16[2,40,4096]{2,1,0:T(8,128)(2,1)S(1)} %get-tuple-element.177), channel_id=1, source_target_pairs={{0,2},{1,3},{2,0},{3,1},{4,6},{5,7},{6,4},{7,5},{8,10},{9,11},{10,... | collective-permute-start | bytes 1966088 | tf_op jit(solution)/shard_map/ppermute | solution.py:355
  111.1 9.3 %collective-permute-start.31 = (bf16[1,40,4096]{2,1,0:T(8,128)(2,1)S(1)}, bf16[1,40,4096]{2,1,0:T(8,128)(2,1)S(1)}, u32[]{:S(2)}, u32[]{:S(2)}) collective-permute-start(bf16[1,40,4096]{2,1,0:T(8,128)(2,1)S(1)} %get-tuple-element.175), channel_id=1, source_target_pairs={{0,1},{1,0},{2,3},{3,2},{4,5},{5,4},{6,7},{7,6},{8,9},{9,8},{10,11... | collective-permute-start | bytes 983048 | tf_op jit(solution)/shard_map/ppermute | solution.py:326
  112.0 2.6 %collective-permute-start.30 = (bf16[2,40,1792]{2,1,0:T(8,128)(2,1)S(1)}, bf16[2,40,1792]{2,1,0:T(8,128)(2,1)S(1)}, u32[]{:S(2)}, u32[]{:S(2)}) collective-permute-start(bf16[2,40,1792]{2,1,0:T(8,128)(2,1)S(1)} %get-tuple-element.168.own_ref), channel_id=1, source_target_pairs={{0,8},{8,0},{16,24},{24,16},{1,9},{9,1},{17,25},{25,17},{2,10},{10... | collective-permute-start | bytes 860168 | tf_op jit(solution)/shard_map/ppermute | solution.py:326
  112.1 16.2 %collective-permute-start.25 = (bf16[2,2,40,1792]{3,2,1,0:T(8,128)(2,1)S(1)}, bf16[2,2,40,1792]{3,2,1,0:T(8,128)(2,1)S(1)}, u32[]{:S(2)}, u32[]{:S(2)}) collective-permute-start(bf16[2,2,40,1792]{3,2,1,0:T(8,128)(2,1)S(1)} %get-tuple-element.154), channel_id=1, source_target_pairs={{0,16},{8,24},{16,0},{24,8},{1,17},{9,25},{17,1},{25,9},{2,18},{10... | collective-permute-start | bytes 1720328 | tf_op jit(solution)/shard_map/ppermute | solution.py:326
  113.3 14.2 %collective-permute-start.34 = (bf16[1,40,4096]{2,1,0:T(8,128)(2,1)S(1)}, bf16[1,40,4096]{2,1,0:T(8,128)(2,1)S(1)}, u32[]{:S(2)}, u32[]{:S(2)}) collective-permute-start(bf16[1,40,4096]{2,1,0:T(8,128)(2,1)S(1)} %get-tuple-element.174), channel_id=1, source_target_pairs={{0,2},{1,3},{2,0},{3,1},{4,6},{5,7},{6,4},{7,5},{8,10},{9,11},{10,... | collective-permute-start | bytes 983048 | tf_op jit(solution)/shard_map/ppermute | solution.py:355
  120.5 7.7 %collective-permute-start.33 = (bf16[1,40,4096]{2,1,0:T(8,128)(2,1)S(1)}, bf16[1,40,4096]{2,1,0:T(8,128)(2,1)S(1)}, u32[]{:S(2)}, u32[]{:S(2)}) collective-permute-start(bf16[1,40,4096]{2,1,0:T(8,128)(2,1)S(1)} %get-tuple-element.179), channel_id=1, source_target_pairs={{0,1},{1,0},{2,3},{3,2},{4,5},{5,4},{6,7},{7,6},{8,9},{9,8},{10,11... | collective-permute-start | bytes 983048 | tf_op jit(solution)/shard_map/ppermute | solution.py:326
  122.1 12.7 %collective-permute-start.38 = (bf16[1,40,4096]{2,1,0:T(8,128)(2,1)S(1)}, bf16[1,40,4096]{2,1,0:T(8,128)(2,1)S(1)}, u32[]{:S(2)}, u32[]{:S(2)}) collective-permute-start(bf16[1,40,4096]{2,1,0:T(8,128)(2,1)S(1)} %get-tuple-element.178), channel_id=1, source_target_pairs={{0,2},{1,3},{2,0},{3,1},{4,6},{5,7},{6,4},{7,5},{8,10},{9,11},{10,... | collective-permute-start | bytes 983048 | tf_op jit(solution)/shard_map/ppermute | solution.py:355
  128.6 2.3 %collective-permute-start.35 = (bf16[2,40,1792]{2,1,0:T(8,128)(2,1)S(1)}, bf16[2,40,1792]{2,1,0:T(8,128)(2,1)S(1)}, u32[]{:S(2)}, u32[]{:S(2)}) collective-permute-start(bf16[2,40,1792]{2,1,0:T(8,128)(2,1)S(1)} %get-tuple-element.182.own_ref), channel_id=1, source_target_pairs={{0,8},{8,0},{16,24},{24,16},{1,9},{9,1},{17,25},{25,17},{2,10},{10... | collective-permute-start | bytes 860168 | tf_op jit(solution)/shard_map/ppermute | solution.py:326
  128.7 10.1 %collective-permute-start.36 = (bf16[1,40,4096]{2,1,0:T(8,128)(2,1)S(1)}, bf16[1,40,4096]{2,1,0:T(8,128)(2,1)S(1)}, u32[]{:S(2)}, u32[]{:S(2)}) collective-permute-start(bf16[1,40,4096]{2,1,0:T(8,128)(2,1)S(1)} %get-tuple-element.188), channel_id=1, source_target_pairs={{0,1},{1,0},{2,3},{3,2},{4,5},{5,4},{6,7},{7,6},{8,9},{9,8},{10,11... | collective-permute-start | bytes 983048 | tf_op jit(solution)/shard_map/ppermute | solution.py:326
  130.2 25.0 %collective-permute-start.40 = (bf16[1,40,4096]{2,1,0:T(8,128)(2,1)S(1)}, bf16[1,40,4096]{2,1,0:T(8,128)(2,1)S(1)}, u32[]{:S(2)}, u32[]{:S(2)}) collective-permute-start(bf16[1,40,4096]{2,1,0:T(8,128)(2,1)S(1)} %get-tuple-element.187), channel_id=1, source_target_pairs={{0,4},{1,5},{4,0},{5,1},{2,6},{3,7},{6,2},{7,3},{8,12},{9,13},{12,... | collective-permute-start | bytes 983048 | tf_op jit(solution)/shard_map/ppermute | solution.py:355
  138.9 23.1 %collective-permute-start.39 = (bf16[1,40,4096]{2,1,0:T(8,128)(2,1)S(1)}, bf16[1,40,4096]{2,1,0:T(8,128)(2,1)S(1)}, u32[]{:S(2)}, u32[]{:S(2)}) collective-permute-start(bf16[1,40,4096]{2,1,0:T(8,128)(2,1)S(1)} %get-tuple-element.194), channel_id=1, source_target_pairs={{0,4},{1,5},{4,0},{5,1},{2,6},{3,7},{6,2},{7,3},{8,12},{9,13},{12,... | collective-permute-start | bytes 983048 | tf_op jit(solution)/shard_map/ppermute | solution.py:355
  140.0 16.0 %collective-permute-start.37 = (bf16[2,40,4096]{2,1,0:T(8,128)(2,1)S(1)}, bf16[2,40,4096]{2,1,0:T(8,128)(2,1)S(1)}, u32[]{:S(2)}, u32[]{:S(2)}) collective-permute-start(bf16[2,40,4096]{2,1,0:T(8,128)(2,1)S(1)} %get-tuple-element.189), channel_id=1, source_target_pairs={{0,1},{1,0},{2,3},{3,2},{4,5},{5,4},{6,7},{7,6},{8,9},{9,8},{10,11... | collective-permute-start | bytes 1966088 | tf_op jit(solution)/shard_map/ppermute | solution.py:326
  156.1 5.9 %collective-permute-start.41 = (bf16[40,4096]{1,0:T(8,128)(2,1)S(1)}, bf16[40,4096]{1,0:T(8,128)(2,1)S(1)}, u32[]{:S(2)}, u32[]{:S(2)}) collective-permute-start(bf16[40,4096]{1,0:T(8,128)(2,1)S(1)} %fusion.4), channel_id=1, source_target_pairs={{0,8},{8,0},{16,24},{24,16},{1,9},{9,1},{17,25},{25,17},{2,10},{10... | collective-permute-start | bytes 983048 | tf_op jit(solution)/shard_map/ppermute | solution.py:326

commit v18 on v16

--- a/solution.py
+++ b/solution.py
@@ -142,22 +142,22 @@
     return rearranged(join_kernel, "join", (rows, stacks[0].shape[3]), stacks, after, hint)
 
 
-def pick_kernel(after_count, place_ref, inner_three_ref, outer_three_ref, mine_ref, *refs):
+def pick_kernel(after_count, side_ref, inner_three_ref, outer_three_ref, mine_ref, *refs):
     three_ref, passed_ref, token_ref = refs[after_count:]
     token_ref[...] = jnp.zeros_like(token_ref)
 
-    @pl.when(place_ref[1] == 1)
+    @pl.when(side_ref[0] == 1)
     def _():
         three_ref[...] = inner_three_ref[...]
         passed_ref[...] = inner_three_ref[...]
 
-    @pl.when(place_ref[1] == 0)
+    @pl.when(side_ref[0] == 0)
     def _():
         three_ref[...] = outer_three_ref[...]
         passed_ref[...] = mine_ref[...]
 
 
-def pick(place, inner_three, outer_three, mine, after):
+def pick(side, inner_three, outer_three, mine, after):
     return pl.pallas_call(
         functools.partial(pick_kernel, len(after)),
         in_specs=[pl.BlockSpec(memory_space=pltpu.SMEM)] + [INSIDE] * 3 + [ANYWHERE] * len(after),
@@ -166,7 +166,7 @@
         compiler_params=pltpu.CompilerParams(vmem_limit_bytes=VMEM // 2),
         cost_estimate=as_if(8),
         name="pick",
-    )(place, inner_three, outer_three, mine, *after)
+    )(side, inner_three, outer_three, mine, *after)
 
 
 def resident(values):
@@ -331,7 +331,8 @@
     row = lax.axis_index("rows")
     core = row % CORES
     inner = (lax.axis_index("cols") // per_plane) % (PLANES - 1) != 0
-    place = jnp.stack([core, inner.astype(core.dtype)])
+    place = jnp.reshape(core, (1,)).astype(jnp.int32)
+    side = jnp.reshape(inner, (1,)).astype(jnp.int32)
 
     normed = rms_normed(tokens, norm_gain)
     def block(step):
@@ -339,7 +340,7 @@
 
     from_core = swap(jnp.stack([block(chip * CORES + 1) for chip in range(chips)]), "rows", row_count, 1)
     to_chips_rows = [stack([block(chip * CORES), from_core[chip]], [])[0] for chip in range(1, chips)]
-    first, token = stack([block(0), from_core[0]], to_chips_rows[:1])
+    first, token = stack([block(0), from_core[0]], [*to_chips_rows[:1], side])
     gate_kept, token = masked(gate_weight, gate_mask, tile_of(features, 256), place, 1, lambda core: 0, [token])
     second = [swap(part, "rows", row_count, (chip + 1) * CORES) for chip, part in enumerate(to_chips_rows)]
     second = jnp.concatenate(second, 1) if len(second) > 1 else second[0]
@@ -414,7 +415,7 @@
     )
     last[0] = waited([*last, across_stacks[0], *(stacks[0] for stacks in row_stacks.values())], 0.07)
     one_away, last[0] = join(next_stacks, last)
-    inner_three, last[0] = join(across_stacks, last + [stacks[1] for stacks in row_stacks.values()])
+    inner_three, last[0] = join(across_stacks, last)
     outer_three = by_plane(mine, AROUND, last)
     down_kept = []
 
@@ -429,12 +430,11 @@
         part, last[0] = join(stacks, last)
         parts[0].append(part)
     forward(1, one_away, last)
-    multiply_in(0, hint=0)
+    multiply_in(0, hint=HURRY)
     exchange(0)
     exchange_near(0)
     keep_down(0)
-    keep_down(1)
-    three_away, passed, last[0] = pick(place, inner_three, outer_three, mine, last)
+    three_away, passed, last[0] = pick(side, inner_three, outer_three, mine, last)
     two_away = by_plane(passed, CYCLE)
     to_chips(0, [near[0]])
     forward(3, three_away, [*parts[1][1:], *last])
@@ -443,6 +443,7 @@
     exchange_near(1)
     to_chips(1, [near[1]])
     send_chips(1)
+    keep_down(1)
     forward(2, two_away, last)
     multiply_in(3, after=[two_away])
     exchange(3)

time: 160 us -> 156 us (0.975)
  Pallas kernels: 59.6 us -> 56.7 us
    ppermute x11, waiting for transfers between devices: 31.3 us -> 27.8 us  [by_plane(): return lax.ppermute(behind(values, after), 'cols', pairs)]
    ppermute x11, starting transfers between devices: 15.5 us -> 17.8 us  [by_plane(): return lax.ppermute(behind(values, after), 'cols', pairs)]
    ppermute x31, waiting for transfers between devices: 24 us -> 26.3 us  [swap(): lax.ppermute(values, axis, [(place, place ^ step) for place in range(size)])]
    pallas_call x4, Pallas kernels: 15.4 us -> 13 us  [masked(): pl.pallas_call(functools.partial(mask_kernel, share, rows, len(after)), i...]
  transfers between devices with their start and end apart: 42 -> 42, of which waited for: 19 -> 18; matrix products, arithmetic and copies ran while one was open for 0% -> 0% of each run, Pallas kernels for 37% -> 36%
where the time goes in v18:
time: 156 us
  Pallas kernels  56.7 us (36%)
  waiting for transfers between devices  54.1 us (35%)
  starting transfers between devices  40.9 us (26%)
  other arithmetic  3.93 us (3%)
    ppermute x11, waiting for transfers between devices, by_plane(): return lax.ppermute(behind(values, after), 'cols', pairs)  27.8 us
    ppermute x31, waiting for transfers between devices, swap(): lax.ppermute(values, axis, [(place, place ^ step) for place in range(size)])  26.3 us
    pallas_call x4, Pallas kernels, gate_up(): pl.pallas_call(functools.partial(gate_up_kernel, len(parts), len(after)),...  24.3 us
    ppermute x31, starting transfers between devices, swap(): lax.ppermute(values, axis, [(place, place ^ step) for place in range(size)])  23 us
    ppermute x11, starting transfers between devices, by_plane(): return lax.ppermute(behind(values, after), 'cols', pairs)  17.8 us
    pallas_call x4, Pallas kernels, down(): pl.pallas_call(functools.partial(down_kernel, pieces, len(down_kept), len...  15.5 us
    pallas_call x4, Pallas kernels, masked(): pl.pallas_call(functools.partial(mask_kernel, share, rows, len(after)), i...  13 us
  transfers between devices with their start and end apart: 42, of which 18 were waited for; matrix products, arithmetic and copies ran while one was open for 0% of the time, Pallas kernels for 36%

profile of v18, /device:TPU:0, one launch (start us, length us, event | category | flops | bytes accessed | tf_op | source)
XLA Modules:
  0.0 156.2 jit_solution(1671003180360309431)
XLA Ops:
  0.0 1.3 fusion
  1.3 1.3 fusion.2
  3.3 1.3 collective-permute-done
  5.2 2.9 %collective-permute-start.1 = (bf16[2,1,40,2048]{3,2,1,0:T(8,128)(2,1)S(1)}, bf16[2,1,40,2048]{3,2,1,0:T(8,128)(2,1)S(1)}, u32[]{:S(2)}, u32[]{:S(2)}) collective-permute-start(bf16[2,1,40,2048]{3,2,1,0:T(8,128)(2,1)S(1)} %get-tuple-element.101.refs_2_), channel_id=1, source_target_pairs={{0,16},{8,24},{16,0},{24,8},{1,17},{9,25},{17,1},{25,9},{2,18},{10... | collective-permute-start | bytes 983048 | tf_op jit(solution)/shard_map/ppermute | solution.py:324
  8.1 1.6 %collective-permute-start.6 = (bf16[2,1,40,2048]{3,2,1,0:T(8,128)(2,1)S(1)}, bf16[2,1,40,2048]{3,2,1,0:T(8,128)(2,1)S(1)}, u32[]{:S(2)}, u32[]{:S(2)}) collective-permute-start(bf16[2,1,40,2048]{3,2,1,0:T(8,128)(2,1)S(1)} %get-tuple-element.102.refs_0_), channel_id=1, source_target_pairs={{0,2},{1,3},{2,0},{3,1},{4,6},{5,7},{6,4},{7,5},{8,10},{9,11},{10,... | collective-permute-start | bytes 983048 | tf_op jit(solution)/shard_map/ppermute | solution.py:354
  10.4 1.6 %collective-permute-start.2 = (bf16[2,1,40,2048]{3,2,1,0:T(8,128)(2,1)S(1)}, bf16[2,1,40,2048]{3,2,1,0:T(8,128)(2,1)S(1)}, u32[]{:S(2)}, u32[]{:S(2)}) collective-permute-start(bf16[2,1,40,2048]{3,2,1,0:T(8,128)(2,1)S(1)} %get-tuple-element.102.refs_0_), channel_id=1, source_target_pairs={{0,1},{1,0},{2,3},{3,2},{4,5},{5,4},{6,7},{7,6},{8,9},{9,8},{10,11... | collective-permute-start | bytes 983048 | tf_op jit(solution)/shard_map/ppermute | solution.py:324
  12.0 4.1 %collective-permute-done.1.refs_1_ = bf16[2,1,40,2048]{3,2,1,0:T(8,128)(2,1)S(1)} collective-permute-done((bf16[2,1,40,2048]{3,2,1,0:T(8,128)(2,1)S(1)}, bf16[2,1,40,2048]{3,2,1,0:T(8,128)(2,1)S(1)}, u32[]{:S(2)}, u32[]{:S(2)}) %collective-permute-start.1) | collective-permute-done | bytes 327712 | tf_op jit(solution)/shard_map/ppermute | solution.py:324
  16.1 1.8 %collective-permute-start.7 = (bf16[2,1,40,2048]{3,2,1,0:T(8,128)(2,1)S(1)}, bf16[2,1,40,2048]{3,2,1,0:T(8,128)(2,1)S(1)}, u32[]{:S(2)}, u32[]{:S(2)}) collective-permute-start(bf16[2,1,40,2048]{3,2,1,0:T(8,128)(2,1)S(1)} %collective-permute-done.1.refs_1_), channel_id=1, source_target_pairs={{0,2},{1,3},{2,0},{3,1},{4,6},{5,7},{6,4},{7,5},{8,10},{9,11},{10,... | collective-permute-start | bytes 983048 | tf_op jit(solution)/shard_map/ppermute | solution.py:354
  18.6 1.6 %collective-permute-start.3 = (bf16[2,1,40,2048]{3,2,1,0:T(8,128)(2,1)S(1)}, bf16[2,1,40,2048]{3,2,1,0:T(8,128)(2,1)S(1)}, u32[]{:S(2)}, u32[]{:S(2)}) collective-permute-start(bf16[2,1,40,2048]{3,2,1,0:T(8,128)(2,1)S(1)} %collective-permute-done.1.refs_1_), channel_id=1, source_target_pairs={{0,1},{1,0},{2,3},{3,2},{4,5},{5,4},{6,7},{7,6},{8,9},{9,8},{10,11... | collective-permute-start | bytes 983048 | tf_op jit(solution)/shard_map/ppermute | solution.py:324
  20.2 3.3 %masked.4 = (bf16[2048,1792]{1,0:T(8,128)(2,1)S(1)}, f32[8,128]{1,0:T(8,128)S(1)}) custom-call(s32[1]{0:T(128)} %bitcast.5.core_ref, bf16[2048,1792]{1,0:T(8,128)(2,1)} %weight_ref.4, s32[32,28]{1,0:T(8,128)S(1)} %copy-done.1, f32[8,128]{1,0:T(8,128)S(1)} %get-tuple-element.103.refs_0_), custom_call_target="tpu_custom_call" | custom-call | tf_op jit(solution)/shard_map/masked/pallas_call | solution.py:81
  23.5 3.2 %masked.5 = (bf16[2048,1792]{1,0:T(8,128)(2,1)S(1)}, f32[8,128]{1,0:T(8,128)S(1)}) custom-call(s32[1]{0:T(128)} %bitcast.5.core_ref, bf16[2048,1792]{1,0:T(8,128)(2,1)} %weight_ref.5, s32[32,28]{1,0:T(8,128)S(1)} %copy-done.2, f32[8,128]{1,0:T(8,128)S(1)} %get-tuple-element.106.refs_0_, bf16[2,1,40,2048]{3,2,1,0:T(8,128)(2,1)S(1)} %collective-permute-done.6.refs_1_.refs_0_), custom_call_target="tpu_custom_call" | custom-call | flops 172500000 | tf_op jit(solution)/shard_map/masked/pallas_call | solution.py:81
  26.9 4.5 %collective-permute-start.10 = (bf16[160,2048]{1,0:T(8,128)(2,1)S(1)}, bf16[160,2048]{1,0:T(8,128)(2,1)S(1)}, u32[]{:S(2)}, u32[]{:S(2)}) collective-permute-start(bf16[160,2048]{1,0:T(8,128)(2,1)S(1)} %get-tuple-element.118.refs_0_.mine_ref), channel_id=1, source_target_pairs={{0,6},{1,7},{6,0},{7,1},{8,14},{9,15},{14,8},{15,9},{16,22},{17,23... | collective-permute-start | bytes 1966088 | tf_op jit(solution)/shard_map/ppermute | solution.py:354
  31.5 1.1 collective-permute-start.12
  32.5 6.1 %gate_up.4 = (bf16[2,2,2,40,1792]{4,3,2,1,0:T(8,128)(2,1)S(1)}, bf16[2,2,40,1792]{3,2,1,0:T(8,128)(2,1)S(1)}, bf16[2,2,1,40,1792]{4,3,2,1,0:T(8,128)(2,1)S(1)}, f32[8,128]{1,0:T(8,128)S(1)}) custom-call(bf16[160,2048]{1,0:T(8,128)(2,1)S(1)} %get-tuple-element.118.refs_0_.mine_ref, bf16[160,2048]{1,0:T(8,128)(2,1)S(1)} %get-tuple-element.110.refs_1_, ...), custom_call_target="tpu_custom_call" | custom-call | flops 4697620480 | tf_op jit(solution)/shard_map/gate_up/pallas_call | solution.py:206
  39.2 3.3 %masked.6 = (bf16[1792,2048]{1,0:T(8,128)(2,1)S(1)}, f32[8,128]{1,0:T(8,128)S(1)}) custom-call(s32[1]{0:T(128)} %bitcast.5.core_ref, bf16[1792,8192]{1,0:T(8,128)(2,1)} %weight_ref.7, s32[28,128]{1,0:T(8,128)S(1)} %copy-done, f32[8,128]{1,0:T(8,128)S(1)} %get-tuple-element.119.refs_0_), custom_call_target="tpu_custom_call" | custom-call | tf_op jit(solution)/shard_map/masked/pallas_call | solution.py:81
  42.5 3.5 %collective-permute-done.10.outer_three_ref = bf16[160,2048]{1,0:T(8,128)(2,1)S(1)} collective-permute-done((bf16[160,2048]{1,0:T(8,128)(2,1)S(1)}, bf16[160,2048]{1,0:T(8,128)(2,1)S(1)}, u32[]{:S(2)}, u32[]{:S(2)}) %collective-permute-start.10) | collective-permute-done | bytes 655392 | tf_op jit(solution)/shard_map/ppermute | solution.py:354
  47.3 1.1 collective-permute-start.11
  48.3 6.1 %gate_up.5 = (bf16[2,2,2,40,1792]{4,3,2,1,0:T(8,128)(2,1)S(1)}, bf16[2,2,40,1792]{3,2,1,0:T(8,128)(2,1)S(1)}, bf16[2,2,1,40,1792]{4,3,2,1,0:T(8,128)(2,1)S(1)}, f32[8,128]{1,0:T(8,128)S(1)}) custom-call(bf16[160,2048]{1,0:T(8,128)(2,1)S(1)} %get-tuple-element.125.refs_0_, bf16[160,2048]{1,0:T(8,128)(2,1)S(1)} %collective-permute-done.12.refs_1_, ...), custom_call_target="tpu_custom_call" | custom-call | flops 4697620480 | tf_op jit(solution)/shard_map/gate_up/pallas_call | solution.py:206
  55.0 1.5 collective-permute-done.13.refs_1_
  56.5 0.8 collective-permute-done.14.refs_3_.refs_1_
  57.4 1.6 collective-permute-start.16
  59.0 3.3 %masked.7 = (bf16[1792,2048]{1,0:T(8,128)(2,1)S(1)}, f32[8,128]{1,0:T(8,128)S(1)}) custom-call(s32[1]{0:T(128)} %bitcast.5.core_ref, bf16[1792,8192]{1,0:T(8,128)(2,1)} %weight_ref.7, s32[28,128]{1,0:T(8,128)S(1)} %copy-done, f32[8,128]{1,0:T(8,128)S(1)} %get-tuple-element.131.refs_0_), custom_call_target="tpu_custom_call" | custom-call | tf_op jit(solution)/shard_map/masked/pallas_call | solution.py:81
  63.0 6.1 %gate_up.6 = (bf16[2,2,2,40,1792]{4,3,2,1,0:T(8,128)(2,1)S(1)}, bf16[2,2,40,1792]{3,2,1,0:T(8,128)(2,1)S(1)}, bf16[2,2,1,40,1792]{4,3,2,1,0:T(8,128)(2,1)S(1)}, f32[8,128]{1,0:T(8,128)S(1)}) custom-call(bf16[160,2048]{1,0:T(8,128)(2,1)S(1)} %get-tuple-element.136.refs_0_, bf16[160,2048]{1,0:T(8,128)(2,1)S(1)} %collective-permute-done.17.refs_1_, ...), custom_call_target="tpu_custom_call" | custom-call | flops 4697620480 | tf_op jit(solution)/shard_map/gate_up/pallas_call | solution.py:206
  69.7 2.8 %collective-permute-done.16.refs_2_ = bf16[2,2,40,1792]{3,2,1,0:T(8,128)(2,1)S(1)} collective-permute-done((bf16[2,2,40,1792]{3,2,1,0:T(8,128)(2,1)S(1)}, bf16[2,2,40,1792]{3,2,1,0:T(8,128)(2,1)S(1)}, u32[]{:S(2)}, u32[]{:S(2)}) %collective-permute-start.16) | collective-permute-done | bytes 573472 | tf_op jit(solution)/shard_map/ppermute | solution.py:324
  73.1 1.6 collective-permute-start.23
  74.6 3.9 %down.4 = (bf16[2,40,4096]{2,1,0:T(8,128)(2,1)S(1)}, bf16[2,40,4096]{2,1,0:T(8,128)(2,1)S(1)}, f32[8,128]{1,0:T(8,128)S(1)}) custom-call(bf16[2,40,1792]{2,1,0:T(8,128)(2,1)S(1)} %get-tuple-element.138.own_ref, bf16[2,40,1792]{2,1,0:T(8,128)(2,1)S(1)} %collective-permute-done.18.other_ref, bf16[1792,2048]{1,0:T(8,128)(2,1)S(1)} %get-tuple-element.139.refs_0_, ...), custom_call_target="tpu_custom_call" | custom-call | flops 2348810 | tf_op jit(solution)/shard_map/down/pallas_call | solution.py:248
  79.5 6.1 %gate_up.7 = (bf16[2,2,2,40,1792]{4,3,2,1,0:T(8,128)(2,1)S(1)}, bf16[2,2,40,1792]{3,2,1,0:T(8,128)(2,1)S(1)}, bf16[1,2,1,40,1792]{4,3,2,1,0:T(8,128)(2,1)S(1)}, ...) custom-call(bf16[160,2048]{1,0:T(8,128)(2,1)S(1)} %collective-permute-done.11.refs_5_.refs_0_, ...), custom_call_target="tpu_custom_call" | custom-call | flops 4697620480 | tf_op jit(solution)/shard_map/gate_up/pallas_call | solution.py:206
  86.2 2.3 %collective-permute-done.23.refs_2_ = bf16[2,2,40,1792]{3,2,1,0:T(8,128)(2,1)S(1)} collective-permute-done((bf16[2,2,40,1792]{3,2,1,0:T(8,128)(2,1)S(1)}, bf16[2,2,40,1792]{3,2,1,0:T(8,128)(2,1)S(1)}, u32[]{:S(2)}, u32[]{:S(2)}) %collective-permute-start.23) | collective-permute-done | bytes 573472 | tf_op jit(solution)/shard_map/ppermute | solution.py:324
  89.6 1.5 collective-permute-start.24
  91.1 3.9 %down.5 = (bf16[1,40,4096]{2,1,0:T(8,128)(2,1)S(1)}, bf16[1,40,4096]{2,1,0:T(8,128)(2,1)S(1)}, bf16[1,40,4096]{2,1,0:T(8,128)(2,1)S(1)}, bf16[1,40,4096]{2,1,0:T(8,128)(2,1)S(1)}, f32[8,128]{1,0:T(8,128)S(1)}) custom-call(bf16[2,40,1792]{2,1,0:T(8,128)(2,1)S(1)} %get-tuple-element.158.own_ref, bf16[2,40,1792]{2,1,0:T(8,128)(2,1)S(1)} %collective-permute-done.27.other_ref, ...), custom_call_target="tpu_custom_call" | custom-call | flops 2348810 | tf_op jit(solution)/shard_map/down/pallas_call | solution.py:248
  96.3 1.7 %collective-permute-start.32 = (bf16[2,40,4096]{2,1,0:T(8,128)(2,1)S(1)}, bf16[2,40,4096]{2,1,0:T(8,128)(2,1)S(1)}, u32[]{:S(2)}, u32[]{:S(2)}) collective-permute-start(bf16[2,40,4096]{2,1,0:T(8,128)(2,1)S(1)} %get-tuple-element.177), channel_id=1, source_target_pairs={{0,2},{1,3},{2,0},{3,1},{4,6},{5,7},{6,4},{7,5},{8,10},{9,11},{10,... | collective-permute-start | bytes 1966088 | tf_op jit(solution)/shard_map/ppermute | solution.py:354
  97.9 6.5 %collective-permute-done.29.refs_1_ = bf16[1,40,4096]{2,1,0:T(8,128)(2,1)S(1)} collective-permute-done((bf16[1,40,4096]{2,1,0:T(8,128)(2,1)S(1)}, bf16[1,40,4096]{2,1,0:T(8,128)(2,1)S(1)}, u32[]{:S(2)}, u32[]{:S(2)}) %collective-permute-start.29) | collective-permute-done | bytes 327712 | tf_op jit(solution)/shard_map/ppermute | solution.py:324
  105.6 1.2 collective-permute-start.25
  106.9 1.6 %collective-permute-start.34 = (bf16[1,40,4096]{2,1,0:T(8,128)(2,1)S(1)}, bf16[1,40,4096]{2,1,0:T(8,128)(2,1)S(1)}, u32[]{:S(2)}, u32[]{:S(2)}) collective-permute-start(bf16[1,40,4096]{2,1,0:T(8,128)(2,1)S(1)} %get-tuple-element.174), channel_id=1, source_target_pairs={{0,2},{1,3},{2,0},{3,1},{4,6},{5,7},{6,4},{7,5},{8,10},{9,11},{10,... | collective-permute-start | bytes 983048 | tf_op jit(solution)/shard_map/ppermute | solution.py:354
  108.5 3.9 %down.6 = (bf16[1,40,4096]{2,1,0:T(8,128)(2,1)S(1)}, bf16[1,40,4096]{2,1,0:T(8,128)(2,1)S(1)}, bf16[1,40,4096]{2,1,0:T(8,128)(2,1)S(1)}, bf16[1,40,4096]{2,1,0:T(8,128)(2,1)S(1)}, f32[8,128]{1,0:T(8,128)S(1)}) custom-call(bf16[2,40,1792]{2,1,0:T(8,128)(2,1)S(1)} %get-tuple-element.168.own_ref, bf16[2,40,1792]{2,1,0:T(8,128)(2,1)S(1)} %collective-permute-done.30.other_ref, ...), custom_call_target="tpu_custom_call" | custom-call | flops 2348810 | tf_op jit(solution)/shard_map/down/pallas_call | solution.py:248
  112.3 1.7 %collective-permute-done.32.refs_3_.refs_1_ = bf16[2,40,4096]{2,1,0:T(8,128)(2,1)S(1)} collective-permute-done((bf16[2,40,4096]{2,1,0:T(8,128)(2,1)S(1)}, bf16[2,40,4096]{2,1,0:T(8,128)(2,1)S(1)}, u32[]{:S(2)}, u32[]{:S(2)}) %collective-permute-start.32) | collective-permute-done | bytes 655392 | tf_op jit(solution)/shard_map/ppermute | solution.py:354
  114.1 1.4 collective-permute-start.33
  115.5 1.0 collective-permute-start.38
  116.5 4.6 %collective-permute-done.34.refs_2_ = bf16[1,40,4096]{2,1,0:T(8,128)(2,1)S(1)} collective-permute-done((bf16[1,40,4096]{2,1,0:T(8,128)(2,1)S(1)}, bf16[1,40,4096]{2,1,0:T(8,128)(2,1)S(1)}, u32[]{:S(2)}, u32[]{:S(2)}) %collective-permute-start.34) | collective-permute-done | bytes 327712 | tf_op jit(solution)/shard_map/ppermute | solution.py:354
  121.0 1.0 collective-permute-done.33.refs_1_
  123.3 1.6 %collective-permute-start.40 = (bf16[1,40,4096]{2,1,0:T(8,128)(2,1)S(1)}, bf16[1,40,4096]{2,1,0:T(8,128)(2,1)S(1)}, u32[]{:S(2)}, u32[]{:S(2)}) collective-permute-start(bf16[1,40,4096]{2,1,0:T(8,128)(2,1)S(1)} %get-tuple-element.187), channel_id=1, source_target_pairs={{0,4},{1,5},{4,0},{5,1},{2,6},{3,7},{6,2},{7,3},{8,12},{9,13},{12,... | collective-permute-start | bytes 983048 | tf_op jit(solution)/shard_map/ppermute | solution.py:354
  124.9 3.9 %down.7 = (bf16[2,40,4096]{2,1,0:T(8,128)(2,1)S(1)}, bf16[2,40,4096]{2,1,0:T(8,128)(2,1)S(1)}, f32[8,128]{1,0:T(8,128)S(1)}) custom-call(bf16[2,40,1792]{2,1,0:T(8,128)(2,1)S(1)} %get-tuple-element.182.own_ref, bf16[2,40,1792]{2,1,0:T(8,128)(2,1)S(1)} %collective-permute-done.35.other_ref, bf16[1792,2048]{1,0:T(8,128)(2,1)S(1)} %get-tuple-element.139.refs_0_, ...), custom_call_target="tpu_custom_call" | custom-call | flops 2348810 | tf_op jit(solution)/shard_map/down/pallas_call | solution.py:248
  128.9 3.8 %collective-permute-done.36.refs_1_ = bf16[1,40,4096]{2,1,0:T(8,128)(2,1)S(1)} collective-permute-done((bf16[1,40,4096]{2,1,0:T(8,128)(2,1)S(1)}, bf16[1,40,4096]{2,1,0:T(8,128)(2,1)S(1)}, u32[]{:S(2)}, u32[]{:S(2)}) %collective-permute-start.36) | collective-permute-done | bytes 327712 | tf_op jit(solution)/shard_map/ppermute | solution.py:324
  132.7 1.7 %collective-permute-start.39 = (bf16[1,40,4096]{2,1,0:T(8,128)(2,1)S(1)}, bf16[1,40,4096]{2,1,0:T(8,128)(2,1)S(1)}, u32[]{:S(2)}, u32[]{:S(2)}) collective-permute-start(bf16[1,40,4096]{2,1,0:T(8,128)(2,1)S(1)} %get-tuple-element.194), channel_id=1, source_target_pairs={{0,4},{1,5},{4,0},{5,1},{2,6},{3,7},{6,2},{7,3},{8,12},{9,13},{12,... | collective-permute-start | bytes 983048 | tf_op jit(solution)/shard_map/ppermute | solution.py:354
  135.1 13.5 %collective-permute-done.40.refs_0_ = bf16[1,40,4096]{2,1,0:T(8,128)(2,1)S(1)} collective-permute-done((bf16[1,40,4096]{2,1,0:T(8,128)(2,1)S(1)}, bf16[1,40,4096]{2,1,0:T(8,128)(2,1)S(1)}, u32[]{:S(2)}, u32[]{:S(2)}) %collective-permute-start.40) | collective-permute-done | bytes 327712 | tf_op jit(solution)/shard_map/ppermute | solution.py:354
  149.3 1.1 collective-permute-done.37
  150.6 4.4 %collective-permute-done.39 = bf16[1,40,4096]{2,1,0:T(8,128)(2,1)S(1)} collective-permute-done((bf16[1,40,4096]{2,1,0:T(8,128)(2,1)S(1)}, bf16[1,40,4096]{2,1,0:T(8,128)(2,1)S(1)}, u32[]{:S(2)}, u32[]{:S(2)}) %collective-permute-start.39) | collective-permute-done | bytes 327712 | tf_op jit(solution)/shard_map/ppermute | solution.py:354
  155.3 0.9 pad_maximum_fusion
  (87 shorter events, 15.6 us)
Async XLA Ops:
  2.7 17.4 %copy-start.1 = (s32[32,28]{1,0:T(8,128)S(1)}, s32[32,28]{1,0:T(8,128)}, u32[]{:S(2)}) copy-start(s32[32,28]{1,0:T(8,128)} %mask_ref.4) | copy-start | bytes 10756
  2.8 1.8 %collective-permute-start = (bf16[2,40,2048]{2,1,0:T(8,128)(2,1)S(1)}, bf16[2,40,2048]{2,1,0:T(8,128)(2,1)S(1)}, u32[]{:S(2)}, u32[]{:S(2)}) collective-permute-start(bf16[2,40,2048]{2,1,0:T(8,128)(2,1)S(1)} %pad_maximum_fusion.1), channel_id=1, source_target_pairs={{0,8},{8,0},{16,24},{24,16},{1,9},{9,1},{17,25},{25,17},{2,10},{10... | collective-permute-start | bytes 983048 | tf_op jit(solution)/shard_map/ppermute | solution.py:324
  5.2 10.9 %collective-permute-start.1 = (bf16[2,1,40,2048]{3,2,1,0:T(8,128)(2,1)S(1)}, bf16[2,1,40,2048]{3,2,1,0:T(8,128)(2,1)S(1)}, u32[]{:S(2)}, u32[]{:S(2)}) collective-permute-start(bf16[2,1,40,2048]{3,2,1,0:T(8,128)(2,1)S(1)} %get-tuple-element.101.refs_2_), channel_id=1, source_target_pairs={{0,16},{8,24},{16,0},{24,8},{1,17},{9,25},{17,1},{25,9},{2,18},{10... | collective-permute-start | bytes 983048 | tf_op jit(solution)/shard_map/ppermute | solution.py:324
  8.1 10.5 %collective-permute-start.6 = (bf16[2,1,40,2048]{3,2,1,0:T(8,128)(2,1)S(1)}, bf16[2,1,40,2048]{3,2,1,0:T(8,128)(2,1)S(1)}, u32[]{:S(2)}, u32[]{:S(2)}) collective-permute-start(bf16[2,1,40,2048]{3,2,1,0:T(8,128)(2,1)S(1)} %get-tuple-element.102.refs_0_), channel_id=1, source_target_pairs={{0,2},{1,3},{2,0},{3,1},{4,6},{5,7},{6,4},{7,5},{8,10},{9,11},{10,... | collective-permute-start | bytes 983048 | tf_op jit(solution)/shard_map/ppermute | solution.py:354
  9.7 17.0 %collective-permute-start.4 = (bf16[2,1,40,2048]{3,2,1,0:T(8,128)(2,1)S(1)}, bf16[2,1,40,2048]{3,2,1,0:T(8,128)(2,1)S(1)}, u32[]{:S(2)}, u32[]{:S(2)}) collective-permute-start(bf16[2,1,40,2048]{3,2,1,0:T(8,128)(2,1)S(1)} %get-tuple-element.102.refs_0_), channel_id=1, source_target_pairs={{2,4},{3,5},{4,2},{5,3},{10,12},{11,13},{12,10},{13,11},{18,20},{1... | collective-permute-start | bytes 983048 | tf_op jit(solution)/shard_map/ppermute | solution.py:354
  10.4 16.4 %collective-permute-start.2 = (bf16[2,1,40,2048]{3,2,1,0:T(8,128)(2,1)S(1)}, bf16[2,1,40,2048]{3,2,1,0:T(8,128)(2,1)S(1)}, u32[]{:S(2)}, u32[]{:S(2)}) collective-permute-start(bf16[2,1,40,2048]{3,2,1,0:T(8,128)(2,1)S(1)} %get-tuple-element.102.refs_0_), channel_id=1, source_target_pairs={{0,1},{1,0},{2,3},{3,2},{4,5},{5,4},{6,7},{7,6},{8,9},{9,8},{10,11... | collective-permute-start | bytes 983048 | tf_op jit(solution)/shard_map/ppermute | solution.py:324
  16.1 10.7 %collective-permute-start.7 = (bf16[2,1,40,2048]{3,2,1,0:T(8,128)(2,1)S(1)}, bf16[2,1,40,2048]{3,2,1,0:T(8,128)(2,1)S(1)}, u32[]{:S(2)}, u32[]{:S(2)}) collective-permute-start(bf16[2,1,40,2048]{3,2,1,0:T(8,128)(2,1)S(1)} %collective-permute-done.1.refs_1_), channel_id=1, source_target_pairs={{0,2},{1,3},{2,0},{3,1},{4,6},{5,7},{6,4},{7,5},{8,10},{9,11},{10,... | collective-permute-start | bytes 983048 | tf_op jit(solution)/shard_map/ppermute | solution.py:354
  17.9 9.0 %collective-permute-start.5 = (bf16[2,1,40,2048]{3,2,1,0:T(8,128)(2,1)S(1)}, bf16[2,1,40,2048]{3,2,1,0:T(8,128)(2,1)S(1)}, u32[]{:S(2)}, u32[]{:S(2)}) collective-permute-start(bf16[2,1,40,2048]{3,2,1,0:T(8,128)(2,1)S(1)} %collective-permute-done.1.refs_1_), channel_id=1, source_target_pairs={{2,4},{3,5},{4,2},{5,3},{10,12},{11,13},{12,10},{13,11},{18,20},{1... | collective-permute-start | bytes 983048 | tf_op jit(solution)/shard_map/ppermute | solution.py:354
  18.6 12.8 %collective-permute-start.3 = (bf16[2,1,40,2048]{3,2,1,0:T(8,128)(2,1)S(1)}, bf16[2,1,40,2048]{3,2,1,0:T(8,128)(2,1)S(1)}, u32[]{:S(2)}, u32[]{:S(2)}) collective-permute-start(bf16[2,1,40,2048]{3,2,1,0:T(8,128)(2,1)S(1)} %collective-permute-done.1.refs_1_), channel_id=1, source_target_pairs={{0,1},{1,0},{2,3},{3,2},{4,5},{5,4},{6,7},{7,6},{8,9},{9,8},{10,11... | collective-permute-start | bytes 983048 | tf_op jit(solution)/shard_map/ppermute | solution.py:324
  20.2 3.3 %copy-start.2 = (s32[32,28]{1,0:T(8,128)S(1)}, s32[32,28]{1,0:T(8,128)}, u32[]{:S(2)}) copy-start(s32[32,28]{1,0:T(8,128)} %mask_ref.5) | copy-start | bytes 10756
  26.9 19.1 %collective-permute-start.10 = (bf16[160,2048]{1,0:T(8,128)(2,1)S(1)}, bf16[160,2048]{1,0:T(8,128)(2,1)S(1)}, u32[]{:S(2)}, u32[]{:S(2)}) collective-permute-start(bf16[160,2048]{1,0:T(8,128)(2,1)S(1)} %get-tuple-element.118.refs_0_.mine_ref), channel_id=1, source_target_pairs={{0,6},{1,7},{6,0},{7,1},{8,14},{9,15},{14,8},{15,9},{16,22},{17,23... | collective-permute-start | bytes 1966088 | tf_op jit(solution)/shard_map/ppermute | solution.py:354
  31.5 15.1 %collective-permute-start.12 = (bf16[160,2048]{1,0:T(8,128)(2,1)S(1)}, bf16[160,2048]{1,0:T(8,128)(2,1)S(1)}, u32[]{:S(2)}, u32[]{:S(2)}) collective-permute-start(bf16[160,2048]{1,0:T(8,128)(2,1)S(1)} %get-tuple-element.125.refs_0_), channel_id=1, source_target_pairs={{0,1},{1,0},{2,3},{3,2},{4,5},{5,4},{6,7},{7,6},{8,9},{9,8},{10,11... | collective-permute-start | bytes 1966088 | tf_op jit(solution)/shard_map/ppermute | solution.py:324
  32.5 6.7 %copy-start = (s32[28,128]{1,0:T(8,128)S(1)}, s32[28,128]{1,0:T(8,128)}, u32[]{:S(2)}) copy-start(s32[28,128]{1,0:T(8,128)} %mask_ref.7) | copy-start | bytes 43012
  38.6 7.5 %collective-permute-start.8 = (bf16[2,2,40,1792]{3,2,1,0:T(8,128)(2,1)S(1)}, bf16[2,2,40,1792]{3,2,1,0:T(8,128)(2,1)S(1)}, u32[]{:S(2)}, u32[]{:S(2)}) collective-permute-start(bf16[2,2,40,1792]{3,2,1,0:T(8,128)(2,1)S(1)} %get-tuple-element.115), channel_id=1, source_target_pairs={{0,8},{8,0},{16,24},{24,16},{1,9},{9,1},{17,25},{25,17},{2,10},{10... | collective-permute-start | bytes 1720328 | tf_op jit(solution)/shard_map/ppermute | solution.py:324
  38.7 7.4 %collective-permute-start.9 = (bf16[2,2,1,40,1792]{4,3,2,1,0:T(8,128)(2,1)S(1)}, bf16[2,2,1,40,1792]{4,3,2,1,0:T(8,128)(2,1)S(1)}, u32[]{:S(2)}, u32[]{:S(2)}) collective-permute-start(bf16[2,2,1,40,1792]{4,3,2,1,0:T(8,128)(2,1)S(1)} %get-tuple-element.116), channel_id=1, source_target_pairs={{0,8},{8,0},{16,24},{24,16},{1,9},{9,1},{17,25},{25,17},{2,10},{10... | collective-permute-start | bytes 1720328 | tf_op jit(solution)/shard_map/ppermute | solution.py:324
  46.6 16.4 %collective-permute-start.17 = (bf16[160,2048]{1,0:T(8,128)(2,1)S(1)}, bf16[160,2048]{1,0:T(8,128)(2,1)S(1)}, u32[]{:S(2)}, u32[]{:S(2)}) collective-permute-start(bf16[160,2048]{1,0:T(8,128)(2,1)S(1)} %get-tuple-element.136.refs_0_), channel_id=1, source_target_pairs={{0,1},{1,0},{2,3},{3,2},{4,5},{5,4},{6,7},{7,6},{8,9},{9,8},{10,11... | collective-permute-start | bytes 1966088 | tf_op jit(solution)/shard_map/ppermute | solution.py:324
  47.3 15.0 %collective-permute-start.11 = (bf16[160,2048]{1,0:T(8,128)(2,1)S(1)}, bf16[160,2048]{1,0:T(8,128)(2,1)S(1)}, u32[]{:S(2)}, u32[]{:S(2)}) collective-permute-start(bf16[160,2048]{1,0:T(8,128)(2,1)S(1)} %get-tuple-element.123), channel_id=1, source_target_pairs={{0,4},{1,5},{4,6},{5,7},{6,2},{7,3},{2,0},{3,1},{8,12},{9,13},{12,... | collective-permute-start | bytes 1966088 | tf_op jit(solution)/shard_map/ppermute | solution.py:354
  54.4 2.0 %collective-permute-start.13 = (bf16[2,2,1,40,1792]{4,3,2,1,0:T(8,128)(2,1)S(1)}, bf16[2,2,1,40,1792]{4,3,2,1,0:T(8,128)(2,1)S(1)}, u32[]{:S(2)}, u32[]{:S(2)}) collective-permute-start(bf16[2,2,1,40,1792]{4,3,2,1,0:T(8,128)(2,1)S(1)} %get-tuple-element.128), channel_id=1, source_target_pairs={{0,8},{8,0},{16,24},{24,16},{1,9},{9,1},{17,25},{25,17},{2,10},{10... | collective-permute-start | bytes 1720328 | tf_op jit(solution)/shard_map/ppermute | solution.py:324
  54.5 2.8 %collective-permute-start.14 = (bf16[2,2,40,1792]{3,2,1,0:T(8,128)(2,1)S(1)}, bf16[2,2,40,1792]{3,2,1,0:T(8,128)(2,1)S(1)}, u32[]{:S(2)}, u32[]{:S(2)}) collective-permute-start(bf16[2,2,40,1792]{3,2,1,0:T(8,128)(2,1)S(1)} %get-tuple-element.130), channel_id=1, source_target_pairs={{0,8},{8,0},{16,24},{24,16},{1,9},{9,1},{17,25},{25,17},{2,10},{10... | collective-permute-start | bytes 1720328 | tf_op jit(solution)/shard_map/ppermute | solution.py:324
  57.4 15.1 %collective-permute-start.16 = (bf16[2,2,40,1792]{3,2,1,0:T(8,128)(2,1)S(1)}, bf16[2,2,40,1792]{3,2,1,0:T(8,128)(2,1)S(1)}, u32[]{:S(2)}, u32[]{:S(2)}) collective-permute-start(bf16[2,2,40,1792]{3,2,1,0:T(8,128)(2,1)S(1)} %get-tuple-element.134), channel_id=1, source_target_pairs={{0,16},{8,24},{16,0},{24,8},{1,17},{9,25},{17,1},{25,9},{2,18},{10... | collective-permute-start | bytes 1720328 | tf_op jit(solution)/shard_map/ppermute | solution.py:324
  62.3 16.6 %collective-permute-start.15 = (bf16[160,2048]{1,0:T(8,128)(2,1)S(1)}, bf16[160,2048]{1,0:T(8,128)(2,1)S(1)}, u32[]{:S(2)}, u32[]{:S(2)}) collective-permute-start(bf16[160,2048]{1,0:T(8,128)(2,1)S(1)} %collective-permute-done.11.refs_5_.refs_0_), channel_id=1, source_target_pairs={{0,1},{1,0},{2,3},{3,2},{4,5},{5,4},{6,7},{7,6},{8,9},{9,8},{10,11... | collective-permute-start | bytes 1966088 | tf_op jit(solution)/shard_map/ppermute | solution.py:324
  69.1 3.8 %collective-permute-start.19 = (bf16[2,2,1,40,1792]{4,3,2,1,0:T(8,128)(2,1)S(1)}, bf16[2,2,1,40,1792]{4,3,2,1,0:T(8,128)(2,1)S(1)}, u32[]{:S(2)}, u32[]{:S(2)}) collective-permute-start(bf16[2,2,1,40,1792]{4,3,2,1,0:T(8,128)(2,1)S(1)} %get-tuple-element.142), channel_id=1, source_target_pairs={{0,8},{8,0},{16,24},{24,16},{1,9},{9,1},{17,25},{25,17},{2,10},{10... | collective-permute-start | bytes 1720328 | tf_op jit(solution)/shard_map/ppermute | solution.py:324
  69.2 3.7 %collective-permute-start.20 = (bf16[2,2,40,1792]{3,2,1,0:T(8,128)(2,1)S(1)}, bf16[2,2,40,1792]{3,2,1,0:T(8,128)(2,1)S(1)}, u32[]{:S(2)}, u32[]{:S(2)}) collective-permute-start(bf16[2,2,40,1792]{3,2,1,0:T(8,128)(2,1)S(1)} %get-tuple-element.144), channel_id=1, source_target_pairs={{0,8},{8,0},{16,24},{24,16},{1,9},{9,1},{17,25},{25,17},{2,10},{10... | collective-permute-start | bytes 1720328 | tf_op jit(solution)/shard_map/ppermute | solution.py:324
  72.8 1.8 %collective-permute-start.18 = (bf16[2,40,1792]{2,1,0:T(8,128)(2,1)S(1)}, bf16[2,40,1792]{2,1,0:T(8,128)(2,1)S(1)}, u32[]{:S(2)}, u32[]{:S(2)}) collective-permute-start(bf16[2,40,1792]{2,1,0:T(8,128)(2,1)S(1)} %get-tuple-element.138.own_ref), channel_id=1, source_target_pairs={{0,8},{8,0},{16,24},{24,16},{1,9},{9,1},{17,25},{25,17},{2,10},{10... | collective-permute-start | bytes 860168 | tf_op jit(solution)/shard_map/ppermute | solution.py:324
  73.1 15.4 %collective-permute-start.23 = (bf16[2,2,40,1792]{3,2,1,0:T(8,128)(2,1)S(1)}, bf16[2,2,40,1792]{3,2,1,0:T(8,128)(2,1)S(1)}, u32[]{:S(2)}, u32[]{:S(2)}) collective-permute-start(bf16[2,2,40,1792]{3,2,1,0:T(8,128)(2,1)S(1)} %get-tuple-element.150), channel_id=1, source_target_pairs={{0,16},{8,24},{16,0},{24,8},{1,17},{9,25},{17,1},{25,9},{2,18},{10... | collective-permute-start | bytes 1720328 | tf_op jit(solution)/shard_map/ppermute | solution.py:324
  78.8 16.6 %collective-permute-start.28 = (bf16[2,40,4096]{2,1,0:T(8,128)(2,1)S(1)}, bf16[2,40,4096]{2,1,0:T(8,128)(2,1)S(1)}, u32[]{:S(2)}, u32[]{:S(2)}) collective-permute-start(bf16[2,40,4096]{2,1,0:T(8,128)(2,1)S(1)} %get-tuple-element.162), channel_id=1, source_target_pairs={{0,1},{1,0},{2,3},{3,2},{4,5},{5,4},{6,7},{7,6},{8,9},{9,8},{10,11... | collective-permute-start | bytes 1966088 | tf_op jit(solution)/shard_map/ppermute | solution.py:324
  85.6 3.3 %collective-permute-start.21 = (bf16[1,2,1,40,1792]{4,3,2,1,0:T(8,128)(2,1)S(1)}, bf16[1,2,1,40,1792]{4,3,2,1,0:T(8,128)(2,1)S(1)}, u32[]{:S(2)}, u32[]{:S(2)}) collective-permute-start(bf16[1,2,1,40,1792]{4,3,2,1,0:T(8,128)(2,1)S(1)} %get-tuple-element.148), channel_id=1, source_target_pairs={{0,8},{8,0},{16,24},{24,16},{1,9},{9,1},{17,25},{25,17},{2,10},{10... | collective-permute-start | bytes 860168 | tf_op jit(solution)/shard_map/ppermute | solution.py:324
  85.7 3.2 %collective-permute-start.22 = (bf16[1,2,1,40,1792]{4,3,2,1,0:T(8,128)(2,1)S(1)}, bf16[1,2,1,40,1792]{4,3,2,1,0:T(8,128)(2,1)S(1)}, u32[]{:S(2)}, u32[]{:S(2)}) collective-permute-start(bf16[1,2,1,40,1792]{4,3,2,1,0:T(8,128)(2,1)S(1)} %get-tuple-element.149), channel_id=1, source_target_pairs={{0,8},{8,0},{16,24},{24,16},{1,9},{9,1},{17,25},{25,17},{2,10},{10... | collective-permute-start | bytes 860168 | tf_op jit(solution)/shard_map/ppermute | solution.py:324
  88.8 2.3 %collective-permute-start.27 = (bf16[2,40,1792]{2,1,0:T(8,128)(2,1)S(1)}, bf16[2,40,1792]{2,1,0:T(8,128)(2,1)S(1)}, u32[]{:S(2)}, u32[]{:S(2)}) collective-permute-start(bf16[2,40,1792]{2,1,0:T(8,128)(2,1)S(1)} %get-tuple-element.158.own_ref), channel_id=1, source_target_pairs={{0,8},{8,0},{16,24},{24,16},{1,9},{9,1},{17,25},{25,17},{2,10},{10... | collective-permute-start | bytes 860168 | tf_op jit(solution)/shard_map/ppermute | solution.py:324
  89.0 16.2 %collective-permute-start.26 = (bf16[2,2,40,1792]{3,2,1,0:T(8,128)(2,1)S(1)}, bf16[2,2,40,1792]{3,2,1,0:T(8,128)(2,1)S(1)}, u32[]{:S(2)}, u32[]{:S(2)}) collective-permute-start(bf16[2,2,40,1792]{3,2,1,0:T(8,128)(2,1)S(1)} %get-tuple-element.157), channel_id=1, source_target_pairs={{0,8},{8,0},{16,24},{24,16},{1,9},{9,1},{17,25},{25,17},{2,10},{10... | collective-permute-start | bytes 1720328 | tf_op jit(solution)/shard_map/ppermute | solution.py:324
  89.6 15.7 %collective-permute-start.24 = (bf16[2,2,40,1792]{3,2,1,0:T(8,128)(2,1)S(1)}, bf16[2,2,40,1792]{3,2,1,0:T(8,128)(2,1)S(1)}, u32[]{:S(2)}, u32[]{:S(2)}) collective-permute-start(bf16[2,2,40,1792]{3,2,1,0:T(8,128)(2,1)S(1)} %get-tuple-element.153), channel_id=1, source_target_pairs={{0,16},{8,24},{16,0},{24,8},{1,17},{9,25},{17,1},{25,9},{2,18},{10... | collective-permute-start | bytes 1720328 | tf_op jit(solution)/shard_map/ppermute | solution.py:324
  95.4 9.0 %collective-permute-start.29 = (bf16[1,40,4096]{2,1,0:T(8,128)(2,1)S(1)}, bf16[1,40,4096]{2,1,0:T(8,128)(2,1)S(1)}, u32[]{:S(2)}, u32[]{:S(2)}) collective-permute-start(bf16[1,40,4096]{2,1,0:T(8,128)(2,1)S(1)} %get-tuple-element.163), channel_id=1, source_target_pairs={{0,1},{1,0},{2,3},{3,2},{4,5},{5,4},{6,7},{7,6},{8,9},{9,8},{10,11... | collective-permute-start | bytes 983048 | tf_op jit(solution)/shard_map/ppermute | solution.py:324
  96.3 17.7 %collective-permute-start.32 = (bf16[2,40,4096]{2,1,0:T(8,128)(2,1)S(1)}, bf16[2,40,4096]{2,1,0:T(8,128)(2,1)S(1)}, u32[]{:S(2)}, u32[]{:S(2)}) collective-permute-start(bf16[2,40,4096]{2,1,0:T(8,128)(2,1)S(1)} %get-tuple-element.177), channel_id=1, source_target_pairs={{0,2},{1,3},{2,0},{3,1},{4,6},{5,7},{6,4},{7,5},{8,10},{9,11},{10,... | collective-permute-start | bytes 1966088 | tf_op jit(solution)/shard_map/ppermute | solution.py:354
  104.5 9.5 %collective-permute-start.31 = (bf16[1,40,4096]{2,1,0:T(8,128)(2,1)S(1)}, bf16[1,40,4096]{2,1,0:T(8,128)(2,1)S(1)}, u32[]{:S(2)}, u32[]{:S(2)}) collective-permute-start(bf16[1,40,4096]{2,1,0:T(8,128)(2,1)S(1)} %get-tuple-element.175), channel_id=1, source_target_pairs={{0,1},{1,0},{2,3},{3,2},{4,5},{5,4},{6,7},{7,6},{8,9},{9,8},{10,11... | collective-permute-start | bytes 983048 | tf_op jit(solution)/shard_map/ppermute | solution.py:324
  105.6 2.9 %collective-permute-start.30 = (bf16[2,40,1792]{2,1,0:T(8,128)(2,1)S(1)}, bf16[2,40,1792]{2,1,0:T(8,128)(2,1)S(1)}, u32[]{:S(2)}, u32[]{:S(2)}) collective-permute-start(bf16[2,40,1792]{2,1,0:T(8,128)(2,1)S(1)} %get-tuple-element.168.own_ref), channel_id=1, source_target_pairs={{0,8},{8,0},{16,24},{24,16},{1,9},{9,1},{17,25},{25,17},{2,10},{10... | collective-permute-start | bytes 860168 | tf_op jit(solution)/shard_map/ppermute | solution.py:324
  105.6 16.5 %collective-permute-start.25 = (bf16[2,2,40,1792]{3,2,1,0:T(8,128)(2,1)S(1)}, bf16[2,2,40,1792]{3,2,1,0:T(8,128)(2,1)S(1)}, u32[]{:S(2)}, u32[]{:S(2)}) collective-permute-start(bf16[2,2,40,1792]{3,2,1,0:T(8,128)(2,1)S(1)} %get-tuple-element.154), channel_id=1, source_target_pairs={{0,16},{8,24},{16,0},{24,8},{1,17},{9,25},{17,1},{25,9},{2,18},{10... | collective-permute-start | bytes 1720328 | tf_op jit(solution)/shard_map/ppermute | solution.py:324
  106.9 14.2 %collective-permute-start.34 = (bf16[1,40,4096]{2,1,0:T(8,128)(2,1)S(1)}, bf16[1,40,4096]{2,1,0:T(8,128)(2,1)S(1)}, u32[]{:S(2)}, u32[]{:S(2)}) collective-permute-start(bf16[1,40,4096]{2,1,0:T(8,128)(2,1)S(1)} %get-tuple-element.174), channel_id=1, source_target_pairs={{0,2},{1,3},{2,0},{3,1},{4,6},{5,7},{6,4},{7,5},{8,10},{9,11},{10,... | collective-permute-start | bytes 983048 | tf_op jit(solution)/shard_map/ppermute | solution.py:354
  114.1 7.9 %collective-permute-start.33 = (bf16[1,40,4096]{2,1,0:T(8,128)(2,1)S(1)}, bf16[1,40,4096]{2,1,0:T(8,128)(2,1)S(1)}, u32[]{:S(2)}, u32[]{:S(2)}) collective-permute-start(bf16[1,40,4096]{2,1,0:T(8,128)(2,1)S(1)} %get-tuple-element.179), channel_id=1, source_target_pairs={{0,1},{1,0},{2,3},{3,2},{4,5},{5,4},{6,7},{7,6},{8,9},{9,8},{10,11... | collective-permute-start | bytes 983048 | tf_op jit(solution)/shard_map/ppermute | solution.py:324
  115.5 13.3 %collective-permute-start.38 = (bf16[1,40,4096]{2,1,0:T(8,128)(2,1)S(1)}, bf16[1,40,4096]{2,1,0:T(8,128)(2,1)S(1)}, u32[]{:S(2)}, u32[]{:S(2)}) collective-permute-start(bf16[1,40,4096]{2,1,0:T(8,128)(2,1)S(1)} %get-tuple-element.178), channel_id=1, source_target_pairs={{0,2},{1,3},{2,0},{3,1},{4,6},{5,7},{6,4},{7,5},{8,10},{9,11},{10,... | collective-permute-start | bytes 983048 | tf_op jit(solution)/shard_map/ppermute | solution.py:354
  122.4 2.5 %collective-permute-start.35 = (bf16[2,40,1792]{2,1,0:T(8,128)(2,1)S(1)}, bf16[2,40,1792]{2,1,0:T(8,128)(2,1)S(1)}, u32[]{:S(2)}, u32[]{:S(2)}) collective-permute-start(bf16[2,40,1792]{2,1,0:T(8,128)(2,1)S(1)} %get-tuple-element.182.own_ref), channel_id=1, source_target_pairs={{0,8},{8,0},{16,24},{24,16},{1,9},{9,1},{17,25},{25,17},{2,10},{10... | collective-permute-start | bytes 860168 | tf_op jit(solution)/shard_map/ppermute | solution.py:324
  122.5 10.1 %collective-permute-start.36 = (bf16[1,40,4096]{2,1,0:T(8,128)(2,1)S(1)}, bf16[1,40,4096]{2,1,0:T(8,128)(2,1)S(1)}, u32[]{:S(2)}, u32[]{:S(2)}) collective-permute-start(bf16[1,40,4096]{2,1,0:T(8,128)(2,1)S(1)} %get-tuple-element.188), channel_id=1, source_target_pairs={{0,1},{1,0},{2,3},{3,2},{4,5},{5,4},{6,7},{7,6},{8,9},{9,8},{10,11... | collective-permute-start | bytes 983048 | tf_op jit(solution)/shard_map/ppermute | solution.py:324
  123.3 25.4 %collective-permute-start.40 = (bf16[1,40,4096]{2,1,0:T(8,128)(2,1)S(1)}, bf16[1,40,4096]{2,1,0:T(8,128)(2,1)S(1)}, u32[]{:S(2)}, u32[]{:S(2)}) collective-permute-start(bf16[1,40,4096]{2,1,0:T(8,128)(2,1)S(1)} %get-tuple-element.187), channel_id=1, source_target_pairs={{0,4},{1,5},{4,0},{5,1},{2,6},{3,7},{6,2},{7,3},{8,12},{9,13},{12,... | collective-permute-start | bytes 983048 | tf_op jit(solution)/shard_map/ppermute | solution.py:354
  132.7 22.3 %collective-permute-start.39 = (bf16[1,40,4096]{2,1,0:T(8,128)(2,1)S(1)}, bf16[1,40,4096]{2,1,0:T(8,128)(2,1)S(1)}, u32[]{:S(2)}, u32[]{:S(2)}) collective-permute-start(bf16[1,40,4096]{2,1,0:T(8,128)(2,1)S(1)} %get-tuple-element.194), channel_id=1, source_target_pairs={{0,4},{1,5},{4,0},{5,1},{2,6},{3,7},{6,2},{7,3},{8,12},{9,13},{12,... | collective-permute-start | bytes 983048 | tf_op jit(solution)/shard_map/ppermute | solution.py:354
  134.4 16.0 %collective-permute-start.37 = (bf16[2,40,4096]{2,1,0:T(8,128)(2,1)S(1)}, bf16[2,40,4096]{2,1,0:T(8,128)(2,1)S(1)}, u32[]{:S(2)}, u32[]{:S(2)}) collective-permute-start(bf16[2,40,4096]{2,1,0:T(8,128)(2,1)S(1)} %get-tuple-element.189), channel_id=1, source_target_pairs={{0,1},{1,0},{2,3},{3,2},{4,5},{5,4},{6,7},{7,6},{8,9},{9,8},{10,11... | collective-permute-start | bytes 1966088 | tf_op jit(solution)/shard_map/ppermute | solution.py:324
  150.5 4.5 %collective-permute-start.41 = (bf16[40,4096]{1,0:T(8,128)(2,1)S(1)}, bf16[40,4096]{1,0:T(8,128)(2,1)S(1)}, u32[]{:S(2)}, u32[]{:S(2)}) collective-permute-start(bf16[40,4096]{1,0:T(8,128)(2,1)S(1)} %fusion.4), channel_id=1, source_target_pairs={{0,8},{8,0},{16,24},{24,16},{1,9},{9,1},{17,25},{25,17},{2,10},{10... | collective-permute-start | bytes 983048 | tf_op jit(solution)/shard_map/ppermute | solution.py:324

commit v19 on v18

--- a/solution.py
+++ b/solution.py
@@ -471,13 +471,13 @@
     multiply_out(2, pieces=CORES)
     three = to_rows(*rows_in[3, 0], after=[one_out])
     three_out[0] = by_plane(three, NEXT)
-    send_rows(2, [three], CORES, 1)
+    send_rows(2, rows_in[3, 0][1:], CORES, 1)
     two = to_rows(*rows_in[2, 1], three_out[1])
     two_out[1] = by_plane(two, SECOND)
     send_rows(2, [two], CORES, 0)
     to_hidden(0)
     multiply_out(0)
-    two = to_rows(rows_in[2, 0][0], three_out[0], hint=0.5)
+    two = to_rows(rows_in[2, 0][0], three_out[0], hint=0.1)
     two = to_rows(two, *rows_in[2, 0][1:])
     two_out[0] = by_plane(two, SECOND)
     send_rows(0, rows_in[2, 0][1:])

time: 156 us -> 154 us (0.987)
  waiting for transfers between devices: 54.1 us -> 51.9 us
    ppermute x31, waiting for transfers between devices: 26.3 us -> 23.5 us  [swap(): lax.ppermute(values, axis, [(place, place ^ step) for place in range(size)])]
  transfers between devices with their start and end apart: 42 -> 42, of which waited for: 18 -> 19; matrix products, arithmetic and copies ran while one was open for 0% -> 0% of each run, Pallas kernels for 36% -> 36%
where the time goes in v19:
time: 154 us
  Pallas kernels  56.7 us (37%)
  waiting for transfers between devices  51.9 us (34%)
  starting transfers between devices  40.9 us (27%)
  other arithmetic  3.93 us (3%)
    ppermute x11, waiting for transfers between devices, by_plane(): return lax.ppermute(behind(values, after), 'cols', pairs)  28.4 us
    pallas_call x4, Pallas kernels, gate_up(): pl.pallas_call(functools.partial(gate_up_kernel, len(parts), len(after)),...  24.3 us
    ppermute x31, waiting for transfers between devices, swap(): lax.ppermute(values, axis, [(place, place ^ step) for place in range(size)])  23.5 us
    ppermute x31, starting transfers between devices, swap(): lax.ppermute(values, axis, [(place, place ^ step) for place in range(size)])  22.7 us
    ppermute x11, starting transfers between devices, by_plane(): return lax.ppermute(behind(values, after), 'cols', pairs)  18.2 us
    pallas_call x4, Pallas kernels, down(): pl.pallas_call(functools.partial(down_kernel, pieces, len(down_kept), len...  15.5 us
    pallas_call x4, Pallas kernels, masked(): pl.pallas_call(functools.partial(mask_kernel, share, rows, len(after)), i...  13 us
  transfers between devices with their start and end apart: 42, of which 19 were waited for; matrix products, arithmetic and copies ran while one was open for 0% of the time, Pallas kernels for 36%

profile of v19, /device:TPU:0, one launch (start us, length us, event | category | flops | bytes accessed | tf_op | source)
XLA Modules:
  0.0 154.1 jit_solution(10380865822174107810)
XLA Ops:
  0.0 1.3 fusion
  1.3 1.3 fusion.2
  3.3 1.3 collective-permute-done
  5.2 2.9 %collective-permute-start.1 = (bf16[2,1,40,2048]{3,2,1,0:T(8,128)(2,1)S(1)}, bf16[2,1,40,2048]{3,2,1,0:T(8,128)(2,1)S(1)}, u32[]{:S(2)}, u32[]{:S(2)}) collective-permute-start(bf16[2,1,40,2048]{3,2,1,0:T(8,128)(2,1)S(1)} %get-tuple-element.101.refs_2_), channel_id=1, source_target_pairs={{0,16},{8,24},{16,0},{24,8},{1,17},{9,25},{17,1},{25,9},{2,18},{10... | collective-permute-start | bytes 983048 | tf_op jit(solution)/shard_map/ppermute | solution.py:324
  8.1 1.6 %collective-permute-start.6 = (bf16[2,1,40,2048]{3,2,1,0:T(8,128)(2,1)S(1)}, bf16[2,1,40,2048]{3,2,1,0:T(8,128)(2,1)S(1)}, u32[]{:S(2)}, u32[]{:S(2)}) collective-permute-start(bf16[2,1,40,2048]{3,2,1,0:T(8,128)(2,1)S(1)} %get-tuple-element.102.refs_0_), channel_id=1, source_target_pairs={{0,2},{1,3},{2,0},{3,1},{4,6},{5,7},{6,4},{7,5},{8,10},{9,11},{10,... | collective-permute-start | bytes 983048 | tf_op jit(solution)/shard_map/ppermute | solution.py:354
  10.4 1.6 %collective-permute-start.2 = (bf16[2,1,40,2048]{3,2,1,0:T(8,128)(2,1)S(1)}, bf16[2,1,40,2048]{3,2,1,0:T(8,128)(2,1)S(1)}, u32[]{:S(2)}, u32[]{:S(2)}) collective-permute-start(bf16[2,1,40,2048]{3,2,1,0:T(8,128)(2,1)S(1)} %get-tuple-element.102.refs_0_), channel_id=1, source_target_pairs={{0,1},{1,0},{2,3},{3,2},{4,5},{5,4},{6,7},{7,6},{8,9},{9,8},{10,11... | collective-permute-start | bytes 983048 | tf_op jit(solution)/shard_map/ppermute | solution.py:324
  12.0 4.1 %collective-permute-done.1.refs_1_ = bf16[2,1,40,2048]{3,2,1,0:T(8,128)(2,1)S(1)} collective-permute-done((bf16[2,1,40,2048]{3,2,1,0:T(8,128)(2,1)S(1)}, bf16[2,1,40,2048]{3,2,1,0:T(8,128)(2,1)S(1)}, u32[]{:S(2)}, u32[]{:S(2)}) %collective-permute-start.1) | collective-permute-done | bytes 327712 | tf_op jit(solution)/shard_map/ppermute | solution.py:324
  16.1 1.8 %collective-permute-start.7 = (bf16[2,1,40,2048]{3,2,1,0:T(8,128)(2,1)S(1)}, bf16[2,1,40,2048]{3,2,1,0:T(8,128)(2,1)S(1)}, u32[]{:S(2)}, u32[]{:S(2)}) collective-permute-start(bf16[2,1,40,2048]{3,2,1,0:T(8,128)(2,1)S(1)} %collective-permute-done.1.refs_1_), channel_id=1, source_target_pairs={{0,2},{1,3},{2,0},{3,1},{4,6},{5,7},{6,4},{7,5},{8,10},{9,11},{10,... | collective-permute-start | bytes 983048 | tf_op jit(solution)/shard_map/ppermute | solution.py:354
  18.6 1.6 %collective-permute-start.3 = (bf16[2,1,40,2048]{3,2,1,0:T(8,128)(2,1)S(1)}, bf16[2,1,40,2048]{3,2,1,0:T(8,128)(2,1)S(1)}, u32[]{:S(2)}, u32[]{:S(2)}) collective-permute-start(bf16[2,1,40,2048]{3,2,1,0:T(8,128)(2,1)S(1)} %collective-permute-done.1.refs_1_), channel_id=1, source_target_pairs={{0,1},{1,0},{2,3},{3,2},{4,5},{5,4},{6,7},{7,6},{8,9},{9,8},{10,11... | collective-permute-start | bytes 983048 | tf_op jit(solution)/shard_map/ppermute | solution.py:324
  20.2 3.3 %masked.4 = (bf16[2048,1792]{1,0:T(8,128)(2,1)S(1)}, f32[8,128]{1,0:T(8,128)S(1)}) custom-call(s32[1]{0:T(128)} %bitcast.5.core_ref, bf16[2048,1792]{1,0:T(8,128)(2,1)} %weight_ref.4, s32[32,28]{1,0:T(8,128)S(1)} %copy-done.1, f32[8,128]{1,0:T(8,128)S(1)} %get-tuple-element.103.refs_0_), custom_call_target="tpu_custom_call" | custom-call | tf_op jit(solution)/shard_map/masked/pallas_call | solution.py:81
  23.5 3.2 %masked.5 = (bf16[2048,1792]{1,0:T(8,128)(2,1)S(1)}, f32[8,128]{1,0:T(8,128)S(1)}) custom-call(s32[1]{0:T(128)} %bitcast.5.core_ref, bf16[2048,1792]{1,0:T(8,128)(2,1)} %weight_ref.5, s32[32,28]{1,0:T(8,128)S(1)} %copy-done.2, f32[8,128]{1,0:T(8,128)S(1)} %get-tuple-element.106.refs_0_, bf16[2,1,40,2048]{3,2,1,0:T(8,128)(2,1)S(1)} %collective-permute-done.6.refs_1_.refs_0_), custom_call_target="tpu_custom_call" | custom-call | flops 172500000 | tf_op jit(solution)/shard_map/masked/pallas_call | solution.py:81
  26.9 4.5 %collective-permute-start.10 = (bf16[160,2048]{1,0:T(8,128)(2,1)S(1)}, bf16[160,2048]{1,0:T(8,128)(2,1)S(1)}, u32[]{:S(2)}, u32[]{:S(2)}) collective-permute-start(bf16[160,2048]{1,0:T(8,128)(2,1)S(1)} %get-tuple-element.118.refs_0_.mine_ref), channel_id=1, source_target_pairs={{0,6},{1,7},{6,0},{7,1},{8,14},{9,15},{14,8},{15,9},{16,22},{17,23... | collective-permute-start | bytes 1966088 | tf_op jit(solution)/shard_map/ppermute | solution.py:354
  31.5 1.1 collective-permute-start.12
  32.5 6.1 %gate_up.4 = (bf16[2,2,2,40,1792]{4,3,2,1,0:T(8,128)(2,1)S(1)}, bf16[2,2,40,1792]{3,2,1,0:T(8,128)(2,1)S(1)}, bf16[2,2,1,40,1792]{4,3,2,1,0:T(8,128)(2,1)S(1)}, f32[8,128]{1,0:T(8,128)S(1)}) custom-call(bf16[160,2048]{1,0:T(8,128)(2,1)S(1)} %get-tuple-element.118.refs_0_.mine_ref, bf16[160,2048]{1,0:T(8,128)(2,1)S(1)} %get-tuple-element.110.refs_1_, ...), custom_call_target="tpu_custom_call" | custom-call | flops 4697620480 | tf_op jit(solution)/shard_map/gate_up/pallas_call | solution.py:206
  39.2 3.3 %masked.6 = (bf16[1792,2048]{1,0:T(8,128)(2,1)S(1)}, f32[8,128]{1,0:T(8,128)S(1)}) custom-call(s32[1]{0:T(128)} %bitcast.5.core_ref, bf16[1792,8192]{1,0:T(8,128)(2,1)} %weight_ref.7, s32[28,128]{1,0:T(8,128)S(1)} %copy-done, f32[8,128]{1,0:T(8,128)S(1)} %get-tuple-element.119.refs_0_), custom_call_target="tpu_custom_call" | custom-call | tf_op jit(solution)/shard_map/masked/pallas_call | solution.py:81
  42.5 3.5 %collective-permute-done.10.outer_three_ref = bf16[160,2048]{1,0:T(8,128)(2,1)S(1)} collective-permute-done((bf16[160,2048]{1,0:T(8,128)(2,1)S(1)}, bf16[160,2048]{1,0:T(8,128)(2,1)S(1)}, u32[]{:S(2)}, u32[]{:S(2)}) %collective-permute-start.10) | collective-permute-done | bytes 655392 | tf_op jit(solution)/shard_map/ppermute | solution.py:354
  47.3 1.1 collective-permute-start.11
  48.3 6.1 %gate_up.5 = (bf16[2,2,2,40,1792]{4,3,2,1,0:T(8,128)(2,1)S(1)}, bf16[2,2,40,1792]{3,2,1,0:T(8,128)(2,1)S(1)}, bf16[2,2,1,40,1792]{4,3,2,1,0:T(8,128)(2,1)S(1)}, f32[8,128]{1,0:T(8,128)S(1)}) custom-call(bf16[160,2048]{1,0:T(8,128)(2,1)S(1)} %get-tuple-element.125.refs_0_, bf16[160,2048]{1,0:T(8,128)(2,1)S(1)} %collective-permute-done.12.refs_1_, ...), custom_call_target="tpu_custom_call" | custom-call | flops 4697620480 | tf_op jit(solution)/shard_map/gate_up/pallas_call | solution.py:206
  55.0 1.5 collective-permute-done.13.refs_1_
  56.5 0.8 collective-permute-done.14.refs_3_.refs_1_
  57.4 1.6 %collective-permute-start.16 = (bf16[2,2,40,1792]{3,2,1,0:T(8,128)(2,1)S(1)}, bf16[2,2,40,1792]{3,2,1,0:T(8,128)(2,1)S(1)}, u32[]{:S(2)}, u32[]{:S(2)}) collective-permute-start(bf16[2,2,40,1792]{3,2,1,0:T(8,128)(2,1)S(1)} %get-tuple-element.134), channel_id=1, source_target_pairs={{0,16},{8,24},{16,0},{24,8},{1,17},{9,25},{17,1},{25,9},{2,18},{10... | collective-permute-start | bytes 1720328 | tf_op jit(solution)/shard_map/ppermute | solution.py:324
  59.0 3.3 %masked.7 = (bf16[1792,2048]{1,0:T(8,128)(2,1)S(1)}, f32[8,128]{1,0:T(8,128)S(1)}) custom-call(s32[1]{0:T(128)} %bitcast.5.core_ref, bf16[1792,8192]{1,0:T(8,128)(2,1)} %weight_ref.7, s32[28,128]{1,0:T(8,128)S(1)} %copy-done, f32[8,128]{1,0:T(8,128)S(1)} %get-tuple-element.131.refs_0_), custom_call_target="tpu_custom_call" | custom-call | tf_op jit(solution)/shard_map/masked/pallas_call | solution.py:81
  62.3 0.7 collective-permute-start.15
  63.0 6.1 %gate_up.6 = (bf16[2,2,2,40,1792]{4,3,2,1,0:T(8,128)(2,1)S(1)}, bf16[2,2,40,1792]{3,2,1,0:T(8,128)(2,1)S(1)}, bf16[2,2,1,40,1792]{4,3,2,1,0:T(8,128)(2,1)S(1)}, f32[8,128]{1,0:T(8,128)S(1)}) custom-call(bf16[160,2048]{1,0:T(8,128)(2,1)S(1)} %get-tuple-element.136.refs_0_, bf16[160,2048]{1,0:T(8,128)(2,1)S(1)} %collective-permute-done.17.refs_1_, ...), custom_call_target="tpu_custom_call" | custom-call | flops 4697620480 | tf_op jit(solution)/shard_map/gate_up/pallas_call | solution.py:206
  69.7 2.8 %collective-permute-done.16.refs_2_ = bf16[2,2,40,1792]{3,2,1,0:T(8,128)(2,1)S(1)} collective-permute-done((bf16[2,2,40,1792]{3,2,1,0:T(8,128)(2,1)S(1)}, bf16[2,2,40,1792]{3,2,1,0:T(8,128)(2,1)S(1)}, u32[]{:S(2)}, u32[]{:S(2)}) %collective-permute-start.16) | collective-permute-done | bytes 573472 | tf_op jit(solution)/shard_map/ppermute | solution.py:324
  73.1 1.6 %collective-permute-start.23 = (bf16[2,2,40,1792]{3,2,1,0:T(8,128)(2,1)S(1)}, bf16[2,2,40,1792]{3,2,1,0:T(8,128)(2,1)S(1)}, u32[]{:S(2)}, u32[]{:S(2)}) collective-permute-start(bf16[2,2,40,1792]{3,2,1,0:T(8,128)(2,1)S(1)} %get-tuple-element.150), channel_id=1, source_target_pairs={{0,16},{8,24},{16,0},{24,8},{1,17},{9,25},{17,1},{25,9},{2,18},{10... | collective-permute-start | bytes 1720328 | tf_op jit(solution)/shard_map/ppermute | solution.py:324
  74.6 3.9 %down.4 = (bf16[2,40,4096]{2,1,0:T(8,128)(2,1)S(1)}, bf16[2,40,4096]{2,1,0:T(8,128)(2,1)S(1)}, f32[8,128]{1,0:T(8,128)S(1)}) custom-call(bf16[2,40,1792]{2,1,0:T(8,128)(2,1)S(1)} %get-tuple-element.138.own_ref, bf16[2,40,1792]{2,1,0:T(8,128)(2,1)S(1)} %collective-permute-done.18.other_ref, bf16[1792,2048]{1,0:T(8,128)(2,1)S(1)} %get-tuple-element.139.refs_0_, ...), custom_call_target="tpu_custom_call" | custom-call | flops 2348810 | tf_op jit(solution)/shard_map/down/pallas_call | solution.py:248
  79.5 6.1 %gate_up.7 = (bf16[2,2,2,40,1792]{4,3,2,1,0:T(8,128)(2,1)S(1)}, bf16[2,2,40,1792]{3,2,1,0:T(8,128)(2,1)S(1)}, bf16[1,2,1,40,1792]{4,3,2,1,0:T(8,128)(2,1)S(1)}, ...) custom-call(bf16[160,2048]{1,0:T(8,128)(2,1)S(1)} %collective-permute-done.11.refs_5_.refs_0_, ...), custom_call_target="tpu_custom_call" | custom-call | flops 4697620480 | tf_op jit(solution)/shard_map/gate_up/pallas_call | solution.py:206
  86.2 2.3 %collective-permute-done.23.refs_2_ = bf16[2,2,40,1792]{3,2,1,0:T(8,128)(2,1)S(1)} collective-permute-done((bf16[2,2,40,1792]{3,2,1,0:T(8,128)(2,1)S(1)}, bf16[2,2,40,1792]{3,2,1,0:T(8,128)(2,1)S(1)}, u32[]{:S(2)}, u32[]{:S(2)}) %collective-permute-start.23) | collective-permute-done | bytes 573472 | tf_op jit(solution)/shard_map/ppermute | solution.py:324
  89.6 1.5 collective-permute-start.24
  91.1 3.9 %down.5 = (bf16[1,40,4096]{2,1,0:T(8,128)(2,1)S(1)}, bf16[1,40,4096]{2,1,0:T(8,128)(2,1)S(1)}, bf16[1,40,4096]{2,1,0:T(8,128)(2,1)S(1)}, bf16[1,40,4096]{2,1,0:T(8,128)(2,1)S(1)}, f32[8,128]{1,0:T(8,128)S(1)}) custom-call(bf16[2,40,1792]{2,1,0:T(8,128)(2,1)S(1)} %get-tuple-element.158.own_ref, bf16[2,40,1792]{2,1,0:T(8,128)(2,1)S(1)} %collective-permute-done.27.other_ref, ...), custom_call_target="tpu_custom_call" | custom-call | flops 2348810 | tf_op jit(solution)/shard_map/down/pallas_call | solution.py:248
  96.3 1.6 %collective-permute-start.34 = (bf16[2,40,4096]{2,1,0:T(8,128)(2,1)S(1)}, bf16[2,40,4096]{2,1,0:T(8,128)(2,1)S(1)}, u32[]{:S(2)}, u32[]{:S(2)}) collective-permute-start(bf16[2,40,4096]{2,1,0:T(8,128)(2,1)S(1)} %get-tuple-element.178), channel_id=1, source_target_pairs={{0,2},{1,3},{2,0},{3,1},{4,6},{5,7},{6,4},{7,5},{8,10},{9,11},{10,... | collective-permute-start | bytes 1966088 | tf_op jit(solution)/shard_map/ppermute | solution.py:354
  97.9 6.5 %collective-permute-done.29.refs_1_ = bf16[1,40,4096]{2,1,0:T(8,128)(2,1)S(1)} collective-permute-done((bf16[1,40,4096]{2,1,0:T(8,128)(2,1)S(1)}, bf16[1,40,4096]{2,1,0:T(8,128)(2,1)S(1)}, u32[]{:S(2)}, u32[]{:S(2)}) %collective-permute-start.29) | collective-permute-done | bytes 327712 | tf_op jit(solution)/shard_map/ppermute | solution.py:324
  105.6 1.2 collective-permute-start.25
  106.9 1.6 %collective-permute-start.33 = (bf16[1,40,4096]{2,1,0:T(8,128)(2,1)S(1)}, bf16[1,40,4096]{2,1,0:T(8,128)(2,1)S(1)}, u32[]{:S(2)}, u32[]{:S(2)}) collective-permute-start(bf16[1,40,4096]{2,1,0:T(8,128)(2,1)S(1)} %get-tuple-element.173), channel_id=1, source_target_pairs={{0,2},{1,3},{2,0},{3,1},{4,6},{5,7},{6,4},{7,5},{8,10},{9,11},{10,... | collective-permute-start | bytes 983048 | tf_op jit(solution)/shard_map/ppermute | solution.py:354
  108.5 3.9 %down.6 = (bf16[1,40,4096]{2,1,0:T(8,128)(2,1)S(1)}, bf16[1,40,4096]{2,1,0:T(8,128)(2,1)S(1)}, bf16[1,40,4096]{2,1,0:T(8,128)(2,1)S(1)}, bf16[1,40,4096]{2,1,0:T(8,128)(2,1)S(1)}, f32[8,128]{1,0:T(8,128)S(1)}) custom-call(bf16[2,40,1792]{2,1,0:T(8,128)(2,1)S(1)} %get-tuple-element.168.own_ref, bf16[2,40,1792]{2,1,0:T(8,128)(2,1)S(1)} %collective-permute-done.30.other_ref, ...), custom_call_target="tpu_custom_call" | custom-call | flops 2348810 | tf_op jit(solution)/shard_map/down/pallas_call | solution.py:248
  114.1 1.6 %collective-permute-start.38 = (bf16[1,40,4096]{2,1,0:T(8,128)(2,1)S(1)}, bf16[1,40,4096]{2,1,0:T(8,128)(2,1)S(1)}, u32[]{:S(2)}, u32[]{:S(2)}) collective-permute-start(bf16[1,40,4096]{2,1,0:T(8,128)(2,1)S(1)} %get-tuple-element.190), channel_id=1, source_target_pairs={{0,2},{1,3},{2,0},{3,1},{4,6},{5,7},{6,4},{7,5},{8,10},{9,11},{10,... | collective-permute-start | bytes 983048 | tf_op jit(solution)/shard_map/ppermute | solution.py:354
  115.7 5.3 %collective-permute-done.33.refs_2_ = bf16[1,40,4096]{2,1,0:T(8,128)(2,1)S(1)} collective-permute-done((bf16[1,40,4096]{2,1,0:T(8,128)(2,1)S(1)}, bf16[1,40,4096]{2,1,0:T(8,128)(2,1)S(1)}, u32[]{:S(2)}, u32[]{:S(2)}) %collective-permute-start.33) | collective-permute-done | bytes 327712 | tf_op jit(solution)/shard_map/ppermute | solution.py:354
  121.0 0.9 collective-permute-done.32.refs_1_
  122.1 0.8 collective-permute-start.36
  122.8 1.5 collective-permute-start.40
  124.7 1.6 %collective-permute-done.35.other_ref = bf16[2,40,1792]{2,1,0:T(8,128)(2,1)S(1)} collective-permute-done((bf16[2,40,1792]{2,1,0:T(8,128)(2,1)S(1)}, bf16[2,40,1792]{2,1,0:T(8,128)(2,1)S(1)}, u32[]{:S(2)}, u32[]{:S(2)}) %collective-permute-start.35) | collective-permute-done | bytes 286752 | tf_op jit(solution)/shard_map/ppermute | solution.py:324
  126.3 3.9 %down.7 = (bf16[2,40,4096]{2,1,0:T(8,128)(2,1)S(1)}, bf16[2,40,4096]{2,1,0:T(8,128)(2,1)S(1)}, f32[8,128]{1,0:T(8,128)S(1)}) custom-call(bf16[2,40,1792]{2,1,0:T(8,128)(2,1)S(1)} %get-tuple-element.181.own_ref, bf16[2,40,1792]{2,1,0:T(8,128)(2,1)S(1)} %collective-permute-done.35.other_ref, bf16[1792,2048]{1,0:T(8,128)(2,1)S(1)} %get-tuple-element.139.refs_0_, ...), custom_call_target="tpu_custom_call" | custom-call | flops 2348810 | tf_op jit(solution)/shard_map/down/pallas_call | solution.py:248
  130.5 1.4 collective-permute-start.39
  131.9 1.2 collective-permute-start.37
  133.1 14.7 %collective-permute-done.40.refs_0_ = bf16[1,40,4096]{2,1,0:T(8,128)(2,1)S(1)} collective-permute-done((bf16[1,40,4096]{2,1,0:T(8,128)(2,1)S(1)}, bf16[1,40,4096]{2,1,0:T(8,128)(2,1)S(1)}, u32[]{:S(2)}, u32[]{:S(2)}) %collective-permute-start.40) | collective-permute-done | bytes 327712 | tf_op jit(solution)/shard_map/ppermute | solution.py:354
  148.6 4.3 %collective-permute-done.39 = bf16[1,40,4096]{2,1,0:T(8,128)(2,1)S(1)} collective-permute-done((bf16[1,40,4096]{2,1,0:T(8,128)(2,1)S(1)}, bf16[1,40,4096]{2,1,0:T(8,128)(2,1)S(1)}, u32[]{:S(2)}, u32[]{:S(2)}) %collective-permute-start.39) | collective-permute-done | bytes 327712 | tf_op jit(solution)/shard_map/ppermute | solution.py:354
  153.2 0.9 pad_maximum_fusion
  (87 shorter events, 15.2 us)
Async XLA Ops:
  2.7 17.4 %copy-start.1 = (s32[32,28]{1,0:T(8,128)S(1)}, s32[32,28]{1,0:T(8,128)}, u32[]{:S(2)}) copy-start(s32[32,28]{1,0:T(8,128)} %mask_ref.4) | copy-start | bytes 10756
  2.8 1.8 %collective-permute-start = (bf16[2,40,2048]{2,1,0:T(8,128)(2,1)S(1)}, bf16[2,40,2048]{2,1,0:T(8,128)(2,1)S(1)}, u32[]{:S(2)}, u32[]{:S(2)}) collective-permute-start(bf16[2,40,2048]{2,1,0:T(8,128)(2,1)S(1)} %pad_maximum_fusion.1), channel_id=1, source_target_pairs={{0,8},{8,0},{16,24},{24,16},{1,9},{9,1},{17,25},{25,17},{2,10},{10... | collective-permute-start | bytes 983048 | tf_op jit(solution)/shard_map/ppermute | solution.py:324
  5.2 10.9 %collective-permute-start.1 = (bf16[2,1,40,2048]{3,2,1,0:T(8,128)(2,1)S(1)}, bf16[2,1,40,2048]{3,2,1,0:T(8,128)(2,1)S(1)}, u32[]{:S(2)}, u32[]{:S(2)}) collective-permute-start(bf16[2,1,40,2048]{3,2,1,0:T(8,128)(2,1)S(1)} %get-tuple-element.101.refs_2_), channel_id=1, source_target_pairs={{0,16},{8,24},{16,0},{24,8},{1,17},{9,25},{17,1},{25,9},{2,18},{10... | collective-permute-start | bytes 983048 | tf_op jit(solution)/shard_map/ppermute | solution.py:324
  8.1 10.5 %collective-permute-start.6 = (bf16[2,1,40,2048]{3,2,1,0:T(8,128)(2,1)S(1)}, bf16[2,1,40,2048]{3,2,1,0:T(8,128)(2,1)S(1)}, u32[]{:S(2)}, u32[]{:S(2)}) collective-permute-start(bf16[2,1,40,2048]{3,2,1,0:T(8,128)(2,1)S(1)} %get-tuple-element.102.refs_0_), channel_id=1, source_target_pairs={{0,2},{1,3},{2,0},{3,1},{4,6},{5,7},{6,4},{7,5},{8,10},{9,11},{10,... | collective-permute-start | bytes 983048 | tf_op jit(solution)/shard_map/ppermute | solution.py:354
  9.7 17.0 %collective-permute-start.4 = (bf16[2,1,40,2048]{3,2,1,0:T(8,128)(2,1)S(1)}, bf16[2,1,40,2048]{3,2,1,0:T(8,128)(2,1)S(1)}, u32[]{:S(2)}, u32[]{:S(2)}) collective-permute-start(bf16[2,1,40,2048]{3,2,1,0:T(8,128)(2,1)S(1)} %get-tuple-element.102.refs_0_), channel_id=1, source_target_pairs={{2,4},{3,5},{4,2},{5,3},{10,12},{11,13},{12,10},{13,11},{18,20},{1... | collective-permute-start | bytes 983048 | tf_op jit(solution)/shard_map/ppermute | solution.py:354
  10.4 16.4 %collective-permute-start.2 = (bf16[2,1,40,2048]{3,2,1,0:T(8,128)(2,1)S(1)}, bf16[2,1,40,2048]{3,2,1,0:T(8,128)(2,1)S(1)}, u32[]{:S(2)}, u32[]{:S(2)}) collective-permute-start(bf16[2,1,40,2048]{3,2,1,0:T(8,128)(2,1)S(1)} %get-tuple-element.102.refs_0_), channel_id=1, source_target_pairs={{0,1},{1,0},{2,3},{3,2},{4,5},{5,4},{6,7},{7,6},{8,9},{9,8},{10,11... | collective-permute-start | bytes 983048 | tf_op jit(solution)/shard_map/ppermute | solution.py:324
  16.1 10.7 %collective-permute-start.7 = (bf16[2,1,40,2048]{3,2,1,0:T(8,128)(2,1)S(1)}, bf16[2,1,40,2048]{3,2,1,0:T(8,128)(2,1)S(1)}, u32[]{:S(2)}, u32[]{:S(2)}) collective-permute-start(bf16[2,1,40,2048]{3,2,1,0:T(8,128)(2,1)S(1)} %collective-permute-done.1.refs_1_), channel_id=1, source_target_pairs={{0,2},{1,3},{2,0},{3,1},{4,6},{5,7},{6,4},{7,5},{8,10},{9,11},{10,... | collective-permute-start | bytes 983048 | tf_op jit(solution)/shard_map/ppermute | solution.py:354
  17.9 9.0 %collective-permute-start.5 = (bf16[2,1,40,2048]{3,2,1,0:T(8,128)(2,1)S(1)}, bf16[2,1,40,2048]{3,2,1,0:T(8,128)(2,1)S(1)}, u32[]{:S(2)}, u32[]{:S(2)}) collective-permute-start(bf16[2,1,40,2048]{3,2,1,0:T(8,128)(2,1)S(1)} %collective-permute-done.1.refs_1_), channel_id=1, source_target_pairs={{2,4},{3,5},{4,2},{5,3},{10,12},{11,13},{12,10},{13,11},{18,20},{1... | collective-permute-start | bytes 983048 | tf_op jit(solution)/shard_map/ppermute | solution.py:354
  18.6 12.8 %collective-permute-start.3 = (bf16[2,1,40,2048]{3,2,1,0:T(8,128)(2,1)S(1)}, bf16[2,1,40,2048]{3,2,1,0:T(8,128)(2,1)S(1)}, u32[]{:S(2)}, u32[]{:S(2)}) collective-permute-start(bf16[2,1,40,2048]{3,2,1,0:T(8,128)(2,1)S(1)} %collective-permute-done.1.refs_1_), channel_id=1, source_target_pairs={{0,1},{1,0},{2,3},{3,2},{4,5},{5,4},{6,7},{7,6},{8,9},{9,8},{10,11... | collective-permute-start | bytes 983048 | tf_op jit(solution)/shard_map/ppermute | solution.py:324
  20.2 3.3 %copy-start.2 = (s32[32,28]{1,0:T(8,128)S(1)}, s32[32,28]{1,0:T(8,128)}, u32[]{:S(2)}) copy-start(s32[32,28]{1,0:T(8,128)} %mask_ref.5) | copy-start | bytes 10756
  26.9 19.1 %collective-permute-start.10 = (bf16[160,2048]{1,0:T(8,128)(2,1)S(1)}, bf16[160,2048]{1,0:T(8,128)(2,1)S(1)}, u32[]{:S(2)}, u32[]{:S(2)}) collective-permute-start(bf16[160,2048]{1,0:T(8,128)(2,1)S(1)} %get-tuple-element.118.refs_0_.mine_ref), channel_id=1, source_target_pairs={{0,6},{1,7},{6,0},{7,1},{8,14},{9,15},{14,8},{15,9},{16,22},{17,23... | collective-permute-start | bytes 1966088 | tf_op jit(solution)/shard_map/ppermute | solution.py:354
  31.5 15.1 %collective-permute-start.12 = (bf16[160,2048]{1,0:T(8,128)(2,1)S(1)}, bf16[160,2048]{1,0:T(8,128)(2,1)S(1)}, u32[]{:S(2)}, u32[]{:S(2)}) collective-permute-start(bf16[160,2048]{1,0:T(8,128)(2,1)S(1)} %get-tuple-element.125.refs_0_), channel_id=1, source_target_pairs={{0,1},{1,0},{2,3},{3,2},{4,5},{5,4},{6,7},{7,6},{8,9},{9,8},{10,11... | collective-permute-start | bytes 1966088 | tf_op jit(solution)/shard_map/ppermute | solution.py:324
  32.5 6.7 %copy-start = (s32[28,128]{1,0:T(8,128)S(1)}, s32[28,128]{1,0:T(8,128)}, u32[]{:S(2)}) copy-start(s32[28,128]{1,0:T(8,128)} %mask_ref.7) | copy-start | bytes 43012
  38.6 7.5 %collective-permute-start.8 = (bf16[2,2,40,1792]{3,2,1,0:T(8,128)(2,1)S(1)}, bf16[2,2,40,1792]{3,2,1,0:T(8,128)(2,1)S(1)}, u32[]{:S(2)}, u32[]{:S(2)}) collective-permute-start(bf16[2,2,40,1792]{3,2,1,0:T(8,128)(2,1)S(1)} %get-tuple-element.115), channel_id=1, source_target_pairs={{0,8},{8,0},{16,24},{24,16},{1,9},{9,1},{17,25},{25,17},{2,10},{10... | collective-permute-start | bytes 1720328 | tf_op jit(solution)/shard_map/ppermute | solution.py:324
  38.7 7.4 %collective-permute-start.9 = (bf16[2,2,1,40,1792]{4,3,2,1,0:T(8,128)(2,1)S(1)}, bf16[2,2,1,40,1792]{4,3,2,1,0:T(8,128)(2,1)S(1)}, u32[]{:S(2)}, u32[]{:S(2)}) collective-permute-start(bf16[2,2,1,40,1792]{4,3,2,1,0:T(8,128)(2,1)S(1)} %get-tuple-element.116), channel_id=1, source_target_pairs={{0,8},{8,0},{16,24},{24,16},{1,9},{9,1},{17,25},{25,17},{2,10},{10... | collective-permute-start | bytes 1720328 | tf_op jit(solution)/shard_map/ppermute | solution.py:324
  46.6 16.4 %collective-permute-start.17 = (bf16[160,2048]{1,0:T(8,128)(2,1)S(1)}, bf16[160,2048]{1,0:T(8,128)(2,1)S(1)}, u32[]{:S(2)}, u32[]{:S(2)}) collective-permute-start(bf16[160,2048]{1,0:T(8,128)(2,1)S(1)} %get-tuple-element.136.refs_0_), channel_id=1, source_target_pairs={{0,1},{1,0},{2,3},{3,2},{4,5},{5,4},{6,7},{7,6},{8,9},{9,8},{10,11... | collective-permute-start | bytes 1966088 | tf_op jit(solution)/shard_map/ppermute | solution.py:324
  47.3 15.0 %collective-permute-start.11 = (bf16[160,2048]{1,0:T(8,128)(2,1)S(1)}, bf16[160,2048]{1,0:T(8,128)(2,1)S(1)}, u32[]{:S(2)}, u32[]{:S(2)}) collective-permute-start(bf16[160,2048]{1,0:T(8,128)(2,1)S(1)} %get-tuple-element.123), channel_id=1, source_target_pairs={{0,4},{1,5},{4,6},{5,7},{6,2},{7,3},{2,0},{3,1},{8,12},{9,13},{12,... | collective-permute-start | bytes 1966088 | tf_op jit(solution)/shard_map/ppermute | solution.py:354
  54.4 2.0 %collective-permute-start.13 = (bf16[2,2,1,40,1792]{4,3,2,1,0:T(8,128)(2,1)S(1)}, bf16[2,2,1,40,1792]{4,3,2,1,0:T(8,128)(2,1)S(1)}, u32[]{:S(2)}, u32[]{:S(2)}) collective-permute-start(bf16[2,2,1,40,1792]{4,3,2,1,0:T(8,128)(2,1)S(1)} %get-tuple-element.128), channel_id=1, source_target_pairs={{0,8},{8,0},{16,24},{24,16},{1,9},{9,1},{17,25},{25,17},{2,10},{10... | collective-permute-start | bytes 1720328 | tf_op jit(solution)/shard_map/ppermute | solution.py:324
  54.5 2.8 %collective-permute-start.14 = (bf16[2,2,40,1792]{3,2,1,0:T(8,128)(2,1)S(1)}, bf16[2,2,40,1792]{3,2,1,0:T(8,128)(2,1)S(1)}, u32[]{:S(2)}, u32[]{:S(2)}) collective-permute-start(bf16[2,2,40,1792]{3,2,1,0:T(8,128)(2,1)S(1)} %get-tuple-element.130), channel_id=1, source_target_pairs={{0,8},{8,0},{16,24},{24,16},{1,9},{9,1},{17,25},{25,17},{2,10},{10... | collective-permute-start | bytes 1720328 | tf_op jit(solution)/shard_map/ppermute | solution.py:324
  57.4 15.1 %collective-permute-start.16 = (bf16[2,2,40,1792]{3,2,1,0:T(8,128)(2,1)S(1)}, bf16[2,2,40,1792]{3,2,1,0:T(8,128)(2,1)S(1)}, u32[]{:S(2)}, u32[]{:S(2)}) collective-permute-start(bf16[2,2,40,1792]{3,2,1,0:T(8,128)(2,1)S(1)} %get-tuple-element.134), channel_id=1, source_target_pairs={{0,16},{8,24},{16,0},{24,8},{1,17},{9,25},{17,1},{25,9},{2,18},{10... | collective-permute-start | bytes 1720328 | tf_op jit(solution)/shard_map/ppermute | solution.py:324
  62.3 16.6 %collective-permute-start.15 = (bf16[160,2048]{1,0:T(8,128)(2,1)S(1)}, bf16[160,2048]{1,0:T(8,128)(2,1)S(1)}, u32[]{:S(2)}, u32[]{:S(2)}) collective-permute-start(bf16[160,2048]{1,0:T(8,128)(2,1)S(1)} %collective-permute-done.11.refs_5_.refs_0_), channel_id=1, source_target_pairs={{0,1},{1,0},{2,3},{3,2},{4,5},{5,4},{6,7},{7,6},{8,9},{9,8},{10,11... | collective-permute-start | bytes 1966088 | tf_op jit(solution)/shard_map/ppermute | solution.py:324
  69.1 3.8 %collective-permute-start.19 = (bf16[2,2,1,40,1792]{4,3,2,1,0:T(8,128)(2,1)S(1)}, bf16[2,2,1,40,1792]{4,3,2,1,0:T(8,128)(2,1)S(1)}, u32[]{:S(2)}, u32[]{:S(2)}) collective-permute-start(bf16[2,2,1,40,1792]{4,3,2,1,0:T(8,128)(2,1)S(1)} %get-tuple-element.142), channel_id=1, source_target_pairs={{0,8},{8,0},{16,24},{24,16},{1,9},{9,1},{17,25},{25,17},{2,10},{10... | collective-permute-start | bytes 1720328 | tf_op jit(solution)/shard_map/ppermute | solution.py:324
  69.2 3.7 %collective-permute-start.20 = (bf16[2,2,40,1792]{3,2,1,0:T(8,128)(2,1)S(1)}, bf16[2,2,40,1792]{3,2,1,0:T(8,128)(2,1)S(1)}, u32[]{:S(2)}, u32[]{:S(2)}) collective-permute-start(bf16[2,2,40,1792]{3,2,1,0:T(8,128)(2,1)S(1)} %get-tuple-element.144), channel_id=1, source_target_pairs={{0,8},{8,0},{16,24},{24,16},{1,9},{9,1},{17,25},{25,17},{2,10},{10... | collective-permute-start | bytes 1720328 | tf_op jit(solution)/shard_map/ppermute | solution.py:324
  72.8 1.8 %collective-permute-start.18 = (bf16[2,40,1792]{2,1,0:T(8,128)(2,1)S(1)}, bf16[2,40,1792]{2,1,0:T(8,128)(2,1)S(1)}, u32[]{:S(2)}, u32[]{:S(2)}) collective-permute-start(bf16[2,40,1792]{2,1,0:T(8,128)(2,1)S(1)} %get-tuple-element.138.own_ref), channel_id=1, source_target_pairs={{0,8},{8,0},{16,24},{24,16},{1,9},{9,1},{17,25},{25,17},{2,10},{10... | collective-permute-start | bytes 860168 | tf_op jit(solution)/shard_map/ppermute | solution.py:324
  73.1 15.4 %collective-permute-start.23 = (bf16[2,2,40,1792]{3,2,1,0:T(8,128)(2,1)S(1)}, bf16[2,2,40,1792]{3,2,1,0:T(8,128)(2,1)S(1)}, u32[]{:S(2)}, u32[]{:S(2)}) collective-permute-start(bf16[2,2,40,1792]{3,2,1,0:T(8,128)(2,1)S(1)} %get-tuple-element.150), channel_id=1, source_target_pairs={{0,16},{8,24},{16,0},{24,8},{1,17},{9,25},{17,1},{25,9},{2,18},{10... | collective-permute-start | bytes 1720328 | tf_op jit(solution)/shard_map/ppermute | solution.py:324
  78.8 16.6 %collective-permute-start.28 = (bf16[2,40,4096]{2,1,0:T(8,128)(2,1)S(1)}, bf16[2,40,4096]{2,1,0:T(8,128)(2,1)S(1)}, u32[]{:S(2)}, u32[]{:S(2)}) collective-permute-start(bf16[2,40,4096]{2,1,0:T(8,128)(2,1)S(1)} %get-tuple-element.162), channel_id=1, source_target_pairs={{0,1},{1,0},{2,3},{3,2},{4,5},{5,4},{6,7},{7,6},{8,9},{9,8},{10,11... | collective-permute-start | bytes 1966088 | tf_op jit(solution)/shard_map/ppermute | solution.py:324
  85.6 3.3 %collective-permute-start.21 = (bf16[1,2,1,40,1792]{4,3,2,1,0:T(8,128)(2,1)S(1)}, bf16[1,2,1,40,1792]{4,3,2,1,0:T(8,128)(2,1)S(1)}, u32[]{:S(2)}, u32[]{:S(2)}) collective-permute-start(bf16[1,2,1,40,1792]{4,3,2,1,0:T(8,128)(2,1)S(1)} %get-tuple-element.148), channel_id=1, source_target_pairs={{0,8},{8,0},{16,24},{24,16},{1,9},{9,1},{17,25},{25,17},{2,10},{10... | collective-permute-start | bytes 860168 | tf_op jit(solution)/shard_map/ppermute | solution.py:324
  85.7 3.2 %collective-permute-start.22 = (bf16[1,2,1,40,1792]{4,3,2,1,0:T(8,128)(2,1)S(1)}, bf16[1,2,1,40,1792]{4,3,2,1,0:T(8,128)(2,1)S(1)}, u32[]{:S(2)}, u32[]{:S(2)}) collective-permute-start(bf16[1,2,1,40,1792]{4,3,2,1,0:T(8,128)(2,1)S(1)} %get-tuple-element.149), channel_id=1, source_target_pairs={{0,8},{8,0},{16,24},{24,16},{1,9},{9,1},{17,25},{25,17},{2,10},{10... | collective-permute-start | bytes 860168 | tf_op jit(solution)/shard_map/ppermute | solution.py:324
  88.8 2.3 %collective-permute-start.27 = (bf16[2,40,1792]{2,1,0:T(8,128)(2,1)S(1)}, bf16[2,40,1792]{2,1,0:T(8,128)(2,1)S(1)}, u32[]{:S(2)}, u32[]{:S(2)}) collective-permute-start(bf16[2,40,1792]{2,1,0:T(8,128)(2,1)S(1)} %get-tuple-element.158.own_ref), channel_id=1, source_target_pairs={{0,8},{8,0},{16,24},{24,16},{1,9},{9,1},{17,25},{25,17},{2,10},{10... | collective-permute-start | bytes 860168 | tf_op jit(solution)/shard_map/ppermute | solution.py:324
  89.0 16.2 %collective-permute-start.26 = (bf16[2,2,40,1792]{3,2,1,0:T(8,128)(2,1)S(1)}, bf16[2,2,40,1792]{3,2,1,0:T(8,128)(2,1)S(1)}, u32[]{:S(2)}, u32[]{:S(2)}) collective-permute-start(bf16[2,2,40,1792]{3,2,1,0:T(8,128)(2,1)S(1)} %get-tuple-element.157), channel_id=1, source_target_pairs={{0,8},{8,0},{16,24},{24,16},{1,9},{9,1},{17,25},{25,17},{2,10},{10... | collective-permute-start | bytes 1720328 | tf_op jit(solution)/shard_map/ppermute | solution.py:324
  89.6 15.7 %collective-permute-start.24 = (bf16[2,2,40,1792]{3,2,1,0:T(8,128)(2,1)S(1)}, bf16[2,2,40,1792]{3,2,1,0:T(8,128)(2,1)S(1)}, u32[]{:S(2)}, u32[]{:S(2)}) collective-permute-start(bf16[2,2,40,1792]{3,2,1,0:T(8,128)(2,1)S(1)} %get-tuple-element.153), channel_id=1, source_target_pairs={{0,16},{8,24},{16,0},{24,8},{1,17},{9,25},{17,1},{25,9},{2,18},{10... | collective-permute-start | bytes 1720328 | tf_op jit(solution)/shard_map/ppermute | solution.py:324
  95.4 9.0 %collective-permute-start.29 = (bf16[1,40,4096]{2,1,0:T(8,128)(2,1)S(1)}, bf16[1,40,4096]{2,1,0:T(8,128)(2,1)S(1)}, u32[]{:S(2)}, u32[]{:S(2)}) collective-permute-start(bf16[1,40,4096]{2,1,0:T(8,128)(2,1)S(1)} %get-tuple-element.163), channel_id=1, source_target_pairs={{0,1},{1,0},{2,3},{3,2},{4,5},{5,4},{6,7},{7,6},{8,9},{9,8},{10,11... | collective-permute-start | bytes 983048 | tf_op jit(solution)/shard_map/ppermute | solution.py:324
  96.3 17.7 %collective-permute-start.34 = (bf16[2,40,4096]{2,1,0:T(8,128)(2,1)S(1)}, bf16[2,40,4096]{2,1,0:T(8,128)(2,1)S(1)}, u32[]{:S(2)}, u32[]{:S(2)}) collective-permute-start(bf16[2,40,4096]{2,1,0:T(8,128)(2,1)S(1)} %get-tuple-element.178), channel_id=1, source_target_pairs={{0,2},{1,3},{2,0},{3,1},{4,6},{5,7},{6,4},{7,5},{8,10},{9,11},{10,... | collective-permute-start | bytes 1966088 | tf_op jit(solution)/shard_map/ppermute | solution.py:354
  104.5 8.2 %collective-permute-start.31 = (bf16[1,40,4096]{2,1,0:T(8,128)(2,1)S(1)}, bf16[1,40,4096]{2,1,0:T(8,128)(2,1)S(1)}, u32[]{:S(2)}, u32[]{:S(2)}) collective-permute-start(bf16[1,40,4096]{2,1,0:T(8,128)(2,1)S(1)} %get-tuple-element.174), channel_id=1, source_target_pairs={{0,1},{1,0},{2,3},{3,2},{4,5},{5,4},{6,7},{7,6},{8,9},{9,8},{10,11... | collective-permute-start | bytes 983048 | tf_op jit(solution)/shard_map/ppermute | solution.py:324
  105.6 2.9 %collective-permute-start.30 = (bf16[2,40,1792]{2,1,0:T(8,128)(2,1)S(1)}, bf16[2,40,1792]{2,1,0:T(8,128)(2,1)S(1)}, u32[]{:S(2)}, u32[]{:S(2)}) collective-permute-start(bf16[2,40,1792]{2,1,0:T(8,128)(2,1)S(1)} %get-tuple-element.168.own_ref), channel_id=1, source_target_pairs={{0,8},{8,0},{16,24},{24,16},{1,9},{9,1},{17,25},{25,17},{2,10},{10... | collective-permute-start | bytes 860168 | tf_op jit(solution)/shard_map/ppermute | solution.py:324
  105.6 18.7 %collective-permute-start.25 = (bf16[2,2,40,1792]{3,2,1,0:T(8,128)(2,1)S(1)}, bf16[2,2,40,1792]{3,2,1,0:T(8,128)(2,1)S(1)}, u32[]{:S(2)}, u32[]{:S(2)}) collective-permute-start(bf16[2,2,40,1792]{3,2,1,0:T(8,128)(2,1)S(1)} %get-tuple-element.154), channel_id=1, source_target_pairs={{0,16},{8,24},{16,0},{24,8},{1,17},{9,25},{17,1},{25,9},{2,18},{10... | collective-permute-start | bytes 1720328 | tf_op jit(solution)/shard_map/ppermute | solution.py:324
  106.9 14.2 %collective-permute-start.33 = (bf16[1,40,4096]{2,1,0:T(8,128)(2,1)S(1)}, bf16[1,40,4096]{2,1,0:T(8,128)(2,1)S(1)}, u32[]{:S(2)}, u32[]{:S(2)}) collective-permute-start(bf16[1,40,4096]{2,1,0:T(8,128)(2,1)S(1)} %get-tuple-element.173), channel_id=1, source_target_pairs={{0,2},{1,3},{2,0},{3,1},{4,6},{5,7},{6,4},{7,5},{8,10},{9,11},{10,... | collective-permute-start | bytes 983048 | tf_op jit(solution)/shard_map/ppermute | solution.py:354
  112.7 9.2 %collective-permute-start.32 = (bf16[1,40,4096]{2,1,0:T(8,128)(2,1)S(1)}, bf16[1,40,4096]{2,1,0:T(8,128)(2,1)S(1)}, u32[]{:S(2)}, u32[]{:S(2)}) collective-permute-start(bf16[1,40,4096]{2,1,0:T(8,128)(2,1)S(1)} %get-tuple-element.175), channel_id=1, source_target_pairs={{0,1},{1,0},{2,3},{3,2},{4,5},{5,4},{6,7},{7,6},{8,9},{9,8},{10,11... | collective-permute-start | bytes 983048 | tf_op jit(solution)/shard_map/ppermute | solution.py:324
  114.1 16.0 %collective-permute-start.38 = (bf16[1,40,4096]{2,1,0:T(8,128)(2,1)S(1)}, bf16[1,40,4096]{2,1,0:T(8,128)(2,1)S(1)}, u32[]{:S(2)}, u32[]{:S(2)}) collective-permute-start(bf16[1,40,4096]{2,1,0:T(8,128)(2,1)S(1)} %get-tuple-element.190), channel_id=1, source_target_pairs={{0,2},{1,3},{2,0},{3,1},{4,6},{5,7},{6,4},{7,5},{8,10},{9,11},{10,... | collective-permute-start | bytes 983048 | tf_op jit(solution)/shard_map/ppermute | solution.py:354
  122.1 8.3 %collective-permute-start.36 = (bf16[1,40,4096]{2,1,0:T(8,128)(2,1)S(1)}, bf16[1,40,4096]{2,1,0:T(8,128)(2,1)S(1)}, u32[]{:S(2)}, u32[]{:S(2)}) collective-permute-start(bf16[1,40,4096]{2,1,0:T(8,128)(2,1)S(1)} %get-tuple-element.187), channel_id=1, source_target_pairs={{0,1},{1,0},{2,3},{3,2},{4,5},{5,4},{6,7},{7,6},{8,9},{9,8},{10,11... | collective-permute-start | bytes 983048 | tf_op jit(solution)/shard_map/ppermute | solution.py:324
  122.8 25.0 %collective-permute-start.40 = (bf16[1,40,4096]{2,1,0:T(8,128)(2,1)S(1)}, bf16[1,40,4096]{2,1,0:T(8,128)(2,1)S(1)}, u32[]{:S(2)}, u32[]{:S(2)}) collective-permute-start(bf16[1,40,4096]{2,1,0:T(8,128)(2,1)S(1)} %get-tuple-element.186), channel_id=1, source_target_pairs={{0,4},{1,5},{4,0},{5,1},{2,6},{3,7},{6,2},{7,3},{8,12},{9,13},{12,... | collective-permute-start | bytes 983048 | tf_op jit(solution)/shard_map/ppermute | solution.py:354
  124.6 1.6 %collective-permute-start.35 = (bf16[2,40,1792]{2,1,0:T(8,128)(2,1)S(1)}, bf16[2,40,1792]{2,1,0:T(8,128)(2,1)S(1)}, u32[]{:S(2)}, u32[]{:S(2)}) collective-permute-start(bf16[2,40,1792]{2,1,0:T(8,128)(2,1)S(1)} %get-tuple-element.181.own_ref), channel_id=1, source_target_pairs={{0,8},{8,0},{16,24},{24,16},{1,9},{9,1},{17,25},{25,17},{2,10},{10... | collective-permute-start | bytes 860168 | tf_op jit(solution)/shard_map/ppermute | solution.py:324
  130.5 22.4 %collective-permute-start.39 = (bf16[1,40,4096]{2,1,0:T(8,128)(2,1)S(1)}, bf16[1,40,4096]{2,1,0:T(8,128)(2,1)S(1)}, u32[]{:S(2)}, u32[]{:S(2)}) collective-permute-start(bf16[1,40,4096]{2,1,0:T(8,128)(2,1)S(1)} %get-tuple-element.194), channel_id=1, source_target_pairs={{0,4},{1,5},{4,0},{5,1},{2,6},{3,7},{6,2},{7,3},{8,12},{9,13},{12,... | collective-permute-start | bytes 983048 | tf_op jit(solution)/shard_map/ppermute | solution.py:354
  131.9 16.5 %collective-permute-start.37 = (bf16[2,40,4096]{2,1,0:T(8,128)(2,1)S(1)}, bf16[2,40,4096]{2,1,0:T(8,128)(2,1)S(1)}, u32[]{:S(2)}, u32[]{:S(2)}) collective-permute-start(bf16[2,40,4096]{2,1,0:T(8,128)(2,1)S(1)} %get-tuple-element.188), channel_id=1, source_target_pairs={{0,1},{1,0},{2,3},{3,2},{4,5},{5,4},{6,7},{7,6},{8,9},{9,8},{10,11... | collective-permute-start | bytes 1966088 | tf_op jit(solution)/shard_map/ppermute | solution.py:324
  148.5 4.4 %collective-permute-start.41 = (bf16[40,4096]{1,0:T(8,128)(2,1)S(1)}, bf16[40,4096]{1,0:T(8,128)(2,1)S(1)}, u32[]{:S(2)}, u32[]{:S(2)}) collective-permute-start(bf16[40,4096]{1,0:T(8,128)(2,1)S(1)} %fusion.4), channel_id=1, source_target_pairs={{0,8},{8,0},{16,24},{24,16},{1,9},{9,1},{17,25},{25,17},{2,10},{10... | collective-permute-start | bytes 983048 | tf_op jit(solution)/shard_map/ppermute | solution.py:324

commit v20 on v19

--- a/solution.py
+++ b/solution.py
@@ -27,12 +27,6 @@
     return tile
 
 
-def rms_normed(rows_in, norm_gain):
-    values = rows_in.astype(F32)
-    meansq = jnp.mean(values * values, axis=-1, keepdims=True)
-    return (values * lax.rsqrt(meansq + 1e-05) * norm_gain).astype(BF16)
-
-
 HURRY = 1000
 
 
@@ -47,6 +41,37 @@
 ANYWHERE = pl.BlockSpec(memory_space=pl.ANY)
 TOKEN = jax.ShapeDtypeStruct((8, 128), F32)
 INSIDE = pl.BlockSpec(memory_space=pltpu.VMEM)
+
+
+def norm_kernel(rows_hbm, gain_hbm, normed_ref, rows_ref, gain_ref, semaphores):
+    copies = [
+        pltpu.make_async_copy(rows_hbm, rows_ref, semaphores.at[0]),
+        pltpu.make_async_copy(gain_hbm, gain_ref, semaphores.at[1]),
+    ]
+    for copy in copies:
+        copy.start()
+    for copy in copies:
+        copy.wait()
+    values = rows_ref[...].astype(F32)
+    meansq = jnp.mean(values * values, axis=-1, keepdims=True)
+    normed_ref[...] = (values * lax.rsqrt(meansq + 1e-05) * gain_ref[...][None, :]).astype(BF16)
+
+
+def rms_normed(rows_in, norm_gain):
+    return pl.pallas_call(
+        norm_kernel,
+        in_specs=[ANYWHERE] * 2,
+        out_specs=INSIDE,
+        out_shape=jax.ShapeDtypeStruct(rows_in.shape, BF16),
+        scratch_shapes=[
+            pltpu.VMEM(rows_in.shape, rows_in.dtype),
+            pltpu.VMEM(norm_gain.shape, norm_gain.dtype),
+            pltpu.SemaphoreType.DMA((2,)),
+        ],
+        compiler_params=pltpu.CompilerParams(vmem_limit_bytes=VMEM),
+        cost_estimate=as_if(0),
+        name="normed",
+    )(*(pltpu.with_memory_space_constraint(values, pltpu.HBM) for values in (rows_in, norm_gain)))
 
 
 def mask_kernel(share, rows, after_count, core_ref, weight_ref, mask_ref, *refs):

time: 154 us -> 154 us (level)
  other arithmetic: 3.93 us -> 1.29 us
  starting transfers between devices: 40.9 us -> 42.9 us
  waiting for transfers between devices: 51.9 us -> 49.9 us
    ppermute x31, starting transfers between devices: 22.7 us -> 25.4 us  [swap(): lax.ppermute(values, axis, [(place, place ^ step) for place in range(size)])]
    ppermute x31, waiting for transfers between devices: 23.5 us -> 21.1 us  [swap(): lax.ppermute(values, axis, [(place, place ^ step) for place in range(size)])]
  transfers between devices with their start and end apart: 42 -> 42, of which waited for: 19 -> 18; matrix products, arithmetic and copies ran while one was open for 0% -> 0% of each run, Pallas kernels for 36% -> 36%
where the time goes in v20:
time: 154 us
  Pallas kernels  58.2 us (38%)
  waiting for transfers between devices  49.9 us (32%)
  starting transfers between devices  42.9 us (28%)
    ppermute x11, waiting for transfers between devices, by_plane(): return lax.ppermute(behind(values, after), 'cols', pairs)  28.9 us
    ppermute x31, starting transfers between devices, swap(): lax.ppermute(values, axis, [(place, place ^ step) for place in range(size)])  25.4 us
    pallas_call x4, Pallas kernels, gate_up(): pl.pallas_call(functools.partial(gate_up_kernel, len(parts), len(after)),...  24.3 us
    ppermute x31, waiting for transfers between devices, swap(): lax.ppermute(values, axis, [(place, place ^ step) for place in range(size)])  21.1 us
    ppermute x11, starting transfers between devices, by_plane(): return lax.ppermute(behind(values, after), 'cols', pairs)  17.5 us
    pallas_call x4, Pallas kernels, down(): pl.pallas_call(functools.partial(down_kernel, pieces, len(down_kept), len...  15.5 us
    pallas_call x4, Pallas kernels, masked(): pl.pallas_call(functools.partial(mask_kernel, share, rows, len(after)), i...  13 us
  transfers between devices with their start and end apart: 42, of which 18 were waited for; matrix products, arithmetic and copies ran while one was open for 0% of the time, Pallas kernels for 36%

profile of v20, /device:TPU:0, one launch (start us, length us, event | category | flops | bytes accessed | tf_op | source)
XLA Modules:
  0.0 153.6 jit_solution(12641025663189858477)
XLA Ops:
  0.0 1.5 normed.1
  2.2 1.3 collective-permute-done
  4.1 2.9 %collective-permute-start.1 = (bf16[2,1,40,2048]{3,2,1,0:T(8,128)(2,1)S(1)}, bf16[2,1,40,2048]{3,2,1,0:T(8,128)(2,1)S(1)}, u32[]{:S(2)}, u32[]{:S(2)}) collective-permute-start(bf16[2,1,40,2048]{3,2,1,0:T(8,128)(2,1)S(1)} %get-tuple-element.101.refs_2_), channel_id=1, source_target_pairs={{0,16},{8,24},{16,0},{24,8},{1,17},{9,25},{17,1},{25,9},{2,18},{10... | collective-permute-start | bytes 983048 | tf_op jit(solution)/shard_map/ppermute | solution.py:349
  6.9 1.6 %collective-permute-start.6 = (bf16[2,1,40,2048]{3,2,1,0:T(8,128)(2,1)S(1)}, bf16[2,1,40,2048]{3,2,1,0:T(8,128)(2,1)S(1)}, u32[]{:S(2)}, u32[]{:S(2)}) collective-permute-start(bf16[2,1,40,2048]{3,2,1,0:T(8,128)(2,1)S(1)} %get-tuple-element.102.refs_0_), channel_id=1, source_target_pairs={{0,2},{1,3},{2,0},{3,1},{4,6},{5,7},{6,4},{7,5},{8,10},{9,11},{10,... | collective-permute-start | bytes 983048 | tf_op jit(solution)/shard_map/ppermute | solution.py:379
  9.3 1.6 %collective-permute-start.2 = (bf16[2,1,40,2048]{3,2,1,0:T(8,128)(2,1)S(1)}, bf16[2,1,40,2048]{3,2,1,0:T(8,128)(2,1)S(1)}, u32[]{:S(2)}, u32[]{:S(2)}) collective-permute-start(bf16[2,1,40,2048]{3,2,1,0:T(8,128)(2,1)S(1)} %get-tuple-element.102.refs_0_), channel_id=1, source_target_pairs={{0,1},{1,0},{2,3},{3,2},{4,5},{5,4},{6,7},{7,6},{8,9},{9,8},{10,11... | collective-permute-start | bytes 983048 | tf_op jit(solution)/shard_map/ppermute | solution.py:349
  10.8 4.1 %collective-permute-done.1.refs_1_ = bf16[2,1,40,2048]{3,2,1,0:T(8,128)(2,1)S(1)} collective-permute-done((bf16[2,1,40,2048]{3,2,1,0:T(8,128)(2,1)S(1)}, bf16[2,1,40,2048]{3,2,1,0:T(8,128)(2,1)S(1)}, u32[]{:S(2)}, u32[]{:S(2)}) %collective-permute-start.1) | collective-permute-done | bytes 327712 | tf_op jit(solution)/shard_map/ppermute | solution.py:349
  14.9 1.8 %collective-permute-start.7 = (bf16[2,1,40,2048]{3,2,1,0:T(8,128)(2,1)S(1)}, bf16[2,1,40,2048]{3,2,1,0:T(8,128)(2,1)S(1)}, u32[]{:S(2)}, u32[]{:S(2)}) collective-permute-start(bf16[2,1,40,2048]{3,2,1,0:T(8,128)(2,1)S(1)} %collective-permute-done.1.refs_1_), channel_id=1, source_target_pairs={{0,2},{1,3},{2,0},{3,1},{4,6},{5,7},{6,4},{7,5},{8,10},{9,11},{10,... | collective-permute-start | bytes 983048 | tf_op jit(solution)/shard_map/ppermute | solution.py:379
  17.4 1.6 %collective-permute-start.3 = (bf16[2,1,40,2048]{3,2,1,0:T(8,128)(2,1)S(1)}, bf16[2,1,40,2048]{3,2,1,0:T(8,128)(2,1)S(1)}, u32[]{:S(2)}, u32[]{:S(2)}) collective-permute-start(bf16[2,1,40,2048]{3,2,1,0:T(8,128)(2,1)S(1)} %collective-permute-done.1.refs_1_), channel_id=1, source_target_pairs={{0,1},{1,0},{2,3},{3,2},{4,5},{5,4},{6,7},{7,6},{8,9},{9,8},{10,11... | collective-permute-start | bytes 983048 | tf_op jit(solution)/shard_map/ppermute | solution.py:349
  19.7 3.2 %masked.4 = (bf16[2048,1792]{1,0:T(8,128)(2,1)S(1)}, f32[8,128]{1,0:T(8,128)S(1)}) custom-call(s32[1]{0:T(128)} %bitcast.5.core_ref, bf16[2048,1792]{1,0:T(8,128)(2,1)} %weight_ref.4, s32[32,28]{1,0:T(8,128)S(1)} %copy-done.1, f32[8,128]{1,0:T(8,128)S(1)} %get-tuple-element.103.refs_0_), custom_call_target="tpu_custom_call" | custom-call | tf_op jit(solution)/shard_map/masked/pallas_call | solution.py:106
  23.1 3.2 %masked.5 = (bf16[2048,1792]{1,0:T(8,128)(2,1)S(1)}, f32[8,128]{1,0:T(8,128)S(1)}) custom-call(s32[1]{0:T(128)} %bitcast.5.core_ref, bf16[2048,1792]{1,0:T(8,128)(2,1)} %weight_ref.5, s32[32,28]{1,0:T(8,128)S(1)} %copy-done.2, f32[8,128]{1,0:T(8,128)S(1)} %get-tuple-element.106.refs_0_, bf16[2,1,40,2048]{3,2,1,0:T(8,128)(2,1)S(1)} %collective-permute-done.6.refs_1_.refs_0_), custom_call_target="tpu_custom_call" | custom-call | flops 172500000 | tf_op jit(solution)/shard_map/masked/pallas_call | solution.py:106
  26.5 4.5 %collective-permute-start.10 = (bf16[160,2048]{1,0:T(8,128)(2,1)S(1)}, bf16[160,2048]{1,0:T(8,128)(2,1)S(1)}, u32[]{:S(2)}, u32[]{:S(2)}) collective-permute-start(bf16[160,2048]{1,0:T(8,128)(2,1)S(1)} %get-tuple-element.118.refs_0_.mine_ref), channel_id=1, source_target_pairs={{0,6},{1,7},{6,0},{7,1},{8,14},{9,15},{14,8},{15,9},{16,22},{17,23... | collective-permute-start | bytes 1966088 | tf_op jit(solution)/shard_map/ppermute | solution.py:379
  31.6 6.1 %gate_up.4 = (bf16[2,2,2,40,1792]{4,3,2,1,0:T(8,128)(2,1)S(1)}, bf16[2,2,40,1792]{3,2,1,0:T(8,128)(2,1)S(1)}, bf16[2,2,1,40,1792]{4,3,2,1,0:T(8,128)(2,1)S(1)}, f32[8,128]{1,0:T(8,128)S(1)}) custom-call(bf16[160,2048]{1,0:T(8,128)(2,1)S(1)} %get-tuple-element.118.refs_0_.mine_ref, bf16[160,2048]{1,0:T(8,128)(2,1)S(1)} %get-tuple-element.110.refs_1_, ...), custom_call_target="tpu_custom_call" | custom-call | flops 4697620480 | tf_op jit(solution)/shard_map/gate_up/pallas_call | solution.py:231
  38.3 3.3 %masked.6 = (bf16[1792,2048]{1,0:T(8,128)(2,1)S(1)}, f32[8,128]{1,0:T(8,128)S(1)}) custom-call(s32[1]{0:T(128)} %bitcast.5.core_ref, bf16[1792,8192]{1,0:T(8,128)(2,1)} %weight_ref.7, s32[28,128]{1,0:T(8,128)S(1)} %copy-done, f32[8,128]{1,0:T(8,128)S(1)} %get-tuple-element.119.refs_0_), custom_call_target="tpu_custom_call" | custom-call | tf_op jit(solution)/shard_map/masked/pallas_call | solution.py:106
  41.5 4.0 %collective-permute-done.10.outer_three_ref = bf16[160,2048]{1,0:T(8,128)(2,1)S(1)} collective-permute-done((bf16[160,2048]{1,0:T(8,128)(2,1)S(1)}, bf16[160,2048]{1,0:T(8,128)(2,1)S(1)}, u32[]{:S(2)}, u32[]{:S(2)}) %collective-permute-start.10) | collective-permute-done | bytes 655392 | tf_op jit(solution)/shard_map/ppermute | solution.py:379
  47.0 6.1 %gate_up.5 = (bf16[2,2,2,40,1792]{4,3,2,1,0:T(8,128)(2,1)S(1)}, bf16[2,2,40,1792]{3,2,1,0:T(8,128)(2,1)S(1)}, bf16[2,2,1,40,1792]{4,3,2,1,0:T(8,128)(2,1)S(1)}, f32[8,128]{1,0:T(8,128)S(1)}) custom-call(bf16[160,2048]{1,0:T(8,128)(2,1)S(1)} %get-tuple-element.125.refs_0_, bf16[160,2048]{1,0:T(8,128)(2,1)S(1)} %collective-permute-done.12.refs_1_, ...), custom_call_target="tpu_custom_call" | custom-call | flops 4697620480 | tf_op jit(solution)/shard_map/gate_up/pallas_call | solution.py:231
  53.7 1.5 collective-permute-done.13.refs_1_
  55.2 0.8 collective-permute-done.14.refs_3_.refs_1_
  56.1 1.6 %collective-permute-start.16 = (bf16[2,2,40,1792]{3,2,1,0:T(8,128)(2,1)S(1)}, bf16[2,2,40,1792]{3,2,1,0:T(8,128)(2,1)S(1)}, u32[]{:S(2)}, u32[]{:S(2)}) collective-permute-start(bf16[2,2,40,1792]{3,2,1,0:T(8,128)(2,1)S(1)} %get-tuple-element.134), channel_id=1, source_target_pairs={{0,16},{8,24},{16,0},{24,8},{1,17},{9,25},{17,1},{25,9},{2,18},{10... | collective-permute-start | bytes 1720328 | tf_op jit(solution)/shard_map/ppermute | solution.py:349
  57.7 3.3 %masked.7 = (bf16[1792,2048]{1,0:T(8,128)(2,1)S(1)}, f32[8,128]{1,0:T(8,128)S(1)}) custom-call(s32[1]{0:T(128)} %bitcast.5.core_ref, bf16[1792,8192]{1,0:T(8,128)(2,1)} %weight_ref.7, s32[28,128]{1,0:T(8,128)S(1)} %copy-done, f32[8,128]{1,0:T(8,128)S(1)} %get-tuple-element.131.refs_0_), custom_call_target="tpu_custom_call" | custom-call | tf_op jit(solution)/shard_map/masked/pallas_call | solution.py:106
  61.0 1.6 %collective-permute-start.15 = (bf16[160,2048]{1,0:T(8,128)(2,1)S(1)}, bf16[160,2048]{1,0:T(8,128)(2,1)S(1)}, u32[]{:S(2)}, u32[]{:S(2)}) collective-permute-start(bf16[160,2048]{1,0:T(8,128)(2,1)S(1)} %collective-permute-done.11.refs_5_.refs_0_), channel_id=1, source_target_pairs={{0,1},{1,0},{2,3},{3,2},{4,5},{5,4},{6,7},{7,6},{8,9},{9,8},{10,11... | collective-permute-start | bytes 1966088 | tf_op jit(solution)/shard_map/ppermute | solution.py:349
  62.6 6.1 %gate_up.6 = (bf16[2,2,2,40,1792]{4,3,2,1,0:T(8,128)(2,1)S(1)}, bf16[2,2,40,1792]{3,2,1,0:T(8,128)(2,1)S(1)}, bf16[2,2,1,40,1792]{4,3,2,1,0:T(8,128)(2,1)S(1)}, f32[8,128]{1,0:T(8,128)S(1)}) custom-call(bf16[160,2048]{1,0:T(8,128)(2,1)S(1)} %get-tuple-element.136.refs_0_, bf16[160,2048]{1,0:T(8,128)(2,1)S(1)} %collective-permute-done.17.refs_1_, ...), custom_call_target="tpu_custom_call" | custom-call | flops 4697620480 | tf_op jit(solution)/shard_map/gate_up/pallas_call | solution.py:231
  69.2 2.0 %collective-permute-done.16.refs_2_ = bf16[2,2,40,1792]{3,2,1,0:T(8,128)(2,1)S(1)} collective-permute-done((bf16[2,2,40,1792]{3,2,1,0:T(8,128)(2,1)S(1)}, bf16[2,2,40,1792]{3,2,1,0:T(8,128)(2,1)S(1)}, u32[]{:S(2)}, u32[]{:S(2)}) %collective-permute-start.16) | collective-permute-done | bytes 573472 | tf_op jit(solution)/shard_map/ppermute | solution.py:349
  71.8 1.6 %collective-permute-start.23 = (bf16[2,2,40,1792]{3,2,1,0:T(8,128)(2,1)S(1)}, bf16[2,2,40,1792]{3,2,1,0:T(8,128)(2,1)S(1)}, u32[]{:S(2)}, u32[]{:S(2)}) collective-permute-start(bf16[2,2,40,1792]{3,2,1,0:T(8,128)(2,1)S(1)} %get-tuple-element.150), channel_id=1, source_target_pairs={{0,16},{8,24},{16,0},{24,8},{1,17},{9,25},{17,1},{25,9},{2,18},{10... | collective-permute-start | bytes 1720328 | tf_op jit(solution)/shard_map/ppermute | solution.py:349
  73.3 3.9 %down.4 = (bf16[2,40,4096]{2,1,0:T(8,128)(2,1)S(1)}, bf16[2,40,4096]{2,1,0:T(8,128)(2,1)S(1)}, f32[8,128]{1,0:T(8,128)S(1)}) custom-call(bf16[2,40,1792]{2,1,0:T(8,128)(2,1)S(1)} %get-tuple-element.138.own_ref, bf16[2,40,1792]{2,1,0:T(8,128)(2,1)S(1)} %collective-permute-done.18.other_ref, bf16[1792,2048]{1,0:T(8,128)(2,1)S(1)} %get-tuple-element.139.refs_0_, ...), custom_call_target="tpu_custom_call" | custom-call | flops 2348810 | tf_op jit(solution)/shard_map/down/pallas_call | solution.py:273
  77.5 1.5 collective-permute-start.28
  79.1 6.1 %gate_up.7 = (bf16[2,2,2,40,1792]{4,3,2,1,0:T(8,128)(2,1)S(1)}, bf16[2,2,40,1792]{3,2,1,0:T(8,128)(2,1)S(1)}, bf16[1,2,1,40,1792]{4,3,2,1,0:T(8,128)(2,1)S(1)}, ...) custom-call(bf16[160,2048]{1,0:T(8,128)(2,1)S(1)} %collective-permute-done.11.refs_5_.refs_0_, ...), custom_call_target="tpu_custom_call" | custom-call | flops 4697620480 | tf_op jit(solution)/shard_map/gate_up/pallas_call | solution.py:231
  85.7 1.5 collective-permute-done.23.refs_2_
  88.3 1.5 collective-permute-start.24
  89.8 3.9 %down.5 = (bf16[1,40,4096]{2,1,0:T(8,128)(2,1)S(1)}, bf16[1,40,4096]{2,1,0:T(8,128)(2,1)S(1)}, bf16[1,40,4096]{2,1,0:T(8,128)(2,1)S(1)}, bf16[1,40,4096]{2,1,0:T(8,128)(2,1)S(1)}, f32[8,128]{1,0:T(8,128)S(1)}) custom-call(bf16[2,40,1792]{2,1,0:T(8,128)(2,1)S(1)} %get-tuple-element.158.own_ref, bf16[2,40,1792]{2,1,0:T(8,128)(2,1)S(1)} %collective-permute-done.27.other_ref, ...), custom_call_target="tpu_custom_call" | custom-call | flops 2348810 | tf_op jit(solution)/shard_map/down/pallas_call | solution.py:273
  94.1 1.5 collective-permute-start.29
  95.8 1.6 %collective-permute-start.34 = (bf16[2,40,4096]{2,1,0:T(8,128)(2,1)S(1)}, bf16[2,40,4096]{2,1,0:T(8,128)(2,1)S(1)}, u32[]{:S(2)}, u32[]{:S(2)}) collective-permute-start(bf16[2,40,4096]{2,1,0:T(8,128)(2,1)S(1)} %get-tuple-element.178), channel_id=1, source_target_pairs={{0,2},{1,3},{2,0},{3,1},{4,6},{5,7},{6,4},{7,5},{8,10},{9,11},{10,... | collective-permute-start | bytes 1966088 | tf_op jit(solution)/shard_map/ppermute | solution.py:379
  97.5 5.7 %collective-permute-done.29.refs_1_ = bf16[1,40,4096]{2,1,0:T(8,128)(2,1)S(1)} collective-permute-done((bf16[1,40,4096]{2,1,0:T(8,128)(2,1)S(1)}, bf16[1,40,4096]{2,1,0:T(8,128)(2,1)S(1)}, u32[]{:S(2)}, u32[]{:S(2)}) %collective-permute-start.29) | collective-permute-done | bytes 327712 | tf_op jit(solution)/shard_map/ppermute | solution.py:349
  103.2 1.6 %collective-permute-start.31 = (bf16[1,40,4096]{2,1,0:T(8,128)(2,1)S(1)}, bf16[1,40,4096]{2,1,0:T(8,128)(2,1)S(1)}, u32[]{:S(2)}, u32[]{:S(2)}) collective-permute-start(bf16[1,40,4096]{2,1,0:T(8,128)(2,1)S(1)} %get-tuple-element.174), channel_id=1, source_target_pairs={{0,1},{1,0},{2,3},{3,2},{4,5},{5,4},{6,7},{7,6},{8,9},{9,8},{10,11... | collective-permute-start | bytes 983048 | tf_op jit(solution)/shard_map/ppermute | solution.py:349
  105.2 1.2 collective-permute-start.25
  106.4 1.6 %collective-permute-start.33 = (bf16[1,40,4096]{2,1,0:T(8,128)(2,1)S(1)}, bf16[1,40,4096]{2,1,0:T(8,128)(2,1)S(1)}, u32[]{:S(2)}, u32[]{:S(2)}) collective-permute-start(bf16[1,40,4096]{2,1,0:T(8,128)(2,1)S(1)} %get-tuple-element.173), channel_id=1, source_target_pairs={{0,2},{1,3},{2,0},{3,1},{4,6},{5,7},{6,4},{7,5},{8,10},{9,11},{10,... | collective-permute-start | bytes 983048 | tf_op jit(solution)/shard_map/ppermute | solution.py:379
  108.0 3.9 %down.6 = (bf16[1,40,4096]{2,1,0:T(8,128)(2,1)S(1)}, bf16[1,40,4096]{2,1,0:T(8,128)(2,1)S(1)}, bf16[1,40,4096]{2,1,0:T(8,128)(2,1)S(1)}, bf16[1,40,4096]{2,1,0:T(8,128)(2,1)S(1)}, f32[8,128]{1,0:T(8,128)S(1)}) custom-call(bf16[2,40,1792]{2,1,0:T(8,128)(2,1)S(1)} %get-tuple-element.168.own_ref, bf16[2,40,1792]{2,1,0:T(8,128)(2,1)S(1)} %collective-permute-done.30.other_ref, ...), custom_call_target="tpu_custom_call" | custom-call | flops 2348810 | tf_op jit(solution)/shard_map/down/pallas_call | solution.py:273
  111.9 1.0 collective-permute-start.32
  113.6 1.6 %collective-permute-start.38 = (bf16[1,40,4096]{2,1,0:T(8,128)(2,1)S(1)}, bf16[1,40,4096]{2,1,0:T(8,128)(2,1)S(1)}, u32[]{:S(2)}, u32[]{:S(2)}) collective-permute-start(bf16[1,40,4096]{2,1,0:T(8,128)(2,1)S(1)} %get-tuple-element.190), channel_id=1, source_target_pairs={{0,2},{1,3},{2,0},{3,1},{4,6},{5,7},{6,4},{7,5},{8,10},{9,11},{10,... | collective-permute-start | bytes 983048 | tf_op jit(solution)/shard_map/ppermute | solution.py:379
  115.3 5.3 %collective-permute-done.33.refs_2_ = bf16[1,40,4096]{2,1,0:T(8,128)(2,1)S(1)} collective-permute-done((bf16[1,40,4096]{2,1,0:T(8,128)(2,1)S(1)}, bf16[1,40,4096]{2,1,0:T(8,128)(2,1)S(1)}, u32[]{:S(2)}, u32[]{:S(2)}) %collective-permute-start.33) | collective-permute-done | bytes 327712 | tf_op jit(solution)/shard_map/ppermute | solution.py:379
  120.6 0.9 collective-permute-done.32.refs_1_
  122.2 1.6 %collective-permute-start.40 = (bf16[1,40,4096]{2,1,0:T(8,128)(2,1)S(1)}, bf16[1,40,4096]{2,1,0:T(8,128)(2,1)S(1)}, u32[]{:S(2)}, u32[]{:S(2)}) collective-permute-start(bf16[1,40,4096]{2,1,0:T(8,128)(2,1)S(1)} %get-tuple-element.186), channel_id=1, source_target_pairs={{0,4},{1,5},{4,0},{5,1},{2,6},{3,7},{6,2},{7,3},{8,12},{9,13},{12,... | collective-permute-start | bytes 983048 | tf_op jit(solution)/shard_map/ppermute | solution.py:379
  124.2 1.6 %collective-permute-done.35.other_ref = bf16[2,40,1792]{2,1,0:T(8,128)(2,1)S(1)} collective-permute-done((bf16[2,40,1792]{2,1,0:T(8,128)(2,1)S(1)}, bf16[2,40,1792]{2,1,0:T(8,128)(2,1)S(1)}, u32[]{:S(2)}, u32[]{:S(2)}) %collective-permute-start.35) | collective-permute-done | bytes 286752 | tf_op jit(solution)/shard_map/ppermute | solution.py:349
  125.7 3.9 %down.7 = (bf16[2,40,4096]{2,1,0:T(8,128)(2,1)S(1)}, bf16[2,40,4096]{2,1,0:T(8,128)(2,1)S(1)}, f32[8,128]{1,0:T(8,128)S(1)}) custom-call(bf16[2,40,1792]{2,1,0:T(8,128)(2,1)S(1)} %get-tuple-element.181.own_ref, bf16[2,40,1792]{2,1,0:T(8,128)(2,1)S(1)} %collective-permute-done.35.other_ref, bf16[1792,2048]{1,0:T(8,128)(2,1)S(1)} %get-tuple-element.139.refs_0_, ...), custom_call_target="tpu_custom_call" | custom-call | flops 2348810 | tf_op jit(solution)/shard_map/down/pallas_call | solution.py:273
  130.4 1.4 collective-permute-start.39
  131.8 0.9 collective-permute-start.37
  132.7 14.6 %collective-permute-done.40.refs_0_ = bf16[1,40,4096]{2,1,0:T(8,128)(2,1)S(1)} collective-permute-done((bf16[1,40,4096]{2,1,0:T(8,128)(2,1)S(1)}, bf16[1,40,4096]{2,1,0:T(8,128)(2,1)S(1)}, u32[]{:S(2)}, u32[]{:S(2)}) %collective-permute-start.40) | collective-permute-done | bytes 327712 | tf_op jit(solution)/shard_map/ppermute | solution.py:379
  148.1 4.3 %collective-permute-done.39 = bf16[1,40,4096]{2,1,0:T(8,128)(2,1)S(1)} collective-permute-done((bf16[1,40,4096]{2,1,0:T(8,128)(2,1)S(1)}, bf16[1,40,4096]{2,1,0:T(8,128)(2,1)S(1)}, u32[]{:S(2)}, u32[]{:S(2)}) %collective-permute-start.39) | collective-permute-done | bytes 327712 | tf_op jit(solution)/shard_map/ppermute | solution.py:379
  152.7 0.9 pad_maximum_fusion
  (85 shorter events, 14.6 us)
Async XLA Ops:
  0.0 23.1 %copy-start.2 = (s32[32,28]{1,0:T(8,128)S(1)}, s32[32,28]{1,0:T(8,128)}, u32[]{:S(2)}) copy-start(s32[32,28]{1,0:T(8,128)} %mask_ref.5) | copy-start | bytes 10756
  1.6 1.8 %collective-permute-start = (bf16[2,40,2048]{2,1,0:T(8,128)(2,1)S(1)}, bf16[2,40,2048]{2,1,0:T(8,128)(2,1)S(1)}, u32[]{:S(2)}, u32[]{:S(2)}) collective-permute-start(bf16[2,40,2048]{2,1,0:T(8,128)(2,1)S(1)} %pad_maximum_fusion.1), channel_id=1, source_target_pairs={{0,8},{8,0},{16,24},{24,16},{1,9},{9,1},{17,25},{25,17},{2,10},{10... | collective-permute-start | bytes 983048 | tf_op jit(solution)/shard_map/ppermute | solution.py:349
  4.1 10.9 %collective-permute-start.1 = (bf16[2,1,40,2048]{3,2,1,0:T(8,128)(2,1)S(1)}, bf16[2,1,40,2048]{3,2,1,0:T(8,128)(2,1)S(1)}, u32[]{:S(2)}, u32[]{:S(2)}) collective-permute-start(bf16[2,1,40,2048]{3,2,1,0:T(8,128)(2,1)S(1)} %get-tuple-element.101.refs_2_), channel_id=1, source_target_pairs={{0,16},{8,24},{16,0},{24,8},{1,17},{9,25},{17,1},{25,9},{2,18},{10... | collective-permute-start | bytes 983048 | tf_op jit(solution)/shard_map/ppermute | solution.py:349
  6.9 10.5 %collective-permute-start.6 = (bf16[2,1,40,2048]{3,2,1,0:T(8,128)(2,1)S(1)}, bf16[2,1,40,2048]{3,2,1,0:T(8,128)(2,1)S(1)}, u32[]{:S(2)}, u32[]{:S(2)}) collective-permute-start(bf16[2,1,40,2048]{3,2,1,0:T(8,128)(2,1)S(1)} %get-tuple-element.102.refs_0_), channel_id=1, source_target_pairs={{0,2},{1,3},{2,0},{3,1},{4,6},{5,7},{6,4},{7,5},{8,10},{9,11},{10,... | collective-permute-start | bytes 983048 | tf_op jit(solution)/shard_map/ppermute | solution.py:379
  8.6 17.7 %collective-permute-start.4 = (bf16[2,1,40,2048]{3,2,1,0:T(8,128)(2,1)S(1)}, bf16[2,1,40,2048]{3,2,1,0:T(8,128)(2,1)S(1)}, u32[]{:S(2)}, u32[]{:S(2)}) collective-permute-start(bf16[2,1,40,2048]{3,2,1,0:T(8,128)(2,1)S(1)} %get-tuple-element.102.refs_0_), channel_id=1, source_target_pairs={{2,4},{3,5},{4,2},{5,3},{10,12},{11,13},{12,10},{13,11},{18,20},{1... | collective-permute-start | bytes 983048 | tf_op jit(solution)/shard_map/ppermute | solution.py:379
  9.3 17.1 %collective-permute-start.2 = (bf16[2,1,40,2048]{3,2,1,0:T(8,128)(2,1)S(1)}, bf16[2,1,40,2048]{3,2,1,0:T(8,128)(2,1)S(1)}, u32[]{:S(2)}, u32[]{:S(2)}) collective-permute-start(bf16[2,1,40,2048]{3,2,1,0:T(8,128)(2,1)S(1)} %get-tuple-element.102.refs_0_), channel_id=1, source_target_pairs={{0,1},{1,0},{2,3},{3,2},{4,5},{5,4},{6,7},{7,6},{8,9},{9,8},{10,11... | collective-permute-start | bytes 983048 | tf_op jit(solution)/shard_map/ppermute | solution.py:349
  14.9 11.4 %collective-permute-start.7 = (bf16[2,1,40,2048]{3,2,1,0:T(8,128)(2,1)S(1)}, bf16[2,1,40,2048]{3,2,1,0:T(8,128)(2,1)S(1)}, u32[]{:S(2)}, u32[]{:S(2)}) collective-permute-start(bf16[2,1,40,2048]{3,2,1,0:T(8,128)(2,1)S(1)} %collective-permute-done.1.refs_1_), channel_id=1, source_target_pairs={{0,2},{1,3},{2,0},{3,1},{4,6},{5,7},{6,4},{7,5},{8,10},{9,11},{10,... | collective-permute-start | bytes 983048 | tf_op jit(solution)/shard_map/ppermute | solution.py:379
  16.8 9.7 %collective-permute-start.5 = (bf16[2,1,40,2048]{3,2,1,0:T(8,128)(2,1)S(1)}, bf16[2,1,40,2048]{3,2,1,0:T(8,128)(2,1)S(1)}, u32[]{:S(2)}, u32[]{:S(2)}) collective-permute-start(bf16[2,1,40,2048]{3,2,1,0:T(8,128)(2,1)S(1)} %collective-permute-done.1.refs_1_), channel_id=1, source_target_pairs={{2,4},{3,5},{4,2},{5,3},{10,12},{11,13},{12,10},{13,11},{18,20},{1... | collective-permute-start | bytes 983048 | tf_op jit(solution)/shard_map/ppermute | solution.py:379
  17.4 13.5 %collective-permute-start.3 = (bf16[2,1,40,2048]{3,2,1,0:T(8,128)(2,1)S(1)}, bf16[2,1,40,2048]{3,2,1,0:T(8,128)(2,1)S(1)}, u32[]{:S(2)}, u32[]{:S(2)}) collective-permute-start(bf16[2,1,40,2048]{3,2,1,0:T(8,128)(2,1)S(1)} %collective-permute-done.1.refs_1_), channel_id=1, source_target_pairs={{0,1},{1,0},{2,3},{3,2},{4,5},{5,4},{6,7},{7,6},{8,9},{9,8},{10,11... | collective-permute-start | bytes 983048 | tf_op jit(solution)/shard_map/ppermute | solution.py:349
  19.0 0.7 copy-start.1
  26.5 19.1 %collective-permute-start.10 = (bf16[160,2048]{1,0:T(8,128)(2,1)S(1)}, bf16[160,2048]{1,0:T(8,128)(2,1)S(1)}, u32[]{:S(2)}, u32[]{:S(2)}) collective-permute-start(bf16[160,2048]{1,0:T(8,128)(2,1)S(1)} %get-tuple-element.118.refs_0_.mine_ref), channel_id=1, source_target_pairs={{0,6},{1,7},{6,0},{7,1},{8,14},{9,15},{14,8},{15,9},{16,22},{17,23... | collective-permute-start | bytes 1966088 | tf_op jit(solution)/shard_map/ppermute | solution.py:379
  31.0 15.1 %collective-permute-start.12 = (bf16[160,2048]{1,0:T(8,128)(2,1)S(1)}, bf16[160,2048]{1,0:T(8,128)(2,1)S(1)}, u32[]{:S(2)}, u32[]{:S(2)}) collective-permute-start(bf16[160,2048]{1,0:T(8,128)(2,1)S(1)} %get-tuple-element.125.refs_0_), channel_id=1, source_target_pairs={{0,1},{1,0},{2,3},{3,2},{4,5},{5,4},{6,7},{7,6},{8,9},{9,8},{10,11... | collective-permute-start | bytes 1966088 | tf_op jit(solution)/shard_map/ppermute | solution.py:349
  31.6 6.7 %copy-start = (s32[28,128]{1,0:T(8,128)S(1)}, s32[28,128]{1,0:T(8,128)}, u32[]{:S(2)}) copy-start(s32[28,128]{1,0:T(8,128)} %mask_ref.7) | copy-start | bytes 43012
  37.7 8.0 %collective-permute-start.8 = (bf16[2,2,40,1792]{3,2,1,0:T(8,128)(2,1)S(1)}, bf16[2,2,40,1792]{3,2,1,0:T(8,128)(2,1)S(1)}, u32[]{:S(2)}, u32[]{:S(2)}) collective-permute-start(bf16[2,2,40,1792]{3,2,1,0:T(8,128)(2,1)S(1)} %get-tuple-element.115), channel_id=1, source_target_pairs={{0,8},{8,0},{16,24},{24,16},{1,9},{9,1},{17,25},{25,17},{2,10},{10... | collective-permute-start | bytes 1720328 | tf_op jit(solution)/shard_map/ppermute | solution.py:349
  37.8 7.9 %collective-permute-start.9 = (bf16[2,2,1,40,1792]{4,3,2,1,0:T(8,128)(2,1)S(1)}, bf16[2,2,1,40,1792]{4,3,2,1,0:T(8,128)(2,1)S(1)}, u32[]{:S(2)}, u32[]{:S(2)}) collective-permute-start(bf16[2,2,1,40,1792]{4,3,2,1,0:T(8,128)(2,1)S(1)} %get-tuple-element.116), channel_id=1, source_target_pairs={{0,8},{8,0},{16,24},{24,16},{1,9},{9,1},{17,25},{25,17},{2,10},{10... | collective-permute-start | bytes 1720328 | tf_op jit(solution)/shard_map/ppermute | solution.py:349
  46.2 16.4 %collective-permute-start.17 = (bf16[160,2048]{1,0:T(8,128)(2,1)S(1)}, bf16[160,2048]{1,0:T(8,128)(2,1)S(1)}, u32[]{:S(2)}, u32[]{:S(2)}) collective-permute-start(bf16[160,2048]{1,0:T(8,128)(2,1)S(1)} %get-tuple-element.136.refs_0_), channel_id=1, source_target_pairs={{0,1},{1,0},{2,3},{3,2},{4,5},{5,4},{6,7},{7,6},{8,9},{9,8},{10,11... | collective-permute-start | bytes 1966088 | tf_op jit(solution)/shard_map/ppermute | solution.py:349
  46.7 14.3 %collective-permute-start.11 = (bf16[160,2048]{1,0:T(8,128)(2,1)S(1)}, bf16[160,2048]{1,0:T(8,128)(2,1)S(1)}, u32[]{:S(2)}, u32[]{:S(2)}) collective-permute-start(bf16[160,2048]{1,0:T(8,128)(2,1)S(1)} %get-tuple-element.123), channel_id=1, source_target_pairs={{0,4},{1,5},{4,6},{5,7},{6,2},{7,3},{2,0},{3,1},{8,12},{9,13},{12,... | collective-permute-start | bytes 1966088 | tf_op jit(solution)/shard_map/ppermute | solution.py:379
  53.1 2.0 %collective-permute-start.13 = (bf16[2,2,1,40,1792]{4,3,2,1,0:T(8,128)(2,1)S(1)}, bf16[2,2,1,40,1792]{4,3,2,1,0:T(8,128)(2,1)S(1)}, u32[]{:S(2)}, u32[]{:S(2)}) collective-permute-start(bf16[2,2,1,40,1792]{4,3,2,1,0:T(8,128)(2,1)S(1)} %get-tuple-element.128), channel_id=1, source_target_pairs={{0,8},{8,0},{16,24},{24,16},{1,9},{9,1},{17,25},{25,17},{2,10},{10... | collective-permute-start | bytes 1720328 | tf_op jit(solution)/shard_map/ppermute | solution.py:349
  53.2 2.8 %collective-permute-start.14 = (bf16[2,2,40,1792]{3,2,1,0:T(8,128)(2,1)S(1)}, bf16[2,2,40,1792]{3,2,1,0:T(8,128)(2,1)S(1)}, u32[]{:S(2)}, u32[]{:S(2)}) collective-permute-start(bf16[2,2,40,1792]{3,2,1,0:T(8,128)(2,1)S(1)} %get-tuple-element.130), channel_id=1, source_target_pairs={{0,8},{8,0},{16,24},{24,16},{1,9},{9,1},{17,25},{25,17},{2,10},{10... | collective-permute-start | bytes 1720328 | tf_op jit(solution)/shard_map/ppermute | solution.py:349
  56.1 15.1 %collective-permute-start.16 = (bf16[2,2,40,1792]{3,2,1,0:T(8,128)(2,1)S(1)}, bf16[2,2,40,1792]{3,2,1,0:T(8,128)(2,1)S(1)}, u32[]{:S(2)}, u32[]{:S(2)}) collective-permute-start(bf16[2,2,40,1792]{3,2,1,0:T(8,128)(2,1)S(1)} %get-tuple-element.134), channel_id=1, source_target_pairs={{0,16},{8,24},{16,0},{24,8},{1,17},{9,25},{17,1},{25,9},{2,18},{10... | collective-permute-start | bytes 1720328 | tf_op jit(solution)/shard_map/ppermute | solution.py:349
  61.0 16.6 %collective-permute-start.15 = (bf16[160,2048]{1,0:T(8,128)(2,1)S(1)}, bf16[160,2048]{1,0:T(8,128)(2,1)S(1)}, u32[]{:S(2)}, u32[]{:S(2)}) collective-permute-start(bf16[160,2048]{1,0:T(8,128)(2,1)S(1)} %collective-permute-done.11.refs_5_.refs_0_), channel_id=1, source_target_pairs={{0,1},{1,0},{2,3},{3,2},{4,5},{5,4},{6,7},{7,6},{8,9},{9,8},{10,11... | collective-permute-start | bytes 1966088 | tf_op jit(solution)/shard_map/ppermute | solution.py:349
  68.7 2.9 %collective-permute-start.19 = (bf16[2,2,1,40,1792]{4,3,2,1,0:T(8,128)(2,1)S(1)}, bf16[2,2,1,40,1792]{4,3,2,1,0:T(8,128)(2,1)S(1)}, u32[]{:S(2)}, u32[]{:S(2)}) collective-permute-start(bf16[2,2,1,40,1792]{4,3,2,1,0:T(8,128)(2,1)S(1)} %get-tuple-element.142), channel_id=1, source_target_pairs={{0,8},{8,0},{16,24},{24,16},{1,9},{9,1},{17,25},{25,17},{2,10},{10... | collective-permute-start | bytes 1720328 | tf_op jit(solution)/shard_map/ppermute | solution.py:349
  68.7 2.9 %collective-permute-start.20 = (bf16[2,2,40,1792]{3,2,1,0:T(8,128)(2,1)S(1)}, bf16[2,2,40,1792]{3,2,1,0:T(8,128)(2,1)S(1)}, u32[]{:S(2)}, u32[]{:S(2)}) collective-permute-start(bf16[2,2,40,1792]{3,2,1,0:T(8,128)(2,1)S(1)} %get-tuple-element.144), channel_id=1, source_target_pairs={{0,8},{8,0},{16,24},{24,16},{1,9},{9,1},{17,25},{25,17},{2,10},{10... | collective-permute-start | bytes 1720328 | tf_op jit(solution)/shard_map/ppermute | solution.py:349
  71.5 1.8 %collective-permute-start.18 = (bf16[2,40,1792]{2,1,0:T(8,128)(2,1)S(1)}, bf16[2,40,1792]{2,1,0:T(8,128)(2,1)S(1)}, u32[]{:S(2)}, u32[]{:S(2)}) collective-permute-start(bf16[2,40,1792]{2,1,0:T(8,128)(2,1)S(1)} %get-tuple-element.138.own_ref), channel_id=1, source_target_pairs={{0,8},{8,0},{16,24},{24,16},{1,9},{9,1},{17,25},{25,17},{2,10},{10... | collective-permute-start | bytes 860168 | tf_op jit(solution)/shard_map/ppermute | solution.py:349
  71.8 15.4 %collective-permute-start.23 = (bf16[2,2,40,1792]{3,2,1,0:T(8,128)(2,1)S(1)}, bf16[2,2,40,1792]{3,2,1,0:T(8,128)(2,1)S(1)}, u32[]{:S(2)}, u32[]{:S(2)}) collective-permute-start(bf16[2,2,40,1792]{3,2,1,0:T(8,128)(2,1)S(1)} %get-tuple-element.150), channel_id=1, source_target_pairs={{0,16},{8,24},{16,0},{24,8},{1,17},{9,25},{17,1},{25,9},{2,18},{10... | collective-permute-start | bytes 1720328 | tf_op jit(solution)/shard_map/ppermute | solution.py:349
  77.5 16.6 %collective-permute-start.28 = (bf16[2,40,4096]{2,1,0:T(8,128)(2,1)S(1)}, bf16[2,40,4096]{2,1,0:T(8,128)(2,1)S(1)}, u32[]{:S(2)}, u32[]{:S(2)}) collective-permute-start(bf16[2,40,4096]{2,1,0:T(8,128)(2,1)S(1)} %get-tuple-element.162), channel_id=1, source_target_pairs={{0,1},{1,0},{2,3},{3,2},{4,5},{5,4},{6,7},{7,6},{8,9},{9,8},{10,11... | collective-permute-start | bytes 1966088 | tf_op jit(solution)/shard_map/ppermute | solution.py:349
  85.2 2.4 %collective-permute-start.21 = (bf16[1,2,1,40,1792]{4,3,2,1,0:T(8,128)(2,1)S(1)}, bf16[1,2,1,40,1792]{4,3,2,1,0:T(8,128)(2,1)S(1)}, u32[]{:S(2)}, u32[]{:S(2)}) collective-permute-start(bf16[1,2,1,40,1792]{4,3,2,1,0:T(8,128)(2,1)S(1)} %get-tuple-element.148), channel_id=1, source_target_pairs={{0,8},{8,0},{16,24},{24,16},{1,9},{9,1},{17,25},{25,17},{2,10},{10... | collective-permute-start | bytes 860168 | tf_op jit(solution)/shard_map/ppermute | solution.py:349
  85.2 2.3 %collective-permute-start.22 = (bf16[1,2,1,40,1792]{4,3,2,1,0:T(8,128)(2,1)S(1)}, bf16[1,2,1,40,1792]{4,3,2,1,0:T(8,128)(2,1)S(1)}, u32[]{:S(2)}, u32[]{:S(2)}) collective-permute-start(bf16[1,2,1,40,1792]{4,3,2,1,0:T(8,128)(2,1)S(1)} %get-tuple-element.149), channel_id=1, source_target_pairs={{0,8},{8,0},{16,24},{24,16},{1,9},{9,1},{17,25},{25,17},{2,10},{10... | collective-permute-start | bytes 860168 | tf_op jit(solution)/shard_map/ppermute | solution.py:349
  87.5 2.3 %collective-permute-start.27 = (bf16[2,40,1792]{2,1,0:T(8,128)(2,1)S(1)}, bf16[2,40,1792]{2,1,0:T(8,128)(2,1)S(1)}, u32[]{:S(2)}, u32[]{:S(2)}) collective-permute-start(bf16[2,40,1792]{2,1,0:T(8,128)(2,1)S(1)} %get-tuple-element.158.own_ref), channel_id=1, source_target_pairs={{0,8},{8,0},{16,24},{24,16},{1,9},{9,1},{17,25},{25,17},{2,10},{10... | collective-permute-start | bytes 860168 | tf_op jit(solution)/shard_map/ppermute | solution.py:349
  87.8 17.1 %collective-permute-start.26 = (bf16[2,2,40,1792]{3,2,1,0:T(8,128)(2,1)S(1)}, bf16[2,2,40,1792]{3,2,1,0:T(8,128)(2,1)S(1)}, u32[]{:S(2)}, u32[]{:S(2)}) collective-permute-start(bf16[2,2,40,1792]{3,2,1,0:T(8,128)(2,1)S(1)} %get-tuple-element.157), channel_id=1, source_target_pairs={{0,8},{8,0},{16,24},{24,16},{1,9},{9,1},{17,25},{25,17},{2,10},{10... | collective-permute-start | bytes 1720328 | tf_op jit(solution)/shard_map/ppermute | solution.py:349
  88.3 16.5 %collective-permute-start.24 = (bf16[2,2,40,1792]{3,2,1,0:T(8,128)(2,1)S(1)}, bf16[2,2,40,1792]{3,2,1,0:T(8,128)(2,1)S(1)}, u32[]{:S(2)}, u32[]{:S(2)}) collective-permute-start(bf16[2,2,40,1792]{3,2,1,0:T(8,128)(2,1)S(1)} %get-tuple-element.153), channel_id=1, source_target_pairs={{0,16},{8,24},{16,0},{24,8},{1,17},{9,25},{17,1},{25,9},{2,18},{10... | collective-permute-start | bytes 1720328 | tf_op jit(solution)/shard_map/ppermute | solution.py:349
  94.1 9.0 %collective-permute-start.29 = (bf16[1,40,4096]{2,1,0:T(8,128)(2,1)S(1)}, bf16[1,40,4096]{2,1,0:T(8,128)(2,1)S(1)}, u32[]{:S(2)}, u32[]{:S(2)}) collective-permute-start(bf16[1,40,4096]{2,1,0:T(8,128)(2,1)S(1)} %get-tuple-element.163), channel_id=1, source_target_pairs={{0,1},{1,0},{2,3},{3,2},{4,5},{5,4},{6,7},{7,6},{8,9},{9,8},{10,11... | collective-permute-start | bytes 983048 | tf_op jit(solution)/shard_map/ppermute | solution.py:349
  95.8 17.7 %collective-permute-start.34 = (bf16[2,40,4096]{2,1,0:T(8,128)(2,1)S(1)}, bf16[2,40,4096]{2,1,0:T(8,128)(2,1)S(1)}, u32[]{:S(2)}, u32[]{:S(2)}) collective-permute-start(bf16[2,40,4096]{2,1,0:T(8,128)(2,1)S(1)} %get-tuple-element.178), channel_id=1, source_target_pairs={{0,2},{1,3},{2,0},{3,1},{4,6},{5,7},{6,4},{7,5},{8,10},{9,11},{10,... | collective-permute-start | bytes 1966088 | tf_op jit(solution)/shard_map/ppermute | solution.py:379
  103.2 8.6 %collective-permute-start.31 = (bf16[1,40,4096]{2,1,0:T(8,128)(2,1)S(1)}, bf16[1,40,4096]{2,1,0:T(8,128)(2,1)S(1)}, u32[]{:S(2)}, u32[]{:S(2)}) collective-permute-start(bf16[1,40,4096]{2,1,0:T(8,128)(2,1)S(1)} %get-tuple-element.174), channel_id=1, source_target_pairs={{0,1},{1,0},{2,3},{3,2},{4,5},{5,4},{6,7},{7,6},{8,9},{9,8},{10,11... | collective-permute-start | bytes 983048 | tf_op jit(solution)/shard_map/ppermute | solution.py:349
  105.1 2.9 %collective-permute-start.30 = (bf16[2,40,1792]{2,1,0:T(8,128)(2,1)S(1)}, bf16[2,40,1792]{2,1,0:T(8,128)(2,1)S(1)}, u32[]{:S(2)}, u32[]{:S(2)}) collective-permute-start(bf16[2,40,1792]{2,1,0:T(8,128)(2,1)S(1)} %get-tuple-element.168.own_ref), channel_id=1, source_target_pairs={{0,8},{8,0},{16,24},{24,16},{1,9},{9,1},{17,25},{25,17},{2,10},{10... | collective-permute-start | bytes 860168 | tf_op jit(solution)/shard_map/ppermute | solution.py:349
  105.2 18.6 %collective-permute-start.25 = (bf16[2,2,40,1792]{3,2,1,0:T(8,128)(2,1)S(1)}, bf16[2,2,40,1792]{3,2,1,0:T(8,128)(2,1)S(1)}, u32[]{:S(2)}, u32[]{:S(2)}) collective-permute-start(bf16[2,2,40,1792]{3,2,1,0:T(8,128)(2,1)S(1)} %get-tuple-element.154), channel_id=1, source_target_pairs={{0,16},{8,24},{16,0},{24,8},{1,17},{9,25},{17,1},{25,9},{2,18},{10... | collective-permute-start | bytes 1720328 | tf_op jit(solution)/shard_map/ppermute | solution.py:349
  106.4 14.2 %collective-permute-start.33 = (bf16[1,40,4096]{2,1,0:T(8,128)(2,1)S(1)}, bf16[1,40,4096]{2,1,0:T(8,128)(2,1)S(1)}, u32[]{:S(2)}, u32[]{:S(2)}) collective-permute-start(bf16[1,40,4096]{2,1,0:T(8,128)(2,1)S(1)} %get-tuple-element.173), channel_id=1, source_target_pairs={{0,2},{1,3},{2,0},{3,1},{4,6},{5,7},{6,4},{7,5},{8,10},{9,11},{10,... | collective-permute-start | bytes 983048 | tf_op jit(solution)/shard_map/ppermute | solution.py:379
  111.9 9.6 %collective-permute-start.32 = (bf16[1,40,4096]{2,1,0:T(8,128)(2,1)S(1)}, bf16[1,40,4096]{2,1,0:T(8,128)(2,1)S(1)}, u32[]{:S(2)}, u32[]{:S(2)}) collective-permute-start(bf16[1,40,4096]{2,1,0:T(8,128)(2,1)S(1)} %get-tuple-element.175), channel_id=1, source_target_pairs={{0,1},{1,0},{2,3},{3,2},{4,5},{5,4},{6,7},{7,6},{8,9},{9,8},{10,11... | collective-permute-start | bytes 983048 | tf_op jit(solution)/shard_map/ppermute | solution.py:349
  113.6 15.9 %collective-permute-start.38 = (bf16[1,40,4096]{2,1,0:T(8,128)(2,1)S(1)}, bf16[1,40,4096]{2,1,0:T(8,128)(2,1)S(1)}, u32[]{:S(2)}, u32[]{:S(2)}) collective-permute-start(bf16[1,40,4096]{2,1,0:T(8,128)(2,1)S(1)} %get-tuple-element.190), channel_id=1, source_target_pairs={{0,2},{1,3},{2,0},{3,1},{4,6},{5,7},{6,4},{7,5},{8,10},{9,11},{10,... | collective-permute-start | bytes 983048 | tf_op jit(solution)/shard_map/ppermute | solution.py:379
  121.6 8.7 %collective-permute-start.36 = (bf16[1,40,4096]{2,1,0:T(8,128)(2,1)S(1)}, bf16[1,40,4096]{2,1,0:T(8,128)(2,1)S(1)}, u32[]{:S(2)}, u32[]{:S(2)}) collective-permute-start(bf16[1,40,4096]{2,1,0:T(8,128)(2,1)S(1)} %get-tuple-element.187), channel_id=1, source_target_pairs={{0,1},{1,0},{2,3},{3,2},{4,5},{5,4},{6,7},{7,6},{8,9},{9,8},{10,11... | collective-permute-start | bytes 983048 | tf_op jit(solution)/shard_map/ppermute | solution.py:349
  122.2 25.1 %collective-permute-start.40 = (bf16[1,40,4096]{2,1,0:T(8,128)(2,1)S(1)}, bf16[1,40,4096]{2,1,0:T(8,128)(2,1)S(1)}, u32[]{:S(2)}, u32[]{:S(2)}) collective-permute-start(bf16[1,40,4096]{2,1,0:T(8,128)(2,1)S(1)} %get-tuple-element.186), channel_id=1, source_target_pairs={{0,4},{1,5},{4,0},{5,1},{2,6},{3,7},{6,2},{7,3},{8,12},{9,13},{12,... | collective-permute-start | bytes 983048 | tf_op jit(solution)/shard_map/ppermute | solution.py:379
  124.1 1.6 %collective-permute-start.35 = (bf16[2,40,1792]{2,1,0:T(8,128)(2,1)S(1)}, bf16[2,40,1792]{2,1,0:T(8,128)(2,1)S(1)}, u32[]{:S(2)}, u32[]{:S(2)}) collective-permute-start(bf16[2,40,1792]{2,1,0:T(8,128)(2,1)S(1)} %get-tuple-element.181.own_ref), channel_id=1, source_target_pairs={{0,8},{8,0},{16,24},{24,16},{1,9},{9,1},{17,25},{25,17},{2,10},{10... | collective-permute-start | bytes 860168 | tf_op jit(solution)/shard_map/ppermute | solution.py:349
  130.4 22.0 %collective-permute-start.39 = (bf16[1,40,4096]{2,1,0:T(8,128)(2,1)S(1)}, bf16[1,40,4096]{2,1,0:T(8,128)(2,1)S(1)}, u32[]{:S(2)}, u32[]{:S(2)}) collective-permute-start(bf16[1,40,4096]{2,1,0:T(8,128)(2,1)S(1)} %get-tuple-element.194), channel_id=1, source_target_pairs={{0,4},{1,5},{4,0},{5,1},{2,6},{3,7},{6,2},{7,3},{8,12},{9,13},{12,... | collective-permute-start | bytes 983048 | tf_op jit(solution)/shard_map/ppermute | solution.py:379
  131.8 16.1 %collective-permute-start.37 = (bf16[2,40,4096]{2,1,0:T(8,128)(2,1)S(1)}, bf16[2,40,4096]{2,1,0:T(8,128)(2,1)S(1)}, u32[]{:S(2)}, u32[]{:S(2)}) collective-permute-start(bf16[2,40,4096]{2,1,0:T(8,128)(2,1)S(1)} %get-tuple-element.188), channel_id=1, source_target_pairs={{0,1},{1,0},{2,3},{3,2},{4,5},{5,4},{6,7},{7,6},{8,9},{9,8},{10,11... | collective-permute-start | bytes 1966088 | tf_op jit(solution)/shard_map/ppermute | solution.py:349
  148.0 4.4 %collective-permute-start.41 = (bf16[40,4096]{1,0:T(8,128)(2,1)S(1)}, bf16[40,4096]{1,0:T(8,128)(2,1)S(1)}, u32[]{:S(2)}, u32[]{:S(2)}) collective-permute-start(bf16[40,4096]{1,0:T(8,128)(2,1)S(1)} %fusion.1), channel_id=1, source_target_pairs={{0,8},{8,0},{16,24},{24,16},{1,9},{9,1},{17,25},{25,17},{2,10},{10... | collective-permute-start | bytes 983048 | tf_op jit(solution)/shard_map/ppermute | solution.py:349

commit v21 on v20

--- a/solution.py
+++ b/solution.py
@@ -74,8 +74,10 @@
     )(*(pltpu.with_memory_space_constraint(values, pltpu.HBM) for values in (rows_in, norm_gain)))
 
 
-def mask_kernel(share, rows, after_count, core_ref, weight_ref, mask_ref, *refs):
-    kept_ref, token_ref, spread, semaphores = refs[after_count:]
+def mask_kernel(share, rows, after_count, core_ref, weight_ref, mask_hbm, *refs):
+    kept_ref, token_ref, spread, mask_ref, mask_semaphore, semaphores = refs[after_count:]
+    mask_copy = pltpu.make_async_copy(mask_hbm, mask_ref, mask_semaphore)
+    mask_copy.start()
     token_ref[...] = jnp.zeros_like(token_ref)
     depth, width = kept_ref.shape
     number = share(core_ref[0])
@@ -88,6 +90,7 @@
     ]
     for copy in copies:
         copy.start()
+    mask_copy.wait()
     marks = mask_ref.shape[1]
     owner = lax.broadcasted_iota(jnp.int32, (marks, width), 1) // BLOCK + number * (width // BLOCK)
     chosen = (owner == lax.broadcasted_iota(jnp.int32, (marks, width), 0)).astype(F32)
@@ -105,14 +108,19 @@
     width = width // shares
     return pl.pallas_call(
         functools.partial(mask_kernel, share, rows, len(after)),
-        in_specs=[pl.BlockSpec(memory_space=pltpu.SMEM), ANYWHERE, INSIDE] + [ANYWHERE] * len(after),
+        in_specs=[pl.BlockSpec(memory_space=pltpu.SMEM)] + [ANYWHERE] * (2 + len(after)),
         out_specs=[INSIDE] * 2,
         out_shape=[jax.ShapeDtypeStruct((depth, width), weight.dtype), TOKEN],
-        scratch_shapes=[pltpu.VMEM((mask.shape[0], width), F32), pltpu.SemaphoreType.DMA((depth // rows,))],
+        scratch_shapes=[
+            pltpu.VMEM((mask.shape[0], width), F32),
+            pltpu.VMEM(mask.shape, mask.dtype),
+            pltpu.SemaphoreType.DMA,
+            pltpu.SemaphoreType.DMA((depth // rows,)),
+        ],
         compiler_params=pltpu.CompilerParams(vmem_limit_bytes=VMEM),
         cost_estimate=as_if(hint),
         name="masked",
-    )(core, pltpu.with_memory_space_constraint(weight, pltpu.HBM), mask, *after)
+    )(core, *(pltpu.with_memory_space_constraint(values, pltpu.HBM) for values in (weight, mask)), *after)
 
 
 def stack_kernel(after_count, *refs):
@@ -435,9 +443,7 @@
     row_stacks = {
         step: [by_row_of_plane(first, step), by_row_of_plane(second, step)] for step in range(1, per_plane)
     }
-    up_kept, last[0] = masked(
-        up_weight, up_mask, tile_of(features, 256), place, 1, lambda core: 0, last + next_stacks[:1], 0.15
-    )
+    last[0] = waited(last + next_stacks[:1], 0.15)
     last[0] = waited([*last, across_stacks[0], *(stacks[0] for stacks in row_stacks.values())], 0.07)
     one_away, last[0] = join(next_stacks, last)
     inner_three, last[0] = join(across_stacks, last)
@@ -455,6 +461,7 @@
         part, last[0] = join(stacks, last)
         parts[0].append(part)
     forward(1, one_away, last)
+    up_kept, last[0] = masked(up_weight, up_mask, tile_of(features, 256), place, 1, lambda core: 0, last)
     multiply_in(0, hint=HURRY)
     exchange(0)
     exchange_near(0)

time: 154 us -> 155 us (level)
  transfers between devices with their start and end apart: 42 -> 42, of which waited for: 18 -> 20; matrix products, arithmetic and copies ran while one was open for 0% -> 0% of each run, Pallas kernels for 36% -> 37%
where the time goes in v21:
time: 155 us; the launch traced here: 154 us
  Pallas kernels  59.6 us (38%)
  waiting for transfers between devices  50.2 us (32%)
  starting transfers between devices  42.8 us (28%)
    ppermute x11, waiting for transfers between devices, by_plane(): return lax.ppermute(behind(values, after), 'cols', pairs)  27.8 us
    pallas_call x4, Pallas kernels, gate_up(): pl.pallas_call(functools.partial(gate_up_kernel, len(parts), len(after)),...  24.3 us
    ppermute x31, starting transfers between devices, swap(): lax.ppermute(values, axis, [(place, place ^ step) for place in range(size)])  24.3 us
    ppermute x31, waiting for transfers between devices, swap(): lax.ppermute(values, axis, [(place, place ^ step) for place in range(size)])  22.3 us
    ppermute x11, starting transfers between devices, by_plane(): return lax.ppermute(behind(values, after), 'cols', pairs)  18.4 us
    pallas_call x4, Pallas kernels, down(): pl.pallas_call(functools.partial(down_kernel, pieces, len(down_kept), len...  15.5 us
    pallas_call x4, Pallas kernels, masked(): pl.pallas_call(functools.partial(mask_kernel, share, rows, len(after)), i...  14.5 us
  transfers between devices with their start and end apart: 42, of which 20 were waited for; matrix products, arithmetic and copies ran while one was open for 0% of the time, Pallas kernels for 37%

profile of v21, /device:TPU:0, one launch (start us, length us, event | category | flops | bytes accessed | tf_op | source)
XLA Modules:
  0.0 154.4 jit_solution(6031830836681629977)
XLA Ops:
  0.0 1.5 normed.1
  2.1 1.3 collective-permute-done
  4.0 2.9 %collective-permute-start.1 = (bf16[2,1,40,2048]{3,2,1,0:T(8,128)(2,1)S(1)}, bf16[2,1,40,2048]{3,2,1,0:T(8,128)(2,1)S(1)}, u32[]{:S(2)}, u32[]{:S(2)}) collective-permute-start(bf16[2,1,40,2048]{3,2,1,0:T(8,128)(2,1)S(1)} %get-tuple-element.101.refs_2_), channel_id=1, source_target_pairs={{0,16},{8,24},{16,0},{24,8},{1,17},{9,25},{17,1},{25,9},{2,18},{10... | collective-permute-start | bytes 983048 | tf_op jit(solution)/shard_map/ppermute | solution.py:357
  6.9 1.6 %collective-permute-start.6 = (bf16[2,1,40,2048]{3,2,1,0:T(8,128)(2,1)S(1)}, bf16[2,1,40,2048]{3,2,1,0:T(8,128)(2,1)S(1)}, u32[]{:S(2)}, u32[]{:S(2)}) collective-permute-start(bf16[2,1,40,2048]{3,2,1,0:T(8,128)(2,1)S(1)} %get-tuple-element.102.refs_0_), channel_id=1, source_target_pairs={{0,2},{1,3},{2,0},{3,1},{4,6},{5,7},{6,4},{7,5},{8,10},{9,11},{10,... | collective-permute-start | bytes 983048 | tf_op jit(solution)/shard_map/ppermute | solution.py:387
  9.2 1.6 %collective-permute-start.2 = (bf16[2,1,40,2048]{3,2,1,0:T(8,128)(2,1)S(1)}, bf16[2,1,40,2048]{3,2,1,0:T(8,128)(2,1)S(1)}, u32[]{:S(2)}, u32[]{:S(2)}) collective-permute-start(bf16[2,1,40,2048]{3,2,1,0:T(8,128)(2,1)S(1)} %get-tuple-element.102.refs_0_), channel_id=1, source_target_pairs={{0,1},{1,0},{2,3},{3,2},{4,5},{5,4},{6,7},{7,6},{8,9},{9,8},{10,11... | collective-permute-start | bytes 983048 | tf_op jit(solution)/shard_map/ppermute | solution.py:357
  10.8 4.1 %collective-permute-done.1.refs_1_ = bf16[2,1,40,2048]{3,2,1,0:T(8,128)(2,1)S(1)} collective-permute-done((bf16[2,1,40,2048]{3,2,1,0:T(8,128)(2,1)S(1)}, bf16[2,1,40,2048]{3,2,1,0:T(8,128)(2,1)S(1)}, u32[]{:S(2)}, u32[]{:S(2)}) %collective-permute-start.1) | collective-permute-done | bytes 327712 | tf_op jit(solution)/shard_map/ppermute | solution.py:357
  14.9 1.8 %collective-permute-start.7 = (bf16[2,1,40,2048]{3,2,1,0:T(8,128)(2,1)S(1)}, bf16[2,1,40,2048]{3,2,1,0:T(8,128)(2,1)S(1)}, u32[]{:S(2)}, u32[]{:S(2)}) collective-permute-start(bf16[2,1,40,2048]{3,2,1,0:T(8,128)(2,1)S(1)} %collective-permute-done.1.refs_1_), channel_id=1, source_target_pairs={{0,2},{1,3},{2,0},{3,1},{4,6},{5,7},{6,4},{7,5},{8,10},{9,11},{10,... | collective-permute-start | bytes 983048 | tf_op jit(solution)/shard_map/ppermute | solution.py:387
  17.4 1.6 %collective-permute-start.3 = (bf16[2,1,40,2048]{3,2,1,0:T(8,128)(2,1)S(1)}, bf16[2,1,40,2048]{3,2,1,0:T(8,128)(2,1)S(1)}, u32[]{:S(2)}, u32[]{:S(2)}) collective-permute-start(bf16[2,1,40,2048]{3,2,1,0:T(8,128)(2,1)S(1)} %collective-permute-done.1.refs_1_), channel_id=1, source_target_pairs={{0,1},{1,0},{2,3},{3,2},{4,5},{5,4},{6,7},{7,6},{8,9},{9,8},{10,11... | collective-permute-start | bytes 983048 | tf_op jit(solution)/shard_map/ppermute | solution.py:357
  19.0 3.6 %masked.4 = (bf16[2048,1792]{1,0:T(8,128)(2,1)S(1)}, f32[8,128]{1,0:T(8,128)S(1)}) custom-call(s32[1]{0:T(128)} %bitcast.5.core_ref, bf16[2048,1792]{1,0:T(8,128)(2,1)} %weight_ref.4, s32[32,28]{1,0:T(8,128)} %mask_hbm.4, f32[8,128]{1,0:T(8,128)S(1)} %get-tuple-element.103.refs_0_), custom_call_target="tpu_custom_call" | custom-call | tf_op jit(solution)/shard_map/masked/pallas_call | solution.py:109
  22.7 1.5 collective-permute-done.7.refs_1_
  24.3 5.4 %collective-permute-start.10 = (bf16[160,2048]{1,0:T(8,128)(2,1)S(1)}, bf16[160,2048]{1,0:T(8,128)(2,1)S(1)}, u32[]{:S(2)}, u32[]{:S(2)}) collective-permute-start(bf16[160,2048]{1,0:T(8,128)(2,1)S(1)} %get-tuple-element.118.refs_0_.mine_ref), channel_id=1, source_target_pairs={{0,6},{1,7},{6,0},{7,1},{8,14},{9,15},{14,8},{15,9},{16,22},{17,23... | collective-permute-start | bytes 1966088 | tf_op jit(solution)/shard_map/ppermute | solution.py:387
  29.8 1.6 %collective-permute-start.12 = (bf16[160,2048]{1,0:T(8,128)(2,1)S(1)}, bf16[160,2048]{1,0:T(8,128)(2,1)S(1)}, u32[]{:S(2)}, u32[]{:S(2)}) collective-permute-start(bf16[160,2048]{1,0:T(8,128)(2,1)S(1)} %get-tuple-element.125.refs_0_), channel_id=1, source_target_pairs={{0,1},{1,0},{2,3},{3,2},{4,5},{5,4},{6,7},{7,6},{8,9},{9,8},{10,11... | collective-permute-start | bytes 1966088 | tf_op jit(solution)/shard_map/ppermute | solution.py:357
  31.4 3.5 %masked.5 = (bf16[2048,1792]{1,0:T(8,128)(2,1)S(1)}, f32[8,128]{1,0:T(8,128)S(1)}) custom-call(s32[1]{0:T(128)} %bitcast.5.core_ref, bf16[2048,1792]{1,0:T(8,128)(2,1)} %weight_ref.5, s32[32,28]{1,0:T(8,128)} %mask_hbm.5, f32[8,128]{1,0:T(8,128)S(1)} %get-tuple-element.111.refs_0_), custom_call_target="tpu_custom_call" | custom-call | tf_op jit(solution)/shard_map/masked/pallas_call | solution.py:109
  34.9 6.1 %gate_up.4 = (bf16[2,2,2,40,1792]{4,3,2,1,0:T(8,128)(2,1)S(1)}, bf16[2,2,40,1792]{3,2,1,0:T(8,128)(2,1)S(1)}, bf16[2,2,1,40,1792]{4,3,2,1,0:T(8,128)(2,1)S(1)}, f32[8,128]{1,0:T(8,128)S(1)}) custom-call(bf16[160,2048]{1,0:T(8,128)(2,1)S(1)} %get-tuple-element.118.refs_0_.mine_ref, bf16[160,2048]{1,0:T(8,128)(2,1)S(1)} %get-tuple-element.109.refs_1_, ...), custom_call_target="tpu_custom_call" | custom-call | flops 4697620480 | tf_op jit(solution)/shard_map/gate_up/pallas_call | solution.py:239
  41.5 3.7 %masked.6 = (bf16[1792,2048]{1,0:T(8,128)(2,1)S(1)}, f32[8,128]{1,0:T(8,128)S(1)}) custom-call(s32[1]{0:T(128)} %bitcast.5.core_ref, bf16[1792,8192]{1,0:T(8,128)(2,1)} %weight_ref.7, s32[28,128]{1,0:T(8,128)} %mask_hbm.7, f32[8,128]{1,0:T(8,128)S(1)} %get-tuple-element.119.refs_0_), custom_call_target="tpu_custom_call" | custom-call | tf_op jit(solution)/shard_map/masked/pallas_call | solution.py:109
  46.1 0.9 collective-permute-start.11
  47.0 6.1 %gate_up.5 = (bf16[2,2,2,40,1792]{4,3,2,1,0:T(8,128)(2,1)S(1)}, bf16[2,2,40,1792]{3,2,1,0:T(8,128)(2,1)S(1)}, bf16[2,2,1,40,1792]{4,3,2,1,0:T(8,128)(2,1)S(1)}, f32[8,128]{1,0:T(8,128)S(1)}) custom-call(bf16[160,2048]{1,0:T(8,128)(2,1)S(1)} %get-tuple-element.125.refs_0_, bf16[160,2048]{1,0:T(8,128)(2,1)S(1)} %collective-permute-done.12.refs_1_, ...), custom_call_target="tpu_custom_call" | custom-call | flops 4697620480 | tf_op jit(solution)/shard_map/gate_up/pallas_call | solution.py:239
  53.7 1.5 collective-permute-done.13.refs_1_
  55.1 0.8 collective-permute-done.14.refs_3_.refs_1_
  56.1 1.6 %collective-permute-start.16 = (bf16[2,2,40,1792]{3,2,1,0:T(8,128)(2,1)S(1)}, bf16[2,2,40,1792]{3,2,1,0:T(8,128)(2,1)S(1)}, u32[]{:S(2)}, u32[]{:S(2)}) collective-permute-start(bf16[2,2,40,1792]{3,2,1,0:T(8,128)(2,1)S(1)} %get-tuple-element.134), channel_id=1, source_target_pairs={{0,16},{8,24},{16,0},{24,8},{1,17},{9,25},{17,1},{25,9},{2,18},{10... | collective-permute-start | bytes 1720328 | tf_op jit(solution)/shard_map/ppermute | solution.py:357
  57.7 3.7 %masked.7 = (bf16[1792,2048]{1,0:T(8,128)(2,1)S(1)}, f32[8,128]{1,0:T(8,128)S(1)}) custom-call(s32[1]{0:T(128)} %bitcast.5.core_ref, bf16[1792,8192]{1,0:T(8,128)(2,1)} %weight_ref.7, s32[28,128]{1,0:T(8,128)} %mask_hbm.7, f32[8,128]{1,0:T(8,128)S(1)} %get-tuple-element.131.refs_0_), custom_call_target="tpu_custom_call" | custom-call | tf_op jit(solution)/shard_map/masked/pallas_call | solution.py:109
  61.4 1.2 collective-permute-done.11.refs_5_.refs_0_
  62.6 1.5 collective-permute-start.15
  64.1 6.1 %gate_up.6 = (bf16[2,2,2,40,1792]{4,3,2,1,0:T(8,128)(2,1)S(1)}, bf16[2,2,40,1792]{3,2,1,0:T(8,128)(2,1)S(1)}, bf16[2,2,1,40,1792]{4,3,2,1,0:T(8,128)(2,1)S(1)}, f32[8,128]{1,0:T(8,128)S(1)}) custom-call(bf16[160,2048]{1,0:T(8,128)(2,1)S(1)} %get-tuple-element.136.refs_0_, bf16[160,2048]{1,0:T(8,128)(2,1)S(1)} %collective-permute-done.17.refs_1_, ...), custom_call_target="tpu_custom_call" | custom-call | flops 4697620480 | tf_op jit(solution)/shard_map/gate_up/pallas_call | solution.py:239
  72.2 0.8 collective-permute-done.20.refs_3_.refs_1_
  73.2 1.5 collective-permute-start.23
  74.7 3.9 %down.4 = (bf16[2,40,4096]{2,1,0:T(8,128)(2,1)S(1)}, bf16[2,40,4096]{2,1,0:T(8,128)(2,1)S(1)}, f32[8,128]{1,0:T(8,128)S(1)}) custom-call(bf16[2,40,1792]{2,1,0:T(8,128)(2,1)S(1)} %get-tuple-element.138.own_ref, bf16[2,40,1792]{2,1,0:T(8,128)(2,1)S(1)} %collective-permute-done.18.other_ref, bf16[1792,2048]{1,0:T(8,128)(2,1)S(1)} %get-tuple-element.139.refs_0_, ...), custom_call_target="tpu_custom_call" | custom-call | flops 2348810 | tf_op jit(solution)/shard_map/down/pallas_call | solution.py:281
  78.6 1.0 collective-permute-start.28
  79.6 6.1 %gate_up.7 = (bf16[2,2,2,40,1792]{4,3,2,1,0:T(8,128)(2,1)S(1)}, bf16[2,2,40,1792]{3,2,1,0:T(8,128)(2,1)S(1)}, bf16[1,2,1,40,1792]{4,3,2,1,0:T(8,128)(2,1)S(1)}, ...) custom-call(bf16[160,2048]{1,0:T(8,128)(2,1)S(1)} %collective-permute-done.11.refs_5_.refs_0_, ...), custom_call_target="tpu_custom_call" | custom-call | flops 4697620480 | tf_op jit(solution)/shard_map/gate_up/pallas_call | solution.py:239
  86.3 2.0 %collective-permute-done.23.refs_2_ = bf16[2,2,40,1792]{3,2,1,0:T(8,128)(2,1)S(1)} collective-permute-done((bf16[2,2,40,1792]{3,2,1,0:T(8,128)(2,1)S(1)}, bf16[2,2,40,1792]{3,2,1,0:T(8,128)(2,1)S(1)}, u32[]{:S(2)}, u32[]{:S(2)}) %collective-permute-start.23) | collective-permute-done | bytes 573472 | tf_op jit(solution)/shard_map/ppermute | solution.py:357
  89.4 1.5 collective-permute-start.24
  90.9 3.9 %down.5 = (bf16[1,40,4096]{2,1,0:T(8,128)(2,1)S(1)}, bf16[1,40,4096]{2,1,0:T(8,128)(2,1)S(1)}, bf16[1,40,4096]{2,1,0:T(8,128)(2,1)S(1)}, bf16[1,40,4096]{2,1,0:T(8,128)(2,1)S(1)}, f32[8,128]{1,0:T(8,128)S(1)}) custom-call(bf16[2,40,1792]{2,1,0:T(8,128)(2,1)S(1)} %get-tuple-element.158.own_ref, bf16[2,40,1792]{2,1,0:T(8,128)(2,1)S(1)} %collective-permute-done.27.other_ref, ...), custom_call_target="tpu_custom_call" | custom-call | flops 2348810 | tf_op jit(solution)/shard_map/down/pallas_call | solution.py:281
  95.9 1.5 collective-permute-start.34
  97.3 6.9 %collective-permute-done.29.refs_1_ = bf16[1,40,4096]{2,1,0:T(8,128)(2,1)S(1)} collective-permute-done((bf16[1,40,4096]{2,1,0:T(8,128)(2,1)S(1)}, bf16[1,40,4096]{2,1,0:T(8,128)(2,1)S(1)}, u32[]{:S(2)}, u32[]{:S(2)}) %collective-permute-start.29) | collective-permute-done | bytes 327712 | tf_op jit(solution)/shard_map/ppermute | solution.py:357
  105.3 1.2 collective-permute-start.25
  106.5 1.4 collective-permute-start.33
  107.9 3.9 %down.6 = (bf16[1,40,4096]{2,1,0:T(8,128)(2,1)S(1)}, bf16[1,40,4096]{2,1,0:T(8,128)(2,1)S(1)}, bf16[1,40,4096]{2,1,0:T(8,128)(2,1)S(1)}, bf16[1,40,4096]{2,1,0:T(8,128)(2,1)S(1)}, f32[8,128]{1,0:T(8,128)S(1)}) custom-call(bf16[2,40,1792]{2,1,0:T(8,128)(2,1)S(1)} %get-tuple-element.168.own_ref, bf16[2,40,1792]{2,1,0:T(8,128)(2,1)S(1)} %collective-permute-done.30.other_ref, ...), custom_call_target="tpu_custom_call" | custom-call | flops 2348810 | tf_op jit(solution)/shard_map/down/pallas_call | solution.py:281
  112.5 0.9 collective-permute-start.32
  113.7 1.5 collective-permute-start.38
  115.2 5.5 %collective-permute-done.33.refs_2_ = bf16[1,40,4096]{2,1,0:T(8,128)(2,1)S(1)} collective-permute-done((bf16[1,40,4096]{2,1,0:T(8,128)(2,1)S(1)}, bf16[1,40,4096]{2,1,0:T(8,128)(2,1)S(1)}, u32[]{:S(2)}, u32[]{:S(2)}) %collective-permute-start.33) | collective-permute-done | bytes 327712 | tf_op jit(solution)/shard_map/ppermute | solution.py:387
  121.5 1.6 %collective-permute-start.36 = (bf16[1,40,4096]{2,1,0:T(8,128)(2,1)S(1)}, bf16[1,40,4096]{2,1,0:T(8,128)(2,1)S(1)}, u32[]{:S(2)}, u32[]{:S(2)}) collective-permute-start(bf16[1,40,4096]{2,1,0:T(8,128)(2,1)S(1)} %get-tuple-element.187), channel_id=1, source_target_pairs={{0,1},{1,0},{2,3},{3,2},{4,5},{5,4},{6,7},{7,6},{8,9},{9,8},{10,11... | collective-permute-start | bytes 983048 | tf_op jit(solution)/shard_map/ppermute | solution.py:357
  123.0 1.1 collective-permute-start.40
  124.5 1.6 %collective-permute-done.35.other_ref = bf16[2,40,1792]{2,1,0:T(8,128)(2,1)S(1)} collective-permute-done((bf16[2,40,1792]{2,1,0:T(8,128)(2,1)S(1)}, bf16[2,40,1792]{2,1,0:T(8,128)(2,1)S(1)}, u32[]{:S(2)}, u32[]{:S(2)}) %collective-permute-start.35) | collective-permute-done | bytes 286752 | tf_op jit(solution)/shard_map/ppermute | solution.py:357
  126.1 3.9 %down.7 = (bf16[2,40,4096]{2,1,0:T(8,128)(2,1)S(1)}, bf16[2,40,4096]{2,1,0:T(8,128)(2,1)S(1)}, f32[8,128]{1,0:T(8,128)S(1)}) custom-call(bf16[2,40,1792]{2,1,0:T(8,128)(2,1)S(1)} %get-tuple-element.181.own_ref, bf16[2,40,1792]{2,1,0:T(8,128)(2,1)S(1)} %collective-permute-done.35.other_ref, bf16[1792,2048]{1,0:T(8,128)(2,1)S(1)} %get-tuple-element.139.refs_0_, ...), custom_call_target="tpu_custom_call" | custom-call | flops 2348810 | tf_op jit(solution)/shard_map/down/pallas_call | solution.py:281
  130.1 1.9 %collective-permute-start.39 = (bf16[1,40,4096]{2,1,0:T(8,128)(2,1)S(1)}, bf16[1,40,4096]{2,1,0:T(8,128)(2,1)S(1)}, u32[]{:S(2)}, u32[]{:S(2)}) collective-permute-start(bf16[1,40,4096]{2,1,0:T(8,128)(2,1)S(1)} %get-tuple-element.194), channel_id=1, source_target_pairs={{0,4},{1,5},{4,0},{5,1},{2,6},{3,7},{6,2},{7,3},{8,12},{9,13},{12,... | collective-permute-start | bytes 983048 | tf_op jit(solution)/shard_map/ppermute | solution.py:387
  132.6 14.9 %collective-permute-done.40.refs_0_ = bf16[1,40,4096]{2,1,0:T(8,128)(2,1)S(1)} collective-permute-done((bf16[1,40,4096]{2,1,0:T(8,128)(2,1)S(1)}, bf16[1,40,4096]{2,1,0:T(8,128)(2,1)S(1)}, u32[]{:S(2)}, u32[]{:S(2)}) %collective-permute-start.40) | collective-permute-done | bytes 327712 | tf_op jit(solution)/shard_map/ppermute | solution.py:387
  148.7 4.5 %collective-permute-done.39 = bf16[1,40,4096]{2,1,0:T(8,128)(2,1)S(1)} collective-permute-done((bf16[1,40,4096]{2,1,0:T(8,128)(2,1)S(1)}, bf16[1,40,4096]{2,1,0:T(8,128)(2,1)S(1)}, u32[]{:S(2)}, u32[]{:S(2)}) %collective-permute-start.39) | collective-permute-done | bytes 327712 | tf_op jit(solution)/shard_map/ppermute | solution.py:387
  153.5 0.9 pad_maximum_fusion
  (80 shorter events, 15.4 us)
Async XLA Ops:
  1.6 1.8 %collective-permute-start = (bf16[2,40,2048]{2,1,0:T(8,128)(2,1)S(1)}, bf16[2,40,2048]{2,1,0:T(8,128)(2,1)S(1)}, u32[]{:S(2)}, u32[]{:S(2)}) collective-permute-start(bf16[2,40,2048]{2,1,0:T(8,128)(2,1)S(1)} %pad_maximum_fusion.1), channel_id=1, source_target_pairs={{0,8},{8,0},{16,24},{24,16},{1,9},{9,1},{17,25},{25,17},{2,10},{10... | collective-permute-start | bytes 983048 | tf_op jit(solution)/shard_map/ppermute | solution.py:357
  4.0 10.9 %collective-permute-start.1 = (bf16[2,1,40,2048]{3,2,1,0:T(8,128)(2,1)S(1)}, bf16[2,1,40,2048]{3,2,1,0:T(8,128)(2,1)S(1)}, u32[]{:S(2)}, u32[]{:S(2)}) collective-permute-start(bf16[2,1,40,2048]{3,2,1,0:T(8,128)(2,1)S(1)} %get-tuple-element.101.refs_2_), channel_id=1, source_target_pairs={{0,16},{8,24},{16,0},{24,8},{1,17},{9,25},{17,1},{25,9},{2,18},{10... | collective-permute-start | bytes 983048 | tf_op jit(solution)/shard_map/ppermute | solution.py:357
  6.9 10.5 %collective-permute-start.6 = (bf16[2,1,40,2048]{3,2,1,0:T(8,128)(2,1)S(1)}, bf16[2,1,40,2048]{3,2,1,0:T(8,128)(2,1)S(1)}, u32[]{:S(2)}, u32[]{:S(2)}) collective-permute-start(bf16[2,1,40,2048]{3,2,1,0:T(8,128)(2,1)S(1)} %get-tuple-element.102.refs_0_), channel_id=1, source_target_pairs={{0,2},{1,3},{2,0},{3,1},{4,6},{5,7},{6,4},{7,5},{8,10},{9,11},{10,... | collective-permute-start | bytes 983048 | tf_op jit(solution)/shard_map/ppermute | solution.py:387
  8.6 14.1 %collective-permute-start.4 = (bf16[2,1,40,2048]{3,2,1,0:T(8,128)(2,1)S(1)}, bf16[2,1,40,2048]{3,2,1,0:T(8,128)(2,1)S(1)}, u32[]{:S(2)}, u32[]{:S(2)}) collective-permute-start(bf16[2,1,40,2048]{3,2,1,0:T(8,128)(2,1)S(1)} %get-tuple-element.102.refs_0_), channel_id=1, source_target_pairs={{2,4},{3,5},{4,2},{5,3},{10,12},{11,13},{12,10},{13,11},{18,20},{1... | collective-permute-start | bytes 983048 | tf_op jit(solution)/shard_map/ppermute | solution.py:387
  9.2 13.4 %collective-permute-start.2 = (bf16[2,1,40,2048]{3,2,1,0:T(8,128)(2,1)S(1)}, bf16[2,1,40,2048]{3,2,1,0:T(8,128)(2,1)S(1)}, u32[]{:S(2)}, u32[]{:S(2)}) collective-permute-start(bf16[2,1,40,2048]{3,2,1,0:T(8,128)(2,1)S(1)} %get-tuple-element.102.refs_0_), channel_id=1, source_target_pairs={{0,1},{1,0},{2,3},{3,2},{4,5},{5,4},{6,7},{7,6},{8,9},{9,8},{10,11... | collective-permute-start | bytes 983048 | tf_op jit(solution)/shard_map/ppermute | solution.py:357
  14.9 9.2 %collective-permute-start.7 = (bf16[2,1,40,2048]{3,2,1,0:T(8,128)(2,1)S(1)}, bf16[2,1,40,2048]{3,2,1,0:T(8,128)(2,1)S(1)}, u32[]{:S(2)}, u32[]{:S(2)}) collective-permute-start(bf16[2,1,40,2048]{3,2,1,0:T(8,128)(2,1)S(1)} %collective-permute-done.1.refs_1_), channel_id=1, source_target_pairs={{0,2},{1,3},{2,0},{3,1},{4,6},{5,7},{6,4},{7,5},{8,10},{9,11},{10,... | collective-permute-start | bytes 983048 | tf_op jit(solution)/shard_map/ppermute | solution.py:387
  16.7 7.5 %collective-permute-start.5 = (bf16[2,1,40,2048]{3,2,1,0:T(8,128)(2,1)S(1)}, bf16[2,1,40,2048]{3,2,1,0:T(8,128)(2,1)S(1)}, u32[]{:S(2)}, u32[]{:S(2)}) collective-permute-start(bf16[2,1,40,2048]{3,2,1,0:T(8,128)(2,1)S(1)} %collective-permute-done.1.refs_1_), channel_id=1, source_target_pairs={{2,4},{3,5},{4,2},{5,3},{10,12},{11,13},{12,10},{13,11},{18,20},{1... | collective-permute-start | bytes 983048 | tf_op jit(solution)/shard_map/ppermute | solution.py:387
  17.4 12.3 %collective-permute-start.3 = (bf16[2,1,40,2048]{3,2,1,0:T(8,128)(2,1)S(1)}, bf16[2,1,40,2048]{3,2,1,0:T(8,128)(2,1)S(1)}, u32[]{:S(2)}, u32[]{:S(2)}) collective-permute-start(bf16[2,1,40,2048]{3,2,1,0:T(8,128)(2,1)S(1)} %collective-permute-done.1.refs_1_), channel_id=1, source_target_pairs={{0,1},{1,0},{2,3},{3,2},{4,5},{5,4},{6,7},{7,6},{8,9},{9,8},{10,11... | collective-permute-start | bytes 983048 | tf_op jit(solution)/shard_map/ppermute | solution.py:357
  24.3 21.0 %collective-permute-start.10 = (bf16[160,2048]{1,0:T(8,128)(2,1)S(1)}, bf16[160,2048]{1,0:T(8,128)(2,1)S(1)}, u32[]{:S(2)}, u32[]{:S(2)}) collective-permute-start(bf16[160,2048]{1,0:T(8,128)(2,1)S(1)} %get-tuple-element.118.refs_0_.mine_ref), channel_id=1, source_target_pairs={{0,6},{1,7},{6,0},{7,1},{8,14},{9,15},{14,8},{15,9},{16,22},{17,23... | collective-permute-start | bytes 1966088 | tf_op jit(solution)/shard_map/ppermute | solution.py:387
  29.8 15.8 %collective-permute-start.12 = (bf16[160,2048]{1,0:T(8,128)(2,1)S(1)}, bf16[160,2048]{1,0:T(8,128)(2,1)S(1)}, u32[]{:S(2)}, u32[]{:S(2)}) collective-permute-start(bf16[160,2048]{1,0:T(8,128)(2,1)S(1)} %get-tuple-element.125.refs_0_), channel_id=1, source_target_pairs={{0,1},{1,0},{2,3},{3,2},{4,5},{5,4},{6,7},{7,6},{8,9},{9,8},{10,11... | collective-permute-start | bytes 1966088 | tf_op jit(solution)/shard_map/ppermute | solution.py:357
  41.0 4.4 %collective-permute-start.8 = (bf16[2,2,40,1792]{3,2,1,0:T(8,128)(2,1)S(1)}, bf16[2,2,40,1792]{3,2,1,0:T(8,128)(2,1)S(1)}, u32[]{:S(2)}, u32[]{:S(2)}) collective-permute-start(bf16[2,2,40,1792]{3,2,1,0:T(8,128)(2,1)S(1)} %get-tuple-element.115), channel_id=1, source_target_pairs={{0,8},{8,0},{16,24},{24,16},{1,9},{9,1},{17,25},{25,17},{2,10},{10... | collective-permute-start | bytes 1720328 | tf_op jit(solution)/shard_map/ppermute | solution.py:357
  41.0 4.4 %collective-permute-start.9 = (bf16[2,2,1,40,1792]{4,3,2,1,0:T(8,128)(2,1)S(1)}, bf16[2,2,1,40,1792]{4,3,2,1,0:T(8,128)(2,1)S(1)}, u32[]{:S(2)}, u32[]{:S(2)}) collective-permute-start(bf16[2,2,1,40,1792]{4,3,2,1,0:T(8,128)(2,1)S(1)} %get-tuple-element.116), channel_id=1, source_target_pairs={{0,8},{8,0},{16,24},{24,16},{1,9},{9,1},{17,25},{25,17},{2,10},{10... | collective-permute-start | bytes 1720328 | tf_op jit(solution)/shard_map/ppermute | solution.py:357
  45.5 18.5 %collective-permute-start.17 = (bf16[160,2048]{1,0:T(8,128)(2,1)S(1)}, bf16[160,2048]{1,0:T(8,128)(2,1)S(1)}, u32[]{:S(2)}, u32[]{:S(2)}) collective-permute-start(bf16[160,2048]{1,0:T(8,128)(2,1)S(1)} %get-tuple-element.136.refs_0_), channel_id=1, source_target_pairs={{0,1},{1,0},{2,3},{3,2},{4,5},{5,4},{6,7},{7,6},{8,9},{9,8},{10,11... | collective-permute-start | bytes 1966088 | tf_op jit(solution)/shard_map/ppermute | solution.py:357
  46.1 16.5 %collective-permute-start.11 = (bf16[160,2048]{1,0:T(8,128)(2,1)S(1)}, bf16[160,2048]{1,0:T(8,128)(2,1)S(1)}, u32[]{:S(2)}, u32[]{:S(2)}) collective-permute-start(bf16[160,2048]{1,0:T(8,128)(2,1)S(1)} %get-tuple-element.123), channel_id=1, source_target_pairs={{0,4},{1,5},{4,6},{5,7},{6,2},{7,3},{2,0},{3,1},{8,12},{9,13},{12,... | collective-permute-start | bytes 1966088 | tf_op jit(solution)/shard_map/ppermute | solution.py:387
  53.1 2.0 %collective-permute-start.13 = (bf16[2,2,1,40,1792]{4,3,2,1,0:T(8,128)(2,1)S(1)}, bf16[2,2,1,40,1792]{4,3,2,1,0:T(8,128)(2,1)S(1)}, u32[]{:S(2)}, u32[]{:S(2)}) collective-permute-start(bf16[2,2,1,40,1792]{4,3,2,1,0:T(8,128)(2,1)S(1)} %get-tuple-element.128), channel_id=1, source_target_pairs={{0,8},{8,0},{16,24},{24,16},{1,9},{9,1},{17,25},{25,17},{2,10},{10... | collective-permute-start | bytes 1720328 | tf_op jit(solution)/shard_map/ppermute | solution.py:357
  53.2 2.8 %collective-permute-start.14 = (bf16[2,2,40,1792]{3,2,1,0:T(8,128)(2,1)S(1)}, bf16[2,2,40,1792]{3,2,1,0:T(8,128)(2,1)S(1)}, u32[]{:S(2)}, u32[]{:S(2)}) collective-permute-start(bf16[2,2,40,1792]{3,2,1,0:T(8,128)(2,1)S(1)} %get-tuple-element.130), channel_id=1, source_target_pairs={{0,8},{8,0},{16,24},{24,16},{1,9},{9,1},{17,25},{25,17},{2,10},{10... | collective-permute-start | bytes 1720328 | tf_op jit(solution)/shard_map/ppermute | solution.py:357
  56.1 15.1 %collective-permute-start.16 = (bf16[2,2,40,1792]{3,2,1,0:T(8,128)(2,1)S(1)}, bf16[2,2,40,1792]{3,2,1,0:T(8,128)(2,1)S(1)}, u32[]{:S(2)}, u32[]{:S(2)}) collective-permute-start(bf16[2,2,40,1792]{3,2,1,0:T(8,128)(2,1)S(1)} %get-tuple-element.134), channel_id=1, source_target_pairs={{0,16},{8,24},{16,0},{24,8},{1,17},{9,25},{17,1},{25,9},{2,18},{10... | collective-permute-start | bytes 1720328 | tf_op jit(solution)/shard_map/ppermute | solution.py:357
  62.6 16.0 %collective-permute-start.15 = (bf16[160,2048]{1,0:T(8,128)(2,1)S(1)}, bf16[160,2048]{1,0:T(8,128)(2,1)S(1)}, u32[]{:S(2)}, u32[]{:S(2)}) collective-permute-start(bf16[160,2048]{1,0:T(8,128)(2,1)S(1)} %collective-permute-done.11.refs_5_.refs_0_), channel_id=1, source_target_pairs={{0,1},{1,0},{2,3},{3,2},{4,5},{5,4},{6,7},{7,6},{8,9},{9,8},{10,11... | collective-permute-start | bytes 1966088 | tf_op jit(solution)/shard_map/ppermute | solution.py:357
  70.2 2.0 %collective-permute-start.19 = (bf16[2,2,1,40,1792]{4,3,2,1,0:T(8,128)(2,1)S(1)}, bf16[2,2,1,40,1792]{4,3,2,1,0:T(8,128)(2,1)S(1)}, u32[]{:S(2)}, u32[]{:S(2)}) collective-permute-start(bf16[2,2,1,40,1792]{4,3,2,1,0:T(8,128)(2,1)S(1)} %get-tuple-element.142), channel_id=1, source_target_pairs={{0,8},{8,0},{16,24},{24,16},{1,9},{9,1},{17,25},{25,17},{2,10},{10... | collective-permute-start | bytes 1720328 | tf_op jit(solution)/shard_map/ppermute | solution.py:357
  70.2 2.8 %collective-permute-start.20 = (bf16[2,2,40,1792]{3,2,1,0:T(8,128)(2,1)S(1)}, bf16[2,2,40,1792]{3,2,1,0:T(8,128)(2,1)S(1)}, u32[]{:S(2)}, u32[]{:S(2)}) collective-permute-start(bf16[2,2,40,1792]{3,2,1,0:T(8,128)(2,1)S(1)} %get-tuple-element.144), channel_id=1, source_target_pairs={{0,8},{8,0},{16,24},{24,16},{1,9},{9,1},{17,25},{25,17},{2,10},{10... | collective-permute-start | bytes 1720328 | tf_op jit(solution)/shard_map/ppermute | solution.py:357
  71.5 3.2 %collective-permute-start.18 = (bf16[2,40,1792]{2,1,0:T(8,128)(2,1)S(1)}, bf16[2,40,1792]{2,1,0:T(8,128)(2,1)S(1)}, u32[]{:S(2)}, u32[]{:S(2)}) collective-permute-start(bf16[2,40,1792]{2,1,0:T(8,128)(2,1)S(1)} %get-tuple-element.138.own_ref), channel_id=1, source_target_pairs={{0,8},{8,0},{16,24},{24,16},{1,9},{9,1},{17,25},{25,17},{2,10},{10... | collective-permute-start | bytes 860168 | tf_op jit(solution)/shard_map/ppermute | solution.py:357
  73.2 15.1 %collective-permute-start.23 = (bf16[2,2,40,1792]{3,2,1,0:T(8,128)(2,1)S(1)}, bf16[2,2,40,1792]{3,2,1,0:T(8,128)(2,1)S(1)}, u32[]{:S(2)}, u32[]{:S(2)}) collective-permute-start(bf16[2,2,40,1792]{3,2,1,0:T(8,128)(2,1)S(1)} %get-tuple-element.150), channel_id=1, source_target_pairs={{0,16},{8,24},{16,0},{24,8},{1,17},{9,25},{17,1},{25,9},{2,18},{10... | collective-permute-start | bytes 1720328 | tf_op jit(solution)/shard_map/ppermute | solution.py:357
  78.6 16.6 %collective-permute-start.28 = (bf16[2,40,4096]{2,1,0:T(8,128)(2,1)S(1)}, bf16[2,40,4096]{2,1,0:T(8,128)(2,1)S(1)}, u32[]{:S(2)}, u32[]{:S(2)}) collective-permute-start(bf16[2,40,4096]{2,1,0:T(8,128)(2,1)S(1)} %get-tuple-element.162), channel_id=1, source_target_pairs={{0,1},{1,0},{2,3},{3,2},{4,5},{5,4},{6,7},{7,6},{8,9},{9,8},{10,11... | collective-permute-start | bytes 1966088 | tf_op jit(solution)/shard_map/ppermute | solution.py:357
  85.7 2.9 %collective-permute-start.21 = (bf16[1,2,1,40,1792]{4,3,2,1,0:T(8,128)(2,1)S(1)}, bf16[1,2,1,40,1792]{4,3,2,1,0:T(8,128)(2,1)S(1)}, u32[]{:S(2)}, u32[]{:S(2)}) collective-permute-start(bf16[1,2,1,40,1792]{4,3,2,1,0:T(8,128)(2,1)S(1)} %get-tuple-element.148), channel_id=1, source_target_pairs={{0,8},{8,0},{16,24},{24,16},{1,9},{9,1},{17,25},{25,17},{2,10},{10... | collective-permute-start | bytes 860168 | tf_op jit(solution)/shard_map/ppermute | solution.py:357
  85.8 2.8 %collective-permute-start.22 = (bf16[1,2,1,40,1792]{4,3,2,1,0:T(8,128)(2,1)S(1)}, bf16[1,2,1,40,1792]{4,3,2,1,0:T(8,128)(2,1)S(1)}, u32[]{:S(2)}, u32[]{:S(2)}) collective-permute-start(bf16[1,2,1,40,1792]{4,3,2,1,0:T(8,128)(2,1)S(1)} %get-tuple-element.149), channel_id=1, source_target_pairs={{0,8},{8,0},{16,24},{24,16},{1,9},{9,1},{17,25},{25,17},{2,10},{10... | collective-permute-start | bytes 860168 | tf_op jit(solution)/shard_map/ppermute | solution.py:357
  88.6 2.3 %collective-permute-start.27 = (bf16[2,40,1792]{2,1,0:T(8,128)(2,1)S(1)}, bf16[2,40,1792]{2,1,0:T(8,128)(2,1)S(1)}, u32[]{:S(2)}, u32[]{:S(2)}) collective-permute-start(bf16[2,40,1792]{2,1,0:T(8,128)(2,1)S(1)} %get-tuple-element.158.own_ref), channel_id=1, source_target_pairs={{0,8},{8,0},{16,24},{24,16},{1,9},{9,1},{17,25},{25,17},{2,10},{10... | collective-permute-start | bytes 860168 | tf_op jit(solution)/shard_map/ppermute | solution.py:357
  88.8 16.1 %collective-permute-start.26 = (bf16[2,2,40,1792]{3,2,1,0:T(8,128)(2,1)S(1)}, bf16[2,2,40,1792]{3,2,1,0:T(8,128)(2,1)S(1)}, u32[]{:S(2)}, u32[]{:S(2)}) collective-permute-start(bf16[2,2,40,1792]{3,2,1,0:T(8,128)(2,1)S(1)} %get-tuple-element.157), channel_id=1, source_target_pairs={{0,8},{8,0},{16,24},{24,16},{1,9},{9,1},{17,25},{25,17},{2,10},{10... | collective-permute-start | bytes 1720328 | tf_op jit(solution)/shard_map/ppermute | solution.py:357
  89.4 15.5 %collective-permute-start.24 = (bf16[2,2,40,1792]{3,2,1,0:T(8,128)(2,1)S(1)}, bf16[2,2,40,1792]{3,2,1,0:T(8,128)(2,1)S(1)}, u32[]{:S(2)}, u32[]{:S(2)}) collective-permute-start(bf16[2,2,40,1792]{3,2,1,0:T(8,128)(2,1)S(1)} %get-tuple-element.153), channel_id=1, source_target_pairs={{0,16},{8,24},{16,0},{24,8},{1,17},{9,25},{17,1},{25,9},{2,18},{10... | collective-permute-start | bytes 1720328 | tf_op jit(solution)/shard_map/ppermute | solution.py:357
  95.2 9.0 %collective-permute-start.29 = (bf16[1,40,4096]{2,1,0:T(8,128)(2,1)S(1)}, bf16[1,40,4096]{2,1,0:T(8,128)(2,1)S(1)}, u32[]{:S(2)}, u32[]{:S(2)}) collective-permute-start(bf16[1,40,4096]{2,1,0:T(8,128)(2,1)S(1)} %get-tuple-element.163), channel_id=1, source_target_pairs={{0,1},{1,0},{2,3},{3,2},{4,5},{5,4},{6,7},{7,6},{8,9},{9,8},{10,11... | collective-permute-start | bytes 983048 | tf_op jit(solution)/shard_map/ppermute | solution.py:357
  95.9 17.7 %collective-permute-start.34 = (bf16[2,40,4096]{2,1,0:T(8,128)(2,1)S(1)}, bf16[2,40,4096]{2,1,0:T(8,128)(2,1)S(1)}, u32[]{:S(2)}, u32[]{:S(2)}) collective-permute-start(bf16[2,40,4096]{2,1,0:T(8,128)(2,1)S(1)} %get-tuple-element.178), channel_id=1, source_target_pairs={{0,2},{1,3},{2,0},{3,1},{4,6},{5,7},{6,4},{7,5},{8,10},{9,11},{10,... | collective-permute-start | bytes 1966088 | tf_op jit(solution)/shard_map/ppermute | solution.py:387
  104.3 8.2 %collective-permute-start.31 = (bf16[1,40,4096]{2,1,0:T(8,128)(2,1)S(1)}, bf16[1,40,4096]{2,1,0:T(8,128)(2,1)S(1)}, u32[]{:S(2)}, u32[]{:S(2)}) collective-permute-start(bf16[1,40,4096]{2,1,0:T(8,128)(2,1)S(1)} %get-tuple-element.174), channel_id=1, source_target_pairs={{0,1},{1,0},{2,3},{3,2},{4,5},{5,4},{6,7},{7,6},{8,9},{9,8},{10,11... | collective-permute-start | bytes 983048 | tf_op jit(solution)/shard_map/ppermute | solution.py:357
  105.2 2.7 %collective-permute-start.30 = (bf16[2,40,1792]{2,1,0:T(8,128)(2,1)S(1)}, bf16[2,40,1792]{2,1,0:T(8,128)(2,1)S(1)}, u32[]{:S(2)}, u32[]{:S(2)}) collective-permute-start(bf16[2,40,1792]{2,1,0:T(8,128)(2,1)S(1)} %get-tuple-element.168.own_ref), channel_id=1, source_target_pairs={{0,8},{8,0},{16,24},{24,16},{1,9},{9,1},{17,25},{25,17},{2,10},{10... | collective-permute-start | bytes 860168 | tf_op jit(solution)/shard_map/ppermute | solution.py:357
  105.3 18.9 %collective-permute-start.25 = (bf16[2,2,40,1792]{3,2,1,0:T(8,128)(2,1)S(1)}, bf16[2,2,40,1792]{3,2,1,0:T(8,128)(2,1)S(1)}, u32[]{:S(2)}, u32[]{:S(2)}) collective-permute-start(bf16[2,2,40,1792]{3,2,1,0:T(8,128)(2,1)S(1)} %get-tuple-element.154), channel_id=1, source_target_pairs={{0,16},{8,24},{16,0},{24,8},{1,17},{9,25},{17,1},{25,9},{2,18},{10... | collective-permute-start | bytes 1720328 | tf_op jit(solution)/shard_map/ppermute | solution.py:357
  106.5 14.2 %collective-permute-start.33 = (bf16[1,40,4096]{2,1,0:T(8,128)(2,1)S(1)}, bf16[1,40,4096]{2,1,0:T(8,128)(2,1)S(1)}, u32[]{:S(2)}, u32[]{:S(2)}) collective-permute-start(bf16[1,40,4096]{2,1,0:T(8,128)(2,1)S(1)} %get-tuple-element.173), channel_id=1, source_target_pairs={{0,2},{1,3},{2,0},{3,1},{4,6},{5,7},{6,4},{7,5},{8,10},{9,11},{10,... | collective-permute-start | bytes 983048 | tf_op jit(solution)/shard_map/ppermute | solution.py:387
  112.5 8.9 %collective-permute-start.32 = (bf16[1,40,4096]{2,1,0:T(8,128)(2,1)S(1)}, bf16[1,40,4096]{2,1,0:T(8,128)(2,1)S(1)}, u32[]{:S(2)}, u32[]{:S(2)}) collective-permute-start(bf16[1,40,4096]{2,1,0:T(8,128)(2,1)S(1)} %get-tuple-element.175), channel_id=1, source_target_pairs={{0,1},{1,0},{2,3},{3,2},{4,5},{5,4},{6,7},{7,6},{8,9},{9,8},{10,11... | collective-permute-start | bytes 983048 | tf_op jit(solution)/shard_map/ppermute | solution.py:357
  113.7 16.2 %collective-permute-start.38 = (bf16[1,40,4096]{2,1,0:T(8,128)(2,1)S(1)}, bf16[1,40,4096]{2,1,0:T(8,128)(2,1)S(1)}, u32[]{:S(2)}, u32[]{:S(2)}) collective-permute-start(bf16[1,40,4096]{2,1,0:T(8,128)(2,1)S(1)} %get-tuple-element.190), channel_id=1, source_target_pairs={{0,2},{1,3},{2,0},{3,1},{4,6},{5,7},{6,4},{7,5},{8,10},{9,11},{10,... | collective-permute-start | bytes 983048 | tf_op jit(solution)/shard_map/ppermute | solution.py:387
  121.5 8.6 %collective-permute-start.36 = (bf16[1,40,4096]{2,1,0:T(8,128)(2,1)S(1)}, bf16[1,40,4096]{2,1,0:T(8,128)(2,1)S(1)}, u32[]{:S(2)}, u32[]{:S(2)}) collective-permute-start(bf16[1,40,4096]{2,1,0:T(8,128)(2,1)S(1)} %get-tuple-element.187), channel_id=1, source_target_pairs={{0,1},{1,0},{2,3},{3,2},{4,5},{5,4},{6,7},{7,6},{8,9},{9,8},{10,11... | collective-permute-start | bytes 983048 | tf_op jit(solution)/shard_map/ppermute | solution.py:357
  123.0 24.4 %collective-permute-start.40 = (bf16[1,40,4096]{2,1,0:T(8,128)(2,1)S(1)}, bf16[1,40,4096]{2,1,0:T(8,128)(2,1)S(1)}, u32[]{:S(2)}, u32[]{:S(2)}) collective-permute-start(bf16[1,40,4096]{2,1,0:T(8,128)(2,1)S(1)} %get-tuple-element.186), channel_id=1, source_target_pairs={{0,4},{1,5},{4,0},{5,1},{2,6},{3,7},{6,2},{7,3},{8,12},{9,13},{12,... | collective-permute-start | bytes 983048 | tf_op jit(solution)/shard_map/ppermute | solution.py:387
  124.4 1.6 %collective-permute-start.35 = (bf16[2,40,1792]{2,1,0:T(8,128)(2,1)S(1)}, bf16[2,40,1792]{2,1,0:T(8,128)(2,1)S(1)}, u32[]{:S(2)}, u32[]{:S(2)}) collective-permute-start(bf16[2,40,1792]{2,1,0:T(8,128)(2,1)S(1)} %get-tuple-element.181.own_ref), channel_id=1, source_target_pairs={{0,8},{8,0},{16,24},{24,16},{1,9},{9,1},{17,25},{25,17},{2,10},{10... | collective-permute-start | bytes 860168 | tf_op jit(solution)/shard_map/ppermute | solution.py:357
  130.1 23.1 %collective-permute-start.39 = (bf16[1,40,4096]{2,1,0:T(8,128)(2,1)S(1)}, bf16[1,40,4096]{2,1,0:T(8,128)(2,1)S(1)}, u32[]{:S(2)}, u32[]{:S(2)}) collective-permute-start(bf16[1,40,4096]{2,1,0:T(8,128)(2,1)S(1)} %get-tuple-element.194), channel_id=1, source_target_pairs={{0,4},{1,5},{4,0},{5,1},{2,6},{3,7},{6,2},{7,3},{8,12},{9,13},{12,... | collective-permute-start | bytes 983048 | tf_op jit(solution)/shard_map/ppermute | solution.py:387
  132.0 16.5 %collective-permute-start.37 = (bf16[2,40,4096]{2,1,0:T(8,128)(2,1)S(1)}, bf16[2,40,4096]{2,1,0:T(8,128)(2,1)S(1)}, u32[]{:S(2)}, u32[]{:S(2)}) collective-permute-start(bf16[2,40,4096]{2,1,0:T(8,128)(2,1)S(1)} %get-tuple-element.188), channel_id=1, source_target_pairs={{0,1},{1,0},{2,3},{3,2},{4,5},{5,4},{6,7},{7,6},{8,9},{9,8},{10,11... | collective-permute-start | bytes 1966088 | tf_op jit(solution)/shard_map/ppermute | solution.py:357
  148.7 4.6 %collective-permute-start.41 = (bf16[40,4096]{1,0:T(8,128)(2,1)S(1)}, bf16[40,4096]{1,0:T(8,128)(2,1)S(1)}, u32[]{:S(2)}, u32[]{:S(2)}) collective-permute-start(bf16[40,4096]{1,0:T(8,128)(2,1)S(1)} %fusion.1), channel_id=1, source_target_pairs={{0,8},{8,0},{16,24},{24,16},{1,9},{9,1},{17,25},{25,17},{2,10},{10... | collective-permute-start | bytes 983048 | tf_op jit(solution)/shard_map/ppermute | solution.py:357

commit v22 on v20

--- a/solution.py
+++ b/solution.py
@@ -208,7 +208,7 @@
     for place, part in enumerate(parts):
         all_rows[pl.ds(place * half, half), :] = part[:half, :]
         all_rows[pl.ds(kept + place * half, half), :] = part[half:, :]
-    tile = tile_of(gate_ref.shape[1], 256)
+    tile = tile_of(gate_ref.shape[1], 896)
 
     @pl.loop(0, gate_ref.shape[1] // tile)
     def _(number):
@@ -250,7 +250,7 @@
     both[rows:, :] = other_ref[...].astype(F32).reshape(rows, depth).astype(BF16)
     for number, weight_ref in enumerate(weight_refs):
         width = weight_ref.shape[1]
-        down_columns(pieces, both, weight_ref, partial_refs, number * width, tile_of(width, 512))
+        down_columns(pieces, both, weight_ref, partial_refs, number * width, tile_of(width, 1024))
 
 
 def down_columns(pieces, both, weight_ref, partial_refs, first, tile):

time: 154 us -> 152 us (0.987)
  Pallas kernels: 58.2 us -> 55.4 us
    pallas_call x4, Pallas kernels: 15.5 us -> 13.2 us  [down(): pl.pallas_call(functools.partial(down_kernel, pieces, len(down_kept), len...]
  transfers between devices with their start and end apart: 42 -> 42, of which waited for: 18 -> 19; matrix products, arithmetic and copies ran while one was open for 0% -> 0% of each run, Pallas kernels for 36% -> 35%
where the time goes in v22:
time: 152 us
  Pallas kernels  55.4 us (36%)
  waiting for transfers between devices  51.4 us (34%)
  starting transfers between devices  42.7 us (28%)
    ppermute x11, waiting for transfers between devices, by_plane(): return lax.ppermute(behind(values, after), 'cols', pairs)  30.1 us
    ppermute x31, starting transfers between devices, swap(): lax.ppermute(values, axis, [(place, place ^ step) for place in range(size)])  25.9 us
    pallas_call x4, Pallas kernels, gate_up(): pl.pallas_call(functools.partial(gate_up_kernel, len(parts), len(after)),...  23.8 us
    ppermute x31, waiting for transfers between devices, swap(): lax.ppermute(values, axis, [(place, place ^ step) for place in range(size)])  21.3 us
    ppermute x11, starting transfers between devices, by_plane(): return lax.ppermute(behind(values, after), 'cols', pairs)  16.8 us
    pallas_call x4, Pallas kernels, down(): pl.pallas_call(functools.partial(down_kernel, pieces, len(down_kept), len...  13.2 us
    pallas_call x4, Pallas kernels, masked(): pl.pallas_call(functools.partial(mask_kernel, share, rows, len(after)), i...  13 us
  transfers between devices with their start and end apart: 42, of which 19 were waited for; matrix products, arithmetic and copies ran while one was open for 0% of the time, Pallas kernels for 35%

profile of v22, /device:TPU:0, one launch (start us, length us, event | category | flops | bytes accessed | tf_op | source)
XLA Modules:
  0.0 152.1 jit_solution(6732180088644281792)
XLA Ops:
  0.0 1.5 normed.1
  2.2 1.3 collective-permute-done
  4.1 2.9 %collective-permute-start.1 = (bf16[2,1,40,2048]{3,2,1,0:T(8,128)(2,1)S(1)}, bf16[2,1,40,2048]{3,2,1,0:T(8,128)(2,1)S(1)}, u32[]{:S(2)}, u32[]{:S(2)}) collective-permute-start(bf16[2,1,40,2048]{3,2,1,0:T(8,128)(2,1)S(1)} %get-tuple-element.101.refs_2_), channel_id=1, source_target_pairs={{0,16},{8,24},{16,0},{24,8},{1,17},{9,25},{17,1},{25,9},{2,18},{10... | collective-permute-start | bytes 983048 | tf_op jit(solution)/shard_map/ppermute | solution.py:349
  6.9 1.6 %collective-permute-start.6 = (bf16[2,1,40,2048]{3,2,1,0:T(8,128)(2,1)S(1)}, bf16[2,1,40,2048]{3,2,1,0:T(8,128)(2,1)S(1)}, u32[]{:S(2)}, u32[]{:S(2)}) collective-permute-start(bf16[2,1,40,2048]{3,2,1,0:T(8,128)(2,1)S(1)} %get-tuple-element.102.refs_0_), channel_id=1, source_target_pairs={{0,2},{1,3},{2,0},{3,1},{4,6},{5,7},{6,4},{7,5},{8,10},{9,11},{10,... | collective-permute-start | bytes 983048 | tf_op jit(solution)/shard_map/ppermute | solution.py:379
  9.3 1.6 %collective-permute-start.2 = (bf16[2,1,40,2048]{3,2,1,0:T(8,128)(2,1)S(1)}, bf16[2,1,40,2048]{3,2,1,0:T(8,128)(2,1)S(1)}, u32[]{:S(2)}, u32[]{:S(2)}) collective-permute-start(bf16[2,1,40,2048]{3,2,1,0:T(8,128)(2,1)S(1)} %get-tuple-element.102.refs_0_), channel_id=1, source_target_pairs={{0,1},{1,0},{2,3},{3,2},{4,5},{5,4},{6,7},{7,6},{8,9},{9,8},{10,11... | collective-permute-start | bytes 983048 | tf_op jit(solution)/shard_map/ppermute | solution.py:349
  10.8 4.1 %collective-permute-done.1.refs_1_ = bf16[2,1,40,2048]{3,2,1,0:T(8,128)(2,1)S(1)} collective-permute-done((bf16[2,1,40,2048]{3,2,1,0:T(8,128)(2,1)S(1)}, bf16[2,1,40,2048]{3,2,1,0:T(8,128)(2,1)S(1)}, u32[]{:S(2)}, u32[]{:S(2)}) %collective-permute-start.1) | collective-permute-done | bytes 327712 | tf_op jit(solution)/shard_map/ppermute | solution.py:349
  14.9 1.8 %collective-permute-start.7 = (bf16[2,1,40,2048]{3,2,1,0:T(8,128)(2,1)S(1)}, bf16[2,1,40,2048]{3,2,1,0:T(8,128)(2,1)S(1)}, u32[]{:S(2)}, u32[]{:S(2)}) collective-permute-start(bf16[2,1,40,2048]{3,2,1,0:T(8,128)(2,1)S(1)} %collective-permute-done.1.refs_1_), channel_id=1, source_target_pairs={{0,2},{1,3},{2,0},{3,1},{4,6},{5,7},{6,4},{7,5},{8,10},{9,11},{10,... | collective-permute-start | bytes 983048 | tf_op jit(solution)/shard_map/ppermute | solution.py:379
  17.4 1.6 %collective-permute-start.3 = (bf16[2,1,40,2048]{3,2,1,0:T(8,128)(2,1)S(1)}, bf16[2,1,40,2048]{3,2,1,0:T(8,128)(2,1)S(1)}, u32[]{:S(2)}, u32[]{:S(2)}) collective-permute-start(bf16[2,1,40,2048]{3,2,1,0:T(8,128)(2,1)S(1)} %collective-permute-done.1.refs_1_), channel_id=1, source_target_pairs={{0,1},{1,0},{2,3},{3,2},{4,5},{5,4},{6,7},{7,6},{8,9},{9,8},{10,11... | collective-permute-start | bytes 983048 | tf_op jit(solution)/shard_map/ppermute | solution.py:349
  19.7 3.2 %masked.4 = (bf16[2048,1792]{1,0:T(8,128)(2,1)S(1)}, f32[8,128]{1,0:T(8,128)S(1)}) custom-call(s32[1]{0:T(128)} %bitcast.5.core_ref, bf16[2048,1792]{1,0:T(8,128)(2,1)} %weight_ref.4, s32[32,28]{1,0:T(8,128)S(1)} %copy-done.1, f32[8,128]{1,0:T(8,128)S(1)} %get-tuple-element.103.refs_0_), custom_call_target="tpu_custom_call" | custom-call | tf_op jit(solution)/shard_map/masked/pallas_call | solution.py:106
  23.1 3.2 %masked.5 = (bf16[2048,1792]{1,0:T(8,128)(2,1)S(1)}, f32[8,128]{1,0:T(8,128)S(1)}) custom-call(s32[1]{0:T(128)} %bitcast.5.core_ref, bf16[2048,1792]{1,0:T(8,128)(2,1)} %weight_ref.5, s32[32,28]{1,0:T(8,128)S(1)} %copy-done.2, f32[8,128]{1,0:T(8,128)S(1)} %get-tuple-element.106.refs_0_, bf16[2,1,40,2048]{3,2,1,0:T(8,128)(2,1)S(1)} %collective-permute-done.6.refs_1_.refs_0_), custom_call_target="tpu_custom_call" | custom-call | flops 172500000 | tf_op jit(solution)/shard_map/masked/pallas_call | solution.py:106
  26.5 4.5 %collective-permute-start.10 = (bf16[160,2048]{1,0:T(8,128)(2,1)S(1)}, bf16[160,2048]{1,0:T(8,128)(2,1)S(1)}, u32[]{:S(2)}, u32[]{:S(2)}) collective-permute-start(bf16[160,2048]{1,0:T(8,128)(2,1)S(1)} %get-tuple-element.118.refs_0_.mine_ref), channel_id=1, source_target_pairs={{0,6},{1,7},{6,0},{7,1},{8,14},{9,15},{14,8},{15,9},{16,22},{17,23... | collective-permute-start | bytes 1966088 | tf_op jit(solution)/shard_map/ppermute | solution.py:379
  31.6 5.9 %gate_up.4 = (bf16[2,2,2,40,1792]{4,3,2,1,0:T(8,128)(2,1)S(1)}, bf16[2,2,40,1792]{3,2,1,0:T(8,128)(2,1)S(1)}, bf16[2,2,1,40,1792]{4,3,2,1,0:T(8,128)(2,1)S(1)}, f32[8,128]{1,0:T(8,128)S(1)}) custom-call(bf16[160,2048]{1,0:T(8,128)(2,1)S(1)} %get-tuple-element.118.refs_0_.mine_ref, bf16[160,2048]{1,0:T(8,128)(2,1)S(1)} %get-tuple-element.110.refs_1_, ...), custom_call_target="tpu_custom_call" | custom-call | flops 4697620480 | tf_op jit(solution)/shard_map/gate_up/pallas_call | solution.py:231
  38.1 3.3 %masked.6 = (bf16[1792,2048]{1,0:T(8,128)(2,1)S(1)}, f32[8,128]{1,0:T(8,128)S(1)}) custom-call(s32[1]{0:T(128)} %bitcast.5.core_ref, bf16[1792,8192]{1,0:T(8,128)(2,1)} %weight_ref.7, s32[28,128]{1,0:T(8,128)S(1)} %copy-done, f32[8,128]{1,0:T(8,128)S(1)} %get-tuple-element.119.refs_0_), custom_call_target="tpu_custom_call" | custom-call | tf_op jit(solution)/shard_map/masked/pallas_call | solution.py:106
  41.4 4.2 %collective-permute-done.10.outer_three_ref = bf16[160,2048]{1,0:T(8,128)(2,1)S(1)} collective-permute-done((bf16[160,2048]{1,0:T(8,128)(2,1)S(1)}, bf16[160,2048]{1,0:T(8,128)(2,1)S(1)}, u32[]{:S(2)}, u32[]{:S(2)}) %collective-permute-start.10) | collective-permute-done | bytes 655392 | tf_op jit(solution)/shard_map/ppermute | solution.py:379
  47.0 5.9 %gate_up.5 = (bf16[2,2,2,40,1792]{4,3,2,1,0:T(8,128)(2,1)S(1)}, bf16[2,2,40,1792]{3,2,1,0:T(8,128)(2,1)S(1)}, bf16[2,2,1,40,1792]{4,3,2,1,0:T(8,128)(2,1)S(1)}, f32[8,128]{1,0:T(8,128)S(1)}) custom-call(bf16[160,2048]{1,0:T(8,128)(2,1)S(1)} %get-tuple-element.125.refs_0_, bf16[160,2048]{1,0:T(8,128)(2,1)S(1)} %collective-permute-done.12.refs_1_, ...), custom_call_target="tpu_custom_call" | custom-call | flops 4697620480 | tf_op jit(solution)/shard_map/gate_up/pallas_call | solution.py:231
  53.6 1.5 collective-permute-done.13.refs_1_
  55.0 0.8 collective-permute-done.14.refs_3_.refs_1_
  56.0 1.6 %collective-permute-start.16 = (bf16[2,2,40,1792]{3,2,1,0:T(8,128)(2,1)S(1)}, bf16[2,2,40,1792]{3,2,1,0:T(8,128)(2,1)S(1)}, u32[]{:S(2)}, u32[]{:S(2)}) collective-permute-start(bf16[2,2,40,1792]{3,2,1,0:T(8,128)(2,1)S(1)} %get-tuple-element.134), channel_id=1, source_target_pairs={{0,16},{8,24},{16,0},{24,8},{1,17},{9,25},{17,1},{25,9},{2,18},{10... | collective-permute-start | bytes 1720328 | tf_op jit(solution)/shard_map/ppermute | solution.py:349
  57.6 3.3 %masked.7 = (bf16[1792,2048]{1,0:T(8,128)(2,1)S(1)}, f32[8,128]{1,0:T(8,128)S(1)}) custom-call(s32[1]{0:T(128)} %bitcast.5.core_ref, bf16[1792,8192]{1,0:T(8,128)(2,1)} %weight_ref.7, s32[28,128]{1,0:T(8,128)S(1)} %copy-done, f32[8,128]{1,0:T(8,128)S(1)} %get-tuple-element.131.refs_0_), custom_call_target="tpu_custom_call" | custom-call | tf_op jit(solution)/shard_map/masked/pallas_call | solution.py:106
  60.8 1.6 %collective-permute-start.15 = (bf16[160,2048]{1,0:T(8,128)(2,1)S(1)}, bf16[160,2048]{1,0:T(8,128)(2,1)S(1)}, u32[]{:S(2)}, u32[]{:S(2)}) collective-permute-start(bf16[160,2048]{1,0:T(8,128)(2,1)S(1)} %collective-permute-done.11.refs_5_.refs_0_), channel_id=1, source_target_pairs={{0,1},{1,0},{2,3},{3,2},{4,5},{5,4},{6,7},{7,6},{8,9},{9,8},{10,11... | collective-permute-start | bytes 1966088 | tf_op jit(solution)/shard_map/ppermute | solution.py:349
  62.4 6.0 %gate_up.6 = (bf16[2,2,2,40,1792]{4,3,2,1,0:T(8,128)(2,1)S(1)}, bf16[2,2,40,1792]{3,2,1,0:T(8,128)(2,1)S(1)}, bf16[2,2,1,40,1792]{4,3,2,1,0:T(8,128)(2,1)S(1)}, f32[8,128]{1,0:T(8,128)S(1)}) custom-call(bf16[160,2048]{1,0:T(8,128)(2,1)S(1)} %get-tuple-element.136.refs_0_, bf16[160,2048]{1,0:T(8,128)(2,1)S(1)} %collective-permute-done.17.refs_1_, ...), custom_call_target="tpu_custom_call" | custom-call | flops 4697620480 | tf_op jit(solution)/shard_map/gate_up/pallas_call | solution.py:231
  69.0 2.1 %collective-permute-done.16.refs_2_ = bf16[2,2,40,1792]{3,2,1,0:T(8,128)(2,1)S(1)} collective-permute-done((bf16[2,2,40,1792]{3,2,1,0:T(8,128)(2,1)S(1)}, bf16[2,2,40,1792]{3,2,1,0:T(8,128)(2,1)S(1)}, u32[]{:S(2)}, u32[]{:S(2)}) %collective-permute-start.16) | collective-permute-done | bytes 573472 | tf_op jit(solution)/shard_map/ppermute | solution.py:349
  71.6 1.6 %collective-permute-start.23 = (bf16[2,2,40,1792]{3,2,1,0:T(8,128)(2,1)S(1)}, bf16[2,2,40,1792]{3,2,1,0:T(8,128)(2,1)S(1)}, u32[]{:S(2)}, u32[]{:S(2)}) collective-permute-start(bf16[2,2,40,1792]{3,2,1,0:T(8,128)(2,1)S(1)} %get-tuple-element.150), channel_id=1, source_target_pairs={{0,16},{8,24},{16,0},{24,8},{1,17},{9,25},{17,1},{25,9},{2,18},{10... | collective-permute-start | bytes 1720328 | tf_op jit(solution)/shard_map/ppermute | solution.py:349
  73.2 3.2 %down.4 = (bf16[2,40,4096]{2,1,0:T(8,128)(2,1)S(1)}, bf16[2,40,4096]{2,1,0:T(8,128)(2,1)S(1)}, f32[8,128]{1,0:T(8,128)S(1)}) custom-call(bf16[2,40,1792]{2,1,0:T(8,128)(2,1)S(1)} %get-tuple-element.138.own_ref, bf16[2,40,1792]{2,1,0:T(8,128)(2,1)S(1)} %collective-permute-done.18.other_ref, bf16[1792,2048]{1,0:T(8,128)(2,1)S(1)} %get-tuple-element.139.refs_0_, ...), custom_call_target="tpu_custom_call" | custom-call | flops 2348810 | tf_op jit(solution)/shard_map/down/pallas_call | solution.py:273
  76.5 0.9 collective-permute-done.15.refs_1_
  77.4 1.5 %collective-permute-start.28 = (bf16[2,40,4096]{2,1,0:T(8,128)(2,1)S(1)}, bf16[2,40,4096]{2,1,0:T(8,128)(2,1)S(1)}, u32[]{:S(2)}, u32[]{:S(2)}) collective-permute-start(bf16[2,40,4096]{2,1,0:T(8,128)(2,1)S(1)} %get-tuple-element.162), channel_id=1, source_target_pairs={{0,1},{1,0},{2,3},{3,2},{4,5},{5,4},{6,7},{7,6},{8,9},{9,8},{10,11... | collective-permute-start | bytes 1966088 | tf_op jit(solution)/shard_map/ppermute | solution.py:349
  78.9 5.9 %gate_up.7 = (bf16[2,2,2,40,1792]{4,3,2,1,0:T(8,128)(2,1)S(1)}, bf16[2,2,40,1792]{3,2,1,0:T(8,128)(2,1)S(1)}, bf16[1,2,1,40,1792]{4,3,2,1,0:T(8,128)(2,1)S(1)}, ...) custom-call(bf16[160,2048]{1,0:T(8,128)(2,1)S(1)} %collective-permute-done.11.refs_5_.refs_0_, ...), custom_call_target="tpu_custom_call" | custom-call | flops 4697620480 | tf_op jit(solution)/shard_map/gate_up/pallas_call | solution.py:231
  85.5 1.6 %collective-permute-done.23.refs_2_ = bf16[2,2,40,1792]{3,2,1,0:T(8,128)(2,1)S(1)} collective-permute-done((bf16[2,2,40,1792]{3,2,1,0:T(8,128)(2,1)S(1)}, bf16[2,2,40,1792]{3,2,1,0:T(8,128)(2,1)S(1)}, u32[]{:S(2)}, u32[]{:S(2)}) %collective-permute-start.23) | collective-permute-done | bytes 573472 | tf_op jit(solution)/shard_map/ppermute | solution.py:349
  88.2 1.5 collective-permute-start.24
  89.7 3.5 %down.5 = (bf16[1,40,4096]{2,1,0:T(8,128)(2,1)S(1)}, bf16[1,40,4096]{2,1,0:T(8,128)(2,1)S(1)}, bf16[1,40,4096]{2,1,0:T(8,128)(2,1)S(1)}, bf16[1,40,4096]{2,1,0:T(8,128)(2,1)S(1)}, f32[8,128]{1,0:T(8,128)S(1)}) custom-call(bf16[2,40,1792]{2,1,0:T(8,128)(2,1)S(1)} %get-tuple-element.158.own_ref, bf16[2,40,1792]{2,1,0:T(8,128)(2,1)S(1)} %collective-permute-done.27.other_ref, ...), custom_call_target="tpu_custom_call" | custom-call | flops 2348810 | tf_op jit(solution)/shard_map/down/pallas_call | solution.py:273
  93.4 1.5 %collective-permute-start.29 = (bf16[1,40,4096]{2,1,0:T(8,128)(2,1)S(1)}, bf16[1,40,4096]{2,1,0:T(8,128)(2,1)S(1)}, u32[]{:S(2)}, u32[]{:S(2)}) collective-permute-start(bf16[1,40,4096]{2,1,0:T(8,128)(2,1)S(1)} %get-tuple-element.163), channel_id=1, source_target_pairs={{0,1},{1,0},{2,3},{3,2},{4,5},{5,4},{6,7},{7,6},{8,9},{9,8},{10,11... | collective-permute-start | bytes 983048 | tf_op jit(solution)/shard_map/ppermute | solution.py:349
  95.1 1.7 %collective-permute-start.34 = (bf16[2,40,4096]{2,1,0:T(8,128)(2,1)S(1)}, bf16[2,40,4096]{2,1,0:T(8,128)(2,1)S(1)}, u32[]{:S(2)}, u32[]{:S(2)}) collective-permute-start(bf16[2,40,4096]{2,1,0:T(8,128)(2,1)S(1)} %get-tuple-element.178), channel_id=1, source_target_pairs={{0,2},{1,3},{2,0},{3,1},{4,6},{5,7},{6,4},{7,5},{8,10},{9,11},{10,... | collective-permute-start | bytes 1966088 | tf_op jit(solution)/shard_map/ppermute | solution.py:379
  96.7 5.9 %collective-permute-done.29.refs_1_ = bf16[1,40,4096]{2,1,0:T(8,128)(2,1)S(1)} collective-permute-done((bf16[1,40,4096]{2,1,0:T(8,128)(2,1)S(1)}, bf16[1,40,4096]{2,1,0:T(8,128)(2,1)S(1)}, u32[]{:S(2)}, u32[]{:S(2)}) %collective-permute-start.29) | collective-permute-done | bytes 327712 | tf_op jit(solution)/shard_map/ppermute | solution.py:349
  102.7 1.6 %collective-permute-start.31 = (bf16[1,40,4096]{2,1,0:T(8,128)(2,1)S(1)}, bf16[1,40,4096]{2,1,0:T(8,128)(2,1)S(1)}, u32[]{:S(2)}, u32[]{:S(2)}) collective-permute-start(bf16[1,40,4096]{2,1,0:T(8,128)(2,1)S(1)} %get-tuple-element.174), channel_id=1, source_target_pairs={{0,1},{1,0},{2,3},{3,2},{4,5},{5,4},{6,7},{7,6},{8,9},{9,8},{10,11... | collective-permute-start | bytes 983048 | tf_op jit(solution)/shard_map/ppermute | solution.py:349
  104.7 1.2 collective-permute-start.25
  105.9 1.6 %collective-permute-start.33 = (bf16[1,40,4096]{2,1,0:T(8,128)(2,1)S(1)}, bf16[1,40,4096]{2,1,0:T(8,128)(2,1)S(1)}, u32[]{:S(2)}, u32[]{:S(2)}) collective-permute-start(bf16[1,40,4096]{2,1,0:T(8,128)(2,1)S(1)} %get-tuple-element.173), channel_id=1, source_target_pairs={{0,2},{1,3},{2,0},{3,1},{4,6},{5,7},{6,4},{7,5},{8,10},{9,11},{10,... | collective-permute-start | bytes 983048 | tf_op jit(solution)/shard_map/ppermute | solution.py:379
  107.5 3.2 %down.6 = (bf16[1,40,4096]{2,1,0:T(8,128)(2,1)S(1)}, bf16[1,40,4096]{2,1,0:T(8,128)(2,1)S(1)}, bf16[1,40,4096]{2,1,0:T(8,128)(2,1)S(1)}, bf16[1,40,4096]{2,1,0:T(8,128)(2,1)S(1)}, f32[8,128]{1,0:T(8,128)S(1)}) custom-call(bf16[2,40,1792]{2,1,0:T(8,128)(2,1)S(1)} %get-tuple-element.168.own_ref, bf16[2,40,1792]{2,1,0:T(8,128)(2,1)S(1)} %collective-permute-done.30.other_ref, ...), custom_call_target="tpu_custom_call" | custom-call | flops 2348810 | tf_op jit(solution)/shard_map/down/pallas_call | solution.py:273
  111.1 1.6 %collective-permute-start.32 = (bf16[1,40,4096]{2,1,0:T(8,128)(2,1)S(1)}, bf16[1,40,4096]{2,1,0:T(8,128)(2,1)S(1)}, u32[]{:S(2)}, u32[]{:S(2)}) collective-permute-start(bf16[1,40,4096]{2,1,0:T(8,128)(2,1)S(1)} %get-tuple-element.175), channel_id=1, source_target_pairs={{0,1},{1,0},{2,3},{3,2},{4,5},{5,4},{6,7},{7,6},{8,9},{9,8},{10,11... | collective-permute-start | bytes 983048 | tf_op jit(solution)/shard_map/ppermute | solution.py:349
  112.9 1.7 %collective-permute-start.38 = (bf16[1,40,4096]{2,1,0:T(8,128)(2,1)S(1)}, bf16[1,40,4096]{2,1,0:T(8,128)(2,1)S(1)}, u32[]{:S(2)}, u32[]{:S(2)}) collective-permute-start(bf16[1,40,4096]{2,1,0:T(8,128)(2,1)S(1)} %get-tuple-element.190), channel_id=1, source_target_pairs={{0,2},{1,3},{2,0},{3,1},{4,6},{5,7},{6,4},{7,5},{8,10},{9,11},{10,... | collective-permute-start | bytes 983048 | tf_op jit(solution)/shard_map/ppermute | solution.py:379
  114.5 5.3 %collective-permute-done.33.refs_2_ = bf16[1,40,4096]{2,1,0:T(8,128)(2,1)S(1)} collective-permute-done((bf16[1,40,4096]{2,1,0:T(8,128)(2,1)S(1)}, bf16[1,40,4096]{2,1,0:T(8,128)(2,1)S(1)}, u32[]{:S(2)}, u32[]{:S(2)}) %collective-permute-start.33) | collective-permute-done | bytes 327712 | tf_op jit(solution)/shard_map/ppermute | solution.py:379
  121.2 1.7 %collective-permute-start.40 = (bf16[1,40,4096]{2,1,0:T(8,128)(2,1)S(1)}, bf16[1,40,4096]{2,1,0:T(8,128)(2,1)S(1)}, u32[]{:S(2)}, u32[]{:S(2)}) collective-permute-start(bf16[1,40,4096]{2,1,0:T(8,128)(2,1)S(1)} %get-tuple-element.186), channel_id=1, source_target_pairs={{0,4},{1,5},{4,0},{5,1},{2,6},{3,7},{6,2},{7,3},{8,12},{9,13},{12,... | collective-permute-start | bytes 983048 | tf_op jit(solution)/shard_map/ppermute | solution.py:379
  123.3 1.6 %collective-permute-done.35.other_ref = bf16[2,40,1792]{2,1,0:T(8,128)(2,1)S(1)} collective-permute-done((bf16[2,40,1792]{2,1,0:T(8,128)(2,1)S(1)}, bf16[2,40,1792]{2,1,0:T(8,128)(2,1)S(1)}, u32[]{:S(2)}, u32[]{:S(2)}) %collective-permute-start.35) | collective-permute-done | bytes 286752 | tf_op jit(solution)/shard_map/ppermute | solution.py:349
  124.8 3.2 %down.7 = (bf16[2,40,4096]{2,1,0:T(8,128)(2,1)S(1)}, bf16[2,40,4096]{2,1,0:T(8,128)(2,1)S(1)}, f32[8,128]{1,0:T(8,128)S(1)}) custom-call(bf16[2,40,1792]{2,1,0:T(8,128)(2,1)S(1)} %get-tuple-element.181.own_ref, bf16[2,40,1792]{2,1,0:T(8,128)(2,1)S(1)} %collective-permute-done.35.other_ref, bf16[1792,2048]{1,0:T(8,128)(2,1)S(1)} %get-tuple-element.139.refs_0_, ...), custom_call_target="tpu_custom_call" | custom-call | flops 2348810 | tf_op jit(solution)/shard_map/down/pallas_call | solution.py:273
  128.1 1.4 collective-permute-done.38.refs_1_
  130.1 0.8 collective-permute-start.37
  130.9 15.7 %collective-permute-done.40.refs_0_ = bf16[1,40,4096]{2,1,0:T(8,128)(2,1)S(1)} collective-permute-done((bf16[1,40,4096]{2,1,0:T(8,128)(2,1)S(1)}, bf16[1,40,4096]{2,1,0:T(8,128)(2,1)S(1)}, u32[]{:S(2)}, u32[]{:S(2)}) %collective-permute-start.40) | collective-permute-done | bytes 327712 | tf_op jit(solution)/shard_map/ppermute | solution.py:379
  147.5 3.5 %collective-permute-done.39 = bf16[1,40,4096]{2,1,0:T(8,128)(2,1)S(1)} collective-permute-done((bf16[1,40,4096]{2,1,0:T(8,128)(2,1)S(1)}, bf16[1,40,4096]{2,1,0:T(8,128)(2,1)S(1)}, u32[]{:S(2)}, u32[]{:S(2)}) %collective-permute-start.39) | collective-permute-done | bytes 327712 | tf_op jit(solution)/shard_map/ppermute | solution.py:379
  151.2 0.9 pad_maximum_fusion
  (85 shorter events, 14.5 us)
Async XLA Ops:
  0.0 23.1 %copy-start.2 = (s32[32,28]{1,0:T(8,128)S(1)}, s32[32,28]{1,0:T(8,128)}, u32[]{:S(2)}) copy-start(s32[32,28]{1,0:T(8,128)} %mask_ref.5) | copy-start | bytes 10756
  1.6 1.8 %collective-permute-start = (bf16[2,40,2048]{2,1,0:T(8,128)(2,1)S(1)}, bf16[2,40,2048]{2,1,0:T(8,128)(2,1)S(1)}, u32[]{:S(2)}, u32[]{:S(2)}) collective-permute-start(bf16[2,40,2048]{2,1,0:T(8,128)(2,1)S(1)} %pad_maximum_fusion.1), channel_id=1, source_target_pairs={{0,8},{8,0},{16,24},{24,16},{1,9},{9,1},{17,25},{25,17},{2,10},{10... | collective-permute-start | bytes 983048 | tf_op jit(solution)/shard_map/ppermute | solution.py:349
  4.1 10.9 %collective-permute-start.1 = (bf16[2,1,40,2048]{3,2,1,0:T(8,128)(2,1)S(1)}, bf16[2,1,40,2048]{3,2,1,0:T(8,128)(2,1)S(1)}, u32[]{:S(2)}, u32[]{:S(2)}) collective-permute-start(bf16[2,1,40,2048]{3,2,1,0:T(8,128)(2,1)S(1)} %get-tuple-element.101.refs_2_), channel_id=1, source_target_pairs={{0,16},{8,24},{16,0},{24,8},{1,17},{9,25},{17,1},{25,9},{2,18},{10... | collective-permute-start | bytes 983048 | tf_op jit(solution)/shard_map/ppermute | solution.py:349
  6.9 10.5 %collective-permute-start.6 = (bf16[2,1,40,2048]{3,2,1,0:T(8,128)(2,1)S(1)}, bf16[2,1,40,2048]{3,2,1,0:T(8,128)(2,1)S(1)}, u32[]{:S(2)}, u32[]{:S(2)}) collective-permute-start(bf16[2,1,40,2048]{3,2,1,0:T(8,128)(2,1)S(1)} %get-tuple-element.102.refs_0_), channel_id=1, source_target_pairs={{0,2},{1,3},{2,0},{3,1},{4,6},{5,7},{6,4},{7,5},{8,10},{9,11},{10,... | collective-permute-start | bytes 983048 | tf_op jit(solution)/shard_map/ppermute | solution.py:379
  8.6 17.7 %collective-permute-start.4 = (bf16[2,1,40,2048]{3,2,1,0:T(8,128)(2,1)S(1)}, bf16[2,1,40,2048]{3,2,1,0:T(8,128)(2,1)S(1)}, u32[]{:S(2)}, u32[]{:S(2)}) collective-permute-start(bf16[2,1,40,2048]{3,2,1,0:T(8,128)(2,1)S(1)} %get-tuple-element.102.refs_0_), channel_id=1, source_target_pairs={{2,4},{3,5},{4,2},{5,3},{10,12},{11,13},{12,10},{13,11},{18,20},{1... | collective-permute-start | bytes 983048 | tf_op jit(solution)/shard_map/ppermute | solution.py:379
  9.3 17.1 %collective-permute-start.2 = (bf16[2,1,40,2048]{3,2,1,0:T(8,128)(2,1)S(1)}, bf16[2,1,40,2048]{3,2,1,0:T(8,128)(2,1)S(1)}, u32[]{:S(2)}, u32[]{:S(2)}) collective-permute-start(bf16[2,1,40,2048]{3,2,1,0:T(8,128)(2,1)S(1)} %get-tuple-element.102.refs_0_), channel_id=1, source_target_pairs={{0,1},{1,0},{2,3},{3,2},{4,5},{5,4},{6,7},{7,6},{8,9},{9,8},{10,11... | collective-permute-start | bytes 983048 | tf_op jit(solution)/shard_map/ppermute | solution.py:349
  14.9 11.4 %collective-permute-start.7 = (bf16[2,1,40,2048]{3,2,1,0:T(8,128)(2,1)S(1)}, bf16[2,1,40,2048]{3,2,1,0:T(8,128)(2,1)S(1)}, u32[]{:S(2)}, u32[]{:S(2)}) collective-permute-start(bf16[2,1,40,2048]{3,2,1,0:T(8,128)(2,1)S(1)} %collective-permute-done.1.refs_1_), channel_id=1, source_target_pairs={{0,2},{1,3},{2,0},{3,1},{4,6},{5,7},{6,4},{7,5},{8,10},{9,11},{10,... | collective-permute-start | bytes 983048 | tf_op jit(solution)/shard_map/ppermute | solution.py:379
  16.8 9.7 %collective-permute-start.5 = (bf16[2,1,40,2048]{3,2,1,0:T(8,128)(2,1)S(1)}, bf16[2,1,40,2048]{3,2,1,0:T(8,128)(2,1)S(1)}, u32[]{:S(2)}, u32[]{:S(2)}) collective-permute-start(bf16[2,1,40,2048]{3,2,1,0:T(8,128)(2,1)S(1)} %collective-permute-done.1.refs_1_), channel_id=1, source_target_pairs={{2,4},{3,5},{4,2},{5,3},{10,12},{11,13},{12,10},{13,11},{18,20},{1... | collective-permute-start | bytes 983048 | tf_op jit(solution)/shard_map/ppermute | solution.py:379
  17.4 13.5 %collective-permute-start.3 = (bf16[2,1,40,2048]{3,2,1,0:T(8,128)(2,1)S(1)}, bf16[2,1,40,2048]{3,2,1,0:T(8,128)(2,1)S(1)}, u32[]{:S(2)}, u32[]{:S(2)}) collective-permute-start(bf16[2,1,40,2048]{3,2,1,0:T(8,128)(2,1)S(1)} %collective-permute-done.1.refs_1_), channel_id=1, source_target_pairs={{0,1},{1,0},{2,3},{3,2},{4,5},{5,4},{6,7},{7,6},{8,9},{9,8},{10,11... | collective-permute-start | bytes 983048 | tf_op jit(solution)/shard_map/ppermute | solution.py:349
  19.0 0.7 copy-start.1
  26.5 19.1 %collective-permute-start.10 = (bf16[160,2048]{1,0:T(8,128)(2,1)S(1)}, bf16[160,2048]{1,0:T(8,128)(2,1)S(1)}, u32[]{:S(2)}, u32[]{:S(2)}) collective-permute-start(bf16[160,2048]{1,0:T(8,128)(2,1)S(1)} %get-tuple-element.118.refs_0_.mine_ref), channel_id=1, source_target_pairs={{0,6},{1,7},{6,0},{7,1},{8,14},{9,15},{14,8},{15,9},{16,22},{17,23... | collective-permute-start | bytes 1966088 | tf_op jit(solution)/shard_map/ppermute | solution.py:379
  31.0 15.1 %collective-permute-start.12 = (bf16[160,2048]{1,0:T(8,128)(2,1)S(1)}, bf16[160,2048]{1,0:T(8,128)(2,1)S(1)}, u32[]{:S(2)}, u32[]{:S(2)}) collective-permute-start(bf16[160,2048]{1,0:T(8,128)(2,1)S(1)} %get-tuple-element.125.refs_0_), channel_id=1, source_target_pairs={{0,1},{1,0},{2,3},{3,2},{4,5},{5,4},{6,7},{7,6},{8,9},{9,8},{10,11... | collective-permute-start | bytes 1966088 | tf_op jit(solution)/shard_map/ppermute | solution.py:349
  31.6 6.5 %copy-start = (s32[28,128]{1,0:T(8,128)S(1)}, s32[28,128]{1,0:T(8,128)}, u32[]{:S(2)}) copy-start(s32[28,128]{1,0:T(8,128)} %mask_ref.7) | copy-start | bytes 43012
  37.6 8.1 %collective-permute-start.8 = (bf16[2,2,40,1792]{3,2,1,0:T(8,128)(2,1)S(1)}, bf16[2,2,40,1792]{3,2,1,0:T(8,128)(2,1)S(1)}, u32[]{:S(2)}, u32[]{:S(2)}) collective-permute-start(bf16[2,2,40,1792]{3,2,1,0:T(8,128)(2,1)S(1)} %get-tuple-element.115), channel_id=1, source_target_pairs={{0,8},{8,0},{16,24},{24,16},{1,9},{9,1},{17,25},{25,17},{2,10},{10... | collective-permute-start | bytes 1720328 | tf_op jit(solution)/shard_map/ppermute | solution.py:349
  37.6 8.0 %collective-permute-start.9 = (bf16[2,2,1,40,1792]{4,3,2,1,0:T(8,128)(2,1)S(1)}, bf16[2,2,1,40,1792]{4,3,2,1,0:T(8,128)(2,1)S(1)}, u32[]{:S(2)}, u32[]{:S(2)}) collective-permute-start(bf16[2,2,1,40,1792]{4,3,2,1,0:T(8,128)(2,1)S(1)} %get-tuple-element.116), channel_id=1, source_target_pairs={{0,8},{8,0},{16,24},{24,16},{1,9},{9,1},{17,25},{25,17},{2,10},{10... | collective-permute-start | bytes 1720328 | tf_op jit(solution)/shard_map/ppermute | solution.py:349
  46.2 16.3 %collective-permute-start.17 = (bf16[160,2048]{1,0:T(8,128)(2,1)S(1)}, bf16[160,2048]{1,0:T(8,128)(2,1)S(1)}, u32[]{:S(2)}, u32[]{:S(2)}) collective-permute-start(bf16[160,2048]{1,0:T(8,128)(2,1)S(1)} %get-tuple-element.136.refs_0_), channel_id=1, source_target_pairs={{0,1},{1,0},{2,3},{3,2},{4,5},{5,4},{6,7},{7,6},{8,9},{9,8},{10,11... | collective-permute-start | bytes 1966088 | tf_op jit(solution)/shard_map/ppermute | solution.py:349
  46.7 14.2 %collective-permute-start.11 = (bf16[160,2048]{1,0:T(8,128)(2,1)S(1)}, bf16[160,2048]{1,0:T(8,128)(2,1)S(1)}, u32[]{:S(2)}, u32[]{:S(2)}) collective-permute-start(bf16[160,2048]{1,0:T(8,128)(2,1)S(1)} %get-tuple-element.123), channel_id=1, source_target_pairs={{0,4},{1,5},{4,6},{5,7},{6,2},{7,3},{2,0},{3,1},{8,12},{9,13},{12,... | collective-permute-start | bytes 1966088 | tf_op jit(solution)/shard_map/ppermute | solution.py:379
  53.0 2.0 %collective-permute-start.13 = (bf16[2,2,1,40,1792]{4,3,2,1,0:T(8,128)(2,1)S(1)}, bf16[2,2,1,40,1792]{4,3,2,1,0:T(8,128)(2,1)S(1)}, u32[]{:S(2)}, u32[]{:S(2)}) collective-permute-start(bf16[2,2,1,40,1792]{4,3,2,1,0:T(8,128)(2,1)S(1)} %get-tuple-element.128), channel_id=1, source_target_pairs={{0,8},{8,0},{16,24},{24,16},{1,9},{9,1},{17,25},{25,17},{2,10},{10... | collective-permute-start | bytes 1720328 | tf_op jit(solution)/shard_map/ppermute | solution.py:349
  53.1 2.8 %collective-permute-start.14 = (bf16[2,2,40,1792]{3,2,1,0:T(8,128)(2,1)S(1)}, bf16[2,2,40,1792]{3,2,1,0:T(8,128)(2,1)S(1)}, u32[]{:S(2)}, u32[]{:S(2)}) collective-permute-start(bf16[2,2,40,1792]{3,2,1,0:T(8,128)(2,1)S(1)} %get-tuple-element.130), channel_id=1, source_target_pairs={{0,8},{8,0},{16,24},{24,16},{1,9},{9,1},{17,25},{25,17},{2,10},{10... | collective-permute-start | bytes 1720328 | tf_op jit(solution)/shard_map/ppermute | solution.py:349
  56.0 15.1 %collective-permute-start.16 = (bf16[2,2,40,1792]{3,2,1,0:T(8,128)(2,1)S(1)}, bf16[2,2,40,1792]{3,2,1,0:T(8,128)(2,1)S(1)}, u32[]{:S(2)}, u32[]{:S(2)}) collective-permute-start(bf16[2,2,40,1792]{3,2,1,0:T(8,128)(2,1)S(1)} %get-tuple-element.134), channel_id=1, source_target_pairs={{0,16},{8,24},{16,0},{24,8},{1,17},{9,25},{17,1},{25,9},{2,18},{10... | collective-permute-start | bytes 1720328 | tf_op jit(solution)/shard_map/ppermute | solution.py:349
  60.8 16.6 %collective-permute-start.15 = (bf16[160,2048]{1,0:T(8,128)(2,1)S(1)}, bf16[160,2048]{1,0:T(8,128)(2,1)S(1)}, u32[]{:S(2)}, u32[]{:S(2)}) collective-permute-start(bf16[160,2048]{1,0:T(8,128)(2,1)S(1)} %collective-permute-done.11.refs_5_.refs_0_), channel_id=1, source_target_pairs={{0,1},{1,0},{2,3},{3,2},{4,5},{5,4},{6,7},{7,6},{8,9},{9,8},{10,11... | collective-permute-start | bytes 1966088 | tf_op jit(solution)/shard_map/ppermute | solution.py:349
  68.4 3.1 %collective-permute-start.19 = (bf16[2,2,1,40,1792]{4,3,2,1,0:T(8,128)(2,1)S(1)}, bf16[2,2,1,40,1792]{4,3,2,1,0:T(8,128)(2,1)S(1)}, u32[]{:S(2)}, u32[]{:S(2)}) collective-permute-start(bf16[2,2,1,40,1792]{4,3,2,1,0:T(8,128)(2,1)S(1)} %get-tuple-element.142), channel_id=1, source_target_pairs={{0,8},{8,0},{16,24},{24,16},{1,9},{9,1},{17,25},{25,17},{2,10},{10... | collective-permute-start | bytes 1720328 | tf_op jit(solution)/shard_map/ppermute | solution.py:349
  68.5 3.0 %collective-permute-start.20 = (bf16[2,2,40,1792]{3,2,1,0:T(8,128)(2,1)S(1)}, bf16[2,2,40,1792]{3,2,1,0:T(8,128)(2,1)S(1)}, u32[]{:S(2)}, u32[]{:S(2)}) collective-permute-start(bf16[2,2,40,1792]{3,2,1,0:T(8,128)(2,1)S(1)} %get-tuple-element.144), channel_id=1, source_target_pairs={{0,8},{8,0},{16,24},{24,16},{1,9},{9,1},{17,25},{25,17},{2,10},{10... | collective-permute-start | bytes 1720328 | tf_op jit(solution)/shard_map/ppermute | solution.py:349
  71.4 1.8 %collective-permute-start.18 = (bf16[2,40,1792]{2,1,0:T(8,128)(2,1)S(1)}, bf16[2,40,1792]{2,1,0:T(8,128)(2,1)S(1)}, u32[]{:S(2)}, u32[]{:S(2)}) collective-permute-start(bf16[2,40,1792]{2,1,0:T(8,128)(2,1)S(1)} %get-tuple-element.138.own_ref), channel_id=1, source_target_pairs={{0,8},{8,0},{16,24},{24,16},{1,9},{9,1},{17,25},{25,17},{2,10},{10... | collective-permute-start | bytes 860168 | tf_op jit(solution)/shard_map/ppermute | solution.py:349
  71.6 15.4 %collective-permute-start.23 = (bf16[2,2,40,1792]{3,2,1,0:T(8,128)(2,1)S(1)}, bf16[2,2,40,1792]{3,2,1,0:T(8,128)(2,1)S(1)}, u32[]{:S(2)}, u32[]{:S(2)}) collective-permute-start(bf16[2,2,40,1792]{3,2,1,0:T(8,128)(2,1)S(1)} %get-tuple-element.150), channel_id=1, source_target_pairs={{0,16},{8,24},{16,0},{24,8},{1,17},{9,25},{17,1},{25,9},{2,18},{10... | collective-permute-start | bytes 1720328 | tf_op jit(solution)/shard_map/ppermute | solution.py:349
  77.4 16.0 %collective-permute-start.28 = (bf16[2,40,4096]{2,1,0:T(8,128)(2,1)S(1)}, bf16[2,40,4096]{2,1,0:T(8,128)(2,1)S(1)}, u32[]{:S(2)}, u32[]{:S(2)}) collective-permute-start(bf16[2,40,4096]{2,1,0:T(8,128)(2,1)S(1)} %get-tuple-element.162), channel_id=1, source_target_pairs={{0,1},{1,0},{2,3},{3,2},{4,5},{5,4},{6,7},{7,6},{8,9},{9,8},{10,11... | collective-permute-start | bytes 1966088 | tf_op jit(solution)/shard_map/ppermute | solution.py:349
  84.9 2.6 %collective-permute-start.21 = (bf16[1,2,1,40,1792]{4,3,2,1,0:T(8,128)(2,1)S(1)}, bf16[1,2,1,40,1792]{4,3,2,1,0:T(8,128)(2,1)S(1)}, u32[]{:S(2)}, u32[]{:S(2)}) collective-permute-start(bf16[1,2,1,40,1792]{4,3,2,1,0:T(8,128)(2,1)S(1)} %get-tuple-element.148), channel_id=1, source_target_pairs={{0,8},{8,0},{16,24},{24,16},{1,9},{9,1},{17,25},{25,17},{2,10},{10... | collective-permute-start | bytes 860168 | tf_op jit(solution)/shard_map/ppermute | solution.py:349
  85.0 2.5 %collective-permute-start.22 = (bf16[1,2,1,40,1792]{4,3,2,1,0:T(8,128)(2,1)S(1)}, bf16[1,2,1,40,1792]{4,3,2,1,0:T(8,128)(2,1)S(1)}, u32[]{:S(2)}, u32[]{:S(2)}) collective-permute-start(bf16[1,2,1,40,1792]{4,3,2,1,0:T(8,128)(2,1)S(1)} %get-tuple-element.149), channel_id=1, source_target_pairs={{0,8},{8,0},{16,24},{24,16},{1,9},{9,1},{17,25},{25,17},{2,10},{10... | collective-permute-start | bytes 860168 | tf_op jit(solution)/shard_map/ppermute | solution.py:349
  87.4 2.3 %collective-permute-start.27 = (bf16[2,40,1792]{2,1,0:T(8,128)(2,1)S(1)}, bf16[2,40,1792]{2,1,0:T(8,128)(2,1)S(1)}, u32[]{:S(2)}, u32[]{:S(2)}) collective-permute-start(bf16[2,40,1792]{2,1,0:T(8,128)(2,1)S(1)} %get-tuple-element.158.own_ref), channel_id=1, source_target_pairs={{0,8},{8,0},{16,24},{24,16},{1,9},{9,1},{17,25},{25,17},{2,10},{10... | collective-permute-start | bytes 860168 | tf_op jit(solution)/shard_map/ppermute | solution.py:349
  87.6 16.7 %collective-permute-start.26 = (bf16[2,2,40,1792]{3,2,1,0:T(8,128)(2,1)S(1)}, bf16[2,2,40,1792]{3,2,1,0:T(8,128)(2,1)S(1)}, u32[]{:S(2)}, u32[]{:S(2)}) collective-permute-start(bf16[2,2,40,1792]{3,2,1,0:T(8,128)(2,1)S(1)} %get-tuple-element.157), channel_id=1, source_target_pairs={{0,8},{8,0},{16,24},{24,16},{1,9},{9,1},{17,25},{25,17},{2,10},{10... | collective-permute-start | bytes 1720328 | tf_op jit(solution)/shard_map/ppermute | solution.py:349
  88.2 16.1 %collective-permute-start.24 = (bf16[2,2,40,1792]{3,2,1,0:T(8,128)(2,1)S(1)}, bf16[2,2,40,1792]{3,2,1,0:T(8,128)(2,1)S(1)}, u32[]{:S(2)}, u32[]{:S(2)}) collective-permute-start(bf16[2,2,40,1792]{3,2,1,0:T(8,128)(2,1)S(1)} %get-tuple-element.153), channel_id=1, source_target_pairs={{0,16},{8,24},{16,0},{24,8},{1,17},{9,25},{17,1},{25,9},{2,18},{10... | collective-permute-start | bytes 1720328 | tf_op jit(solution)/shard_map/ppermute | solution.py:349
  93.4 9.2 %collective-permute-start.29 = (bf16[1,40,4096]{2,1,0:T(8,128)(2,1)S(1)}, bf16[1,40,4096]{2,1,0:T(8,128)(2,1)S(1)}, u32[]{:S(2)}, u32[]{:S(2)}) collective-permute-start(bf16[1,40,4096]{2,1,0:T(8,128)(2,1)S(1)} %get-tuple-element.163), channel_id=1, source_target_pairs={{0,1},{1,0},{2,3},{3,2},{4,5},{5,4},{6,7},{7,6},{8,9},{9,8},{10,11... | collective-permute-start | bytes 983048 | tf_op jit(solution)/shard_map/ppermute | solution.py:349
  95.1 17.7 %collective-permute-start.34 = (bf16[2,40,4096]{2,1,0:T(8,128)(2,1)S(1)}, bf16[2,40,4096]{2,1,0:T(8,128)(2,1)S(1)}, u32[]{:S(2)}, u32[]{:S(2)}) collective-permute-start(bf16[2,40,4096]{2,1,0:T(8,128)(2,1)S(1)} %get-tuple-element.178), channel_id=1, source_target_pairs={{0,2},{1,3},{2,0},{3,1},{4,6},{5,7},{6,4},{7,5},{8,10},{9,11},{10,... | collective-permute-start | bytes 1966088 | tf_op jit(solution)/shard_map/ppermute | solution.py:379
  102.7 8.4 %collective-permute-start.31 = (bf16[1,40,4096]{2,1,0:T(8,128)(2,1)S(1)}, bf16[1,40,4096]{2,1,0:T(8,128)(2,1)S(1)}, u32[]{:S(2)}, u32[]{:S(2)}) collective-permute-start(bf16[1,40,4096]{2,1,0:T(8,128)(2,1)S(1)} %get-tuple-element.174), channel_id=1, source_target_pairs={{0,1},{1,0},{2,3},{3,2},{4,5},{5,4},{6,7},{7,6},{8,9},{9,8},{10,11... | collective-permute-start | bytes 983048 | tf_op jit(solution)/shard_map/ppermute | solution.py:349
  104.6 2.9 %collective-permute-start.30 = (bf16[2,40,1792]{2,1,0:T(8,128)(2,1)S(1)}, bf16[2,40,1792]{2,1,0:T(8,128)(2,1)S(1)}, u32[]{:S(2)}, u32[]{:S(2)}) collective-permute-start(bf16[2,40,1792]{2,1,0:T(8,128)(2,1)S(1)} %get-tuple-element.168.own_ref), channel_id=1, source_target_pairs={{0,8},{8,0},{16,24},{24,16},{1,9},{9,1},{17,25},{25,17},{2,10},{10... | collective-permute-start | bytes 860168 | tf_op jit(solution)/shard_map/ppermute | solution.py:349
  104.7 18.2 %collective-permute-start.25 = (bf16[2,2,40,1792]{3,2,1,0:T(8,128)(2,1)S(1)}, bf16[2,2,40,1792]{3,2,1,0:T(8,128)(2,1)S(1)}, u32[]{:S(2)}, u32[]{:S(2)}) collective-permute-start(bf16[2,2,40,1792]{3,2,1,0:T(8,128)(2,1)S(1)} %get-tuple-element.154), channel_id=1, source_target_pairs={{0,16},{8,24},{16,0},{24,8},{1,17},{9,25},{17,1},{25,9},{2,18},{10... | collective-permute-start | bytes 1720328 | tf_op jit(solution)/shard_map/ppermute | solution.py:349
  105.9 13.9 %collective-permute-start.33 = (bf16[1,40,4096]{2,1,0:T(8,128)(2,1)S(1)}, bf16[1,40,4096]{2,1,0:T(8,128)(2,1)S(1)}, u32[]{:S(2)}, u32[]{:S(2)}) collective-permute-start(bf16[1,40,4096]{2,1,0:T(8,128)(2,1)S(1)} %get-tuple-element.173), channel_id=1, source_target_pairs={{0,2},{1,3},{2,0},{3,1},{4,6},{5,7},{6,4},{7,5},{8,10},{9,11},{10,... | collective-permute-start | bytes 983048 | tf_op jit(solution)/shard_map/ppermute | solution.py:379
  111.1 9.2 %collective-permute-start.32 = (bf16[1,40,4096]{2,1,0:T(8,128)(2,1)S(1)}, bf16[1,40,4096]{2,1,0:T(8,128)(2,1)S(1)}, u32[]{:S(2)}, u32[]{:S(2)}) collective-permute-start(bf16[1,40,4096]{2,1,0:T(8,128)(2,1)S(1)} %get-tuple-element.175), channel_id=1, source_target_pairs={{0,1},{1,0},{2,3},{3,2},{4,5},{5,4},{6,7},{7,6},{8,9},{9,8},{10,11... | collective-permute-start | bytes 983048 | tf_op jit(solution)/shard_map/ppermute | solution.py:349
  112.9 16.6 %collective-permute-start.38 = (bf16[1,40,4096]{2,1,0:T(8,128)(2,1)S(1)}, bf16[1,40,4096]{2,1,0:T(8,128)(2,1)S(1)}, u32[]{:S(2)}, u32[]{:S(2)}) collective-permute-start(bf16[1,40,4096]{2,1,0:T(8,128)(2,1)S(1)} %get-tuple-element.190), channel_id=1, source_target_pairs={{0,2},{1,3},{2,0},{3,1},{4,6},{5,7},{6,4},{7,5},{8,10},{9,11},{10,... | collective-permute-start | bytes 983048 | tf_op jit(solution)/shard_map/ppermute | solution.py:379
  120.5 9.0 %collective-permute-start.36 = (bf16[1,40,4096]{2,1,0:T(8,128)(2,1)S(1)}, bf16[1,40,4096]{2,1,0:T(8,128)(2,1)S(1)}, u32[]{:S(2)}, u32[]{:S(2)}) collective-permute-start(bf16[1,40,4096]{2,1,0:T(8,128)(2,1)S(1)} %get-tuple-element.187), channel_id=1, source_target_pairs={{0,1},{1,0},{2,3},{3,2},{4,5},{5,4},{6,7},{7,6},{8,9},{9,8},{10,11... | collective-permute-start | bytes 983048 | tf_op jit(solution)/shard_map/ppermute | solution.py:349
  121.2 25.4 %collective-permute-start.40 = (bf16[1,40,4096]{2,1,0:T(8,128)(2,1)S(1)}, bf16[1,40,4096]{2,1,0:T(8,128)(2,1)S(1)}, u32[]{:S(2)}, u32[]{:S(2)}) collective-permute-start(bf16[1,40,4096]{2,1,0:T(8,128)(2,1)S(1)} %get-tuple-element.186), channel_id=1, source_target_pairs={{0,4},{1,5},{4,0},{5,1},{2,6},{3,7},{6,2},{7,3},{8,12},{9,13},{12,... | collective-permute-start | bytes 983048 | tf_op jit(solution)/shard_map/ppermute | solution.py:379
  123.2 1.6 %collective-permute-start.35 = (bf16[2,40,1792]{2,1,0:T(8,128)(2,1)S(1)}, bf16[2,40,1792]{2,1,0:T(8,128)(2,1)S(1)}, u32[]{:S(2)}, u32[]{:S(2)}) collective-permute-start(bf16[2,40,1792]{2,1,0:T(8,128)(2,1)S(1)} %get-tuple-element.181.own_ref), channel_id=1, source_target_pairs={{0,8},{8,0},{16,24},{24,16},{1,9},{9,1},{17,25},{25,17},{2,10},{10... | collective-permute-start | bytes 860168 | tf_op jit(solution)/shard_map/ppermute | solution.py:349
  129.6 21.3 %collective-permute-start.39 = (bf16[1,40,4096]{2,1,0:T(8,128)(2,1)S(1)}, bf16[1,40,4096]{2,1,0:T(8,128)(2,1)S(1)}, u32[]{:S(2)}, u32[]{:S(2)}) collective-permute-start(bf16[1,40,4096]{2,1,0:T(8,128)(2,1)S(1)} %get-tuple-element.194), channel_id=1, source_target_pairs={{0,4},{1,5},{4,0},{5,1},{2,6},{3,7},{6,2},{7,3},{8,12},{9,13},{12,... | collective-permute-start | bytes 983048 | tf_op jit(solution)/shard_map/ppermute | solution.py:379
  130.1 17.1 %collective-permute-start.37 = (bf16[2,40,4096]{2,1,0:T(8,128)(2,1)S(1)}, bf16[2,40,4096]{2,1,0:T(8,128)(2,1)S(1)}, u32[]{:S(2)}, u32[]{:S(2)}) collective-permute-start(bf16[2,40,4096]{2,1,0:T(8,128)(2,1)S(1)} %get-tuple-element.188), channel_id=1, source_target_pairs={{0,1},{1,0},{2,3},{3,2},{4,5},{5,4},{6,7},{7,6},{8,9},{9,8},{10,11... | collective-permute-start | bytes 1966088 | tf_op jit(solution)/shard_map/ppermute | solution.py:349
  147.4 3.5 %collective-permute-start.41 = (bf16[40,4096]{1,0:T(8,128)(2,1)S(1)}, bf16[40,4096]{1,0:T(8,128)(2,1)S(1)}, u32[]{:S(2)}, u32[]{:S(2)}) collective-permute-start(bf16[40,4096]{1,0:T(8,128)(2,1)S(1)} %fusion.1), channel_id=1, source_target_pairs={{0,8},{8,0},{16,24},{24,16},{1,9},{9,1},{17,25},{25,17},{2,10},{10... | collective-permute-start | bytes 983048 | tf_op jit(solution)/shard_map/ppermute | solution.py:349

commit v23 on v22

--- a/solution.py
+++ b/solution.py
@@ -208,7 +208,7 @@
     for place, part in enumerate(parts):
         all_rows[pl.ds(place * half, half), :] = part[:half, :]
         all_rows[pl.ds(kept + place * half, half), :] = part[half:, :]
-    tile = tile_of(gate_ref.shape[1], 896)
+    tile = tile_of(gate_ref.shape[1], 1792)
 
     @pl.loop(0, gate_ref.shape[1] // tile)
     def _(number):
@@ -250,7 +250,7 @@
     both[rows:, :] = other_ref[...].astype(F32).reshape(rows, depth).astype(BF16)
     for number, weight_ref in enumerate(weight_refs):
         width = weight_ref.shape[1]
-        down_columns(pieces, both, weight_ref, partial_refs, number * width, tile_of(width, 1024))
+        down_columns(pieces, both, weight_ref, partial_refs, number * width, tile_of(width, 2048))
 
 
 def down_columns(pieces, both, weight_ref, partial_refs, first, tile):

time: 152 us -> 151 us (level)
  Pallas kernels: 55.4 us -> 49.1 us
  waiting for transfers between devices: 51.4 us -> 55.5 us
    pallas_call x4, Pallas kernels: 23.8 us -> 20.2 us  [gate_up(): pl.pallas_call(functools.partial(gate_up_kernel, len(parts), len(after)),...]
    pallas_call x4, Pallas kernels: 13.2 us -> 10.6 us  [down(): pl.pallas_call(functools.partial(down_kernel, pieces, len(down_kept), len...]
    ppermute x11, waiting for transfers between devices: 30.1 us -> 32.7 us  [by_plane(): return lax.ppermute(behind(values, after), 'cols', pairs)]
  transfers between devices with their start and end apart: 42 -> 42, of which waited for: 19 -> 19; matrix products, arithmetic and copies ran while one was open for 0% -> 0% of each run, Pallas kernels for 35% -> 31%
where the time goes in v23:
time: 151 us; the launch traced here: 150 us
  waiting for transfers between devices  55.5 us (37%)
  Pallas kernels  49.1 us (33%)
  starting transfers between devices  43.3 us (29%)
    ppermute x11, waiting for transfers between devices, by_plane(): return lax.ppermute(behind(values, after), 'cols', pairs)  32.7 us
    ppermute x31, starting transfers between devices, swap(): lax.ppermute(values, axis, [(place, place ^ step) for place in range(size)])  26.1 us
    ppermute x31, waiting for transfers between devices, swap(): lax.ppermute(values, axis, [(place, place ^ step) for place in range(size)])  22.8 us
    pallas_call x4, Pallas kernels, gate_up(): pl.pallas_call(functools.partial(gate_up_kernel, len(parts), len(after)),...  20.2 us
    ppermute x11, starting transfers between devices, by_plane(): return lax.ppermute(behind(values, after), 'cols', pairs)  17.2 us
    pallas_call x4, Pallas kernels, masked(): pl.pallas_call(functools.partial(mask_kernel, share, rows, len(after)), i...  13 us
    pallas_call x4, Pallas kernels, down(): pl.pallas_call(functools.partial(down_kernel, pieces, len(down_kept), len...  10.6 us
  transfers between devices with their start and end apart: 42, of which 19 were waited for; matrix products, arithmetic and copies ran while one was open for 0% of the time, Pallas kernels for 31%

profile of v23, /device:TPU:0, one launch (start us, length us, event | category | flops | bytes accessed | tf_op | source)
XLA Modules:
  0.0 150.5 jit_solution(2456418913630983845)
XLA Ops:
  0.0 1.5 %normed.1 = bf16[40,8192]{1,0:T(8,128)(2,1)S(1)} custom-call(bf16[40,8192]{1,0:T(8,128)(2,1)} %rows_hbm.1, f32[8192]{0:T(1024)} %gain_hbm.1), custom_call_target="tpu_custom_call" | custom-call | tf_op jit(solution)/shard_map/normed/pallas_call | solution.py:61
  2.2 1.3 collective-permute-done
  4.1 2.9 %collective-permute-start.1 = (bf16[2,1,40,2048]{3,2,1,0:T(8,128)(2,1)S(1)}, bf16[2,1,40,2048]{3,2,1,0:T(8,128)(2,1)S(1)}, u32[]{:S(2)}, u32[]{:S(2)}) collective-permute-start(bf16[2,1,40,2048]{3,2,1,0:T(8,128)(2,1)S(1)} %get-tuple-element.101.refs_2_), channel_id=1, source_target_pairs={{0,16},{8,24},{16,0},{24,8},{1,17},{9,25},{17,1},{25,9},{2,18},{10... | collective-permute-start | bytes 983048 | tf_op jit(solution)/shard_map/ppermute | solution.py:349
  6.9 1.6 %collective-permute-start.6 = (bf16[2,1,40,2048]{3,2,1,0:T(8,128)(2,1)S(1)}, bf16[2,1,40,2048]{3,2,1,0:T(8,128)(2,1)S(1)}, u32[]{:S(2)}, u32[]{:S(2)}) collective-permute-start(bf16[2,1,40,2048]{3,2,1,0:T(8,128)(2,1)S(1)} %get-tuple-element.102.refs_0_), channel_id=1, source_target_pairs={{0,2},{1,3},{2,0},{3,1},{4,6},{5,7},{6,4},{7,5},{8,10},{9,11},{10,... | collective-permute-start | bytes 983048 | tf_op jit(solution)/shard_map/ppermute | solution.py:379
  9.3 1.6 %collective-permute-start.2 = (bf16[2,1,40,2048]{3,2,1,0:T(8,128)(2,1)S(1)}, bf16[2,1,40,2048]{3,2,1,0:T(8,128)(2,1)S(1)}, u32[]{:S(2)}, u32[]{:S(2)}) collective-permute-start(bf16[2,1,40,2048]{3,2,1,0:T(8,128)(2,1)S(1)} %get-tuple-element.102.refs_0_), channel_id=1, source_target_pairs={{0,1},{1,0},{2,3},{3,2},{4,5},{5,4},{6,7},{7,6},{8,9},{9,8},{10,11... | collective-permute-start | bytes 983048 | tf_op jit(solution)/shard_map/ppermute | solution.py:349
  10.8 4.1 %collective-permute-done.1.refs_1_ = bf16[2,1,40,2048]{3,2,1,0:T(8,128)(2,1)S(1)} collective-permute-done((bf16[2,1,40,2048]{3,2,1,0:T(8,128)(2,1)S(1)}, bf16[2,1,40,2048]{3,2,1,0:T(8,128)(2,1)S(1)}, u32[]{:S(2)}, u32[]{:S(2)}) %collective-permute-start.1) | collective-permute-done | bytes 327712 | tf_op jit(solution)/shard_map/ppermute | solution.py:349
  14.9 1.8 %collective-permute-start.7 = (bf16[2,1,40,2048]{3,2,1,0:T(8,128)(2,1)S(1)}, bf16[2,1,40,2048]{3,2,1,0:T(8,128)(2,1)S(1)}, u32[]{:S(2)}, u32[]{:S(2)}) collective-permute-start(bf16[2,1,40,2048]{3,2,1,0:T(8,128)(2,1)S(1)} %collective-permute-done.1.refs_1_), channel_id=1, source_target_pairs={{0,2},{1,3},{2,0},{3,1},{4,6},{5,7},{6,4},{7,5},{8,10},{9,11},{10,... | collective-permute-start | bytes 983048 | tf_op jit(solution)/shard_map/ppermute | solution.py:379
  17.4 1.6 %collective-permute-start.3 = (bf16[2,1,40,2048]{3,2,1,0:T(8,128)(2,1)S(1)}, bf16[2,1,40,2048]{3,2,1,0:T(8,128)(2,1)S(1)}, u32[]{:S(2)}, u32[]{:S(2)}) collective-permute-start(bf16[2,1,40,2048]{3,2,1,0:T(8,128)(2,1)S(1)} %collective-permute-done.1.refs_1_), channel_id=1, source_target_pairs={{0,1},{1,0},{2,3},{3,2},{4,5},{5,4},{6,7},{7,6},{8,9},{9,8},{10,11... | collective-permute-start | bytes 983048 | tf_op jit(solution)/shard_map/ppermute | solution.py:349
  19.7 3.2 %masked.4 = (bf16[2048,1792]{1,0:T(8,128)(2,1)S(1)}, f32[8,128]{1,0:T(8,128)S(1)}) custom-call(s32[1]{0:T(128)} %bitcast.5.core_ref, bf16[2048,1792]{1,0:T(8,128)(2,1)} %weight_ref.4, s32[32,28]{1,0:T(8,128)S(1)} %copy-done.1, f32[8,128]{1,0:T(8,128)S(1)} %get-tuple-element.103.refs_0_), custom_call_target="tpu_custom_call" | custom-call | tf_op jit(solution)/shard_map/masked/pallas_call | solution.py:106
  23.1 3.2 %masked.5 = (bf16[2048,1792]{1,0:T(8,128)(2,1)S(1)}, f32[8,128]{1,0:T(8,128)S(1)}) custom-call(s32[1]{0:T(128)} %bitcast.5.core_ref, bf16[2048,1792]{1,0:T(8,128)(2,1)} %weight_ref.5, s32[32,28]{1,0:T(8,128)S(1)} %copy-done.2, f32[8,128]{1,0:T(8,128)S(1)} %get-tuple-element.106.refs_0_, bf16[2,1,40,2048]{3,2,1,0:T(8,128)(2,1)S(1)} %collective-permute-done.6.refs_1_.refs_0_), custom_call_target="tpu_custom_call" | custom-call | flops 172500000 | tf_op jit(solution)/shard_map/masked/pallas_call | solution.py:106
  26.5 4.5 %collective-permute-start.10 = (bf16[160,2048]{1,0:T(8,128)(2,1)S(1)}, bf16[160,2048]{1,0:T(8,128)(2,1)S(1)}, u32[]{:S(2)}, u32[]{:S(2)}) collective-permute-start(bf16[160,2048]{1,0:T(8,128)(2,1)S(1)} %get-tuple-element.118.refs_0_.mine_ref), channel_id=1, source_target_pairs={{0,6},{1,7},{6,0},{7,1},{8,14},{9,15},{14,8},{15,9},{16,22},{17,23... | collective-permute-start | bytes 1966088 | tf_op jit(solution)/shard_map/ppermute | solution.py:379
  31.6 5.0 %gate_up.4 = (bf16[2,2,2,40,1792]{4,3,2,1,0:T(8,128)(2,1)S(1)}, bf16[2,2,40,1792]{3,2,1,0:T(8,128)(2,1)S(1)}, bf16[2,2,1,40,1792]{4,3,2,1,0:T(8,128)(2,1)S(1)}, f32[8,128]{1,0:T(8,128)S(1)}) custom-call(bf16[160,2048]{1,0:T(8,128)(2,1)S(1)} %get-tuple-element.118.refs_0_.mine_ref, bf16[160,2048]{1,0:T(8,128)(2,1)S(1)} %get-tuple-element.110.refs_1_, ...), custom_call_target="tpu_custom_call" | custom-call | flops 4697620480 | tf_op jit(solution)/shard_map/gate_up/pallas_call | solution.py:231
  37.2 3.3 %masked.6 = (bf16[1792,2048]{1,0:T(8,128)(2,1)S(1)}, f32[8,128]{1,0:T(8,128)S(1)}) custom-call(s32[1]{0:T(128)} %bitcast.5.core_ref, bf16[1792,8192]{1,0:T(8,128)(2,1)} %weight_ref.7, s32[28,128]{1,0:T(8,128)S(1)} %copy-done, f32[8,128]{1,0:T(8,128)S(1)} %get-tuple-element.119.refs_0_), custom_call_target="tpu_custom_call" | custom-call | tf_op jit(solution)/shard_map/masked/pallas_call | solution.py:106
  40.4 5.1 %collective-permute-done.10.outer_three_ref = bf16[160,2048]{1,0:T(8,128)(2,1)S(1)} collective-permute-done((bf16[160,2048]{1,0:T(8,128)(2,1)S(1)}, bf16[160,2048]{1,0:T(8,128)(2,1)S(1)}, u32[]{:S(2)}, u32[]{:S(2)}) %collective-permute-start.10) | collective-permute-done | bytes 655392 | tf_op jit(solution)/shard_map/ppermute | solution.py:379
  47.0 5.0 %gate_up.5 = (bf16[2,2,2,40,1792]{4,3,2,1,0:T(8,128)(2,1)S(1)}, bf16[2,2,40,1792]{3,2,1,0:T(8,128)(2,1)S(1)}, bf16[2,2,1,40,1792]{4,3,2,1,0:T(8,128)(2,1)S(1)}, f32[8,128]{1,0:T(8,128)S(1)}) custom-call(bf16[160,2048]{1,0:T(8,128)(2,1)S(1)} %get-tuple-element.125.refs_0_, bf16[160,2048]{1,0:T(8,128)(2,1)S(1)} %collective-permute-done.12.refs_1_, ...), custom_call_target="tpu_custom_call" | custom-call | flops 4697620480 | tf_op jit(solution)/shard_map/gate_up/pallas_call | solution.py:231
  52.6 1.5 collective-permute-done.13.refs_1_
  55.0 1.6 %collective-permute-start.16 = (bf16[2,2,40,1792]{3,2,1,0:T(8,128)(2,1)S(1)}, bf16[2,2,40,1792]{3,2,1,0:T(8,128)(2,1)S(1)}, u32[]{:S(2)}, u32[]{:S(2)}) collective-permute-start(bf16[2,2,40,1792]{3,2,1,0:T(8,128)(2,1)S(1)} %get-tuple-element.134), channel_id=1, source_target_pairs={{0,16},{8,24},{16,0},{24,8},{1,17},{9,25},{17,1},{25,9},{2,18},{10... | collective-permute-start | bytes 1720328 | tf_op jit(solution)/shard_map/ppermute | solution.py:349
  56.6 3.3 %masked.7 = (bf16[1792,2048]{1,0:T(8,128)(2,1)S(1)}, f32[8,128]{1,0:T(8,128)S(1)}) custom-call(s32[1]{0:T(128)} %bitcast.5.core_ref, bf16[1792,8192]{1,0:T(8,128)(2,1)} %weight_ref.7, s32[28,128]{1,0:T(8,128)S(1)} %copy-done, f32[8,128]{1,0:T(8,128)S(1)} %get-tuple-element.131.refs_0_), custom_call_target="tpu_custom_call" | custom-call | tf_op jit(solution)/shard_map/masked/pallas_call | solution.py:106
  60.6 1.5 collective-permute-start.15
  62.1 5.0 %gate_up.6 = (bf16[2,2,2,40,1792]{4,3,2,1,0:T(8,128)(2,1)S(1)}, bf16[2,2,40,1792]{3,2,1,0:T(8,128)(2,1)S(1)}, bf16[2,2,1,40,1792]{4,3,2,1,0:T(8,128)(2,1)S(1)}, f32[8,128]{1,0:T(8,128)S(1)}) custom-call(bf16[160,2048]{1,0:T(8,128)(2,1)S(1)} %get-tuple-element.136.refs_0_, bf16[160,2048]{1,0:T(8,128)(2,1)S(1)} %collective-permute-done.17.refs_1_, ...), custom_call_target="tpu_custom_call" | custom-call | flops 4697620480 | tf_op jit(solution)/shard_map/gate_up/pallas_call | solution.py:231
  67.7 2.5 %collective-permute-done.16.refs_2_ = bf16[2,2,40,1792]{3,2,1,0:T(8,128)(2,1)S(1)} collective-permute-done((bf16[2,2,40,1792]{3,2,1,0:T(8,128)(2,1)S(1)}, bf16[2,2,40,1792]{3,2,1,0:T(8,128)(2,1)S(1)}, u32[]{:S(2)}, u32[]{:S(2)}) %collective-permute-start.16) | collective-permute-done | bytes 573472 | tf_op jit(solution)/shard_map/ppermute | solution.py:349
  70.7 1.6 %collective-permute-start.23 = (bf16[2,2,40,1792]{3,2,1,0:T(8,128)(2,1)S(1)}, bf16[2,2,40,1792]{3,2,1,0:T(8,128)(2,1)S(1)}, u32[]{:S(2)}, u32[]{:S(2)}) collective-permute-start(bf16[2,2,40,1792]{3,2,1,0:T(8,128)(2,1)S(1)} %get-tuple-element.150), channel_id=1, source_target_pairs={{0,16},{8,24},{16,0},{24,8},{1,17},{9,25},{17,1},{25,9},{2,18},{10... | collective-permute-start | bytes 1720328 | tf_op jit(solution)/shard_map/ppermute | solution.py:349
  72.2 2.6 %down.4 = (bf16[2,40,4096]{2,1,0:T(8,128)(2,1)S(1)}, bf16[2,40,4096]{2,1,0:T(8,128)(2,1)S(1)}, f32[8,128]{1,0:T(8,128)S(1)}) custom-call(bf16[2,40,1792]{2,1,0:T(8,128)(2,1)S(1)} %get-tuple-element.138.own_ref, bf16[2,40,1792]{2,1,0:T(8,128)(2,1)S(1)} %collective-permute-done.18.other_ref, bf16[1792,2048]{1,0:T(8,128)(2,1)S(1)} %get-tuple-element.139.refs_0_, ...), custom_call_target="tpu_custom_call" | custom-call | flops 2348810 | tf_op jit(solution)/shard_map/down/pallas_call | solution.py:273
  74.9 1.6 %collective-permute-done.15.refs_1_ = bf16[160,2048]{1,0:T(8,128)(2,1)S(1)} collective-permute-done((bf16[160,2048]{1,0:T(8,128)(2,1)S(1)}, bf16[160,2048]{1,0:T(8,128)(2,1)S(1)}, u32[]{:S(2)}, u32[]{:S(2)}) %collective-permute-start.15) | collective-permute-done | bytes 655392 | tf_op jit(solution)/shard_map/ppermute | solution.py:349
  76.4 1.5 %collective-permute-start.28 = (bf16[2,40,4096]{2,1,0:T(8,128)(2,1)S(1)}, bf16[2,40,4096]{2,1,0:T(8,128)(2,1)S(1)}, u32[]{:S(2)}, u32[]{:S(2)}) collective-permute-start(bf16[2,40,4096]{2,1,0:T(8,128)(2,1)S(1)} %get-tuple-element.162), channel_id=1, source_target_pairs={{0,1},{1,0},{2,3},{3,2},{4,5},{5,4},{6,7},{7,6},{8,9},{9,8},{10,11... | collective-permute-start | bytes 1966088 | tf_op jit(solution)/shard_map/ppermute | solution.py:349
  77.9 5.2 %gate_up.7 = (bf16[2,2,2,40,1792]{4,3,2,1,0:T(8,128)(2,1)S(1)}, bf16[2,2,40,1792]{3,2,1,0:T(8,128)(2,1)S(1)}, bf16[1,2,1,40,1792]{4,3,2,1,0:T(8,128)(2,1)S(1)}, ...) custom-call(bf16[160,2048]{1,0:T(8,128)(2,1)S(1)} %collective-permute-done.11.refs_5_.refs_0_, ...), custom_call_target="tpu_custom_call" | custom-call | flops 4697620480 | tf_op jit(solution)/shard_map/gate_up/pallas_call | solution.py:231
  83.7 2.3 %collective-permute-done.23.refs_2_ = bf16[2,2,40,1792]{3,2,1,0:T(8,128)(2,1)S(1)} collective-permute-done((bf16[2,2,40,1792]{3,2,1,0:T(8,128)(2,1)S(1)}, bf16[2,2,40,1792]{3,2,1,0:T(8,128)(2,1)S(1)}, u32[]{:S(2)}, u32[]{:S(2)}) %collective-permute-start.23) | collective-permute-done | bytes 573472 | tf_op jit(solution)/shard_map/ppermute | solution.py:349
  87.2 1.5 collective-permute-start.24
  88.7 2.6 %down.5 = (bf16[1,40,4096]{2,1,0:T(8,128)(2,1)S(1)}, bf16[1,40,4096]{2,1,0:T(8,128)(2,1)S(1)}, bf16[1,40,4096]{2,1,0:T(8,128)(2,1)S(1)}, bf16[1,40,4096]{2,1,0:T(8,128)(2,1)S(1)}, f32[8,128]{1,0:T(8,128)S(1)}) custom-call(bf16[2,40,1792]{2,1,0:T(8,128)(2,1)S(1)} %get-tuple-element.158.own_ref, bf16[2,40,1792]{2,1,0:T(8,128)(2,1)S(1)} %collective-permute-done.27.other_ref, ...), custom_call_target="tpu_custom_call" | custom-call | flops 2348810 | tf_op jit(solution)/shard_map/down/pallas_call | solution.py:273
  91.8 1.5 %collective-permute-start.29 = (bf16[1,40,4096]{2,1,0:T(8,128)(2,1)S(1)}, bf16[1,40,4096]{2,1,0:T(8,128)(2,1)S(1)}, u32[]{:S(2)}, u32[]{:S(2)}) collective-permute-start(bf16[1,40,4096]{2,1,0:T(8,128)(2,1)S(1)} %get-tuple-element.163), channel_id=1, source_target_pairs={{0,1},{1,0},{2,3},{3,2},{4,5},{5,4},{6,7},{7,6},{8,9},{9,8},{10,11... | collective-permute-start | bytes 983048 | tf_op jit(solution)/shard_map/ppermute | solution.py:349
  93.5 1.7 %collective-permute-start.34 = (bf16[2,40,4096]{2,1,0:T(8,128)(2,1)S(1)}, bf16[2,40,4096]{2,1,0:T(8,128)(2,1)S(1)}, u32[]{:S(2)}, u32[]{:S(2)}) collective-permute-start(bf16[2,40,4096]{2,1,0:T(8,128)(2,1)S(1)} %get-tuple-element.178), channel_id=1, source_target_pairs={{0,2},{1,3},{2,0},{3,1},{4,6},{5,7},{6,4},{7,5},{8,10},{9,11},{10,... | collective-permute-start | bytes 1966088 | tf_op jit(solution)/shard_map/ppermute | solution.py:379
  95.1 5.7 %collective-permute-done.29.refs_1_ = bf16[1,40,4096]{2,1,0:T(8,128)(2,1)S(1)} collective-permute-done((bf16[1,40,4096]{2,1,0:T(8,128)(2,1)S(1)}, bf16[1,40,4096]{2,1,0:T(8,128)(2,1)S(1)}, u32[]{:S(2)}, u32[]{:S(2)}) %collective-permute-start.29) | collective-permute-done | bytes 327712 | tf_op jit(solution)/shard_map/ppermute | solution.py:349
  100.9 1.6 %collective-permute-start.31 = (bf16[1,40,4096]{2,1,0:T(8,128)(2,1)S(1)}, bf16[1,40,4096]{2,1,0:T(8,128)(2,1)S(1)}, u32[]{:S(2)}, u32[]{:S(2)}) collective-permute-start(bf16[1,40,4096]{2,1,0:T(8,128)(2,1)S(1)} %get-tuple-element.174), channel_id=1, source_target_pairs={{0,1},{1,0},{2,3},{3,2},{4,5},{5,4},{6,7},{7,6},{8,9},{9,8},{10,11... | collective-permute-start | bytes 983048 | tf_op jit(solution)/shard_map/ppermute | solution.py:349
  102.8 1.2 collective-permute-start.25
  104.1 1.6 %collective-permute-start.33 = (bf16[1,40,4096]{2,1,0:T(8,128)(2,1)S(1)}, bf16[1,40,4096]{2,1,0:T(8,128)(2,1)S(1)}, u32[]{:S(2)}, u32[]{:S(2)}) collective-permute-start(bf16[1,40,4096]{2,1,0:T(8,128)(2,1)S(1)} %get-tuple-element.173), channel_id=1, source_target_pairs={{0,2},{1,3},{2,0},{3,1},{4,6},{5,7},{6,4},{7,5},{8,10},{9,11},{10,... | collective-permute-start | bytes 983048 | tf_op jit(solution)/shard_map/ppermute | solution.py:379
  105.7 2.7 %down.6 = (bf16[1,40,4096]{2,1,0:T(8,128)(2,1)S(1)}, bf16[1,40,4096]{2,1,0:T(8,128)(2,1)S(1)}, bf16[1,40,4096]{2,1,0:T(8,128)(2,1)S(1)}, bf16[1,40,4096]{2,1,0:T(8,128)(2,1)S(1)}, f32[8,128]{1,0:T(8,128)S(1)}) custom-call(bf16[2,40,1792]{2,1,0:T(8,128)(2,1)S(1)} %get-tuple-element.168.own_ref, bf16[2,40,1792]{2,1,0:T(8,128)(2,1)S(1)} %collective-permute-done.30.other_ref, ...), custom_call_target="tpu_custom_call" | custom-call | flops 2348810 | tf_op jit(solution)/shard_map/down/pallas_call | solution.py:273
  109.0 1.5 %collective-permute-start.32 = (bf16[1,40,4096]{2,1,0:T(8,128)(2,1)S(1)}, bf16[1,40,4096]{2,1,0:T(8,128)(2,1)S(1)}, u32[]{:S(2)}, u32[]{:S(2)}) collective-permute-start(bf16[1,40,4096]{2,1,0:T(8,128)(2,1)S(1)} %get-tuple-element.175), channel_id=1, source_target_pairs={{0,1},{1,0},{2,3},{3,2},{4,5},{5,4},{6,7},{7,6},{8,9},{9,8},{10,11... | collective-permute-start | bytes 983048 | tf_op jit(solution)/shard_map/ppermute | solution.py:349
  111.3 1.7 %collective-permute-start.38 = (bf16[1,40,4096]{2,1,0:T(8,128)(2,1)S(1)}, bf16[1,40,4096]{2,1,0:T(8,128)(2,1)S(1)}, u32[]{:S(2)}, u32[]{:S(2)}) collective-permute-start(bf16[1,40,4096]{2,1,0:T(8,128)(2,1)S(1)} %get-tuple-element.190), channel_id=1, source_target_pairs={{0,2},{1,3},{2,0},{3,1},{4,6},{5,7},{6,4},{7,5},{8,10},{9,11},{10,... | collective-permute-start | bytes 983048 | tf_op jit(solution)/shard_map/ppermute | solution.py:379
  112.9 5.3 %collective-permute-done.33.refs_2_ = bf16[1,40,4096]{2,1,0:T(8,128)(2,1)S(1)} collective-permute-done((bf16[1,40,4096]{2,1,0:T(8,128)(2,1)S(1)}, bf16[1,40,4096]{2,1,0:T(8,128)(2,1)S(1)}, u32[]{:S(2)}, u32[]{:S(2)}) %collective-permute-start.33) | collective-permute-done | bytes 327712 | tf_op jit(solution)/shard_map/ppermute | solution.py:379
  118.4 1.3 collective-permute-start.36
  119.7 1.6 %collective-permute-start.40 = (bf16[1,40,4096]{2,1,0:T(8,128)(2,1)S(1)}, bf16[1,40,4096]{2,1,0:T(8,128)(2,1)S(1)}, u32[]{:S(2)}, u32[]{:S(2)}) collective-permute-start(bf16[1,40,4096]{2,1,0:T(8,128)(2,1)S(1)} %get-tuple-element.186), channel_id=1, source_target_pairs={{0,4},{1,5},{4,0},{5,1},{2,6},{3,7},{6,2},{7,3},{8,12},{9,13},{12,... | collective-permute-start | bytes 983048 | tf_op jit(solution)/shard_map/ppermute | solution.py:379
  121.6 1.6 %collective-permute-done.35.other_ref = bf16[2,40,1792]{2,1,0:T(8,128)(2,1)S(1)} collective-permute-done((bf16[2,40,1792]{2,1,0:T(8,128)(2,1)S(1)}, bf16[2,40,1792]{2,1,0:T(8,128)(2,1)S(1)}, u32[]{:S(2)}, u32[]{:S(2)}) %collective-permute-start.35) | collective-permute-done | bytes 286752 | tf_op jit(solution)/shard_map/ppermute | solution.py:349
  123.2 2.7 %down.7 = (bf16[2,40,4096]{2,1,0:T(8,128)(2,1)S(1)}, bf16[2,40,4096]{2,1,0:T(8,128)(2,1)S(1)}, f32[8,128]{1,0:T(8,128)S(1)}) custom-call(bf16[2,40,1792]{2,1,0:T(8,128)(2,1)S(1)} %get-tuple-element.181.own_ref, bf16[2,40,1792]{2,1,0:T(8,128)(2,1)S(1)} %collective-permute-done.35.other_ref, bf16[1792,2048]{1,0:T(8,128)(2,1)S(1)} %get-tuple-element.139.refs_0_, ...), custom_call_target="tpu_custom_call" | custom-call | flops 2348810 | tf_op jit(solution)/shard_map/down/pallas_call | solution.py:273
  125.9 1.3 collective-permute-done.38.refs_1_
  127.3 1.0 collective-permute-start.39
  128.8 15.8 %collective-permute-done.40.refs_0_ = bf16[1,40,4096]{2,1,0:T(8,128)(2,1)S(1)} collective-permute-done((bf16[1,40,4096]{2,1,0:T(8,128)(2,1)S(1)}, bf16[1,40,4096]{2,1,0:T(8,128)(2,1)S(1)}, u32[]{:S(2)}, u32[]{:S(2)}) %collective-permute-start.40) | collective-permute-done | bytes 327712 | tf_op jit(solution)/shard_map/ppermute | solution.py:379
  145.5 3.8 %collective-permute-done.39 = bf16[1,40,4096]{2,1,0:T(8,128)(2,1)S(1)} collective-permute-done((bf16[1,40,4096]{2,1,0:T(8,128)(2,1)S(1)}, bf16[1,40,4096]{2,1,0:T(8,128)(2,1)S(1)}, u32[]{:S(2)}, u32[]{:S(2)}) %collective-permute-start.39) | collective-permute-done | bytes 327712 | tf_op jit(solution)/shard_map/ppermute | solution.py:379
  149.6 0.9 pad_maximum_fusion
  (85 shorter events, 15.9 us)
Async XLA Ops:
  0.0 23.1 %copy-start.2 = (s32[32,28]{1,0:T(8,128)S(1)}, s32[32,28]{1,0:T(8,128)}, u32[]{:S(2)}) copy-start(s32[32,28]{1,0:T(8,128)} %mask_ref.5) | copy-start | bytes 10756
  1.6 1.8 %collective-permute-start = (bf16[2,40,2048]{2,1,0:T(8,128)(2,1)S(1)}, bf16[2,40,2048]{2,1,0:T(8,128)(2,1)S(1)}, u32[]{:S(2)}, u32[]{:S(2)}) collective-permute-start(bf16[2,40,2048]{2,1,0:T(8,128)(2,1)S(1)} %pad_maximum_fusion.1), channel_id=1, source_target_pairs={{0,8},{8,0},{16,24},{24,16},{1,9},{9,1},{17,25},{25,17},{2,10},{10... | collective-permute-start | bytes 983048 | tf_op jit(solution)/shard_map/ppermute | solution.py:349
  4.1 10.9 %collective-permute-start.1 = (bf16[2,1,40,2048]{3,2,1,0:T(8,128)(2,1)S(1)}, bf16[2,1,40,2048]{3,2,1,0:T(8,128)(2,1)S(1)}, u32[]{:S(2)}, u32[]{:S(2)}) collective-permute-start(bf16[2,1,40,2048]{3,2,1,0:T(8,128)(2,1)S(1)} %get-tuple-element.101.refs_2_), channel_id=1, source_target_pairs={{0,16},{8,24},{16,0},{24,8},{1,17},{9,25},{17,1},{25,9},{2,18},{10... | collective-permute-start | bytes 983048 | tf_op jit(solution)/shard_map/ppermute | solution.py:349
  6.9 10.5 %collective-permute-start.6 = (bf16[2,1,40,2048]{3,2,1,0:T(8,128)(2,1)S(1)}, bf16[2,1,40,2048]{3,2,1,0:T(8,128)(2,1)S(1)}, u32[]{:S(2)}, u32[]{:S(2)}) collective-permute-start(bf16[2,1,40,2048]{3,2,1,0:T(8,128)(2,1)S(1)} %get-tuple-element.102.refs_0_), channel_id=1, source_target_pairs={{0,2},{1,3},{2,0},{3,1},{4,6},{5,7},{6,4},{7,5},{8,10},{9,11},{10,... | collective-permute-start | bytes 983048 | tf_op jit(solution)/shard_map/ppermute | solution.py:379
  8.6 17.7 %collective-permute-start.4 = (bf16[2,1,40,2048]{3,2,1,0:T(8,128)(2,1)S(1)}, bf16[2,1,40,2048]{3,2,1,0:T(8,128)(2,1)S(1)}, u32[]{:S(2)}, u32[]{:S(2)}) collective-permute-start(bf16[2,1,40,2048]{3,2,1,0:T(8,128)(2,1)S(1)} %get-tuple-element.102.refs_0_), channel_id=1, source_target_pairs={{2,4},{3,5},{4,2},{5,3},{10,12},{11,13},{12,10},{13,11},{18,20},{1... | collective-permute-start | bytes 983048 | tf_op jit(solution)/shard_map/ppermute | solution.py:379
  9.3 17.1 %collective-permute-start.2 = (bf16[2,1,40,2048]{3,2,1,0:T(8,128)(2,1)S(1)}, bf16[2,1,40,2048]{3,2,1,0:T(8,128)(2,1)S(1)}, u32[]{:S(2)}, u32[]{:S(2)}) collective-permute-start(bf16[2,1,40,2048]{3,2,1,0:T(8,128)(2,1)S(1)} %get-tuple-element.102.refs_0_), channel_id=1, source_target_pairs={{0,1},{1,0},{2,3},{3,2},{4,5},{5,4},{6,7},{7,6},{8,9},{9,8},{10,11... | collective-permute-start | bytes 983048 | tf_op jit(solution)/shard_map/ppermute | solution.py:349
  14.9 11.4 %collective-permute-start.7 = (bf16[2,1,40,2048]{3,2,1,0:T(8,128)(2,1)S(1)}, bf16[2,1,40,2048]{3,2,1,0:T(8,128)(2,1)S(1)}, u32[]{:S(2)}, u32[]{:S(2)}) collective-permute-start(bf16[2,1,40,2048]{3,2,1,0:T(8,128)(2,1)S(1)} %collective-permute-done.1.refs_1_), channel_id=1, source_target_pairs={{0,2},{1,3},{2,0},{3,1},{4,6},{5,7},{6,4},{7,5},{8,10},{9,11},{10,... | collective-permute-start | bytes 983048 | tf_op jit(solution)/shard_map/ppermute | solution.py:379
  16.8 9.7 %collective-permute-start.5 = (bf16[2,1,40,2048]{3,2,1,0:T(8,128)(2,1)S(1)}, bf16[2,1,40,2048]{3,2,1,0:T(8,128)(2,1)S(1)}, u32[]{:S(2)}, u32[]{:S(2)}) collective-permute-start(bf16[2,1,40,2048]{3,2,1,0:T(8,128)(2,1)S(1)} %collective-permute-done.1.refs_1_), channel_id=1, source_target_pairs={{2,4},{3,5},{4,2},{5,3},{10,12},{11,13},{12,10},{13,11},{18,20},{1... | collective-permute-start | bytes 983048 | tf_op jit(solution)/shard_map/ppermute | solution.py:379
  17.4 13.5 %collective-permute-start.3 = (bf16[2,1,40,2048]{3,2,1,0:T(8,128)(2,1)S(1)}, bf16[2,1,40,2048]{3,2,1,0:T(8,128)(2,1)S(1)}, u32[]{:S(2)}, u32[]{:S(2)}) collective-permute-start(bf16[2,1,40,2048]{3,2,1,0:T(8,128)(2,1)S(1)} %collective-permute-done.1.refs_1_), channel_id=1, source_target_pairs={{0,1},{1,0},{2,3},{3,2},{4,5},{5,4},{6,7},{7,6},{8,9},{9,8},{10,11... | collective-permute-start | bytes 983048 | tf_op jit(solution)/shard_map/ppermute | solution.py:349
  19.0 0.7 copy-start.1
  26.5 19.1 %collective-permute-start.10 = (bf16[160,2048]{1,0:T(8,128)(2,1)S(1)}, bf16[160,2048]{1,0:T(8,128)(2,1)S(1)}, u32[]{:S(2)}, u32[]{:S(2)}) collective-permute-start(bf16[160,2048]{1,0:T(8,128)(2,1)S(1)} %get-tuple-element.118.refs_0_.mine_ref), channel_id=1, source_target_pairs={{0,6},{1,7},{6,0},{7,1},{8,14},{9,15},{14,8},{15,9},{16,22},{17,23... | collective-permute-start | bytes 1966088 | tf_op jit(solution)/shard_map/ppermute | solution.py:379
  31.0 15.1 %collective-permute-start.12 = (bf16[160,2048]{1,0:T(8,128)(2,1)S(1)}, bf16[160,2048]{1,0:T(8,128)(2,1)S(1)}, u32[]{:S(2)}, u32[]{:S(2)}) collective-permute-start(bf16[160,2048]{1,0:T(8,128)(2,1)S(1)} %get-tuple-element.125.refs_0_), channel_id=1, source_target_pairs={{0,1},{1,0},{2,3},{3,2},{4,5},{5,4},{6,7},{7,6},{8,9},{9,8},{10,11... | collective-permute-start | bytes 1966088 | tf_op jit(solution)/shard_map/ppermute | solution.py:349
  31.6 5.6 %copy-start = (s32[28,128]{1,0:T(8,128)S(1)}, s32[28,128]{1,0:T(8,128)}, u32[]{:S(2)}) copy-start(s32[28,128]{1,0:T(8,128)} %mask_ref.7) | copy-start | bytes 43012
  36.6 9.0 %collective-permute-start.8 = (bf16[2,2,40,1792]{3,2,1,0:T(8,128)(2,1)S(1)}, bf16[2,2,40,1792]{3,2,1,0:T(8,128)(2,1)S(1)}, u32[]{:S(2)}, u32[]{:S(2)}) collective-permute-start(bf16[2,2,40,1792]{3,2,1,0:T(8,128)(2,1)S(1)} %get-tuple-element.115), channel_id=1, source_target_pairs={{0,8},{8,0},{16,24},{24,16},{1,9},{9,1},{17,25},{25,17},{2,10},{10... | collective-permute-start | bytes 1720328 | tf_op jit(solution)/shard_map/ppermute | solution.py:349
  36.7 9.0 %collective-permute-start.9 = (bf16[2,2,1,40,1792]{4,3,2,1,0:T(8,128)(2,1)S(1)}, bf16[2,2,1,40,1792]{4,3,2,1,0:T(8,128)(2,1)S(1)}, u32[]{:S(2)}, u32[]{:S(2)}) collective-permute-start(bf16[2,2,1,40,1792]{4,3,2,1,0:T(8,128)(2,1)S(1)} %get-tuple-element.116), channel_id=1, source_target_pairs={{0,8},{8,0},{16,24},{24,16},{1,9},{9,1},{17,25},{25,17},{2,10},{10... | collective-permute-start | bytes 1720328 | tf_op jit(solution)/shard_map/ppermute | solution.py:349
  46.2 15.9 %collective-permute-start.17 = (bf16[160,2048]{1,0:T(8,128)(2,1)S(1)}, bf16[160,2048]{1,0:T(8,128)(2,1)S(1)}, u32[]{:S(2)}, u32[]{:S(2)}) collective-permute-start(bf16[160,2048]{1,0:T(8,128)(2,1)S(1)} %get-tuple-element.136.refs_0_), channel_id=1, source_target_pairs={{0,1},{1,0},{2,3},{3,2},{4,5},{5,4},{6,7},{7,6},{8,9},{9,8},{10,11... | collective-permute-start | bytes 1966088 | tf_op jit(solution)/shard_map/ppermute | solution.py:349
  46.7 13.9 %collective-permute-start.11 = (bf16[160,2048]{1,0:T(8,128)(2,1)S(1)}, bf16[160,2048]{1,0:T(8,128)(2,1)S(1)}, u32[]{:S(2)}, u32[]{:S(2)}) collective-permute-start(bf16[160,2048]{1,0:T(8,128)(2,1)S(1)} %get-tuple-element.123), channel_id=1, source_target_pairs={{0,4},{1,5},{4,6},{5,7},{6,2},{7,3},{2,0},{3,1},{8,12},{9,13},{12,... | collective-permute-start | bytes 1966088 | tf_op jit(solution)/shard_map/ppermute | solution.py:379
  52.0 2.0 %collective-permute-start.13 = (bf16[2,2,1,40,1792]{4,3,2,1,0:T(8,128)(2,1)S(1)}, bf16[2,2,1,40,1792]{4,3,2,1,0:T(8,128)(2,1)S(1)}, u32[]{:S(2)}, u32[]{:S(2)}) collective-permute-start(bf16[2,2,1,40,1792]{4,3,2,1,0:T(8,128)(2,1)S(1)} %get-tuple-element.128), channel_id=1, source_target_pairs={{0,8},{8,0},{16,24},{24,16},{1,9},{9,1},{17,25},{25,17},{2,10},{10... | collective-permute-start | bytes 1720328 | tf_op jit(solution)/shard_map/ppermute | solution.py:349
  52.1 2.8 %collective-permute-start.14 = (bf16[2,2,40,1792]{3,2,1,0:T(8,128)(2,1)S(1)}, bf16[2,2,40,1792]{3,2,1,0:T(8,128)(2,1)S(1)}, u32[]{:S(2)}, u32[]{:S(2)}) collective-permute-start(bf16[2,2,40,1792]{3,2,1,0:T(8,128)(2,1)S(1)} %get-tuple-element.130), channel_id=1, source_target_pairs={{0,8},{8,0},{16,24},{24,16},{1,9},{9,1},{17,25},{25,17},{2,10},{10... | collective-permute-start | bytes 1720328 | tf_op jit(solution)/shard_map/ppermute | solution.py:349
  55.0 15.1 %collective-permute-start.16 = (bf16[2,2,40,1792]{3,2,1,0:T(8,128)(2,1)S(1)}, bf16[2,2,40,1792]{3,2,1,0:T(8,128)(2,1)S(1)}, u32[]{:S(2)}, u32[]{:S(2)}) collective-permute-start(bf16[2,2,40,1792]{3,2,1,0:T(8,128)(2,1)S(1)} %get-tuple-element.134), channel_id=1, source_target_pairs={{0,16},{8,24},{16,0},{24,8},{1,17},{9,25},{17,1},{25,9},{2,18},{10... | collective-permute-start | bytes 1720328 | tf_op jit(solution)/shard_map/ppermute | solution.py:349
  60.6 15.8 %collective-permute-start.15 = (bf16[160,2048]{1,0:T(8,128)(2,1)S(1)}, bf16[160,2048]{1,0:T(8,128)(2,1)S(1)}, u32[]{:S(2)}, u32[]{:S(2)}) collective-permute-start(bf16[160,2048]{1,0:T(8,128)(2,1)S(1)} %collective-permute-done.11.refs_5_.refs_0_), channel_id=1, source_target_pairs={{0,1},{1,0},{2,3},{3,2},{4,5},{5,4},{6,7},{7,6},{8,9},{9,8},{10,11... | collective-permute-start | bytes 1966088 | tf_op jit(solution)/shard_map/ppermute | solution.py:349
  67.1 3.4 %collective-permute-start.19 = (bf16[2,2,1,40,1792]{4,3,2,1,0:T(8,128)(2,1)S(1)}, bf16[2,2,1,40,1792]{4,3,2,1,0:T(8,128)(2,1)S(1)}, u32[]{:S(2)}, u32[]{:S(2)}) collective-permute-start(bf16[2,2,1,40,1792]{4,3,2,1,0:T(8,128)(2,1)S(1)} %get-tuple-element.142), channel_id=1, source_target_pairs={{0,8},{8,0},{16,24},{24,16},{1,9},{9,1},{17,25},{25,17},{2,10},{10... | collective-permute-start | bytes 1720328 | tf_op jit(solution)/shard_map/ppermute | solution.py:349
  67.2 3.3 %collective-permute-start.20 = (bf16[2,2,40,1792]{3,2,1,0:T(8,128)(2,1)S(1)}, bf16[2,2,40,1792]{3,2,1,0:T(8,128)(2,1)S(1)}, u32[]{:S(2)}, u32[]{:S(2)}) collective-permute-start(bf16[2,2,40,1792]{3,2,1,0:T(8,128)(2,1)S(1)} %get-tuple-element.144), channel_id=1, source_target_pairs={{0,8},{8,0},{16,24},{24,16},{1,9},{9,1},{17,25},{25,17},{2,10},{10... | collective-permute-start | bytes 1720328 | tf_op jit(solution)/shard_map/ppermute | solution.py:349
  70.4 1.8 %collective-permute-start.18 = (bf16[2,40,1792]{2,1,0:T(8,128)(2,1)S(1)}, bf16[2,40,1792]{2,1,0:T(8,128)(2,1)S(1)}, u32[]{:S(2)}, u32[]{:S(2)}) collective-permute-start(bf16[2,40,1792]{2,1,0:T(8,128)(2,1)S(1)} %get-tuple-element.138.own_ref), channel_id=1, source_target_pairs={{0,8},{8,0},{16,24},{24,16},{1,9},{9,1},{17,25},{25,17},{2,10},{10... | collective-permute-start | bytes 860168 | tf_op jit(solution)/shard_map/ppermute | solution.py:349
  70.7 15.4 %collective-permute-start.23 = (bf16[2,2,40,1792]{3,2,1,0:T(8,128)(2,1)S(1)}, bf16[2,2,40,1792]{3,2,1,0:T(8,128)(2,1)S(1)}, u32[]{:S(2)}, u32[]{:S(2)}) collective-permute-start(bf16[2,2,40,1792]{3,2,1,0:T(8,128)(2,1)S(1)} %get-tuple-element.150), channel_id=1, source_target_pairs={{0,16},{8,24},{16,0},{24,8},{1,17},{9,25},{17,1},{25,9},{2,18},{10... | collective-permute-start | bytes 1720328 | tf_op jit(solution)/shard_map/ppermute | solution.py:349
  76.4 15.4 %collective-permute-start.28 = (bf16[2,40,4096]{2,1,0:T(8,128)(2,1)S(1)}, bf16[2,40,4096]{2,1,0:T(8,128)(2,1)S(1)}, u32[]{:S(2)}, u32[]{:S(2)}) collective-permute-start(bf16[2,40,4096]{2,1,0:T(8,128)(2,1)S(1)} %get-tuple-element.162), channel_id=1, source_target_pairs={{0,1},{1,0},{2,3},{3,2},{4,5},{5,4},{6,7},{7,6},{8,9},{9,8},{10,11... | collective-permute-start | bytes 1966088 | tf_op jit(solution)/shard_map/ppermute | solution.py:349
  83.2 3.3 %collective-permute-start.21 = (bf16[1,2,1,40,1792]{4,3,2,1,0:T(8,128)(2,1)S(1)}, bf16[1,2,1,40,1792]{4,3,2,1,0:T(8,128)(2,1)S(1)}, u32[]{:S(2)}, u32[]{:S(2)}) collective-permute-start(bf16[1,2,1,40,1792]{4,3,2,1,0:T(8,128)(2,1)S(1)} %get-tuple-element.148), channel_id=1, source_target_pairs={{0,8},{8,0},{16,24},{24,16},{1,9},{9,1},{17,25},{25,17},{2,10},{10... | collective-permute-start | bytes 860168 | tf_op jit(solution)/shard_map/ppermute | solution.py:349
  83.3 3.2 %collective-permute-start.22 = (bf16[1,2,1,40,1792]{4,3,2,1,0:T(8,128)(2,1)S(1)}, bf16[1,2,1,40,1792]{4,3,2,1,0:T(8,128)(2,1)S(1)}, u32[]{:S(2)}, u32[]{:S(2)}) collective-permute-start(bf16[1,2,1,40,1792]{4,3,2,1,0:T(8,128)(2,1)S(1)} %get-tuple-element.149), channel_id=1, source_target_pairs={{0,8},{8,0},{16,24},{24,16},{1,9},{9,1},{17,25},{25,17},{2,10},{10... | collective-permute-start | bytes 860168 | tf_op jit(solution)/shard_map/ppermute | solution.py:349
  86.4 2.3 %collective-permute-start.27 = (bf16[2,40,1792]{2,1,0:T(8,128)(2,1)S(1)}, bf16[2,40,1792]{2,1,0:T(8,128)(2,1)S(1)}, u32[]{:S(2)}, u32[]{:S(2)}) collective-permute-start(bf16[2,40,1792]{2,1,0:T(8,128)(2,1)S(1)} %get-tuple-element.158.own_ref), channel_id=1, source_target_pairs={{0,8},{8,0},{16,24},{24,16},{1,9},{9,1},{17,25},{25,17},{2,10},{10... | collective-permute-start | bytes 860168 | tf_op jit(solution)/shard_map/ppermute | solution.py:349
  86.6 15.8 %collective-permute-start.26 = (bf16[2,2,40,1792]{3,2,1,0:T(8,128)(2,1)S(1)}, bf16[2,2,40,1792]{3,2,1,0:T(8,128)(2,1)S(1)}, u32[]{:S(2)}, u32[]{:S(2)}) collective-permute-start(bf16[2,2,40,1792]{3,2,1,0:T(8,128)(2,1)S(1)} %get-tuple-element.157), channel_id=1, source_target_pairs={{0,8},{8,0},{16,24},{24,16},{1,9},{9,1},{17,25},{25,17},{2,10},{10... | collective-permute-start | bytes 1720328 | tf_op jit(solution)/shard_map/ppermute | solution.py:349
  87.2 15.3 %collective-permute-start.24 = (bf16[2,2,40,1792]{3,2,1,0:T(8,128)(2,1)S(1)}, bf16[2,2,40,1792]{3,2,1,0:T(8,128)(2,1)S(1)}, u32[]{:S(2)}, u32[]{:S(2)}) collective-permute-start(bf16[2,2,40,1792]{3,2,1,0:T(8,128)(2,1)S(1)} %get-tuple-element.153), channel_id=1, source_target_pairs={{0,16},{8,24},{16,0},{24,8},{1,17},{9,25},{17,1},{25,9},{2,18},{10... | collective-permute-start | bytes 1720328 | tf_op jit(solution)/shard_map/ppermute | solution.py:349
  91.8 9.0 %collective-permute-start.29 = (bf16[1,40,4096]{2,1,0:T(8,128)(2,1)S(1)}, bf16[1,40,4096]{2,1,0:T(8,128)(2,1)S(1)}, u32[]{:S(2)}, u32[]{:S(2)}) collective-permute-start(bf16[1,40,4096]{2,1,0:T(8,128)(2,1)S(1)} %get-tuple-element.163), channel_id=1, source_target_pairs={{0,1},{1,0},{2,3},{3,2},{4,5},{5,4},{6,7},{7,6},{8,9},{9,8},{10,11... | collective-permute-start | bytes 983048 | tf_op jit(solution)/shard_map/ppermute | solution.py:349
  93.5 17.7 %collective-permute-start.34 = (bf16[2,40,4096]{2,1,0:T(8,128)(2,1)S(1)}, bf16[2,40,4096]{2,1,0:T(8,128)(2,1)S(1)}, u32[]{:S(2)}, u32[]{:S(2)}) collective-permute-start(bf16[2,40,4096]{2,1,0:T(8,128)(2,1)S(1)} %get-tuple-element.178), channel_id=1, source_target_pairs={{0,2},{1,3},{2,0},{3,1},{4,6},{5,7},{6,4},{7,5},{8,10},{9,11},{10,... | collective-permute-start | bytes 1966088 | tf_op jit(solution)/shard_map/ppermute | solution.py:379
  100.9 8.2 %collective-permute-start.31 = (bf16[1,40,4096]{2,1,0:T(8,128)(2,1)S(1)}, bf16[1,40,4096]{2,1,0:T(8,128)(2,1)S(1)}, u32[]{:S(2)}, u32[]{:S(2)}) collective-permute-start(bf16[1,40,4096]{2,1,0:T(8,128)(2,1)S(1)} %get-tuple-element.174), channel_id=1, source_target_pairs={{0,1},{1,0},{2,3},{3,2},{4,5},{5,4},{6,7},{7,6},{8,9},{9,8},{10,11... | collective-permute-start | bytes 983048 | tf_op jit(solution)/shard_map/ppermute | solution.py:349
  102.8 2.9 %collective-permute-start.30 = (bf16[2,40,1792]{2,1,0:T(8,128)(2,1)S(1)}, bf16[2,40,1792]{2,1,0:T(8,128)(2,1)S(1)}, u32[]{:S(2)}, u32[]{:S(2)}) collective-permute-start(bf16[2,40,1792]{2,1,0:T(8,128)(2,1)S(1)} %get-tuple-element.168.own_ref), channel_id=1, source_target_pairs={{0,8},{8,0},{16,24},{24,16},{1,9},{9,1},{17,25},{25,17},{2,10},{10... | collective-permute-start | bytes 860168 | tf_op jit(solution)/shard_map/ppermute | solution.py:349
  102.8 18.4 %collective-permute-start.25 = (bf16[2,2,40,1792]{3,2,1,0:T(8,128)(2,1)S(1)}, bf16[2,2,40,1792]{3,2,1,0:T(8,128)(2,1)S(1)}, u32[]{:S(2)}, u32[]{:S(2)}) collective-permute-start(bf16[2,2,40,1792]{3,2,1,0:T(8,128)(2,1)S(1)} %get-tuple-element.154), channel_id=1, source_target_pairs={{0,16},{8,24},{16,0},{24,8},{1,17},{9,25},{17,1},{25,9},{2,18},{10... | collective-permute-start | bytes 1720328 | tf_op jit(solution)/shard_map/ppermute | solution.py:349
  104.1 14.1 %collective-permute-start.33 = (bf16[1,40,4096]{2,1,0:T(8,128)(2,1)S(1)}, bf16[1,40,4096]{2,1,0:T(8,128)(2,1)S(1)}, u32[]{:S(2)}, u32[]{:S(2)}) collective-permute-start(bf16[1,40,4096]{2,1,0:T(8,128)(2,1)S(1)} %get-tuple-element.173), channel_id=1, source_target_pairs={{0,2},{1,3},{2,0},{3,1},{4,6},{5,7},{6,4},{7,5},{8,10},{9,11},{10,... | collective-permute-start | bytes 983048 | tf_op jit(solution)/shard_map/ppermute | solution.py:379
  109.0 9.2 %collective-permute-start.32 = (bf16[1,40,4096]{2,1,0:T(8,128)(2,1)S(1)}, bf16[1,40,4096]{2,1,0:T(8,128)(2,1)S(1)}, u32[]{:S(2)}, u32[]{:S(2)}) collective-permute-start(bf16[1,40,4096]{2,1,0:T(8,128)(2,1)S(1)} %get-tuple-element.175), channel_id=1, source_target_pairs={{0,1},{1,0},{2,3},{3,2},{4,5},{5,4},{6,7},{7,6},{8,9},{9,8},{10,11... | collective-permute-start | bytes 983048 | tf_op jit(solution)/shard_map/ppermute | solution.py:349
  111.3 15.8 %collective-permute-start.38 = (bf16[1,40,4096]{2,1,0:T(8,128)(2,1)S(1)}, bf16[1,40,4096]{2,1,0:T(8,128)(2,1)S(1)}, u32[]{:S(2)}, u32[]{:S(2)}) collective-permute-start(bf16[1,40,4096]{2,1,0:T(8,128)(2,1)S(1)} %get-tuple-element.190), channel_id=1, source_target_pairs={{0,2},{1,3},{2,0},{3,1},{4,6},{5,7},{6,4},{7,5},{8,10},{9,11},{10,... | collective-permute-start | bytes 983048 | tf_op jit(solution)/shard_map/ppermute | solution.py:379
  118.4 8.8 %collective-permute-start.36 = (bf16[1,40,4096]{2,1,0:T(8,128)(2,1)S(1)}, bf16[1,40,4096]{2,1,0:T(8,128)(2,1)S(1)}, u32[]{:S(2)}, u32[]{:S(2)}) collective-permute-start(bf16[1,40,4096]{2,1,0:T(8,128)(2,1)S(1)} %get-tuple-element.187), channel_id=1, source_target_pairs={{0,1},{1,0},{2,3},{3,2},{4,5},{5,4},{6,7},{7,6},{8,9},{9,8},{10,11... | collective-permute-start | bytes 983048 | tf_op jit(solution)/shard_map/ppermute | solution.py:349
  119.7 25.0 %collective-permute-start.40 = (bf16[1,40,4096]{2,1,0:T(8,128)(2,1)S(1)}, bf16[1,40,4096]{2,1,0:T(8,128)(2,1)S(1)}, u32[]{:S(2)}, u32[]{:S(2)}) collective-permute-start(bf16[1,40,4096]{2,1,0:T(8,128)(2,1)S(1)} %get-tuple-element.186), channel_id=1, source_target_pairs={{0,4},{1,5},{4,0},{5,1},{2,6},{3,7},{6,2},{7,3},{8,12},{9,13},{12,... | collective-permute-start | bytes 983048 | tf_op jit(solution)/shard_map/ppermute | solution.py:379
  121.5 1.6 %collective-permute-start.35 = (bf16[2,40,1792]{2,1,0:T(8,128)(2,1)S(1)}, bf16[2,40,1792]{2,1,0:T(8,128)(2,1)S(1)}, u32[]{:S(2)}, u32[]{:S(2)}) collective-permute-start(bf16[2,40,1792]{2,1,0:T(8,128)(2,1)S(1)} %get-tuple-element.181.own_ref), channel_id=1, source_target_pairs={{0,8},{8,0},{16,24},{24,16},{1,9},{9,1},{17,25},{25,17},{2,10},{10... | collective-permute-start | bytes 860168 | tf_op jit(solution)/shard_map/ppermute | solution.py:349
  127.3 22.1 %collective-permute-start.39 = (bf16[1,40,4096]{2,1,0:T(8,128)(2,1)S(1)}, bf16[1,40,4096]{2,1,0:T(8,128)(2,1)S(1)}, u32[]{:S(2)}, u32[]{:S(2)}) collective-permute-start(bf16[1,40,4096]{2,1,0:T(8,128)(2,1)S(1)} %get-tuple-element.194), channel_id=1, source_target_pairs={{0,4},{1,5},{4,0},{5,1},{2,6},{3,7},{6,2},{7,3},{8,12},{9,13},{12,... | collective-permute-start | bytes 983048 | tf_op jit(solution)/shard_map/ppermute | solution.py:379
  128.3 17.0 %collective-permute-start.37 = (bf16[2,40,4096]{2,1,0:T(8,128)(2,1)S(1)}, bf16[2,40,4096]{2,1,0:T(8,128)(2,1)S(1)}, u32[]{:S(2)}, u32[]{:S(2)}) collective-permute-start(bf16[2,40,4096]{2,1,0:T(8,128)(2,1)S(1)} %get-tuple-element.188), channel_id=1, source_target_pairs={{0,1},{1,0},{2,3},{3,2},{4,5},{5,4},{6,7},{7,6},{8,9},{9,8},{10,11... | collective-permute-start | bytes 1966088 | tf_op jit(solution)/shard_map/ppermute | solution.py:349
  145.4 3.9 %collective-permute-start.41 = (bf16[40,4096]{1,0:T(8,128)(2,1)S(1)}, bf16[40,4096]{1,0:T(8,128)(2,1)S(1)}, u32[]{:S(2)}, u32[]{:S(2)}) collective-permute-start(bf16[40,4096]{1,0:T(8,128)(2,1)S(1)} %fusion.1), channel_id=1, source_target_pairs={{0,8},{8,0},{16,24},{24,16},{1,9},{9,1},{17,25},{25,17},{2,10},{10... | collective-permute-start | bytes 983048 | tf_op jit(solution)/shard_map/ppermute | solution.py:349
